TPU v7x, 32 devices: a whole 2x2x4 slice. The times are simulated.
32 devices in a mesh: grp: 2 (over x), row: 16 (over z, y, core), feat: 1.
Axes of the slice: x: 2, y: 2, z: 4, core: 2. Of those that a mesh axis runs over, the one named last changes fastest.
Arguments:
- tokens_in: bfloat16 [192, 64, 1024], P(('grp', 'row'), None, 'feat'), parts along dimension 0, may hold values from -40 to 40
- upstream: bfloat16 [192, 64, 1024], P(('grp', 'row'), None, 'feat'), parts along dimension 0, may hold values from -6 to 6
- member_pick: int32 [192, 1], P(('grp', 'row')), parts along dimension 0, may hold values from 0 to 1
- norm_gain: float32 [2, 1024], replicated, may hold values from 0.1 to 1.9
- up_proj: bfloat16 [2, 1024, 4096], P(None, 'row', 'feat'), may hold values from -0.1875 to 0.1875
- down_proj: bfloat16 [2, 1024, 4096], P(None, 'row', 'feat'), may hold values from -0.09375 to 0.09375
Outputs:
- value_out: bfloat16 [192, 64, 1024], P(('grp', 'row'), None, 'feat'), parts along dimension 0
- grad_in: bfloat16 [192, 64, 1024], P(('grp', 'row'), None, 'feat'), parts along dimension 0
- norm_coupling: float32 [192, 64], P(('grp', 'row')), parts along dimension 0
There are 2 independent parts, one for each index of `grp`. A program takes and returns all parts, laid end to end along the dimension named above; an argument that names none is the same for every part. Nothing has to cross between parts.
Inputs may be any that keep to these rules, and one draw needn't show every extreme that they name: `member_pick`: each row names exactly one member, and every member is named by at least one row.
All inputs are finite; a program needn't handle non-finite values.
Results may differ from a plain program's by a relative error of at most 0.0095.
Values may be sent and summed in bfloat16 or wider, within the bound.
No kernel may reach another device: no remote copies, remote signals or barrier semaphores. Data moves between devices by JAX's collectives and lax.ppermute only.
A program may use at most 128 MiB of HBM per device.

v0:
```python
import math

import jax
import jax.numpy as jnp
from jax import lax
from jax.sharding import PartitionSpec as P

coef_c = math.sqrt(2.0 / math.pi)


def gelu_tanh(v):
    return 0.5 * v * (1.0 + jnp.tanh(coef_c * (v + 0.044715 * v * v * v)))


def gelu_slope(v):
    inner = jnp.tanh(coef_c * (v + 0.044715 * v * v * v))
    return 0.5 * (1.0 + inner) + 0.5 * v * (1.0 - inner * inner) * coef_c * (
        1.0 + 3.0 * 0.044715 * v * v
    )


def on_device(tokens_in, upstream, member_pick, norm_gain, up_proj, down_proj):
    rows, seq, half = tokens_in.shape
    count = rows * seq
    members = up_proj.shape[0]
    pick = member_pick.shape[1]
    whole_x, whole_g = (
        lax.all_gather(tokens_in, "feat", axis=2, tiled=True),
        lax.all_gather(upstream, "feat", axis=2, tiled=True),
    )
    width = whole_x.shape[2]
    flat_x = whole_x.reshape(count, width).astype(jnp.float32)
    flat_g = whole_g.reshape(count, width)
    inv_rms = 1.0 / jnp.sqrt(jnp.mean(flat_x * flat_x, axis=1, keepdims=True) + 1e-06)
    normed = flat_x * inv_rms
    labels = jnp.arange(members, dtype=jnp.int32)
    chosen = (
        jnp.sum((member_pick[:, :, None] == labels[None, None, :]).astype(jnp.float32), axis=1)
        / pick
    )
    chosen_tok = jnp.repeat(chosen, seq, axis=0)
    out_half = jnp.zeros((count, half), jnp.float32)
    back_half = jnp.zeros((count, half), jnp.float32)
    for member in range(members):
        lifted = (normed * norm_gain[member][None, :]).astype(jnp.bfloat16)
        up_full = lax.all_gather(up_proj[member], "row", axis=0, tiled=True)
        hidden = jnp.dot(lifted, up_full, preferred_element_type=jnp.float32)
        act = gelu_tanh(hidden).astype(jnp.bfloat16)
        piece = lax.all_gather(down_proj[member], "row", axis=0, tiled=True)
        block = lax.dot_general(
            act, piece, (((1,), (1,)), ((), ())), preferred_element_type=jnp.float32
        )
        grads = jnp.dot(flat_g, piece, preferred_element_type=jnp.float32)
        pre_grad = (grads * gelu_slope(hidden)).astype(jnp.bfloat16)
        in_grad = lax.dot_general(
            pre_grad, up_full, (((1,), (1,)), ((), ())), preferred_element_type=jnp.float32
        )
        weight_col = chosen_tok[:, member : member + 1]
        out_term = weight_col * block
        back_term = weight_col * norm_gain[member][None, :] * in_grad
        out_part, back_part = (
            lax.psum_scatter(
                out_term.astype(jnp.bfloat16), "feat", scatter_dimension=1, tiled=True
            ).astype(jnp.float32),
            lax.psum_scatter(
                back_term.astype(jnp.bfloat16), "feat", scatter_dimension=1, tiled=True
            ).astype(jnp.float32),
        )
        out_half = out_half + out_part
        back_half = back_half + back_part
    own_x = tokens_in.reshape(count, half).astype(jnp.float32)
    normed_half = own_x * inv_rms
    stat = lax.psum(jnp.sum(normed_half * back_half, axis=1, keepdims=True), "feat") / width
    coupling = stat * math.sqrt(width)
    own_g = upstream.reshape(count, half).astype(jnp.float32)
    value_out = (own_x + out_half).astype(jnp.bfloat16)
    grad_in = (own_g + (back_half - normed_half * stat) * inv_rms).astype(jnp.bfloat16)
    return (
        value_out.reshape(rows, seq, half),
        grad_in.reshape(rows, seq, half),
        coupling.reshape(rows, seq),
    )


def solution(mesh):
    in_specs = (
        P(("grp", "row"), None, "feat"),
        P(("grp", "row"), None, "feat"),
        P(("grp", "row"), None),
        P(),
        P(None, "row", "feat"),
        P(None, "row", "feat"),
    )
    out_specs = (
        P(("grp", "row"), None, "feat"),
        P(("grp", "row"), None, "feat"),
        P(("grp", "row"), None),
    )
    return jax.shard_map(
        on_device, mesh=mesh, in_specs=in_specs, out_specs=out_specs, check_vma=False
    )
```

profile of v0, /device:TPU:8, one launch (start us, length us, event | category | flops | bytes accessed | tf_op | source)
XLA Modules:
  0.0 354.4 jit_solution(5110411133346224361)
XLA Ops:
  7.2 2.4 fusion.101
  9.6 0.0 all-gather.13.cloned.1.call-start
  9.7 0.7 all-gather.13.cloned.1.call-update
  10.4 0.0 all-gather.11.cloned.1.call-start
  10.4 2.3 fusion.102
  12.7 0.0 all-gather.15.cloned.1.call-start
  12.8 0.5 all-gather.15.cloned.1.call-update
  13.3 0.2 fusion.67
  13.5 0.1 sqrt.6
  13.6 0.1 broadcast_in_dim.2
  13.7 0.1 reshape.68
  13.8 0.3 fusion.60
  14.2 71.5 %all-gather.9.cloned.1.call-done = bf16[1,1024,4096]{2,1,0:T(8,128)(2,1)} async-done(((bf16[1,64,4096]{2,1,0:T(8,128)(2,1)}), bf16[1,1024,4096]{2,1,0:T(8,128)(2,1)}) %all-gather.9.cloned.1.call-update) | async-done | bytes 8388624 | tf_op jit(solution)/shard_map/all_gather | solution.py:46
  85.7 8.7 %fusion.14 = f32[384,4096]{1,0:T(8,128)} fusion(bf16[384,1024]{1,0:T(8,128)(2,1)S(1)} %get-tuple-element.9, bf16[1,1024,4096]{2,1,0:T(8,128)(2,1)} %all-gather.9.cloned.1.call-done), kind=kOutput, calls=%fused_computation.18 | convolution fusion | flops 3221225472 | bytes 15466496 | tf_op jit(solution)/shard_map/dot_general | solution.py:47
  94.4 66.7 %all-gather.13.cloned.1.call-done = bf16[1,1024,4096]{2,1,0:T(8,128)(2,1)} async-done(((bf16[1,64,4096]{2,1,0:T(8,128)(2,1)}), bf16[1,1024,4096]{2,1,0:T(8,128)(2,1)}) %all-gather.13.cloned.1.call-update) | async-done | bytes 8388624 | tf_op jit(solution)/shard_map/all_gather | solution.py:46
  161.0 8.7 %fusion.6 = f32[384,4096]{1,0:T(8,128)} fusion(bf16[384,1024]{1,0:T(8,128)(2,1)S(1)} %get-tuple-element.10, bf16[1,1024,4096]{2,1,0:T(8,128)(2,1)} %all-gather.13.cloned.1.call-done), kind=kOutput, calls=%fused_computation.10 | convolution fusion | flops 3221225472 | bytes 15466496 | tf_op jit(solution)/shard_map/dot_general | solution.py:47
  169.8 67.2 %all-gather.11.cloned.1.call-done = bf16[1,1024,4096]{2,1,0:T(8,128)(2,1)} async-done(((bf16[1,64,4096]{2,1,0:T(8,128)(2,1)}), bf16[1,1024,4096]{2,1,0:T(8,128)(2,1)}) %all-gather.11.cloned.1.call-update) | async-done | bytes 8388624 | tf_op jit(solution)/shard_map/all_gather | solution.py:49
  237.0 15.3 %multiply_convert_fusion.5 = bf16[384,1024]{1,0:T(8,128)(2,1)S(1)} fusion(bf16[1,1024,4096]{2,1,0:T(8,128)(2,1)} %all-gather.9.cloned.1.call-done, f32[384,4096]{1,0:T(8,128)} %fusion.14, bf16[384,1024]{1,0:T(8,128)(2,1)S(1)} %bitcast.86, bf16[1,1024,4096]{2,1,0:T(8,128)(2,1)} %all-gather.11.cloned.1.call-done, f32[1024]{0:T(1024)S(1)} %bitcast.92, ...), kind=kOutput, calls=%fused_computation.72 | convolution fusion | flops 6473515008 | bytes 24647168 | tf_op jit(solution)/shard_map/dot_general | solution.py:55
  252.3 60.4 %all-gather.15.cloned.1.call-done = bf16[1,1024,4096]{2,1,0:T(8,128)(2,1)} async-done(((bf16[1,64,4096]{2,1,0:T(8,128)(2,1)}), bf16[1,1024,4096]{2,1,0:T(8,128)(2,1)}) %all-gather.15.cloned.1.call-update) | async-done | bytes 8388624 | tf_op jit(solution)/shard_map/all_gather | solution.py:49
  312.7 15.8 %fusion.62 = (f32[384]{0:T(512)S(1)}, bf16[384,1024]{1,0:T(8,128)(2,1)S(1)}) fusion(bf16[6,64,1024]{2,1,0:T(8,128)(2,1)S(1)} %copy-done, bf16[384,1024]{1,0:T(8,128)(2,1)S(1)} %multiply_convert_fusion.5, f32[384]{0:T(512)S(1)} %sqrt.6, bf16[1,1024,4096]{2,1,0:T(8,128)(2,1)} %all-gather.13.cloned.1.call-done, f32[384,4096]{1,0:T(8,128)} %fusion.6, ...), kind=kOutput, calls=%fused_computation.63 | convolution fusion | flops 6476267008 | bytes 26223104 | tf_op jit(solution)/shard_map/dot_general | solution.py:55
  328.6 0.7 mul.256
  329.2 1.5 fusion.66
  330.7 9.3 %multiply_convert_fusion.6 = bf16[384,1024]{1,0:T(8,128)(2,1)S(1)} fusion(bf16[1,1024,4096]{2,1,0:T(8,128)(2,1)} %all-gather.15.cloned.1.call-done, f32[384,4096]{1,0:T(8,128)} %fusion.6, f32[384]{0:T(512)S(1)} %get-tuple-element.4), kind=kOutput, calls=%fused_computation.73 | convolution fusion | flops 3236167680 | bytes 15468032 | tf_op jit(solution)/shard_map/dot_general | solution.py:50
  340.0 7.8 %fusion.68 = bf16[384,1024]{1,0:T(8,128)(2,1)} fusion(bf16[6,64,1024]{2,1,0:T(8,128)(2,1)S(1)} %copy-done, bf16[384,1024]{1,0:T(8,128)(2,1)S(1)} %multiply_convert_fusion.6, bf16[1,1024,4096]{2,1,0:T(8,128)(2,1)S(1)} %bitcast.94, f32[384,4096]{1,0:T(8,128)} %fusion.14, f32[384]{0:T(512)S(1)} %get-tuple-element.3), kind=kOutput, calls=%fused_computation.69 | convolution fusion | flops 3238526976 | bytes 17040896 | tf_op jit(solution)/shard_map/dot_general | solution.py:50
  (21 shorter events, 0.1 us)
Async XLA Ops:
  7.2 6.1 %copy-start = (bf16[6,64,1024]{2,1,0:T(8,128)(2,1)S(1)}, bf16[6,64,1024]{2,1,0:T(8,128)(2,1)}, u32[]{:S(2)}) copy-start(bf16[6,64,1024]{2,1,0:T(8,128)(2,1)} %param.6) | copy-start | bytes 2359300
  7.2 6.4 %copy-start.3 = (s32[6,1]{0,1:T(1,128)S(1)}, s32[6,1]{0,1:T(1,128)}, u32[]{:S(2)}) copy-start(s32[6,1]{0,1:T(1,128)} %param.8) | copy-start | bytes 76
  7.2 6.6 %copy-start.2 = (f32[2,1024]{1,0:T(2,128)S(1)}, f32[2,1024]{1,0:T(2,128)}, u32[]{:S(2)}) copy-start(f32[2,1024]{1,0:T(2,128)} %param.9) | copy-start | bytes 24580
  7.2 78.5 %all-gather.9.cloned.1.call-start = ((), (), s32[]{:S(2)}) async-start(), calls=%async_computation | async-start | bytes 8912896 | tf_op jit(solution)/shard_map/all_gather | solution.py:46
  9.6 151.4 %all-gather.13.cloned.1.call-start = ((), (), s32[]{:S(2)}) async-start(), calls=%async_computation.2 | async-start | bytes 8912896 | tf_op jit(solution)/shard_map/all_gather | solution.py:46
  10.4 226.6 %all-gather.11.cloned.1.call-start = ((), (), s32[]{:S(2)}) async-start(), calls=%async_computation.1 | async-start | bytes 8912896 | tf_op jit(solution)/shard_map/all_gather | solution.py:49
  12.7 300.0 %all-gather.15.cloned.1.call-start = ((), (), s32[]{:S(2)}) async-start(), calls=%async_computation.3 | async-start | bytes 8912896 | tf_op jit(solution)/shard_map/all_gather | solution.py:49
  161.0 75.9 %copy-start.1 = (bf16[6,64,1024]{2,1,0:T(8,128)(2,1)S(1)}, bf16[6,64,1024]{2,1,0:T(8,128)(2,1)}, u32[]{:S(2)}) copy-start(bf16[6,64,1024]{2,1,0:T(8,128)(2,1)} %param.7) | copy-start | bytes 2359300
  329.2 10.8 %slice-start = ((s8[8388608]{0:T(1024)(128)(4,1)}), s8[4194304]{0:T(1024)(128)(4,1)S(1)}, s32[]{:S(2)}) async-start(s8[8388608]{0:T(1024)(128)(4,1)} %bitcast.93), calls=%async_computation.4 | async-start | bytes 8388608
  330.7 9.3 %slice-start.1 = ((s8[8388608]{0:T(1024)(128)(4,1)}), s8[4194304]{0:T(1024)(128)(4,1)S(1)}, s32[]{:S(2)}) async-start(s8[8388608]{0:T(1024)(128)(4,1)} %bitcast.93), calls=%async_computation.5 | async-start | bytes 8388608
Sparse Core Ops, SparseCore 0:
  10.2 75.4 all-gather.8
  87.8 73.1 all-gather.12
  163.8 73.1 all-gather.10
  239.5 73.1 all-gather.14
where the time goes:
time: 357 us; the launch traced here: 354 us
  waiting for transfers between devices  267 us (75%)
  matrix products  65.7 us (18%)
  between operations  13.9 us (4%)
  local copies, waits for them, and re-layouts  5.58 us (2%)
    all_gather x2, waiting for transfers between devices, on_device(): up_full = lax.all_gather(up_proj[member], 'row', axis=0, tiled=True)  138 us
    all_gather x2, waiting for transfers between devices, on_device(): piece = lax.all_gather(down_proj[member], 'row', axis=0, tiled=True)  128 us
    dot_general x2, matrix products, on_device(): lax.dot_general(pre_grad, up_full, (((1,), (1,)), ((), ())), preferred_el...  31.2 us
    dot_general x2, matrix products, on_device(): hidden = jnp.dot(lifted, up_full, preferred_element_type=jnp.float32)  17.4 us
    dot_general x2, matrix products, on_device(): lax.dot_general(act, piece, (((1,), (1,)), ((), ())), preferred_element_t...  17.1 us
  transfers between devices with their start and end apart: 4, of which 4 were waited for; matrix products, arithmetic and copies ran while one was open for 10% of the time, Pallas kernels for 0%

commit v1 on v0

--- a/solution.py
+++ b/solution.py
@@ -1,8 +1,11 @@
+import functools
 import math
 
 import jax
 import jax.numpy as jnp
 from jax import lax
+from jax.experimental import pallas as pl
+from jax.experimental.pallas import tpu as pltpu
 from jax.sharding import PartitionSpec as P
 
 coef_c = math.sqrt(2.0 / math.pi)
@@ -19,7 +22,7 @@
     )
 
 
-def on_device(tokens_in, upstream, member_pick, norm_gain, up_proj, down_proj):
+def on_device_general(tokens_in, upstream, member_pick, norm_gain, up_proj, down_proj):
     rows, seq, half = tokens_in.shape
     count = rows * seq
     members = up_proj.shape[0]
@@ -82,7 +85,260 @@
     )
 
 
+VMEM_LIMIT = 56 * 1024 * 1024
+BF16 = jnp.bfloat16
+F32 = jnp.float32
+
+
+def prep_kernel(perm_ref, sorted_ref, x_ref, g_ref, gain_ref, lifted_ref, gs_ref):
+    p = pl.program_id(0)
+    x = x_ref[0].astype(F32)
+    inv = 1.0 / jnp.sqrt(jnp.mean(x * x, axis=1, keepdims=True) + 1e-06)
+    gain = gain_ref[pl.ds(sorted_ref[p], 1), :]
+    lifted_ref[0] = ((x * inv) * gain).astype(BF16)
+    gs_ref[0] = g_ref[0]
+
+
+def prep(perm, member_sorted, x_pair, g_pair, gain):
+    rows, seq, width = x_pair.shape
+    block = pl.BlockSpec((1, seq, width), lambda p, perm, ms: (perm[p], 0, 0))
+    out = pl.BlockSpec((1, seq, width), lambda p, perm, ms: (p, 0, 0))
+    return pl.pallas_call(
+        prep_kernel,
+        grid_spec=pltpu.PrefetchScalarGridSpec(
+            num_scalar_prefetch=2,
+            grid=(rows,),
+            in_specs=[block, block, pl.BlockSpec(gain.shape, lambda p, perm, ms: (0, 0))],
+            out_specs=[out, out],
+        ),
+        out_shape=[jax.ShapeDtypeStruct((rows, seq, width), BF16)] * 2,
+        name="prep",
+    )(perm, member_sorted, x_pair, g_pair, gain)
+
+
+def chunk_kernel(member, per_block, seq, sub, first, flag_ref, sorted_ref, *refs):
+    if first:
+        lifted_ref, g_ref, up_ref, down_ref, out_ref, back_ref = refs
+    else:
+        lifted_ref, g_ref, up_ref, down_ref, out_in, back_in, out_ref, back_ref = refs
+    j = pl.program_id(0)
+    used = flag_ref[member * pl.num_programs(0) + j] > 0
+
+    @pl.when(used)
+    def _():
+        width = lifted_ref.shape[1]
+        lifted = lifted_ref[...]
+        g = g_ref[...]
+        weight = jnp.concatenate(
+            [
+                jnp.full((seq, 1), (sorted_ref[j * per_block + i] == member).astype(F32), F32)
+                for i in range(per_block)
+            ],
+            axis=0,
+        )
+        hidden_units = up_ref.shape[-1]
+        out_sum = jnp.zeros(out_ref.shape, F32)
+        back_sum = jnp.zeros(back_ref.shape, F32)
+        for s in range(hidden_units // sub):
+            cols = slice(s * sub, (s + 1) * sub)
+            up = up_ref[:, 0, :, cols].reshape(width, sub)
+            down = down_ref[:, 0, :, cols].reshape(width, sub)
+            v = jnp.dot(lifted, up, preferred_element_type=F32)
+            grads = jnp.dot(g, down, preferred_element_type=F32)
+            square = v * v
+            t = jnp.tanh(coef_c * (v + 0.044715 * square * v))
+            act = (0.5 * v * (1.0 + t)).astype(BF16)
+            slope = 0.5 * (1.0 + t) + 0.5 * v * (1.0 - t * t) * coef_c * (
+                1.0 + 3.0 * 0.044715 * square
+            )
+            pre = (grads * slope).astype(BF16)
+            dims = (((1,), (1,)), ((), ()))
+            out_sum += lax.dot_general(act, down, dims, preferred_element_type=F32)
+            back_sum += lax.dot_general(pre, up, dims, preferred_element_type=F32)
+        if first:
+            out_ref[...] = weight * out_sum
+            back_ref[...] = weight * back_sum
+        else:
+            out_ref[...] = out_in[...] + weight * out_sum
+            back_ref[...] = back_in[...] + weight * back_sum
+
+    @pl.when(jnp.logical_not(used))
+    def _():
+        if first:
+            out_ref[...] = jnp.zeros_like(out_ref)
+            back_ref[...] = jnp.zeros_like(back_ref)
+        else:
+            out_ref[...] = out_in[...]
+            back_ref[...] = back_in[...]
+
+
+def chunk(member, per_block, seq, flags, member_sorted, lifted, g, weights, sums):
+    tokens, width = lifted.shape
+    blocks, _, depth, hidden = weights.shape
+    size = per_block * seq
+    first = sums is None
+    tok = pl.BlockSpec((size, width), lambda j, f, s: (j, 0))
+    up = pl.BlockSpec((blocks, 1, depth, hidden), lambda j, f, s: (0, 0, 0, 0))
+    down = pl.BlockSpec((blocks, 1, depth, hidden), lambda j, f, s: (0, 1, 0, 0))
+    sub = math.gcd(hidden, 512)
+    args = [flags, member_sorted, lifted, g, weights, weights]
+    specs = [tok, tok, up, down]
+    alias = {}
+    if not first:
+        args += list(sums)
+        specs += [tok, tok]
+        alias = {6: 0, 7: 1}
+    return pl.pallas_call(
+        functools.partial(chunk_kernel, member, per_block, seq, sub, first),
+        grid_spec=pltpu.PrefetchScalarGridSpec(
+            num_scalar_prefetch=2, grid=(tokens // size,), in_specs=specs, out_specs=[tok, tok]
+        ),
+        out_shape=[jax.ShapeDtypeStruct((tokens, width), F32)] * 2,
+        input_output_aliases=alias,
+        compiler_params=pltpu.CompilerParams(vmem_limit_bytes=VMEM_LIMIT),
+        cost_estimate=pl.CostEstimate(
+            flops=8 * tokens * width * hidden * 2 // 3,
+            bytes_accessed=2 * weights.size + 20 * lifted.size,
+            transcendentals=tokens * hidden,
+        ),
+        name="chunk",
+    )(*args)
+
+
+def pack_kernel(pos_ref, out_ref, back_ref, packed_ref):
+    packed_ref[0, 0] = out_ref[...].astype(BF16)
+    packed_ref[1, 0] = back_ref[...].astype(BF16)
+
+
+def pack(pos_partner, out_sum, back_sum, rows, seq):
+    width = out_sum.shape[1]
+    tok = pl.BlockSpec((seq, width), lambda r, pos: (pos[r], 0))
+    return pl.pallas_call(
+        pack_kernel,
+        grid_spec=pltpu.PrefetchScalarGridSpec(
+            num_scalar_prefetch=1,
+            grid=(rows,),
+            in_specs=[tok, tok],
+            out_specs=pl.BlockSpec((2, 1, seq, width), lambda r, pos: (0, r, 0, 0)),
+        ),
+        out_shape=jax.ShapeDtypeStruct((2, rows, seq, width), BF16),
+        name="pack",
+    )(pos_partner, out_sum, back_sum)
+
+
+def finish_kernel(
+    pos_ref, member_ref, x_ref, g_ref, gain_ref, out_ref, back_ref, other_ref,
+    value_ref, grad_ref, coupling_ref,
+):
+    r = pl.program_id(0)
+    width = x_ref.shape[2]
+    x = x_ref[0].astype(F32)
+    inv = 1.0 / jnp.sqrt(jnp.mean(x * x, axis=1, keepdims=True) + 1e-06)
+    normed = x * inv
+    gain = gain_ref[pl.ds(member_ref[r], 1), :]
+    back = gain * (back_ref[...] + other_ref[1, 0].astype(F32))
+    stat = jnp.sum(normed * back, axis=1, keepdims=True) / width
+    value_ref[0] = (x + (out_ref[...] + other_ref[0, 0].astype(F32))).astype(BF16)
+    grad_ref[0] = (g_ref[0].astype(F32) + (back - normed * stat) * inv).astype(BF16)
+    coupling_ref[0] = stat * math.sqrt(width)
+
+
+def finish(pos_own, member_own, x, g, gain, out_sum, back_sum, other):
+    rows, seq, width = x.shape
+    row = pl.BlockSpec((1, seq, width), lambda r, pos, mem: (r, 0, 0))
+    tok = pl.BlockSpec((seq, width), lambda r, pos, mem: (pos[r], 0))
+    return pl.pallas_call(
+        finish_kernel,
+        grid_spec=pltpu.PrefetchScalarGridSpec(
+            num_scalar_prefetch=2,
+            grid=(rows,),
+            in_specs=[
+                row,
+                row,
+                pl.BlockSpec(gain.shape, lambda r, pos, mem: (0, 0)),
+                tok,
+                tok,
+                pl.BlockSpec((2, 1, seq, width), lambda r, pos, mem: (0, r, 0, 0)),
+            ],
+            out_specs=[row, row, pl.BlockSpec((1, seq, 1), lambda r, pos, mem: (r, 0, 0))],
+        ),
+        out_shape=[
+            jax.ShapeDtypeStruct((rows, seq, width), BF16),
+            jax.ShapeDtypeStruct((rows, seq, width), BF16),
+            jax.ShapeDtypeStruct((rows, seq, 1), F32),
+        ],
+        name="finish",
+    )(pos_own, member_own, x, g, gain, out_sum, back_sum, other)
+
+
+def on_device_pairs(ranks, tokens_in, upstream, member_pick, norm_gain, up_proj, down_proj):
+    rows, seq, width = tokens_in.shape
+    members, depth, hidden = up_proj.shape
+    half = hidden // 2
+    core = lax.rem(lax.axis_index("row"), 2)
+    swap = [(i, i ^ 1) for i in range(ranks)]
+
+    def partner(a):
+        return lax.ppermute(a, "row", swap)
+
+    both = jnp.stack([up_proj, down_proj])
+    mine = lax.dynamic_slice_in_dim(both, core * half, half, 3)
+    theirs = partner(lax.dynamic_slice_in_dim(both, (1 - core) * half, half, 3))
+    even = core == 0
+    shard = jnp.concatenate(
+        [jnp.where(even, mine, theirs), jnp.where(even, theirs, mine)], axis=2
+    )
+    same_core = [list(range(c, ranks, 2)) for c in range(2)]
+    parts = 2
+    size = half // parts
+
+    pick_own = member_pick[:, 0]
+    pick_pair = jnp.concatenate([pick_own, partner(pick_own)])
+    x_pair = jnp.concatenate([tokens_in, partner(tokens_in)])
+    g_pair = jnp.concatenate([upstream, partner(upstream)])
+    index = jnp.arange(2 * rows, dtype=jnp.int32)
+    before = (pick_pair[None, :] < pick_pair[:, None]) | (
+        (pick_pair[None, :] == pick_pair[:, None]) & (index[None, :] < index[:, None])
+    )
+    pos = jnp.sum(before.astype(jnp.int32), axis=1)
+    at = pos[None, :] == index[:, None]
+    perm = jnp.sum(jnp.where(at, index[None, :], 0), axis=1)
+    member_sorted = jnp.sum(jnp.where(at, pick_pair[None, :], 0), axis=1)
+    per_block = math.gcd(2 * rows, 4)
+    labels = jnp.arange(members, dtype=jnp.int32)
+    flags = jnp.any(
+        member_sorted.reshape(1, -1, per_block) == labels[:, None, None], axis=2
+    ).astype(jnp.int32).reshape(-1)
+
+    lifted, g_sorted = prep(perm, member_sorted, x_pair, g_pair, norm_gain)
+    lifted = lifted.reshape(2 * rows * seq, width)
+    g_sorted = g_sorted.reshape(2 * rows * seq, width)
+
+    sums = None
+    for member in range(members):
+        for part in range(parts):
+            piece = shard[:, member, :, part * size : (part + 1) * size]
+            weights = lax.all_gather(piece, "row", axis_index_groups=same_core)
+            sums = chunk(
+                member, per_block, seq, flags, member_sorted, lifted, g_sorted, weights, sums
+            )
+    other = partner(pack(pos[rows:], sums[0], sums[1], rows, seq))
+    value_out, grad_in, coupling = finish(
+        pos[:rows], pick_own, tokens_in, upstream, norm_gain, sums[0], sums[1], other
+    )
+    return value_out, grad_in, coupling.reshape(rows, seq)
+
+
 def solution(mesh):
+    ranks = mesh.shape["row"]
+    paired = mesh.shape["feat"] == 1 and ranks % 2 == 0
+
+    def on_device(tokens_in, upstream, member_pick, norm_gain, up_proj, down_proj):
+        args = (tokens_in, upstream, member_pick, norm_gain, up_proj, down_proj)
+        if paired and member_pick.shape[1] == 1:
+            return on_device_pairs(ranks, *args)
+        return on_device_general(*args)
+
     in_specs = (
         P(("grp", "row"), None, "feat"),
         P(("grp", "row"), None, "feat"),

time: 357 us -> 350 us (0.980)
  matrix products: 65.7 us -> 0 us
  Pallas kernels: 0 us -> 65.5 us
  waiting for transfers between devices: 267 us -> 255 us
  other arithmetic: 2.08 us -> 9.83 us
    dot_general x6 -> x0, matrix products: 65.7 us -> none  [the longest x2 31.2 us: on_device(): lax.dot_general(pre_grad, up_full, (((1,), (1,)), ((), ())), preferred_el...]
    pallas_call x0 -> x7, Pallas kernels: none -> 65.5 us  [the longest x4 44.2 us: chunk(): pl.pallas_call(functools.partial(chunk_kernel, member, per_block, seq, su...]
    all_gather x4, waiting for transfers between devices: 266 us -> 245 us  [on_device_pairs(): weights = lax.all_gather(piece, 'row', axis_index_groups=same_core)]
    ppermute x0 -> x5, waiting for transfers between devices: none -> 8.02 us  [partner(): return lax.ppermute(a, 'row', swap)]
    slice x4 -> x1, local copies, waits for them, and re-layouts: 4.66 us -> 0.58 us  [on_device_pairs(): other = partner(pack(pos[rows:], sums[0], sums[1], rows, seq))]
    concatenate x0 -> x4, other arithmetic: none -> 4.02 us  [the longest x1 1.36 us: on_device_pairs(): jnp.concatenate([jnp.where(even, mine, theirs), jnp.where(even, theirs, m...]
  transfers between devices with their start and end apart: 4 -> 9, of which waited for: 4 -> 7; matrix products, arithmetic and copies ran while one was open for 10% -> 1% of each run, Pallas kernels for 0% -> 12%
where the time goes in v1:
time: 350 us; the launch traced here: 347 us
  waiting for transfers between devices  255 us (73%)
  Pallas kernels  65.5 us (19%)
  between operations  13.8 us (4%)
  other arithmetic  9.83 us (3%)
    all_gather x4, waiting for transfers between devices, on_device_pairs(): weights = lax.all_gather(piece, 'row', axis_index_groups=same_core)  245 us
    pallas_call x4, Pallas kernels, chunk(): pl.pallas_call(functools.partial(chunk_kernel, member, per_block, seq, su...  44.2 us
    pallas_call x1, Pallas kernels, prep(): pl.pallas_call(prep_kernel, grid_spec=pltpu.PrefetchScalarGridSpec(num_sc...  9.12 us
    ppermute x5, waiting for transfers between devices, partner(): return lax.ppermute(a, 'row', swap)  8.02 us
  transfers between devices with their start and end apart: 9, of which 7 were waited for; matrix products, arithmetic and copies ran while one was open for 1% of the time, Pallas kernels for 12%

profile of v1, /device:TPU:8, one launch (start us, length us, event | category | flops | bytes accessed | tf_op | source)
XLA Modules:
  0.0 347.3 jit_solution(5629367283678386764)
XLA Ops:
  7.2 1.4 fusion
  8.7 2.8 collective-permute-done.3
  11.5 1.7 broadcast_select_fusion
  13.2 1.4 pad_maximum_fusion.2
  14.7 0.7 all-gather.13.cloned.1.call-update
  15.4 0.7 all-gather.11.cloned.1.call-update
  17.4 1.6 collective-permute-done
  19.3 0.7 select_reduce_fusion
  21.4 1.3 pad_maximum_fusion.x_ref
  22.8 1.3 pad_maximum_fusion.1.g_ref
  24.0 9.1 %prep.1 = (bf16[12,64,1024]{2,1,0:T(8,128)(2,1)}, bf16[12,64,1024]{2,1,0:T(8,128)(2,1)}) custom-call(s32[12]{0:T(128)} %get-tuple-element.29.perm_ref, s32[12]{0:T(128)} %copy-done.5, bf16[12,64,1024]{2,1,0:T(8,128)(2,1)} %pad_maximum_fusion.x_ref, bf16[12,64,1024]{2,1,0:T(8,128)(2,1)} %pad_maximum_fusion.1.g_ref, f32[2,1024]{1,0:T(2,128)} %gain_ref.3), custom_call_target="tpu_custom_call" | custom-call | tf_op jit(solution)/shard_map/prep/pallas_call | solution.py:106
  33.2 55.5 %all-gather.15.cloned.1.call-done = bf16[16,1,128,1024]{3,2,1,0:T(8,128)(2,1)} async-done(((bf16[2,1,128,1024]{3,2,1,0:T(8,128)(2,1)}), bf16[16,1,128,1024]{3,2,1,0:T(8,128)(2,1)}) %all-gather.15.cloned.1.call-update) | async-done | bytes 4194320 | tf_op jit(solution)/shard_map/all_gather | solution.py:321
  88.7 10.3 %chunk.4 = (f32[768,1024]{1,0:T(8,128)}, f32[768,1024]{1,0:T(8,128)}) custom-call(s32[6]{0:T(128)} %reshape.27.flag_ref, s32[12]{0:T(128)} %copy-done.5, bf16[768,1024]{1,0:T(8,128)(2,1)} %bitcast.15, bf16[768,1024]{1,0:T(8,128)(2,1)} %bitcast.19, bf16[8,2,128,1024]{3,2,1,0:T(8,128)(2,1)} %bitcast.30, bf16[8,2,128,1024]{3,2,1,0:T(8,128)(2,1)} %bitcast.31), custom_call_target="tpu_custom_call" | custom-call | flops 4294967296 | bytes 19922944 | tf_op jit(solution)/shard_map/chunk/pallas_call | solution.py:191
  99.0 63.5 %all-gather.13.cloned.1.call-done = bf16[16,1,128,1024]{3,2,1,0:T(8,128)(2,1)} async-done(((bf16[2,1,128,1024]{3,2,1,0:T(8,128)(2,1)}), bf16[16,1,128,1024]{3,2,1,0:T(8,128)(2,1)}) %all-gather.13.cloned.1.call-update) | async-done | bytes 4194320 | tf_op jit(solution)/shard_map/all_gather | solution.py:321
  162.5 11.0 %chunk.5 = (f32[768,1024]{1,0:T(8,128)}, f32[768,1024]{1,0:T(8,128)}) custom-call(s32[6]{0:T(128)} %reshape.27.flag_ref, s32[12]{0:T(128)} %copy-done.5, bf16[768,1024]{1,0:T(8,128)(2,1)} %bitcast.16, bf16[768,1024]{1,0:T(8,128)(2,1)} %bitcast.20, bf16[8,2,128,1024]{3,2,1,0:T(8,128)(2,1)} %bitcast.13, ...), custom_call_target="tpu_custom_call", output_to_operand_aliasing={{0}: (6, {}), {1}: (7, {})} | custom-call | flops 4294967296 | bytes 19922944 | tf_op jit(solution)/shard_map/chunk/pallas_call | solution.py:191
  173.5 62.9 %all-gather.11.cloned.1.call-done = bf16[16,1,128,1024]{3,2,1,0:T(8,128)(2,1)} async-done(((bf16[2,1,128,1024]{3,2,1,0:T(8,128)(2,1)}), bf16[16,1,128,1024]{3,2,1,0:T(8,128)(2,1)}) %all-gather.11.cloned.1.call-update) | async-done | bytes 4194320 | tf_op jit(solution)/shard_map/all_gather | solution.py:321
  236.4 11.4 %chunk.6 = (f32[768,1024]{1,0:T(8,128)}, f32[768,1024]{1,0:T(8,128)}) custom-call(s32[6]{0:T(128)} %reshape.27.flag_ref, s32[12]{0:T(128)} %copy-done.5, bf16[768,1024]{1,0:T(8,128)(2,1)} %bitcast.17, bf16[768,1024]{1,0:T(8,128)(2,1)} %bitcast.21, bf16[8,2,128,1024]{3,2,1,0:T(8,128)(2,1)} %bitcast.9, ...), custom_call_target="tpu_custom_call", output_to_operand_aliasing={{0}: (6, {}), {1}: (7, {})} | custom-call | flops 4294967296 | bytes 19922944 | tf_op jit(solution)/shard_map/chunk/pallas_call | solution.py:191
  247.8 62.8 %all-gather.9.cloned.1.call-done = bf16[16,1,128,1024]{3,2,1,0:T(8,128)(2,1)} async-done(((bf16[2,1,128,1024]{3,2,1,0:T(8,128)(2,1)}), bf16[16,1,128,1024]{3,2,1,0:T(8,128)(2,1)}) %all-gather.9.cloned.1.call-update) | async-done | bytes 4194320 | tf_op jit(solution)/shard_map/all_gather | solution.py:321
  310.6 11.4 %chunk.7 = (f32[768,1024]{1,0:T(8,128)}, f32[768,1024]{1,0:T(8,128)}) custom-call(s32[6]{0:T(128)} %reshape.27.flag_ref, s32[12]{0:T(128)} %copy-done.5, bf16[768,1024]{1,0:T(8,128)(2,1)} %bitcast.18, bf16[768,1024]{1,0:T(8,128)(2,1)} %bitcast.22, bf16[8,2,128,1024]{3,2,1,0:T(8,128)(2,1)} %bitcast.11, ...), custom_call_target="tpu_custom_call", output_to_operand_aliasing={{0}: (6, {}), {1}: (7, {})} | custom-call | flops 4294967296 | bytes 19922944 | tf_op jit(solution)/shard_map/chunk/pallas_call | solution.py:191
  322.1 5.5 %pack.1 = bf16[2,6,64,1024]{3,2,1,0:T(8,128)(2,1)} custom-call(s32[6]{0:T(128)} %get-tuple-element.37.pos_ref, f32[768,1024]{1,0:T(8,128)} %get-tuple-element.24.out_ref, f32[768,1024]{1,0:T(8,128)} %get-tuple-element.25.back_ref), custom_call_target="tpu_custom_call" | custom-call | tf_op jit(solution)/shard_map/pack/pallas_call | solution.py:216
  327.6 3.6 %collective-permute-done.4.other_ref = bf16[2,6,64,1024]{3,2,1,0:T(8,128)(2,1)S(1)} collective-permute-done((bf16[2,6,64,1024]{3,2,1,0:T(8,128)(2,1)}, bf16[2,6,64,1024]{3,2,1,0:T(8,128)(2,1)S(1)}, u32[]{:S(2)}, u32[]{:S(2)}) %collective-permute-start.4) | collective-permute-done | bytes 1572896 | tf_op jit(solution)/shard_map/ppermute | solution.py:282
  331.2 1.2 copy-done.4
  332.4 6.7 %finish.1 = (bf16[6,64,1024]{2,1,0:T(8,128)(2,1)}, bf16[6,64,1024]{2,1,0:T(8,128)(2,1)}, f32[6,64,1]{2,1,0:T(8,128)}) custom-call(s32[6]{0:T(128)} %get-tuple-element.38.pos_ref, s32[6]{0:T(128)} %bitcast.27, bf16[6,64,1024]{2,1,0:T(8,128)(2,1)} %x_ref.1, bf16[6,64,1024]{2,1,0:T(8,128)(2,1)} %g_ref.1, f32[2,1024]{1,0:T(2,128)} %gain_ref.3, ...), custom_call_target="tpu_custom_call" | custom-call | tf_op jit(solution)/shard_map/finish/pallas_call | solution.py:250
  339.1 1.6 reduce
  (33 shorter events, 3.2 us)
Async XLA Ops:
  7.2 4.3 %copy-start = (bf16[2,64,4096]{2,1,0:T(8,128)(2,1)S(1)}, bf16[2,64,4096]{2,1,0:T(8,128)(2,1)}, u32[]{:S(2)}) copy-start(bf16[2,64,4096]{2,1,0:T(8,128)(2,1)} %param.10) | copy-start | bytes 3145732
  7.2 4.3 %copy-start.1 = (bf16[2,64,4096]{2,1,0:T(8,128)(2,1)S(1)}, bf16[2,64,4096]{2,1,0:T(8,128)(2,1)}, u32[]{:S(2)}) copy-start(bf16[2,64,4096]{2,1,0:T(8,128)(2,1)} %param.11) | copy-start | bytes 3145732
  7.2 81.5 %all-gather.15.cloned.1.call-start = ((), (), s32[]{:S(2)}) async-start(), calls=%async_computation.3 | async-start | bytes 4718592 | tf_op jit(solution)/shard_map/all_gather | solution.py:321
  8.6 2.9 collective-permute-start.3
  14.6 2.1 copy-start.2
  14.6 2.3 copy-start.6
  14.6 2.7 copy-start.3
  14.6 147.9 %all-gather.13.cloned.1.call-start = ((), (), s32[]{:S(2)}) async-start(), calls=%async_computation.2 | async-start | bytes 4718592 | tf_op jit(solution)/shard_map/all_gather | solution.py:321
  15.4 221.0 %all-gather.11.cloned.1.call-start = ((), (), s32[]{:S(2)}) async-start(), calls=%async_computation.1 | async-start | bytes 4718592 | tf_op jit(solution)/shard_map/all_gather | solution.py:321
  16.1 294.5 %all-gather.9.cloned.1.call-start = ((), (), s32[]{:S(2)}) async-start(), calls=%async_computation | async-start | bytes 4718592 | tf_op jit(solution)/shard_map/all_gather | solution.py:321
  16.7 4.8 %collective-permute-start.1 = (bf16[6,64,1024]{2,1,0:T(8,128)(2,1)S(1)}, bf16[6,64,1024]{2,1,0:T(8,128)(2,1)S(1)}, u32[]{:S(2)}, u32[]{:S(2)}) collective-permute-start(bf16[6,64,1024]{2,1,0:T(8,128)(2,1)S(1)} %copy-done.2), channel_id=1, source_target_pairs={{0,1},{1,0},{2,3},{3,2},{4,5},{5,4},{6,7},{7,6},{8,9},{9,8},{10,11... | collective-permute-start | bytes 2359304 | tf_op jit(solution)/shard_map/ppermute | solution.py:282
  16.9 2.1 collective-permute-start
  17.3 5.5 %collective-permute-start.2 = (bf16[6,64,1024]{2,1,0:T(8,128)(2,1)S(1)}, bf16[6,64,1024]{2,1,0:T(8,128)(2,1)S(1)}, u32[]{:S(2)}, u32[]{:S(2)}) collective-permute-start(bf16[6,64,1024]{2,1,0:T(8,128)(2,1)S(1)} %copy-done.3), channel_id=1, source_target_pairs={{0,1},{1,0},{2,3},{3,2},{4,5},{5,4},{6,7},{7,6},{8,9},{9,8},{10,11... | collective-permute-start | bytes 2359304 | tf_op jit(solution)/shard_map/ppermute | solution.py:282
  20.0 4.0 %copy-start.5 = (s32[12]{0:T(128)}, s32[12]{0:T(128)S(1)}, u32[]{:S(2)}) copy-start(s32[12]{0:T(128)S(1)} %get-tuple-element.30.sorted_ref) | copy-start | bytes 148
  327.6 3.6 %collective-permute-start.4 = (bf16[2,6,64,1024]{3,2,1,0:T(8,128)(2,1)}, bf16[2,6,64,1024]{3,2,1,0:T(8,128)(2,1)S(1)}, u32[]{:S(2)}, u32[]{:S(2)}) collective-permute-start(bf16[2,6,64,1024]{3,2,1,0:T(8,128)(2,1)} %pack.1), channel_id=1, source_target_pairs={{0,1},{1,0},{2,3},{3,2},{4,5},{5,4},{6,7},{7,6},{8,9},{9,8},{10,11... | collective-permute-start | bytes 4718600 | tf_op jit(solution)/shard_map/ppermute | solution.py:282
  331.2 1.2 copy-start.4
Sparse Core Ops, SparseCore 0:
  14.7 73.8 all-gather.14
  90.8 71.6 all-gather.12
  164.6 71.6 all-gather.10
  238.9 71.6 all-gather.8

commit v2 on v1

v2 whole, which is shorter than its diff:
```python
import functools
import math

import jax
import jax.numpy as jnp
from jax import lax
from jax.experimental import pallas as pl
from jax.experimental.pallas import tpu as pltpu
from jax.sharding import PartitionSpec as P

coef_c = math.sqrt(2.0 / math.pi)


def gelu_tanh(v):
    return 0.5 * v * (1.0 + jnp.tanh(coef_c * (v + 0.044715 * v * v * v)))


def gelu_slope(v):
    inner = jnp.tanh(coef_c * (v + 0.044715 * v * v * v))
    return 0.5 * (1.0 + inner) + 0.5 * v * (1.0 - inner * inner) * coef_c * (
        1.0 + 3.0 * 0.044715 * v * v
    )


def on_device_general(tokens_in, upstream, member_pick, norm_gain, up_proj, down_proj):
    rows, seq, half = tokens_in.shape
    count = rows * seq
    members = up_proj.shape[0]
    pick = member_pick.shape[1]
    whole_x, whole_g = (
        lax.all_gather(tokens_in, "feat", axis=2, tiled=True),
        lax.all_gather(upstream, "feat", axis=2, tiled=True),
    )
    width = whole_x.shape[2]
    flat_x = whole_x.reshape(count, width).astype(jnp.float32)
    flat_g = whole_g.reshape(count, width)
    inv_rms = 1.0 / jnp.sqrt(jnp.mean(flat_x * flat_x, axis=1, keepdims=True) + 1e-06)
    normed = flat_x * inv_rms
    labels = jnp.arange(members, dtype=jnp.int32)
    chosen = (
        jnp.sum((member_pick[:, :, None] == labels[None, None, :]).astype(jnp.float32), axis=1)
        / pick
    )
    chosen_tok = jnp.repeat(chosen, seq, axis=0)
    out_half = jnp.zeros((count, half), jnp.float32)
    back_half = jnp.zeros((count, half), jnp.float32)
    for member in range(members):
        lifted = (normed * norm_gain[member][None, :]).astype(jnp.bfloat16)
        up_full = lax.all_gather(up_proj[member], "row", axis=0, tiled=True)
        hidden = jnp.dot(lifted, up_full, preferred_element_type=jnp.float32)
        act = gelu_tanh(hidden).astype(jnp.bfloat16)
        piece = lax.all_gather(down_proj[member], "row", axis=0, tiled=True)
        block = lax.dot_general(
            act, piece, (((1,), (1,)), ((), ())), preferred_element_type=jnp.float32
        )
        grads = jnp.dot(flat_g, piece, preferred_element_type=jnp.float32)
        pre_grad = (grads * gelu_slope(hidden)).astype(jnp.bfloat16)
        in_grad = lax.dot_general(
            pre_grad, up_full, (((1,), (1,)), ((), ())), preferred_element_type=jnp.float32
        )
        weight_col = chosen_tok[:, member : member + 1]
        out_term = weight_col * block
        back_term = weight_col * norm_gain[member][None, :] * in_grad
        out_part, back_part = (
            lax.psum_scatter(
                out_term.astype(jnp.bfloat16), "feat", scatter_dimension=1, tiled=True
            ).astype(jnp.float32),
            lax.psum_scatter(
                back_term.astype(jnp.bfloat16), "feat", scatter_dimension=1, tiled=True
            ).astype(jnp.float32),
        )
        out_half = out_half + out_part
        back_half = back_half + back_part
    own_x = tokens_in.reshape(count, half).astype(jnp.float32)
    normed_half = own_x * inv_rms
    stat = lax.psum(jnp.sum(normed_half * back_half, axis=1, keepdims=True), "feat") / width
    coupling = stat * math.sqrt(width)
    own_g = upstream.reshape(count, half).astype(jnp.float32)
    value_out = (own_x + out_half).astype(jnp.bfloat16)
    grad_in = (own_g + (back_half - normed_half * stat) * inv_rms).astype(jnp.bfloat16)
    return (
        value_out.reshape(rows, seq, half),
        grad_in.reshape(rows, seq, half),
        coupling.reshape(rows, seq),
    )


VMEM_LIMIT = 56 * 1024 * 1024
BF16 = jnp.bfloat16
F32 = jnp.float32


def prep_kernel(perm_ref, sorted_ref, x_ref, g_ref, gain_ref, lifted_ref, gs_ref):
    def row(p, carry):
        x = x_ref[perm_ref[p]].astype(F32)
        inv = 1.0 / jnp.sqrt(jnp.mean(x * x, axis=1, keepdims=True) + 1e-06)
        gain = gain_ref[pl.ds(sorted_ref[p], 1), :]
        lifted_ref[p] = ((x * inv) * gain).astype(BF16)
        gs_ref[p] = g_ref[perm_ref[p]]
        return carry

    lax.fori_loop(0, x_ref.shape[0], row, 0)


def prep(perm, member_sorted, x_pair, g_pair, gain):
    smem = pl.BlockSpec(memory_space=pltpu.SMEM)
    vmem = pl.BlockSpec(memory_space=pltpu.VMEM)
    return pl.pallas_call(
        prep_kernel,
        in_specs=[smem, smem, vmem, vmem, vmem],
        out_specs=[vmem, vmem],
        out_shape=[jax.ShapeDtypeStruct(x_pair.shape, BF16)] * 2,
        compiler_params=pltpu.CompilerParams(vmem_limit_bytes=VMEM_LIMIT),
        name="prep",
    )(perm, member_sorted, x_pair, g_pair, gain)


def chunk_kernel(
    member, per_block, seq, sub, own, first, opens,
    low_ref, high_ref, sorted_ref, place_ref, lifted_ref, g_ref, here_ref, there_ref,
    here_x_ref, there_x_ref, *refs,
):
    if first:
        out_ref, back_ref, weights_ref, sems = refs
    else:
        out_in, back_in, out_ref, back_ref, weights_ref, sems = refs
    j = pl.program_id(0)
    _, _, depth2, hidden_units = weights_ref.shape
    lines = weights_ref.shape[0]
    depth = depth2 // 2
    common = here_ref.shape[1] - own

    @pl.when(j == 0)
    def _():
        x, y = place_ref[0], place_ref[1]
        mine = pl.multiple_of(x * (depth2 - own), 16)
        others = pl.multiple_of((1 - x) * (depth2 - own), 16)
        copies = []
        for line, ref, x_ref in ((y, here_ref, here_x_ref), (1 - y, there_ref, there_x_ref)):
            for src, at, size in (
                (ref.at[:, pl.ds(0, own)], mine, own),
                (ref.at[:, pl.ds(own, common)], own, common),
                (x_ref, others, own),
            ):
                copies.append(
                    pltpu.make_async_copy(
                        src, weights_ref.at[:, line, pl.ds(at, size)], sems.at[len(copies)]
                    )
                )
        for copy in copies:
            copy.start()
        for copy in copies:
            copy.wait()

    if not first:

        @pl.when(jnp.logical_and(j == 0, high_ref[member] < low_ref[member]))
        def _():
            out_ref[...] = out_in[...]
            back_ref[...] = back_in[...]

    @pl.when(low_ref[member] + j <= high_ref[member])
    def _():
        at = low_ref[member] + j
        width = lifted_ref.shape[1]
        lifted = lifted_ref[...]
        g = g_ref[...]
        weight = jnp.concatenate(
            [
                jnp.full((seq, 1), (sorted_ref[at * per_block + i] == member).astype(F32), F32)
                for i in range(per_block)
            ],
            axis=0,
        )
        out_sum = jnp.zeros(out_ref.shape, F32)
        back_sum = jnp.zeros(back_ref.shape, F32)
        for s in range(hidden_units // sub):
            cols = slice(s * sub, (s + 1) * sub)
            up = weights_ref[:, :, :depth, cols].reshape(width, sub)
            down = weights_ref[:, :, depth:, cols].reshape(width, sub)
            v = jnp.dot(lifted, up, preferred_element_type=F32)
            grads = jnp.dot(g, down, preferred_element_type=F32)
            square = v * v
            t = jnp.tanh(coef_c * (v + 0.044715 * square * v))
            act = (0.5 * v * (1.0 + t)).astype(BF16)
            slope = 0.5 * (1.0 + t) + 0.5 * v * (1.0 - t * t) * coef_c * (
                1.0 + 3.0 * 0.044715 * square
            )
            pre = (grads * slope).astype(BF16)
            dims = (((1,), (1,)), ((), ()))
            out_sum += lax.dot_general(act, down, dims, preferred_element_type=F32)
            back_sum += lax.dot_general(pre, up, dims, preferred_element_type=F32)
        if first:
            out_ref[...] = weight * out_sum
            back_ref[...] = weight * back_sum
        elif opens:
            old = (sorted_ref[at * per_block] < member)
            out_ref[...] = jnp.where(old, out_in[...], 0.0) + weight * out_sum
            back_ref[...] = jnp.where(old, back_in[...], 0.0) + weight * back_sum
        else:
            out_ref[...] = out_in[...] + weight * out_sum
            back_ref[...] = back_in[...] + weight * back_sum


def chunk(member, opens, per_block, seq, scalars, lifted, g, pieces, sums):
    tokens, width = lifted.shape
    lines, rows, hidden = pieces[0].shape
    own = pieces[2].shape[1]
    depth2 = 2 * own + (rows - own)
    size = per_block * seq
    first = sums is None
    tok = pl.BlockSpec(
        (size, width),
        lambda j, low, high, s, p: (
            jnp.maximum(jnp.minimum(low[member] + j, high[member]), 0), 0
        ),
    )
    hbm = pl.BlockSpec(memory_space=pl.ANY)
    sub = math.gcd(hidden, 512)
    args = [*scalars, lifted, g, *pieces]
    specs = [tok, tok, hbm, hbm, hbm, hbm]
    alias = {}
    if not first:
        alias = {len(args): 0, len(args) + 1: 1}
        args += list(sums)
        specs += [tok, tok]
    return pl.pallas_call(
        functools.partial(chunk_kernel, member, per_block, seq, sub, own, first, opens),
        grid_spec=pltpu.PrefetchScalarGridSpec(
            num_scalar_prefetch=4,
            grid=(tokens // size,),
            in_specs=specs,
            out_specs=[tok, tok],
            scratch_shapes=[
                pltpu.VMEM((lines, 2, depth2, hidden), BF16),
                pltpu.SemaphoreType.DMA((6,)),
            ],
        ),
        out_shape=[jax.ShapeDtypeStruct((tokens, width), F32)] * 2,
        input_output_aliases=alias,
        compiler_params=pltpu.CompilerParams(vmem_limit_bytes=VMEM_LIMIT),
        cost_estimate=pl.CostEstimate(
            flops=8 * tokens * width * hidden * 2 // 3,
            bytes_accessed=4 * width * hidden + 20 * lifted.size,
            transcendentals=tokens * hidden,
        ),
        name="chunk",
    )(*args)


def pack_kernel(pos_ref, out_ref, back_ref, packed_ref, buffer, sems):
    rows = packed_ref.shape[1]
    seq = packed_ref.shape[2]
    copies = []
    for r in range(rows):
        at = pl.ds(pl.multiple_of(pos_ref[r] * seq, seq), seq)
        for i, ref in enumerate((out_ref, back_ref)):
            copy = pltpu.make_async_copy(ref.at[at], buffer.at[i, r], sems.at[i, r])
            copy.start()
            copies.append((copy, i, r))
    for copy, i, r in copies:
        copy.wait()
        packed_ref[i, r] = buffer[i, r].astype(BF16)


def pack(pos_partner, out_sum, back_sum, rows, seq):
    width = out_sum.shape[1]
    hbm = pl.BlockSpec(memory_space=pl.ANY)
    return pl.pallas_call(
        pack_kernel,
        in_specs=[pl.BlockSpec(memory_space=pltpu.SMEM), hbm, hbm],
        out_specs=pl.BlockSpec(memory_space=pltpu.VMEM),
        out_shape=jax.ShapeDtypeStruct((2, rows, seq, width), BF16),
        scratch_shapes=[
            pltpu.VMEM((2, rows, seq, width), F32),
            pltpu.SemaphoreType.DMA((2, rows)),
        ],
        compiler_params=pltpu.CompilerParams(vmem_limit_bytes=VMEM_LIMIT),
        name="pack",
    )(pos_partner, out_sum, back_sum)


def finish_kernel(
    pos_ref, member_ref, x_ref, g_ref, gain_ref, out_ref, back_ref, other_ref,
    value_ref, grad_ref, coupling_ref, buffer, sems,
):
    rows, seq, width = x_ref.shape
    copies = []
    for r in range(rows):
        at = pl.ds(pl.multiple_of(pos_ref[r] * seq, seq), seq)
        for i, ref in enumerate((out_ref, back_ref)):
            copy = pltpu.make_async_copy(ref.at[at], buffer.at[i, r], sems.at[i, r])
            copy.start()
            copies.append(copy)
    diagonal = lax.broadcasted_iota(jnp.int32, (seq, seq), 0) == lax.broadcasted_iota(
        jnp.int32, (seq, seq), 1
    )
    for r in range(rows):
        copies[2 * r].wait()
        copies[2 * r + 1].wait()
        x = x_ref[r].astype(F32)
        inv = 1.0 / jnp.sqrt(jnp.mean(x * x, axis=1, keepdims=True) + 1e-06)
        normed = x * inv
        gain = gain_ref[pl.ds(member_ref[r], 1), :]
        back = gain * (buffer[1, r] + other_ref[1, r].astype(F32))
        stat = jnp.sum(normed * back, axis=1, keepdims=True) / width
        value_ref[r] = (x + (buffer[0, r] + other_ref[0, r].astype(F32))).astype(BF16)
        grad_ref[r] = (g_ref[r].astype(F32) + (back - normed * stat) * inv).astype(BF16)
        line = jnp.sum(jnp.where(diagonal, stat, 0.0), axis=0, keepdims=True)
        coupling_ref[pl.ds(r, 1), :] = line * math.sqrt(width)


def finish(pos_own, member_own, x, g, gain, out_sum, back_sum, other):
    rows, seq, width = x.shape
    smem = pl.BlockSpec(memory_space=pltpu.SMEM)
    vmem = pl.BlockSpec(memory_space=pltpu.VMEM)
    hbm = pl.BlockSpec(memory_space=pl.ANY)
    return pl.pallas_call(
        finish_kernel,
        in_specs=[smem, smem, vmem, vmem, vmem, hbm, hbm, vmem],
        out_specs=[vmem, vmem, vmem],
        out_shape=[
            jax.ShapeDtypeStruct((rows, seq, width), BF16),
            jax.ShapeDtypeStruct((rows, seq, width), BF16),
            jax.ShapeDtypeStruct((rows, seq), F32),
        ],
        scratch_shapes=[
            pltpu.VMEM((2, rows, seq, width), F32),
            pltpu.SemaphoreType.DMA((2, rows)),
        ],
        compiler_params=pltpu.CompilerParams(vmem_limit_bytes=VMEM_LIMIT),
        name="finish",
    )(pos_own, member_own, x, g, gain, out_sum, back_sum, other)


def chunk_sizes(half, members):
    unit = half // 8
    if unit % 128:
        return [[half]] * members
    small = [unit, unit, 2 * unit, 2 * unit, 2 * unit]
    plan = [[2 * unit] * 4 for _ in range(members)]
    plan[0] = small
    plan[-1] = small[::-1]
    return plan


def on_device_pairs(ranks, tokens_in, upstream, member_pick, norm_gain, up_proj, down_proj):
    rows, seq, width = tokens_in.shape
    members, depth, hidden = up_proj.shape
    half = hidden // 2
    rank = lax.axis_index("row")
    core = lax.rem(rank, 2)
    x_at = lax.axis_index("grp")
    y_at = lax.rem(rank // 2, 2)

    def partner(a):
        return lax.ppermute(a, "row", [(i, i ^ 1) for i in range(ranks)])

    def over_y(a):
        return lax.ppermute(a, "row", [(i, i ^ 2) for i in range(ranks)])

    def over_x(a):
        return lax.ppermute(a, "grp", [(0, 1), (1, 0)])

    lines = [list(range(i, ranks, 4)) for i in range(4)]

    both = jnp.stack([up_proj, down_proj], axis=1)
    mine = lax.dynamic_slice_in_dim(both, core * half, half, 3)
    theirs = partner(lax.dynamic_slice_in_dim(both, (1 - core) * half, half, 3))
    even = core == 0
    shard = jnp.concatenate(
        [jnp.where(even, mine, theirs), jnp.where(even, theirs, mine)], axis=2
    ).reshape(members, 4 * depth, half)
    own = 5 * depth // 4
    piece_all = jnp.concatenate(
        [
            jnp.where(x_at == 0, shard[:, :own], shard[:, 4 * depth - own :]),
            shard[:, own : 4 * depth - own],
        ],
        axis=1,
    )

    pick_own = member_pick[:, 0]
    pick_pair = jnp.concatenate([pick_own, partner(pick_own)])
    x_pair = jnp.concatenate([tokens_in, partner(tokens_in)])
    g_pair = jnp.concatenate([upstream, partner(upstream)])
    index = jnp.arange(2 * rows, dtype=jnp.int32)
    before = (pick_pair[None, :] < pick_pair[:, None]) | (
        (pick_pair[None, :] == pick_pair[:, None]) & (index[None, :] < index[:, None])
    )
    pos = jnp.sum(before.astype(jnp.int32), axis=1)
    at = pos[None, :] == index[:, None]
    perm = jnp.sum(jnp.where(at, index[None, :], 0), axis=1)
    member_sorted = jnp.sum(jnp.where(at, pick_pair[None, :], 0), axis=1)
    per_block = math.gcd(2 * rows, 4)
    labels = jnp.arange(members, dtype=jnp.int32)[:, None]
    start = jnp.sum((pick_pair[None, :] < labels).astype(jnp.int32), axis=1)
    count = jnp.sum((pick_pair[None, :] == labels).astype(jnp.int32), axis=1)
    low = jnp.minimum(start, 2 * rows - 1) // per_block
    high = jnp.where(count > 0, (start + count - 1) // per_block, low - 1)

    lifted, g_sorted = prep(perm, member_sorted, x_pair, g_pair, norm_gain)
    lifted = lifted.reshape(2 * rows * seq, width)
    g_sorted = g_sorted.reshape(2 * rows * seq, width)
    scalars = (low, high, member_sorted, jnp.stack([x_at, y_at]))

    sums = None
    for member, sizes in enumerate(chunk_sizes(half, members)):
        for part, size in enumerate(sizes):
            first_unit = sum(sizes[:part])
            piece = piece_all[member, :, first_unit : first_unit + size]
            here = lax.all_gather(piece, "row", axis_index_groups=lines)
            there = over_y(here)
            here_x = over_x(here[:, :own])
            there_x = over_x(there[:, :own])
            pieces = (here, there, here_x, there_x)
            sums = chunk(
                member, part == 0, per_block, seq, scalars, lifted, g_sorted, pieces, sums
            )
    other = partner(pack(pos[rows:], sums[0], sums[1], rows, seq))
    return tuple(
        finish(pos[:rows], pick_own, tokens_in, upstream, norm_gain, sums[0], sums[1], other)
    )


def solution(mesh):
    ranks = mesh.shape["row"]
    paired = mesh.shape["feat"] == 1 and ranks % 4 == 0 and mesh.shape["grp"] == 2

    def on_device(tokens_in, upstream, member_pick, norm_gain, up_proj, down_proj):
        args = (tokens_in, upstream, member_pick, norm_gain, up_proj, down_proj)
        if paired and member_pick.shape[1] == 1:
            return on_device_pairs(ranks, *args)
        return on_device_general(*args)

    in_specs = (
        P(("grp", "row"), None, "feat"),
        P(("grp", "row"), None, "feat"),
        P(("grp", "row"), None),
        P(),
        P(None, "row", "feat"),
        P(None, "row", "feat"),
    )
    out_specs = (
        P(("grp", "row"), None, "feat"),
        P(("grp", "row"), None, "feat"),
        P(("grp", "row"), None),
    )
    return jax.shard_map(
        on_device, mesh=mesh, in_specs=in_specs, out_specs=out_specs, check_vma=False
    )
```

time: 350 us -> 332 us (0.949)
  the two profiles are of different devices: /device:TPU:8 before, /device:TPU:25 now
where the time goes in v2:
time: 332 us; the launch traced here: 338 us
  blocking collectives  136 us (41%)
  Pallas kernels  104 us (31%)
  starting transfers between devices  64 us (19%)
  local copies, waits for them, and re-layouts  13.2 us (4%)
  other arithmetic  11.3 us (3%)
  waiting for transfers between devices  7.39 us (2%)
    all_gather x10, blocking collectives, on_device_pairs(): here = lax.all_gather(piece, 'row', axis_index_groups=lines)  136 us
    pallas_call x10, Pallas kernels, chunk(): pl.pallas_call(functools.partial(chunk_kernel, member, per_block, seq, su...  89.5 us
    ppermute x5, starting transfers between devices, partner(): return lax.ppermute(a, 'row', [(i, i ^ 1) for i in range(ranks)])  37.9 us
    ppermute x20, starting transfers between devices, over_x(): return lax.ppermute(a, 'grp', [(0, 1), (1, 0)])  16.4 us
    ppermute x10, starting transfers between devices, over_y(): return lax.ppermute(a, 'row', [(i, i ^ 2) for i in range(ranks)])  9.75 us
  transfers between devices with their start and end apart: 35, of which 4 were waited for; matrix products, arithmetic and copies ran while one was open for 5% of the time, Pallas kernels for 25%

profile of v2, /device:TPU:25, one launch (start us, length us, event | category | flops | bytes accessed | tf_op | source)
XLA Modules:
  0.0 337.5 jit_solution(8915116461237936721)
XLA Ops:
  10.2 12.0 %all_gather.39.here_ref = bf16[4,176,256]{2,1,0:T(8,128)(2,1)S(1)} all-gather(bf16[1,176,256]{2,1,0:T(8,128)(2,1)S(1)} %get-tuple-element.55), channel_id=1, replica_groups={{0,4,8,12},{1,5,9,13},{2,6,10,14},{3,7,11,15},{16,20,24,28},{17,21,25,2..., dimensions={0}, use_global_device_ids=true | all-gather | bytes 450560 | tf_op jit(solution)/shard_map/all_gather | solution.py:412
  23.5 12.8 %all_gather.38.here_ref = bf16[4,176,256]{2,1,0:T(8,128)(2,1)S(1)} all-gather(bf16[1,176,256]{2,1,0:T(8,128)(2,1)S(1)} %get-tuple-element.58), channel_id=1, replica_groups={{0,4,8,12},{1,5,9,13},{2,6,10,14},{3,7,11,15},{16,20,24,28},{17,21,25,2..., dimensions={0}, use_global_device_ids=true | all-gather | bytes 450560 | tf_op jit(solution)/shard_map/all_gather | solution.py:412
  36.5 15.1 %all_gather.37.here_ref = bf16[4,176,512]{2,1,0:T(8,128)(2,1)S(1)} all-gather(bf16[1,176,512]{2,1,0:T(8,128)(2,1)S(1)} %get-tuple-element.59), channel_id=1, replica_groups={{0,4,8,12},{1,5,9,13},{2,6,10,14},{3,7,11,15},{16,20,24,28},{17,21,25,2..., dimensions={0}, use_global_device_ids=true | all-gather | bytes 901120 | tf_op jit(solution)/shard_map/all_gather | solution.py:412
  51.6 12.1 %all_gather.31.here_ref = bf16[4,176,256]{2,1,0:T(8,128)(2,1)S(1)} all-gather(bf16[1,176,256]{2,1,0:T(8,128)(2,1)S(1)} %get-tuple-element.56), channel_id=1, replica_groups={{0,4,8,12},{1,5,9,13},{2,6,10,14},{3,7,11,15},{16,20,24,28},{17,21,25,2..., dimensions={0}, use_global_device_ids=true | all-gather | bytes 450560 | tf_op jit(solution)/shard_map/all_gather | solution.py:412
  65.0 12.8 %all_gather.36.here_ref = bf16[4,176,512]{2,1,0:T(8,128)(2,1)S(1)} all-gather(bf16[1,176,512]{2,1,0:T(8,128)(2,1)S(1)} %get-tuple-element.64), channel_id=1, replica_groups={{0,4,8,12},{1,5,9,13},{2,6,10,14},{3,7,11,15},{16,20,24,28},{17,21,25,2..., dimensions={0}, use_global_device_ids=true | all-gather | bytes 901120 | tf_op jit(solution)/shard_map/all_gather | solution.py:412
  77.9 13.3 %all_gather.30.here_ref = bf16[4,176,256]{2,1,0:T(8,128)(2,1)S(1)} all-gather(bf16[1,176,256]{2,1,0:T(8,128)(2,1)S(1)} %get-tuple-element.57), channel_id=1, replica_groups={{0,4,8,12},{1,5,9,13},{2,6,10,14},{3,7,11,15},{16,20,24,28},{17,21,25,2..., dimensions={0}, use_global_device_ids=true | all-gather | bytes 450560 | tf_op jit(solution)/shard_map/all_gather | solution.py:412
  91.7 13.3 %all_gather.35.here_ref = bf16[4,176,512]{2,1,0:T(8,128)(2,1)S(1)} all-gather(bf16[1,176,512]{2,1,0:T(8,128)(2,1)S(1)} %get-tuple-element.63), channel_id=1, replica_groups={{0,4,8,12},{1,5,9,13},{2,6,10,14},{3,7,11,15},{16,20,24,28},{17,21,25,2..., dimensions={0}, use_global_device_ids=true | all-gather | bytes 901120 | tf_op jit(solution)/shard_map/all_gather | solution.py:412
  109.0 15.7 %all_gather.34.here_ref = bf16[4,176,512]{2,1,0:T(8,128)(2,1)S(1)} all-gather(bf16[1,176,512]{2,1,0:T(8,128)(2,1)S(1)} %get-tuple-element.62), channel_id=1, replica_groups={{0,4,8,12},{1,5,9,13},{2,6,10,14},{3,7,11,15},{16,20,24,28},{17,21,25,2..., dimensions={0}, use_global_device_ids=true | all-gather | bytes 901120 | tf_op jit(solution)/shard_map/all_gather | solution.py:412
  127.8 15.3 %all_gather.33.here_ref = bf16[4,176,512]{2,1,0:T(8,128)(2,1)S(1)} all-gather(bf16[1,176,512]{2,1,0:T(8,128)(2,1)S(1)} %get-tuple-element.61), channel_id=1, replica_groups={{0,4,8,12},{1,5,9,13},{2,6,10,14},{3,7,11,15},{16,20,24,28},{17,21,25,2..., dimensions={0}, use_global_device_ids=true | all-gather | bytes 901120 | tf_op jit(solution)/shard_map/all_gather | solution.py:412
  144.6 13.3 %all_gather.32.here_ref = bf16[4,176,512]{2,1,0:T(8,128)(2,1)S(1)} all-gather(bf16[1,176,512]{2,1,0:T(8,128)(2,1)S(1)} %get-tuple-element.60), channel_id=1, replica_groups={{0,4,8,12},{1,5,9,13},{2,6,10,14},{3,7,11,15},{16,20,24,28},{17,21,25,2..., dimensions={0}, use_global_device_ids=true | all-gather | bytes 901120 | tf_op jit(solution)/shard_map/all_gather | solution.py:412
  166.9 5.4 %prep.1 = (bf16[12,64,1024]{2,1,0:T(8,128)(2,1)}, bf16[12,64,1024]{2,1,0:T(8,128)(2,1)}) custom-call(s32[12]{0:T(128)} %get-tuple-element.47.perm_ref, s32[12]{0:T(128)} %get-tuple-element.48.sorted_ref, bf16[12,64,1024]{2,1,0:T(8,128)(2,1)} %pad_maximum_fusion.1.x_ref, bf16[12,64,1024]{2,1,0:T(8,128)(2,1)} %pad_maximum_fusion.2.g_ref, f32[2,1024]{1,0:T(2,128)} %gain_ref.3), custom_call_target="tpu_custom_call" | custom-call | tf_op jit(solution)/shard_map/prep/pallas_call | solution.py:108
  182.9 5.7 %chunk.10 = (f32[768,1024]{1,0:T(8,128)}, f32[768,1024]{1,0:T(8,128)}) custom-call(s32[2]{0:T(128)} %get-tuple-element.52.low_ref, s32[2]{0:T(128)} %get-tuple-element.51.high_ref, s32[12]{0:T(128)} %get-tuple-element.48.sorted_ref, s32[2]{0:T(128)} %get-tuple-element.67.place_ref, bf16[768,1024]{1,0:T(8,128)(2,1)} %bitcast.8, bf16[768,1024]{1,0:T(8,128)(2,1)} %bitcast.18, ...), custom_call_target="tpu_custom_call" | custom-call | flops 1073741824 | bytes 16777216 | tf_op jit(solution)/shard_map/chunk/pallas_call | solution.py:227
  188.6 6.4 %chunk.11 = (f32[768,1024]{1,0:T(8,128)}, f32[768,1024]{1,0:T(8,128)}) custom-call(s32[2]{0:T(128)} %get-tuple-element.52.low_ref, s32[2]{0:T(128)} %get-tuple-element.51.high_ref, s32[12]{0:T(128)} %get-tuple-element.48.sorted_ref, s32[2]{0:T(128)} %get-tuple-element.67.place_ref, ...), custom_call_target="tpu_custom_call", output_to_operand_aliasing={{0}: (10, {}), {1}: (11, {})} | custom-call | flops 1073741824 | bytes 16777216 | tf_op jit(solution)/shard_map/chunk/pallas_call | solution.py:227
  199.9 7.1 %chunk.12 = (f32[768,1024]{1,0:T(8,128)}, f32[768,1024]{1,0:T(8,128)}) custom-call(s32[2]{0:T(128)} %get-tuple-element.52.low_ref, s32[2]{0:T(128)} %get-tuple-element.51.high_ref, s32[12]{0:T(128)} %get-tuple-element.48.sorted_ref, s32[2]{0:T(128)} %get-tuple-element.67.place_ref, ...), custom_call_target="tpu_custom_call", output_to_operand_aliasing={{0}: (10, {}), {1}: (11, {})} | custom-call | flops 2147483648 | bytes 17825792 | tf_op jit(solution)/shard_map/chunk/pallas_call | solution.py:227
  208.5 7.1 %chunk.13 = (f32[768,1024]{1,0:T(8,128)}, f32[768,1024]{1,0:T(8,128)}) custom-call(s32[2]{0:T(128)} %get-tuple-element.52.low_ref, s32[2]{0:T(128)} %get-tuple-element.51.high_ref, s32[12]{0:T(128)} %get-tuple-element.48.sorted_ref, s32[2]{0:T(128)} %get-tuple-element.67.place_ref, ...), custom_call_target="tpu_custom_call", output_to_operand_aliasing={{0}: (10, {}), {1}: (11, {})} | custom-call | flops 2147483648 | bytes 17825792 | tf_op jit(solution)/shard_map/chunk/pallas_call | solution.py:227
  217.2 7.2 %chunk.14 = (f32[768,1024]{1,0:T(8,128)}, f32[768,1024]{1,0:T(8,128)}) custom-call(s32[2]{0:T(128)} %get-tuple-element.52.low_ref, s32[2]{0:T(128)} %get-tuple-element.51.high_ref, s32[12]{0:T(128)} %get-tuple-element.48.sorted_ref, s32[2]{0:T(128)} %get-tuple-element.67.place_ref, ...), custom_call_target="tpu_custom_call", output_to_operand_aliasing={{0}: (10, {}), {1}: (11, {})} | custom-call | flops 2147483648 | bytes 17825792 | tf_op jit(solution)/shard_map/chunk/pallas_call | solution.py:227
  225.9 11.8 %chunk.15 = (f32[768,1024]{1,0:T(8,128)}, f32[768,1024]{1,0:T(8,128)}) custom-call(s32[2]{0:T(128)} %get-tuple-element.52.low_ref, s32[2]{0:T(128)} %get-tuple-element.51.high_ref, s32[12]{0:T(128)} %get-tuple-element.48.sorted_ref, s32[2]{0:T(128)} %get-tuple-element.67.place_ref, ...), custom_call_target="tpu_custom_call", output_to_operand_aliasing={{0}: (10, {}), {1}: (11, {})} | custom-call | flops 2147483648 | bytes 17825792 | tf_op jit(solution)/shard_map/chunk/pallas_call | solution.py:227
  239.4 11.7 %chunk.16 = (f32[768,1024]{1,0:T(8,128)}, f32[768,1024]{1,0:T(8,128)}) custom-call(s32[2]{0:T(128)} %get-tuple-element.52.low_ref, s32[2]{0:T(128)} %get-tuple-element.51.high_ref, s32[12]{0:T(128)} %get-tuple-element.48.sorted_ref, s32[2]{0:T(128)} %get-tuple-element.67.place_ref, ...), custom_call_target="tpu_custom_call", output_to_operand_aliasing={{0}: (10, {}), {1}: (11, {})} | custom-call | flops 2147483648 | bytes 17825792 | tf_op jit(solution)/shard_map/chunk/pallas_call | solution.py:227
  252.7 11.6 %chunk.17 = (f32[768,1024]{1,0:T(8,128)}, f32[768,1024]{1,0:T(8,128)}) custom-call(s32[2]{0:T(128)} %get-tuple-element.52.low_ref, s32[2]{0:T(128)} %get-tuple-element.51.high_ref, s32[12]{0:T(128)} %get-tuple-element.48.sorted_ref, s32[2]{0:T(128)} %get-tuple-element.67.place_ref, ...), custom_call_target="tpu_custom_call", output_to_operand_aliasing={{0}: (10, {}), {1}: (11, {})} | custom-call | flops 2147483648 | bytes 17825792 | tf_op jit(solution)/shard_map/chunk/pallas_call | solution.py:227
  265.1 10.5 %chunk.18 = (f32[768,1024]{1,0:T(8,128)}, f32[768,1024]{1,0:T(8,128)}) custom-call(s32[2]{0:T(128)} %get-tuple-element.52.low_ref, s32[2]{0:T(128)} %get-tuple-element.51.high_ref, s32[12]{0:T(128)} %get-tuple-element.48.sorted_ref, s32[2]{0:T(128)} %get-tuple-element.67.place_ref, ...), custom_call_target="tpu_custom_call", output_to_operand_aliasing={{0}: (10, {}), {1}: (11, {})} | custom-call | flops 1073741824 | bytes 16777216 | tf_op jit(solution)/shard_map/chunk/pallas_call | solution.py:227
  276.3 10.5 %chunk.19 = (f32[768,1024]{1,0:T(8,128)}, f32[768,1024]{1,0:T(8,128)}) custom-call(s32[2]{0:T(128)} %get-tuple-element.52.low_ref, s32[2]{0:T(128)} %get-tuple-element.51.high_ref, s32[12]{0:T(128)} %get-tuple-element.48.sorted_ref, s32[2]{0:T(128)} %get-tuple-element.67.place_ref, ...), custom_call_target="tpu_custom_call", output_to_operand_aliasing={{0}: (10, {}), {1}: (11, {})} | custom-call | flops 1073741824 | bytes 16777216 | tf_op jit(solution)/shard_map/chunk/pallas_call | solution.py:227
  286.9 3.8 %pack.1 = bf16[2,6,64,1024]{3,2,1,0:T(8,128)(2,1)} custom-call(s32[6]{0:T(128)} %get-tuple-element.65.pos_ref, f32[768,1024]{1,0:T(8,128)} %get-tuple-element.45.out_ref, f32[768,1024]{1,0:T(8,128)} %get-tuple-element.46.back_ref), custom_call_target="tpu_custom_call" | custom-call | tf_op jit(solution)/shard_map/pack/pallas_call | solution.py:269
  290.7 36.7 %collective-permute-start.34 = (bf16[2,6,64,1024]{3,2,1,0:T(8,128)(2,1)}, bf16[2,6,64,1024]{3,2,1,0:T(8,128)(2,1)S(1)}, u32[]{:S(2)}, u32[]{:S(2)}) collective-permute-start(bf16[2,6,64,1024]{3,2,1,0:T(8,128)(2,1)} %pack.1), channel_id=1, source_target_pairs={{0,1},{1,0},{2,3},{3,2},{4,5},{5,4},{6,7},{7,6},{8,9},{9,8},{10,11... | collective-permute-start | bytes 4718600 | tf_op jit(solution)/shard_map/ppermute | solution.py:357
  331.8 5.5 %finish.1 = (bf16[6,64,1024]{2,1,0:T(8,128)(2,1)}, bf16[6,64,1024]{2,1,0:T(8,128)(2,1)}, f32[6,64]{1,0:T(8,128)}) custom-call(s32[6]{0:T(128)} %get-tuple-element.66.pos_ref, s32[6]{0:T(128)} %bitcast.34, bf16[6,64,1024]{2,1,0:T(8,128)(2,1)} %x_ref.1, bf16[6,64,1024]{2,1,0:T(8,128)(2,1)} %g_ref.1, f32[2,1024]{1,0:T(2,128)} %gain_ref.3, ...), custom_call_target="tpu_custom_call" | custom-call | tf_op jit(solution)/shard_map/finish/pallas_call | solution.py:318
  (205 shorter events, 59.2 us)
Async XLA Ops:
  3.8 87.4 %collective-permute-start.1 = (bf16[6,64,1024]{2,1,0:T(8,128)(2,1)S(1)}, bf16[6,64,1024]{2,1,0:T(8,128)(2,1)}, u32[]{:S(2)}, u32[]{:S(2)}) collective-permute-start(bf16[6,64,1024]{2,1,0:T(8,128)(2,1)S(1)} %copy-done.8), channel_id=1, source_target_pairs={{0,1},{1,0},{2,3},{3,2},{4,5},{5,4},{6,7},{7,6},{8,9},{9,8},{10,11... | collective-permute-start | bytes 2359304 | tf_op jit(solution)/shard_map/ppermute | solution.py:357
  4.3 100.8 %collective-permute-start.2 = (bf16[6,64,1024]{2,1,0:T(8,128)(2,1)}, bf16[6,64,1024]{2,1,0:T(8,128)(2,1)}, u32[]{:S(2)}, u32[]{:S(2)}) collective-permute-start(bf16[6,64,1024]{2,1,0:T(8,128)(2,1)} %g_ref.1), channel_id=1, source_target_pairs={{0,1},{1,0},{2,3},{3,2},{4,5},{5,4},{6,7},{7,6},{8,9},{9,8},{10,11... | collective-permute-start | bytes 2359304 | tf_op jit(solution)/shard_map/ppermute | solution.py:357
  22.2 84.1 %collective-permute-start.31 = (bf16[4,176,256]{2,1,0:T(8,128)(2,1)S(1)}, bf16[4,176,256]{2,1,0:T(8,128)(2,1)S(1)}, u32[]{:S(2)}, u32[]{:S(2)}) collective-permute-start(bf16[4,176,256]{2,1,0:T(8,128)(2,1)S(1)} %all_gather.39.here_ref), channel_id=1, source_target_pairs={{0,2},{1,3},{2,0},{3,1},{4,6},{5,7},{6,4},{7,5},{8,10},{9,11},{10,... | collective-permute-start | bytes 1081352 | tf_op jit(solution)/shard_map/ppermute | solution.py:360
  36.3 70.3 %collective-permute-start.28 = (bf16[4,176,256]{2,1,0:T(8,128)(2,1)S(1)}, bf16[4,176,256]{2,1,0:T(8,128)(2,1)S(1)}, u32[]{:S(2)}, u32[]{:S(2)}) collective-permute-start(bf16[4,176,256]{2,1,0:T(8,128)(2,1)S(1)} %all_gather.38.here_ref), channel_id=1, source_target_pairs={{0,2},{1,3},{2,0},{3,1},{4,6},{5,7},{6,4},{7,5},{8,10},{9,11},{10,... | collective-permute-start | bytes 1081352 | tf_op jit(solution)/shard_map/ppermute | solution.py:360
  63.7 62.5 %collective-permute-start.7 = (bf16[4,176,256]{2,1,0:T(8,128)(2,1)S(1)}, bf16[4,176,256]{2,1,0:T(8,128)(2,1)S(1)}, u32[]{:S(2)}, u32[]{:S(2)}) collective-permute-start(bf16[4,176,256]{2,1,0:T(8,128)(2,1)S(1)} %all_gather.31.here_ref), channel_id=1, source_target_pairs={{0,2},{1,3},{2,0},{3,1},{4,6},{5,7},{6,4},{7,5},{8,10},{9,11},{10,... | collective-permute-start | bytes 1081352 | tf_op jit(solution)/shard_map/ppermute | solution.py:360
  91.2 36.3 %collective-permute-start.4 = (bf16[4,176,256]{2,1,0:T(8,128)(2,1)S(1)}, bf16[4,176,256]{2,1,0:T(8,128)(2,1)S(1)}, u32[]{:S(2)}, u32[]{:S(2)}) collective-permute-start(bf16[4,176,256]{2,1,0:T(8,128)(2,1)S(1)} %all_gather.30.here_ref), channel_id=1, source_target_pairs={{0,2},{1,3},{2,0},{3,1},{4,6},{5,7},{6,4},{7,5},{8,10},{9,11},{10,... | collective-permute-start | bytes 1081352 | tf_op jit(solution)/shard_map/ppermute | solution.py:360
  106.6 51.3 %collective-permute-start.25 = (bf16[4,176,512]{2,1,0:T(8,128)(2,1)S(1)}, bf16[4,176,512]{2,1,0:T(8,128)(2,1)S(1)}, u32[]{:S(2)}, u32[]{:S(2)}) collective-permute-start(bf16[4,176,512]{2,1,0:T(8,128)(2,1)S(1)} %all_gather.37.here_ref), channel_id=1, source_target_pairs={{0,2},{1,3},{2,0},{3,1},{4,6},{5,7},{6,4},{7,5},{8,10},{9,11},{10,... | collective-permute-start | bytes 2162696 | tf_op jit(solution)/shard_map/ppermute | solution.py:360
  124.7 38.2 %collective-permute-start.22 = (bf16[4,176,512]{2,1,0:T(8,128)(2,1)S(1)}, bf16[4,176,512]{2,1,0:T(8,128)(2,1)S(1)}, u32[]{:S(2)}, u32[]{:S(2)}) collective-permute-start(bf16[4,176,512]{2,1,0:T(8,128)(2,1)S(1)} %all_gather.36.here_ref), channel_id=1, source_target_pairs={{0,2},{1,3},{2,0},{3,1},{4,6},{5,7},{6,4},{7,5},{8,10},{9,11},{10,... | collective-permute-start | bytes 2162696 | tf_op jit(solution)/shard_map/ppermute | solution.py:360
  124.8 39.0 %collective-permute-start.19 = (bf16[4,176,512]{2,1,0:T(8,128)(2,1)S(1)}, bf16[4,176,512]{2,1,0:T(8,128)(2,1)S(1)}, u32[]{:S(2)}, u32[]{:S(2)}) collective-permute-start(bf16[4,176,512]{2,1,0:T(8,128)(2,1)S(1)} %all_gather.35.here_ref), channel_id=1, source_target_pairs={{0,2},{1,3},{2,0},{3,1},{4,6},{5,7},{6,4},{7,5},{8,10},{9,11},{10,... | collective-permute-start | bytes 2162696 | tf_op jit(solution)/shard_map/ppermute | solution.py:360
  143.1 37.2 %collective-permute-start.16 = (bf16[4,176,512]{2,1,0:T(8,128)(2,1)S(1)}, bf16[4,176,512]{2,1,0:T(8,128)(2,1)S(1)}, u32[]{:S(2)}, u32[]{:S(2)}) collective-permute-start(bf16[4,176,512]{2,1,0:T(8,128)(2,1)S(1)} %all_gather.34.here_ref), channel_id=1, source_target_pairs={{0,2},{1,3},{2,0},{3,1},{4,6},{5,7},{6,4},{7,5},{8,10},{9,11},{10,... | collective-permute-start | bytes 2162696 | tf_op jit(solution)/shard_map/ppermute | solution.py:360
  143.2 38.5 %collective-permute-start.13 = (bf16[4,176,512]{2,1,0:T(8,128)(2,1)S(1)}, bf16[4,176,512]{2,1,0:T(8,128)(2,1)S(1)}, u32[]{:S(2)}, u32[]{:S(2)}) collective-permute-start(bf16[4,176,512]{2,1,0:T(8,128)(2,1)S(1)} %all_gather.33.here_ref), channel_id=1, source_target_pairs={{0,2},{1,3},{2,0},{3,1},{4,6},{5,7},{6,4},{7,5},{8,10},{9,11},{10,... | collective-permute-start | bytes 2162696 | tf_op jit(solution)/shard_map/ppermute | solution.py:360
  158.0 39.1 %collective-permute-start.10 = (bf16[4,176,512]{2,1,0:T(8,128)(2,1)S(1)}, bf16[4,176,512]{2,1,0:T(8,128)(2,1)S(1)}, u32[]{:S(2)}, u32[]{:S(2)}) collective-permute-start(bf16[4,176,512]{2,1,0:T(8,128)(2,1)S(1)} %all_gather.32.here_ref), channel_id=1, source_target_pairs={{0,2},{1,3},{2,0},{3,1},{4,6},{5,7},{6,4},{7,5},{8,10},{9,11},{10,... | collective-permute-start | bytes 2162696 | tf_op jit(solution)/shard_map/ppermute | solution.py:360
  162.9 35.4 %collective-permute-start.26 = (bf16[4,80,512]{2,1,0:T(8,128)(2,1)S(1)}, bf16[4,80,512]{2,1,0:T(8,128)(2,1)S(1)}, u32[]{:S(2)}, u32[]{:S(2)}) collective-permute-start(bf16[4,80,512]{2,1,0:T(8,128)(2,1)S(1)} %slice.169), channel_id=1, source_target_pairs={{0,16},{16,0},{1,17},{17,1},{2,18},{18,2},{3,19},{19,3},{4,20},{20... | collective-permute-start | bytes 983048 | tf_op jit(solution)/shard_map/ppermute | solution.py:363
  163.8 34.9 %collective-permute-start.27 = (bf16[4,80,512]{2,1,0:T(8,128)(2,1)}, bf16[4,80,512]{2,1,0:T(8,128)(2,1)S(1)}, u32[]{:S(2)}, u32[]{:S(2)}) collective-permute-start(bf16[4,80,512]{2,1,0:T(8,128)(2,1)} %slice.170), channel_id=1, source_target_pairs={{0,16},{16,0},{1,17},{17,1},{2,18},{18,2},{3,19},{19,3},{4,20},{20... | collective-permute-start | bytes 983048 | tf_op jit(solution)/shard_map/ppermute | solution.py:363
  180.3 26.7 %collective-permute-start.23 = (bf16[4,80,512]{2,1,0:T(8,128)(2,1)}, bf16[4,80,512]{2,1,0:T(8,128)(2,1)S(1)}, u32[]{:S(2)}, u32[]{:S(2)}) collective-permute-start(bf16[4,80,512]{2,1,0:T(8,128)(2,1)} %slice.165), channel_id=1, source_target_pairs={{0,16},{16,0},{1,17},{17,1},{2,18},{18,2},{3,19},{19,3},{4,20},{20... | collective-permute-start | bytes 983048 | tf_op jit(solution)/shard_map/ppermute | solution.py:363
  181.6 26.1 %collective-permute-start.24 = (bf16[4,80,512]{2,1,0:T(8,128)(2,1)}, bf16[4,80,512]{2,1,0:T(8,128)(2,1)S(1)}, u32[]{:S(2)}, u32[]{:S(2)}) collective-permute-start(bf16[4,80,512]{2,1,0:T(8,128)(2,1)} %slice.166), channel_id=1, source_target_pairs={{0,16},{16,0},{1,17},{17,1},{2,18},{18,2},{3,19},{19,3},{4,20},{20... | collective-permute-start | bytes 983048 | tf_op jit(solution)/shard_map/ppermute | solution.py:363
  198.4 26.0 %collective-permute-start.17 = (bf16[4,80,512]{2,1,0:T(8,128)(2,1)S(1)}, bf16[4,80,512]{2,1,0:T(8,128)(2,1)S(1)}, u32[]{:S(2)}, u32[]{:S(2)}) collective-permute-start(bf16[4,80,512]{2,1,0:T(8,128)(2,1)S(1)} %slice.157), channel_id=1, source_target_pairs={{0,16},{16,0},{1,17},{17,1},{2,18},{18,2},{3,19},{19,3},{4,20},{20... | collective-permute-start | bytes 983048 | tf_op jit(solution)/shard_map/ppermute | solution.py:363
  207.0 30.7 %collective-permute-start.14 = (bf16[4,80,512]{2,1,0:T(8,128)(2,1)S(1)}, bf16[4,80,512]{2,1,0:T(8,128)(2,1)S(1)}, u32[]{:S(2)}, u32[]{:S(2)}) collective-permute-start(bf16[4,80,512]{2,1,0:T(8,128)(2,1)S(1)} %slice.153), channel_id=1, source_target_pairs={{0,16},{16,0},{1,17},{17,1},{2,18},{18,2},{3,19},{19,3},{4,20},{20... | collective-permute-start | bytes 983048 | tf_op jit(solution)/shard_map/ppermute | solution.py:363
  215.6 35.6 %collective-permute-start.11 = (bf16[4,80,512]{2,1,0:T(8,128)(2,1)S(1)}, bf16[4,80,512]{2,1,0:T(8,128)(2,1)S(1)}, u32[]{:S(2)}, u32[]{:S(2)}) collective-permute-start(bf16[4,80,512]{2,1,0:T(8,128)(2,1)S(1)} %slice.149), channel_id=1, source_target_pairs={{0,16},{16,0},{1,17},{17,1},{2,18},{18,2},{3,19},{19,3},{4,20},{20... | collective-permute-start | bytes 983048 | tf_op jit(solution)/shard_map/ppermute | solution.py:363
  224.4 39.9 %collective-permute-start.8 = (bf16[4,80,256]{2,1,0:T(8,128)(2,1)S(1)}, bf16[4,80,256]{2,1,0:T(8,128)(2,1)S(1)}, u32[]{:S(2)}, u32[]{:S(2)}) collective-permute-start(bf16[4,80,256]{2,1,0:T(8,128)(2,1)S(1)} %copy-done.40), channel_id=1, source_target_pairs={{0,16},{16,0},{1,17},{17,1},{2,18},{18,2},{3,19},{19,3},{4,20},{20... | collective-permute-start | bytes 491528 | tf_op jit(solution)/shard_map/ppermute | solution.py:363
  225.2 26.8 %collective-permute-start.12 = (bf16[4,80,512]{2,1,0:T(8,128)(2,1)S(1)}, bf16[4,80,512]{2,1,0:T(8,128)(2,1)S(1)}, u32[]{:S(2)}, u32[]{:S(2)}) collective-permute-start(bf16[4,80,512]{2,1,0:T(8,128)(2,1)S(1)} %slice.150), channel_id=1, source_target_pairs={{0,16},{16,0},{1,17},{17,1},{2,18},{18,2},{3,19},{19,3},{4,20},{20... | collective-permute-start | bytes 983048 | tf_op jit(solution)/shard_map/ppermute | solution.py:363
  237.7 37.9 %collective-permute-start.5 = (bf16[4,80,256]{2,1,0:T(8,128)(2,1)S(1)}, bf16[4,80,256]{2,1,0:T(8,128)(2,1)S(1)}, u32[]{:S(2)}, u32[]{:S(2)}) collective-permute-start(bf16[4,80,256]{2,1,0:T(8,128)(2,1)S(1)} %copy-done.38), channel_id=1, source_target_pairs={{0,16},{16,0},{1,17},{17,1},{2,18},{18,2},{3,19},{19,3},{4,20},{20... | collective-permute-start | bytes 491528 | tf_op jit(solution)/shard_map/ppermute | solution.py:363
  238.5 25.8 %collective-permute-start.9 = (bf16[4,80,256]{2,1,0:T(8,128)(2,1)S(1)}, bf16[4,80,256]{2,1,0:T(8,128)(2,1)S(1)}, u32[]{:S(2)}, u32[]{:S(2)}) collective-permute-start(bf16[4,80,256]{2,1,0:T(8,128)(2,1)S(1)} %copy-done.39), channel_id=1, source_target_pairs={{0,16},{16,0},{1,17},{17,1},{2,18},{18,2},{3,19},{19,3},{4,20},{20... | collective-permute-start | bytes 491528 | tf_op jit(solution)/shard_map/ppermute | solution.py:363
  290.7 39.9 %collective-permute-start.34 = (bf16[2,6,64,1024]{3,2,1,0:T(8,128)(2,1)}, bf16[2,6,64,1024]{3,2,1,0:T(8,128)(2,1)S(1)}, u32[]{:S(2)}, u32[]{:S(2)}) collective-permute-start(bf16[2,6,64,1024]{3,2,1,0:T(8,128)(2,1)} %pack.1), channel_id=1, source_target_pairs={{0,1},{1,0},{2,3},{3,2},{4,5},{5,4},{6,7},{7,6},{8,9},{9,8},{10,11... | collective-permute-start | bytes 4718600 | tf_op jit(solution)/shard_map/ppermute | solution.py:357
  (61 other events, 1210.2 us)

commit v3 on v2

--- a/solution.py
+++ b/solution.py
@@ -116,37 +116,44 @@
 
 
 def chunk_kernel(
-    member, per_block, seq, sub, own, first, opens,
-    low_ref, high_ref, sorted_ref, place_ref, lifted_ref, g_ref, here_ref, there_ref,
-    here_x_ref, there_x_ref, *refs,
+    member, per_block, seq, sub, first, opens, parts,
+    low_ref, high_ref, sorted_ref, place_ref, lifted_ref, g_ref, *refs,
 ):
+    pieces, refs = refs[: 6 * parts], refs[6 * parts :]
     if first:
         out_ref, back_ref, weights_ref, sems = refs
     else:
         out_in, back_in, out_ref, back_ref, weights_ref, sems = refs
     j = pl.program_id(0)
-    _, _, depth2, hidden_units = weights_ref.shape
-    lines = weights_ref.shape[0]
+    lines, _, depth2, hidden_units = weights_ref.shape
     depth = depth2 // 2
-    common = here_ref.shape[1] - own
 
     @pl.when(j == 0)
     def _():
-        x, y = place_ref[0], place_ref[1]
-        mine = pl.multiple_of(x * (depth2 - own), 16)
-        others = pl.multiple_of((1 - x) * (depth2 - own), 16)
+        x, y, z = place_ref[0], place_ref[1], place_ref[2]
+        mine = pl.multiple_of(x * depth, depth)
+        others = pl.multiple_of((1 - x) * depth, depth)
         copies = []
-        for line, ref, x_ref in ((y, here_ref, here_x_ref), (1 - y, there_ref, there_x_ref)):
-            for src, at, size in (
-                (ref.at[:, pl.ds(0, own)], mine, own),
-                (ref.at[:, pl.ds(own, common)], own, common),
-                (x_ref, others, own),
-            ):
-                copies.append(
-                    pltpu.make_async_copy(
-                        src, weights_ref.at[:, line, pl.ds(at, size)], sems.at[len(copies)]
-                    )
+
+        def put(src, to_z, to_y, at, size, cols):
+            copies.append(
+                pltpu.make_async_copy(
+                    src, weights_ref.at[to_z, to_y, pl.ds(at, size), cols], sems.at[len(copies)]
                 )
+            )
+
+        for part in range(parts):
+            own, own_y, here, there, here_x, there_x = pieces[6 * part : 6 * part + 6]
+            units = hidden_units // parts
+            cols = pl.ds(part * units, units)
+            put(own, z, y, 0, depth2, cols)
+            put(own_y, z, 1 - y, 0, depth2, cols)
+            for d in range(1, lines):
+                from_z = lax.rem(z + lines - d, lines)
+                put(here.at[d - 1], from_z, y, mine, depth, cols)
+                put(there.at[d - 1], from_z, 1 - y, mine, depth, cols)
+                put(here_x.at[d - 1], from_z, y, others, depth, cols)
+                put(there_x.at[d - 1], from_z, 1 - y, others, depth, cols)
         for copy in copies:
             copy.start()
         for copy in copies:
@@ -194,7 +201,7 @@
             out_ref[...] = weight * out_sum
             back_ref[...] = weight * back_sum
         elif opens:
-            old = (sorted_ref[at * per_block] < member)
+            old = sorted_ref[at * per_block] < member
             out_ref[...] = jnp.where(old, out_in[...], 0.0) + weight * out_sum
             back_ref[...] = jnp.where(old, back_in[...], 0.0) + weight * back_sum
         else:
@@ -204,9 +211,10 @@
 
 def chunk(member, opens, per_block, seq, scalars, lifted, g, pieces, sums):
     tokens, width = lifted.shape
-    lines, rows, hidden = pieces[0].shape
-    own = pieces[2].shape[1]
-    depth2 = 2 * own + (rows - own)
+    parts = len(pieces)
+    depth2, units = pieces[0][0].shape
+    lines = pieces[0][2].shape[0] + 1
+    hidden = parts * units
     size = per_block * seq
     first = sums is None
     tok = pl.BlockSpec(
@@ -217,15 +225,17 @@
     )
     hbm = pl.BlockSpec(memory_space=pl.ANY)
     sub = math.gcd(hidden, 512)
-    args = [*scalars, lifted, g, *pieces]
-    specs = [tok, tok, hbm, hbm, hbm, hbm]
+    args = [*scalars, lifted, g]
+    for part in pieces:
+        args += part
+    specs = [tok, tok] + [hbm] * (6 * parts)
     alias = {}
     if not first:
         alias = {len(args): 0, len(args) + 1: 1}
         args += list(sums)
         specs += [tok, tok]
     return pl.pallas_call(
-        functools.partial(chunk_kernel, member, per_block, seq, sub, own, first, opens),
+        functools.partial(chunk_kernel, member, per_block, seq, sub, first, opens, parts),
         grid_spec=pltpu.PrefetchScalarGridSpec(
             num_scalar_prefetch=4,
             grid=(tokens // size,),
@@ -233,7 +243,7 @@
             out_specs=[tok, tok],
             scratch_shapes=[
                 pltpu.VMEM((lines, 2, depth2, hidden), BF16),
-                pltpu.SemaphoreType.DMA((6,)),
+                pltpu.SemaphoreType.DMA((parts * (4 * lines - 2),)),
             ],
         ),
         out_shape=[jax.ShapeDtypeStruct((tokens, width), F32)] * 2,
@@ -333,17 +343,6 @@
     )(pos_own, member_own, x, g, gain, out_sum, back_sum, other)
 
 
-def chunk_sizes(half, members):
-    unit = half // 8
-    if unit % 128:
-        return [[half]] * members
-    small = [unit, unit, 2 * unit, 2 * unit, 2 * unit]
-    plan = [[2 * unit] * 4 for _ in range(members)]
-    plan[0] = small
-    plan[-1] = small[::-1]
-    return plan
-
-
 def on_device_pairs(ranks, tokens_in, upstream, member_pick, norm_gain, up_proj, down_proj):
     rows, seq, width = tokens_in.shape
     members, depth, hidden = up_proj.shape
@@ -362,7 +361,11 @@
     def over_x(a):
         return lax.ppermute(a, "grp", [(0, 1), (1, 0)])
 
-    lines = [list(range(i, ranks, 4)) for i in range(4)]
+    def shift_z(a, d):
+        return lax.ppermute(a, "row", [(i, (i + 4 * d) % ranks) for i in range(ranks)])
+
+    def after(a, *others):
+        return lax.optimization_barrier((a, *others))[0]
 
     both = jnp.stack([up_proj, down_proj], axis=1)
     mine = lax.dynamic_slice_in_dim(both, core * half, half, 3)
@@ -371,15 +374,7 @@
     shard = jnp.concatenate(
         [jnp.where(even, mine, theirs), jnp.where(even, theirs, mine)], axis=2
     ).reshape(members, 4 * depth, half)
-    own = 5 * depth // 4
-    piece_all = jnp.concatenate(
-        [
-            jnp.where(x_at == 0, shard[:, :own], shard[:, 4 * depth - own :]),
-            shard[:, own : 4 * depth - own],
-        ],
-        axis=1,
-    )
-
+    along = jnp.where(x_at == 0, shard[:, : 2 * depth], shard[:, 2 * depth :])
     pick_own = member_pick[:, 0]
     pick_pair = jnp.concatenate([pick_own, partner(pick_own)])
     x_pair = jnp.concatenate([tokens_in, partner(tokens_in)])
@@ -395,27 +390,44 @@
     per_block = math.gcd(2 * rows, 4)
     labels = jnp.arange(members, dtype=jnp.int32)[:, None]
     start = jnp.sum((pick_pair[None, :] < labels).astype(jnp.int32), axis=1)
-    count = jnp.sum((pick_pair[None, :] == labels).astype(jnp.int32), axis=1)
+    end = jnp.sum((pick_pair[None, :] <= labels).astype(jnp.int32), axis=1)
     low = jnp.minimum(start, 2 * rows - 1) // per_block
-    high = jnp.where(count > 0, (start + count - 1) // per_block, low - 1)
+    high = jnp.where(end > start, (end - 1) // per_block, low - 1)
 
     lifted, g_sorted = prep(perm, member_sorted, x_pair, g_pair, norm_gain)
     lifted = lifted.reshape(2 * rows * seq, width)
     g_sorted = g_sorted.reshape(2 * rows * seq, width)
-    scalars = (low, high, member_sorted, jnp.stack([x_at, y_at]))
-
+    scalars = (low, high, member_sorted, jnp.stack([x_at, y_at, rank // 4]))
+
+    count = 4
+    size = half // count
     sums = None
-    for member, sizes in enumerate(chunk_sizes(half, members)):
-        for part, size in enumerate(sizes):
-            first_unit = sum(sizes[:part])
-            piece = piece_all[member, :, first_unit : first_unit + size]
-            here = lax.all_gather(piece, "row", axis_index_groups=lines)
+    pieces, y_done = [], []
+    for member in range(members):
+        for part in range(count):
+            cols = slice(part * size, (part + 1) * size)
+            own, mine = shard[member, :, cols], along[member, :, cols]
+            at = len(pieces)
+            if at >= 2:
+                mine = after(mine, pieces[at - 2][2])
+            if at >= 3:
+                mine = after(mine, y_done[at - 3])
+            own_y = over_y(own)
+            here = jnp.stack([shift_z(mine, d) for d in range(1, ranks // 4)])
+            here_x = over_x(here)
             there = over_y(here)
-            here_x = over_x(here[:, :own])
-            there_x = over_x(there[:, :own])
-            pieces = (here, there, here_x, there_x)
+            if at == members * count - 3:
+                there_x = over_y(here_x)
+            else:
+                there_x = over_x(there)
+            y_done.append(there)
+            pieces.append((own, own_y, here, there, here_x, there_x))
+    for member in range(members):
+        for part in range(0, count, 2):
+            at = member * count + part
             sums = chunk(
-                member, part == 0, per_block, seq, scalars, lifted, g_sorted, pieces, sums
+                member, part == 0, per_block, seq, scalars, lifted, g_sorted,
+                pieces[at : at + 2], sums,
             )
     other = partner(pack(pos[rows:], sums[0], sums[1], rows, seq))
     return tuple(

time: 332 us -> 265 us (0.80)
  the two profiles are of different devices: /device:TPU:25 before, /device:TPU:8 now
where the time goes in v3:
time: 265 us; the launch traced here: 261 us
  waiting for transfers between devices  97.9 us (37%)
  starting transfers between devices  80.4 us (30%)
  Pallas kernels  60.8 us (23%)
  other arithmetic  14.1 us (5%)
  local copies, waits for them, and re-layouts  6.27 us (2%)
    pallas_call x4, Pallas kernels, chunk(): pl.pallas_call(functools.partial(chunk_kernel, member, per_block, seq, su...  46.1 us
    ppermute x24, starting transfers between devices, shift_z(): lax.ppermute(a, 'row', [(i, (i + 4 * d) % ranks) for i in range(ranks)])  41.8 us
    ppermute x15, waiting for transfers between devices, over_x(): return lax.ppermute(a, 'grp', [(0, 1), (1, 0)])  39.5 us
    ppermute x24, waiting for transfers between devices, shift_z(): lax.ppermute(a, 'row', [(i, (i + 4 * d) % ranks) for i in range(ranks)])  27.1 us
    ppermute x17, waiting for transfers between devices, over_y(): return lax.ppermute(a, 'row', [(i, i ^ 2) for i in range(ranks)])  24 us
    ppermute x17, starting transfers between devices, over_y(): return lax.ppermute(a, 'row', [(i, i ^ 2) for i in range(ranks)])  21.3 us
    ppermute x15, starting transfers between devices, over_x(): return lax.ppermute(a, 'grp', [(0, 1), (1, 0)])  16.7 us
    ppermute x5, waiting for transfers between devices, partner(): return lax.ppermute(a, 'row', [(i, i ^ 1) for i in range(ranks)])  7.23 us
  transfers between devices with their start and end apart: 61, of which 29 were waited for; matrix products, arithmetic and copies ran while one was open for 5% of the time, Pallas kernels for 15%

profile of v3, /device:TPU:8, one launch (start us, length us, event | category | flops | bytes accessed | tf_op | source)
XLA Modules:
  0.0 260.8 jit_solution(15153552177174257809)
XLA Ops:
  3.7 3.6 %collective-permute-done.3 = bf16[2,2,64,2048]{3,2,0,1:T(8,128)(2,1)} collective-permute-done((bf16[2,2,64,2048]{3,2,0,1:T(8,128)(2,1)}, bf16[2,2,64,2048]{3,2,0,1:T(8,128)(2,1)}, u32[]{:S(2)}, u32[]{:S(2)}) %collective-permute-start.3) | collective-permute-done | bytes 1048608 | tf_op jit(solution)/shard_map/ppermute | solution.py:356
  15.1 6.3 %collective-permute-done.5 = bf16[128,512]{1,0:T(8,128)(2,1)S(1)} collective-permute-done((bf16[128,512]{1,0:T(8,128)(2,1)S(1)}, bf16[128,512]{1,0:T(8,128)(2,1)S(1)}, u32[]{:S(2)}, u32[]{:S(2)}) %collective-permute-start.5) | collective-permute-done | bytes 131104 | tf_op jit(solution)/shard_map/ppermute | solution.py:365
  24.4 3.7 %collective-permute-start.12 = (bf16[128,512]{1,0:T(8,128)(2,1)S(1)}, bf16[128,512]{1,0:T(8,128)(2,1)S(1)}, u32[]{:S(2)}, u32[]{:S(2)}) collective-permute-start(bf16[128,512]{1,0:T(8,128)(2,1)S(1)} %get-tuple-element.64), channel_id=1, source_target_pairs={{0,8},{1,9},{2,10},{3,11},{4,12},{5,13},{6,14},{7,15},{8,0},{9,1},... | collective-permute-start | bytes 393224 | tf_op jit(solution)/shard_map/ppermute | solution.py:365
  29.7 3.5 %collective-permute-done.11 = bf16[128,512]{1,0:T(8,128)(2,1)S(1)} collective-permute-done((bf16[128,512]{1,0:T(8,128)(2,1)S(1)}, bf16[128,512]{1,0:T(8,128)(2,1)S(1)}, u32[]{:S(2)}, u32[]{:S(2)}) %collective-permute-start.11) | collective-permute-done | bytes 131104 | tf_op jit(solution)/shard_map/ppermute | solution.py:365
  45.0 3.7 %collective-permute-done.9 = bf16[128,512]{1,0:T(8,128)(2,1)S(1)} collective-permute-done((bf16[128,512]{1,0:T(8,128)(2,1)S(1)}, bf16[128,512]{1,0:T(8,128)(2,1)S(1)}, u32[]{:S(2)}, u32[]{:S(2)}) %collective-permute-start.9) | collective-permute-done | bytes 131104 | tf_op jit(solution)/shard_map/ppermute | solution.py:365
  62.6 4.1 %collective-permute-done.57.refs_7_ = bf16[256,512]{1,0:T(8,128)(2,1)} collective-permute-done((bf16[256,512]{1,0:T(8,128)(2,1)S(1)}, bf16[256,512]{1,0:T(8,128)(2,1)}, u32[]{:S(2)}, u32[]{:S(2)}) %collective-permute-start.57) | collective-permute-done | bytes 262176 | tf_op jit(solution)/shard_map/ppermute | solution.py:359
  73.0 4.9 %collective-permute-done.51.refs_7_ = bf16[256,512]{1,0:T(8,128)(2,1)} collective-permute-done((bf16[256,512]{1,0:T(8,128)(2,1)S(1)}, bf16[256,512]{1,0:T(8,128)(2,1)}, u32[]{:S(2)}, u32[]{:S(2)}) %collective-permute-start.51) | collective-permute-done | bytes 262176 | tf_op jit(solution)/shard_map/ppermute | solution.py:359
  89.0 3.9 %collective-permute-done.21 = bf16[128,512]{1,0:T(8,128)(2,1)S(1)} collective-permute-done((bf16[128,512]{1,0:T(8,128)(2,1)}, bf16[128,512]{1,0:T(8,128)(2,1)S(1)}, u32[]{:S(2)}, u32[]{:S(2)}) %collective-permute-start.21) | collective-permute-done | bytes 131104 | tf_op jit(solution)/shard_map/ppermute | solution.py:365
  97.8 3.5 %collective-permute-start.32 = (bf16[128,512]{1,0:T(8,128)(2,1)S(1)}, bf16[128,512]{1,0:T(8,128)(2,1)S(1)}, u32[]{:S(2)}, u32[]{:S(2)}) collective-permute-start(bf16[128,512]{1,0:T(8,128)(2,1)S(1)} %copy-done.21), channel_id=1, source_target_pairs={{0,8},{1,9},{2,10},{3,11},{4,12},{5,13},{6,14},{7,15},{8,0},{9,1},... | collective-permute-start | bytes 393224 | tf_op jit(solution)/shard_map/ppermute | solution.py:365
  113.1 6.6 %collective-permute-done.22.refs_9_ = bf16[3,128,512]{2,1,0:T(8,128)(2,1)S(1)} collective-permute-done((bf16[3,128,512]{2,1,0:T(8,128)(2,1)S(1)}, bf16[3,128,512]{2,1,0:T(8,128)(2,1)S(1)}, u32[]{:S(2)}, u32[]{:S(2)}) %collective-permute-start.22) | collective-permute-done | bytes 393248 | tf_op jit(solution)/shard_map/ppermute | solution.py:359
  129.2 4.4 %collective-permute-done.59.refs_11_ = bf16[3,128,512]{2,1,0:T(8,128)(2,1)S(1)} collective-permute-done((bf16[3,128,512]{2,1,0:T(8,128)(2,1)S(1)}, bf16[3,128,512]{2,1,0:T(8,128)(2,1)S(1)}, u32[]{:S(2)}, u32[]{:S(2)}) %collective-permute-start.59) | collective-permute-done | bytes 393248 | tf_op jit(solution)/shard_map/ppermute | solution.py:362
  143.5 5.3 %prep.1 = (bf16[12,64,1024]{2,1,0:T(8,128)(2,1)}, bf16[12,64,1024]{2,1,0:T(8,128)(2,1)}) custom-call(s32[12]{0:T(128)} %get-tuple-element.45.perm_ref, s32[12]{0:T(128)} %get-tuple-element.46.sorted_ref, bf16[12,64,1024]{2,1,0:T(8,128)(2,1)} %pad_maximum_fusion.1.x_ref, bf16[12,64,1024]{2,1,0:T(8,128)(2,1)} %pad_maximum_fusion.2.g_ref, f32[2,1024]{1,0:T(2,128)} %gain_ref.3), custom_call_target="tpu_custom_call" | custom-call | tf_op jit(solution)/shard_map/prep/pallas_call | solution.py:108
  154.5 11.0 %chunk.4 = (f32[768,1024]{1,0:T(8,128)}, f32[768,1024]{1,0:T(8,128)}) custom-call(s32[2]{0:T(128)} %get-tuple-element.50.low_ref, s32[2]{0:T(128)} %get-tuple-element.49.high_ref, s32[12]{0:T(128)} %get-tuple-element.46.sorted_ref, s32[3]{0:T(128)} %pad_add_fusion.1.place_ref, bf16[768,1024]{1,0:T(8,128)(2,1)} %bitcast.97, bf16[768,1024]{1,0:T(8,128)(2,1)} %bitcast.101, ...), custom_call_target="tpu_custom_call" | custom-call | flops 4294967296 | bytes 19922944 | tf_op jit(solution)/shard_map/chunk/pallas_call | solution.py:237
  167.3 10.5 %collective-permute-done.50.refs_5_ = bf16[3,128,512]{2,1,0:T(8,128)(2,1)S(1)} collective-permute-done((bf16[3,128,512]{2,1,0:T(8,128)(2,1)S(1)}, bf16[3,128,512]{2,1,0:T(8,128)(2,1)S(1)}, u32[]{:S(2)}, u32[]{:S(2)}) %collective-permute-start.50) | collective-permute-done | bytes 393248 | tf_op jit(solution)/shard_map/ppermute | solution.py:362
  180.9 5.3 %collective-permute-done.46.refs_10_ = bf16[3,128,512]{2,1,0:T(8,128)(2,1)S(1)} collective-permute-done((bf16[3,128,512]{2,1,0:T(8,128)(2,1)S(1)}, bf16[3,128,512]{2,1,0:T(8,128)(2,1)S(1)}, u32[]{:S(2)}, u32[]{:S(2)}) %collective-permute-start.46) | collective-permute-done | bytes 393248 | tf_op jit(solution)/shard_map/ppermute | solution.py:362
  187.8 5.7 %collective-permute-done.53.refs_11_ = bf16[3,128,512]{2,1,0:T(8,128)(2,1)S(1)} collective-permute-done((bf16[3,128,512]{2,1,0:T(8,128)(2,1)S(1)}, bf16[3,128,512]{2,1,0:T(8,128)(2,1)S(1)}, u32[]{:S(2)}, u32[]{:S(2)}) %collective-permute-start.53) | collective-permute-done | bytes 393248 | tf_op jit(solution)/shard_map/ppermute | solution.py:362
  194.9 11.7 %chunk.5 = (f32[768,1024]{1,0:T(8,128)}, f32[768,1024]{1,0:T(8,128)}) custom-call(s32[2]{0:T(128)} %get-tuple-element.50.low_ref, s32[2]{0:T(128)} %get-tuple-element.49.high_ref, s32[12]{0:T(128)} %get-tuple-element.46.sorted_ref, s32[3]{0:T(128)} %pad_add_fusion.1.place_ref, ...), custom_call_target="tpu_custom_call", output_to_operand_aliasing={{0}: (18, {}), {1}: (19, {})} | custom-call | flops 4294967296 | bytes 19922944 | tf_op jit(solution)/shard_map/chunk/pallas_call | solution.py:237
  211.7 11.7 %chunk.6 = (f32[768,1024]{1,0:T(8,128)}, f32[768,1024]{1,0:T(8,128)}) custom-call(s32[2]{0:T(128)} %get-tuple-element.50.low_ref, s32[2]{0:T(128)} %get-tuple-element.49.high_ref, s32[12]{0:T(128)} %get-tuple-element.46.sorted_ref, s32[3]{0:T(128)} %pad_add_fusion.1.place_ref, ...), custom_call_target="tpu_custom_call", output_to_operand_aliasing={{0}: (18, {}), {1}: (19, {})} | custom-call | flops 4294967296 | bytes 19922944 | tf_op jit(solution)/shard_map/chunk/pallas_call | solution.py:237
  225.5 4.2 %collective-permute-done.40.refs_11_ = bf16[3,128,512]{2,1,0:T(8,128)(2,1)S(1)} collective-permute-done((bf16[3,128,512]{2,1,0:T(8,128)(2,1)S(1)}, bf16[3,128,512]{2,1,0:T(8,128)(2,1)S(1)}, u32[]{:S(2)}, u32[]{:S(2)}) %collective-permute-start.40) | collective-permute-done | bytes 393248 | tf_op jit(solution)/shard_map/ppermute | solution.py:362
  229.7 4.2 %collective-permute-done.28.refs_5_ = bf16[3,128,512]{2,1,0:T(8,128)(2,1)S(1)} collective-permute-done((bf16[3,128,512]{2,1,0:T(8,128)(2,1)S(1)}, bf16[3,128,512]{2,1,0:T(8,128)(2,1)S(1)}, u32[]{:S(2)}, u32[]{:S(2)}) %collective-permute-start.28) | collective-permute-done | bytes 393248 | tf_op jit(solution)/shard_map/ppermute | solution.py:362
  234.6 11.7 %chunk.7 = (f32[768,1024]{1,0:T(8,128)}, f32[768,1024]{1,0:T(8,128)}) custom-call(s32[2]{0:T(128)} %get-tuple-element.50.low_ref, s32[2]{0:T(128)} %get-tuple-element.49.high_ref, s32[12]{0:T(128)} %get-tuple-element.46.sorted_ref, s32[3]{0:T(128)} %pad_add_fusion.1.place_ref, ...), custom_call_target="tpu_custom_call", output_to_operand_aliasing={{0}: (18, {}), {1}: (19, {})} | custom-call | flops 4294967296 | bytes 19922944 | tf_op jit(solution)/shard_map/chunk/pallas_call | solution.py:237
  246.3 3.8 %pack.1 = bf16[2,6,64,1024]{3,2,1,0:T(8,128)(2,1)} custom-call(s32[6]{0:T(128)} %get-tuple-element.69.pos_ref, f32[768,1024]{1,0:T(8,128)} %get-tuple-element.43.out_ref, f32[768,1024]{1,0:T(8,128)} %get-tuple-element.44.back_ref), custom_call_target="tpu_custom_call" | custom-call | tf_op jit(solution)/shard_map/pack/pallas_call | solution.py:279
  250.3 3.6 %collective-permute-done.60.other_ref = bf16[2,6,64,1024]{3,2,1,0:T(8,128)(2,1)S(1)} collective-permute-done((bf16[2,6,64,1024]{3,2,1,0:T(8,128)(2,1)}, bf16[2,6,64,1024]{3,2,1,0:T(8,128)(2,1)S(1)}, u32[]{:S(2)}, u32[]{:S(2)}) %collective-permute-start.60) | collective-permute-done | bytes 1572896 | tf_op jit(solution)/shard_map/ppermute | solution.py:356
  255.1 5.5 %finish.1 = (bf16[6,64,1024]{2,1,0:T(8,128)(2,1)}, bf16[6,64,1024]{2,1,0:T(8,128)(2,1)}, f32[6,64]{1,0:T(8,128)}) custom-call(s32[6]{0:T(128)} %get-tuple-element.70.pos_ref, s32[6]{0:T(128)} %bitcast.94, bf16[6,64,1024]{2,1,0:T(8,128)(2,1)} %x_ref.1, bf16[6,64,1024]{2,1,0:T(8,128)(2,1)} %g_ref.1, f32[2,1024]{1,0:T(2,128)} %gain_ref.3, ...), custom_call_target="tpu_custom_call" | custom-call | tf_op jit(solution)/shard_map/finish/pallas_call | solution.py:328
  (243 shorter events, 116.9 us)
Async XLA Ops:
  3.1 37.2 %collective-permute-start.1 = (bf16[6,64,1024]{2,1,0:T(8,128)(2,1)S(1)}, bf16[6,64,1024]{2,1,0:T(8,128)(2,1)}, u32[]{:S(2)}, u32[]{:S(2)}) collective-permute-start(bf16[6,64,1024]{2,1,0:T(8,128)(2,1)S(1)} %copy-done.2), channel_id=1, source_target_pairs={{0,1},{1,0},{2,3},{3,2},{4,5},{5,4},{6,7},{7,6},{8,9},{9,8},{10,11... | collective-permute-start | bytes 2359304 | tf_op jit(solution)/shard_map/ppermute | solution.py:356
  3.6 38.3 %collective-permute-start.2 = (bf16[6,64,1024]{2,1,0:T(8,128)(2,1)}, bf16[6,64,1024]{2,1,0:T(8,128)(2,1)}, u32[]{:S(2)}, u32[]{:S(2)}) collective-permute-start(bf16[6,64,1024]{2,1,0:T(8,128)(2,1)} %g_ref.1), channel_id=1, source_target_pairs={{0,1},{1,0},{2,3},{3,2},{4,5},{5,4},{6,7},{7,6},{8,9},{9,8},{10,11... | collective-permute-start | bytes 2359304 | tf_op jit(solution)/shard_map/ppermute | solution.py:356
  34.8 18.1 %collective-permute-start.18 = (bf16[3,128,512]{2,1,0:T(8,128)(2,1)S(1)}, bf16[3,128,512]{2,1,0:T(8,128)(2,1)S(1)}, u32[]{:S(2)}, u32[]{:S(2)}) collective-permute-start(bf16[3,128,512]{2,1,0:T(8,128)(2,1)S(1)} %pad_maximum_fusion.3.refs_2_), channel_id=1, source_target_pairs={{0,2},{1,3},{2,0},{3,1},{4,6},{5,7},{6,4},{7,5},{8,10},{9,11},{10,... | collective-permute-start | bytes 1179656 | tf_op jit(solution)/shard_map/ppermute | solution.py:359
  51.7 20.5 %collective-permute-start.48 = (bf16[256,512]{1,0:T(8,128)(2,1)S(1)}, bf16[256,512]{1,0:T(8,128)(2,1)}, u32[]{:S(2)}, u32[]{:S(2)}) collective-permute-start(bf16[256,512]{1,0:T(8,128)(2,1)S(1)} %get-tuple-element.56.refs_0_), channel_id=1, source_target_pairs={{0,2},{1,3},{2,0},{3,1},{4,6},{5,7},{6,4},{7,5},{8,10},{9,11},{10,... | collective-permute-start | bytes 786440 | tf_op jit(solution)/shard_map/ppermute | solution.py:359
  52.9 25.0 %collective-permute-start.51 = (bf16[256,512]{1,0:T(8,128)(2,1)S(1)}, bf16[256,512]{1,0:T(8,128)(2,1)}, u32[]{:S(2)}, u32[]{:S(2)}) collective-permute-start(bf16[256,512]{1,0:T(8,128)(2,1)S(1)} %get-tuple-element.55.refs_6_), channel_id=1, source_target_pairs={{0,2},{1,3},{2,0},{3,1},{4,6},{5,7},{6,4},{7,5},{8,10},{9,11},{10,... | collective-permute-start | bytes 786440 | tf_op jit(solution)/shard_map/ppermute | solution.py:359
  56.1 25.2 %collective-permute-start.19 = (bf16[128,512]{1,0:T(8,128)(2,1)}, bf16[128,512]{1,0:T(8,128)(2,1)}, u32[]{:S(2)}, u32[]{:S(2)}) collective-permute-start(bf16[128,512]{1,0:T(8,128)(2,1)} %get-tuple-element.31), channel_id=1, source_target_pairs={{0,4},{1,5},{2,6},{3,7},{4,8},{5,9},{6,10},{7,11},{8,12},{9,13},{1... | collective-permute-start | bytes 393224 | tf_op jit(solution)/shard_map/ppermute | solution.py:365
  61.0 33.4 %collective-permute-start.30 = (bf16[3,128,512]{2,1,0:T(8,128)(2,1)S(1)}, bf16[3,128,512]{2,1,0:T(8,128)(2,1)S(1)}, u32[]{:S(2)}, u32[]{:S(2)}) collective-permute-start(bf16[3,128,512]{2,1,0:T(8,128)(2,1)S(1)} %pad_maximum_fusion.4.refs_2_), channel_id=1, source_target_pairs={{0,2},{1,3},{2,0},{3,1},{4,6},{5,7},{6,4},{7,5},{8,10},{9,11},{10,... | collective-permute-start | bytes 1179656 | tf_op jit(solution)/shard_map/ppermute | solution.py:359
  104.7 20.3 %collective-permute-start.55 = (bf16[3,128,512]{2,1,0:T(8,128)(2,1)S(1)}, bf16[3,128,512]{2,1,0:T(8,128)(2,1)S(1)}, u32[]{:S(2)}, u32[]{:S(2)}) collective-permute-start(bf16[3,128,512]{2,1,0:T(8,128)(2,1)S(1)} %pad_maximum_fusion.3.refs_2_), channel_id=1, source_target_pairs={{0,16},{16,0},{1,17},{17,1},{2,18},{18,2},{3,19},{19,3},{4,20},{20... | collective-permute-start | bytes 1179656 | tf_op jit(solution)/shard_map/ppermute | solution.py:362
  106.2 20.0 %collective-permute-start.49 = (bf16[3,128,512]{2,1,0:T(8,128)(2,1)S(1)}, bf16[3,128,512]{2,1,0:T(8,128)(2,1)S(1)}, u32[]{:S(2)}, u32[]{:S(2)}) collective-permute-start(bf16[3,128,512]{2,1,0:T(8,128)(2,1)S(1)} %pad_maximum_fusion.4.refs_2_), channel_id=1, source_target_pairs={{0,16},{16,0},{1,17},{17,1},{2,18},{18,2},{3,19},{19,3},{4,20},{20... | collective-permute-start | bytes 1179656 | tf_op jit(solution)/shard_map/ppermute | solution.py:362
  106.8 26.8 %collective-permute-start.59 = (bf16[3,128,512]{2,1,0:T(8,128)(2,1)S(1)}, bf16[3,128,512]{2,1,0:T(8,128)(2,1)S(1)}, u32[]{:S(2)}, u32[]{:S(2)}) collective-permute-start(bf16[3,128,512]{2,1,0:T(8,128)(2,1)S(1)} %copy-done.29), channel_id=1, source_target_pairs={{0,16},{16,0},{1,17},{17,1},{2,18},{18,2},{3,19},{19,3},{4,20},{20... | collective-permute-start | bytes 1179656 | tf_op jit(solution)/shard_map/ppermute | solution.py:362
  109.9 28.1 %collective-permute-start.56 = (bf16[3,128,512]{2,1,0:T(8,128)(2,1)S(1)}, bf16[3,128,512]{2,1,0:T(8,128)(2,1)S(1)}, u32[]{:S(2)}, u32[]{:S(2)}) collective-permute-start(bf16[3,128,512]{2,1,0:T(8,128)(2,1)S(1)} %copy-done.27), channel_id=1, source_target_pairs={{0,16},{16,0},{1,17},{17,1},{2,18},{18,2},{3,19},{19,3},{4,20},{20... | collective-permute-start | bytes 1179656 | tf_op jit(solution)/shard_map/ppermute | solution.py:362
  120.4 20.3 %collective-permute-start.35 = (bf16[128,512]{1,0:T(8,128)(2,1)S(1)}, bf16[128,512]{1,0:T(8,128)(2,1)S(1)}, u32[]{:S(2)}, u32[]{:S(2)}) collective-permute-start(bf16[128,512]{1,0:T(8,128)(2,1)S(1)} %copy-done.20), channel_id=1, source_target_pairs={{0,4},{1,5},{2,6},{3,7},{4,8},{5,9},{6,10},{7,11},{8,12},{9,13},{1... | collective-permute-start | bytes 393224 | tf_op jit(solution)/shard_map/ppermute | solution.py:365
  125.0 23.8 %collective-permute-start.36 = (bf16[128,512]{1,0:T(8,128)(2,1)S(1)}, bf16[128,512]{1,0:T(8,128)(2,1)S(1)}, u32[]{:S(2)}, u32[]{:S(2)}) collective-permute-start(bf16[128,512]{1,0:T(8,128)(2,1)S(1)} %copy-done.20), channel_id=1, source_target_pairs={{0,8},{1,9},{2,10},{3,11},{4,12},{5,13},{6,14},{7,15},{8,0},{9,1},... | collective-permute-start | bytes 393224 | tf_op jit(solution)/shard_map/ppermute | solution.py:365
  126.3 24.2 %collective-permute-start.37 = (bf16[128,512]{1,0:T(8,128)(2,1)S(1)}, bf16[128,512]{1,0:T(8,128)(2,1)S(1)}, u32[]{:S(2)}, u32[]{:S(2)}) collective-permute-start(bf16[128,512]{1,0:T(8,128)(2,1)S(1)} %copy-done.20), channel_id=1, source_target_pairs={{0,12},{1,13},{2,14},{3,15},{4,0},{5,1},{6,2},{7,3},{8,4},{9,5},{1... | collective-permute-start | bytes 393224 | tf_op jit(solution)/shard_map/ppermute | solution.py:365
  150.5 28.9 %collective-permute-start.42 = (bf16[3,128,512]{2,1,0:T(8,128)(2,1)S(1)}, bf16[3,128,512]{2,1,0:T(8,128)(2,1)S(1)}, u32[]{:S(2)}, u32[]{:S(2)}) collective-permute-start(bf16[3,128,512]{2,1,0:T(8,128)(2,1)S(1)} %pad_maximum_fusion.6.refs_2_), channel_id=1, source_target_pairs={{0,16},{16,0},{1,17},{17,1},{2,18},{18,2},{3,19},{19,3},{4,20},{20... | collective-permute-start | bytes 1179656 | tf_op jit(solution)/shard_map/ppermute | solution.py:362
  150.9 26.9 %collective-permute-start.50 = (bf16[3,128,512]{2,1,0:T(8,128)(2,1)S(1)}, bf16[3,128,512]{2,1,0:T(8,128)(2,1)S(1)}, u32[]{:S(2)}, u32[]{:S(2)}) collective-permute-start(bf16[3,128,512]{2,1,0:T(8,128)(2,1)S(1)} %collective-permute-done.30.refs_3_), channel_id=1, source_target_pairs={{0,16},{16,0},{1,17},{17,1},{2,18},{18,2},{3,19},{19,3},{4,20},{20... | collective-permute-start | bytes 1179656 | tf_op jit(solution)/shard_map/ppermute | solution.py:362
  152.5 33.7 %collective-permute-start.46 = (bf16[3,128,512]{2,1,0:T(8,128)(2,1)S(1)}, bf16[3,128,512]{2,1,0:T(8,128)(2,1)S(1)}, u32[]{:S(2)}, u32[]{:S(2)}) collective-permute-start(bf16[3,128,512]{2,1,0:T(8,128)(2,1)S(1)} %pad_maximum_fusion.9.refs_8_), channel_id=1, source_target_pairs={{0,16},{16,0},{1,17},{17,1},{2,18},{18,2},{3,19},{19,3},{4,20},{20... | collective-permute-start | bytes 1179656 | tf_op jit(solution)/shard_map/ppermute | solution.py:362
  153.0 40.6 %collective-permute-start.53 = (bf16[3,128,512]{2,1,0:T(8,128)(2,1)S(1)}, bf16[3,128,512]{2,1,0:T(8,128)(2,1)S(1)}, u32[]{:S(2)}, u32[]{:S(2)}) collective-permute-start(bf16[3,128,512]{2,1,0:T(8,128)(2,1)S(1)} %copy-done.36), channel_id=1, source_target_pairs={{0,16},{16,0},{1,17},{17,1},{2,18},{18,2},{3,19},{19,3},{4,20},{20... | collective-permute-start | bytes 1179656 | tf_op jit(solution)/shard_map/ppermute | solution.py:362
  165.7 40.9 %collective-permute-start.45 = (bf16[3,128,512]{2,1,0:T(8,128)(2,1)S(1)}, bf16[3,128,512]{2,1,0:T(8,128)(2,1)S(1)}, u32[]{:S(2)}, u32[]{:S(2)}) collective-permute-start(bf16[3,128,512]{2,1,0:T(8,128)(2,1)S(1)} %pad_maximum_fusion.9.refs_8_), channel_id=1, source_target_pairs={{0,2},{1,3},{2,0},{3,1},{4,6},{5,7},{6,4},{7,5},{8,10},{9,11},{10,... | collective-permute-start | bytes 1179656 | tf_op jit(solution)/shard_map/ppermute | solution.py:359
  177.8 29.7 %collective-permute-start.43 = (bf16[3,128,512]{2,1,0:T(8,128)(2,1)S(1)}, bf16[3,128,512]{2,1,0:T(8,128)(2,1)S(1)}, u32[]{:S(2)}, u32[]{:S(2)}) collective-permute-start(bf16[3,128,512]{2,1,0:T(8,128)(2,1)S(1)} %copy-done.32), channel_id=1, source_target_pairs={{0,16},{16,0},{1,17},{17,1},{2,18},{18,2},{3,19},{19,3},{4,20},{20... | collective-permute-start | bytes 1179656 | tf_op jit(solution)/shard_map/ppermute | solution.py:362
  179.4 30.3 %collective-permute-start.38 = (bf16[3,128,512]{2,1,0:T(8,128)(2,1)S(1)}, bf16[3,128,512]{2,1,0:T(8,128)(2,1)S(1)}, u32[]{:S(2)}, u32[]{:S(2)}) collective-permute-start(bf16[3,128,512]{2,1,0:T(8,128)(2,1)S(1)} %pad_maximum_fusion.10.refs_8_), channel_id=1, source_target_pairs={{0,2},{1,3},{2,0},{3,1},{4,6},{5,7},{6,4},{7,5},{8,10},{9,11},{10,... | collective-permute-start | bytes 1179656 | tf_op jit(solution)/shard_map/ppermute | solution.py:359
  186.2 24.9 %collective-permute-start.26 = (bf16[3,128,512]{2,1,0:T(8,128)(2,1)S(1)}, bf16[3,128,512]{2,1,0:T(8,128)(2,1)S(1)}, u32[]{:S(2)}, u32[]{:S(2)}) collective-permute-start(bf16[3,128,512]{2,1,0:T(8,128)(2,1)S(1)} %pad_maximum_fusion.8.refs_2_), channel_id=1, source_target_pairs={{0,2},{1,3},{2,0},{3,1},{4,6},{5,7},{6,4},{7,5},{8,10},{9,11},{10,... | collective-permute-start | bytes 1179656 | tf_op jit(solution)/shard_map/ppermute | solution.py:359
  209.6 20.0 %collective-permute-start.40 = (bf16[3,128,512]{2,1,0:T(8,128)(2,1)S(1)}, bf16[3,128,512]{2,1,0:T(8,128)(2,1)S(1)}, u32[]{:S(2)}, u32[]{:S(2)}) collective-permute-start(bf16[3,128,512]{2,1,0:T(8,128)(2,1)S(1)} %collective-permute-done.38.refs_9_), channel_id=1, source_target_pairs={{0,16},{16,0},{1,17},{17,1},{2,18},{18,2},{3,19},{19,3},{4,20},{20... | collective-permute-start | bytes 1179656 | tf_op jit(solution)/shard_map/ppermute | solution.py:362
  211.1 22.7 %collective-permute-start.28 = (bf16[3,128,512]{2,1,0:T(8,128)(2,1)S(1)}, bf16[3,128,512]{2,1,0:T(8,128)(2,1)S(1)}, u32[]{:S(2)}, u32[]{:S(2)}) collective-permute-start(bf16[3,128,512]{2,1,0:T(8,128)(2,1)S(1)} %collective-permute-done.26.refs_3_), channel_id=1, source_target_pairs={{0,16},{16,0},{1,17},{17,1},{2,18},{18,2},{3,19},{19,3},{4,20},{20... | collective-permute-start | bytes 1179656 | tf_op jit(solution)/shard_map/ppermute | solution.py:362
  (94 other events, 2279.3 us)

commit v4 on v3

--- a/solution.py
+++ b/solution.py
@@ -116,9 +116,11 @@
 
 
 def chunk_kernel(
-    member, per_block, seq, sub, first, opens, parts,
-    low_ref, high_ref, sorted_ref, place_ref, lifted_ref, g_ref, *refs,
+    member, per_block, seq, kind, units,
+    low_ref, high_ref, sorted_ref, place_ref, perm_ref, lifted_ref, g_ref, *refs,
 ):
+    first, opens, last = kind
+    parts = len(units)
     pieces, refs = refs[: 6 * parts], refs[6 * parts :]
     if first:
         out_ref, back_ref, weights_ref, sems = refs
@@ -127,6 +129,8 @@
     j = pl.program_id(0)
     lines, _, depth2, hidden_units = weights_ref.shape
     depth = depth2 // 2
+    at = j if last else low_ref[member] + j
+    inside = jnp.logical_and(at >= low_ref[member], at <= high_ref[member])
 
     @pl.when(j == 0)
     def _():
@@ -144,8 +148,11 @@
 
         for part in range(parts):
             own, own_y, here, there, here_x, there_x = pieces[6 * part : 6 * part + 6]
-            units = hidden_units // parts
-            cols = pl.ds(part * units, units)
+            cols = pl.ds(sum(units[:part]), units[part])
+            own, own_y = (
+                ref.at[min(member, ref.shape[0] - 1), :, pl.ds(start, units[part])]
+                for ref, start in (own, own_y)
+            )
             put(own, z, y, 0, depth2, cols)
             put(own_y, z, 1 - y, 0, depth2, cols)
             for d in range(1, lines):
@@ -159,16 +166,7 @@
         for copy in copies:
             copy.wait()
 
-    if not first:
-
-        @pl.when(jnp.logical_and(j == 0, high_ref[member] < low_ref[member]))
-        def _():
-            out_ref[...] = out_in[...]
-            back_ref[...] = back_in[...]
-
-    @pl.when(low_ref[member] + j <= high_ref[member])
-    def _():
-        at = low_ref[member] + j
+    def sums():
         width = lifted_ref.shape[1]
         lifted = lifted_ref[...]
         g = g_ref[...]
@@ -179,12 +177,12 @@
             ],
             axis=0,
         )
-        out_sum = jnp.zeros(out_ref.shape, F32)
-        back_sum = jnp.zeros(back_ref.shape, F32)
-        for s in range(hidden_units // sub):
-            cols = slice(s * sub, (s + 1) * sub)
-            up = weights_ref[:, :, :depth, cols].reshape(width, sub)
-            down = weights_ref[:, :, depth:, cols].reshape(width, sub)
+        out_sum = jnp.zeros(lifted.shape, F32)
+        back_sum = jnp.zeros(lifted.shape, F32)
+        bounds = list(range(0, hidden_units, 512)) + [hidden_units]
+        for s, e in zip(bounds[:-1], bounds[1:]):
+            up = weights_ref[:, :, :depth, s:e].reshape(width, e - s)
+            down = weights_ref[:, :, depth:, s:e].reshape(width, e - s)
             v = jnp.dot(lifted, up, preferred_element_type=F32)
             grads = jnp.dot(g, down, preferred_element_type=F32)
             square = v * v
@@ -197,56 +195,115 @@
             dims = (((1,), (1,)), ((), ()))
             out_sum += lax.dot_general(act, down, dims, preferred_element_type=F32)
             back_sum += lax.dot_general(pre, up, dims, preferred_element_type=F32)
+        return weight * out_sum, weight * back_sum
+
+    if last:
+        rows = out_ref.shape[1]
+
+        def store(i, value):
+            for p in range(per_block):
+                row = perm_ref[at * per_block + p]
+                tokens = value[p * seq : (p + 1) * seq]
+
+                @pl.when(row < rows)
+                def _():
+                    out_ref[i, jnp.minimum(row, rows - 1)] = tokens
+
+                @pl.when(row >= rows)
+                def _():
+                    back_ref[i, jnp.maximum(row - rows, 0)] = tokens.astype(BF16)
+
+        @pl.when(inside)
+        def _():
+            out_sum, back_sum = sums()
+            store(0, out_in[...] + out_sum)
+            store(1, back_in[...] + back_sum)
+
+        @pl.when(jnp.logical_not(inside))
+        def _():
+            store(0, out_in[...])
+            store(1, back_in[...])
+
+        return
+
+    if not first:
+
+        @pl.when(jnp.logical_and(j == 0, high_ref[member] < low_ref[member]))
+        def _():
+            out_ref[...] = out_in[...]
+            back_ref[...] = back_in[...]
+
+    @pl.when(inside)
+    def _():
+        out_sum, back_sum = sums()
         if first:
-            out_ref[...] = weight * out_sum
-            back_ref[...] = weight * back_sum
+            out_ref[...] = out_sum
+            back_ref[...] = back_sum
         elif opens:
             old = sorted_ref[at * per_block] < member
-            out_ref[...] = jnp.where(old, out_in[...], 0.0) + weight * out_sum
-            back_ref[...] = jnp.where(old, back_in[...], 0.0) + weight * back_sum
+            out_ref[...] = jnp.where(old, out_in[...], 0.0) + out_sum
+            back_ref[...] = jnp.where(old, back_in[...], 0.0) + back_sum
         else:
-            out_ref[...] = out_in[...] + weight * out_sum
-            back_ref[...] = back_in[...] + weight * back_sum
-
-
-def chunk(member, opens, per_block, seq, scalars, lifted, g, pieces, sums):
+            out_ref[...] = out_in[...] + out_sum
+            back_ref[...] = back_in[...] + back_sum
+
+
+def chunk(member, kind, per_block, seq, scalars, lifted, g, pieces, sums):
+    first, _, last = kind
     tokens, width = lifted.shape
-    parts = len(pieces)
-    depth2, units = pieces[0][0].shape
+    units = [part[2].shape[2] for part in pieces]
+    depth2 = pieces[0][0][0].shape[1]
     lines = pieces[0][2].shape[0] + 1
-    hidden = parts * units
+    hidden = sum(units)
     size = per_block * seq
-    first = sums is None
-    tok = pl.BlockSpec(
-        (size, width),
-        lambda j, low, high, s, p: (
-            jnp.maximum(jnp.minimum(low[member] + j, high[member]), 0), 0
-        ),
-    )
+
+    def block(j, low, high, *_):
+        if last:
+            return j, 0
+        return jnp.maximum(jnp.minimum(low[member] + j, high[member]), 0), 0
+
+    tok = pl.BlockSpec((size, width), block)
     hbm = pl.BlockSpec(memory_space=pl.ANY)
-    sub = math.gcd(hidden, 512)
     args = [*scalars, lifted, g]
-    for part in pieces:
-        args += part
-    specs = [tok, tok] + [hbm] * (6 * parts)
+    starts = []
+    for own, own_y, *rest in pieces:
+        args += [own[0], own_y[0], *rest]
+        starts.append((own[1], own_y[1]))
+    specs = [tok, tok] + [hbm] * (6 * len(pieces))
     alias = {}
+    out_specs = [tok, tok]
+    out_shape = [jax.ShapeDtypeStruct((tokens, width), F32)] * 2
     if not first:
         alias = {len(args): 0, len(args) + 1: 1}
         args += list(sums)
         specs += [tok, tok]
+    if last:
+        alias = {}
+        shape = (2, tokens // (2 * seq), seq, width)
+        out_specs = [pl.BlockSpec(shape, lambda *_: (0, 0, 0, 0))] * 2
+        out_shape = [jax.ShapeDtypeStruct(shape, F32), jax.ShapeDtypeStruct(shape, BF16)]
+
+    def kernel(*refs):
+        refs = list(refs)
+        base = len(scalars) + 2
+        for part, (own, own_y) in enumerate(starts):
+            refs[base + 6 * part] = (refs[base + 6 * part], own)
+            refs[base + 6 * part + 1] = (refs[base + 6 * part + 1], own_y)
+        chunk_kernel(member, per_block, seq, kind, units, *refs)
+
     return pl.pallas_call(
-        functools.partial(chunk_kernel, member, per_block, seq, sub, first, opens, parts),
+        kernel,
         grid_spec=pltpu.PrefetchScalarGridSpec(
-            num_scalar_prefetch=4,
+            num_scalar_prefetch=len(scalars),
             grid=(tokens // size,),
             in_specs=specs,
-            out_specs=[tok, tok],
+            out_specs=out_specs,
             scratch_shapes=[
                 pltpu.VMEM((lines, 2, depth2, hidden), BF16),
-                pltpu.SemaphoreType.DMA((parts * (4 * lines - 2),)),
+                pltpu.SemaphoreType.DMA((len(pieces) * (4 * lines - 2),)),
             ],
         ),
-        out_shape=[jax.ShapeDtypeStruct((tokens, width), F32)] * 2,
+        out_shape=out_shape,
         input_output_aliases=alias,
         compiler_params=pltpu.CompilerParams(vmem_limit_bytes=VMEM_LIMIT),
         cost_estimate=pl.CostEstimate(
@@ -258,89 +315,59 @@
     )(*args)
 
 
-def pack_kernel(pos_ref, out_ref, back_ref, packed_ref, buffer, sems):
-    rows = packed_ref.shape[1]
-    seq = packed_ref.shape[2]
-    copies = []
-    for r in range(rows):
-        at = pl.ds(pl.multiple_of(pos_ref[r] * seq, seq), seq)
-        for i, ref in enumerate((out_ref, back_ref)):
-            copy = pltpu.make_async_copy(ref.at[at], buffer.at[i, r], sems.at[i, r])
-            copy.start()
-            copies.append((copy, i, r))
-    for copy, i, r in copies:
-        copy.wait()
-        packed_ref[i, r] = buffer[i, r].astype(BF16)
-
-
-def pack(pos_partner, out_sum, back_sum, rows, seq):
-    width = out_sum.shape[1]
-    hbm = pl.BlockSpec(memory_space=pl.ANY)
-    return pl.pallas_call(
-        pack_kernel,
-        in_specs=[pl.BlockSpec(memory_space=pltpu.SMEM), hbm, hbm],
-        out_specs=pl.BlockSpec(memory_space=pltpu.VMEM),
-        out_shape=jax.ShapeDtypeStruct((2, rows, seq, width), BF16),
-        scratch_shapes=[
-            pltpu.VMEM((2, rows, seq, width), F32),
-            pltpu.SemaphoreType.DMA((2, rows)),
-        ],
-        compiler_params=pltpu.CompilerParams(vmem_limit_bytes=VMEM_LIMIT),
-        name="pack",
-    )(pos_partner, out_sum, back_sum)
-
-
 def finish_kernel(
-    pos_ref, member_ref, x_ref, g_ref, gain_ref, out_ref, back_ref, other_ref,
-    value_ref, grad_ref, coupling_ref, buffer, sems,
+    member_ref, x_ref, g_ref, gain_ref, own_ref, other_ref, value_ref, grad_ref, coupling_ref
 ):
     rows, seq, width = x_ref.shape
-    copies = []
-    for r in range(rows):
-        at = pl.ds(pl.multiple_of(pos_ref[r] * seq, seq), seq)
-        for i, ref in enumerate((out_ref, back_ref)):
-            copy = pltpu.make_async_copy(ref.at[at], buffer.at[i, r], sems.at[i, r])
-            copy.start()
-            copies.append(copy)
     diagonal = lax.broadcasted_iota(jnp.int32, (seq, seq), 0) == lax.broadcasted_iota(
         jnp.int32, (seq, seq), 1
     )
     for r in range(rows):
-        copies[2 * r].wait()
-        copies[2 * r + 1].wait()
         x = x_ref[r].astype(F32)
         inv = 1.0 / jnp.sqrt(jnp.mean(x * x, axis=1, keepdims=True) + 1e-06)
         normed = x * inv
-        gain = gain_ref[pl.ds(member_ref[r], 1), :]
-        back = gain * (buffer[1, r] + other_ref[1, r].astype(F32))
+        gain = gain_ref[pl.ds(member_ref[pl.program_id(0) * rows + r], 1), :]
+        back = gain * (own_ref[1, r] + other_ref[1, r].astype(F32))
         stat = jnp.sum(normed * back, axis=1, keepdims=True) / width
-        value_ref[r] = (x + (buffer[0, r] + other_ref[0, r].astype(F32))).astype(BF16)
+        value_ref[r] = (x + (own_ref[0, r] + other_ref[0, r].astype(F32))).astype(BF16)
         grad_ref[r] = (g_ref[r].astype(F32) + (back - normed * stat) * inv).astype(BF16)
         line = jnp.sum(jnp.where(diagonal, stat, 0.0), axis=0, keepdims=True)
-        coupling_ref[pl.ds(r, 1), :] = line * math.sqrt(width)
-
-
-def finish(pos_own, member_own, x, g, gain, out_sum, back_sum, other):
+        coupling_ref[r] = line * math.sqrt(width)
+
+
+def finish(member_own, x, g, gain, own, other):
     rows, seq, width = x.shape
-    smem = pl.BlockSpec(memory_space=pltpu.SMEM)
-    vmem = pl.BlockSpec(memory_space=pltpu.VMEM)
-    hbm = pl.BlockSpec(memory_space=pl.ANY)
+    step = math.gcd(rows, 2)
+    row = pl.BlockSpec((step, seq, width), lambda r, mem: (r, 0, 0))
+    two = pl.BlockSpec((2, step, seq, width), lambda r, mem: (0, r, 0, 0))
     return pl.pallas_call(
         finish_kernel,
-        in_specs=[smem, smem, vmem, vmem, vmem, hbm, hbm, vmem],
-        out_specs=[vmem, vmem, vmem],
+        grid_spec=pltpu.PrefetchScalarGridSpec(
+            num_scalar_prefetch=1,
+            grid=(rows // step,),
+            in_specs=[row, row, pl.BlockSpec(gain.shape, lambda r, mem: (0, 0)), two, two],
+            out_specs=[row, row, pl.BlockSpec((step, 1, seq), lambda r, mem: (r, 0, 0))],
+        ),
         out_shape=[
             jax.ShapeDtypeStruct((rows, seq, width), BF16),
             jax.ShapeDtypeStruct((rows, seq, width), BF16),
-            jax.ShapeDtypeStruct((rows, seq), F32),
-        ],
-        scratch_shapes=[
-            pltpu.VMEM((2, rows, seq, width), F32),
-            pltpu.SemaphoreType.DMA((2, rows)),
+            jax.ShapeDtypeStruct((rows, 1, seq), F32),
         ],
         compiler_params=pltpu.CompilerParams(vmem_limit_bytes=VMEM_LIMIT),
         name="finish",
-    )(pos_own, member_own, x, g, gain, out_sum, back_sum, other)
+    )(member_own, x, g, gain, own, other)
+
+
+def plan_chunks(half, members):
+    unit = half // 8
+    if unit % 128 or members != 2:
+        return [(m, [half // 2, half - half // 2], False) for m in range(members)]
+    return [
+        (0, [unit, 2 * unit], False),
+        (0, [3 * unit, 2 * unit], False),
+        (1, [2 * unit, 3 * unit], True),
+        (1, [2 * unit, unit], False),
+    ]
 
 
 def on_device_pairs(ranks, tokens_in, upstream, member_pick, norm_gain, up_proj, down_proj):
@@ -397,42 +424,50 @@
     lifted, g_sorted = prep(perm, member_sorted, x_pair, g_pair, norm_gain)
     lifted = lifted.reshape(2 * rows * seq, width)
     g_sorted = g_sorted.reshape(2 * rows * seq, width)
-    scalars = (low, high, member_sorted, jnp.stack([x_at, y_at, rank // 4]))
-
-    count = 4
-    size = half // count
+    scalars = (low, high, member_sorted, jnp.stack([x_at, y_at, rank // 4]), perm)
+
+    own_y = [over_y(shard[member]) for member in range(members)]
+    steps = plan_chunks(half, members)
     sums = None
-    pieces, y_done = [], []
-    for member in range(members):
-        for part in range(count):
-            cols = slice(part * size, (part + 1) * size)
-            own, mine = shard[member, :, cols], along[member, :, cols]
-            at = len(pieces)
-            if at >= 2:
-                mine = after(mine, pieces[at - 2][2])
-            if at >= 3:
-                mine = after(mine, y_done[at - 3])
-            own_y = over_y(own)
+    z_done, y_done, x_done, yx_done, all_sums = [], [], [], [], []
+    start = [0] * members
+    for i, (member, sizes, x_first) in enumerate(steps):
+        pieces = []
+        for part, size in enumerate(sizes):
+            first_unit = start[member]
+            start[member] += size
+            at = len(z_done)
+            mine = along[member, :, first_unit : first_unit + size]
+            waits = []
+            for done, behind in ((z_done, 2), (y_done, 3), (x_done, 3), (yx_done, 4)):
+                if at >= behind:
+                    waits.append(done[at - behind])
+            if i >= 3 and part == 0:
+                waits.append(all_sums[i - 3][0])
+            if waits:
+                mine = after(mine, *waits)
             here = jnp.stack([shift_z(mine, d) for d in range(1, ranks // 4)])
             here_x = over_x(here)
             there = over_y(here)
-            if at == members * count - 3:
-                there_x = over_y(here_x)
-            else:
-                there_x = over_x(there)
+            there_x = over_y(here_x) if x_first and part else over_x(there)
+            z_done.append(here)
             y_done.append(there)
-            pieces.append((own, own_y, here, there, here_x, there_x))
-    for member in range(members):
-        for part in range(0, count, 2):
-            at = member * count + part
-            sums = chunk(
-                member, part == 0, per_block, seq, scalars, lifted, g_sorted,
-                pieces[at : at + 2], sums,
+            x_done.append(here_x)
+            yx_done.append(there_x)
+            pieces.append(
+                ((shard, first_unit), (own_y[member][None], first_unit), here, there, here_x, there_x)
             )
-    other = partner(pack(pos[rows:], sums[0], sums[1], rows, seq))
-    return tuple(
-        finish(pos[:rows], pick_own, tokens_in, upstream, norm_gain, sums[0], sums[1], other)
-    )
+        first, last = i == 0, i == len(steps) - 1
+        opens = not any(m == member for m, _, _ in steps[:i])
+        sums = chunk(
+            member, (first, opens, last), per_block, seq, scalars, lifted, g_sorted, pieces, sums
+        )
+        all_sums.append(sums)
+    own, packed = sums
+    value_out, grad_in, coupling = finish(
+        pick_own, tokens_in, upstream, norm_gain, own, partner(packed)
+    )
+    return value_out, grad_in, coupling.reshape(rows, seq)
 
 
 def solution(mesh):

time: 265 us -> 237 us (0.89)
  the two profiles are of different devices: /device:TPU:8 before, /device:TPU:13 now
where the time goes in v4:
time: 237 us; the launch traced here: 233 us
  waiting for transfers between devices  92.3 us (39%)
  starting transfers between devices  60.9 us (26%)
  Pallas kernels  59 us (25%)
  other arithmetic  12.1 us (5%)
  local copies, waits for them, and re-layouts  7.58 us (3%)
    pallas_call x4, Pallas kernels, chunk(): pl.pallas_call(kernel, grid_spec=pltpu.PrefetchScalarGridSpec(num_scalar_...  48.3 us
    ppermute x24, waiting for transfers between devices, shift_z(): lax.ppermute(a, 'row', [(i, (i + 4 * d) % ranks) for i in range(ranks)])  39.4 us
    ppermute x24, starting transfers between devices, shift_z(): lax.ppermute(a, 'row', [(i, (i + 4 * d) % ranks) for i in range(ranks)])  28.5 us
    ppermute x15, waiting for transfers between devices, over_x(): return lax.ppermute(a, 'grp', [(0, 1), (1, 0)])  27.9 us
    ppermute x11, waiting for transfers between devices, over_y(): return lax.ppermute(a, 'row', [(i, i ^ 2) for i in range(ranks)])  18.5 us
    ppermute x15, starting transfers between devices, over_x(): return lax.ppermute(a, 'grp', [(0, 1), (1, 0)])  15.6 us
    ppermute x5, starting transfers between devices, partner(): return lax.ppermute(a, 'row', [(i, i ^ 1) for i in range(ranks)])  12.9 us
    ppermute x5, waiting for transfers between devices, partner(): return lax.ppermute(a, 'row', [(i, i ^ 1) for i in range(ranks)])  6.49 us
  transfers between devices with their start and end apart: 55, of which 22 were waited for; matrix products, arithmetic and copies ran while one was open for 4% of the time, Pallas kernels for 18%

profile of v4, /device:TPU:13, one launch (start us, length us, event | category | flops | bytes accessed | tf_op | source)
XLA Modules:
  0.0 233.2 jit_solution(1406589965253334330)
XLA Ops:
  12.9 3.1 %collective-permute-start.12 = (bf16[128,512]{1,0:T(8,128)(2,1)S(1)}, bf16[128,512]{1,0:T(8,128)(2,1)S(1)}, u32[]{:S(2)}, u32[]{:S(2)}) collective-permute-start(bf16[128,512]{1,0:T(8,128)(2,1)S(1)} %get-tuple-element.56), channel_id=1, source_target_pairs={{0,8},{1,9},{2,10},{3,11},{4,12},{5,13},{6,14},{7,15},{8,0},{9,1},... | collective-permute-start | bytes 393224 | tf_op jit(solution)/shard_map/ppermute | solution.py:392
  16.0 5.4 %collective-permute-done.7 = bf16[128,256]{1,0:T(8,128)(2,1)S(1)} collective-permute-done((bf16[128,256]{1,0:T(8,128)(2,1)S(1)}, bf16[128,256]{1,0:T(8,128)(2,1)S(1)}, u32[]{:S(2)}, u32[]{:S(2)}) %collective-permute-start.7) | collective-permute-done | bytes 65568 | tf_op jit(solution)/shard_map/ppermute | solution.py:392
  23.7 3.1 %collective-permute-done.12 = bf16[128,512]{1,0:T(8,128)(2,1)S(1)} collective-permute-done((bf16[128,512]{1,0:T(8,128)(2,1)S(1)}, bf16[128,512]{1,0:T(8,128)(2,1)S(1)}, u32[]{:S(2)}, u32[]{:S(2)}) %collective-permute-start.12) | collective-permute-done | bytes 131104 | tf_op jit(solution)/shard_map/ppermute | solution.py:392
  26.8 3.1 %collective-permute-start.9 = (bf16[128,768]{1,0:T(8,128)(2,1)S(1)}, bf16[128,768]{1,0:T(8,128)(2,1)S(1)}, u32[]{:S(2)}, u32[]{:S(2)}) collective-permute-start(bf16[128,768]{1,0:T(8,128)(2,1)S(1)} %get-tuple-element.24), channel_id=1, source_target_pairs={{0,8},{1,9},{2,10},{3,11},{4,12},{5,13},{6,14},{7,15},{8,0},{9,1},... | collective-permute-start | bytes 589832 | tf_op jit(solution)/shard_map/ppermute | solution.py:392
  29.9 7.2 %collective-permute-done.13 = bf16[128,512]{1,0:T(8,128)(2,1)S(1)} collective-permute-done((bf16[128,512]{1,0:T(8,128)(2,1)S(1)}, bf16[128,512]{1,0:T(8,128)(2,1)S(1)}, u32[]{:S(2)}, u32[]{:S(2)}) %collective-permute-start.13) | collective-permute-done | bytes 131104 | tf_op jit(solution)/shard_map/ppermute | solution.py:392
  39.0 4.1 %collective-permute-done.9 = bf16[128,768]{1,0:T(8,128)(2,1)S(1)} collective-permute-done((bf16[128,768]{1,0:T(8,128)(2,1)S(1)}, bf16[128,768]{1,0:T(8,128)(2,1)S(1)}, u32[]{:S(2)}, u32[]{:S(2)}) %collective-permute-start.9) | collective-permute-done | bytes 196640 | tf_op jit(solution)/shard_map/ppermute | solution.py:392
  45.6 3.1 %collective-permute-start.23 = (bf16[128,512]{1,0:T(8,128)(2,1)}, bf16[128,512]{1,0:T(8,128)(2,1)}, u32[]{:S(2)}, u32[]{:S(2)}) collective-permute-start(bf16[128,512]{1,0:T(8,128)(2,1)} %get-tuple-element.26), channel_id=1, source_target_pairs={{0,8},{1,9},{2,10},{3,11},{4,12},{5,13},{6,14},{7,15},{8,0},{9,1},... | collective-permute-start | bytes 393224 | tf_op jit(solution)/shard_map/ppermute | solution.py:392
  57.7 3.1 %collective-permute-done.24 = bf16[128,512]{1,0:T(8,128)(2,1)} collective-permute-done((bf16[128,512]{1,0:T(8,128)(2,1)}, bf16[128,512]{1,0:T(8,128)(2,1)}, u32[]{:S(2)}, u32[]{:S(2)}) %collective-permute-start.24) | collective-permute-done | bytes 131104 | tf_op jit(solution)/shard_map/ppermute | solution.py:392
  60.8 6.4 %collective-permute-start.2 = (bf16[6,64,1024]{2,1,0:T(8,128)(2,1)S(1)}, bf16[6,64,1024]{2,1,0:T(8,128)(2,1)S(1)}, u32[]{:S(2)}, u32[]{:S(2)}) collective-permute-start(bf16[6,64,1024]{2,1,0:T(8,128)(2,1)S(1)} %copy-done.6), channel_id=1, source_target_pairs={{0,1},{1,0},{2,3},{3,2},{4,5},{5,4},{6,7},{7,6},{8,9},{9,8},{10,11... | collective-permute-start | bytes 2359304 | tf_op jit(solution)/shard_map/ppermute | solution.py:383
  77.3 4.8 %collective-permute-done.37.refs_11_ = bf16[3,128,768]{2,1,0:T(8,128)(2,1)S(1)} collective-permute-done((bf16[3,128,768]{2,1,0:T(8,128)(2,1)S(1)}, bf16[3,128,768]{2,1,0:T(8,128)(2,1)S(1)}, u32[]{:S(2)}, u32[]{:S(2)}) %collective-permute-start.37) | collective-permute-done | bytes 589856 | tf_op jit(solution)/shard_map/ppermute | solution.py:389
  82.1 8.4 %collective-permute-done.30.refs_18_ = bf16[3,128,512]{2,1,0:T(8,128)(2,1)S(1)} collective-permute-done((bf16[3,128,512]{2,1,0:T(8,128)(2,1)}, bf16[3,128,512]{2,1,0:T(8,128)(2,1)S(1)}, u32[]{:S(2)}, u32[]{:S(2)}) %collective-permute-start.30) | collective-permute-done | bytes 393248 | tf_op jit(solution)/shard_map/ppermute | solution.py:389
  93.1 3.7 %collective-permute-start.39 = (bf16[128,768]{1,0:T(8,128)(2,1)S(1)}, bf16[128,768]{1,0:T(8,128)(2,1)S(1)}, u32[]{:S(2)}, u32[]{:S(2)}) collective-permute-start(bf16[128,768]{1,0:T(8,128)(2,1)S(1)} %copy-done.22), channel_id=1, source_target_pairs={{0,8},{1,9},{2,10},{3,11},{4,12},{5,13},{6,14},{7,15},{8,0},{9,1},... | collective-permute-start | bytes 589832 | tf_op jit(solution)/shard_map/ppermute | solution.py:392
  101.8 6.5 %collective-permute-done.39 = bf16[128,768]{1,0:T(8,128)(2,1)S(1)} collective-permute-done((bf16[128,768]{1,0:T(8,128)(2,1)S(1)}, bf16[128,768]{1,0:T(8,128)(2,1)S(1)}, u32[]{:S(2)}, u32[]{:S(2)}) %collective-permute-start.39) | collective-permute-done | bytes 196640 | tf_op jit(solution)/shard_map/ppermute | solution.py:392
  115.5 5.2 %prep.1 = (bf16[12,64,1024]{2,1,0:T(8,128)(2,1)}, bf16[12,64,1024]{2,1,0:T(8,128)(2,1)}) custom-call(s32[12]{0:T(128)} %get-tuple-element.41.perm_ref.refs_4_, s32[12]{0:T(128)} %get-tuple-element.42.sorted_ref.refs_2_, bf16[12,64,1024]{2,1,0:T(8,128)(2,1)} %pad_maximum_fusion.1.x_ref, bf16[12,64,1024]{2,1,0:T(8,128)(2,1)} %pad_maximum_fusion.2.g_ref, ...), custom_call_target="tpu_custom_call" | custom-call | tf_op jit(solution)/shard_map/prep/pallas_call | solution.py:108
  120.7 9.2 %collective-permute-done.26.refs_17_ = bf16[3,128,512]{2,1,0:T(8,128)(2,1)} collective-permute-done((bf16[3,128,512]{2,1,0:T(8,128)(2,1)S(1)}, bf16[3,128,512]{2,1,0:T(8,128)(2,1)}, u32[]{:S(2)}, u32[]{:S(2)}) %collective-permute-start.26) | collective-permute-done | bytes 393248 | tf_op jit(solution)/shard_map/ppermute | solution.py:389
  131.5 9.7 %chunk.4 = (f32[768,1024]{1,0:T(8,128)}, f32[768,1024]{1,0:T(8,128)}) custom-call(s32[2]{0:T(128)} %get-tuple-element.46.refs_0_, s32[2]{0:T(128)} %get-tuple-element.45.refs_1_, s32[12]{0:T(128)} %get-tuple-element.42.sorted_ref.refs_2_, s32[3]{0:T(128)} %pad_add_fusion.1.refs_3_, s32[12]{0:T(128)} %get-tuple-element.41.perm_ref.refs_4_, ...), custom_call_target="tpu_custom_call" | custom-call | flops 3221225472 | bytes 18874368 | tf_op jit(solution)/shard_map/chunk/pallas_call | solution.py:294
  141.3 4.1 %collective-permute-start.32 = (bf16[128,512]{1,0:T(8,128)(2,1)S(1)}, bf16[128,512]{1,0:T(8,128)(2,1)S(1)}, u32[]{:S(2)}, u32[]{:S(2)}) collective-permute-start(bf16[128,512]{1,0:T(8,128)(2,1)S(1)} %copy-done.23), channel_id=1, source_target_pairs={{0,8},{1,9},{2,10},{3,11},{4,12},{5,13},{6,14},{7,15},{8,0},{9,1},... | collective-permute-start | bytes 393224 | tf_op jit(solution)/shard_map/ppermute | solution.py:392
  148.4 5.4 %collective-permute-done.32 = bf16[128,512]{1,0:T(8,128)(2,1)S(1)} collective-permute-done((bf16[128,512]{1,0:T(8,128)(2,1)S(1)}, bf16[128,512]{1,0:T(8,128)(2,1)S(1)}, u32[]{:S(2)}, u32[]{:S(2)}) %collective-permute-start.32) | collective-permute-done | bytes 131104 | tf_op jit(solution)/shard_map/ppermute | solution.py:392
  157.4 13.3 %chunk.5 = (f32[768,1024]{1,0:T(8,128)}, f32[768,1024]{1,0:T(8,128)}) custom-call(s32[2]{0:T(128)} %get-tuple-element.46.refs_0_, s32[2]{0:T(128)} %get-tuple-element.45.refs_1_, s32[12]{0:T(128)} %get-tuple-element.42.sorted_ref.refs_2_, s32[3]{0:T(128)} %pad_add_fusion.1.refs_3_, ...), custom_call_target="tpu_custom_call", output_to_operand_aliasing={{0}: (19, {}), {1}: (20, {})} | custom-call | flops 5368709120 | bytes 20971520 | tf_op jit(solution)/shard_map/chunk/pallas_call | solution.py:294
  174.4 17.7 %collective-permute-done.34.refs_10_ = bf16[3,128,512]{2,1,0:T(8,128)(2,1)S(1)} collective-permute-done((bf16[3,128,512]{2,1,0:T(8,128)(2,1)S(1)}, bf16[3,128,512]{2,1,0:T(8,128)(2,1)S(1)}, u32[]{:S(2)}, u32[]{:S(2)}) %collective-permute-start.34) | collective-permute-done | bytes 393248 | tf_op jit(solution)/shard_map/ppermute | solution.py:386
  192.9 13.3 %chunk.6 = (f32[768,1024]{1,0:T(8,128)}, f32[768,1024]{1,0:T(8,128)}) custom-call(s32[2]{0:T(128)} %get-tuple-element.46.refs_0_, s32[2]{0:T(128)} %get-tuple-element.45.refs_1_, s32[12]{0:T(128)} %get-tuple-element.42.sorted_ref.refs_2_, s32[3]{0:T(128)} %pad_add_fusion.1.refs_3_, ...), custom_call_target="tpu_custom_call", output_to_operand_aliasing={{0}: (19, {}), {1}: (20, {})} | custom-call | flops 5368709120 | bytes 20971520 | tf_op jit(solution)/shard_map/chunk/pallas_call | solution.py:294
  207.3 12.0 %chunk.7 = (f32[2,6,64,1024]{3,2,1,0:T(8,128)}, bf16[2,6,64,1024]{3,2,1,0:T(8,128)(2,1)}) custom-call(s32[2]{0:T(128)} %get-tuple-element.46.refs_0_, s32[2]{0:T(128)} %get-tuple-element.45.refs_1_, s32[12]{0:T(128)} %get-tuple-element.42.sorted_ref.refs_2_, s32[3]{0:T(128)} %pad_add_fusion.1.refs_3_, s32[12]{0:T(128)} %get-tuple-element.41.perm_ref.refs_4_, ...), custom_call_target="tpu_custom_call" | custom-call | flops 3221225472 | bytes 18874368 | tf_op jit(solution)/shard_map/chunk/pallas_call | solution.py:294
  222.1 3.2 %collective-permute-done.54.other_ref = bf16[2,6,64,1024]{3,2,1,0:T(8,128)(2,1)S(1)} collective-permute-done((bf16[2,6,64,1024]{3,2,1,0:T(8,128)(2,1)}, bf16[2,6,64,1024]{3,2,1,0:T(8,128)(2,1)S(1)}, u32[]{:S(2)}, u32[]{:S(2)}) %collective-permute-start.54) | collective-permute-done | bytes 1572896 | tf_op jit(solution)/shard_map/ppermute | solution.py:383
  226.5 5.5 %finish.1 = (bf16[6,64,1024]{2,1,0:T(8,128)(2,1)}, bf16[6,64,1024]{2,1,0:T(8,128)(2,1)}, f32[6,1,64]{2,1,0:T(1,128)}) custom-call(s32[6]{0:T(128)} %bitcast.103, bf16[6,64,1024]{2,1,0:T(8,128)(2,1)} %x_ref.1, bf16[6,64,1024]{2,1,0:T(8,128)(2,1)} %g_ref.1, f32[2,1024]{1,0:T(2,128)} %gain_ref.3, f32[2,6,64,1024]{3,2,1,0:T(8,128)} %get-tuple-element.36.own_ref, ...), custom_call_target="tpu_custom_call" | custom-call | tf_op jit(solution)/shard_map/finish/pallas_call | solution.py:343
  (200 shorter events, 71.2 us)
Async XLA Ops:
  16.0 21.0 %collective-permute-start.13 = (bf16[128,512]{1,0:T(8,128)(2,1)S(1)}, bf16[128,512]{1,0:T(8,128)(2,1)S(1)}, u32[]{:S(2)}, u32[]{:S(2)}) collective-permute-start(bf16[128,512]{1,0:T(8,128)(2,1)S(1)} %get-tuple-element.56), channel_id=1, source_target_pairs={{0,12},{1,13},{2,14},{3,15},{4,0},{5,1},{6,2},{7,3},{8,4},{9,5},{1... | collective-permute-start | bytes 393224 | tf_op jit(solution)/shard_map/ppermute | solution.py:392
  21.5 16.0 %collective-permute-start.16 = (bf16[3,128,256]{2,1,0:T(8,128)(2,1)S(1)}, bf16[3,128,256]{2,1,0:T(8,128)(2,1)S(1)}, u32[]{:S(2)}, u32[]{:S(2)}) collective-permute-start(bf16[3,128,256]{2,1,0:T(8,128)(2,1)S(1)} %pad_maximum_fusion.9.refs_9_), channel_id=1, source_target_pairs={{0,2},{1,3},{2,0},{3,1},{4,6},{5,7},{6,4},{7,5},{8,10},{9,11},{10,... | collective-permute-start | bytes 589832 | tf_op jit(solution)/shard_map/ppermute | solution.py:386
  21.7 15.7 %collective-permute-start.21 = (bf16[3,128,256]{2,1,0:T(8,128)(2,1)S(1)}, bf16[3,128,256]{2,1,0:T(8,128)(2,1)S(1)}, u32[]{:S(2)}, u32[]{:S(2)}) collective-permute-start(bf16[3,128,256]{2,1,0:T(8,128)(2,1)S(1)} %pad_maximum_fusion.9.refs_9_), channel_id=1, source_target_pairs={{0,16},{16,0},{1,17},{17,1},{2,18},{18,2},{3,19},{19,3},{4,20},{20... | collective-permute-start | bytes 589832 | tf_op jit(solution)/shard_map/ppermute | solution.py:389
  26.8 16.3 %collective-permute-start.9 = (bf16[128,768]{1,0:T(8,128)(2,1)S(1)}, bf16[128,768]{1,0:T(8,128)(2,1)S(1)}, u32[]{:S(2)}, u32[]{:S(2)}) collective-permute-start(bf16[128,768]{1,0:T(8,128)(2,1)S(1)} %get-tuple-element.24), channel_id=1, source_target_pairs={{0,8},{1,9},{2,10},{3,11},{4,12},{5,13},{6,14},{7,15},{8,0},{9,1},... | collective-permute-start | bytes 589832 | tf_op jit(solution)/shard_map/ppermute | solution.py:392
  43.1 32.5 %collective-permute-start.1 = (bf16[6,64,1024]{2,1,0:T(8,128)(2,1)}, bf16[6,64,1024]{2,1,0:T(8,128)(2,1)}, u32[]{:S(2)}, u32[]{:S(2)}) collective-permute-start(bf16[6,64,1024]{2,1,0:T(8,128)(2,1)} %x_ref.1), channel_id=1, source_target_pairs={{0,1},{1,0},{2,3},{3,2},{4,5},{5,4},{6,7},{7,6},{8,9},{9,8},{10,11... | collective-permute-start | bytes 2359304 | tf_op jit(solution)/shard_map/ppermute | solution.py:383
  48.9 26.8 %collective-permute-start.27 = (bf16[3,128,768]{2,1,0:T(8,128)(2,1)S(1)}, bf16[3,128,768]{2,1,0:T(8,128)(2,1)}, u32[]{:S(2)}, u32[]{:S(2)}) collective-permute-start(bf16[3,128,768]{2,1,0:T(8,128)(2,1)S(1)} %pad_maximum_fusion.3.refs_9_), channel_id=1, source_target_pairs={{0,2},{1,3},{2,0},{3,1},{4,6},{5,7},{6,4},{7,5},{8,10},{9,11},{10,... | collective-permute-start | bytes 1769480 | tf_op jit(solution)/shard_map/ppermute | solution.py:386
  60.8 31.5 %collective-permute-start.2 = (bf16[6,64,1024]{2,1,0:T(8,128)(2,1)S(1)}, bf16[6,64,1024]{2,1,0:T(8,128)(2,1)S(1)}, u32[]{:S(2)}, u32[]{:S(2)}) collective-permute-start(bf16[6,64,1024]{2,1,0:T(8,128)(2,1)S(1)} %copy-done.6), channel_id=1, source_target_pairs={{0,1},{1,0},{2,3},{3,2},{4,5},{5,4},{6,7},{7,6},{8,9},{9,8},{10,11... | collective-permute-start | bytes 2359304 | tf_op jit(solution)/shard_map/ppermute | solution.py:383
  73.4 17.1 %collective-permute-start.30 = (bf16[3,128,512]{2,1,0:T(8,128)(2,1)}, bf16[3,128,512]{2,1,0:T(8,128)(2,1)S(1)}, u32[]{:S(2)}, u32[]{:S(2)}) collective-permute-start(bf16[3,128,512]{2,1,0:T(8,128)(2,1)} %collective-permute-done.14.refs_16_), channel_id=1, source_target_pairs={{0,16},{16,0},{1,17},{17,1},{2,18},{18,2},{3,19},{19,3},{4,20},{20... | collective-permute-start | bytes 1179656 | tf_op jit(solution)/shard_map/ppermute | solution.py:389
  75.6 16.4 %collective-permute-start.25 = (bf16[3,128,512]{2,1,0:T(8,128)(2,1)S(1)}, bf16[3,128,512]{2,1,0:T(8,128)(2,1)S(1)}, u32[]{:S(2)}, u32[]{:S(2)}) collective-permute-start(bf16[3,128,512]{2,1,0:T(8,128)(2,1)S(1)} %pad_maximum_fusion.7.refs_15_), channel_id=1, source_target_pairs={{0,2},{1,3},{2,0},{3,1},{4,6},{5,7},{6,4},{7,5},{8,10},{9,11},{10,... | collective-permute-start | bytes 1179656 | tf_op jit(solution)/shard_map/ppermute | solution.py:386
  75.7 17.4 %collective-permute-start.41 = (bf16[3,128,512]{2,1,0:T(8,128)(2,1)S(1)}, bf16[3,128,512]{2,1,0:T(8,128)(2,1)S(1)}, u32[]{:S(2)}, u32[]{:S(2)}) collective-permute-start(bf16[3,128,512]{2,1,0:T(8,128)(2,1)S(1)} %pad_maximum_fusion.6.refs_9_), channel_id=1, source_target_pairs={{0,2},{1,3},{2,0},{3,1},{4,6},{5,7},{6,4},{7,5},{8,10},{9,11},{10,... | collective-permute-start | bytes 1179656 | tf_op jit(solution)/shard_map/ppermute | solution.py:386
  82.1 47.8 %collective-permute-start.29 = (bf16[256,2048]{1,0:T(8,128)(2,1)S(1)}, bf16[256,2048]{1,0:T(8,128)(2,1)S(1)}, u32[]{:S(2)}, u32[]{:S(2)}) collective-permute-start(bf16[256,2048]{1,0:T(8,128)(2,1)S(1)} %bitcast.82), channel_id=1, source_target_pairs={{0,2},{1,3},{2,0},{3,1},{4,6},{5,7},{6,4},{7,5},{8,10},{9,11},{10,... | collective-permute-start | bytes 3145736 | tf_op jit(solution)/shard_map/ppermute | solution.py:386
  92.0 18.3 %collective-permute-start.43 = (bf16[3,128,512]{2,1,0:T(8,128)(2,1)S(1)}, bf16[3,128,512]{2,1,0:T(8,128)(2,1)S(1)}, u32[]{:S(2)}, u32[]{:S(2)}) collective-permute-start(bf16[3,128,512]{2,1,0:T(8,128)(2,1)S(1)} %collective-permute-done.25.refs_16_), channel_id=1, source_target_pairs={{0,16},{16,0},{1,17},{17,1},{2,18},{18,2},{3,19},{19,3},{4,20},{20... | collective-permute-start | bytes 1179656 | tf_op jit(solution)/shard_map/ppermute | solution.py:389
  100.4 29.6 %collective-permute-start.28 = (bf16[3,128,768]{2,1,0:T(8,128)(2,1)}, bf16[3,128,768]{2,1,0:T(8,128)(2,1)S(1)}, u32[]{:S(2)}, u32[]{:S(2)}) collective-permute-start(bf16[3,128,768]{2,1,0:T(8,128)(2,1)} %collective-permute-done.27.refs_10_), channel_id=1, source_target_pairs={{0,16},{16,0},{1,17},{17,1},{2,18},{18,2},{3,19},{19,3},{4,20},{20... | collective-permute-start | bytes 1769480 | tf_op jit(solution)/shard_map/ppermute | solution.py:389
  108.3 48.9 %collective-permute-start.4 = (bf16[256,2048]{1,0:T(8,128)(2,1)S(1)}, bf16[256,2048]{1,0:T(8,128)(2,1)S(1)}, u32[]{:S(2)}, u32[]{:S(2)}) collective-permute-start(bf16[256,2048]{1,0:T(8,128)(2,1)S(1)} %bitcast.81), channel_id=1, source_target_pairs={{0,2},{1,3},{2,0},{3,1},{4,6},{5,7},{6,4},{7,5},{8,10},{9,11},{10,... | collective-permute-start | bytes 3145736 | tf_op jit(solution)/shard_map/ppermute | solution.py:386
  109.2 20.7 %collective-permute-start.26 = (bf16[3,128,512]{2,1,0:T(8,128)(2,1)S(1)}, bf16[3,128,512]{2,1,0:T(8,128)(2,1)}, u32[]{:S(2)}, u32[]{:S(2)}) collective-permute-start(bf16[3,128,512]{2,1,0:T(8,128)(2,1)S(1)} %pad_maximum_fusion.7.refs_15_), channel_id=1, source_target_pairs={{0,16},{16,0},{1,17},{17,1},{2,18},{18,2},{3,19},{19,3},{4,20},{20... | collective-permute-start | bytes 1179656 | tf_op jit(solution)/shard_map/ppermute | solution.py:389
  111.1 44.6 %collective-permute-start.52 = (bf16[3,128,768]{2,1,0:T(8,128)(2,1)S(1)}, bf16[3,128,768]{2,1,0:T(8,128)(2,1)S(1)}, u32[]{:S(2)}, u32[]{:S(2)}) collective-permute-start(bf16[3,128,768]{2,1,0:T(8,128)(2,1)S(1)} %pad_maximum_fusion.4.refs_15_), channel_id=1, source_target_pairs={{0,16},{16,0},{1,17},{17,1},{2,18},{18,2},{3,19},{19,3},{4,20},{20... | collective-permute-start | bytes 1769480 | tf_op jit(solution)/shard_map/ppermute | solution.py:389
  145.7 25.0 %collective-permute-start.50 = (bf16[3,128,512]{2,1,0:T(8,128)(2,1)S(1)}, bf16[3,128,512]{2,1,0:T(8,128)(2,1)S(1)}, u32[]{:S(2)}, u32[]{:S(2)}) collective-permute-start(bf16[3,128,512]{2,1,0:T(8,128)(2,1)S(1)} %copy-done.33), channel_id=1, source_target_pairs={{0,16},{16,0},{1,17},{17,1},{2,18},{18,2},{3,19},{19,3},{4,20},{20... | collective-permute-start | bytes 1179656 | tf_op jit(solution)/shard_map/ppermute | solution.py:389
  153.7 19.2 %collective-permute-start.51 = (bf16[3,128,768]{2,1,0:T(8,128)(2,1)S(1)}, bf16[3,128,768]{2,1,0:T(8,128)(2,1)S(1)}, u32[]{:S(2)}, u32[]{:S(2)}) collective-permute-start(bf16[3,128,768]{2,1,0:T(8,128)(2,1)S(1)} %pad_maximum_fusion.4.refs_15_), channel_id=1, source_target_pairs={{0,2},{1,3},{2,0},{3,1},{4,6},{5,7},{6,4},{7,5},{8,10},{9,11},{10,... | collective-permute-start | bytes 1769480 | tf_op jit(solution)/shard_map/ppermute | solution.py:386
  155.7 17.1 %collective-permute-start.47 = (bf16[3,128,256]{2,1,0:T(8,128)(2,1)S(1)}, bf16[3,128,256]{2,1,0:T(8,128)(2,1)S(1)}, u32[]{:S(2)}, u32[]{:S(2)}) collective-permute-start(bf16[3,128,256]{2,1,0:T(8,128)(2,1)S(1)} %pad_maximum_fusion.10.refs_15_), channel_id=1, source_target_pairs={{0,2},{1,3},{2,0},{3,1},{4,6},{5,7},{6,4},{7,5},{8,10},{9,11},{10,... | collective-permute-start | bytes 589832 | tf_op jit(solution)/shard_map/ppermute | solution.py:386
  155.7 36.3 %collective-permute-start.53 = (bf16[3,128,768]{2,1,0:T(8,128)(2,1)S(1)}, bf16[3,128,768]{2,1,0:T(8,128)(2,1)S(1)}, u32[]{:S(2)}, u32[]{:S(2)}) collective-permute-start(bf16[3,128,768]{2,1,0:T(8,128)(2,1)S(1)} %collective-permute-done.52.refs_17_), channel_id=1, source_target_pairs={{0,2},{1,3},{2,0},{3,1},{4,6},{5,7},{6,4},{7,5},{8,10},{9,11},{10,... | collective-permute-start | bytes 1769480 | tf_op jit(solution)/shard_map/ppermute | solution.py:386
  157.3 34.8 %collective-permute-start.34 = (bf16[3,128,512]{2,1,0:T(8,128)(2,1)S(1)}, bf16[3,128,512]{2,1,0:T(8,128)(2,1)S(1)}, u32[]{:S(2)}, u32[]{:S(2)}) collective-permute-start(bf16[3,128,512]{2,1,0:T(8,128)(2,1)S(1)} %pad_maximum_fusion.8.refs_9_), channel_id=1, source_target_pairs={{0,2},{1,3},{2,0},{3,1},{4,6},{5,7},{6,4},{7,5},{8,10},{9,11},{10,... | collective-permute-start | bytes 1179656 | tf_op jit(solution)/shard_map/ppermute | solution.py:386
  170.7 35.5 %collective-permute-start.48 = (bf16[3,128,256]{2,1,0:T(8,128)(2,1)S(1)}, bf16[3,128,256]{2,1,0:T(8,128)(2,1)S(1)}, u32[]{:S(2)}, u32[]{:S(2)}) collective-permute-start(bf16[3,128,256]{2,1,0:T(8,128)(2,1)S(1)} %pad_maximum_fusion.10.refs_15_), channel_id=1, source_target_pairs={{0,16},{16,0},{1,17},{17,1},{2,18},{18,2},{3,19},{19,3},{4,20},{20... | collective-permute-start | bytes 589832 | tf_op jit(solution)/shard_map/ppermute | solution.py:389
  172.8 33.5 %collective-permute-start.49 = (bf16[3,128,256]{2,1,0:T(8,128)(2,1)S(1)}, bf16[3,128,256]{2,1,0:T(8,128)(2,1)S(1)}, u32[]{:S(2)}, u32[]{:S(2)}) collective-permute-start(bf16[3,128,256]{2,1,0:T(8,128)(2,1)S(1)} %collective-permute-done.47.refs_16_), channel_id=1, source_target_pairs={{0,16},{16,0},{1,17},{17,1},{2,18},{18,2},{3,19},{19,3},{4,20},{20... | collective-permute-start | bytes 589832 | tf_op jit(solution)/shard_map/ppermute | solution.py:389
  172.9 33.4 %collective-permute-start.35 = (bf16[3,128,512]{2,1,0:T(8,128)(2,1)S(1)}, bf16[3,128,512]{2,1,0:T(8,128)(2,1)S(1)}, u32[]{:S(2)}, u32[]{:S(2)}) collective-permute-start(bf16[3,128,512]{2,1,0:T(8,128)(2,1)S(1)} %pad_maximum_fusion.8.refs_9_), channel_id=1, source_target_pairs={{0,16},{16,0},{1,17},{17,1},{2,18},{18,2},{3,19},{19,3},{4,20},{20... | collective-permute-start | bytes 1179656 | tf_op jit(solution)/shard_map/ppermute | solution.py:389
  (72 other events, 984.9 us)

commit v5 on v4

--- a/solution.py
+++ b/solution.py
@@ -117,15 +117,16 @@
 
 def chunk_kernel(
     member, per_block, seq, kind, units,
-    low_ref, high_ref, sorted_ref, place_ref, perm_ref, lifted_ref, g_ref, *refs,
+    low_ref, high_ref, sorted_ref, place_ref, perm_ref, dest_ref, lifted_ref, g_ref, *refs,
 ):
     first, opens, last = kind
     parts = len(units)
-    pieces, refs = refs[: 6 * parts], refs[6 * parts :]
+    pieces, refs = refs[: 4 * parts], refs[4 * parts :]
     if first:
-        out_ref, back_ref, weights_ref, sems = refs
+        *outs, weights_ref, sems = refs
     else:
-        out_in, back_in, out_ref, back_ref, weights_ref, sems = refs
+        out_in, back_in, *outs, weights_ref, sems = refs
+    out_ref, back_ref = outs[:2]
     j = pl.program_id(0)
     lines, _, depth2, hidden_units = weights_ref.shape
     depth = depth2 // 2
@@ -134,33 +135,25 @@
 
     @pl.when(j == 0)
     def _():
-        x, y, z = place_ref[0], place_ref[1], place_ref[2]
-        mine = pl.multiple_of(x * depth, depth)
-        others = pl.multiple_of((1 - x) * depth, depth)
+        y, z = place_ref[0], place_ref[1]
         copies = []
 
-        def put(src, to_z, to_y, at, size, cols):
+        def put(src, to_z, to_y, cols):
             copies.append(
                 pltpu.make_async_copy(
-                    src, weights_ref.at[to_z, to_y, pl.ds(at, size), cols], sems.at[len(copies)]
+                    src, weights_ref.at[to_z, to_y, :, cols], sems.at[len(copies)]
                 )
             )
 
         for part in range(parts):
-            own, own_y, here, there, here_x, there_x = pieces[6 * part : 6 * part + 6]
             cols = pl.ds(sum(units[:part]), units[part])
-            own, own_y = (
-                ref.at[min(member, ref.shape[0] - 1), :, pl.ds(start, units[part])]
-                for ref, start in (own, own_y)
-            )
-            put(own, z, y, 0, depth2, cols)
-            put(own_y, z, 1 - y, 0, depth2, cols)
+            (own, start), (own_y, start_y), here, there = pieces[4 * part : 4 * part + 4]
+            put(own.at[member, :, pl.ds(start, units[part])], z, y, cols)
+            put(own_y.at[:, pl.ds(start_y, units[part])], z, 1 - y, cols)
             for d in range(1, lines):
                 from_z = lax.rem(z + lines - d, lines)
-                put(here.at[d - 1], from_z, y, mine, depth, cols)
-                put(there.at[d - 1], from_z, 1 - y, mine, depth, cols)
-                put(here_x.at[d - 1], from_z, y, others, depth, cols)
-                put(there_x.at[d - 1], from_z, 1 - y, others, depth, cols)
+                put(here.at[d - 1], from_z, y, cols)
+                put(there.at[d - 1], from_z, 1 - y, cols)
         for copy in copies:
             copy.start()
         for copy in copies:
@@ -197,27 +190,43 @@
             back_sum += lax.dot_general(pre, up, dims, preferred_element_type=F32)
         return weight * out_sum, weight * back_sum
 
+    def old_sums():
+        if first:
+            return 0.0, 0.0
+        if opens:
+            old = sorted_ref[at * per_block] < member
+            return jnp.where(old, out_in[...], 0.0), jnp.where(old, back_in[...], 0.0)
+        return out_in[...], back_in[...]
+
     if last:
-        rows = out_ref.shape[1]
+        rows = out_ref.shape[0]
 
         def store(i, value):
             for p in range(per_block):
                 row = perm_ref[at * per_block + p]
+                to = dest_ref[row]
                 tokens = value[p * seq : (p + 1) * seq]
 
                 @pl.when(row < rows)
                 def _():
-                    out_ref[i, jnp.minimum(row, rows - 1)] = tokens
-
-                @pl.when(row >= rows)
-                def _():
-                    back_ref[i, jnp.maximum(row - rows, 0)] = tokens.astype(BF16)
+                    outs[i][to] = tokens
+
+                low_row = rows
+                for packed_ref in outs[2:]:
+                    high_row = low_row + packed_ref.shape[1]
+
+                    @pl.when(jnp.logical_and(row >= low_row, row < high_row))
+                    def _():
+                        packed_ref[i, to] = tokens.astype(BF16)
+
+                    low_row = high_row
 
         @pl.when(inside)
         def _():
             out_sum, back_sum = sums()
-            store(0, out_in[...] + out_sum)
-            store(1, back_in[...] + back_sum)
+            out_old, back_old = old_sums()
+            store(0, out_old + out_sum)
+            store(1, back_old + back_sum)
 
         @pl.when(jnp.logical_not(inside))
         def _():
@@ -236,24 +245,18 @@
     @pl.when(inside)
     def _():
         out_sum, back_sum = sums()
-        if first:
-            out_ref[...] = out_sum
-            back_ref[...] = back_sum
-        elif opens:
-            old = sorted_ref[at * per_block] < member
-            out_ref[...] = jnp.where(old, out_in[...], 0.0) + out_sum
-            back_ref[...] = jnp.where(old, back_in[...], 0.0) + back_sum
-        else:
-            out_ref[...] = out_in[...] + out_sum
-            back_ref[...] = back_in[...] + back_sum
-
-
-def chunk(member, kind, per_block, seq, scalars, lifted, g, pieces, sums):
+        out_old, back_old = old_sums()
+        out_ref[...] = out_old + out_sum
+        back_ref[...] = back_old + back_sum
+
+
+def chunk(member, kind, per_block, scalars, lifted, g, pieces, sums, splits=None):
     first, _, last = kind
-    tokens, width = lifted.shape
+    rows, seq, width = lifted.shape
+    tokens = rows * seq
     units = [part[2].shape[2] for part in pieces]
-    depth2 = pieces[0][0][0].shape[1]
     lines = pieces[0][2].shape[0] + 1
+    depth2 = pieces[0][2].shape[1]
     hidden = sum(units)
     size = per_block * seq
 
@@ -264,31 +267,33 @@
 
     tok = pl.BlockSpec((size, width), block)
     hbm = pl.BlockSpec(memory_space=pl.ANY)
-    args = [*scalars, lifted, g]
+    args = [*scalars, lifted.reshape(tokens, width), g.reshape(tokens, width)]
     starts = []
-    for own, own_y, *rest in pieces:
-        args += [own[0], own_y[0], *rest]
+    for own, own_y, here, there in pieces:
+        args += [own[0], own_y[0], here, there]
         starts.append((own[1], own_y[1]))
-    specs = [tok, tok] + [hbm] * (6 * len(pieces))
+    specs = [tok, tok] + [hbm] * (4 * len(pieces))
     alias = {}
     out_specs = [tok, tok]
     out_shape = [jax.ShapeDtypeStruct((tokens, width), F32)] * 2
     if not first:
         alias = {len(args): 0, len(args) + 1: 1}
-        args += list(sums)
+        args += [a.reshape(tokens, width) for a in sums]
         specs += [tok, tok]
     if last:
         alias = {}
-        shape = (2, tokens // (2 * seq), seq, width)
-        out_specs = [pl.BlockSpec(shape, lambda *_: (0, 0, 0, 0))] * 2
-        out_shape = [jax.ShapeDtypeStruct(shape, F32), jax.ShapeDtypeStruct(shape, BF16)]
+        out_shape = [jax.ShapeDtypeStruct((splits[0], seq, width), F32)] * 2
+        out_shape += [jax.ShapeDtypeStruct((2, n, seq, width), BF16) for n in splits[1:]]
+        out_specs = [
+            pl.BlockSpec(a.shape, lambda *_, n=len(a.shape): (0,) * n) for a in out_shape
+        ]
 
     def kernel(*refs):
         refs = list(refs)
         base = len(scalars) + 2
         for part, (own, own_y) in enumerate(starts):
-            refs[base + 6 * part] = (refs[base + 6 * part], own)
-            refs[base + 6 * part + 1] = (refs[base + 6 * part + 1], own_y)
+            refs[base + 4 * part] = (refs[base + 4 * part], own)
+            refs[base + 4 * part + 1] = (refs[base + 4 * part + 1], own_y)
         chunk_kernel(member, per_block, seq, kind, units, *refs)
 
     return pl.pallas_call(
@@ -300,7 +305,7 @@
             out_specs=out_specs,
             scratch_shapes=[
                 pltpu.VMEM((lines, 2, depth2, hidden), BF16),
-                pltpu.SemaphoreType.DMA((len(pieces) * (4 * lines - 2),)),
+                pltpu.SemaphoreType.DMA((len(pieces) * 2 * lines,)),
             ],
         ),
         out_shape=out_shape,
@@ -316,7 +321,8 @@
 
 
 def finish_kernel(
-    member_ref, x_ref, g_ref, gain_ref, own_ref, other_ref, value_ref, grad_ref, coupling_ref
+    member_ref, x_ref, g_ref, gain_ref, out_ref, back_ref, other_ref, across_ref,
+    value_ref, grad_ref, coupling_ref,
 ):
     rows, seq, width = x_ref.shape
     diagonal = lax.broadcasted_iota(jnp.int32, (seq, seq), 0) == lax.broadcasted_iota(
@@ -327,15 +333,18 @@
         inv = 1.0 / jnp.sqrt(jnp.mean(x * x, axis=1, keepdims=True) + 1e-06)
         normed = x * inv
         gain = gain_ref[pl.ds(member_ref[pl.program_id(0) * rows + r], 1), :]
-        back = gain * (own_ref[1, r] + other_ref[1, r].astype(F32))
+        back = gain * (
+            back_ref[r] + other_ref[1, r].astype(F32) + across_ref[1, r].astype(F32)
+        )
         stat = jnp.sum(normed * back, axis=1, keepdims=True) / width
-        value_ref[r] = (x + (own_ref[0, r] + other_ref[0, r].astype(F32))).astype(BF16)
+        out = out_ref[r] + other_ref[0, r].astype(F32) + across_ref[0, r].astype(F32)
+        value_ref[r] = (x + out).astype(BF16)
         grad_ref[r] = (g_ref[r].astype(F32) + (back - normed * stat) * inv).astype(BF16)
         line = jnp.sum(jnp.where(diagonal, stat, 0.0), axis=0, keepdims=True)
         coupling_ref[r] = line * math.sqrt(width)
 
 
-def finish(member_own, x, g, gain, own, other):
+def finish(member_own, x, g, gain, out, back, other, across):
     rows, seq, width = x.shape
     step = math.gcd(rows, 2)
     row = pl.BlockSpec((step, seq, width), lambda r, mem: (r, 0, 0))
@@ -345,7 +354,9 @@
         grid_spec=pltpu.PrefetchScalarGridSpec(
             num_scalar_prefetch=1,
             grid=(rows // step,),
-            in_specs=[row, row, pl.BlockSpec(gain.shape, lambda r, mem: (0, 0)), two, two],
+            in_specs=[
+                row, row, pl.BlockSpec(gain.shape, lambda r, mem: (0, 0)), row, row, two, two
+            ],
             out_specs=[row, row, pl.BlockSpec((step, 1, seq), lambda r, mem: (r, 0, 0))],
         ),
         out_shape=[
@@ -355,29 +366,35 @@
         ],
         compiler_params=pltpu.CompilerParams(vmem_limit_bytes=VMEM_LIMIT),
         name="finish",
-    )(member_own, x, g, gain, own, other)
-
-
-def plan_chunks(half, members):
-    unit = half // 8
-    if unit % 128 or members != 2:
-        return [(m, [half // 2, half - half // 2], False) for m in range(members)]
-    return [
-        (0, [unit, 2 * unit], False),
-        (0, [3 * unit, 2 * unit], False),
-        (1, [2 * unit, 3 * unit], True),
-        (1, [2 * unit, unit], False),
-    ]
-
-
-def on_device_pairs(ranks, tokens_in, upstream, member_pick, norm_gain, up_proj, down_proj):
+    )(member_own, x, g, gain, out, back, other, across)
+
+
+def sort_rows(picks, members, per_block):
+    n = picks.shape[0]
+    index = jnp.arange(n, dtype=jnp.int32)
+    before = (picks[None, :] < picks[:, None]) | (
+        (picks[None, :] == picks[:, None]) & (index[None, :] < index[:, None])
+    )
+    pos = jnp.sum(before.astype(jnp.int32), axis=1)
+    at = pos[None, :] == index[:, None]
+    perm = jnp.sum(jnp.where(at, index[None, :], 0), axis=1)
+    member_sorted = jnp.sum(jnp.where(at, picks[None, :], 0), axis=1)
+    labels = jnp.arange(members, dtype=jnp.int32)[:, None]
+    start = jnp.sum((picks[None, :] < labels).astype(jnp.int32), axis=1)
+    end = jnp.sum((picks[None, :] <= labels).astype(jnp.int32), axis=1)
+    low = jnp.minimum(start, n - 1) // per_block
+    high = jnp.where(end > start, (end - 1) // per_block, low - 1)
+    return pos, perm, member_sorted, low, high
+
+
+def on_device_shared(ranks, tokens_in, upstream, member_pick, norm_gain, up_proj, down_proj):
     rows, seq, width = tokens_in.shape
     members, depth, hidden = up_proj.shape
-    half = hidden // 2
     rank = lax.axis_index("row")
     core = lax.rem(rank, 2)
     x_at = lax.axis_index("grp")
     y_at = lax.rem(rank // 2, 2)
+    lines = ranks // 4
 
     def partner(a):
         return lax.ppermute(a, "row", [(i, i ^ 1) for i in range(ranks)])
@@ -394,90 +411,110 @@
     def after(a, *others):
         return lax.optimization_barrier((a, *others))[0]
 
+    quarter = 3 * hidden // 16
+    half = hidden // 8
     both = jnp.stack([up_proj, down_proj], axis=1)
-    mine = lax.dynamic_slice_in_dim(both, core * half, half, 3)
-    theirs = partner(lax.dynamic_slice_in_dim(both, (1 - core) * half, half, 3))
+
+    def units_of(c):
+        return jnp.concatenate(
+            [
+                lax.dynamic_slice_in_dim(both, (2 * x_at + c) * quarter, quarter, 3),
+                lax.dynamic_slice_in_dim(both, 4 * quarter + c * half, half, 3),
+            ],
+            axis=3,
+        )
+
+    mine = units_of(core)
+    theirs = partner(units_of(1 - core))
     even = core == 0
     shard = jnp.concatenate(
         [jnp.where(even, mine, theirs), jnp.where(even, theirs, mine)], axis=2
-    ).reshape(members, 4 * depth, half)
-    along = jnp.where(x_at == 0, shard[:, : 2 * depth], shard[:, 2 * depth :])
+    ).reshape(members, 4 * depth, quarter + half)
+
     pick_own = member_pick[:, 0]
+    x_over, g_over, pick_over = over_x(tokens_in), over_x(upstream), over_x(pick_own)
     pick_pair = jnp.concatenate([pick_own, partner(pick_own)])
+    pick_all = jnp.concatenate([pick_pair, pick_over, partner(pick_over)])
     x_pair = jnp.concatenate([tokens_in, partner(tokens_in)])
     g_pair = jnp.concatenate([upstream, partner(upstream)])
-    index = jnp.arange(2 * rows, dtype=jnp.int32)
-    before = (pick_pair[None, :] < pick_pair[:, None]) | (
-        (pick_pair[None, :] == pick_pair[:, None]) & (index[None, :] < index[:, None])
-    )
-    pos = jnp.sum(before.astype(jnp.int32), axis=1)
-    at = pos[None, :] == index[:, None]
-    perm = jnp.sum(jnp.where(at, index[None, :], 0), axis=1)
-    member_sorted = jnp.sum(jnp.where(at, pick_pair[None, :], 0), axis=1)
+    x_all = jnp.concatenate([x_pair, x_over, partner(x_over)])
+    g_all = jnp.concatenate([g_pair, g_over, partner(g_over)])
     per_block = math.gcd(2 * rows, 4)
-    labels = jnp.arange(members, dtype=jnp.int32)[:, None]
-    start = jnp.sum((pick_pair[None, :] < labels).astype(jnp.int32), axis=1)
-    end = jnp.sum((pick_pair[None, :] <= labels).astype(jnp.int32), axis=1)
-    low = jnp.minimum(start, 2 * rows - 1) // per_block
-    high = jnp.where(end > start, (end - 1) // per_block, low - 1)
-
-    lifted, g_sorted = prep(perm, member_sorted, x_pair, g_pair, norm_gain)
-    lifted = lifted.reshape(2 * rows * seq, width)
-    g_sorted = g_sorted.reshape(2 * rows * seq, width)
-    scalars = (low, high, member_sorted, jnp.stack([x_at, y_at, rank // 4]), perm)
-
-    own_y = [over_y(shard[member]) for member in range(members)]
-    steps = plan_chunks(half, members)
-    sums = None
-    z_done, y_done, x_done, yx_done, all_sums = [], [], [], [], []
-    start = [0] * members
-    for i, (member, sizes, x_first) in enumerate(steps):
-        pieces = []
-        for part, size in enumerate(sizes):
-            first_unit = start[member]
-            start[member] += size
-            at = len(z_done)
-            mine = along[member, :, first_unit : first_unit + size]
-            waits = []
-            for done, behind in ((z_done, 2), (y_done, 3), (x_done, 3), (yx_done, 4)):
-                if at >= behind:
-                    waits.append(done[at - behind])
-            if i >= 3 and part == 0:
-                waits.append(all_sums[i - 3][0])
-            if waits:
-                mine = after(mine, *waits)
-            here = jnp.stack([shift_z(mine, d) for d in range(1, ranks // 4)])
-            here_x = over_x(here)
-            there = over_y(here)
-            there_x = over_y(here_x) if x_first and part else over_x(there)
-            z_done.append(here)
-            y_done.append(there)
-            x_done.append(here_x)
-            yx_done.append(there_x)
-            pieces.append(
-                ((shard, first_unit), (own_y[member][None], first_unit), here, there, here_x, there_x)
+    place = jnp.stack([y_at, rank // 4])
+    pos, perm, member_sorted, low, high = sort_rows(pick_pair, members, per_block)
+    index = jnp.arange(4 * rows, dtype=jnp.int32)
+    scalars_alone = (low, high, member_sorted, place, perm, lax.rem(index[: 2 * rows], rows))
+    lifted_alone, g_alone = prep(perm, member_sorted, x_pair, g_pair, norm_gain)
+    _, perm, member_sorted, low, high = sort_rows(pick_all, members, per_block)
+    dest = jnp.concatenate([pos, lax.rem(index[2 * rows :], rows)])
+    scalars_shared = (low, high, member_sorted, place, perm, dest)
+    lifted_shared, g_shared = prep(perm, member_sorted, x_all, g_all, norm_gain)
+
+    third = quarter // 3
+    transfers = [
+        (0, 0, third),
+        (0, third, 2 * third),
+        (1, 0, 2 * third),
+        (1, 2 * third, third),
+        (0, quarter, half),
+        (1, quarter, half),
+    ]
+    z_done, y_done, own_y, pieces = [], [], {}, []
+    for at, (member, start, size) in enumerate(transfers):
+        mine = shard[member, :, start : start + size]
+        waits = []
+        if at >= 2:
+            waits += [z_done[at - 2], y_done[at - 2 if at < 4 else at - 3]]
+        if at == 2:
+            waits.append(own_y[0])
+        if at == 4:
+            waits.append(own_y[1])
+        if waits:
+            mine = after(mine, *waits)
+        if at in (0, 1):
+            own_y[at] = over_y(after(shard[at], *z_done[:at]))
+        here = jnp.stack([shift_z(mine, d) for d in range(1, lines)])
+        z_done.append(here)
+        if at == 4:
+            sums = chunk(
+                0, (True, False, False), per_block, scalars_shared, lifted_shared, g_shared,
+                pieces[0:2], None,
             )
-        first, last = i == 0, i == len(steps) - 1
-        opens = not any(m == member for m, _, _ in steps[:i])
-        sums = chunk(
-            member, (first, opens, last), per_block, seq, scalars, lifted, g_sorted, pieces, sums
-        )
-        all_sums.append(sums)
-    own, packed = sums
+            out, back, over_same, over_other = chunk(
+                1, (False, True, True), per_block, scalars_shared, lifted_shared, g_shared,
+                pieces[2:4], sums, (2 * rows, rows, rows),
+            )
+            across = (over_same.astype(F32) + partner(over_other).astype(F32)).astype(BF16)
+        if at == 5:
+            here = after(here, across)
+            across = over_x(across)
+        there = over_y(here)
+        y_done.append(there)
+        pieces.append(((shard, start), (own_y[member], start), here, there))
+
+    sums = chunk(
+        0, (False, False, False), per_block, scalars_alone, lifted_alone, g_alone, pieces[4:5],
+        (out, back),
+    )
+    sums = (after(sums[0], across), sums[1])
+    out, back, packed = chunk(
+        1, (False, False, True), per_block, scalars_alone, lifted_alone, g_alone, pieces[5:6], sums,
+        (rows, rows),
+    )
     value_out, grad_in, coupling = finish(
-        pick_own, tokens_in, upstream, norm_gain, own, partner(packed)
+        pick_own, tokens_in, upstream, norm_gain, out, back, partner(packed), across
     )
     return value_out, grad_in, coupling.reshape(rows, seq)
 
 
 def solution(mesh):
     ranks = mesh.shape["row"]
-    paired = mesh.shape["feat"] == 1 and ranks % 4 == 0 and mesh.shape["grp"] == 2
+    four = mesh.shape["feat"] == 1 and ranks % 4 == 0 and mesh.shape["grp"] == 2
 
     def on_device(tokens_in, upstream, member_pick, norm_gain, up_proj, down_proj):
         args = (tokens_in, upstream, member_pick, norm_gain, up_proj, down_proj)
-        if paired and member_pick.shape[1] == 1:
-            return on_device_pairs(ranks, *args)
+        if four and member_pick.shape[1] == 1 and up_proj.shape[0] == 2:
+            return on_device_shared(ranks, *args)
         return on_device_general(*args)
 
     in_specs = (

time: 237 us -> 253 us (1.068)
  the two profiles are of different devices: /device:TPU:13 before, /device:TPU:8 now
where the time goes in v5:
time: 253 us; the launch traced here: 252 us
  waiting for transfers between devices  117 us (46%)
  Pallas kernels  70.3 us (28%)
  starting transfers between devices  37.9 us (15%)
  other arithmetic  19.3 us (8%)
  local copies, waits for them, and re-layouts  7 us (3%)
    ppermute x18, waiting for transfers between devices, shift_z(): lax.ppermute(a, 'row', [(i, (i + 4 * d) % ranks) for i in range(ranks)])  63.1 us
    pallas_call x4, Pallas kernels, chunk(): pl.pallas_call(kernel, grid_spec=pltpu.PrefetchScalarGridSpec(num_scalar_...  50.2 us
    ppermute x8, waiting for transfers between devices, over_y(): return lax.ppermute(a, 'row', [(i, i ^ 2) for i in range(ranks)])  37.5 us
    ppermute x18, starting transfers between devices, shift_z(): lax.ppermute(a, 'row', [(i, (i + 4 * d) % ranks) for i in range(ranks)])  20 us
    pallas_call x2, Pallas kernels, prep(): pl.pallas_call(prep_kernel, in_specs=[smem, smem, vmem, vmem, vmem], out_...  14.1 us
    ppermute x8, starting transfers between devices, over_y(): return lax.ppermute(a, 'row', [(i, i ^ 2) for i in range(ranks)])  11.5 us
    ppermute x4, waiting for transfers between devices, over_x(): return lax.ppermute(a, 'grp', [(0, 1), (1, 0)])  8.43 us
    ppermute x9, waiting for transfers between devices, partner(): return lax.ppermute(a, 'row', [(i, i ^ 1) for i in range(ranks)])  7.59 us
  transfers between devices with their start and end apart: 39, of which 23 were waited for; matrix products, arithmetic and copies ran while one was open for 8% of the time, Pallas kernels for 14%

profile of v5, /device:TPU:8, one launch (start us, length us, event | category | flops | bytes accessed | tf_op | source)
XLA Modules:
  0.0 252.1 jit_solution(4805232989073384928)
XLA Ops:
  13.3 4.0 %collective-permute-done.4 = bf16[256,256]{1,0:T(8,128)(2,1)} collective-permute-done((bf16[256,256]{1,0:T(8,128)(2,1)}, bf16[256,256]{1,0:T(8,128)(2,1)}, u32[]{:S(2)}, u32[]{:S(2)}) %collective-permute-start.4) | collective-permute-done | bytes 131104 | tf_op jit(solution)/shard_map/ppermute | solution.py:409
  28.3 8.0 %collective-permute-done.15.refs_11_ = bf16[3,256,256]{2,1,0:T(8,128)(2,1)S(1)} collective-permute-done((bf16[3,256,256]{2,1,0:T(8,128)(2,1)S(1)}, bf16[3,256,256]{2,1,0:T(8,128)(2,1)S(1)}, u32[]{:S(2)}, u32[]{:S(2)}) %collective-permute-start.15) | collective-permute-done | bytes 393248 | tf_op jit(solution)/shard_map/ppermute | solution.py:403
  40.3 8.4 %collective-permute-done.28 = bf16[6,64,1024]{2,1,0:T(8,128)(2,1)S(1)} collective-permute-done((bf16[6,64,1024]{2,1,0:T(8,128)(2,1)S(1)}, bf16[6,64,1024]{2,1,0:T(8,128)(2,1)S(1)}, u32[]{:S(2)}, u32[]{:S(2)}) %collective-permute-start.28) | collective-permute-done | bytes 786464 | tf_op jit(solution)/shard_map/ppermute | solution.py:406
  50.5 4.8 %collective-permute-done.9 = bf16[256,512]{1,0:T(8,128)(2,1)S(1)} collective-permute-done((bf16[256,512]{1,0:T(8,128)(2,1)S(1)}, bf16[256,512]{1,0:T(8,128)(2,1)S(1)}, u32[]{:S(2)}, u32[]{:S(2)}) %collective-permute-start.9) | collective-permute-done | bytes 262176 | tf_op jit(solution)/shard_map/ppermute | solution.py:409
  55.3 11.1 %collective-permute-done.10 = bf16[256,512]{1,0:T(8,128)(2,1)S(1)} collective-permute-done((bf16[256,512]{1,0:T(8,128)(2,1)S(1)}, bf16[256,512]{1,0:T(8,128)(2,1)S(1)}, u32[]{:S(2)}, u32[]{:S(2)}) %collective-permute-start.10) | collective-permute-done | bytes 262176 | tf_op jit(solution)/shard_map/ppermute | solution.py:409
  66.7 3.4 %collective-permute-done.17 = bf16[256,512]{1,0:T(8,128)(2,1)S(1)} collective-permute-done((bf16[256,512]{1,0:T(8,128)(2,1)S(1)}, bf16[256,512]{1,0:T(8,128)(2,1)S(1)}, u32[]{:S(2)}, u32[]{:S(2)}) %collective-permute-start.17) | collective-permute-done | bytes 262176 | tf_op jit(solution)/shard_map/ppermute | solution.py:409
  70.0 5.0 %collective-permute-done.18 = bf16[256,512]{1,0:T(8,128)(2,1)S(1)} collective-permute-done((bf16[256,512]{1,0:T(8,128)(2,1)S(1)}, bf16[256,512]{1,0:T(8,128)(2,1)S(1)}, u32[]{:S(2)}, u32[]{:S(2)}) %collective-permute-start.18) | collective-permute-done | bytes 262176 | tf_op jit(solution)/shard_map/ppermute | solution.py:409
  75.1 2.3 collective-permute-done.19
  84.3 13.5 %collective-permute-done.11.refs_15_ = bf16[3,256,512]{2,1,0:T(8,128)(2,1)S(1)} collective-permute-done((bf16[3,256,512]{2,1,0:T(8,128)(2,1)S(1)}, bf16[3,256,512]{2,1,0:T(8,128)(2,1)S(1)}, u32[]{:S(2)}, u32[]{:S(2)}) %collective-permute-start.11) | collective-permute-done | bytes 786464 | tf_op jit(solution)/shard_map/ppermute | solution.py:403
  102.8 9.0 %prep.3 = (bf16[24,64,1024]{2,1,0:T(8,128)(2,1)}, bf16[24,64,1024]{2,1,0:T(8,128)(2,1)}) custom-call(s32[24]{0:T(128)} %get-tuple-element.53.perm_ref.refs_4_, s32[24]{0:T(128)} %get-tuple-element.54.sorted_ref.refs_2_, bf16[24,64,1024]{2,1,0:T(8,128)(2,1)} %pad_maximum_fusion.x_ref, bf16[24,64,1024]{2,1,0:T(8,128)(2,1)} %pad_maximum_fusion.1.g_ref, ...), custom_call_target="tpu_custom_call" | custom-call | tf_op jit(solution)/shard_map/prep/pallas_call | solution.py:108
  113.4 13.7 %chunk.4 = (f32[1536,1024]{1,0:T(8,128)}, f32[1536,1024]{1,0:T(8,128)}) custom-call(s32[2]{0:T(128)} %get-tuple-element.62.refs_0_, s32[2]{0:T(128)} %get-tuple-element.61.refs_1_, s32[24]{0:T(128)} %get-tuple-element.54.sorted_ref.refs_2_, s32[2]{0:T(128)} %pad_add_fusion.1.refs_3_, s32[24]{0:T(128)} %get-tuple-element.53.perm_ref.refs_4_, ...), custom_call_target="tpu_custom_call" | custom-call | flops 6442450944 | bytes 34603008 | tf_op jit(solution)/shard_map/chunk/pallas_call | solution.py:299
  127.1 8.9 %collective-permute-done.30.refs_15_ = bf16[3,256,256]{2,1,0:T(8,128)(2,1)S(1)} collective-permute-done((bf16[3,256,256]{2,1,0:T(8,128)(2,1)S(1)}, bf16[3,256,256]{2,1,0:T(8,128)(2,1)S(1)}, u32[]{:S(2)}, u32[]{:S(2)}) %collective-permute-start.30) | collective-permute-done | bytes 393248 | tf_op jit(solution)/shard_map/ppermute | solution.py:403
  137.1 19.0 %chunk.5 = (f32[12,64,1024]{2,1,0:T(8,128)}, f32[12,64,1024]{2,1,0:T(8,128)}, bf16[2,6,64,1024]{3,2,1,0:T(8,128)(2,1)}, bf16[2,6,64,1024]{3,2,1,0:T(8,128)(2,1)}) custom-call(s32[2]{0:T(128)} %get-tuple-element.62.refs_0_, s32[2]{0:T(128)} %get-tuple-element.61.refs_1_, s32[24]{0:T(128)} %get-tuple-element.54.sorted_ref.refs_2_, s32[2]{0:T(128)} %pad_add_fusion.1.refs_3_, ...), custom_call_target="tpu_custom_call" | custom-call | flops 6442450944 | bytes 34603008 | tf_op jit(solution)/shard_map/chunk/pallas_call | solution.py:299
  159.8 3.3 %add_convert_fusion = bf16[2,6,64,1024]{3,2,1,0:T(8,128)(2,1)} fusion(bf16[2,6,64,1024]{3,2,1,0:T(8,128)(2,1)S(1)} %collective-permute-done.31, bf16[2,6,64,1024]{3,2,1,0:T(8,128)(2,1)} %get-tuple-element.38), kind=kLoop, calls=%fused_computation.2 | loop fusion | flops 3145728 | bytes 4718592 | tf_op jit(solution)/shard_map/convert_element_type | solution.py:487
  166.6 2.9 %collective-permute-start.22 = (bf16[256,512]{1,0:T(8,128)(2,1)S(1)}, bf16[256,512]{1,0:T(8,128)(2,1)S(1)}, u32[]{:S(2)}, u32[]{:S(2)}) collective-permute-start(bf16[256,512]{1,0:T(8,128)(2,1)S(1)} %copy-done.18), channel_id=1, source_target_pairs={{0,8},{1,9},{2,10},{3,11},{4,12},{5,13},{6,14},{7,15},{8,0},{9,1},... | collective-permute-start | bytes 786440 | tf_op jit(solution)/shard_map/ppermute | solution.py:409
  169.5 11.1 %collective-permute-done.34 = bf16[256,512]{1,0:T(8,128)(2,1)S(1)} collective-permute-done((bf16[256,512]{1,0:T(8,128)(2,1)S(1)}, bf16[256,512]{1,0:T(8,128)(2,1)S(1)}, u32[]{:S(2)}, u32[]{:S(2)}) %collective-permute-start.34) | collective-permute-done | bytes 262176 | tf_op jit(solution)/shard_map/ppermute | solution.py:409
  181.2 11.8 %collective-permute-done.35 = bf16[256,512]{1,0:T(8,128)(2,1)S(1)} collective-permute-done((bf16[256,512]{1,0:T(8,128)(2,1)S(1)}, bf16[256,512]{1,0:T(8,128)(2,1)S(1)}, u32[]{:S(2)}, u32[]{:S(2)}) %collective-permute-start.35) | collective-permute-done | bytes 262176 | tf_op jit(solution)/shard_map/ppermute | solution.py:409
  197.6 5.2 %collective-permute-done.22 = bf16[256,512]{1,0:T(8,128)(2,1)S(1)} collective-permute-done((bf16[256,512]{1,0:T(8,128)(2,1)S(1)}, bf16[256,512]{1,0:T(8,128)(2,1)S(1)}, u32[]{:S(2)}, u32[]{:S(2)}) %collective-permute-start.22) | collective-permute-done | bytes 262176 | tf_op jit(solution)/shard_map/ppermute | solution.py:409
  209.3 5.2 %prep.2 = (bf16[12,64,1024]{2,1,0:T(8,128)(2,1)}, bf16[12,64,1024]{2,1,0:T(8,128)(2,1)}) custom-call(s32[12]{0:T(128)} %get-tuple-element.57.perm_ref.refs_4_, s32[12]{0:T(128)} %get-tuple-element.58.sorted_ref.refs_2_, bf16[12,64,1024]{2,1,0:T(8,128)(2,1)} %pad_maximum_fusion.3.x_ref, bf16[12,64,1024]{2,1,0:T(8,128)(2,1)} %pad_maximum_fusion.4.g_ref, ...), custom_call_target="tpu_custom_call" | custom-call | tf_op jit(solution)/shard_map/prep/pallas_call | solution.py:108
  215.3 7.1 %chunk.6 = (f32[768,1024]{1,0:T(8,128)}, f32[768,1024]{1,0:T(8,128)}) custom-call(s32[2]{0:T(128)} %get-tuple-element.64.refs_0_, s32[2]{0:T(128)} %get-tuple-element.63.refs_1_, s32[12]{0:T(128)} %get-tuple-element.58.sorted_ref.refs_2_, s32[2]{0:T(128)} %pad_add_fusion.1.refs_3_, ...), custom_call_target="tpu_custom_call", output_to_operand_aliasing={{0}: (12, {}), {1}: (13, {})} | custom-call | flops 2147483648 | bytes 17825792 | tf_op jit(solution)/shard_map/chunk/pallas_call | solution.py:299
  222.5 7.1 %collective-permute-done.32.refs_11_ = bf16[3,256,512]{2,1,0:T(8,128)(2,1)} collective-permute-done((bf16[3,256,512]{2,1,0:T(8,128)(2,1)S(1)}, bf16[3,256,512]{2,1,0:T(8,128)(2,1)}, u32[]{:S(2)}, u32[]{:S(2)}) %collective-permute-start.32) | collective-permute-done | bytes 786464 | tf_op jit(solution)/shard_map/ppermute | solution.py:403
  229.5 10.4 %chunk.7 = (f32[6,64,1024]{2,1,0:T(8,128)}, f32[6,64,1024]{2,1,0:T(8,128)}, bf16[2,6,64,1024]{3,2,1,0:T(8,128)(2,1)}) custom-call(s32[2]{0:T(128)} %get-tuple-element.64.refs_0_, s32[2]{0:T(128)} %get-tuple-element.63.refs_1_, s32[12]{0:T(128)} %get-tuple-element.58.sorted_ref.refs_2_, s32[2]{0:T(128)} %pad_add_fusion.1.refs_3_, ...), custom_call_target="tpu_custom_call" | custom-call | flops 2147483648 | bytes 17825792 | tf_op jit(solution)/shard_map/chunk/pallas_call | solution.py:299
  240.1 3.6 %collective-permute-done.38.other_ref = bf16[2,6,64,1024]{3,2,1,0:T(8,128)(2,1)S(1)} collective-permute-done((bf16[2,6,64,1024]{3,2,1,0:T(8,128)(2,1)}, bf16[2,6,64,1024]{3,2,1,0:T(8,128)(2,1)S(1)}, u32[]{:S(2)}, u32[]{:S(2)}) %collective-permute-start.38) | collective-permute-done | bytes 1572896 | tf_op jit(solution)/shard_map/ppermute | solution.py:400
  244.8 5.9 %finish.1 = (bf16[6,64,1024]{2,1,0:T(8,128)(2,1)}, bf16[6,64,1024]{2,1,0:T(8,128)(2,1)}, f32[6,1,64]{2,1,0:T(1,128)}) custom-call(s32[6]{0:T(128)} %bitcast.85, bf16[6,64,1024]{2,1,0:T(8,128)(2,1)} %x_ref.1, bf16[6,64,1024]{2,1,0:T(8,128)(2,1)} %g_ref.1, f32[2,1024]{1,0:T(2,128)} %gain_ref.5, f32[6,64,1024]{2,1,0:T(8,128)} %get-tuple-element.47.out_ref, ...), custom_call_target="tpu_custom_call" | custom-call | tf_op jit(solution)/shard_map/finish/pallas_call | solution.py:352
  (146 shorter events, 66.4 us)
Async XLA Ops:
  3.2 22.0 %collective-permute-start.24 = (s32[6]{0:T(128)S(1)}, s32[6]{0:T(128)S(1)}, u32[]{:S(2)}, u32[]{:S(2)}) collective-permute-start(s32[6]{0:T(128)S(1)} %bitcast.86), channel_id=1, source_target_pairs={{0,16},{16,0},{1,17},{17,1},{2,18},{18,2},{3,19},{19,3},{4,20},{20... | collective-permute-start | bytes 80 | tf_op jit(solution)/shard_map/ppermute | solution.py:406
  11.7 24.9 %collective-permute-start.16 = (bf16[256,1280]{1,0:T(8,128)(2,1)}, bf16[256,1280]{1,0:T(8,128)(2,1)S(1)}, u32[]{:S(2)}, u32[]{:S(2)}) collective-permute-start(bf16[256,1280]{1,0:T(8,128)(2,1)} %bitcast.23), channel_id=1, source_target_pairs={{0,2},{1,3},{2,0},{3,1},{4,6},{5,7},{6,4},{7,5},{8,10},{9,11},{10,... | collective-permute-start | bytes 1966088 | tf_op jit(solution)/shard_map/ppermute | solution.py:403
  17.3 21.6 %collective-permute-start.26 = (bf16[6,64,1024]{2,1,0:T(8,128)(2,1)S(1)}, bf16[6,64,1024]{2,1,0:T(8,128)(2,1)S(1)}, u32[]{:S(2)}, u32[]{:S(2)}) collective-permute-start(bf16[6,64,1024]{2,1,0:T(8,128)(2,1)S(1)} %copy-done.1), channel_id=1, source_target_pairs={{0,16},{16,0},{1,17},{17,1},{2,18},{18,2},{3,19},{19,3},{4,20},{20... | collective-permute-start | bytes 2359304 | tf_op jit(solution)/shard_map/ppermute | solution.py:406
  19.3 29.4 %collective-permute-start.28 = (bf16[6,64,1024]{2,1,0:T(8,128)(2,1)S(1)}, bf16[6,64,1024]{2,1,0:T(8,128)(2,1)S(1)}, u32[]{:S(2)}, u32[]{:S(2)}) collective-permute-start(bf16[6,64,1024]{2,1,0:T(8,128)(2,1)S(1)} %copy-done.2), channel_id=1, source_target_pairs={{0,16},{16,0},{1,17},{17,1},{2,18},{18,2},{3,19},{19,3},{4,20},{20... | collective-permute-start | bytes 2359304 | tf_op jit(solution)/shard_map/ppermute | solution.py:406
  27.5 22.6 %collective-permute-start.8 = (bf16[256,512]{1,0:T(8,128)(2,1)S(1)}, bf16[256,512]{1,0:T(8,128)(2,1)S(1)}, u32[]{:S(2)}, u32[]{:S(2)}) collective-permute-start(bf16[256,512]{1,0:T(8,128)(2,1)S(1)} %get-tuple-element.71), channel_id=1, source_target_pairs={{0,4},{1,5},{2,6},{3,7},{4,8},{5,9},{6,10},{7,11},{8,12},{9,13},{1... | collective-permute-start | bytes 786440 | tf_op jit(solution)/shard_map/ppermute | solution.py:409
  36.6 29.7 %collective-permute-start.10 = (bf16[256,512]{1,0:T(8,128)(2,1)S(1)}, bf16[256,512]{1,0:T(8,128)(2,1)S(1)}, u32[]{:S(2)}, u32[]{:S(2)}) collective-permute-start(bf16[256,512]{1,0:T(8,128)(2,1)S(1)} %get-tuple-element.71), channel_id=1, source_target_pairs={{0,12},{1,13},{2,14},{3,15},{4,0},{5,1},{6,2},{7,3},{8,4},{9,5},{1... | collective-permute-start | bytes 786440 | tf_op jit(solution)/shard_map/ppermute | solution.py:409
  38.9 31.2 %collective-permute-start.17 = (bf16[256,512]{1,0:T(8,128)(2,1)S(1)}, bf16[256,512]{1,0:T(8,128)(2,1)S(1)}, u32[]{:S(2)}, u32[]{:S(2)}) collective-permute-start(bf16[256,512]{1,0:T(8,128)(2,1)S(1)} %get-tuple-element.32), channel_id=1, source_target_pairs={{0,4},{1,5},{2,6},{3,7},{4,8},{5,9},{6,10},{7,11},{8,12},{9,13},{1... | collective-permute-start | bytes 786440 | tf_op jit(solution)/shard_map/ppermute | solution.py:409
  48.7 26.4 %collective-permute-start.18 = (bf16[256,512]{1,0:T(8,128)(2,1)S(1)}, bf16[256,512]{1,0:T(8,128)(2,1)S(1)}, u32[]{:S(2)}, u32[]{:S(2)}) collective-permute-start(bf16[256,512]{1,0:T(8,128)(2,1)S(1)} %get-tuple-element.32), channel_id=1, source_target_pairs={{0,8},{1,9},{2,10},{3,11},{4,12},{5,13},{6,14},{7,15},{8,0},{9,1},... | collective-permute-start | bytes 786440 | tf_op jit(solution)/shard_map/ppermute | solution.py:409
  50.1 27.3 %collective-permute-start.19 = (bf16[256,512]{1,0:T(8,128)(2,1)S(1)}, bf16[256,512]{1,0:T(8,128)(2,1)S(1)}, u32[]{:S(2)}, u32[]{:S(2)}) collective-permute-start(bf16[256,512]{1,0:T(8,128)(2,1)S(1)} %get-tuple-element.32), channel_id=1, source_target_pairs={{0,12},{1,13},{2,14},{3,15},{4,0},{5,1},{6,2},{7,3},{8,4},{9,5},{1... | collective-permute-start | bytes 786440 | tf_op jit(solution)/shard_map/ppermute | solution.py:409
  55.3 25.1 %collective-permute-start.1 = (bf16[6,64,1024]{2,1,0:T(8,128)(2,1)S(1)}, bf16[6,64,1024]{2,1,0:T(8,128)(2,1)S(1)}, u32[]{:S(2)}, u32[]{:S(2)}) collective-permute-start(bf16[6,64,1024]{2,1,0:T(8,128)(2,1)S(1)} %copy-done.1), channel_id=1, source_target_pairs={{0,1},{1,0},{2,3},{3,2},{4,5},{5,4},{6,7},{7,6},{8,9},{9,8},{10,11... | collective-permute-start | bytes 2359304 | tf_op jit(solution)/shard_map/ppermute | solution.py:400
  70.0 27.8 %collective-permute-start.2 = (bf16[6,64,1024]{2,1,0:T(8,128)(2,1)S(1)}, bf16[6,64,1024]{2,1,0:T(8,128)(2,1)S(1)}, u32[]{:S(2)}, u32[]{:S(2)}) collective-permute-start(bf16[6,64,1024]{2,1,0:T(8,128)(2,1)S(1)} %copy-done.2), channel_id=1, source_target_pairs={{0,1},{1,0},{2,3},{3,2},{4,5},{5,4},{6,7},{7,6},{8,9},{9,8},{10,11... | collective-permute-start | bytes 2359304 | tf_op jit(solution)/shard_map/ppermute | solution.py:400
  75.1 23.8 %collective-permute-start.29 = (bf16[6,64,1024]{2,1,0:T(8,128)(2,1)S(1)}, bf16[6,64,1024]{2,1,0:T(8,128)(2,1)S(1)}, u32[]{:S(2)}, u32[]{:S(2)}) collective-permute-start(bf16[6,64,1024]{2,1,0:T(8,128)(2,1)S(1)} %collective-permute-done.28), channel_id=1, source_target_pairs={{0,1},{1,0},{2,3},{3,2},{4,5},{5,4},{6,7},{7,6},{8,9},{9,8},{10,11... | collective-permute-start | bytes 2359304 | tf_op jit(solution)/shard_map/ppermute | solution.py:400
  77.4 20.4 %collective-permute-start.11 = (bf16[3,256,512]{2,1,0:T(8,128)(2,1)S(1)}, bf16[3,256,512]{2,1,0:T(8,128)(2,1)S(1)}, u32[]{:S(2)}, u32[]{:S(2)}) collective-permute-start(bf16[3,256,512]{2,1,0:T(8,128)(2,1)S(1)} %pad_maximum_fusion.5.refs_14_), channel_id=1, source_target_pairs={{0,2},{1,3},{2,0},{3,1},{4,6},{5,7},{6,4},{7,5},{8,10},{9,11},{10,... | collective-permute-start | bytes 2359304 | tf_op jit(solution)/shard_map/ppermute | solution.py:403
  80.4 46.7 %collective-permute-start.7 = (bf16[256,1280]{1,0:T(8,128)(2,1)}, bf16[256,1280]{1,0:T(8,128)(2,1)S(1)}, u32[]{:S(2)}, u32[]{:S(2)}) collective-permute-start(bf16[256,1280]{1,0:T(8,128)(2,1)} %bitcast.8), channel_id=1, source_target_pairs={{0,2},{1,3},{2,0},{3,1},{4,6},{5,7},{6,4},{7,5},{8,10},{9,11},{10,... | collective-permute-start | bytes 1966088 | tf_op jit(solution)/shard_map/ppermute | solution.py:403
  81.0 55.1 %collective-permute-start.20 = (bf16[3,256,512]{2,1,0:T(8,128)(2,1)S(1)}, bf16[3,256,512]{2,1,0:T(8,128)(2,1)S(1)}, u32[]{:S(2)}, u32[]{:S(2)}) collective-permute-start(bf16[3,256,512]{2,1,0:T(8,128)(2,1)S(1)} %pad_maximum_fusion.6.refs_10_), channel_id=1, source_target_pairs={{0,2},{1,3},{2,0},{3,1},{4,6},{5,7},{6,4},{7,5},{8,10},{9,11},{10,... | collective-permute-start | bytes 2359304 | tf_op jit(solution)/shard_map/ppermute | solution.py:403
  111.8 24.2 %collective-permute-start.30 = (bf16[3,256,256]{2,1,0:T(8,128)(2,1)S(1)}, bf16[3,256,256]{2,1,0:T(8,128)(2,1)S(1)}, u32[]{:S(2)}, u32[]{:S(2)}) collective-permute-start(bf16[3,256,256]{2,1,0:T(8,128)(2,1)S(1)} %pad_maximum_fusion.12.refs_14_), channel_id=1, source_target_pairs={{0,2},{1,3},{2,0},{3,1},{4,6},{5,7},{6,4},{7,5},{8,10},{9,11},{10,... | collective-permute-start | bytes 1179656 | tf_op jit(solution)/shard_map/ppermute | solution.py:403
  157.2 23.4 %collective-permute-start.34 = (bf16[256,512]{1,0:T(8,128)(2,1)S(1)}, bf16[256,512]{1,0:T(8,128)(2,1)S(1)}, u32[]{:S(2)}, u32[]{:S(2)}) collective-permute-start(bf16[256,512]{1,0:T(8,128)(2,1)S(1)} %copy-done.19), channel_id=1, source_target_pairs={{0,8},{1,9},{2,10},{3,11},{4,12},{5,13},{6,14},{7,15},{8,0},{9,1},... | collective-permute-start | bytes 786440 | tf_op jit(solution)/shard_map/ppermute | solution.py:409
  163.1 59.3 %collective-permute-start.37 = (bf16[2,6,64,1024]{3,2,1,0:T(8,128)(2,1)}, bf16[2,6,64,1024]{3,2,1,0:T(8,128)(2,1)S(1)}, u32[]{:S(2)}, u32[]{:S(2)}) collective-permute-start(bf16[2,6,64,1024]{3,2,1,0:T(8,128)(2,1)} %add_convert_fusion), channel_id=1, source_target_pairs={{0,16},{16,0},{1,17},{17,1},{2,18},{18,2},{3,19},{19,3},{4,20},{20... | collective-permute-start | bytes 4718600 | tf_op jit(solution)/shard_map/ppermute | solution.py:406
  164.5 28.5 %collective-permute-start.35 = (bf16[256,512]{1,0:T(8,128)(2,1)S(1)}, bf16[256,512]{1,0:T(8,128)(2,1)S(1)}, u32[]{:S(2)}, u32[]{:S(2)}) collective-permute-start(bf16[256,512]{1,0:T(8,128)(2,1)S(1)} %copy-done.19), channel_id=1, source_target_pairs={{0,12},{1,13},{2,14},{3,15},{4,0},{5,1},{6,2},{7,3},{8,4},{9,5},{1... | collective-permute-start | bytes 786440 | tf_op jit(solution)/shard_map/ppermute | solution.py:409
  164.5 33.0 %collective-permute-start.21 = (bf16[256,512]{1,0:T(8,128)(2,1)S(1)}, bf16[256,512]{1,0:T(8,128)(2,1)S(1)}, u32[]{:S(2)}, u32[]{:S(2)}) collective-permute-start(bf16[256,512]{1,0:T(8,128)(2,1)S(1)} %copy-done.18), channel_id=1, source_target_pairs={{0,4},{1,5},{2,6},{3,7},{4,8},{5,9},{6,10},{7,11},{8,12},{9,13},{1... | collective-permute-start | bytes 786440 | tf_op jit(solution)/shard_map/ppermute | solution.py:409
  166.6 36.1 %collective-permute-start.22 = (bf16[256,512]{1,0:T(8,128)(2,1)S(1)}, bf16[256,512]{1,0:T(8,128)(2,1)S(1)}, u32[]{:S(2)}, u32[]{:S(2)}) collective-permute-start(bf16[256,512]{1,0:T(8,128)(2,1)S(1)} %copy-done.18), channel_id=1, source_target_pairs={{0,8},{1,9},{2,10},{3,11},{4,12},{5,13},{6,14},{7,15},{8,0},{9,1},... | collective-permute-start | bytes 786440 | tf_op jit(solution)/shard_map/ppermute | solution.py:409
  180.6 23.6 %collective-permute-start.23 = (bf16[256,512]{1,0:T(8,128)(2,1)S(1)}, bf16[256,512]{1,0:T(8,128)(2,1)S(1)}, u32[]{:S(2)}, u32[]{:S(2)}) collective-permute-start(bf16[256,512]{1,0:T(8,128)(2,1)S(1)} %copy-done.18), channel_id=1, source_target_pairs={{0,12},{1,13},{2,14},{3,15},{4,0},{5,1},{6,2},{7,3},{8,4},{9,5},{1... | collective-permute-start | bytes 786440 | tf_op jit(solution)/shard_map/ppermute | solution.py:409
  193.1 21.3 %collective-permute-start.36 = (bf16[3,256,512]{2,1,0:T(8,128)(2,1)S(1)}, bf16[3,256,512]{2,1,0:T(8,128)(2,1)S(1)}, u32[]{:S(2)}, u32[]{:S(2)}) collective-permute-start(bf16[3,256,512]{2,1,0:T(8,128)(2,1)S(1)} %pad_maximum_fusion.8.refs_10_), channel_id=1, source_target_pairs={{0,2},{1,3},{2,0},{3,1},{4,6},{5,7},{6,4},{7,5},{8,10},{9,11},{10,... | collective-permute-start | bytes 2359304 | tf_op jit(solution)/shard_map/ppermute | solution.py:403
  204.3 25.3 %collective-permute-start.32 = (bf16[3,256,512]{2,1,0:T(8,128)(2,1)S(1)}, bf16[3,256,512]{2,1,0:T(8,128)(2,1)}, u32[]{:S(2)}, u32[]{:S(2)}) collective-permute-start(bf16[3,256,512]{2,1,0:T(8,128)(2,1)S(1)} %pad_maximum_fusion.7.refs_10_), channel_id=1, source_target_pairs={{0,2},{1,3},{2,0},{3,1},{4,6},{5,7},{6,4},{7,5},{8,10},{9,11},{10,... | collective-permute-start | bytes 2359304 | tf_op jit(solution)/shard_map/ppermute | solution.py:403
  (39 other events, 430.2 us)

commit v6 on v5

--- a/solution.py
+++ b/solution.py
@@ -147,13 +147,15 @@
 
         for part in range(parts):
             cols = pl.ds(sum(units[:part]), units[part])
-            (own, start), (own_y, start_y), here, there = pieces[4 * part : 4 * part + 4]
-            put(own.at[member, :, pl.ds(start, units[part])], z, y, cols)
-            put(own_y.at[:, pl.ds(start_y, units[part])], z, 1 - y, cols)
+            own, own_y, here, there = (
+                (ref, pl.ds(start, units[part])) for ref, start in pieces[4 * part : 4 * part + 4]
+            )
+            put(own[0].at[member, :, own[1]], z, y, cols)
+            put(own_y[0].at[:, own_y[1]], z, 1 - y, cols)
             for d in range(1, lines):
                 from_z = lax.rem(z + lines - d, lines)
-                put(here.at[d - 1], from_z, y, cols)
-                put(there.at[d - 1], from_z, 1 - y, cols)
+                put(here[0].at[d - 1, :, here[1]], from_z, y, cols)
+                put(there[0].at[d - 1, :, there[1]], from_z, 1 - y, cols)
         for copy in copies:
             copy.start()
         for copy in copies:
@@ -254,9 +256,9 @@
     first, _, last = kind
     rows, seq, width = lifted.shape
     tokens = rows * seq
-    units = [part[2].shape[2] for part in pieces]
-    lines = pieces[0][2].shape[0] + 1
-    depth2 = pieces[0][2].shape[1]
+    units = [part[0] for part in pieces]
+    lines = pieces[0][3][0].shape[0] + 1
+    depth2 = pieces[0][3][0].shape[1]
     hidden = sum(units)
     size = per_block * seq
 
@@ -269,9 +271,9 @@
     hbm = pl.BlockSpec(memory_space=pl.ANY)
     args = [*scalars, lifted.reshape(tokens, width), g.reshape(tokens, width)]
     starts = []
-    for own, own_y, here, there in pieces:
-        args += [own[0], own_y[0], here, there]
-        starts.append((own[1], own_y[1]))
+    for _, *four in pieces:
+        args += [array for array, _ in four]
+        starts += [start for _, start in four]
     specs = [tok, tok] + [hbm] * (4 * len(pieces))
     alias = {}
     out_specs = [tok, tok]
@@ -291,9 +293,8 @@
     def kernel(*refs):
         refs = list(refs)
         base = len(scalars) + 2
-        for part, (own, own_y) in enumerate(starts):
-            refs[base + 4 * part] = (refs[base + 4 * part], own)
-            refs[base + 4 * part + 1] = (refs[base + 4 * part + 1], own_y)
+        for i, start in enumerate(starts):
+            refs[base + i] = (refs[base + i], start)
         chunk_kernel(member, per_block, seq, kind, units, *refs)
 
     return pl.pallas_call(
@@ -321,8 +322,8 @@
 
 
 def finish_kernel(
-    member_ref, x_ref, g_ref, gain_ref, out_ref, back_ref, other_ref, across_ref,
-    value_ref, grad_ref, coupling_ref,
+    member_ref, x_ref, g_ref, gain_ref, out_ref, back_ref, other_ref, across_out_ref,
+    across_back_ref, value_ref, grad_ref, coupling_ref,
 ):
     rows, seq, width = x_ref.shape
     diagonal = lax.broadcasted_iota(jnp.int32, (seq, seq), 0) == lax.broadcasted_iota(
@@ -334,17 +335,17 @@
         normed = x * inv
         gain = gain_ref[pl.ds(member_ref[pl.program_id(0) * rows + r], 1), :]
         back = gain * (
-            back_ref[r] + other_ref[1, r].astype(F32) + across_ref[1, r].astype(F32)
+            back_ref[r] + other_ref[1, r].astype(F32) + across_back_ref[r].astype(F32)
         )
         stat = jnp.sum(normed * back, axis=1, keepdims=True) / width
-        out = out_ref[r] + other_ref[0, r].astype(F32) + across_ref[0, r].astype(F32)
+        out = out_ref[r] + other_ref[0, r].astype(F32) + across_out_ref[r].astype(F32)
         value_ref[r] = (x + out).astype(BF16)
         grad_ref[r] = (g_ref[r].astype(F32) + (back - normed * stat) * inv).astype(BF16)
         line = jnp.sum(jnp.where(diagonal, stat, 0.0), axis=0, keepdims=True)
-        coupling_ref[r] = line * math.sqrt(width)
-
-
-def finish(member_own, x, g, gain, out, back, other, across):
+        coupling_ref[pl.ds(pl.program_id(0) * rows + r, 1), :] = line * math.sqrt(width)
+
+
+def finish(member_own, x, g, gain, out, back, other, across_out, across_back):
     rows, seq, width = x.shape
     step = math.gcd(rows, 2)
     row = pl.BlockSpec((step, seq, width), lambda r, mem: (r, 0, 0))
@@ -355,18 +356,18 @@
             num_scalar_prefetch=1,
             grid=(rows // step,),
             in_specs=[
-                row, row, pl.BlockSpec(gain.shape, lambda r, mem: (0, 0)), row, row, two, two
+                row, row, pl.BlockSpec(gain.shape, lambda r, mem: (0, 0)), row, row, two, row, row
             ],
-            out_specs=[row, row, pl.BlockSpec((step, 1, seq), lambda r, mem: (r, 0, 0))],
+            out_specs=[row, row, pl.BlockSpec((rows, seq), lambda r, mem: (0, 0))],
         ),
         out_shape=[
             jax.ShapeDtypeStruct((rows, seq, width), BF16),
             jax.ShapeDtypeStruct((rows, seq, width), BF16),
-            jax.ShapeDtypeStruct((rows, 1, seq), F32),
+            jax.ShapeDtypeStruct((rows, seq), F32),
         ],
         compiler_params=pltpu.CompilerParams(vmem_limit_bytes=VMEM_LIMIT),
         name="finish",
-    )(member_own, x, g, gain, out, back, other, across)
+    )(member_own, x, g, gain, out, back, other, across_out, across_back)
 
 
 def sort_rows(picks, members, per_block):
@@ -431,80 +432,108 @@
         [jnp.where(even, mine, theirs), jnp.where(even, theirs, mine)], axis=2
     ).reshape(members, 4 * depth, quarter + half)
 
+    third = quarter // 3
+    groups = [
+        [(0, 0, third)],
+        [(0, third, 2 * third)],
+        [(1, 0, 2 * third)],
+        [(1, 2 * third, third), (0, quarter, half // 2)],
+        [(0, quarter + half // 2, half // 2), (1, quarter, half // 2)],
+        [(1, quarter + half // 2, half // 2)],
+    ]
+    send = [
+        jnp.concatenate([shard[m, :, at : at + n] for m, at, n in group], axis=1)
+        for group in groups
+    ]
+    here, there, own_y = [], [], []
+
+    def exchange(step, arrived):
+        results = []
+        if step < len(groups):
+            mine = after(send[step], *arrived)
+            results += [shift_z(mine, d) for d in range(1, lines)]
+        if step > 0:
+            there.append(over_y(after(here[step - 1], *arrived)))
+            results.append(there[-1])
+        if step < len(groups):
+            here.append(jnp.stack(results[: lines - 1]))
+        return results
+
+    def piece(group, i):
+        member, start, units = groups[group][i]
+        at = sum(n for _, _, n in groups[group][:i])
+        return (
+            units, (shard, start), (own_y[member], start), (here[group], at), (there[group], at)
+        )
+
     pick_own = member_pick[:, 0]
-    x_over, g_over, pick_over = over_x(tokens_in), over_x(upstream), over_x(pick_own)
+    pick_over = over_x(pick_own)
     pick_pair = jnp.concatenate([pick_own, partner(pick_own)])
     pick_all = jnp.concatenate([pick_pair, pick_over, partner(pick_over)])
-    x_pair = jnp.concatenate([tokens_in, partner(tokens_in)])
-    g_pair = jnp.concatenate([upstream, partner(upstream)])
-    x_all = jnp.concatenate([x_pair, x_over, partner(x_over)])
-    g_all = jnp.concatenate([g_pair, g_over, partner(g_over)])
     per_block = math.gcd(2 * rows, 4)
     place = jnp.stack([y_at, rank // 4])
+    index = jnp.arange(4 * rows, dtype=jnp.int32)
     pos, perm, member_sorted, low, high = sort_rows(pick_pair, members, per_block)
-    index = jnp.arange(4 * rows, dtype=jnp.int32)
     scalars_alone = (low, high, member_sorted, place, perm, lax.rem(index[: 2 * rows], rows))
+    _, perm_all, member_sorted_all, low, high = sort_rows(pick_all, members, per_block)
+    dest = jnp.concatenate([pos, lax.rem(index[2 * rows :], rows)])
+    scalars_shared = (low, high, member_sorted_all, place, perm_all, dest)
+
+    arrived = exchange(0, [])
+    own_y.append(over_y(shard[0]))
+    x_over, x_partner, g_partner = over_x(tokens_in), partner(tokens_in), partner(upstream)
+    arrived += [own_y[0], x_over, x_partner, g_partner]
+
+    set_0, arrived = arrived, exchange(1, arrived)
+    g_over, x_other = over_x(after(upstream, *set_0)), partner(after(x_over, *set_0))
+    arrived += [g_over, x_other]
+
+    set_1, arrived = arrived, exchange(2, arrived)
+    own_y.append(over_y(after(shard[1], *set_1)))
+    g_other = partner(after(g_over, *set_1))
+    arrived += [own_y[1], g_other]
+
+    set_2, arrived = arrived, exchange(3, arrived)
+    x_all = jnp.concatenate([tokens_in, x_partner, x_over, after(x_other, *set_2)])
+    g_all = jnp.concatenate([upstream, g_partner, g_over, g_other])
+    lifted_shared, g_shared = prep(perm_all, member_sorted_all, x_all, g_all, norm_gain)
+    sums = chunk(
+        0, (True, False, False), per_block, scalars_shared, lifted_shared, g_shared,
+        [piece(0, 0), piece(1, 0)], None,
+    )
+    arrived += [sums[0]]
+
+    set_3, arrived = arrived, exchange(4, arrived)
+    x_pair = jnp.concatenate([tokens_in, after(x_partner, *set_3)])
+    g_pair = jnp.concatenate([upstream, g_partner])
     lifted_alone, g_alone = prep(perm, member_sorted, x_pair, g_pair, norm_gain)
-    _, perm, member_sorted, low, high = sort_rows(pick_all, members, per_block)
-    dest = jnp.concatenate([pos, lax.rem(index[2 * rows :], rows)])
-    scalars_shared = (low, high, member_sorted, place, perm, dest)
-    lifted_shared, g_shared = prep(perm, member_sorted, x_all, g_all, norm_gain)
-
-    third = quarter // 3
-    transfers = [
-        (0, 0, third),
-        (0, third, 2 * third),
-        (1, 0, 2 * third),
-        (1, 2 * third, third),
-        (0, quarter, half),
-        (1, quarter, half),
-    ]
-    z_done, y_done, own_y, pieces = [], [], {}, []
-    for at, (member, start, size) in enumerate(transfers):
-        mine = shard[member, :, start : start + size]
-        waits = []
-        if at >= 2:
-            waits += [z_done[at - 2], y_done[at - 2 if at < 4 else at - 3]]
-        if at == 2:
-            waits.append(own_y[0])
-        if at == 4:
-            waits.append(own_y[1])
-        if waits:
-            mine = after(mine, *waits)
-        if at in (0, 1):
-            own_y[at] = over_y(after(shard[at], *z_done[:at]))
-        here = jnp.stack([shift_z(mine, d) for d in range(1, lines)])
-        z_done.append(here)
-        if at == 4:
-            sums = chunk(
-                0, (True, False, False), per_block, scalars_shared, lifted_shared, g_shared,
-                pieces[0:2], None,
-            )
-            out, back, over_same, over_other = chunk(
-                1, (False, True, True), per_block, scalars_shared, lifted_shared, g_shared,
-                pieces[2:4], sums, (2 * rows, rows, rows),
-            )
-            across = (over_same.astype(F32) + partner(over_other).astype(F32)).astype(BF16)
-        if at == 5:
-            here = after(here, across)
-            across = over_x(across)
-        there = over_y(here)
-        y_done.append(there)
-        pieces.append(((shard, start), (own_y[member], start), here, there))
-
+    arrived += [lifted_alone]
+
+    set_4, arrived = arrived, exchange(5, arrived)
+    out, back, over_same, over_other = chunk(
+        1, (False, True, True), per_block, scalars_shared, lifted_shared, g_shared,
+        [piece(2, 0), piece(3, 0)], (after(sums[0], *set_4), sums[1]), (2 * rows, rows, rows),
+    )
+
+    exchange(6, arrived)
+    across = (over_same.astype(F32) + partner(over_other).astype(F32)).astype(BF16)
+    across_out = over_x(across[0])
+    across_back = over_x(after(across[1], across_out))
     sums = chunk(
-        0, (False, False, False), per_block, scalars_alone, lifted_alone, g_alone, pieces[4:5],
-        (out, back),
-    )
-    sums = (after(sums[0], across), sums[1])
+        0, (False, False, False), per_block, scalars_alone, lifted_alone, g_alone,
+        [piece(3, 1), piece(4, 0)], (after(out, across), back),
+    )
     out, back, packed = chunk(
-        1, (False, False, True), per_block, scalars_alone, lifted_alone, g_alone, pieces[5:6], sums,
+        1, (False, False, True), per_block, scalars_alone, lifted_alone, g_alone,
+        [piece(4, 1), piece(5, 0)], (after(sums[0], across_out, across_back), sums[1]),
         (rows, rows),
     )
-    value_out, grad_in, coupling = finish(
-        pick_own, tokens_in, upstream, norm_gain, out, back, partner(packed), across
-    )
-    return value_out, grad_in, coupling.reshape(rows, seq)
+    return tuple(
+        finish(
+            pick_own, tokens_in, upstream, norm_gain, out, back, partner(packed),
+            across_out, across_back,
+        )
+    )
 
 
 def solution(mesh):

time: 253 us -> 243 us (0.960)
  waiting for transfers between devices: 117 us -> 92.8 us
  starting transfers between devices: 37.9 us -> 48.2 us
  other arithmetic: 19.3 us -> 22.7 us
    ppermute x8, waiting for transfers between devices: 37.5 us -> 9.69 us  [over_y(): return lax.ppermute(a, 'row', [(i, i ^ 2) for i in range(ranks)])]
    ppermute x18, starting transfers between devices: 20 us -> 34.2 us  [shift_z(): lax.ppermute(a, 'row', [(i, (i + 4 * d) % ranks) for i in range(ranks)])]
    ppermute x4 -> x5, waiting for transfers between devices: 8.43 us -> 22.1 us  [over_x(): return lax.ppermute(a, 'grp', [(0, 1), (1, 0)])]
    ppermute x18, waiting for transfers between devices: 63.1 us -> 53.8 us  [shift_z(): lax.ppermute(a, 'row', [(i, (i + 4 * d) % ranks) for i in range(ranks)])]
    ppermute x8, starting transfers between devices: 11.5 us -> 8.48 us  [over_y(): return lax.ppermute(a, 'row', [(i, i ^ 2) for i in range(ranks)])]
    concatenate x4 -> x5, other arithmetic: 6.39 us -> 9.42 us  [the longest x1 4.53 us: on_device_shared(): jnp.concatenate([tokens_in, x_partner, x_over, after(x_other, *set_2)])]
    ppermute x4 -> x5, starting transfers between devices: 5.92 us -> 4.3 us  [over_x(): return lax.ppermute(a, 'grp', [(0, 1), (1, 0)])]
    unnamed x49 -> x64, local copies, waits for them, and re-layouts: 5.32 us -> 4.79 us
  transfers between devices with their start and end apart: 39 -> 40, of which waited for: 23 -> 17; matrix products, arithmetic and copies ran while one was open for 8% -> 9% of each run, Pallas kernels for 14% -> 14%
where the time goes in v6:
time: 243 us
  waiting for transfers between devices  92.8 us (38%)
  Pallas kernels  70.9 us (29%)
  starting transfers between devices  48.2 us (20%)
  other arithmetic  22.7 us (9%)
  local copies, waits for them, and re-layouts  6.66 us (3%)
    ppermute x18, waiting for transfers between devices, shift_z(): lax.ppermute(a, 'row', [(i, (i + 4 * d) % ranks) for i in range(ranks)])  53.8 us
    pallas_call x4, Pallas kernels, chunk(): pl.pallas_call(kernel, grid_spec=pltpu.PrefetchScalarGridSpec(num_scalar_...  51.1 us
    ppermute x18, starting transfers between devices, shift_z(): lax.ppermute(a, 'row', [(i, (i + 4 * d) % ranks) for i in range(ranks)])  34.2 us
    ppermute x5, waiting for transfers between devices, over_x(): return lax.ppermute(a, 'grp', [(0, 1), (1, 0)])  22.1 us
    pallas_call x2, Pallas kernels, prep(): pl.pallas_call(prep_kernel, in_specs=[smem, smem, vmem, vmem, vmem], out_...  13.9 us
    ppermute x8, waiting for transfers between devices, over_y(): return lax.ppermute(a, 'row', [(i, i ^ 2) for i in range(ranks)])  9.69 us
    ppermute x8, starting transfers between devices, over_y(): return lax.ppermute(a, 'row', [(i, i ^ 2) for i in range(ranks)])  8.48 us
    ppermute x9, waiting for transfers between devices, partner(): return lax.ppermute(a, 'row', [(i, i ^ 1) for i in range(ranks)])  7.23 us
  transfers between devices with their start and end apart: 40, of which 17 were waited for; matrix products, arithmetic and copies ran while one was open for 9% of the time, Pallas kernels for 14%

profile of v6, /device:TPU:8, one launch (start us, length us, event | category | flops | bytes accessed | tf_op | source)
XLA Modules:
  0.0 242.6 jit_solution(1120578795914757328)
XLA Ops:
  10.7 3.8 %collective-permute-done.3 = bf16[256,256]{1,0:T(8,128)(2,1)S(1)} collective-permute-done((bf16[256,256]{1,0:T(8,128)(2,1)S(1)}, bf16[256,256]{1,0:T(8,128)(2,1)S(1)}, u32[]{:S(2)}, u32[]{:S(2)}) %collective-permute-start.3) | collective-permute-done | bytes 131104 | tf_op jit(solution)/shard_map/ppermute | solution.py:410
  17.2 4.9 %collective-permute-done.4 = bf16[256,256]{1,0:T(8,128)(2,1)S(1)} collective-permute-done((bf16[256,256]{1,0:T(8,128)(2,1)S(1)}, bf16[256,256]{1,0:T(8,128)(2,1)S(1)}, u32[]{:S(2)}, u32[]{:S(2)}) %collective-permute-start.4) | collective-permute-done | bytes 131104 | tf_op jit(solution)/shard_map/ppermute | solution.py:410
  30.0 5.2 %collective-permute-start.10 = (bf16[256,512]{1,0:T(8,128)(2,1)}, bf16[256,512]{1,0:T(8,128)(2,1)}, u32[]{:S(2)}, u32[]{:S(2)}) collective-permute-start(bf16[256,512]{1,0:T(8,128)(2,1)} %get-tuple-element.39), channel_id=1, source_target_pairs={{0,8},{1,9},{2,10},{3,11},{4,12},{5,13},{6,14},{7,15},{8,0},{9,1},... | collective-permute-start | bytes 786440 | tf_op jit(solution)/shard_map/ppermute | solution.py:410
  39.3 11.0 %collective-permute-done.10 = bf16[256,512]{1,0:T(8,128)(2,1)} collective-permute-done((bf16[256,512]{1,0:T(8,128)(2,1)}, bf16[256,512]{1,0:T(8,128)(2,1)}, u32[]{:S(2)}, u32[]{:S(2)}) %collective-permute-start.10) | collective-permute-done | bytes 262176 | tf_op jit(solution)/shard_map/ppermute | solution.py:410
  52.4 4.5 %collective-permute-done.11 = bf16[256,512]{1,0:T(8,128)(2,1)S(1)} collective-permute-done((bf16[256,512]{1,0:T(8,128)(2,1)}, bf16[256,512]{1,0:T(8,128)(2,1)S(1)}, u32[]{:S(2)}, u32[]{:S(2)}) %collective-permute-start.11) | collective-permute-done | bytes 262176 | tf_op jit(solution)/shard_map/ppermute | solution.py:410
  64.3 3.4 %collective-permute-start.16 = (bf16[256,512]{1,0:T(8,128)(2,1)S(1)}, bf16[256,512]{1,0:T(8,128)(2,1)S(1)}, u32[]{:S(2)}, u32[]{:S(2)}) collective-permute-start(bf16[256,512]{1,0:T(8,128)(2,1)S(1)} %copy-done.25), channel_id=1, source_target_pairs={{0,8},{1,9},{2,10},{3,11},{4,12},{5,13},{6,14},{7,15},{8,0},{9,1},... | collective-permute-start | bytes 786440 | tf_op jit(solution)/shard_map/ppermute | solution.py:410
  74.8 10.2 %collective-permute-done.16 = bf16[256,512]{1,0:T(8,128)(2,1)S(1)} collective-permute-done((bf16[256,512]{1,0:T(8,128)(2,1)S(1)}, bf16[256,512]{1,0:T(8,128)(2,1)S(1)}, u32[]{:S(2)}, u32[]{:S(2)}) %collective-permute-start.16) | collective-permute-done | bytes 262176 | tf_op jit(solution)/shard_map/ppermute | solution.py:410
  84.9 3.9 %collective-permute-done.17 = bf16[256,512]{1,0:T(8,128)(2,1)S(1)} collective-permute-done((bf16[256,512]{1,0:T(8,128)(2,1)S(1)}, bf16[256,512]{1,0:T(8,128)(2,1)S(1)}, u32[]{:S(2)}, u32[]{:S(2)}) %collective-permute-start.17) | collective-permute-done | bytes 262176 | tf_op jit(solution)/shard_map/ppermute | solution.py:410
  89.0 6.4 %collective-permute-done.19.refs_9_.refs_13_ = bf16[256,1280]{1,0:T(8,128)(2,1)S(1)} collective-permute-done((bf16[256,1280]{1,0:T(8,128)(2,1)S(1)}, bf16[256,1280]{1,0:T(8,128)(2,1)S(1)}, u32[]{:S(2)}, u32[]{:S(2)}) %collective-permute-start.19) | collective-permute-done | bytes 655392 | tf_op jit(solution)/shard_map/ppermute | solution.py:404
  95.4 3.4 %collective-permute-start.22 = (bf16[256,512]{1,0:T(8,128)(2,1)S(1)}, bf16[256,512]{1,0:T(8,128)(2,1)S(1)}, u32[]{:S(2)}, u32[]{:S(2)}) collective-permute-start(bf16[256,512]{1,0:T(8,128)(2,1)S(1)} %pad_maximum_fusion.13), channel_id=1, source_target_pairs={{0,8},{1,9},{2,10},{3,11},{4,12},{5,13},{6,14},{7,15},{8,0},{9,1},... | collective-permute-start | bytes 786440 | tf_op jit(solution)/shard_map/ppermute | solution.py:410
  101.3 4.5 %pad_maximum_fusion = (bf16[24,64,1024]{2,1,0:T(8,128)(2,1)}, bf16[24,64,1024]{2,1,0:T(8,128)(2,1)}) fusion(bf16[6,64,1024]{2,1,0:T(8,128)(2,1)} %collective-permute-done.14, bf16[6,64,1024]{2,1,0:T(8,128)(2,1)} %collective-permute-done.7, bf16[6,64,1024]{2,1,0:T(8,128)(2,1)} %collective-permute-done.1, bf16[6,64,1024]{2,1,0:T(8,128)(2,1)S(1)} %copy-done.4, ...), kind=kLoop, calls=%fused_computation | loop fusion | flops 9437184 | bytes 12582912 | tf_op jit(solution)/shard_map/concatenate | solution.py:497
  105.9 8.8 %prep.2 = (bf16[24,64,1024]{2,1,0:T(8,128)(2,1)}, bf16[24,64,1024]{2,1,0:T(8,128)(2,1)}) custom-call(s32[24]{0:T(128)} %get-tuple-element.75.perm_ref.refs_4_, s32[24]{0:T(128)} %get-tuple-element.76.sorted_ref.refs_2_, bf16[24,64,1024]{2,1,0:T(8,128)(2,1)} %get-tuple-element.106.x_ref, bf16[24,64,1024]{2,1,0:T(8,128)(2,1)} %get-tuple-element.107.g_ref, ...), custom_call_target="tpu_custom_call" | custom-call | tf_op jit(solution)/shard_map/prep/pallas_call | solution.py:108
  114.7 11.7 %chunk.4 = (f32[1536,1024]{1,0:T(8,128)}, f32[1536,1024]{1,0:T(8,128)}) custom-call(s32[2]{0:T(128)} %get-tuple-element.84.refs_0_, s32[2]{0:T(128)} %get-tuple-element.83.refs_1_, s32[24]{0:T(128)} %get-tuple-element.76.sorted_ref.refs_2_, s32[2]{0:T(128)} %get-tuple-element.105.refs_3_, s32[24]{0:T(128)} %get-tuple-element.75.perm_ref.refs_4_, ...), custom_call_target="tpu_custom_call" | custom-call | flops 6442450944 | bytes 34603008 | tf_op jit(solution)/shard_map/chunk/pallas_call | solution.py:300
  126.6 3.6 %collective-permute-start.30 = (bf16[3,256,512]{2,1,0:T(8,128)(2,1)S(1)}, bf16[3,256,512]{2,1,0:T(8,128)(2,1)S(1)}, u32[]{:S(2)}, u32[]{:S(2)}) collective-permute-start(bf16[3,256,512]{2,1,0:T(8,128)(2,1)S(1)} %pad_maximum_fusion.8.refs_14_.refs_10_), channel_id=1, source_target_pairs={{0,2},{1,3},{2,0},{3,1},{4,6},{5,7},{6,4},{7,5},{8,10},{9,11},{10,... | collective-permute-start | bytes 2359304 | tf_op jit(solution)/shard_map/ppermute | solution.py:404
  139.4 5.1 %prep.3 = (bf16[12,64,1024]{2,1,0:T(8,128)(2,1)}, bf16[12,64,1024]{2,1,0:T(8,128)(2,1)}) custom-call(s32[12]{0:T(128)} %get-tuple-element.79.perm_ref.refs_4_, s32[12]{0:T(128)} %get-tuple-element.80.sorted_ref.refs_2_, bf16[12,64,1024]{2,1,0:T(8,128)(2,1)} %pad_maximum_fusion.3.x_ref, bf16[12,64,1024]{2,1,0:T(8,128)(2,1)} %pad_maximum_fusion.4.g_ref, ...), custom_call_target="tpu_custom_call" | custom-call | tf_op jit(solution)/shard_map/prep/pallas_call | solution.py:108
  144.5 6.2 %collective-permute-done.27 = bf16[256,512]{1,0:T(8,128)(2,1)S(1)} collective-permute-done((bf16[256,512]{1,0:T(8,128)(2,1)S(1)}, bf16[256,512]{1,0:T(8,128)(2,1)S(1)}, u32[]{:S(2)}, u32[]{:S(2)}) %collective-permute-start.27) | collective-permute-done | bytes 262176 | tf_op jit(solution)/shard_map/ppermute | solution.py:410
  155.8 20.3 %chunk.5 = (f32[12,64,1024]{2,1,0:T(8,128)}, f32[12,64,1024]{2,1,0:T(8,128)}, bf16[2,6,64,1024]{3,2,1,0:T(8,128)(2,1)}, bf16[2,6,64,1024]{3,2,1,0:T(8,128)(2,1)}) custom-call(s32[2]{0:T(128)} %get-tuple-element.84.refs_0_, s32[2]{0:T(128)} %get-tuple-element.83.refs_1_, s32[24]{0:T(128)} %get-tuple-element.76.sorted_ref.refs_2_, ...), custom_call_target="tpu_custom_call" | custom-call | flops 6442450944 | bytes 34603008 | tf_op jit(solution)/shard_map/chunk/pallas_call | solution.py:300
  176.2 3.6 %collective-permute-done.36 = bf16[2,6,64,1024]{3,2,1,0:T(8,128)(2,1)S(1)} collective-permute-done((bf16[2,6,64,1024]{3,2,1,0:T(8,128)(2,1)}, bf16[2,6,64,1024]{3,2,1,0:T(8,128)(2,1)S(1)}, u32[]{:S(2)}, u32[]{:S(2)}) %collective-permute-start.36) | collective-permute-done | bytes 1572896 | tf_op jit(solution)/shard_map/ppermute | solution.py:401
  187.6 14.1 %collective-permute-done.37.across_out_ref = bf16[6,64,1024]{2,1,0:T(8,128)(2,1)S(1)} collective-permute-done((bf16[6,64,1024]{2,1,0:T(8,128)(2,1)S(1)}, bf16[6,64,1024]{2,1,0:T(8,128)(2,1)S(1)}, u32[]{:S(2)}, u32[]{:S(2)}) %collective-permute-start.37) | collective-permute-done | bytes 786464 | tf_op jit(solution)/shard_map/ppermute | solution.py:407
  203.8 8.6 %chunk.6 = (f32[768,1024]{1,0:T(8,128)}, f32[768,1024]{1,0:T(8,128)}) custom-call(s32[2]{0:T(128)} %get-tuple-element.86.refs_0_, s32[2]{0:T(128)} %get-tuple-element.85.refs_1_, s32[12]{0:T(128)} %get-tuple-element.80.sorted_ref.refs_2_, s32[2]{0:T(128)} %get-tuple-element.105.refs_3_, ...), custom_call_target="tpu_custom_call", output_to_operand_aliasing={{0}: (16, {}), {1}: (17, {})} | custom-call | flops 2147483648 | bytes 17825792 | tf_op jit(solution)/shard_map/chunk/pallas_call | solution.py:300
  212.4 8.0 %collective-permute-done.38.across_back_ref = bf16[6,64,1024]{2,1,0:T(8,128)(2,1)S(1)} collective-permute-done((bf16[6,64,1024]{2,1,0:T(8,128)(2,1)S(1)}, bf16[6,64,1024]{2,1,0:T(8,128)(2,1)S(1)}, u32[]{:S(2)}, u32[]{:S(2)}) %collective-permute-start.38) | collective-permute-done | bytes 786464 | tf_op jit(solution)/shard_map/ppermute | solution.py:407
  221.2 10.4 %chunk.7 = (f32[6,64,1024]{2,1,0:T(8,128)}, f32[6,64,1024]{2,1,0:T(8,128)}, bf16[2,6,64,1024]{3,2,1,0:T(8,128)(2,1)}) custom-call(s32[2]{0:T(128)} %get-tuple-element.86.refs_0_, s32[2]{0:T(128)} %get-tuple-element.85.refs_1_, s32[12]{0:T(128)} %get-tuple-element.80.sorted_ref.refs_2_, s32[2]{0:T(128)} %get-tuple-element.105.refs_3_, ...), custom_call_target="tpu_custom_call" | custom-call | flops 2147483648 | bytes 17825792 | tf_op jit(solution)/shard_map/chunk/pallas_call | solution.py:300
  231.7 3.6 %collective-permute-done.39.other_ref = bf16[2,6,64,1024]{3,2,1,0:T(8,128)(2,1)S(1)} collective-permute-done((bf16[2,6,64,1024]{3,2,1,0:T(8,128)(2,1)}, bf16[2,6,64,1024]{3,2,1,0:T(8,128)(2,1)S(1)}, u32[]{:S(2)}, u32[]{:S(2)}) %collective-permute-start.39) | collective-permute-done | bytes 1572896 | tf_op jit(solution)/shard_map/ppermute | solution.py:401
  236.5 5.9 %finish.1 = (bf16[6,64,1024]{2,1,0:T(8,128)(2,1)}, bf16[6,64,1024]{2,1,0:T(8,128)(2,1)}, f32[6,64]{1,0:T(8,128)}) custom-call(s32[6]{0:T(128)} %bitcast.94, bf16[6,64,1024]{2,1,0:T(8,128)(2,1)} %x_ref.1, bf16[6,64,1024]{2,1,0:T(8,128)(2,1)} %g_ref.1, f32[2,1024]{1,0:T(2,128)} %gain_ref.5, f32[6,64,1024]{2,1,0:T(8,128)} %get-tuple-element.72.out_ref, ...), custom_call_target="tpu_custom_call" | custom-call | tf_op jit(solution)/shard_map/finish/pallas_call | solution.py:353
  (164 shorter events, 70.0 us)
Async XLA Ops:
  3.7 24.0 %collective-permute-start.1 = (bf16[6,64,1024]{2,1,0:T(8,128)(2,1)S(1)}, bf16[6,64,1024]{2,1,0:T(8,128)(2,1)}, u32[]{:S(2)}, u32[]{:S(2)}) collective-permute-start(bf16[6,64,1024]{2,1,0:T(8,128)(2,1)S(1)} %copy-done.4), channel_id=1, source_target_pairs={{0,1},{1,0},{2,3},{3,2},{4,5},{5,4},{6,7},{7,6},{8,9},{9,8},{10,11... | collective-permute-start | bytes 2359304 | tf_op jit(solution)/shard_map/ppermute | solution.py:401
  3.7 24.0 %collective-permute-start.7 = (bf16[6,64,1024]{2,1,0:T(8,128)(2,1)S(1)}, bf16[6,64,1024]{2,1,0:T(8,128)(2,1)}, u32[]{:S(2)}, u32[]{:S(2)}) collective-permute-start(bf16[6,64,1024]{2,1,0:T(8,128)(2,1)S(1)} %copy-done.4), channel_id=1, source_target_pairs={{0,16},{16,0},{1,17},{17,1},{2,18},{18,2},{3,19},{19,3},{4,20},{20... | collective-permute-start | bytes 2359304 | tf_op jit(solution)/shard_map/ppermute | solution.py:407
  5.2 22.5 %collective-permute-start.8 = (bf16[6,64,1024]{2,1,0:T(8,128)(2,1)S(1)}, bf16[6,64,1024]{2,1,0:T(8,128)(2,1)}, u32[]{:S(2)}, u32[]{:S(2)}) collective-permute-start(bf16[6,64,1024]{2,1,0:T(8,128)(2,1)S(1)} %copy-done.5), channel_id=1, source_target_pairs={{0,1},{1,0},{2,3},{3,2},{4,5},{5,4},{6,7},{7,6},{8,9},{9,8},{10,11... | collective-permute-start | bytes 2359304 | tf_op jit(solution)/shard_map/ppermute | solution.py:401
  6.6 21.1 %collective-permute-start.6 = (bf16[256,1280]{1,0:T(8,128)(2,1)S(1)}, bf16[256,1280]{1,0:T(8,128)(2,1)S(1)}, u32[]{:S(2)}, u32[]{:S(2)}) collective-permute-start(bf16[256,1280]{1,0:T(8,128)(2,1)S(1)} %bitcast.77), channel_id=1, source_target_pairs={{0,2},{1,3},{2,0},{3,1},{4,6},{5,7},{6,4},{7,5},{8,10},{9,11},{10,... | collective-permute-start | bytes 1966088 | tf_op jit(solution)/shard_map/ppermute | solution.py:404
  27.7 33.5 %collective-permute-start.14 = (bf16[6,64,1024]{2,1,0:T(8,128)(2,1)}, bf16[6,64,1024]{2,1,0:T(8,128)(2,1)}, u32[]{:S(2)}, u32[]{:S(2)}) collective-permute-start(bf16[6,64,1024]{2,1,0:T(8,128)(2,1)} %collective-permute-done.7), channel_id=1, source_target_pairs={{0,1},{1,0},{2,3},{3,2},{4,5},{5,4},{6,7},{7,6},{8,9},{9,8},{10,11... | collective-permute-start | bytes 2359304 | tf_op jit(solution)/shard_map/ppermute | solution.py:401
  28.3 33.0 %collective-permute-start.13 = (bf16[6,64,1024]{2,1,0:T(8,128)(2,1)S(1)}, bf16[6,64,1024]{2,1,0:T(8,128)(2,1)}, u32[]{:S(2)}, u32[]{:S(2)}) collective-permute-start(bf16[6,64,1024]{2,1,0:T(8,128)(2,1)S(1)} %copy-done.5), channel_id=1, source_target_pairs={{0,16},{16,0},{1,17},{17,1},{2,18},{18,2},{3,19},{19,3},{4,20},{20... | collective-permute-start | bytes 2359304 | tf_op jit(solution)/shard_map/ppermute | solution.py:407
  30.0 20.3 %collective-permute-start.10 = (bf16[256,512]{1,0:T(8,128)(2,1)}, bf16[256,512]{1,0:T(8,128)(2,1)}, u32[]{:S(2)}, u32[]{:S(2)}) collective-permute-start(bf16[256,512]{1,0:T(8,128)(2,1)} %get-tuple-element.39), channel_id=1, source_target_pairs={{0,8},{1,9},{2,10},{3,11},{4,12},{5,13},{6,14},{7,15},{8,0},{9,1},... | collective-permute-start | bytes 786440 | tf_op jit(solution)/shard_map/ppermute | solution.py:410
  37.2 19.7 %collective-permute-start.11 = (bf16[256,512]{1,0:T(8,128)(2,1)}, bf16[256,512]{1,0:T(8,128)(2,1)S(1)}, u32[]{:S(2)}, u32[]{:S(2)}) collective-permute-start(bf16[256,512]{1,0:T(8,128)(2,1)} %get-tuple-element.39), channel_id=1, source_target_pairs={{0,12},{1,13},{2,14},{3,15},{4,0},{5,1},{6,2},{7,3},{8,4},{9,5},{1... | collective-permute-start | bytes 786440 | tf_op jit(solution)/shard_map/ppermute | solution.py:410
  37.3 19.7 %collective-permute-start.9 = (bf16[256,512]{1,0:T(8,128)(2,1)}, bf16[256,512]{1,0:T(8,128)(2,1)S(1)}, u32[]{:S(2)}, u32[]{:S(2)}) collective-permute-start(bf16[256,512]{1,0:T(8,128)(2,1)} %get-tuple-element.39), channel_id=1, source_target_pairs={{0,4},{1,5},{2,6},{3,7},{4,8},{5,9},{6,10},{7,11},{8,12},{9,13},{1... | collective-permute-start | bytes 786440 | tf_op jit(solution)/shard_map/ppermute | solution.py:410
  61.3 34.1 %collective-permute-start.20 = (bf16[6,64,1024]{2,1,0:T(8,128)(2,1)}, bf16[6,64,1024]{2,1,0:T(8,128)(2,1)S(1)}, u32[]{:S(2)}, u32[]{:S(2)}) collective-permute-start(bf16[6,64,1024]{2,1,0:T(8,128)(2,1)} %collective-permute-done.13), channel_id=1, source_target_pairs={{0,1},{1,0},{2,3},{3,2},{4,5},{5,4},{6,7},{7,6},{8,9},{9,8},{10,11... | collective-permute-start | bytes 2359304 | tf_op jit(solution)/shard_map/ppermute | solution.py:401
  61.3 34.0 %collective-permute-start.18 = (bf16[3,256,512]{2,1,0:T(8,128)(2,1)S(1)}, bf16[3,256,512]{2,1,0:T(8,128)(2,1)S(1)}, u32[]{:S(2)}, u32[]{:S(2)}) collective-permute-start(bf16[3,256,512]{2,1,0:T(8,128)(2,1)S(1)} %pad_maximum_fusion.5.refs_14_), channel_id=1, source_target_pairs={{0,2},{1,3},{2,0},{3,1},{4,6},{5,7},{6,4},{7,5},{8,10},{9,11},{10,... | collective-permute-start | bytes 2359304 | tf_op jit(solution)/shard_map/ppermute | solution.py:404
  62.1 33.3 %collective-permute-start.19 = (bf16[256,1280]{1,0:T(8,128)(2,1)S(1)}, bf16[256,1280]{1,0:T(8,128)(2,1)S(1)}, u32[]{:S(2)}, u32[]{:S(2)}) collective-permute-start(bf16[256,1280]{1,0:T(8,128)(2,1)S(1)} %bitcast.76), channel_id=1, source_target_pairs={{0,2},{1,3},{2,0},{3,1},{4,6},{5,7},{6,4},{7,5},{8,10},{9,11},{10,... | collective-permute-start | bytes 1966088 | tf_op jit(solution)/shard_map/ppermute | solution.py:404
  64.3 20.7 %collective-permute-start.16 = (bf16[256,512]{1,0:T(8,128)(2,1)S(1)}, bf16[256,512]{1,0:T(8,128)(2,1)S(1)}, u32[]{:S(2)}, u32[]{:S(2)}) collective-permute-start(bf16[256,512]{1,0:T(8,128)(2,1)S(1)} %copy-done.25), channel_id=1, source_target_pairs={{0,8},{1,9},{2,10},{3,11},{4,12},{5,13},{6,14},{7,15},{8,0},{9,1},... | collective-permute-start | bytes 786440 | tf_op jit(solution)/shard_map/ppermute | solution.py:410
  95.4 31.1 %collective-permute-start.21 = (bf16[256,512]{1,0:T(8,128)(2,1)S(1)}, bf16[256,512]{1,0:T(8,128)(2,1)S(1)}, u32[]{:S(2)}, u32[]{:S(2)}) collective-permute-start(bf16[256,512]{1,0:T(8,128)(2,1)S(1)} %pad_maximum_fusion.13), channel_id=1, source_target_pairs={{0,4},{1,5},{2,6},{3,7},{4,8},{5,9},{6,10},{7,11},{8,12},{9,13},{1... | collective-permute-start | bytes 786440 | tf_op jit(solution)/shard_map/ppermute | solution.py:410
  95.4 31.0 %collective-permute-start.22 = (bf16[256,512]{1,0:T(8,128)(2,1)S(1)}, bf16[256,512]{1,0:T(8,128)(2,1)S(1)}, u32[]{:S(2)}, u32[]{:S(2)}) collective-permute-start(bf16[256,512]{1,0:T(8,128)(2,1)S(1)} %pad_maximum_fusion.13), channel_id=1, source_target_pairs={{0,8},{1,9},{2,10},{3,11},{4,12},{5,13},{6,14},{7,15},{8,0},{9,1},... | collective-permute-start | bytes 786440 | tf_op jit(solution)/shard_map/ppermute | solution.py:410
  98.9 27.6 %collective-permute-start.23 = (bf16[256,512]{1,0:T(8,128)(2,1)S(1)}, bf16[256,512]{1,0:T(8,128)(2,1)S(1)}, u32[]{:S(2)}, u32[]{:S(2)}) collective-permute-start(bf16[256,512]{1,0:T(8,128)(2,1)S(1)} %pad_maximum_fusion.13), channel_id=1, source_target_pairs={{0,12},{1,13},{2,14},{3,15},{4,0},{5,1},{6,2},{7,3},{8,4},{9,5},{1... | collective-permute-start | bytes 786440 | tf_op jit(solution)/shard_map/ppermute | solution.py:410
  100.8 25.8 %collective-permute-start.24 = (bf16[3,256,512]{2,1,0:T(8,128)(2,1)S(1)}, bf16[3,256,512]{2,1,0:T(8,128)(2,1)S(1)}, u32[]{:S(2)}, u32[]{:S(2)}) collective-permute-start(bf16[3,256,512]{2,1,0:T(8,128)(2,1)S(1)} %pad_maximum_fusion.6.refs_10_), channel_id=1, source_target_pairs={{0,2},{1,3},{2,0},{3,1},{4,6},{5,7},{6,4},{7,5},{8,10},{9,11},{10,... | collective-permute-start | bytes 2359304 | tf_op jit(solution)/shard_map/ppermute | solution.py:404
  126.6 28.3 %collective-permute-start.30 = (bf16[3,256,512]{2,1,0:T(8,128)(2,1)S(1)}, bf16[3,256,512]{2,1,0:T(8,128)(2,1)S(1)}, u32[]{:S(2)}, u32[]{:S(2)}) collective-permute-start(bf16[3,256,512]{2,1,0:T(8,128)(2,1)S(1)} %pad_maximum_fusion.8.refs_14_.refs_10_), channel_id=1, source_target_pairs={{0,2},{1,3},{2,0},{3,1},{4,6},{5,7},{6,4},{7,5},{8,10},{9,11},{10,... | collective-permute-start | bytes 2359304 | tf_op jit(solution)/shard_map/ppermute | solution.py:404
  130.9 19.9 %collective-permute-start.27 = (bf16[256,512]{1,0:T(8,128)(2,1)S(1)}, bf16[256,512]{1,0:T(8,128)(2,1)S(1)}, u32[]{:S(2)}, u32[]{:S(2)}) collective-permute-start(bf16[256,512]{1,0:T(8,128)(2,1)S(1)} %pad_maximum_fusion.14), channel_id=1, source_target_pairs={{0,4},{1,5},{2,6},{3,7},{4,8},{5,9},{6,10},{7,11},{8,12},{9,13},{1... | collective-permute-start | bytes 786440 | tf_op jit(solution)/shard_map/ppermute | solution.py:410
  133.0 21.1 %collective-permute-start.28 = (bf16[256,512]{1,0:T(8,128)(2,1)S(1)}, bf16[256,512]{1,0:T(8,128)(2,1)S(1)}, u32[]{:S(2)}, u32[]{:S(2)}) collective-permute-start(bf16[256,512]{1,0:T(8,128)(2,1)S(1)} %pad_maximum_fusion.14), channel_id=1, source_target_pairs={{0,8},{1,9},{2,10},{3,11},{4,12},{5,13},{6,14},{7,15},{8,0},{9,1},... | collective-permute-start | bytes 786440 | tf_op jit(solution)/shard_map/ppermute | solution.py:410
  133.3 21.6 %collective-permute-start.29 = (bf16[256,512]{1,0:T(8,128)(2,1)S(1)}, bf16[256,512]{1,0:T(8,128)(2,1)S(1)}, u32[]{:S(2)}, u32[]{:S(2)}) collective-permute-start(bf16[256,512]{1,0:T(8,128)(2,1)S(1)} %pad_maximum_fusion.14), channel_id=1, source_target_pairs={{0,12},{1,13},{2,14},{3,15},{4,0},{5,1},{6,2},{7,3},{8,4},{9,5},{1... | collective-permute-start | bytes 786440 | tf_op jit(solution)/shard_map/ppermute | solution.py:410
  182.5 20.3 %collective-permute-start.31 = (bf16[3,256,512]{2,1,0:T(8,128)(2,1)S(1)}, bf16[3,256,512]{2,1,0:T(8,128)(2,1)S(1)}, u32[]{:S(2)}, u32[]{:S(2)}) collective-permute-start(bf16[3,256,512]{2,1,0:T(8,128)(2,1)S(1)} %pad_maximum_fusion.7.refs_14_.refs_10_), channel_id=1, source_target_pairs={{0,2},{1,3},{2,0},{3,1},{4,6},{5,7},{6,4},{7,5},{8,10},{9,11},{10,... | collective-permute-start | bytes 2359304 | tf_op jit(solution)/shard_map/ppermute | solution.py:404
  182.9 19.8 %collective-permute-start.32 = (bf16[256,256]{1,0:T(8,128)(2,1)S(1)}, bf16[256,256]{1,0:T(8,128)(2,1)S(1)}, u32[]{:S(2)}, u32[]{:S(2)}) collective-permute-start(bf16[256,256]{1,0:T(8,128)(2,1)S(1)} %copy-done.26), channel_id=1, source_target_pairs={{0,4},{1,5},{2,6},{3,7},{4,8},{5,9},{6,10},{7,11},{8,12},{9,13},{1... | collective-permute-start | bytes 393224 | tf_op jit(solution)/shard_map/ppermute | solution.py:410
  182.9 19.8 %collective-permute-start.33 = (bf16[256,256]{1,0:T(8,128)(2,1)S(1)}, bf16[256,256]{1,0:T(8,128)(2,1)S(1)}, u32[]{:S(2)}, u32[]{:S(2)}) collective-permute-start(bf16[256,256]{1,0:T(8,128)(2,1)S(1)} %copy-done.26), channel_id=1, source_target_pairs={{0,8},{1,9},{2,10},{3,11},{4,12},{5,13},{6,14},{7,15},{8,0},{9,1},... | collective-permute-start | bytes 393224 | tf_op jit(solution)/shard_map/ppermute | solution.py:410
  (48 other events, 687.6 us)

commit v7 on v6

--- a/solution.py
+++ b/solution.py
@@ -90,29 +90,54 @@
 F32 = jnp.float32
 
 
-def prep_kernel(perm_ref, sorted_ref, x_ref, g_ref, gain_ref, lifted_ref, gs_ref):
+def prep_kernel(
+    perm_ref, sorted_ref, near_ref, over_ref, far_ref, gain_ref, lifted_ref, g_out_ref
+):
+    rows = near_ref.shape[1]
+
     def row(p, carry):
-        x = x_ref[perm_ref[p]].astype(F32)
-        inv = 1.0 / jnp.sqrt(jnp.mean(x * x, axis=1, keepdims=True) + 1e-06)
-        gain = gain_ref[pl.ds(sorted_ref[p], 1), :]
-        lifted_ref[p] = ((x * inv) * gain).astype(BF16)
-        gs_ref[p] = g_ref[perm_ref[p]]
+        at = perm_ref[p]
+        i = lax.rem(at, rows)
+
+        def emit(x, g):
+            x = x.astype(F32)
+            inv = 1.0 / jnp.sqrt(jnp.mean(x * x, axis=1, keepdims=True) + 1e-06)
+            gain = gain_ref[pl.ds(sorted_ref[p], 1), :]
+            lifted_ref[p] = ((x * inv) * gain).astype(BF16)
+            g_out_ref[p] = g
+
+        for source in range(4):
+
+            @pl.when(at // rows == source)
+            def _():
+                if source % 2:
+                    emit(far_ref[source // 2, 0, i], far_ref[source // 2, 1, i])
+                else:
+                    ref = over_ref if source else near_ref
+                    emit(ref[0, i], ref[1, i])
+
         return carry
 
-    lax.fori_loop(0, x_ref.shape[0], row, 0)
-
-
-def prep(perm, member_sorted, x_pair, g_pair, gain):
+    lax.fori_loop(0, lifted_ref.shape[0], row, 0)
+
+
+def prep(perm, member_sorted, near, over, far, gain):
     smem = pl.BlockSpec(memory_space=pltpu.SMEM)
     vmem = pl.BlockSpec(memory_space=pltpu.VMEM)
+    shape = (perm.shape[0], *near.shape[2:])
     return pl.pallas_call(
         prep_kernel,
-        in_specs=[smem, smem, vmem, vmem, vmem],
+        in_specs=[smem, smem, vmem, vmem, vmem, vmem],
         out_specs=[vmem, vmem],
-        out_shape=[jax.ShapeDtypeStruct(x_pair.shape, BF16)] * 2,
+        out_shape=[jax.ShapeDtypeStruct(shape, BF16)] * 2,
         compiler_params=pltpu.CompilerParams(vmem_limit_bytes=VMEM_LIMIT),
+        cost_estimate=pl.CostEstimate(
+            flops=8 * perm.shape[0] * near.shape[2] * near.shape[3],
+            bytes_accessed=16 * perm.shape[0] * near.shape[2] * near.shape[3],
+            transcendentals=0,
+        ),
         name="prep",
-    )(perm, member_sorted, x_pair, g_pair, gain)
+    )(perm, member_sorted, near, over, far, gain)
 
 
 def chunk_kernel(
@@ -121,7 +146,7 @@
 ):
     first, opens, last = kind
     parts = len(units)
-    pieces, refs = refs[: 4 * parts], refs[4 * parts :]
+    pieces, refs = refs[: 2 * parts], refs[2 * parts :]
     if first:
         *outs, weights_ref, sems = refs
     else:
@@ -147,15 +172,10 @@
 
         for part in range(parts):
             cols = pl.ds(sum(units[:part]), units[part])
-            own, own_y, here, there = (
-                (ref, pl.ds(start, units[part])) for ref, start in pieces[4 * part : 4 * part + 4]
-            )
-            put(own[0].at[member, :, own[1]], z, y, cols)
-            put(own_y[0].at[:, own_y[1]], z, 1 - y, cols)
-            for d in range(1, lines):
-                from_z = lax.rem(z + lines - d, lines)
-                put(here[0].at[d - 1, :, here[1]], from_z, y, cols)
-                put(there[0].at[d - 1, :, there[1]], from_z, 1 - y, cols)
+            for to_y, (ref, start) in zip((y, 1 - y), pieces[2 * part : 2 * part + 2]):
+                for d in range(lines):
+                    from_z = lax.rem(z + lines - d, lines)
+                    put(ref.at[d, :, pl.ds(start, units[part])], from_z, to_y, cols)
         for copy in copies:
             copy.start()
         for copy in copies:
@@ -257,8 +277,7 @@
     rows, seq, width = lifted.shape
     tokens = rows * seq
     units = [part[0] for part in pieces]
-    lines = pieces[0][3][0].shape[0] + 1
-    depth2 = pieces[0][3][0].shape[1]
+    lines, depth2, _ = pieces[0][1][0].shape
     hidden = sum(units)
     size = per_block * seq
 
@@ -271,10 +290,10 @@
     hbm = pl.BlockSpec(memory_space=pl.ANY)
     args = [*scalars, lifted.reshape(tokens, width), g.reshape(tokens, width)]
     starts = []
-    for _, *four in pieces:
-        args += [array for array, _ in four]
-        starts += [start for _, start in four]
-    specs = [tok, tok] + [hbm] * (4 * len(pieces))
+    for _, *both in pieces:
+        args += [array for array, _ in both]
+        starts += [start for _, start in both]
+    specs = [tok, tok] + [hbm] * len(starts)
     alias = {}
     out_specs = [tok, tok]
     out_shape = [jax.ShapeDtypeStruct((tokens, width), F32)] * 2
@@ -322,8 +341,8 @@
 
 
 def finish_kernel(
-    member_ref, x_ref, g_ref, gain_ref, out_ref, back_ref, other_ref, across_out_ref,
-    across_back_ref, value_ref, grad_ref, coupling_ref,
+    member_ref, x_ref, g_ref, gain_ref, out_ref, back_ref, other_ref, across_ref,
+    value_ref, grad_ref, coupling_ref,
 ):
     rows, seq, width = x_ref.shape
     diagonal = lax.broadcasted_iota(jnp.int32, (seq, seq), 0) == lax.broadcasted_iota(
@@ -335,17 +354,17 @@
         normed = x * inv
         gain = gain_ref[pl.ds(member_ref[pl.program_id(0) * rows + r], 1), :]
         back = gain * (
-            back_ref[r] + other_ref[1, r].astype(F32) + across_back_ref[r].astype(F32)
+            back_ref[r] + other_ref[1, r].astype(F32) + across_ref[1, r].astype(F32)
         )
         stat = jnp.sum(normed * back, axis=1, keepdims=True) / width
-        out = out_ref[r] + other_ref[0, r].astype(F32) + across_out_ref[r].astype(F32)
+        out = out_ref[r] + other_ref[0, r].astype(F32) + across_ref[0, r].astype(F32)
         value_ref[r] = (x + out).astype(BF16)
         grad_ref[r] = (g_ref[r].astype(F32) + (back - normed * stat) * inv).astype(BF16)
         line = jnp.sum(jnp.where(diagonal, stat, 0.0), axis=0, keepdims=True)
         coupling_ref[pl.ds(pl.program_id(0) * rows + r, 1), :] = line * math.sqrt(width)
 
 
-def finish(member_own, x, g, gain, out, back, other, across_out, across_back):
+def finish(member_own, x, g, gain, out, back, other, across):
     rows, seq, width = x.shape
     step = math.gcd(rows, 2)
     row = pl.BlockSpec((step, seq, width), lambda r, mem: (r, 0, 0))
@@ -356,7 +375,7 @@
             num_scalar_prefetch=1,
             grid=(rows // step,),
             in_specs=[
-                row, row, pl.BlockSpec(gain.shape, lambda r, mem: (0, 0)), row, row, two, row, row
+                row, row, pl.BlockSpec(gain.shape, lambda r, mem: (0, 0)), row, row, two, two
             ],
             out_specs=[row, row, pl.BlockSpec((rows, seq), lambda r, mem: (0, 0))],
         ),
@@ -367,7 +386,7 @@
         ],
         compiler_params=pltpu.CompilerParams(vmem_limit_bytes=VMEM_LIMIT),
         name="finish",
-    )(member_own, x, g, gain, out, back, other, across_out, across_back)
+    )(member_own, x, g, gain, out, back, other, across)
 
 
 def sort_rows(picks, members, per_block):
@@ -412,40 +431,32 @@
     def after(a, *others):
         return lax.optimization_barrier((a, *others))[0]
 
-    quarter = 3 * hidden // 16
-    half = hidden // 8
+    quarter = hidden // 4
     both = jnp.stack([up_proj, down_proj], axis=1)
 
     def units_of(c):
-        return jnp.concatenate(
-            [
-                lax.dynamic_slice_in_dim(both, (2 * x_at + c) * quarter, quarter, 3),
-                lax.dynamic_slice_in_dim(both, 4 * quarter + c * half, half, 3),
-            ],
-            axis=3,
-        )
+        return lax.dynamic_slice_in_dim(both, (2 * x_at + c) * quarter, quarter, 3)
 
     mine = units_of(core)
     theirs = partner(units_of(1 - core))
     even = core == 0
     shard = jnp.concatenate(
         [jnp.where(even, mine, theirs), jnp.where(even, theirs, mine)], axis=2
-    ).reshape(members, 4 * depth, quarter + half)
-
-    third = quarter // 3
+    ).reshape(members, 4 * depth, quarter)
+
+    unit = quarter // 4
     groups = [
-        [(0, 0, third)],
-        [(0, third, 2 * third)],
-        [(1, 0, 2 * third)],
-        [(1, 2 * third, third), (0, quarter, half // 2)],
-        [(0, quarter + half // 2, half // 2), (1, quarter, half // 2)],
-        [(1, quarter + half // 2, half // 2)],
+        [(0, 0, unit)],
+        [(0, unit, 2 * unit)],
+        [(0, 3 * unit, unit), (1, 0, unit)],
+        [(1, unit, 2 * unit)],
+        [(1, 3 * unit, unit)],
     ]
     send = [
         jnp.concatenate([shard[m, :, at : at + n] for m, at, n in group], axis=1)
         for group in groups
     ]
-    here, there, own_y = [], [], []
+    here, there = [], []
 
     def exchange(step, arrived):
         results = []
@@ -456,82 +467,61 @@
             there.append(over_y(after(here[step - 1], *arrived)))
             results.append(there[-1])
         if step < len(groups):
-            here.append(jnp.stack(results[: lines - 1]))
+            here.append(jnp.stack([send[step], *results[: lines - 1]]))
         return results
 
     def piece(group, i):
-        member, start, units = groups[group][i]
         at = sum(n for _, _, n in groups[group][:i])
-        return (
-            units, (shard, start), (own_y[member], start), (here[group], at), (there[group], at)
-        )
+        return groups[group][i][2], (here[group], at), (there[group], at)
 
     pick_own = member_pick[:, 0]
-    pick_over = over_x(pick_own)
-    pick_pair = jnp.concatenate([pick_own, partner(pick_own)])
-    pick_all = jnp.concatenate([pick_pair, pick_over, partner(pick_over)])
+    pick_near = jnp.concatenate([pick_own, over_x(pick_own)])
+    pick_far = partner(pick_near)
+    pick_pair = jnp.concatenate([pick_own, pick_far[:rows]])
+    pick_all = jnp.concatenate([pick_pair, pick_near[rows:], pick_far[rows:]])
     per_block = math.gcd(2 * rows, 4)
     place = jnp.stack([y_at, rank // 4])
     index = jnp.arange(4 * rows, dtype=jnp.int32)
-    pos, perm, member_sorted, low, high = sort_rows(pick_pair, members, per_block)
-    scalars_alone = (low, high, member_sorted, place, perm, lax.rem(index[: 2 * rows], rows))
-    _, perm_all, member_sorted_all, low, high = sort_rows(pick_all, members, per_block)
-    dest = jnp.concatenate([pos, lax.rem(index[2 * rows :], rows)])
-    scalars_shared = (low, high, member_sorted_all, place, perm_all, dest)
-
+    _, perm, member_sorted, low, high = sort_rows(pick_all, members, per_block)
+    scalars = (low, high, member_sorted, place, perm, lax.rem(index, rows))
+
+    near = jnp.stack([tokens_in, upstream])
+    over = over_x(near)
     arrived = exchange(0, [])
-    own_y.append(over_y(shard[0]))
-    x_over, x_partner, g_partner = over_x(tokens_in), partner(tokens_in), partner(upstream)
-    arrived += [own_y[0], x_over, x_partner, g_partner]
-
-    set_0, arrived = arrived, exchange(1, arrived)
-    g_over, x_other = over_x(after(upstream, *set_0)), partner(after(x_over, *set_0))
-    arrived += [g_over, x_other]
+
+    arrived = exchange(1, arrived)
+    arrived += [over]
 
     set_1, arrived = arrived, exchange(2, arrived)
-    own_y.append(over_y(after(shard[1], *set_1)))
-    g_other = partner(after(g_over, *set_1))
-    arrived += [own_y[1], g_other]
+    far = partner(after(jnp.stack([near, over]), *set_1))
+    arrived += [far]
 
     set_2, arrived = arrived, exchange(3, arrived)
-    x_all = jnp.concatenate([tokens_in, x_partner, x_over, after(x_other, *set_2)])
-    g_all = jnp.concatenate([upstream, g_partner, g_over, g_other])
-    lifted_shared, g_shared = prep(perm_all, member_sorted_all, x_all, g_all, norm_gain)
+    lifted, g_sorted = prep(
+        perm, member_sorted, near, over, after(far, *set_2), norm_gain
+    )
+    arrived += [lifted]
+
+    set_3, arrived = arrived, exchange(4, arrived)
     sums = chunk(
-        0, (True, False, False), per_block, scalars_shared, lifted_shared, g_shared,
-        [piece(0, 0), piece(1, 0)], None,
+        0, (True, False, False), per_block, scalars, after(lifted, *set_3), g_sorted,
+        [piece(0, 0), piece(1, 0), piece(2, 0)], None,
     )
     arrived += [sums[0]]
 
-    set_3, arrived = arrived, exchange(4, arrived)
-    x_pair = jnp.concatenate([tokens_in, after(x_partner, *set_3)])
-    g_pair = jnp.concatenate([upstream, g_partner])
-    lifted_alone, g_alone = prep(perm, member_sorted, x_pair, g_pair, norm_gain)
-    arrived += [lifted_alone]
-
     set_4, arrived = arrived, exchange(5, arrived)
-    out, back, over_same, over_other = chunk(
-        1, (False, True, True), per_block, scalars_shared, lifted_shared, g_shared,
-        [piece(2, 0), piece(3, 0)], (after(sums[0], *set_4), sums[1]), (2 * rows, rows, rows),
-    )
-
-    exchange(6, arrived)
-    across = (over_same.astype(F32) + partner(over_other).astype(F32)).astype(BF16)
-    across_out = over_x(across[0])
-    across_back = over_x(after(across[1], across_out))
     sums = chunk(
-        0, (False, False, False), per_block, scalars_alone, lifted_alone, g_alone,
-        [piece(3, 1), piece(4, 0)], (after(out, across), back),
-    )
-    out, back, packed = chunk(
-        1, (False, False, True), per_block, scalars_alone, lifted_alone, g_alone,
-        [piece(4, 1), piece(5, 0)], (after(sums[0], across_out, across_back), sums[1]),
-        (rows, rows),
-    )
+        1, (False, True, False), per_block, scalars, lifted, g_sorted,
+        [piece(2, 1), piece(3, 0)], (after(sums[0], *set_4), sums[1]),
+    )
+    out, back, packed, over_same, over_other = chunk(
+        1, (False, False, True), per_block, scalars, lifted, g_sorted, [piece(4, 0)], sums,
+        (rows, rows, rows, rows),
+    )
+    across = over_x((over_same.astype(F32) + partner(over_other).astype(F32)).astype(BF16))
     return tuple(
         finish(
-            pick_own, tokens_in, upstream, norm_gain, out, back, partner(packed),
-            across_out, across_back,
+            pick_own, tokens_in, upstream, norm_gain, out, back, partner(packed), across
         )
     )
 

time: 243 us -> 214 us (0.88)
  starting transfers between devices: 48.2 us -> 28.8 us
  waiting for transfers between devices: 92.8 us -> 110 us
  Pallas kernels: 70.9 us -> 57.2 us
  other arithmetic: 22.7 us -> 11.9 us
    ppermute x5 -> x3, waiting for transfers between devices: 22.1 us -> 47.5 us  [over_x(): return lax.ppermute(a, 'grp', [(0, 1), (1, 0)])]
    ppermute x18 -> x15, starting transfers between devices: 34.2 us -> 19.2 us  [shift_z(): lax.ppermute(a, 'row', [(i, (i + 4 * d) % ranks) for i in range(ranks)])]
    concatenate x9 -> x2, other arithmetic: 10.9 us -> 0.15 us  [the longest x1 0.08 us: on_device_shared(): pick_all = jnp.concatenate([pick_pair, pick_near[rows:], pick_far[rows:]])]
    pallas_call x4 -> x3, Pallas kernels: 51.1 us -> 41.9 us  [chunk(): pl.pallas_call(kernel, grid_spec=pltpu.PrefetchScalarGridSpec(num_scalar_...]
    pallas_call x2 -> x1, Pallas kernels: 13.9 us -> 9.42 us  [prep(): pl.pallas_call(prep_kernel, in_specs=[smem, smem, vmem, vmem, vmem, vmem]...]
    ppermute x18 -> x15, waiting for transfers between devices: 53.8 us -> 50.1 us  [shift_z(): lax.ppermute(a, 'row', [(i, (i + 4 * d) % ranks) for i in range(ranks)])]
    ppermute x9 -> x5, waiting for transfers between devices: 7.23 us -> 4.23 us  [partner(): return lax.ppermute(a, 'row', [(i, i ^ 1) for i in range(ranks)])]
    ppermute x8 -> x5, starting transfers between devices: 8.48 us -> 6.19 us  [over_y(): return lax.ppermute(a, 'row', [(i, i ^ 2) for i in range(ranks)])]
  transfers between devices with their start and end apart: 40 -> 28, of which waited for: 17 -> 15; matrix products, arithmetic and copies ran while one was open for 9% -> 5% of each run, Pallas kernels for 14% -> 17%
where the time goes in v7:
time: 214 us
  waiting for transfers between devices  110 us (51%)
  Pallas kernels  57.2 us (27%)
  starting transfers between devices  28.8 us (13%)
  other arithmetic  11.9 us (6%)
  local copies, waits for them, and re-layouts  4.57 us (2%)
    ppermute x15, waiting for transfers between devices, shift_z(): lax.ppermute(a, 'row', [(i, (i + 4 * d) % ranks) for i in range(ranks)])  50.1 us
    ppermute x3, waiting for transfers between devices, over_x(): return lax.ppermute(a, 'grp', [(0, 1), (1, 0)])  47.5 us
    pallas_call x3, Pallas kernels, chunk(): pl.pallas_call(kernel, grid_spec=pltpu.PrefetchScalarGridSpec(num_scalar_...  41.9 us
    ppermute x15, starting transfers between devices, shift_z(): lax.ppermute(a, 'row', [(i, (i + 4 * d) % ranks) for i in range(ranks)])  19.2 us
    pallas_call x1, Pallas kernels, prep(): pl.pallas_call(prep_kernel, in_specs=[smem, smem, vmem, vmem, vmem, vmem]...  9.42 us
    ppermute x5, waiting for transfers between devices, over_y(): return lax.ppermute(a, 'row', [(i, i ^ 2) for i in range(ranks)])  8.17 us
    ppermute x5, starting transfers between devices, over_y(): return lax.ppermute(a, 'row', [(i, i ^ 2) for i in range(ranks)])  6.19 us
    pallas_call x1, Pallas kernels, finish(): pl.pallas_call(finish_kernel, grid_spec=pltpu.PrefetchScalarGridSpec(num_...  5.93 us
  transfers between devices with their start and end apart: 28, of which 15 were waited for; matrix products, arithmetic and copies ran while one was open for 5% of the time, Pallas kernels for 17%

profile of v7, /device:TPU:8, one launch (start us, length us, event | category | flops | bytes accessed | tf_op | source)
XLA Modules:
  0.0 213.5 jit_solution(16382534090113192098)
XLA Ops:
  0.7 2.0 fusion
  12.7 6.3 %collective-permute-done.4 = bf16[256,256]{1,0:T(8,128)(2,1)S(1)} collective-permute-done((bf16[256,256]{1,0:T(8,128)(2,1)S(1)}, bf16[256,256]{1,0:T(8,128)(2,1)S(1)}, u32[]{:S(2)}, u32[]{:S(2)}) %collective-permute-start.4) | collective-permute-done | bytes 131104 | tf_op jit(solution)/shard_map/ppermute | solution.py:429
  19.0 2.3 %collective-permute-done.5 = bf16[256,256]{1,0:T(8,128)(2,1)S(1)} collective-permute-done((bf16[256,256]{1,0:T(8,128)(2,1)S(1)}, bf16[256,256]{1,0:T(8,128)(2,1)S(1)}, u32[]{:S(2)}, u32[]{:S(2)}) %collective-permute-start.5) | collective-permute-done | bytes 131104 | tf_op jit(solution)/shard_map/ppermute | solution.py:429
  27.1 2.0 collective-permute-start.9
  29.2 11.7 %collective-permute-done.2.over_ref = bf16[2,6,64,1024]{3,2,1,0:T(8,128)(2,1)S(1)} collective-permute-done((bf16[2,6,64,1024]{3,2,1,0:T(8,128)(2,1)S(1)}, bf16[2,6,64,1024]{3,2,1,0:T(8,128)(2,1)S(1)}, u32[]{:S(2)}, u32[]{:S(2)}) %collective-permute-start.2) | collective-permute-done | bytes 1572896 | tf_op jit(solution)/shard_map/ppermute | solution.py:426
  42.0 6.1 %collective-permute-done.8 = bf16[256,512]{1,0:T(8,128)(2,1)S(1)} collective-permute-done((bf16[256,512]{1,0:T(8,128)(2,1)S(1)}, bf16[256,512]{1,0:T(8,128)(2,1)S(1)}, u32[]{:S(2)}, u32[]{:S(2)}) %collective-permute-start.8) | collective-permute-done | bytes 262176 | tf_op jit(solution)/shard_map/ppermute | solution.py:429
  50.5 2.0 collective-permute-start.13
  52.5 1.9 collective-permute-start.14
  54.4 5.2 %collective-permute-done.12 = bf16[256,512]{1,0:T(8,128)(2,1)S(1)} collective-permute-done((bf16[256,512]{1,0:T(8,128)(2,1)S(1)}, bf16[256,512]{1,0:T(8,128)(2,1)S(1)}, u32[]{:S(2)}, u32[]{:S(2)}) %collective-permute-start.12) | collective-permute-done | bytes 262176 | tf_op jit(solution)/shard_map/ppermute | solution.py:429
  60.3 13.3 %collective-permute-done.13 = bf16[256,512]{1,0:T(8,128)(2,1)S(1)} collective-permute-done((bf16[256,512]{1,0:T(8,128)(2,1)S(1)}, bf16[256,512]{1,0:T(8,128)(2,1)S(1)}, u32[]{:S(2)}, u32[]{:S(2)}) %collective-permute-start.13) | collective-permute-done | bytes 262176 | tf_op jit(solution)/shard_map/ppermute | solution.py:429
  73.6 2.4 %collective-permute-done.14 = bf16[256,512]{1,0:T(8,128)(2,1)S(1)} collective-permute-done((bf16[256,512]{1,0:T(8,128)(2,1)S(1)}, bf16[256,512]{1,0:T(8,128)(2,1)S(1)}, u32[]{:S(2)}, u32[]{:S(2)}) %collective-permute-start.14) | collective-permute-done | bytes 262176 | tf_op jit(solution)/shard_map/ppermute | solution.py:429
  82.2 2.0 collective-permute-start.18
  85.2 9.4 %prep.1 = (bf16[24,64,1024]{2,1,0:T(8,128)(2,1)}, bf16[24,64,1024]{2,1,0:T(8,128)(2,1)}) custom-call(s32[24]{0:T(128)} %get-tuple-element.51.perm_ref.refs_4_, s32[24]{0:T(128)} %get-tuple-element.52.sorted_ref.refs_2_, bf16[2,6,64,1024]{3,2,1,0:T(8,128)(2,1)} %copy-done, bf16[2,6,64,1024]{3,2,1,0:T(8,128)(2,1)} %copy-done.1, ...), custom_call_target="tpu_custom_call" | custom-call | flops 12582912 | bytes 25165824 | tf_op jit(solution)/shard_map/prep/pallas_call | solution.py:128
  94.6 9.9 %collective-permute-done.17 = bf16[256,512]{1,0:T(8,128)(2,1)S(1)} collective-permute-done((bf16[256,512]{1,0:T(8,128)(2,1)}, bf16[256,512]{1,0:T(8,128)(2,1)S(1)}, u32[]{:S(2)}, u32[]{:S(2)}) %collective-permute-start.17) | collective-permute-done | bytes 262176 | tf_op jit(solution)/shard_map/ppermute | solution.py:429
  107.9 1.9 collective-permute-start.21
  109.8 2.0 collective-permute-start.22
  111.8 11.1 %chunk.3 = (f32[1536,1024]{1,0:T(8,128)}, f32[1536,1024]{1,0:T(8,128)}) custom-call(s32[2]{0:T(128)} %get-tuple-element.56.refs_0_, s32[2]{0:T(128)} %get-tuple-element.55.refs_1_, s32[24]{0:T(128)} %get-tuple-element.52.sorted_ref.refs_2_, s32[2]{0:T(128)} %pad_add_fusion.2.refs_3_, s32[24]{0:T(128)} %get-tuple-element.51.perm_ref.refs_4_, ...), custom_call_target="tpu_custom_call" | custom-call | flops 8589934592 | bytes 35651584 | tf_op jit(solution)/shard_map/chunk/pallas_call | solution.py:319
  123.1 8.2 %collective-permute-done.23.refs_11_ = bf16[4,256,512]{2,1,0:T(8,128)(2,1)S(1)} collective-permute-done((bf16[4,256,512]{2,1,0:T(8,128)(2,1)S(1)}, bf16[4,256,512]{2,1,0:T(8,128)(2,1)S(1)}, u32[]{:S(2)}, u32[]{:S(2)}) %collective-permute-start.23) | collective-permute-done | bytes 1048608 | tf_op jit(solution)/shard_map/ppermute | solution.py:423
  132.4 15.3 %chunk.4 = (f32[1536,1024]{1,0:T(8,128)}, f32[1536,1024]{1,0:T(8,128)}) custom-call(s32[2]{0:T(128)} %get-tuple-element.56.refs_0_, s32[2]{0:T(128)} %get-tuple-element.55.refs_1_, s32[24]{0:T(128)} %get-tuple-element.52.sorted_ref.refs_2_, s32[2]{0:T(128)} %pad_add_fusion.2.refs_3_, ...), custom_call_target="tpu_custom_call", output_to_operand_aliasing={{0}: (12, {}), {1}: (13, {})} | custom-call | flops 6442450944 | bytes 34603008 | tf_op jit(solution)/shard_map/chunk/pallas_call | solution.py:319
  148.5 15.5 %chunk.5 = (f32[6,64,1024]{2,1,0:T(8,128)}, f32[6,64,1024]{2,1,0:T(8,128)}, bf16[2,6,64,1024]{3,2,1,0:T(8,128)(2,1)}, bf16[2,6,64,1024]{3,2,1,0:T(8,128)(2,1)}, bf16[2,6,64,1024]{3,2,1,0:T(8,128)(2,1)}) custom-call(s32[2]{0:T(128)} %get-tuple-element.56.refs_0_, s32[2]{0:T(128)} %get-tuple-element.55.refs_1_, s32[24]{0:T(128)} %get-tuple-element.52.sorted_ref.refs_2_, ...), custom_call_target="tpu_custom_call" | custom-call | flops 2147483648 | bytes 32505856 | tf_op jit(solution)/shard_map/chunk/pallas_call | solution.py:319
  164.6 3.1 %collective-permute-done.26 = bf16[2,6,64,1024]{3,2,1,0:T(8,128)(2,1)S(1)} collective-permute-done((bf16[2,6,64,1024]{3,2,1,0:T(8,128)(2,1)}, bf16[2,6,64,1024]{3,2,1,0:T(8,128)(2,1)S(1)}, u32[]{:S(2)}, u32[]{:S(2)}) %collective-permute-start.26) | collective-permute-done | bytes 1572896 | tf_op jit(solution)/shard_map/ppermute | solution.py:420
  167.7 2.1 add_convert_fusion
  170.5 35.8 %collective-permute-done.27.across_ref = bf16[2,6,64,1024]{3,2,1,0:T(8,128)(2,1)S(1)} collective-permute-done((bf16[2,6,64,1024]{3,2,1,0:T(8,128)(2,1)S(1)}, bf16[2,6,64,1024]{3,2,1,0:T(8,128)(2,1)S(1)}, u32[]{:S(2)}, u32[]{:S(2)}) %collective-permute-start.27) | collective-permute-done | bytes 1572896 | tf_op jit(solution)/shard_map/ppermute | solution.py:426
  207.5 5.9 %finish.1 = (bf16[6,64,1024]{2,1,0:T(8,128)(2,1)}, bf16[6,64,1024]{2,1,0:T(8,128)(2,1)}, f32[6,64]{1,0:T(8,128)}) custom-call(s32[6]{0:T(128)} %bitcast.73, bf16[6,64,1024]{2,1,0:T(8,128)(2,1)} %x_ref.1, bf16[6,64,1024]{2,1,0:T(8,128)(2,1)} %g_ref.1, f32[2,1024]{1,0:T(2,128)} %gain_ref.3, f32[6,64,1024]{2,1,0:T(8,128)} %get-tuple-element.46.out_ref, ...), custom_call_target="tpu_custom_call" | custom-call | tf_op jit(solution)/shard_map/finish/pallas_call | solution.py:372
  (97 shorter events, 35.2 us)
Async XLA Ops:
  4.0 36.8 %collective-permute-start.2 = (bf16[2,6,64,1024]{3,2,1,0:T(8,128)(2,1)S(1)}, bf16[2,6,64,1024]{3,2,1,0:T(8,128)(2,1)S(1)}, u32[]{:S(2)}, u32[]{:S(2)}) collective-permute-start(bf16[2,6,64,1024]{3,2,1,0:T(8,128)(2,1)S(1)} %get-tuple-element.60.near_ref), channel_id=1, source_target_pairs={{0,16},{16,0},{1,17},{17,1},{2,18},{18,2},{3,19},{19,3},{4,20},{20... | collective-permute-start | bytes 4718600 | tf_op jit(solution)/shard_map/ppermute | solution.py:426
  8.1 10.9 %collective-permute-start.4 = (bf16[256,256]{1,0:T(8,128)(2,1)S(1)}, bf16[256,256]{1,0:T(8,128)(2,1)S(1)}, u32[]{:S(2)}, u32[]{:S(2)}) collective-permute-start(bf16[256,256]{1,0:T(8,128)(2,1)S(1)} %get-tuple-element.66), channel_id=1, source_target_pairs={{0,4},{1,5},{2,6},{3,7},{4,8},{5,9},{6,10},{7,11},{8,12},{9,13},{1... | collective-permute-start | bytes 393224 | tf_op jit(solution)/shard_map/ppermute | solution.py:429
  9.7 11.6 %collective-permute-start.5 = (bf16[256,256]{1,0:T(8,128)(2,1)S(1)}, bf16[256,256]{1,0:T(8,128)(2,1)S(1)}, u32[]{:S(2)}, u32[]{:S(2)}) collective-permute-start(bf16[256,256]{1,0:T(8,128)(2,1)S(1)} %get-tuple-element.66), channel_id=1, source_target_pairs={{0,8},{1,9},{2,10},{3,11},{4,12},{5,13},{6,14},{7,15},{8,0},{9,1},... | collective-permute-start | bytes 393224 | tf_op jit(solution)/shard_map/ppermute | solution.py:429
  10.9 12.1 %collective-permute-start.6 = (bf16[256,256]{1,0:T(8,128)(2,1)S(1)}, bf16[256,256]{1,0:T(8,128)(2,1)S(1)}, u32[]{:S(2)}, u32[]{:S(2)}) collective-permute-start(bf16[256,256]{1,0:T(8,128)(2,1)S(1)} %get-tuple-element.66), channel_id=1, source_target_pairs={{0,12},{1,13},{2,14},{3,15},{4,0},{5,1},{6,2},{7,3},{8,4},{9,5},{1... | collective-permute-start | bytes 393224 | tf_op jit(solution)/shard_map/ppermute | solution.py:429
  23.1 26.6 %collective-permute-start.10 = (bf16[4,256,256]{2,1,0:T(8,128)(2,1)S(1)}, bf16[4,256,256]{2,1,0:T(8,128)(2,1)S(1)}, u32[]{:S(2)}, u32[]{:S(2)}) collective-permute-start(bf16[4,256,256]{2,1,0:T(8,128)(2,1)S(1)} %pad_maximum_fusion.6.refs_8_), channel_id=1, source_target_pairs={{0,2},{1,3},{2,0},{3,1},{4,6},{5,7},{6,4},{7,5},{8,10},{9,11},{10,... | collective-permute-start | bytes 1572872 | tf_op jit(solution)/shard_map/ppermute | solution.py:423
  25.5 16.5 %collective-permute-start.7 = (bf16[256,512]{1,0:T(8,128)(2,1)S(1)}, bf16[256,512]{1,0:T(8,128)(2,1)S(1)}, u32[]{:S(2)}, u32[]{:S(2)}) collective-permute-start(bf16[256,512]{1,0:T(8,128)(2,1)S(1)} %get-tuple-element.27), channel_id=1, source_target_pairs={{0,4},{1,5},{2,6},{3,7},{4,8},{5,9},{6,10},{7,11},{8,12},{9,13},{1... | collective-permute-start | bytes 786440 | tf_op jit(solution)/shard_map/ppermute | solution.py:429
  25.5 22.6 %collective-permute-start.8 = (bf16[256,512]{1,0:T(8,128)(2,1)S(1)}, bf16[256,512]{1,0:T(8,128)(2,1)S(1)}, u32[]{:S(2)}, u32[]{:S(2)}) collective-permute-start(bf16[256,512]{1,0:T(8,128)(2,1)S(1)} %get-tuple-element.27), channel_id=1, source_target_pairs={{0,8},{1,9},{2,10},{3,11},{4,12},{5,13},{6,14},{7,15},{8,0},{9,1},... | collective-permute-start | bytes 786440 | tf_op jit(solution)/shard_map/ppermute | solution.py:429
  27.1 22.5 %collective-permute-start.9 = (bf16[256,512]{1,0:T(8,128)(2,1)S(1)}, bf16[256,512]{1,0:T(8,128)(2,1)S(1)}, u32[]{:S(2)}, u32[]{:S(2)}) collective-permute-start(bf16[256,512]{1,0:T(8,128)(2,1)S(1)} %get-tuple-element.27), channel_id=1, source_target_pairs={{0,12},{1,13},{2,14},{3,15},{4,0},{5,1},{6,2},{7,3},{8,4},{9,5},{1... | collective-permute-start | bytes 786440 | tf_op jit(solution)/shard_map/ppermute | solution.py:429
  49.7 27.4 %collective-permute-start.11 = (bf16[2,2,6,64,1024]{4,3,2,1,0:T(8,128)(2,1)S(1)}, bf16[2,2,6,64,1024]{4,3,2,1,0:T(8,128)(2,1)S(1)}, u32[]{:S(2)}, u32[]{:S(2)}) collective-permute-start(bf16[2,2,6,64,1024]{4,3,2,1,0:T(8,128)(2,1)S(1)} %pad_maximum_fusion), channel_id=1, source_target_pairs={{0,1},{1,0},{2,3},{3,2},{4,5},{5,4},{6,7},{7,6},{8,9},{9,8},{10,11... | collective-permute-start | bytes 9437192 | tf_op jit(solution)/shard_map/ppermute | solution.py:420
  49.8 27.3 %collective-permute-start.15 = (bf16[4,256,512]{2,1,0:T(8,128)(2,1)S(1)}, bf16[4,256,512]{2,1,0:T(8,128)(2,1)S(1)}, u32[]{:S(2)}, u32[]{:S(2)}) collective-permute-start(bf16[4,256,512]{2,1,0:T(8,128)(2,1)S(1)} %pad_maximum_fusion.3.refs_10_), channel_id=1, source_target_pairs={{0,2},{1,3},{2,0},{3,1},{4,6},{5,7},{6,4},{7,5},{8,10},{9,11},{10,... | collective-permute-start | bytes 3145736 | tf_op jit(solution)/shard_map/ppermute | solution.py:423
  50.4 9.2 %collective-permute-start.12 = (bf16[256,512]{1,0:T(8,128)(2,1)S(1)}, bf16[256,512]{1,0:T(8,128)(2,1)S(1)}, u32[]{:S(2)}, u32[]{:S(2)}) collective-permute-start(bf16[256,512]{1,0:T(8,128)(2,1)S(1)} %get-tuple-element.30), channel_id=1, source_target_pairs={{0,4},{1,5},{2,6},{3,7},{4,8},{5,9},{6,10},{7,11},{8,12},{9,13},{1... | collective-permute-start | bytes 786440 | tf_op jit(solution)/shard_map/ppermute | solution.py:429
  50.5 23.1 %collective-permute-start.13 = (bf16[256,512]{1,0:T(8,128)(2,1)S(1)}, bf16[256,512]{1,0:T(8,128)(2,1)S(1)}, u32[]{:S(2)}, u32[]{:S(2)}) collective-permute-start(bf16[256,512]{1,0:T(8,128)(2,1)S(1)} %get-tuple-element.30), channel_id=1, source_target_pairs={{0,8},{1,9},{2,10},{3,11},{4,12},{5,13},{6,14},{7,15},{8,0},{9,1},... | collective-permute-start | bytes 786440 | tf_op jit(solution)/shard_map/ppermute | solution.py:429
  52.5 23.5 %collective-permute-start.14 = (bf16[256,512]{1,0:T(8,128)(2,1)S(1)}, bf16[256,512]{1,0:T(8,128)(2,1)S(1)}, u32[]{:S(2)}, u32[]{:S(2)}) collective-permute-start(bf16[256,512]{1,0:T(8,128)(2,1)S(1)} %get-tuple-element.30), channel_id=1, source_target_pairs={{0,12},{1,13},{2,14},{3,15},{4,0},{5,1},{6,2},{7,3},{8,4},{9,5},{1... | collective-permute-start | bytes 786440 | tf_op jit(solution)/shard_map/ppermute | solution.py:429
  59.6 20.1 %collective-permute-start = (s32[6]{0:T(128)S(1)}, s32[6]{0:T(128)S(1)}, u32[]{:S(2)}, u32[]{:S(2)}) collective-permute-start(s32[6]{0:T(128)S(1)} %bitcast.74), channel_id=1, source_target_pairs={{0,16},{16,0},{1,17},{17,1},{2,18},{18,2},{3,19},{19,3},{4,20},{20... | collective-permute-start | bytes 80 | tf_op jit(solution)/shard_map/ppermute | solution.py:426
  77.1 28.9 %collective-permute-start.19 = (bf16[4,256,512]{2,1,0:T(8,128)(2,1)}, bf16[4,256,512]{2,1,0:T(8,128)(2,1)}, u32[]{:S(2)}, u32[]{:S(2)}) collective-permute-start(bf16[4,256,512]{2,1,0:T(8,128)(2,1)} %pad_maximum_fusion.4.refs_12_.refs_8_), channel_id=1, source_target_pairs={{0,2},{1,3},{2,0},{3,1},{4,6},{5,7},{6,4},{7,5},{8,10},{9,11},{10,... | collective-permute-start | bytes 3145736 | tf_op jit(solution)/shard_map/ppermute | solution.py:423
  81.1 13.5 %collective-permute-start.16 = (bf16[256,512]{1,0:T(8,128)(2,1)}, bf16[256,512]{1,0:T(8,128)(2,1)S(1)}, u32[]{:S(2)}, u32[]{:S(2)}) collective-permute-start(bf16[256,512]{1,0:T(8,128)(2,1)} %get-tuple-element.35), channel_id=1, source_target_pairs={{0,4},{1,5},{2,6},{3,7},{4,8},{5,9},{6,10},{7,11},{8,12},{9,13},{1... | collective-permute-start | bytes 786440 | tf_op jit(solution)/shard_map/ppermute | solution.py:429
  81.1 23.4 %collective-permute-start.17 = (bf16[256,512]{1,0:T(8,128)(2,1)}, bf16[256,512]{1,0:T(8,128)(2,1)S(1)}, u32[]{:S(2)}, u32[]{:S(2)}) collective-permute-start(bf16[256,512]{1,0:T(8,128)(2,1)} %get-tuple-element.35), channel_id=1, source_target_pairs={{0,8},{1,9},{2,10},{3,11},{4,12},{5,13},{6,14},{7,15},{8,0},{9,1},... | collective-permute-start | bytes 786440 | tf_op jit(solution)/shard_map/ppermute | solution.py:429
  82.2 23.7 %collective-permute-start.18 = (bf16[256,512]{1,0:T(8,128)(2,1)}, bf16[256,512]{1,0:T(8,128)(2,1)S(1)}, u32[]{:S(2)}, u32[]{:S(2)}) collective-permute-start(bf16[256,512]{1,0:T(8,128)(2,1)} %get-tuple-element.35), channel_id=1, source_target_pairs={{0,12},{1,13},{2,14},{3,15},{4,0},{5,1},{6,2},{7,3},{8,4},{9,5},{1... | collective-permute-start | bytes 786440 | tf_op jit(solution)/shard_map/ppermute | solution.py:429
  106.1 25.1 %collective-permute-start.23 = (bf16[4,256,512]{2,1,0:T(8,128)(2,1)S(1)}, bf16[4,256,512]{2,1,0:T(8,128)(2,1)S(1)}, u32[]{:S(2)}, u32[]{:S(2)}) collective-permute-start(bf16[4,256,512]{2,1,0:T(8,128)(2,1)S(1)} %pad_maximum_fusion.5.refs_10_), channel_id=1, source_target_pairs={{0,2},{1,3},{2,0},{3,1},{4,6},{5,7},{6,4},{7,5},{8,10},{9,11},{10,... | collective-permute-start | bytes 3145736 | tf_op jit(solution)/shard_map/ppermute | solution.py:423
  107.9 15.0 %collective-permute-start.20 = (bf16[256,256]{1,0:T(8,128)(2,1)S(1)}, bf16[256,256]{1,0:T(8,128)(2,1)S(1)}, u32[]{:S(2)}, u32[]{:S(2)}) collective-permute-start(bf16[256,256]{1,0:T(8,128)(2,1)S(1)} %copy-done.13), channel_id=1, source_target_pairs={{0,4},{1,5},{2,6},{3,7},{4,8},{5,9},{6,10},{7,11},{8,12},{9,13},{1... | collective-permute-start | bytes 393224 | tf_op jit(solution)/shard_map/ppermute | solution.py:429
  107.9 15.0 %collective-permute-start.21 = (bf16[256,256]{1,0:T(8,128)(2,1)S(1)}, bf16[256,256]{1,0:T(8,128)(2,1)S(1)}, u32[]{:S(2)}, u32[]{:S(2)}) collective-permute-start(bf16[256,256]{1,0:T(8,128)(2,1)S(1)} %copy-done.13), channel_id=1, source_target_pairs={{0,8},{1,9},{2,10},{3,11},{4,12},{5,13},{6,14},{7,15},{8,0},{9,1},... | collective-permute-start | bytes 393224 | tf_op jit(solution)/shard_map/ppermute | solution.py:429
  109.8 13.2 %collective-permute-start.22 = (bf16[256,256]{1,0:T(8,128)(2,1)S(1)}, bf16[256,256]{1,0:T(8,128)(2,1)S(1)}, u32[]{:S(2)}, u32[]{:S(2)}) collective-permute-start(bf16[256,256]{1,0:T(8,128)(2,1)S(1)} %copy-done.13), channel_id=1, source_target_pairs={{0,12},{1,13},{2,14},{3,15},{4,0},{5,1},{6,2},{7,3},{8,4},{9,5},{1... | collective-permute-start | bytes 393224 | tf_op jit(solution)/shard_map/ppermute | solution.py:429
  131.2 16.5 %collective-permute-start.24 = (bf16[4,256,256]{2,1,0:T(8,128)(2,1)S(1)}, bf16[4,256,256]{2,1,0:T(8,128)(2,1)S(1)}, u32[]{:S(2)}, u32[]{:S(2)}) collective-permute-start(bf16[4,256,256]{2,1,0:T(8,128)(2,1)S(1)} %pad_maximum_fusion.7.refs_8_), channel_id=1, source_target_pairs={{0,2},{1,3},{2,0},{3,1},{4,6},{5,7},{6,4},{7,5},{8,10},{9,11},{10,... | collective-permute-start | bytes 1572872 | tf_op jit(solution)/shard_map/ppermute | solution.py:423
  169.8 36.5 %collective-permute-start.27 = (bf16[2,6,64,1024]{3,2,1,0:T(8,128)(2,1)S(1)}, bf16[2,6,64,1024]{3,2,1,0:T(8,128)(2,1)S(1)}, u32[]{:S(2)}, u32[]{:S(2)}) collective-permute-start(bf16[2,6,64,1024]{3,2,1,0:T(8,128)(2,1)S(1)} %add_convert_fusion), channel_id=1, source_target_pairs={{0,16},{16,0},{1,17},{17,1},{2,18},{18,2},{3,19},{19,3},{4,20},{20... | collective-permute-start | bytes 4718600 | tf_op jit(solution)/shard_map/ppermute | solution.py:426
  (22 other events, 249.8 us)

commit v8 on v7

v8 whole, which is shorter than its diff:
```python
import functools
import math

import jax
import jax.numpy as jnp
from jax import lax
from jax.experimental import pallas as pl
from jax.experimental.pallas import tpu as pltpu
from jax.sharding import PartitionSpec as P

coef_c = math.sqrt(2.0 / math.pi)


def gelu_tanh(v):
    return 0.5 * v * (1.0 + jnp.tanh(coef_c * (v + 0.044715 * v * v * v)))


def gelu_slope(v):
    inner = jnp.tanh(coef_c * (v + 0.044715 * v * v * v))
    return 0.5 * (1.0 + inner) + 0.5 * v * (1.0 - inner * inner) * coef_c * (
        1.0 + 3.0 * 0.044715 * v * v
    )


def on_device_general(tokens_in, upstream, member_pick, norm_gain, up_proj, down_proj):
    rows, seq, half = tokens_in.shape
    count = rows * seq
    members = up_proj.shape[0]
    pick = member_pick.shape[1]
    whole_x, whole_g = (
        lax.all_gather(tokens_in, "feat", axis=2, tiled=True),
        lax.all_gather(upstream, "feat", axis=2, tiled=True),
    )
    width = whole_x.shape[2]
    flat_x = whole_x.reshape(count, width).astype(jnp.float32)
    flat_g = whole_g.reshape(count, width)
    inv_rms = 1.0 / jnp.sqrt(jnp.mean(flat_x * flat_x, axis=1, keepdims=True) + 1e-06)
    normed = flat_x * inv_rms
    labels = jnp.arange(members, dtype=jnp.int32)
    chosen = (
        jnp.sum((member_pick[:, :, None] == labels[None, None, :]).astype(jnp.float32), axis=1)
        / pick
    )
    chosen_tok = jnp.repeat(chosen, seq, axis=0)
    out_half = jnp.zeros((count, half), jnp.float32)
    back_half = jnp.zeros((count, half), jnp.float32)
    for member in range(members):
        lifted = (normed * norm_gain[member][None, :]).astype(jnp.bfloat16)
        up_full = lax.all_gather(up_proj[member], "row", axis=0, tiled=True)
        hidden = jnp.dot(lifted, up_full, preferred_element_type=jnp.float32)
        act = gelu_tanh(hidden).astype(jnp.bfloat16)
        piece = lax.all_gather(down_proj[member], "row", axis=0, tiled=True)
        block = lax.dot_general(
            act, piece, (((1,), (1,)), ((), ())), preferred_element_type=jnp.float32
        )
        grads = jnp.dot(flat_g, piece, preferred_element_type=jnp.float32)
        pre_grad = (grads * gelu_slope(hidden)).astype(jnp.bfloat16)
        in_grad = lax.dot_general(
            pre_grad, up_full, (((1,), (1,)), ((), ())), preferred_element_type=jnp.float32
        )
        weight_col = chosen_tok[:, member : member + 1]
        out_term = weight_col * block
        back_term = weight_col * norm_gain[member][None, :] * in_grad
        out_part, back_part = (
            lax.psum_scatter(
                out_term.astype(jnp.bfloat16), "feat", scatter_dimension=1, tiled=True
            ).astype(jnp.float32),
            lax.psum_scatter(
                back_term.astype(jnp.bfloat16), "feat", scatter_dimension=1, tiled=True
            ).astype(jnp.float32),
        )
        out_half = out_half + out_part
        back_half = back_half + back_part
    own_x = tokens_in.reshape(count, half).astype(jnp.float32)
    normed_half = own_x * inv_rms
    stat = lax.psum(jnp.sum(normed_half * back_half, axis=1, keepdims=True), "feat") / width
    coupling = stat * math.sqrt(width)
    own_g = upstream.reshape(count, half).astype(jnp.float32)
    value_out = (own_x + out_half).astype(jnp.bfloat16)
    grad_in = (own_g + (back_half - normed_half * stat) * inv_rms).astype(jnp.bfloat16)
    return (
        value_out.reshape(rows, seq, half),
        grad_in.reshape(rows, seq, half),
        coupling.reshape(rows, seq),
    )


VMEM_LIMIT = 56 * 1024 * 1024
BF16 = jnp.bfloat16
F32 = jnp.float32


def prep_kernel(perm_ref, sorted_ref, near_ref, far_ref, gain_ref, lifted_ref, g_out_ref):
    rows = near_ref.shape[1]

    def row(p, carry):
        at = perm_ref[p]
        i = lax.rem(at, rows)

        def emit(ref):
            x = ref[0, i].astype(F32)
            inv = 1.0 / jnp.sqrt(jnp.mean(x * x, axis=1, keepdims=True) + 1e-06)
            gain = gain_ref[pl.ds(sorted_ref[p], 1), :]
            lifted_ref[p] = ((x * inv) * gain).astype(BF16)
            g_out_ref[p] = ref[1, i]

        @pl.when(at < rows)
        def _():
            emit(near_ref)

        @pl.when(at >= rows)
        def _():
            emit(far_ref)

        return carry

    lax.fori_loop(0, lifted_ref.shape[0], row, 0)


def prep(perm, member_sorted, near, far, gain):
    smem = pl.BlockSpec(memory_space=pltpu.SMEM)
    vmem = pl.BlockSpec(memory_space=pltpu.VMEM)
    shape = (perm.shape[0], *near.shape[2:])
    return pl.pallas_call(
        prep_kernel,
        in_specs=[smem, smem, vmem, vmem, vmem],
        out_specs=[vmem, vmem],
        out_shape=[jax.ShapeDtypeStruct(shape, BF16)] * 2,
        compiler_params=pltpu.CompilerParams(vmem_limit_bytes=VMEM_LIMIT),
        cost_estimate=pl.CostEstimate(
            flops=8 * perm.shape[0] * near.shape[2] * near.shape[3],
            bytes_accessed=16 * perm.shape[0] * near.shape[2] * near.shape[3],
            transcendentals=0,
        ),
        name="prep",
    )(perm, member_sorted, near, far, gain)


def chunk_kernel(
    per_block, kind, units, sorted_ref, place_ref, perm_ref, lifted_ref, g_ref, *refs
):
    first, last = kind
    parts = len(units)
    pieces, refs = refs[: 2 * parts], refs[2 * parts :]
    if first:
        *outs, weights_ref, sems = refs
    elif last:
        out_in, back_in, *outs, weights_ref, sems, out_acc, back_acc = refs
    else:
        out_in, back_in, *outs, weights_ref, sems = refs
    if not last:
        out_acc, back_acc = outs
    j = pl.program_id(0)
    lines, _, depth2, _ = weights_ref.shape
    depth = depth2 // 2
    starts = [sum(n for _, n in units[:part]) for part in range(parts)]

    @pl.when(j == 0)
    def _():
        y, z = place_ref[0], place_ref[1]
        copies = []
        for part in range(parts):
            n = units[part][1]
            for to_y, (ref, start) in zip((y, 1 - y), pieces[2 * part : 2 * part + 2]):
                for d in range(lines):
                    from_z = lax.rem(z + lines - d, lines)
                    copies.append(
                        pltpu.make_async_copy(
                            ref.at[d, :, pl.ds(start, n)],
                            weights_ref.at[from_z, to_y, :, pl.ds(starts[part], n)],
                            sems.at[len(copies)],
                        )
                    )
        for copy in copies:
            copy.start()
        for copy in copies:
            copy.wait()

    width = lifted_ref.shape[1]
    seq = lifted_ref.shape[0] // per_block
    here = [sorted_ref[j * per_block + i] for i in range(per_block)]
    if first:
        out_acc[...] = jnp.zeros(out_acc.shape, F32)
        back_acc[...] = jnp.zeros(back_acc.shape, F32)
    else:
        out_acc[...] = out_in[...]
        back_acc[...] = back_in[...]

    for member in sorted(set(m for m, _ in units)):
        used = functools.reduce(jnp.logical_or, [m == member for m in here])

        @pl.when(used)
        def _():
            lifted = lifted_ref[...]
            g = g_ref[...]
            weight = jnp.concatenate(
                [jnp.full((seq, 1), (m == member).astype(F32), F32) for m in here], axis=0
            )
            out_sum = jnp.zeros(lifted.shape, F32)
            back_sum = jnp.zeros(lifted.shape, F32)
            spans = []
            for (m, n), start in zip(units, starts):
                if m == member:
                    spans += [(s, min(s + 512, start + n)) for s in range(start, start + n, 512)]
            for s, e in spans:
                up = weights_ref[:, :, :depth, s:e].reshape(width, e - s)
                down = weights_ref[:, :, depth:, s:e].reshape(width, e - s)
                v = jnp.dot(lifted, up, preferred_element_type=F32)
                grads = jnp.dot(g, down, preferred_element_type=F32)
                square = v * v
                t = jnp.tanh(coef_c * (v + 0.044715 * square * v))
                act = (0.5 * v * (1.0 + t)).astype(BF16)
                slope = 0.5 * (1.0 + t) + 0.5 * v * (1.0 - t * t) * coef_c * (
                    1.0 + 3.0 * 0.044715 * square
                )
                pre = (grads * slope).astype(BF16)
                dims = (((1,), (1,)), ((), ()))
                out_sum += lax.dot_general(act, down, dims, preferred_element_type=F32)
                back_sum += lax.dot_general(pre, up, dims, preferred_element_type=F32)
            out_acc[...] += weight * out_sum
            back_acc[...] += weight * back_sum

    if last:
        for p in range(per_block):
            row = perm_ref[j * per_block + p]
            tokens = pl.ds(p * seq, seq)
            low = 0
            for to_out, to_back in zip(outs[::2], outs[1::2]):
                n = to_out.shape[0]

                @pl.when(jnp.logical_and(row >= low, row < low + n))
                def _():
                    to = jnp.clip(row - low, 0, n - 1)
                    to_out[to] = out_acc[tokens, :].astype(to_out.dtype)
                    to_back[to] = back_acc[tokens, :].astype(to_back.dtype)

                low += n


def chunk(kind, per_block, scalars, lifted, g, pieces, sums, outs=None, weight=1):
    first, last = kind
    rows, seq, width = lifted.shape
    tokens = rows * seq
    units = [(member, n) for member, n, *_ in pieces]
    lines, depth2, _ = pieces[0][2][0].shape
    hidden = sum(n for _, n in units)
    size = per_block * seq

    tok = pl.BlockSpec((size, width), lambda j, *_: (j, 0))
    hbm = pl.BlockSpec(memory_space=pl.ANY)
    args = [*scalars, lifted.reshape(tokens, width), g.reshape(tokens, width)]
    starts = []
    for _, _, *both in pieces:
        args += [array for array, _ in both]
        starts += [start for _, start in both]
    specs = [tok, tok] + [hbm] * len(starts)
    alias = {}
    out_specs = [tok, tok]
    out_shape = [jax.ShapeDtypeStruct((tokens, width), F32)] * 2
    scratch = [
        pltpu.VMEM((lines, 2, depth2, hidden), BF16),
        pltpu.SemaphoreType.DMA((len(pieces) * 2 * lines,)),
    ]
    if not first:
        alias = {len(args): 0, len(args) + 1: 1}
        args += list(sums)
        specs += [tok, tok]
    if last:
        alias = {}
        shape = (rows // len(outs), seq, width)
        out_shape = [jax.ShapeDtypeStruct(shape, dtype) for dtype in outs for _ in range(2)]
        out_specs = [pl.BlockSpec(shape, lambda *_: (0, 0, 0))] * len(out_shape)
        scratch += [pltpu.VMEM((size, width), F32)] * 2

    def kernel(*refs):
        refs = list(refs)
        base = len(scalars) + 2
        for i, start in enumerate(starts):
            refs[base + i] = (refs[base + i], start)
        chunk_kernel(per_block, kind, units, *refs)

    return pl.pallas_call(
        kernel,
        grid_spec=pltpu.PrefetchScalarGridSpec(
            num_scalar_prefetch=len(scalars),
            grid=(tokens // size,),
            in_specs=specs,
            out_specs=out_specs,
            scratch_shapes=scratch,
        ),
        out_shape=out_shape,
        input_output_aliases=alias,
        compiler_params=pltpu.CompilerParams(vmem_limit_bytes=VMEM_LIMIT),
        cost_estimate=pl.CostEstimate(
            flops=weight * 8 * tokens * width * hidden * 2 // 3,
            bytes_accessed=weight * (4 * width * hidden + 20 * lifted.size),
            transcendentals=weight * tokens * hidden,
        ),
        name="chunk",
    )(*args)


def finish_kernel(
    member_ref, x_ref, g_ref, gain_ref, out_ref, back_ref, other_out_ref, other_back_ref,
    across_ref, value_ref, grad_ref, coupling_ref,
):
    rows, seq, width = x_ref.shape
    diagonal = lax.broadcasted_iota(jnp.int32, (seq, seq), 0) == lax.broadcasted_iota(
        jnp.int32, (seq, seq), 1
    )
    for r in range(rows):
        x = x_ref[r].astype(F32)
        inv = 1.0 / jnp.sqrt(jnp.mean(x * x, axis=1, keepdims=True) + 1e-06)
        normed = x * inv
        gain = gain_ref[pl.ds(member_ref[pl.program_id(0) * rows + r], 1), :]
        back = gain * (
            back_ref[r] + other_back_ref[r].astype(F32) + across_ref[1, r].astype(F32)
        )
        stat = jnp.sum(normed * back, axis=1, keepdims=True) / width
        out = out_ref[r] + other_out_ref[r].astype(F32) + across_ref[0, r].astype(F32)
        value_ref[r] = (x + out).astype(BF16)
        grad_ref[r] = (g_ref[r].astype(F32) + (back - normed * stat) * inv).astype(BF16)
        line = jnp.sum(jnp.where(diagonal, stat, 0.0), axis=0, keepdims=True)
        coupling_ref[pl.ds(pl.program_id(0) * rows + r, 1), :] = line * math.sqrt(width)


def finish(member_own, x, g, gain, *sums):
    rows, seq, width = x.shape
    step = math.gcd(rows, 2)
    row = pl.BlockSpec((step, seq, width), lambda r, mem: (r, 0, 0))
    two = pl.BlockSpec((2, step, seq, width), lambda r, mem: (0, r, 0, 0))
    return pl.pallas_call(
        finish_kernel,
        grid_spec=pltpu.PrefetchScalarGridSpec(
            num_scalar_prefetch=1,
            grid=(rows // step,),
            in_specs=[
                row, row, pl.BlockSpec(gain.shape, lambda r, mem: (0, 0)), row, row, row, row, two
            ],
            out_specs=[row, row, pl.BlockSpec((rows, seq), lambda r, mem: (0, 0))],
        ),
        out_shape=[
            jax.ShapeDtypeStruct((rows, seq, width), BF16),
            jax.ShapeDtypeStruct((rows, seq, width), BF16),
            jax.ShapeDtypeStruct((rows, seq), F32),
        ],
        compiler_params=pltpu.CompilerParams(vmem_limit_bytes=VMEM_LIMIT),
        name="finish",
    )(member_own, x, g, gain, *sums)


def sort_rows(picks):
    index = jnp.arange(picks.shape[0], dtype=jnp.int32)
    before = (picks[None, :] < picks[:, None]) | (
        (picks[None, :] == picks[:, None]) & (index[None, :] < index[:, None])
    )
    pos = jnp.sum(before.astype(jnp.int32), axis=1)
    at = pos[None, :] == index[:, None]
    perm = jnp.sum(jnp.where(at, index[None, :], 0), axis=1)
    return perm, jnp.sum(jnp.where(at, picks[None, :], 0), axis=1)


def on_device_shared(ranks, tokens_in, upstream, member_pick, norm_gain, up_proj, down_proj):
    rows, seq, width = tokens_in.shape
    members, depth, hidden = up_proj.shape
    rank = lax.axis_index("row")
    core = lax.rem(rank, 2)
    x_at = lax.axis_index("grp")
    y_at = lax.rem(rank // 2, 2)
    lines = ranks // 4

    def partner(a):
        return lax.ppermute(a, "row", [(i, i ^ 1) for i in range(ranks)])

    def over_y(a):
        return lax.ppermute(a, "row", [(i, i ^ 2) for i in range(ranks)])

    def over_x(a):
        return lax.ppermute(a, "grp", [(0, 1), (1, 0)])

    def shift_z(a, d):
        return lax.ppermute(a, "row", [(i, (i + 4 * d) % ranks) for i in range(ranks)])

    def after(a, *others):
        return lax.optimization_barrier((a, *others))[0]

    unit = hidden // 32
    quarter, half = 7 * unit, 2 * unit
    both = jnp.stack([up_proj, down_proj], axis=1)

    def units_of(c):
        return jnp.concatenate(
            [
                lax.dynamic_slice_in_dim(both, (2 * x_at + c) * quarter, quarter, 3),
                lax.dynamic_slice_in_dim(both, 4 * quarter + c * half, half, 3),
            ],
            axis=3,
        )

    pick_own = member_pick[:, 0]
    pick_near = jnp.concatenate([pick_own, over_x(pick_own)])
    mine = units_of(core)
    theirs = after(partner(units_of(1 - core)), pick_near)
    even = core == 0
    shard = jnp.concatenate(
        [jnp.where(even, mine, theirs), jnp.where(even, theirs, mine)], axis=2
    ).reshape(members, 4 * depth, quarter + half)

    groups = [
        [(0, 0, 2 * unit)],
        [(0, 2 * unit, 4 * unit)],
        [(0, 6 * unit, unit), (1, 0, 3 * unit)],
        [(1, 3 * unit, 4 * unit)],
        [(0, quarter, half), (1, quarter, half)],
    ]
    send = [
        jnp.concatenate([shard[m, :, at : at + n] for m, at, n in group], axis=1)
        for group in groups
    ]
    here, there = [], []

    def exchange(step, arrived):
        results = []
        if step < len(groups):
            mine = after(send[step], *arrived)
            results += [shift_z(mine, d) for d in range(1, lines)]
        if step > 0:
            there.append(over_y(after(here[step - 1], *arrived)))
            results.append(there[-1])
        if step < len(groups):
            here.append(jnp.stack([send[step], *results[: lines - 1]]))
        return results

    def chunk_pieces(*at):
        pieces = []
        for group in at:
            start = 0
            for member, _, n in groups[group]:
                pieces.append((member, n, (here[group], start), (there[group], start)))
                start += n
        return pieces

    per_block = math.gcd(2 * rows, 4)
    place = jnp.stack([y_at, rank // 4])
    pick_far = partner(after(pick_near, theirs))

    arrived = exchange(0, [])
    arrived += [pick_far]
    near = jnp.stack([after(tokens_in, send[0]), upstream])
    over = over_x(near)

    arrived = exchange(1, arrived)
    arrived += [over]

    set_1, arrived = arrived, exchange(2, arrived)
    far = partner(after(jnp.stack([near, over]), *set_1))
    chips = []
    for i, mine in enumerate((near, over)):
        perm, member_sorted = sort_rows(
            jnp.concatenate([pick_near[i * rows : (i + 1) * rows], pick_far[i * rows : (i + 1) * rows]])
        )
        lifted, g_sorted = prep(perm, member_sorted, mine, far[i], norm_gain)
        chips.append(((member_sorted, place, perm), lifted, g_sorted))
        arrived.append(lifted)
    chip, over_chip = chips

    set_2, arrived = arrived, exchange(3, arrived)
    first = chunk_pieces(0, 1)
    sums = chunk((True, False), per_block, *chip, first, None)
    over_sums = chunk((True, False), per_block, *over_chip, first, None)
    arrived += [sums[0], over_sums[0]]

    set_3, arrived = arrived, exchange(4, arrived)
    second = chunk_pieces(2)
    sums = chunk(
        (False, False), per_block, *chip, second, (after(sums[0], *set_3), sums[1])
    )
    over_sums = chunk(
        (False, False), per_block, *over_chip, second, (after(over_sums[0], *set_3), over_sums[1])
    )
    arrived += [sums[0], over_sums[0]]

    set_4 = arrived
    exchange(5, arrived)
    over_sums = (after(over_sums[0], *set_4), over_sums[1])
    *same, other_out, other_back = chunk(
        (False, True), per_block, *over_chip, chunk_pieces(3), over_sums, (BF16, BF16), 0
    )
    others = partner(jnp.stack([other_out, other_back]))
    across = (jnp.stack(same).astype(F32) + others.astype(F32)).astype(BF16)
    sums = (after(sums[0], across), sums[1])
    across = over_x(across)
    out, back, packed_out, packed_back = chunk(
        (False, True), per_block, *chip, chunk_pieces(3, 4), sums, (F32, BF16), 0
    )
    return tuple(
        finish(
            pick_own, tokens_in, upstream, norm_gain, out, back,
            partner(packed_out), partner(packed_back), across,
        )
    )


def solution(mesh):
    ranks = mesh.shape["row"]
    four = mesh.shape["feat"] == 1 and ranks % 4 == 0 and mesh.shape["grp"] == 2

    def on_device(tokens_in, upstream, member_pick, norm_gain, up_proj, down_proj):
        args = (tokens_in, upstream, member_pick, norm_gain, up_proj, down_proj)
        if four and member_pick.shape[1] == 1 and up_proj.shape[0] == 2:
            return on_device_shared(ranks, *args)
        return on_device_general(*args)

    in_specs = (
        P(("grp", "row"), None, "feat"),
        P(("grp", "row"), None, "feat"),
        P(("grp", "row"), None),
        P(),
        P(None, "row", "feat"),
        P(None, "row", "feat"),
    )
    out_specs = (
        P(("grp", "row"), None, "feat"),
        P(("grp", "row"), None, "feat"),
        P(("grp", "row"), None),
    )
    return jax.shard_map(
        on_device, mesh=mesh, in_specs=in_specs, out_specs=out_specs, check_vma=False
    )
```

time: 214 us -> 211 us (0.986); the launches traced: 214 us -> 208 us
  waiting for transfers between devices: 110 us -> 76.1 us
  Pallas kernels: 57.2 us -> 82.2 us
  local copies, waits for them, and re-layouts: 4.57 us -> 10.2 us
  other arithmetic: 11.9 us -> 7.85 us
    ppermute x3, waiting for transfers between devices: 47.5 us -> 17 us  [over_x(): return lax.ppermute(a, 'grp', [(0, 1), (1, 0)])]
    pallas_call x3 -> x6, Pallas kernels: 41.9 us -> 65.6 us  [chunk(): pl.pallas_call(kernel, grid_spec=pltpu.PrefetchScalarGridSpec(num_scalar_...]
    ppermute x15, waiting for transfers between devices: 50.1 us -> 32.7 us  [shift_z(): lax.ppermute(a, 'row', [(i, (i + 4 * d) % ranks) for i in range(ranks)])]
    ppermute x5, waiting for transfers between devices: 8.17 us -> 21 us  [over_y(): return lax.ppermute(a, 'row', [(i, i ^ 2) for i in range(ranks)])]
    unnamed x36 -> x46, local copies, waits for them, and re-layouts: 2.91 us -> 7.19 us
    squeeze x0 -> x4, local copies, waits for them, and re-layouts: none -> 2.76 us  [the longest x1 2.05 us: on_device_shared(): lifted, g_sorted = prep(perm, member_sorted, mine, far[i], norm_gain)]
    pallas_call x1 -> x2, Pallas kernels: 9.42 us -> 10.7 us  [prep(): pl.pallas_call(prep_kernel, in_specs=[smem, smem, vmem, vmem, vmem], out_...]
    ppermute x5 -> x6, waiting for transfers between devices: 4.23 us -> 5.42 us  [partner(): return lax.ppermute(a, 'row', [(i, i ^ 1) for i in range(ranks)])]
  transfers between devices with their start and end apart: 28 -> 29, of which waited for: 15 -> 15; matrix products, arithmetic and copies ran while one was open for 5% -> 3% of each run, Pallas kernels for 17% -> 32%
where the time goes in v8:
time: 211 us; the launch traced here: 208 us
  Pallas kernels  82.2 us (39%)
  waiting for transfers between devices  76.1 us (36%)
  starting transfers between devices  30.4 us (14%)
  local copies, waits for them, and re-layouts  10.2 us (5%)
  other arithmetic  7.85 us (4%)
    pallas_call x6, Pallas kernels, chunk(): pl.pallas_call(kernel, grid_spec=pltpu.PrefetchScalarGridSpec(num_scalar_...  65.6 us
    ppermute x15, waiting for transfers between devices, shift_z(): lax.ppermute(a, 'row', [(i, (i + 4 * d) % ranks) for i in range(ranks)])  32.7 us
    ppermute x5, waiting for transfers between devices, over_y(): return lax.ppermute(a, 'row', [(i, i ^ 2) for i in range(ranks)])  21 us
    ppermute x15, starting transfers between devices, shift_z(): lax.ppermute(a, 'row', [(i, (i + 4 * d) % ranks) for i in range(ranks)])  19.4 us
    ppermute x3, waiting for transfers between devices, over_x(): return lax.ppermute(a, 'grp', [(0, 1), (1, 0)])  17 us
    pallas_call x2, Pallas kernels, prep(): pl.pallas_call(prep_kernel, in_specs=[smem, smem, vmem, vmem, vmem], out_...  10.7 us
    unnamed x46, local copies, waits for them, and re-layouts  7.19 us
    ppermute x5, starting transfers between devices, over_y(): return lax.ppermute(a, 'row', [(i, i ^ 2) for i in range(ranks)])  6.51 us
  transfers between devices with their start and end apart: 29, of which 15 were waited for; matrix products, arithmetic and copies ran while one was open for 3% of the time, Pallas kernels for 32%

profile of v8, /device:TPU:8, one launch (start us, length us, event | category | flops | bytes accessed | tf_op | source)
XLA Modules:
  0.0 208.0 jit_solution(10634500354609375892)
XLA Ops:
  4.7 2.0 collective-permute-done
  15.0 5.5 %collective-permute-done.4 = bf16[256,256]{1,0:T(8,128)(2,1)S(1)} collective-permute-done((bf16[256,256]{1,0:T(8,128)(2,1)S(1)}, bf16[256,256]{1,0:T(8,128)(2,1)S(1)}, u32[]{:S(2)}, u32[]{:S(2)}) %collective-permute-start.4) | collective-permute-done | bytes 131104 | tf_op jit(solution)/shard_map/ppermute | solution.py:382
  29.1 14.9 %collective-permute-done.3.near_ref = bf16[2,6,64,1024]{3,2,1,0:T(8,128)(2,1)S(1)} collective-permute-done((bf16[2,6,64,1024]{3,2,1,0:T(8,128)(2,1)S(1)}, bf16[2,6,64,1024]{3,2,1,0:T(8,128)(2,1)S(1)}, u32[]{:S(2)}, u32[]{:S(2)}) %collective-permute-start.3) | collective-permute-done | bytes 1572896 | tf_op jit(solution)/shard_map/ppermute | solution.py:379
  45.3 2.9 %collective-permute-done.8 = bf16[256,512]{1,0:T(8,128)(2,1)S(1)} collective-permute-done((bf16[256,512]{1,0:T(8,128)(2,1)S(1)}, bf16[256,512]{1,0:T(8,128)(2,1)S(1)}, u32[]{:S(2)}, u32[]{:S(2)}) %collective-permute-start.8) | collective-permute-done | bytes 262176 | tf_op jit(solution)/shard_map/ppermute | solution.py:382
  51.0 2.2 %collective-permute-start.13 = (bf16[256,512]{1,0:T(8,128)(2,1)S(1)}, bf16[256,512]{1,0:T(8,128)(2,1)S(1)}, u32[]{:S(2)}, u32[]{:S(2)}) collective-permute-start(bf16[256,512]{1,0:T(8,128)(2,1)S(1)} %get-tuple-element.48), channel_id=1, source_target_pairs={{0,8},{1,9},{2,10},{3,11},{4,12},{5,13},{6,14},{7,15},{8,0},{9,1},... | collective-permute-start | bytes 786440 | tf_op jit(solution)/shard_map/ppermute | solution.py:382
  56.7 3.5 %collective-permute-done.12 = bf16[256,512]{1,0:T(8,128)(2,1)S(1)} collective-permute-done((bf16[256,512]{1,0:T(8,128)(2,1)S(1)}, bf16[256,512]{1,0:T(8,128)(2,1)S(1)}, u32[]{:S(2)}, u32[]{:S(2)}) %collective-permute-start.12) | collective-permute-done | bytes 262176 | tf_op jit(solution)/shard_map/ppermute | solution.py:382
  60.2 13.5 %collective-permute-done.13 = bf16[256,512]{1,0:T(8,128)(2,1)S(1)} collective-permute-done((bf16[256,512]{1,0:T(8,128)(2,1)S(1)}, bf16[256,512]{1,0:T(8,128)(2,1)S(1)}, u32[]{:S(2)}, u32[]{:S(2)}) %collective-permute-start.13) | collective-permute-done | bytes 262176 | tf_op jit(solution)/shard_map/ppermute | solution.py:382
  73.7 2.7 %collective-permute-done.14 = bf16[256,512]{1,0:T(8,128)(2,1)S(1)} collective-permute-done((bf16[256,512]{1,0:T(8,128)(2,1)S(1)}, bf16[256,512]{1,0:T(8,128)(2,1)S(1)}, u32[]{:S(2)}, u32[]{:S(2)}) %collective-permute-start.14) | collective-permute-done | bytes 262176 | tf_op jit(solution)/shard_map/ppermute | solution.py:382
  76.6 2.0 slice_bitcast_fusion
  78.6 5.3 %prep.2 = (bf16[12,64,1024]{2,1,0:T(8,128)(2,1)}, bf16[12,64,1024]{2,1,0:T(8,128)(2,1)}) custom-call(s32[12]{0:T(128)} %get-tuple-element.79.perm_ref.refs_2_, s32[12]{0:T(128)} %get-tuple-element.80.sorted_ref.refs_0_, bf16[2,6,64,1024]{3,2,1,0:T(8,128)(2,1)} %copy-done.5, bf16[2,6,64,1024]{3,2,1,0:T(8,128)(2,1)} %get-tuple-element.82.far_ref, ...), custom_call_target="tpu_custom_call" | custom-call | flops 6291456 | bytes 12582912 | tf_op jit(solution)/shard_map/prep/pallas_call | solution.py:124
  84.0 5.3 %prep.3 = (bf16[12,64,1024]{2,1,0:T(8,128)(2,1)}, bf16[12,64,1024]{2,1,0:T(8,128)(2,1)}) custom-call(s32[12]{0:T(128)} %get-tuple-element.78.perm_ref.refs_2_, s32[12]{0:T(128)} %get-tuple-element.77.sorted_ref.refs_0_, bf16[2,6,64,1024]{3,2,1,0:T(8,128)(2,1)} %copy-done.4, bf16[2,6,64,1024]{3,2,1,0:T(8,128)(2,1)} %get-tuple-element.81.far_ref, ...), custom_call_target="tpu_custom_call" | custom-call | flops 6291456 | bytes 12582912 | tf_op jit(solution)/shard_map/prep/pallas_call | solution.py:124
  93.1 2.0 collective-permute-start.18
  95.2 10.1 %chunk.7 = (f32[768,1024]{1,0:T(8,128)}, f32[768,1024]{1,0:T(8,128)}) custom-call(s32[12]{0:T(128)} %get-tuple-element.77.sorted_ref.refs_0_, s32[2]{0:T(128)} %pad_add_fusion.2.refs_1_, s32[12]{0:T(128)} %get-tuple-element.78.perm_ref.refs_2_, bf16[768,1024]{1,0:T(8,128)(2,1)} %bitcast.63, bf16[768,1024]{1,0:T(8,128)(2,1)} %bitcast.66, ...), custom_call_target="tpu_custom_call" | custom-call | flops 3221225472 | bytes 18874368 | tf_op jit(solution)/shard_map/chunk/pallas_call | solution.py:282
  105.2 10.1 %chunk.6 = (f32[768,1024]{1,0:T(8,128)}, f32[768,1024]{1,0:T(8,128)}) custom-call(s32[12]{0:T(128)} %get-tuple-element.80.sorted_ref.refs_0_, s32[2]{0:T(128)} %pad_add_fusion.2.refs_1_, s32[12]{0:T(128)} %get-tuple-element.79.perm_ref.refs_2_, bf16[768,1024]{1,0:T(8,128)(2,1)} %bitcast.57, bf16[768,1024]{1,0:T(8,128)(2,1)} %bitcast.60, ...), custom_call_target="tpu_custom_call" | custom-call | flops 3221225472 | bytes 18874368 | tf_op jit(solution)/shard_map/chunk/pallas_call | solution.py:282
  115.6 2.0 collective-permute-start.20
  117.9 2.1 %collective-permute-start.22 = (bf16[256,512]{1,0:T(8,128)(2,1)S(1)}, bf16[256,512]{1,0:T(8,128)(2,1)S(1)}, u32[]{:S(2)}, u32[]{:S(2)}) collective-permute-start(bf16[256,512]{1,0:T(8,128)(2,1)S(1)} %get-tuple-element.57), channel_id=1, source_target_pairs={{0,8},{1,9},{2,10},{3,11},{4,12},{5,13},{6,14},{7,15},{8,0},{9,1},... | collective-permute-start | bytes 786440 | tf_op jit(solution)/shard_map/ppermute | solution.py:382
  121.9 11.5 %chunk.9 = (f32[768,1024]{1,0:T(8,128)}, f32[768,1024]{1,0:T(8,128)}) custom-call(s32[12]{0:T(128)} %get-tuple-element.77.sorted_ref.refs_0_, s32[2]{0:T(128)} %pad_add_fusion.2.refs_1_, s32[12]{0:T(128)} %get-tuple-element.78.perm_ref.refs_2_, bf16[768,1024]{1,0:T(8,128)(2,1)} %bitcast.64, ...), custom_call_target="tpu_custom_call", output_to_operand_aliasing={{0}: (9, {}), {1}: (10, {})} | custom-call | flops 2147483648 | bytes 17825792 | tf_op jit(solution)/shard_map/chunk/pallas_call | solution.py:282
  133.4 11.5 %chunk.8 = (f32[768,1024]{1,0:T(8,128)}, f32[768,1024]{1,0:T(8,128)}) custom-call(s32[12]{0:T(128)} %get-tuple-element.80.sorted_ref.refs_0_, s32[2]{0:T(128)} %pad_add_fusion.2.refs_1_, s32[12]{0:T(128)} %get-tuple-element.79.perm_ref.refs_2_, bf16[768,1024]{1,0:T(8,128)(2,1)} %bitcast.58, ...), custom_call_target="tpu_custom_call", output_to_operand_aliasing={{0}: (9, {}), {1}: (10, {})} | custom-call | flops 2147483648 | bytes 17825792 | tf_op jit(solution)/shard_map/chunk/pallas_call | solution.py:282
  145.9 9.8 %chunk.10 = (bf16[6,64,1024]{2,1,0:T(8,128)(2,1)}, bf16[6,64,1024]{2,1,0:T(8,128)(2,1)}, bf16[6,64,1024]{2,1,0:T(8,128)(2,1)}, bf16[6,64,1024]{2,1,0:T(8,128)(2,1)}) custom-call(s32[12]{0:T(128)} %get-tuple-element.77.sorted_ref.refs_0_, s32[2]{0:T(128)} %pad_add_fusion.2.refs_1_, s32[12]{0:T(128)} %get-tuple-element.78.perm_ref.refs_2_, ...), custom_call_target="tpu_custom_call" | custom-call | tf_op jit(solution)/shard_map/chunk/pallas_call | solution.py:282
  158.4 2.3 %collective-permute-done.25 = bf16[2,6,64,1024]{3,2,1,0:T(8,128)(2,1)S(1)} collective-permute-done((bf16[2,6,64,1024]{3,2,1,0:T(8,128)(2,1)S(1)}, bf16[2,6,64,1024]{3,2,1,0:T(8,128)(2,1)S(1)}, u32[]{:S(2)}, u32[]{:S(2)}) %collective-permute-start.25) | collective-permute-done | bytes 1572896 | tf_op jit(solution)/shard_map/ppermute | solution.py:373
  162.1 21.0 %collective-permute-done.24.refs_8_.refs_10_ = bf16[4,256,512]{2,1,0:T(8,128)(2,1)S(1)} collective-permute-done((bf16[4,256,512]{2,1,0:T(8,128)(2,1)S(1)}, bf16[4,256,512]{2,1,0:T(8,128)(2,1)S(1)}, u32[]{:S(2)}, u32[]{:S(2)}) %collective-permute-start.24) | collective-permute-done | bytes 1048608 | tf_op jit(solution)/shard_map/ppermute | solution.py:376
  184.1 12.7 %chunk.11 = (f32[6,64,1024]{2,1,0:T(8,128)}, f32[6,64,1024]{2,1,0:T(8,128)}, bf16[6,64,1024]{2,1,0:T(8,128)(2,1)}, bf16[6,64,1024]{2,1,0:T(8,128)(2,1)}) custom-call(s32[12]{0:T(128)} %get-tuple-element.80.sorted_ref.refs_0_, s32[2]{0:T(128)} %pad_add_fusion.2.refs_1_, s32[12]{0:T(128)} %get-tuple-element.79.perm_ref.refs_2_, bf16[768,1024]{1,0:T(8,128)(2,1)} %bitcast.59, ...), custom_call_target="tpu_custom_call" | custom-call | tf_op jit(solution)/shard_map/chunk/pallas_call | solution.py:282
  197.4 2.0 collective-permute-done.26.other_out_ref
  201.9 5.9 %finish.1 = (bf16[6,64,1024]{2,1,0:T(8,128)(2,1)}, bf16[6,64,1024]{2,1,0:T(8,128)(2,1)}, f32[6,64]{1,0:T(8,128)}) custom-call(s32[6]{0:T(128)} %bitcast.98, bf16[6,64,1024]{2,1,0:T(8,128)(2,1)} %x_ref.1, bf16[6,64,1024]{2,1,0:T(8,128)(2,1)} %g_ref.1, f32[2,1024]{1,0:T(2,128)} %gain_ref.5, f32[6,64,1024]{2,1,0:T(8,128)} %get-tuple-element.73.out_ref, ...), custom_call_target="tpu_custom_call" | custom-call | tf_op jit(solution)/shard_map/finish/pallas_call | solution.py:332
  (119 shorter events, 43.7 us)
Async XLA Ops:
  8.8 35.2 %collective-permute-start.3 = (bf16[2,6,64,1024]{3,2,1,0:T(8,128)(2,1)S(1)}, bf16[2,6,64,1024]{3,2,1,0:T(8,128)(2,1)S(1)}, u32[]{:S(2)}, u32[]{:S(2)}) collective-permute-start(bf16[2,6,64,1024]{3,2,1,0:T(8,128)(2,1)S(1)} %get-tuple-element.88.near_ref), channel_id=1, source_target_pairs={{0,16},{16,0},{1,17},{17,1},{2,18},{18,2},{3,19},{19,3},{4,20},{20... | collective-permute-start | bytes 4718600 | tf_op jit(solution)/shard_map/ppermute | solution.py:379
  10.4 10.1 %collective-permute-start.4 = (bf16[256,256]{1,0:T(8,128)(2,1)S(1)}, bf16[256,256]{1,0:T(8,128)(2,1)S(1)}, u32[]{:S(2)}, u32[]{:S(2)}) collective-permute-start(bf16[256,256]{1,0:T(8,128)(2,1)S(1)} %get-tuple-element.90), channel_id=1, source_target_pairs={{0,4},{1,5},{2,6},{3,7},{4,8},{5,9},{6,10},{7,11},{8,12},{9,13},{1... | collective-permute-start | bytes 393224 | tf_op jit(solution)/shard_map/ppermute | solution.py:382
  12.0 9.9 %collective-permute-start.5 = (bf16[256,256]{1,0:T(8,128)(2,1)S(1)}, bf16[256,256]{1,0:T(8,128)(2,1)S(1)}, u32[]{:S(2)}, u32[]{:S(2)}) collective-permute-start(bf16[256,256]{1,0:T(8,128)(2,1)S(1)} %get-tuple-element.90), channel_id=1, source_target_pairs={{0,8},{1,9},{2,10},{3,11},{4,12},{5,13},{6,14},{7,15},{8,0},{9,1},... | collective-permute-start | bytes 393224 | tf_op jit(solution)/shard_map/ppermute | solution.py:382
  13.2 10.5 %collective-permute-start.6 = (bf16[256,256]{1,0:T(8,128)(2,1)S(1)}, bf16[256,256]{1,0:T(8,128)(2,1)S(1)}, u32[]{:S(2)}, u32[]{:S(2)}) collective-permute-start(bf16[256,256]{1,0:T(8,128)(2,1)S(1)} %get-tuple-element.90), channel_id=1, source_target_pairs={{0,12},{1,13},{2,14},{3,15},{4,0},{5,1},{6,2},{7,3},{8,4},{9,5},{1... | collective-permute-start | bytes 393224 | tf_op jit(solution)/shard_map/ppermute | solution.py:382
  15.0 8.8 %collective-permute-start.2 = (s32[12]{0:T(128)S(1)}, s32[12]{0:T(128)S(1)}, u32[]{:S(2)}, u32[]{:S(2)}) collective-permute-start(s32[12]{0:T(128)S(1)} %pad_add_fusion), channel_id=1, source_target_pairs={{0,1},{1,0},{2,3},{3,2},{4,5},{5,4},{6,7},{7,6},{8,9},{9,8},{10,11... | collective-permute-start | bytes 152 | tf_op jit(solution)/shard_map/ppermute | solution.py:373
  23.9 25.6 %collective-permute-start.10 = (bf16[4,256,256]{2,1,0:T(8,128)(2,1)S(1)}, bf16[4,256,256]{2,1,0:T(8,128)(2,1)S(1)}, u32[]{:S(2)}, u32[]{:S(2)}) collective-permute-start(bf16[4,256,256]{2,1,0:T(8,128)(2,1)S(1)} %pad_maximum_fusion.10.refs_5_), channel_id=1, source_target_pairs={{0,2},{1,3},{2,0},{3,1},{4,6},{5,7},{6,4},{7,5},{8,10},{9,11},{10,... | collective-permute-start | bytes 1572872 | tf_op jit(solution)/shard_map/ppermute | solution.py:376
  25.5 19.7 %collective-permute-start.7 = (bf16[256,512]{1,0:T(8,128)(2,1)S(1)}, bf16[256,512]{1,0:T(8,128)(2,1)S(1)}, u32[]{:S(2)}, u32[]{:S(2)}) collective-permute-start(bf16[256,512]{1,0:T(8,128)(2,1)S(1)} %get-tuple-element.43), channel_id=1, source_target_pairs={{0,4},{1,5},{2,6},{3,7},{4,8},{5,9},{6,10},{7,11},{8,12},{9,13},{1... | collective-permute-start | bytes 786440 | tf_op jit(solution)/shard_map/ppermute | solution.py:382
  25.6 22.6 %collective-permute-start.8 = (bf16[256,512]{1,0:T(8,128)(2,1)S(1)}, bf16[256,512]{1,0:T(8,128)(2,1)S(1)}, u32[]{:S(2)}, u32[]{:S(2)}) collective-permute-start(bf16[256,512]{1,0:T(8,128)(2,1)S(1)} %get-tuple-element.43), channel_id=1, source_target_pairs={{0,8},{1,9},{2,10},{3,11},{4,12},{5,13},{6,14},{7,15},{8,0},{9,1},... | collective-permute-start | bytes 786440 | tf_op jit(solution)/shard_map/ppermute | solution.py:382
  27.2 22.2 %collective-permute-start.9 = (bf16[256,512]{1,0:T(8,128)(2,1)S(1)}, bf16[256,512]{1,0:T(8,128)(2,1)S(1)}, u32[]{:S(2)}, u32[]{:S(2)}) collective-permute-start(bf16[256,512]{1,0:T(8,128)(2,1)S(1)} %get-tuple-element.43), channel_id=1, source_target_pairs={{0,12},{1,13},{2,14},{3,15},{4,0},{5,1},{6,2},{7,3},{8,4},{9,5},{1... | collective-permute-start | bytes 786440 | tf_op jit(solution)/shard_map/ppermute | solution.py:382
  49.4 27.2 %collective-permute-start.11 = (bf16[2,2,6,64,1024]{4,3,2,1,0:T(8,128)(2,1)S(1)}, bf16[2,2,6,64,1024]{4,3,2,1,0:T(8,128)(2,1)S(1)}, u32[]{:S(2)}, u32[]{:S(2)}) collective-permute-start(bf16[2,2,6,64,1024]{4,3,2,1,0:T(8,128)(2,1)S(1)} %pad_maximum_fusion), channel_id=1, source_target_pairs={{0,1},{1,0},{2,3},{3,2},{4,5},{5,4},{6,7},{7,6},{8,9},{9,8},{10,11... | collective-permute-start | bytes 9437192 | tf_op jit(solution)/shard_map/ppermute | solution.py:373
  50.2 39.1 %collective-permute-start.15 = (bf16[4,256,512]{2,1,0:T(8,128)(2,1)S(1)}, bf16[4,256,512]{2,1,0:T(8,128)(2,1)S(1)}, u32[]{:S(2)}, u32[]{:S(2)}) collective-permute-start(bf16[4,256,512]{2,1,0:T(8,128)(2,1)S(1)} %pad_maximum_fusion.4.refs_7_), channel_id=1, source_target_pairs={{0,2},{1,3},{2,0},{3,1},{4,6},{5,7},{6,4},{7,5},{8,10},{9,11},{10,... | collective-permute-start | bytes 3145736 | tf_op jit(solution)/shard_map/ppermute | solution.py:376
  51.0 9.2 %collective-permute-start.12 = (bf16[256,512]{1,0:T(8,128)(2,1)S(1)}, bf16[256,512]{1,0:T(8,128)(2,1)S(1)}, u32[]{:S(2)}, u32[]{:S(2)}) collective-permute-start(bf16[256,512]{1,0:T(8,128)(2,1)S(1)} %get-tuple-element.48), channel_id=1, source_target_pairs={{0,4},{1,5},{2,6},{3,7},{4,8},{5,9},{6,10},{7,11},{8,12},{9,13},{1... | collective-permute-start | bytes 786440 | tf_op jit(solution)/shard_map/ppermute | solution.py:382
  51.0 22.7 %collective-permute-start.13 = (bf16[256,512]{1,0:T(8,128)(2,1)S(1)}, bf16[256,512]{1,0:T(8,128)(2,1)S(1)}, u32[]{:S(2)}, u32[]{:S(2)}) collective-permute-start(bf16[256,512]{1,0:T(8,128)(2,1)S(1)} %get-tuple-element.48), channel_id=1, source_target_pairs={{0,8},{1,9},{2,10},{3,11},{4,12},{5,13},{6,14},{7,15},{8,0},{9,1},... | collective-permute-start | bytes 786440 | tf_op jit(solution)/shard_map/ppermute | solution.py:382
  53.3 23.2 %collective-permute-start.14 = (bf16[256,512]{1,0:T(8,128)(2,1)S(1)}, bf16[256,512]{1,0:T(8,128)(2,1)S(1)}, u32[]{:S(2)}, u32[]{:S(2)}) collective-permute-start(bf16[256,512]{1,0:T(8,128)(2,1)S(1)} %get-tuple-element.48), channel_id=1, source_target_pairs={{0,12},{1,13},{2,14},{3,15},{4,0},{5,1},{6,2},{7,3},{8,4},{9,5},{1... | collective-permute-start | bytes 786440 | tf_op jit(solution)/shard_map/ppermute | solution.py:382
  90.3 25.3 %collective-permute-start.19 = (bf16[4,256,512]{2,1,0:T(8,128)(2,1)S(1)}, bf16[4,256,512]{2,1,0:T(8,128)(2,1)S(1)}, u32[]{:S(2)}, u32[]{:S(2)}) collective-permute-start(bf16[4,256,512]{2,1,0:T(8,128)(2,1)S(1)} %pad_maximum_fusion.6.refs_5_.refs_7_), channel_id=1, source_target_pairs={{0,2},{1,3},{2,0},{3,1},{4,6},{5,7},{6,4},{7,5},{8,10},{9,11},{10,... | collective-permute-start | bytes 3145736 | tf_op jit(solution)/shard_map/ppermute | solution.py:376
  92.5 22.9 %collective-permute-start.16 = (bf16[256,512]{1,0:T(8,128)(2,1)S(1)}, bf16[256,512]{1,0:T(8,128)(2,1)S(1)}, u32[]{:S(2)}, u32[]{:S(2)}) collective-permute-start(bf16[256,512]{1,0:T(8,128)(2,1)S(1)} %get-tuple-element.51), channel_id=1, source_target_pairs={{0,4},{1,5},{2,6},{3,7},{4,8},{5,9},{6,10},{7,11},{8,12},{9,13},{1... | collective-permute-start | bytes 786440 | tf_op jit(solution)/shard_map/ppermute | solution.py:382
  92.5 22.9 %collective-permute-start.17 = (bf16[256,512]{1,0:T(8,128)(2,1)S(1)}, bf16[256,512]{1,0:T(8,128)(2,1)S(1)}, u32[]{:S(2)}, u32[]{:S(2)}) collective-permute-start(bf16[256,512]{1,0:T(8,128)(2,1)S(1)} %get-tuple-element.51), channel_id=1, source_target_pairs={{0,8},{1,9},{2,10},{3,11},{4,12},{5,13},{6,14},{7,15},{8,0},{9,1},... | collective-permute-start | bytes 786440 | tf_op jit(solution)/shard_map/ppermute | solution.py:382
  93.1 22.3 %collective-permute-start.18 = (bf16[256,512]{1,0:T(8,128)(2,1)S(1)}, bf16[256,512]{1,0:T(8,128)(2,1)S(1)}, u32[]{:S(2)}, u32[]{:S(2)}) collective-permute-start(bf16[256,512]{1,0:T(8,128)(2,1)S(1)} %get-tuple-element.51), channel_id=1, source_target_pairs={{0,12},{1,13},{2,14},{3,15},{4,0},{5,1},{6,2},{7,3},{8,4},{9,5},{1... | collective-permute-start | bytes 786440 | tf_op jit(solution)/shard_map/ppermute | solution.py:382
  115.6 29.3 %collective-permute-start.20 = (bf16[4,256,512]{2,1,0:T(8,128)(2,1)S(1)}, bf16[4,256,512]{2,1,0:T(8,128)(2,1)S(1)}, u32[]{:S(2)}, u32[]{:S(2)}) collective-permute-start(bf16[4,256,512]{2,1,0:T(8,128)(2,1)S(1)} %pad_maximum_fusion.5.refs_5_), channel_id=1, source_target_pairs={{0,2},{1,3},{2,0},{3,1},{4,6},{5,7},{6,4},{7,5},{8,10},{9,11},{10,... | collective-permute-start | bytes 3145736 | tf_op jit(solution)/shard_map/ppermute | solution.py:376
  117.6 27.3 %collective-permute-start.21 = (bf16[256,512]{1,0:T(8,128)(2,1)S(1)}, bf16[256,512]{1,0:T(8,128)(2,1)S(1)}, u32[]{:S(2)}, u32[]{:S(2)}) collective-permute-start(bf16[256,512]{1,0:T(8,128)(2,1)S(1)} %get-tuple-element.57), channel_id=1, source_target_pairs={{0,4},{1,5},{2,6},{3,7},{4,8},{5,9},{6,10},{7,11},{8,12},{9,13},{1... | collective-permute-start | bytes 786440 | tf_op jit(solution)/shard_map/ppermute | solution.py:382
  117.9 27.1 %collective-permute-start.22 = (bf16[256,512]{1,0:T(8,128)(2,1)S(1)}, bf16[256,512]{1,0:T(8,128)(2,1)S(1)}, u32[]{:S(2)}, u32[]{:S(2)}) collective-permute-start(bf16[256,512]{1,0:T(8,128)(2,1)S(1)} %get-tuple-element.57), channel_id=1, source_target_pairs={{0,8},{1,9},{2,10},{3,11},{4,12},{5,13},{6,14},{7,15},{8,0},{9,1},... | collective-permute-start | bytes 786440 | tf_op jit(solution)/shard_map/ppermute | solution.py:382
  120.0 25.0 %collective-permute-start.23 = (bf16[256,512]{1,0:T(8,128)(2,1)S(1)}, bf16[256,512]{1,0:T(8,128)(2,1)S(1)}, u32[]{:S(2)}, u32[]{:S(2)}) collective-permute-start(bf16[256,512]{1,0:T(8,128)(2,1)S(1)} %get-tuple-element.57), channel_id=1, source_target_pairs={{0,12},{1,13},{2,14},{3,15},{4,0},{5,1},{6,2},{7,3},{8,4},{9,5},{1... | collective-permute-start | bytes 786440 | tf_op jit(solution)/shard_map/ppermute | solution.py:382
  157.5 25.6 %collective-permute-start.24 = (bf16[4,256,512]{2,1,0:T(8,128)(2,1)S(1)}, bf16[4,256,512]{2,1,0:T(8,128)(2,1)S(1)}, u32[]{:S(2)}, u32[]{:S(2)}) collective-permute-start(bf16[4,256,512]{2,1,0:T(8,128)(2,1)S(1)} %pad_maximum_fusion.7.refs_7_.refs_9_), channel_id=1, source_target_pairs={{0,2},{1,3},{2,0},{3,1},{4,6},{5,7},{6,4},{7,5},{8,10},{9,11},{10,... | collective-permute-start | bytes 3145736 | tf_op jit(solution)/shard_map/ppermute | solution.py:376
  161.5 39.0 %collective-permute-start.28 = (bf16[2,6,64,1024]{3,2,1,0:T(8,128)(2,1)S(1)}, bf16[2,6,64,1024]{3,2,1,0:T(8,128)(2,1)S(1)}, u32[]{:S(2)}, u32[]{:S(2)}) collective-permute-start(bf16[2,6,64,1024]{3,2,1,0:T(8,128)(2,1)S(1)} %add_convert_fusion), channel_id=1, source_target_pairs={{0,16},{16,0},{1,17},{17,1},{2,18},{18,2},{3,19},{19,3},{4,20},{20... | collective-permute-start | bytes 4718600 | tf_op jit(solution)/shard_map/ppermute | solution.py:379
  (28 other events, 168.1 us)

commit v9 on v8

--- a/solution.py
+++ b/solution.py
@@ -90,67 +90,24 @@
 F32 = jnp.float32
 
 
-def prep_kernel(perm_ref, sorted_ref, near_ref, far_ref, gain_ref, lifted_ref, g_out_ref):
-    rows = near_ref.shape[1]
-
-    def row(p, carry):
-        at = perm_ref[p]
-        i = lax.rem(at, rows)
-
-        def emit(ref):
-            x = ref[0, i].astype(F32)
-            inv = 1.0 / jnp.sqrt(jnp.mean(x * x, axis=1, keepdims=True) + 1e-06)
-            gain = gain_ref[pl.ds(sorted_ref[p], 1), :]
-            lifted_ref[p] = ((x * inv) * gain).astype(BF16)
-            g_out_ref[p] = ref[1, i]
-
-        @pl.when(at < rows)
-        def _():
-            emit(near_ref)
-
-        @pl.when(at >= rows)
-        def _():
-            emit(far_ref)
-
-        return carry
-
-    lax.fori_loop(0, lifted_ref.shape[0], row, 0)
-
-
-def prep(perm, member_sorted, near, far, gain):
-    smem = pl.BlockSpec(memory_space=pltpu.SMEM)
-    vmem = pl.BlockSpec(memory_space=pltpu.VMEM)
-    shape = (perm.shape[0], *near.shape[2:])
-    return pl.pallas_call(
-        prep_kernel,
-        in_specs=[smem, smem, vmem, vmem, vmem],
-        out_specs=[vmem, vmem],
-        out_shape=[jax.ShapeDtypeStruct(shape, BF16)] * 2,
-        compiler_params=pltpu.CompilerParams(vmem_limit_bytes=VMEM_LIMIT),
-        cost_estimate=pl.CostEstimate(
-            flops=8 * perm.shape[0] * near.shape[2] * near.shape[3],
-            bytes_accessed=16 * perm.shape[0] * near.shape[2] * near.shape[3],
-            transcendentals=0,
-        ),
-        name="prep",
-    )(perm, member_sorted, near, far, gain)
-
-
 def chunk_kernel(
-    per_block, kind, units, sorted_ref, place_ref, perm_ref, lifted_ref, g_ref, *refs
+    offset, kind, units, sorted_ref, place_ref, perm_ref, near_ref, over_ref, far_ref, *refs
 ):
     first, last = kind
     parts = len(units)
     pieces, refs = refs[: 2 * parts], refs[2 * parts :]
     if first:
-        *outs, weights_ref, sems = refs
+        *outs, weights_ref, sems, lifted_ref, g_ref = refs
     elif last:
-        out_in, back_in, *outs, weights_ref, sems, out_acc, back_acc = refs
+        out_in, back_in, *outs, weights_ref, sems, lifted_ref, g_ref, out_acc, back_acc = refs
     else:
-        out_in, back_in, *outs, weights_ref, sems = refs
+        out_in, back_in, *outs, weights_ref, sems, lifted_ref, g_ref = refs
     if not last:
         out_acc, back_acc = outs
     j = pl.program_id(0)
+    rows, seq = near_ref.shape[1:3]
+    per_block = lifted_ref.shape[0] // seq
+    places = [(j + offset) * per_block + i for i in range(per_block)]
     lines, _, depth2, _ = weights_ref.shape
     depth = depth2 // 2
     starts = [sum(n for _, n in units[:part]) for part in range(parts)]
@@ -176,9 +133,19 @@
         for copy in copies:
             copy.wait()
 
+    for i, at in enumerate(places):
+        row = perm_ref[at]
+        source = row // rows
+        for k, ref in enumerate((near_ref, far_ref.at[0], over_ref, far_ref.at[1])):
+
+            @pl.when(source == k)
+            def _():
+                tokens = pl.ds(i * seq, seq)
+                lifted_ref[tokens, :] = ref[0, row - k * rows]
+                g_ref[tokens, :] = ref[1, row - k * rows]
+
     width = lifted_ref.shape[1]
-    seq = lifted_ref.shape[0] // per_block
-    here = [sorted_ref[j * per_block + i] for i in range(per_block)]
+    here = [sorted_ref[at] for at in places]
     if first:
         out_acc[...] = jnp.zeros(out_acc.shape, F32)
         back_acc[...] = jnp.zeros(back_acc.shape, F32)
@@ -221,8 +188,8 @@
             back_acc[...] += weight * back_sum
 
     if last:
-        for p in range(per_block):
-            row = perm_ref[j * per_block + p]
+        for p, at in enumerate(places):
+            row = lax.rem(perm_ref[at], 2 * rows)
             tokens = pl.ds(p * seq, seq)
             low = 0
             for to_out, to_back in zip(outs[::2], outs[1::2]):
@@ -237,29 +204,35 @@
                 low += n
 
 
-def chunk(kind, per_block, scalars, lifted, g, pieces, sums, outs=None, weight=1):
+def chunk(kind, blocks, scalars, tokens_of, pieces, sums, outs=None, weight=1):
     first, last = kind
-    rows, seq, width = lifted.shape
-    tokens = rows * seq
+    offset, number, per_block = blocks
+    _, rows, seq, width = tokens_of[0].shape
     units = [(member, n) for member, n, *_ in pieces]
     lines, depth2, _ = pieces[0][2][0].shape
     hidden = sum(n for _, n in units)
     size = per_block * seq
 
-    tok = pl.BlockSpec((size, width), lambda j, *_: (j, 0))
+    tok = pl.BlockSpec((size, width), lambda j, *_: (j + offset, 0))
     hbm = pl.BlockSpec(memory_space=pl.ANY)
-    args = [*scalars, lifted.reshape(tokens, width), g.reshape(tokens, width)]
+    args = [*scalars, *tokens_of]
+    specs = [
+        pl.BlockSpec(a.shape, lambda *_, n=a.ndim: (0,) * n, pipeline_mode=pl.Buffered(1))
+        for a in tokens_of
+    ]
     starts = []
     for _, _, *both in pieces:
         args += [array for array, _ in both]
         starts += [start for _, start in both]
-    specs = [tok, tok] + [hbm] * len(starts)
+    specs += [hbm] * len(starts)
     alias = {}
     out_specs = [tok, tok]
-    out_shape = [jax.ShapeDtypeStruct((tokens, width), F32)] * 2
+    out_shape = [jax.ShapeDtypeStruct((4 * rows * seq, width), F32)] * 2
     scratch = [
         pltpu.VMEM((lines, 2, depth2, hidden), BF16),
         pltpu.SemaphoreType.DMA((len(pieces) * 2 * lines,)),
+        pltpu.VMEM((size, width), BF16),
+        pltpu.VMEM((size, width), BF16),
     ]
     if not first:
         alias = {len(args): 0, len(args) + 1: 1}
@@ -267,23 +240,23 @@
         specs += [tok, tok]
     if last:
         alias = {}
-        shape = (rows // len(outs), seq, width)
+        shape = (rows, seq, width)
         out_shape = [jax.ShapeDtypeStruct(shape, dtype) for dtype in outs for _ in range(2)]
         out_specs = [pl.BlockSpec(shape, lambda *_: (0, 0, 0))] * len(out_shape)
         scratch += [pltpu.VMEM((size, width), F32)] * 2
 
     def kernel(*refs):
         refs = list(refs)
-        base = len(scalars) + 2
+        base = len(scalars) + len(tokens_of)
         for i, start in enumerate(starts):
             refs[base + i] = (refs[base + i], start)
-        chunk_kernel(per_block, kind, units, *refs)
+        chunk_kernel(offset, kind, units, *refs)
 
     return pl.pallas_call(
         kernel,
         grid_spec=pltpu.PrefetchScalarGridSpec(
             num_scalar_prefetch=len(scalars),
-            grid=(tokens // size,),
+            grid=(number,),
             in_specs=specs,
             out_specs=out_specs,
             scratch_shapes=scratch,
@@ -292,9 +265,9 @@
         input_output_aliases=alias,
         compiler_params=pltpu.CompilerParams(vmem_limit_bytes=VMEM_LIMIT),
         cost_estimate=pl.CostEstimate(
-            flops=weight * 8 * tokens * width * hidden * 2 // 3,
-            bytes_accessed=weight * (4 * width * hidden + 20 * lifted.size),
-            transcendentals=weight * tokens * hidden,
+            flops=weight * 8 * number * size * width * hidden * 2 // 3,
+            bytes_accessed=weight * (4 * width * hidden + 20 * number * size * width),
+            transcendentals=weight * number * size * hidden,
         ),
         name="chunk",
     )(*args)
@@ -441,12 +414,17 @@
         return pieces
 
     per_block = math.gcd(2 * rows, 4)
-    place = jnp.stack([y_at, rank // 4])
+    per_chip = 2 * rows // per_block
     pick_far = partner(after(pick_near, theirs))
 
     arrived = exchange(0, [])
     arrived += [pick_far]
-    near = jnp.stack([after(tokens_in, send[0]), upstream])
+    x = after(tokens_in, send[0]).astype(F32)
+    gain = jnp.zeros((rows, width), F32)
+    for member in range(members):
+        gain = jnp.where(pick_own[:, None] == member, norm_gain[member][None, :], gain)
+    normed = x * (1.0 / jnp.sqrt(jnp.mean(x * x, axis=2, keepdims=True) + 1e-06))
+    near = jnp.stack([(normed * gain[:, None, :]).astype(BF16), upstream])
     over = over_x(near)
 
     arrived = exchange(1, arrived)
@@ -454,44 +432,44 @@
 
     set_1, arrived = arrived, exchange(2, arrived)
     far = partner(after(jnp.stack([near, over]), *set_1))
-    chips = []
-    for i, mine in enumerate((near, over)):
-        perm, member_sorted = sort_rows(
-            jnp.concatenate([pick_near[i * rows : (i + 1) * rows], pick_far[i * rows : (i + 1) * rows]])
-        )
-        lifted, g_sorted = prep(perm, member_sorted, mine, far[i], norm_gain)
-        chips.append(((member_sorted, place, perm), lifted, g_sorted))
-        arrived.append(lifted)
-    chip, over_chip = chips
+    arrived += [far]
+    perm, member_sorted = sort_rows(jnp.concatenate([pick_near[rows:], pick_far[rows:]]))
+    perm_own, member_sorted_own = sort_rows(jnp.concatenate([pick_own, pick_far[:rows]]))
+    scalars = (
+        jnp.concatenate([member_sorted, member_sorted_own]),
+        jnp.stack([y_at, rank // 4]),
+        jnp.concatenate([perm + 2 * rows, perm_own]),
+    )
+    tokens_of = (near, over, far)
 
     set_2, arrived = arrived, exchange(3, arrived)
-    first = chunk_pieces(0, 1)
-    sums = chunk((True, False), per_block, *chip, first, None)
-    over_sums = chunk((True, False), per_block, *over_chip, first, None)
-    arrived += [sums[0], over_sums[0]]
+    whole = (0, 2 * per_chip, per_block)
+    sums = chunk(
+        (True, False), whole, scalars, (after(near, *set_2), over, far), chunk_pieces(0, 1), None
+    )
+    arrived += [sums[0]]
 
     set_3, arrived = arrived, exchange(4, arrived)
-    second = chunk_pieces(2)
     sums = chunk(
-        (False, False), per_block, *chip, second, (after(sums[0], *set_3), sums[1])
-    )
-    over_sums = chunk(
-        (False, False), per_block, *over_chip, second, (after(over_sums[0], *set_3), over_sums[1])
-    )
-    arrived += [sums[0], over_sums[0]]
+        (False, False), whole, scalars, tokens_of, chunk_pieces(2),
+        (after(sums[0], *set_3), sums[1]),
+    )
+    arrived += [sums[0]]
 
     set_4 = arrived
     exchange(5, arrived)
-    over_sums = (after(over_sums[0], *set_4), over_sums[1])
+    sums = (after(sums[0], *set_4), sums[1])
     *same, other_out, other_back = chunk(
-        (False, True), per_block, *over_chip, chunk_pieces(3), over_sums, (BF16, BF16), 0
+        (False, True), (0, per_chip, per_block), scalars, tokens_of, chunk_pieces(3), sums,
+        (BF16, BF16), 0,
     )
     others = partner(jnp.stack([other_out, other_back]))
     across = (jnp.stack(same).astype(F32) + others.astype(F32)).astype(BF16)
     sums = (after(sums[0], across), sums[1])
     across = over_x(across)
     out, back, packed_out, packed_back = chunk(
-        (False, True), per_block, *chip, chunk_pieces(3, 4), sums, (F32, BF16), 0
+        (False, True), (per_chip, per_chip, per_block), scalars, tokens_of, chunk_pieces(3, 4),
+        sums, (F32, BF16), 0,
     )
     return tuple(
         finish(

time: 211 us -> 206 us (0.976)
  Pallas kernels: 82.2 us -> 71.2 us
  waiting for transfers between devices: 76.1 us -> 80.5 us
  other arithmetic: 7.85 us -> 11.5 us
    pallas_call x2 -> x0, Pallas kernels: 10.7 us -> none  [prep(): pl.pallas_call(prep_kernel, in_specs=[smem, smem, vmem, vmem, vmem], out_...]
    ppermute x15, waiting for transfers between devices: 32.7 us -> 38.2 us  [shift_z(): lax.ppermute(a, 'row', [(i, (i + 4 * d) % ranks) for i in range(ranks)])]
    unnamed x46 -> x58, local copies, waits for them, and re-layouts: 7.19 us -> 6.74 us
    pallas_call x6 -> x4, Pallas kernels: 65.6 us -> 65.3 us  [chunk(): pl.pallas_call(kernel, grid_spec=pltpu.PrefetchScalarGridSpec(num_scalar_...]
  transfers between devices with their start and end apart: 29 -> 29, of which waited for: 15 -> 17; matrix products, arithmetic and copies ran while one was open for 3% -> 5% of each run, Pallas kernels for 32% -> 26%
where the time goes in v9:
time: 206 us; the launch traced here: 205 us
  waiting for transfers between devices  80.5 us (39%)
  Pallas kernels  71.2 us (35%)
  starting transfers between devices  30 us (15%)
  other arithmetic  11.5 us (6%)
  local copies, waits for them, and re-layouts  10.3 us (5%)
    pallas_call x4, Pallas kernels, chunk(): pl.pallas_call(kernel, grid_spec=pltpu.PrefetchScalarGridSpec(num_scalar_...  65.3 us
    ppermute x15, waiting for transfers between devices, shift_z(): lax.ppermute(a, 'row', [(i, (i + 4 * d) % ranks) for i in range(ranks)])  38.2 us
    ppermute x5, waiting for transfers between devices, over_y(): return lax.ppermute(a, 'row', [(i, i ^ 2) for i in range(ranks)])  21 us
    ppermute x15, starting transfers between devices, shift_z(): lax.ppermute(a, 'row', [(i, (i + 4 * d) % ranks) for i in range(ranks)])  19.8 us
    ppermute x3, waiting for transfers between devices, over_x(): return lax.ppermute(a, 'grp', [(0, 1), (1, 0)])  16.1 us
    unnamed x58, local copies, waits for them, and re-layouts  6.74 us
    ppermute x5, starting transfers between devices, over_y(): return lax.ppermute(a, 'row', [(i, i ^ 2) for i in range(ranks)])  5.95 us
    pallas_call x1, Pallas kernels, finish(): pl.pallas_call(finish_kernel, grid_spec=pltpu.PrefetchScalarGridSpec(num_...  5.92 us
  transfers between devices with their start and end apart: 29, of which 17 were waited for; matrix products, arithmetic and copies ran while one was open for 5% of the time, Pallas kernels for 26%

profile of v9, /device:TPU:8, one launch (start us, length us, event | category | flops | bytes accessed | tf_op | source)
XLA Modules:
  0.0 204.8 jit_solution(1239756830858437159)
XLA Ops:
  4.8 2.0 collective-permute-done
  16.6 5.5 %collective-permute-done.4 = bf16[256,256]{1,0:T(8,128)(2,1)S(1)} collective-permute-done((bf16[256,256]{1,0:T(8,128)(2,1)S(1)}, bf16[256,256]{1,0:T(8,128)(2,1)S(1)}, u32[]{:S(2)}, u32[]{:S(2)}) %collective-permute-start.4) | collective-permute-done | bytes 131104 | tf_op jit(solution)/shard_map/ppermute | solution.py:355
  23.5 1.8 collective-permute-done.6
  29.5 2.0 collective-permute-start.9
  31.5 14.2 %collective-permute-done.3.refs_4_ = bf16[2,6,64,1024]{3,2,1,0:T(8,128)(2,1)S(1)} collective-permute-done((bf16[2,6,64,1024]{3,2,1,0:T(8,128)(2,1)S(1)}, bf16[2,6,64,1024]{3,2,1,0:T(8,128)(2,1)S(1)}, u32[]{:S(2)}, u32[]{:S(2)}) %collective-permute-start.3) | collective-permute-done | bytes 1572896 | tf_op jit(solution)/shard_map/ppermute | solution.py:352
  45.7 2.1 %pad_maximum_fusion = bf16[2,2,6,64,1024]{4,3,2,1,0:T(8,128)(2,1)} fusion(bf16[1,2,6,64,1024]{4,3,2,1,0:T(8,128)(2,1)S(1)} %bitcast.55, bf16[1,2,6,64,1024]{4,3,2,1,0:T(8,128)(2,1)S(1)} %get-tuple-element.69), kind=kLoop, calls=%fused_computation | loop fusion | flops 1572864 | bytes 6291456 | tf_op jit(solution)/shard_map/stack | solution.py:434
  47.8 2.7 %collective-permute-done.8 = bf16[256,512]{1,0:T(8,128)(2,1)S(1)} collective-permute-done((bf16[256,512]{1,0:T(8,128)(2,1)S(1)}, bf16[256,512]{1,0:T(8,128)(2,1)S(1)}, u32[]{:S(2)}, u32[]{:S(2)}) %collective-permute-start.8) | collective-permute-done | bytes 262176 | tf_op jit(solution)/shard_map/ppermute | solution.py:355
  57.5 2.3 %collective-permute-start.13 = (bf16[256,512]{1,0:T(8,128)(2,1)S(1)}, bf16[256,512]{1,0:T(8,128)(2,1)S(1)}, u32[]{:S(2)}, u32[]{:S(2)}) collective-permute-start(bf16[256,512]{1,0:T(8,128)(2,1)S(1)} %get-tuple-element.38), channel_id=1, source_target_pairs={{0,8},{1,9},{2,10},{3,11},{4,12},{5,13},{6,14},{7,15},{8,0},{9,1},... | collective-permute-start | bytes 786440 | tf_op jit(solution)/shard_map/ppermute | solution.py:355
  59.8 1.9 collective-permute-start.14
  61.8 4.8 %collective-permute-done.12 = bf16[256,512]{1,0:T(8,128)(2,1)S(1)} collective-permute-done((bf16[256,512]{1,0:T(8,128)(2,1)S(1)}, bf16[256,512]{1,0:T(8,128)(2,1)S(1)}, u32[]{:S(2)}, u32[]{:S(2)}) %collective-permute-start.12) | collective-permute-done | bytes 262176 | tf_op jit(solution)/shard_map/ppermute | solution.py:355
  66.6 13.9 %collective-permute-done.13 = bf16[256,512]{1,0:T(8,128)(2,1)S(1)} collective-permute-done((bf16[256,512]{1,0:T(8,128)(2,1)S(1)}, bf16[256,512]{1,0:T(8,128)(2,1)S(1)}, u32[]{:S(2)}, u32[]{:S(2)}) %collective-permute-start.13) | collective-permute-done | bytes 262176 | tf_op jit(solution)/shard_map/ppermute | solution.py:355
  80.5 2.7 %collective-permute-done.14 = bf16[256,512]{1,0:T(8,128)(2,1)S(1)} collective-permute-done((bf16[256,512]{1,0:T(8,128)(2,1)S(1)}, bf16[256,512]{1,0:T(8,128)(2,1)S(1)}, u32[]{:S(2)}, u32[]{:S(2)}) %collective-permute-start.14) | collective-permute-done | bytes 262176 | tf_op jit(solution)/shard_map/ppermute | solution.py:355
  87.1 2.0 collective-permute-start.18
  89.1 18.1 %chunk.4 = (f32[1536,1024]{1,0:T(8,128)}, f32[1536,1024]{1,0:T(8,128)}) custom-call(s32[24]{0:T(128)} %pad_add_fusion.3.refs_0_, s32[2]{0:T(128)} %pad_add_fusion.4.refs_1_, s32[24]{0:T(128)} %pad_add_fusion.5.refs_2_, bf16[2,6,64,1024]{3,2,1,0:T(8,128)(2,1)} %copy-done.1, bf16[2,6,64,1024]{3,2,1,0:T(8,128)(2,1)} %copy-done.2, ...), custom_call_target="tpu_custom_call" | custom-call | flops 6442450944 | bytes 34603008 | tf_op jit(solution)/shard_map/chunk/pallas_call | solution.py:255
  107.2 1.9 collective-permute-done.17
  111.2 2.6 %collective-permute-start.22 = (bf16[256,512]{1,0:T(8,128)(2,1)S(1)}, bf16[256,512]{1,0:T(8,128)(2,1)S(1)}, u32[]{:S(2)}, u32[]{:S(2)}) collective-permute-start(bf16[256,512]{1,0:T(8,128)(2,1)S(1)} %get-tuple-element.45), channel_id=1, source_target_pairs={{0,8},{1,9},{2,10},{3,11},{4,12},{5,13},{6,14},{7,15},{8,0},{9,1},... | collective-permute-start | bytes 786440 | tf_op jit(solution)/shard_map/ppermute | solution.py:355
  113.8 1.9 collective-permute-start.23
  115.8 19.0 %chunk.5 = (f32[1536,1024]{1,0:T(8,128)}, f32[1536,1024]{1,0:T(8,128)}) custom-call(s32[24]{0:T(128)} %pad_add_fusion.3.refs_0_, s32[2]{0:T(128)} %pad_add_fusion.4.refs_1_, s32[24]{0:T(128)} %pad_add_fusion.5.refs_2_, bf16[2,6,64,1024]{3,2,1,0:T(8,128)(2,1)} %copy-done.1, ...), custom_call_target="tpu_custom_call", output_to_operand_aliasing={{0}: (10, {}), {1}: (11, {})} | custom-call | flops 4294967296 | bytes 33554432 | tf_op jit(solution)/shard_map/chunk/pallas_call | solution.py:255
  137.0 11.8 %chunk.6 = (bf16[6,64,1024]{2,1,0:T(8,128)(2,1)}, bf16[6,64,1024]{2,1,0:T(8,128)(2,1)}, bf16[6,64,1024]{2,1,0:T(8,128)(2,1)}, bf16[6,64,1024]{2,1,0:T(8,128)(2,1)}) custom-call(s32[24]{0:T(128)} %pad_add_fusion.3.refs_0_, s32[2]{0:T(128)} %pad_add_fusion.4.refs_1_, s32[24]{0:T(128)} %pad_add_fusion.5.refs_2_, bf16[2,6,64,1024]{3,2,1,0:T(8,128)(2,1)} %copy-done.1, ...), custom_call_target="tpu_custom_call" | custom-call | tf_op jit(solution)/shard_map/chunk/pallas_call | solution.py:255
  151.9 2.0 collective-permute-done.25
  155.2 21.0 %collective-permute-done.24.refs_9_.refs_11_ = bf16[4,256,512]{2,1,0:T(8,128)(2,1)S(1)} collective-permute-done((bf16[4,256,512]{2,1,0:T(8,128)(2,1)S(1)}, bf16[4,256,512]{2,1,0:T(8,128)(2,1)S(1)}, u32[]{:S(2)}, u32[]{:S(2)}) %collective-permute-start.24) | collective-permute-done | bytes 1048608 | tf_op jit(solution)/shard_map/ppermute | solution.py:349
  177.2 16.4 %chunk.7 = (f32[6,64,1024]{2,1,0:T(8,128)}, f32[6,64,1024]{2,1,0:T(8,128)}, bf16[6,64,1024]{2,1,0:T(8,128)(2,1)}, bf16[6,64,1024]{2,1,0:T(8,128)(2,1)}) custom-call(s32[24]{0:T(128)} %pad_add_fusion.3.refs_0_, s32[2]{0:T(128)} %pad_add_fusion.4.refs_1_, s32[24]{0:T(128)} %pad_add_fusion.5.refs_2_, bf16[2,6,64,1024]{3,2,1,0:T(8,128)(2,1)} %copy-done.1, ...), custom_call_target="tpu_custom_call" | custom-call | tf_op jit(solution)/shard_map/chunk/pallas_call | solution.py:255
  194.2 2.0 collective-permute-done.26.other_out_ref
  198.7 5.9 %finish.1 = (bf16[6,64,1024]{2,1,0:T(8,128)(2,1)}, bf16[6,64,1024]{2,1,0:T(8,128)(2,1)}, f32[6,64]{1,0:T(8,128)}) custom-call(s32[6]{0:T(128)} %bitcast.86, bf16[6,64,1024]{2,1,0:T(8,128)(2,1)} %x_ref.1, bf16[6,64,1024]{2,1,0:T(8,128)(2,1)} %g_ref.1, f32[2,1024]{1,0:T(2,128)} %gain_ref.1, f32[6,64,1024]{2,1,0:T(8,128)} %get-tuple-element.57.out_ref, ...), custom_call_target="tpu_custom_call" | custom-call | tf_op jit(solution)/shard_map/finish/pallas_call | solution.py:305
  (135 shorter events, 42.8 us)
Async XLA Ops:
  10.5 35.2 %collective-permute-start.3 = (bf16[2,6,64,1024]{3,2,1,0:T(8,128)(2,1)S(1)}, bf16[2,6,64,1024]{3,2,1,0:T(8,128)(2,1)S(1)}, u32[]{:S(2)}, u32[]{:S(2)}) collective-permute-start(bf16[2,6,64,1024]{3,2,1,0:T(8,128)(2,1)S(1)} %get-tuple-element.42.refs_3_), channel_id=1, source_target_pairs={{0,16},{16,0},{1,17},{17,1},{2,18},{18,2},{3,19},{19,3},{4,20},{20... | collective-permute-start | bytes 4718600 | tf_op jit(solution)/shard_map/ppermute | solution.py:352
  12.0 10.1 %collective-permute-start.4 = (bf16[256,256]{1,0:T(8,128)(2,1)S(1)}, bf16[256,256]{1,0:T(8,128)(2,1)S(1)}, u32[]{:S(2)}, u32[]{:S(2)}) collective-permute-start(bf16[256,256]{1,0:T(8,128)(2,1)S(1)} %get-tuple-element.72), channel_id=1, source_target_pairs={{0,4},{1,5},{2,6},{3,7},{4,8},{5,9},{6,10},{7,11},{8,12},{9,13},{1... | collective-permute-start | bytes 393224 | tf_op jit(solution)/shard_map/ppermute | solution.py:355
  13.6 9.9 %collective-permute-start.5 = (bf16[256,256]{1,0:T(8,128)(2,1)S(1)}, bf16[256,256]{1,0:T(8,128)(2,1)S(1)}, u32[]{:S(2)}, u32[]{:S(2)}) collective-permute-start(bf16[256,256]{1,0:T(8,128)(2,1)S(1)} %get-tuple-element.72), channel_id=1, source_target_pairs={{0,8},{1,9},{2,10},{3,11},{4,12},{5,13},{6,14},{7,15},{8,0},{9,1},... | collective-permute-start | bytes 393224 | tf_op jit(solution)/shard_map/ppermute | solution.py:355
  14.8 10.5 %collective-permute-start.6 = (bf16[256,256]{1,0:T(8,128)(2,1)S(1)}, bf16[256,256]{1,0:T(8,128)(2,1)S(1)}, u32[]{:S(2)}, u32[]{:S(2)}) collective-permute-start(bf16[256,256]{1,0:T(8,128)(2,1)S(1)} %get-tuple-element.72), channel_id=1, source_target_pairs={{0,12},{1,13},{2,14},{3,15},{4,0},{5,1},{6,2},{7,3},{8,4},{9,5},{1... | collective-permute-start | bytes 393224 | tf_op jit(solution)/shard_map/ppermute | solution.py:355
  16.6 8.8 %collective-permute-start.2 = (s32[12]{0:T(128)S(1)}, s32[12]{0:T(128)S(1)}, u32[]{:S(2)}, u32[]{:S(2)}) collective-permute-start(s32[12]{0:T(128)S(1)} %pad_add_fusion), channel_id=1, source_target_pairs={{0,1},{1,0},{2,3},{3,2},{4,5},{5,4},{6,7},{7,6},{8,9},{9,8},{10,11... | collective-permute-start | bytes 152 | tf_op jit(solution)/shard_map/ppermute | solution.py:346
  25.5 26.3 %collective-permute-start.10 = (bf16[4,256,256]{2,1,0:T(8,128)(2,1)S(1)}, bf16[4,256,256]{2,1,0:T(8,128)(2,1)}, u32[]{:S(2)}, u32[]{:S(2)}) collective-permute-start(bf16[4,256,256]{2,1,0:T(8,128)(2,1)S(1)} %pad_maximum_fusion.10.refs_6_), channel_id=1, source_target_pairs={{0,2},{1,3},{2,0},{3,1},{4,6},{5,7},{6,4},{7,5},{8,10},{9,11},{10,... | collective-permute-start | bytes 1572872 | tf_op jit(solution)/shard_map/ppermute | solution.py:349
  28.0 19.9 %collective-permute-start.7 = (bf16[256,512]{1,0:T(8,128)(2,1)S(1)}, bf16[256,512]{1,0:T(8,128)(2,1)S(1)}, u32[]{:S(2)}, u32[]{:S(2)}) collective-permute-start(bf16[256,512]{1,0:T(8,128)(2,1)S(1)} %get-tuple-element.35), channel_id=1, source_target_pairs={{0,4},{1,5},{2,6},{3,7},{4,8},{5,9},{6,10},{7,11},{8,12},{9,13},{1... | collective-permute-start | bytes 786440 | tf_op jit(solution)/shard_map/ppermute | solution.py:355
  28.0 22.6 %collective-permute-start.8 = (bf16[256,512]{1,0:T(8,128)(2,1)S(1)}, bf16[256,512]{1,0:T(8,128)(2,1)S(1)}, u32[]{:S(2)}, u32[]{:S(2)}) collective-permute-start(bf16[256,512]{1,0:T(8,128)(2,1)S(1)} %get-tuple-element.35), channel_id=1, source_target_pairs={{0,8},{1,9},{2,10},{3,11},{4,12},{5,13},{6,14},{7,15},{8,0},{9,1},... | collective-permute-start | bytes 786440 | tf_op jit(solution)/shard_map/ppermute | solution.py:355
  29.5 22.3 %collective-permute-start.9 = (bf16[256,512]{1,0:T(8,128)(2,1)S(1)}, bf16[256,512]{1,0:T(8,128)(2,1)S(1)}, u32[]{:S(2)}, u32[]{:S(2)}) collective-permute-start(bf16[256,512]{1,0:T(8,128)(2,1)S(1)} %get-tuple-element.35), channel_id=1, source_target_pairs={{0,12},{1,13},{2,14},{3,15},{4,0},{5,1},{6,2},{7,3},{8,4},{9,5},{1... | collective-permute-start | bytes 786440 | tf_op jit(solution)/shard_map/ppermute | solution.py:355
  52.5 31.0 %collective-permute-start.11 = (bf16[2,2,6,64,1024]{4,3,2,1,0:T(8,128)(2,1)}, bf16[2,2,6,64,1024]{4,3,2,1,0:T(8,128)(2,1)S(1)}, u32[]{:S(2)}, u32[]{:S(2)}) collective-permute-start(bf16[2,2,6,64,1024]{4,3,2,1,0:T(8,128)(2,1)} %pad_maximum_fusion), channel_id=1, source_target_pairs={{0,1},{1,0},{2,3},{3,2},{4,5},{5,4},{6,7},{7,6},{8,9},{9,8},{10,11... | collective-permute-start | bytes 9437192 | tf_op jit(solution)/shard_map/ppermute | solution.py:346
  56.2 27.2 %collective-permute-start.15 = (bf16[4,256,512]{2,1,0:T(8,128)(2,1)S(1)}, bf16[4,256,512]{2,1,0:T(8,128)(2,1)S(1)}, u32[]{:S(2)}, u32[]{:S(2)}) collective-permute-start(bf16[4,256,512]{2,1,0:T(8,128)(2,1)S(1)} %pad_maximum_fusion.4.refs_8_), channel_id=1, source_target_pairs={{0,2},{1,3},{2,0},{3,1},{4,6},{5,7},{6,4},{7,5},{8,10},{9,11},{10,... | collective-permute-start | bytes 3145736 | tf_op jit(solution)/shard_map/ppermute | solution.py:349
  57.4 9.2 %collective-permute-start.12 = (bf16[256,512]{1,0:T(8,128)(2,1)S(1)}, bf16[256,512]{1,0:T(8,128)(2,1)S(1)}, u32[]{:S(2)}, u32[]{:S(2)}) collective-permute-start(bf16[256,512]{1,0:T(8,128)(2,1)S(1)} %get-tuple-element.38), channel_id=1, source_target_pairs={{0,4},{1,5},{2,6},{3,7},{4,8},{5,9},{6,10},{7,11},{8,12},{9,13},{1... | collective-permute-start | bytes 786440 | tf_op jit(solution)/shard_map/ppermute | solution.py:355
  57.5 23.1 %collective-permute-start.13 = (bf16[256,512]{1,0:T(8,128)(2,1)S(1)}, bf16[256,512]{1,0:T(8,128)(2,1)S(1)}, u32[]{:S(2)}, u32[]{:S(2)}) collective-permute-start(bf16[256,512]{1,0:T(8,128)(2,1)S(1)} %get-tuple-element.38), channel_id=1, source_target_pairs={{0,8},{1,9},{2,10},{3,11},{4,12},{5,13},{6,14},{7,15},{8,0},{9,1},... | collective-permute-start | bytes 786440 | tf_op jit(solution)/shard_map/ppermute | solution.py:355
  59.8 23.5 %collective-permute-start.14 = (bf16[256,512]{1,0:T(8,128)(2,1)S(1)}, bf16[256,512]{1,0:T(8,128)(2,1)S(1)}, u32[]{:S(2)}, u32[]{:S(2)}) collective-permute-start(bf16[256,512]{1,0:T(8,128)(2,1)S(1)} %get-tuple-element.38), channel_id=1, source_target_pairs={{0,12},{1,13},{2,14},{3,15},{4,0},{5,1},{6,2},{7,3},{8,4},{9,5},{1... | collective-permute-start | bytes 786440 | tf_op jit(solution)/shard_map/ppermute | solution.py:355
  83.5 26.7 %collective-permute-start.19 = (bf16[4,256,512]{2,1,0:T(8,128)(2,1)S(1)}, bf16[4,256,512]{2,1,0:T(8,128)(2,1)S(1)}, u32[]{:S(2)}, u32[]{:S(2)}) collective-permute-start(bf16[4,256,512]{2,1,0:T(8,128)(2,1)S(1)} %pad_maximum_fusion.6.refs_6_.refs_8_), channel_id=1, source_target_pairs={{0,2},{1,3},{2,0},{3,1},{4,6},{5,7},{6,4},{7,5},{8,10},{9,11},{10,... | collective-permute-start | bytes 3145736 | tf_op jit(solution)/shard_map/ppermute | solution.py:349
  86.4 20.8 %collective-permute-start.16 = (bf16[256,512]{1,0:T(8,128)(2,1)S(1)}, bf16[256,512]{1,0:T(8,128)(2,1)S(1)}, u32[]{:S(2)}, u32[]{:S(2)}) collective-permute-start(bf16[256,512]{1,0:T(8,128)(2,1)S(1)} %copy-done.22), channel_id=1, source_target_pairs={{0,4},{1,5},{2,6},{3,7},{4,8},{5,9},{6,10},{7,11},{8,12},{9,13},{1... | collective-permute-start | bytes 786440 | tf_op jit(solution)/shard_map/ppermute | solution.py:355
  86.4 22.7 %collective-permute-start.17 = (bf16[256,512]{1,0:T(8,128)(2,1)S(1)}, bf16[256,512]{1,0:T(8,128)(2,1)S(1)}, u32[]{:S(2)}, u32[]{:S(2)}) collective-permute-start(bf16[256,512]{1,0:T(8,128)(2,1)S(1)} %copy-done.22), channel_id=1, source_target_pairs={{0,8},{1,9},{2,10},{3,11},{4,12},{5,13},{6,14},{7,15},{8,0},{9,1},... | collective-permute-start | bytes 786440 | tf_op jit(solution)/shard_map/ppermute | solution.py:355
  87.1 22.9 %collective-permute-start.18 = (bf16[256,512]{1,0:T(8,128)(2,1)S(1)}, bf16[256,512]{1,0:T(8,128)(2,1)S(1)}, u32[]{:S(2)}, u32[]{:S(2)}) collective-permute-start(bf16[256,512]{1,0:T(8,128)(2,1)S(1)} %copy-done.22), channel_id=1, source_target_pairs={{0,12},{1,13},{2,14},{3,15},{4,0},{5,1},{6,2},{7,3},{8,4},{9,5},{1... | collective-permute-start | bytes 786440 | tf_op jit(solution)/shard_map/ppermute | solution.py:355
  110.1 25.9 %collective-permute-start.20 = (bf16[4,256,512]{2,1,0:T(8,128)(2,1)S(1)}, bf16[4,256,512]{2,1,0:T(8,128)(2,1)S(1)}, u32[]{:S(2)}, u32[]{:S(2)}) collective-permute-start(bf16[4,256,512]{2,1,0:T(8,128)(2,1)S(1)} %pad_maximum_fusion.5.refs_6_), channel_id=1, source_target_pairs={{0,2},{1,3},{2,0},{3,1},{4,6},{5,7},{6,4},{7,5},{8,10},{9,11},{10,... | collective-permute-start | bytes 3145736 | tf_op jit(solution)/shard_map/ppermute | solution.py:349
  111.1 23.6 %collective-permute-start.21 = (bf16[256,512]{1,0:T(8,128)(2,1)S(1)}, bf16[256,512]{1,0:T(8,128)(2,1)S(1)}, u32[]{:S(2)}, u32[]{:S(2)}) collective-permute-start(bf16[256,512]{1,0:T(8,128)(2,1)S(1)} %get-tuple-element.45), channel_id=1, source_target_pairs={{0,4},{1,5},{2,6},{3,7},{4,8},{5,9},{6,10},{7,11},{8,12},{9,13},{1... | collective-permute-start | bytes 786440 | tf_op jit(solution)/shard_map/ppermute | solution.py:355
  111.2 23.6 %collective-permute-start.22 = (bf16[256,512]{1,0:T(8,128)(2,1)S(1)}, bf16[256,512]{1,0:T(8,128)(2,1)S(1)}, u32[]{:S(2)}, u32[]{:S(2)}) collective-permute-start(bf16[256,512]{1,0:T(8,128)(2,1)S(1)} %get-tuple-element.45), channel_id=1, source_target_pairs={{0,8},{1,9},{2,10},{3,11},{4,12},{5,13},{6,14},{7,15},{8,0},{9,1},... | collective-permute-start | bytes 786440 | tf_op jit(solution)/shard_map/ppermute | solution.py:355
  113.8 22.2 %collective-permute-start.23 = (bf16[256,512]{1,0:T(8,128)(2,1)S(1)}, bf16[256,512]{1,0:T(8,128)(2,1)S(1)}, u32[]{:S(2)}, u32[]{:S(2)}) collective-permute-start(bf16[256,512]{1,0:T(8,128)(2,1)S(1)} %get-tuple-element.45), channel_id=1, source_target_pairs={{0,12},{1,13},{2,14},{3,15},{4,0},{5,1},{6,2},{7,3},{8,4},{9,5},{1... | collective-permute-start | bytes 786440 | tf_op jit(solution)/shard_map/ppermute | solution.py:355
  150.6 25.6 %collective-permute-start.24 = (bf16[4,256,512]{2,1,0:T(8,128)(2,1)S(1)}, bf16[4,256,512]{2,1,0:T(8,128)(2,1)S(1)}, u32[]{:S(2)}, u32[]{:S(2)}) collective-permute-start(bf16[4,256,512]{2,1,0:T(8,128)(2,1)S(1)} %pad_maximum_fusion.7.refs_8_.refs_10_), channel_id=1, source_target_pairs={{0,2},{1,3},{2,0},{3,1},{4,6},{5,7},{6,4},{7,5},{8,10},{9,11},{10,... | collective-permute-start | bytes 3145736 | tf_op jit(solution)/shard_map/ppermute | solution.py:349
  154.6 42.7 %collective-permute-start.28 = (bf16[2,6,64,1024]{3,2,1,0:T(8,128)(2,1)S(1)}, bf16[2,6,64,1024]{3,2,1,0:T(8,128)(2,1)S(1)}, u32[]{:S(2)}, u32[]{:S(2)}) collective-permute-start(bf16[2,6,64,1024]{3,2,1,0:T(8,128)(2,1)S(1)} %add_convert_fusion), channel_id=1, source_target_pairs={{0,16},{16,0},{1,17},{17,1},{2,18},{18,2},{3,19},{19,3},{4,20},{20... | collective-permute-start | bytes 4718600 | tf_op jit(solution)/shard_map/ppermute | solution.py:352
  (34 other events, 224.1 us)

commit v10 on v9

--- a/solution.py
+++ b/solution.py
@@ -97,11 +97,12 @@
     parts = len(units)
     pieces, refs = refs[: 2 * parts], refs[2 * parts :]
     if first:
-        *outs, weights_ref, sems, lifted_ref, g_ref = refs
+        *outs, weights_ref, sems, lifted_ref, g_ref, act_ref, pre_ref = refs
     elif last:
-        out_in, back_in, *outs, weights_ref, sems, lifted_ref, g_ref, out_acc, back_acc = refs
+        out_in, back_in, *outs, weights_ref, sems, lifted_ref, g_ref, act_ref, pre_ref = refs[:-2]
+        out_acc, back_acc = refs[-2:]
     else:
-        out_in, back_in, *outs, weights_ref, sems, lifted_ref, g_ref = refs
+        out_in, back_in, *outs, weights_ref, sems, lifted_ref, g_ref, act_ref, pre_ref = refs
     if not last:
         out_acc, back_acc = outs
     j = pl.program_id(0)
@@ -133,59 +134,74 @@
         for copy in copies:
             copy.wait()
 
-    for i, at in enumerate(places):
-        row = perm_ref[at]
-        source = row // rows
-        for k, ref in enumerate((near_ref, far_ref.at[0], over_ref, far_ref.at[1])):
-
-            @pl.when(source == k)
-            def _():
-                tokens = pl.ds(i * seq, seq)
-                lifted_ref[tokens, :] = ref[0, row - k * rows]
-                g_ref[tokens, :] = ref[1, row - k * rows]
-
     width = lifted_ref.shape[1]
     here = [sorted_ref[at] for at in places]
-    if first:
-        out_acc[...] = jnp.zeros(out_acc.shape, F32)
-        back_acc[...] = jnp.zeros(back_acc.shape, F32)
-    else:
-        out_acc[...] = out_in[...]
-        back_acc[...] = back_in[...]
-
-    for member in sorted(set(m for m, _ in units)):
+
+    def pick_up(member):
+        for i, at in enumerate(places):
+            row = perm_ref[at]
+            source = jnp.where(here[i] == member, row // rows, 4)
+            tokens = pl.ds(i * seq, seq)
+            for k, ref in enumerate((near_ref, far_ref.at[0], over_ref, far_ref.at[1])):
+
+                @pl.when(source == k)
+                def _():
+                    lifted_ref[tokens, :] = ref[0, row - k * rows]
+                    g_ref[tokens, :] = ref[1, row - k * rows]
+
+            @pl.when(source == 4)
+            def _():
+                lifted_ref[tokens, :] = jnp.zeros((seq, width), BF16)
+                g_ref[tokens, :] = jnp.zeros((seq, width), BF16)
+
+    def sums(member):
+        pick_up(member)
+        mine = [(start, n) for (m, n), start in zip(units, starts) if m == member]
+        low, high = mine[0][0], mine[-1][0] + mine[-1][1]
+        for s in range(low, high, 256):
+            e = min(s + 256, high)
+            up = weights_ref[:, :, :depth, s:e].reshape(width, e - s)
+            down = weights_ref[:, :, depth:, s:e].reshape(width, e - s)
+            v = jnp.dot(lifted_ref[...], up, preferred_element_type=F32)
+            grads = jnp.dot(g_ref[...], down, preferred_element_type=F32)
+            square = v * v
+            t = jnp.tanh(v * (coef_c + (coef_c * 0.044715) * square))
+            half_v = 0.5 * v
+            act_ref[:, s - low : e - low] = (half_v + half_v * t).astype(BF16)
+            slope = (0.5 + 0.5 * t) + (half_v * (1.0 - t * t)) * (
+                coef_c + (3.0 * coef_c * 0.044715) * square
+            )
+            pre_ref[:, s - low : e - low] = (grads * slope).astype(BF16)
+        up = weights_ref[:, :, :depth, low:high].reshape(width, high - low)
+        down = weights_ref[:, :, depth:, low:high].reshape(width, high - low)
+        dims = (((1,), (1,)), ((), ()))
+        return (
+            lax.dot_general(act_ref[:, : high - low], down, dims, preferred_element_type=F32),
+            lax.dot_general(pre_ref[:, : high - low], up, dims, preferred_element_type=F32),
+        )
+
+    for at, member in enumerate(sorted(set(m for m, _ in units))):
         used = functools.reduce(jnp.logical_or, [m == member for m in here])
 
         @pl.when(used)
         def _():
-            lifted = lifted_ref[...]
-            g = g_ref[...]
-            weight = jnp.concatenate(
-                [jnp.full((seq, 1), (m == member).astype(F32), F32) for m in here], axis=0
-            )
-            out_sum = jnp.zeros(lifted.shape, F32)
-            back_sum = jnp.zeros(lifted.shape, F32)
-            spans = []
-            for (m, n), start in zip(units, starts):
-                if m == member:
-                    spans += [(s, min(s + 512, start + n)) for s in range(start, start + n, 512)]
-            for s, e in spans:
-                up = weights_ref[:, :, :depth, s:e].reshape(width, e - s)
-                down = weights_ref[:, :, depth:, s:e].reshape(width, e - s)
-                v = jnp.dot(lifted, up, preferred_element_type=F32)
-                grads = jnp.dot(g, down, preferred_element_type=F32)
-                square = v * v
-                t = jnp.tanh(coef_c * (v + 0.044715 * square * v))
-                act = (0.5 * v * (1.0 + t)).astype(BF16)
-                slope = 0.5 * (1.0 + t) + 0.5 * v * (1.0 - t * t) * coef_c * (
-                    1.0 + 3.0 * 0.044715 * square
-                )
-                pre = (grads * slope).astype(BF16)
-                dims = (((1,), (1,)), ((), ()))
-                out_sum += lax.dot_general(act, down, dims, preferred_element_type=F32)
-                back_sum += lax.dot_general(pre, up, dims, preferred_element_type=F32)
-            out_acc[...] += weight * out_sum
-            back_acc[...] += weight * back_sum
+            out_sum, back_sum = sums(member)
+            if at > 0:
+                out_acc[...] += out_sum
+                back_acc[...] += back_sum
+            elif first:
+                out_acc[...] = out_sum
+                back_acc[...] = back_sum
+            else:
+                out_acc[...] = out_in[...] + out_sum
+                back_acc[...] = back_in[...] + back_sum
+
+        if at == 0:
+
+            @pl.when(jnp.logical_not(used))
+            def _():
+                out_acc[...] = jnp.zeros(out_acc.shape, F32) if first else out_in[...]
+                back_acc[...] = jnp.zeros(back_acc.shape, F32) if first else back_in[...]
 
     if last:
         for p, at in enumerate(places):
@@ -233,6 +249,8 @@
         pltpu.SemaphoreType.DMA((len(pieces) * 2 * lines,)),
         pltpu.VMEM((size, width), BF16),
         pltpu.VMEM((size, width), BF16),
+        pltpu.VMEM((size, hidden), BF16),
+        pltpu.VMEM((size, hidden), BF16),
     ]
     if not first:
         alias = {len(args): 0, len(args) + 1: 1}
@@ -418,21 +436,15 @@
     pick_far = partner(after(pick_near, theirs))
 
     arrived = exchange(0, [])
-    arrived += [pick_far]
-    x = after(tokens_in, send[0]).astype(F32)
+    x = after(tokens_in, arrived[0]).astype(F32)
     gain = jnp.zeros((rows, width), F32)
     for member in range(members):
         gain = jnp.where(pick_own[:, None] == member, norm_gain[member][None, :], gain)
     normed = x * (1.0 / jnp.sqrt(jnp.mean(x * x, axis=2, keepdims=True) + 1e-06))
     near = jnp.stack([(normed * gain[:, None, :]).astype(BF16), upstream])
     over = over_x(near)
-
-    arrived = exchange(1, arrived)
-    arrived += [over]
-
-    set_1, arrived = arrived, exchange(2, arrived)
-    far = partner(after(jnp.stack([near, over]), *set_1))
-    arrived += [far]
+    arrived += [pick_far, *send[1:]]
+
     perm, member_sorted = sort_rows(jnp.concatenate([pick_near[rows:], pick_far[rows:]]))
     perm_own, member_sorted_own = sort_rows(jnp.concatenate([pick_own, pick_far[:rows]]))
     scalars = (
@@ -440,6 +452,13 @@
         jnp.stack([y_at, rank // 4]),
         jnp.concatenate([perm + 2 * rows, perm_own]),
     )
+
+    arrived = exchange(1, arrived)
+    arrived += [*scalars]
+
+    set_1, arrived = arrived, exchange(2, arrived)
+    far = partner(jnp.stack([near, after(over, *set_1)]))
+    arrived += [far]
     tokens_of = (near, over, far)
 
     set_2, arrived = arrived, exchange(3, arrived)
@@ -465,11 +484,12 @@
     )
     others = partner(jnp.stack([other_out, other_back]))
     across = (jnp.stack(same).astype(F32) + others.astype(F32)).astype(BF16)
-    sums = (after(sums[0], across), sums[1])
+    sums = tuple(after(a, across) for a in sums)
     across = over_x(across)
+    own = (per_chip, per_chip, per_block)
+    sums = chunk((False, False), own, scalars, tokens_of, chunk_pieces(3), sums, None, 0)
     out, back, packed_out, packed_back = chunk(
-        (False, True), (per_chip, per_chip, per_block), scalars, tokens_of, chunk_pieces(3, 4),
-        sums, (F32, BF16), 0,
+        (False, True), own, scalars, tokens_of, chunk_pieces(4), sums, (F32, BF16), 0
     )
     return tuple(
         finish(

time: 206 us -> 200 us (0.971)
  Pallas kernels: 71.2 us -> 77.1 us
  waiting for transfers between devices: 80.5 us -> 75.1 us
  local copies, waits for them, and re-layouts: 10.3 us -> 6.43 us
  other arithmetic: 11.5 us -> 9.11 us
  starting transfers between devices: 30 us -> 27.8 us
    ppermute x15, waiting for transfers between devices: 38.2 us -> 53.3 us  [shift_z(): lax.ppermute(a, 'row', [(i, (i + 4 * d) % ranks) for i in range(ranks)])]
    ppermute x5, waiting for transfers between devices: 21 us -> 9.76 us  [over_y(): return lax.ppermute(a, 'row', [(i, i ^ 2) for i in range(ranks)])]
    ppermute x3, waiting for transfers between devices: 16.1 us -> 5.78 us  [over_x(): return lax.ppermute(a, 'grp', [(0, 1), (1, 0)])]
    pallas_call x4 -> x5, Pallas kernels: 65.3 us -> 71.2 us  [chunk(): pl.pallas_call(kernel, grid_spec=pltpu.PrefetchScalarGridSpec(num_scalar_...]
    squeeze x3 -> x2, local copies, waits for them, and re-layouts: 2.48 us -> 0.03 us  [on_device_shared(): shard[m, :, at:at + n]]
    unnamed x58 -> x50, local copies, waits for them, and re-layouts: 6.74 us -> 6.12 us
  transfers between devices with their start and end apart: 29 -> 29, of which waited for: 17 -> 18; matrix products, arithmetic and copies ran while one was open for 5% -> 3% of each run, Pallas kernels for 26% -> 30%
where the time goes in v10:
time: 200 us; the launch traced here: 197 us
  Pallas kernels  77.1 us (39%)
  waiting for transfers between devices  75.1 us (38%)
  starting transfers between devices  27.8 us (14%)
  other arithmetic  9.11 us (5%)
  local copies, waits for them, and re-layouts  6.43 us (3%)
    pallas_call x5, Pallas kernels, chunk(): pl.pallas_call(kernel, grid_spec=pltpu.PrefetchScalarGridSpec(num_scalar_...  71.2 us
    ppermute x15, waiting for transfers between devices, shift_z(): lax.ppermute(a, 'row', [(i, (i + 4 * d) % ranks) for i in range(ranks)])  53.3 us
    ppermute x15, starting transfers between devices, shift_z(): lax.ppermute(a, 'row', [(i, (i + 4 * d) % ranks) for i in range(ranks)])  18.1 us
    ppermute x5, waiting for transfers between devices, over_y(): return lax.ppermute(a, 'row', [(i, i ^ 2) for i in range(ranks)])  9.76 us
    ppermute x6, waiting for transfers between devices, partner(): return lax.ppermute(a, 'row', [(i, i ^ 1) for i in range(ranks)])  6.28 us
    unnamed x50, local copies, waits for them, and re-layouts  6.12 us
    pallas_call x1, Pallas kernels, finish(): pl.pallas_call(finish_kernel, grid_spec=pltpu.PrefetchScalarGridSpec(num_...  5.92 us
    ppermute x3, waiting for transfers between devices, over_x(): return lax.ppermute(a, 'grp', [(0, 1), (1, 0)])  5.78 us
  transfers between devices with their start and end apart: 29, of which 18 were waited for; matrix products, arithmetic and copies ran while one was open for 3% of the time, Pallas kernels for 30%

profile of v10, /device:TPU:8, one launch (start us, length us, event | category | flops | bytes accessed | tf_op | source)
XLA Modules:
  0.0 196.9 jit_solution(5244173228005684705)
XLA Ops:
  10.1 1.9 collective-permute-start.6
  12.9 5.0 %collective-permute-done.3 = bf16[256,256]{1,0:T(8,128)(2,1)S(1)} collective-permute-done((bf16[256,256]{1,0:T(8,128)(2,1)S(1)}, bf16[256,256]{1,0:T(8,128)(2,1)S(1)}, u32[]{:S(2)}, u32[]{:S(2)}) %collective-permute-start.3) | collective-permute-done | bytes 131104 | tf_op jit(solution)/shard_map/ppermute | solution.py:373
  22.8 2.3 %collective-permute-start.7 = (bf16[256,512]{1,0:T(8,128)(2,1)S(1)}, bf16[256,512]{1,0:T(8,128)(2,1)S(1)}, u32[]{:S(2)}, u32[]{:S(2)}) collective-permute-start(bf16[256,512]{1,0:T(8,128)(2,1)S(1)} %get-tuple-element.38), channel_id=1, source_target_pairs={{0,4},{1,5},{2,6},{3,7},{4,8},{5,9},{6,10},{7,11},{8,12},{9,13},{1... | collective-permute-start | bytes 786440 | tf_op jit(solution)/shard_map/ppermute | solution.py:373
  27.8 14.8 %collective-permute-done.7 = bf16[256,512]{1,0:T(8,128)(2,1)S(1)} collective-permute-done((bf16[256,512]{1,0:T(8,128)(2,1)S(1)}, bf16[256,512]{1,0:T(8,128)(2,1)S(1)}, u32[]{:S(2)}, u32[]{:S(2)}) %collective-permute-start.7) | collective-permute-done | bytes 262176 | tf_op jit(solution)/shard_map/ppermute | solution.py:373
  42.6 2.8 %collective-permute-done.8 = bf16[256,512]{1,0:T(8,128)(2,1)S(1)} collective-permute-done((bf16[256,512]{1,0:T(8,128)(2,1)S(1)}, bf16[256,512]{1,0:T(8,128)(2,1)S(1)}, u32[]{:S(2)}, u32[]{:S(2)}) %collective-permute-start.8) | collective-permute-done | bytes 262176 | tf_op jit(solution)/shard_map/ppermute | solution.py:373
  46.6 4.4 %collective-permute-done.4.refs_4_ = bf16[2,6,64,1024]{3,2,1,0:T(8,128)(2,1)S(1)} collective-permute-done((bf16[2,6,64,1024]{3,2,1,0:T(8,128)(2,1)S(1)}, bf16[2,6,64,1024]{3,2,1,0:T(8,128)(2,1)S(1)}, u32[]{:S(2)}, u32[]{:S(2)}) %collective-permute-start.4) | collective-permute-done | bytes 1572896 | tf_op jit(solution)/shard_map/ppermute | solution.py:370
  54.1 3.5 %collective-permute-start.13 = (bf16[256,512]{1,0:T(8,128)(2,1)S(1)}, bf16[256,512]{1,0:T(8,128)(2,1)S(1)}, u32[]{:S(2)}, u32[]{:S(2)}) collective-permute-start(bf16[256,512]{1,0:T(8,128)(2,1)S(1)} %get-tuple-element.41), channel_id=1, source_target_pairs={{0,8},{1,9},{2,10},{3,11},{4,12},{5,13},{6,14},{7,15},{8,0},{9,1},... | collective-permute-start | bytes 786440 | tf_op jit(solution)/shard_map/ppermute | solution.py:373
  57.6 5.4 %collective-permute-done.12 = bf16[256,512]{1,0:T(8,128)(2,1)S(1)} collective-permute-done((bf16[256,512]{1,0:T(8,128)(2,1)S(1)}, bf16[256,512]{1,0:T(8,128)(2,1)S(1)}, u32[]{:S(2)}, u32[]{:S(2)}) %collective-permute-start.12) | collective-permute-done | bytes 262176 | tf_op jit(solution)/shard_map/ppermute | solution.py:373
  63.1 14.0 %collective-permute-done.13 = bf16[256,512]{1,0:T(8,128)(2,1)S(1)} collective-permute-done((bf16[256,512]{1,0:T(8,128)(2,1)S(1)}, bf16[256,512]{1,0:T(8,128)(2,1)S(1)}, u32[]{:S(2)}, u32[]{:S(2)}) %collective-permute-start.13) | collective-permute-done | bytes 262176 | tf_op jit(solution)/shard_map/ppermute | solution.py:373
  77.0 3.4 %collective-permute-done.14 = bf16[256,512]{1,0:T(8,128)(2,1)S(1)} collective-permute-done((bf16[256,512]{1,0:T(8,128)(2,1)S(1)}, bf16[256,512]{1,0:T(8,128)(2,1)S(1)}, u32[]{:S(2)}, u32[]{:S(2)}) %collective-permute-start.14) | collective-permute-done | bytes 262176 | tf_op jit(solution)/shard_map/ppermute | solution.py:373
  82.1 2.1 %collective-permute-start.17 = (bf16[256,512]{1,0:T(8,128)(2,1)S(1)}, bf16[256,512]{1,0:T(8,128)(2,1)S(1)}, u32[]{:S(2)}, u32[]{:S(2)}) collective-permute-start(bf16[256,512]{1,0:T(8,128)(2,1)S(1)} %get-tuple-element.43), channel_id=1, source_target_pairs={{0,8},{1,9},{2,10},{3,11},{4,12},{5,13},{6,14},{7,15},{8,0},{9,1},... | collective-permute-start | bytes 786440 | tf_op jit(solution)/shard_map/ppermute | solution.py:373
  84.2 16.9 %chunk.5 = (f32[1536,1024]{1,0:T(8,128)}, f32[1536,1024]{1,0:T(8,128)}) custom-call(s32[24]{0:T(128)} %pad_add_fusion.3.refs_0_, s32[2]{0:T(128)} %pad_add_fusion.4.refs_1_, s32[24]{0:T(128)} %pad_add_fusion.5.refs_2_, bf16[2,6,64,1024]{3,2,1,0:T(8,128)(2,1)} %copy-done.1, bf16[2,6,64,1024]{3,2,1,0:T(8,128)(2,1)} %copy-done.2, ...), custom_call_target="tpu_custom_call" | custom-call | flops 6442450944 | bytes 34603008 | tf_op jit(solution)/shard_map/chunk/pallas_call | solution.py:273
  101.1 3.1 %collective-permute-done.17 = bf16[256,512]{1,0:T(8,128)(2,1)S(1)} collective-permute-done((bf16[256,512]{1,0:T(8,128)(2,1)S(1)}, bf16[256,512]{1,0:T(8,128)(2,1)S(1)}, u32[]{:S(2)}, u32[]{:S(2)}) %collective-permute-start.17) | collective-permute-done | bytes 262176 | tf_op jit(solution)/shard_map/ppermute | solution.py:373
  104.2 2.5 %collective-permute-done.18 = bf16[256,512]{1,0:T(8,128)(2,1)S(1)} collective-permute-done((bf16[256,512]{1,0:T(8,128)(2,1)S(1)}, bf16[256,512]{1,0:T(8,128)(2,1)S(1)}, u32[]{:S(2)}, u32[]{:S(2)}) %collective-permute-start.18) | collective-permute-done | bytes 262176 | tf_op jit(solution)/shard_map/ppermute | solution.py:373
  107.5 1.9 collective-permute-start.21
  109.4 2.0 %collective-permute-start.22 = (bf16[256,512]{1,0:T(8,128)(2,1)S(1)}, bf16[256,512]{1,0:T(8,128)(2,1)S(1)}, u32[]{:S(2)}, u32[]{:S(2)}) collective-permute-start(bf16[256,512]{1,0:T(8,128)(2,1)S(1)} %copy-done.20), channel_id=1, source_target_pairs={{0,12},{1,13},{2,14},{3,15},{4,0},{5,1},{6,2},{7,3},{8,4},{9,5},{1... | collective-permute-start | bytes 786440 | tf_op jit(solution)/shard_map/ppermute | solution.py:373
  111.4 18.6 %chunk.6 = (f32[1536,1024]{1,0:T(8,128)}, f32[1536,1024]{1,0:T(8,128)}) custom-call(s32[24]{0:T(128)} %pad_add_fusion.3.refs_0_, s32[2]{0:T(128)} %pad_add_fusion.4.refs_1_, s32[24]{0:T(128)} %pad_add_fusion.5.refs_2_, bf16[2,6,64,1024]{3,2,1,0:T(8,128)(2,1)} %copy-done.1, ...), custom_call_target="tpu_custom_call", output_to_operand_aliasing={{0}: (10, {}), {1}: (11, {})} | custom-call | flops 4294967296 | bytes 33554432 | tf_op jit(solution)/shard_map/chunk/pallas_call | solution.py:273
  133.0 11.8 %chunk.7 = (bf16[6,64,1024]{2,1,0:T(8,128)(2,1)}, bf16[6,64,1024]{2,1,0:T(8,128)(2,1)}, bf16[6,64,1024]{2,1,0:T(8,128)(2,1)}, bf16[6,64,1024]{2,1,0:T(8,128)(2,1)}) custom-call(s32[24]{0:T(128)} %pad_add_fusion.3.refs_0_, s32[2]{0:T(128)} %pad_add_fusion.4.refs_1_, s32[24]{0:T(128)} %pad_add_fusion.5.refs_2_, bf16[2,6,64,1024]{3,2,1,0:T(8,128)(2,1)} %copy-done.1, ...), custom_call_target="tpu_custom_call" | custom-call | tf_op jit(solution)/shard_map/chunk/pallas_call | solution.py:273
  146.6 3.2 %collective-permute-done.25 = bf16[2,6,64,1024]{3,2,1,0:T(8,128)(2,1)S(1)} collective-permute-done((bf16[2,6,64,1024]{3,2,1,0:T(8,128)(2,1)S(1)}, bf16[2,6,64,1024]{3,2,1,0:T(8,128)(2,1)S(1)}, u32[]{:S(2)}, u32[]{:S(2)}) %collective-permute-start.25) | collective-permute-done | bytes 1572896 | tf_op jit(solution)/shard_map/ppermute | solution.py:364
  152.1 11.4 %chunk.8 = (f32[1536,1024]{1,0:T(8,128)}, f32[1536,1024]{1,0:T(8,128)}) custom-call(s32[24]{0:T(128)} %pad_add_fusion.3.refs_0_, s32[2]{0:T(128)} %pad_add_fusion.4.refs_1_, s32[24]{0:T(128)} %pad_add_fusion.5.refs_2_, bf16[2,6,64,1024]{3,2,1,0:T(8,128)(2,1)} %copy-done.1, ...), custom_call_target="tpu_custom_call", output_to_operand_aliasing={{0}: (8, {}), {1}: (9, {})} | custom-call | tf_op jit(solution)/shard_map/chunk/pallas_call | solution.py:273
  163.5 8.7 %collective-permute-done.24.refs_7_.refs_9_ = bf16[4,256,512]{2,1,0:T(8,128)(2,1)S(1)} collective-permute-done((bf16[4,256,512]{2,1,0:T(8,128)(2,1)S(1)}, bf16[4,256,512]{2,1,0:T(8,128)(2,1)S(1)}, u32[]{:S(2)}, u32[]{:S(2)}) %collective-permute-start.24) | collective-permute-done | bytes 1048608 | tf_op jit(solution)/shard_map/ppermute | solution.py:367
  173.1 12.5 %chunk.9 = (f32[6,64,1024]{2,1,0:T(8,128)}, f32[6,64,1024]{2,1,0:T(8,128)}, bf16[6,64,1024]{2,1,0:T(8,128)(2,1)}, bf16[6,64,1024]{2,1,0:T(8,128)(2,1)}) custom-call(s32[24]{0:T(128)} %pad_add_fusion.3.refs_0_, s32[2]{0:T(128)} %pad_add_fusion.4.refs_1_, s32[24]{0:T(128)} %pad_add_fusion.5.refs_2_, bf16[2,6,64,1024]{3,2,1,0:T(8,128)(2,1)} %copy-done.1, ...), custom_call_target="tpu_custom_call" | custom-call | tf_op jit(solution)/shard_map/chunk/pallas_call | solution.py:273
  186.3 2.0 %collective-permute-done.26.other_out_ref = bf16[6,64,1024]{2,1,0:T(8,128)(2,1)S(1)} collective-permute-done((bf16[6,64,1024]{2,1,0:T(8,128)(2,1)}, bf16[6,64,1024]{2,1,0:T(8,128)(2,1)S(1)}, u32[]{:S(2)}, u32[]{:S(2)}) %collective-permute-start.26) | collective-permute-done | bytes 786464 | tf_op jit(solution)/shard_map/ppermute | solution.py:364
  190.8 5.9 %finish.1 = (bf16[6,64,1024]{2,1,0:T(8,128)(2,1)}, bf16[6,64,1024]{2,1,0:T(8,128)(2,1)}, f32[6,64]{1,0:T(8,128)}) custom-call(s32[6]{0:T(128)} %bitcast.86, bf16[6,64,1024]{2,1,0:T(8,128)(2,1)} %x_ref.1, bf16[6,64,1024]{2,1,0:T(8,128)(2,1)} %g_ref.1, f32[2,1024]{1,0:T(2,128)} %gain_ref.1, f32[6,64,1024]{2,1,0:T(8,128)} %get-tuple-element.63.out_ref, ...), custom_call_target="tpu_custom_call" | custom-call | tf_op jit(solution)/shard_map/finish/pallas_call | solution.py:323
  (128 shorter events, 35.5 us)
Async XLA Ops:
  7.4 10.4 %collective-permute-start.3 = (bf16[256,256]{1,0:T(8,128)(2,1)S(1)}, bf16[256,256]{1,0:T(8,128)(2,1)S(1)}, u32[]{:S(2)}, u32[]{:S(2)}) collective-permute-start(bf16[256,256]{1,0:T(8,128)(2,1)S(1)} %get-tuple-element.82), channel_id=1, source_target_pairs={{0,4},{1,5},{2,6},{3,7},{4,8},{5,9},{6,10},{7,11},{8,12},{9,13},{1... | collective-permute-start | bytes 393224 | tf_op jit(solution)/shard_map/ppermute | solution.py:373
  9.0 11.9 %collective-permute-start.5 = (bf16[256,256]{1,0:T(8,128)(2,1)S(1)}, bf16[256,256]{1,0:T(8,128)(2,1)S(1)}, u32[]{:S(2)}, u32[]{:S(2)}) collective-permute-start(bf16[256,256]{1,0:T(8,128)(2,1)S(1)} %get-tuple-element.82), channel_id=1, source_target_pairs={{0,8},{1,9},{2,10},{3,11},{4,12},{5,13},{6,14},{7,15},{8,0},{9,1},... | collective-permute-start | bytes 393224 | tf_op jit(solution)/shard_map/ppermute | solution.py:373
  10.1 10.9 %collective-permute-start.6 = (bf16[256,256]{1,0:T(8,128)(2,1)S(1)}, bf16[256,256]{1,0:T(8,128)(2,1)S(1)}, u32[]{:S(2)}, u32[]{:S(2)}) collective-permute-start(bf16[256,256]{1,0:T(8,128)(2,1)S(1)} %get-tuple-element.82), channel_id=1, source_target_pairs={{0,12},{1,13},{2,14},{3,15},{4,0},{5,1},{6,2},{7,3},{8,4},{9,5},{1... | collective-permute-start | bytes 393224 | tf_op jit(solution)/shard_map/ppermute | solution.py:373
  12.1 8.2 %collective-permute-start.2 = (s32[12]{0:T(128)S(1)}, s32[12]{0:T(128)S(1)}, u32[]{:S(2)}, u32[]{:S(2)}) collective-permute-start(s32[12]{0:T(128)S(1)} %pad_add_fusion), channel_id=1, source_target_pairs={{0,1},{1,0},{2,3},{3,2},{4,5},{5,4},{6,7},{7,6},{8,9},{9,8},{10,11... | collective-permute-start | bytes 152 | tf_op jit(solution)/shard_map/ppermute | solution.py:364
  18.6 32.4 %collective-permute-start.4 = (bf16[2,6,64,1024]{3,2,1,0:T(8,128)(2,1)S(1)}, bf16[2,6,64,1024]{3,2,1,0:T(8,128)(2,1)S(1)}, u32[]{:S(2)}, u32[]{:S(2)}) collective-permute-start(bf16[2,6,64,1024]{3,2,1,0:T(8,128)(2,1)S(1)} %get-tuple-element.45.refs_3_), channel_id=1, source_target_pairs={{0,16},{16,0},{1,17},{17,1},{2,18},{18,2},{3,19},{19,3},{4,20},{20... | collective-permute-start | bytes 4718600 | tf_op jit(solution)/shard_map/ppermute | solution.py:370
  21.1 25.5 %collective-permute-start.10 = (bf16[4,256,256]{2,1,0:T(8,128)(2,1)S(1)}, bf16[4,256,256]{2,1,0:T(8,128)(2,1)S(1)}, u32[]{:S(2)}, u32[]{:S(2)}) collective-permute-start(bf16[4,256,256]{2,1,0:T(8,128)(2,1)S(1)} %pad_maximum_fusion.10.refs_6_), channel_id=1, source_target_pairs={{0,2},{1,3},{2,0},{3,1},{4,6},{5,7},{6,4},{7,5},{8,10},{9,11},{10,... | collective-permute-start | bytes 1572872 | tf_op jit(solution)/shard_map/ppermute | solution.py:367
  22.8 19.8 %collective-permute-start.7 = (bf16[256,512]{1,0:T(8,128)(2,1)S(1)}, bf16[256,512]{1,0:T(8,128)(2,1)S(1)}, u32[]{:S(2)}, u32[]{:S(2)}) collective-permute-start(bf16[256,512]{1,0:T(8,128)(2,1)S(1)} %get-tuple-element.38), channel_id=1, source_target_pairs={{0,4},{1,5},{2,6},{3,7},{4,8},{5,9},{6,10},{7,11},{8,12},{9,13},{1... | collective-permute-start | bytes 786440 | tf_op jit(solution)/shard_map/ppermute | solution.py:373
  25.1 20.3 %collective-permute-start.8 = (bf16[256,512]{1,0:T(8,128)(2,1)S(1)}, bf16[256,512]{1,0:T(8,128)(2,1)S(1)}, u32[]{:S(2)}, u32[]{:S(2)}) collective-permute-start(bf16[256,512]{1,0:T(8,128)(2,1)S(1)} %get-tuple-element.38), channel_id=1, source_target_pairs={{0,8},{1,9},{2,10},{3,11},{4,12},{5,13},{6,14},{7,15},{8,0},{9,1},... | collective-permute-start | bytes 786440 | tf_op jit(solution)/shard_map/ppermute | solution.py:373
  25.1 21.5 %collective-permute-start.9 = (bf16[256,512]{1,0:T(8,128)(2,1)S(1)}, bf16[256,512]{1,0:T(8,128)(2,1)S(1)}, u32[]{:S(2)}, u32[]{:S(2)}) collective-permute-start(bf16[256,512]{1,0:T(8,128)(2,1)S(1)} %get-tuple-element.38), channel_id=1, source_target_pairs={{0,12},{1,13},{2,14},{3,15},{4,0},{5,1},{6,2},{7,3},{8,4},{9,5},{1... | collective-permute-start | bytes 786440 | tf_op jit(solution)/shard_map/ppermute | solution.py:373
  52.2 29.4 %collective-permute-start.11 = (bf16[2,2,6,64,1024]{4,3,2,1,0:T(8,128)(2,1)S(1)}, bf16[2,2,6,64,1024]{4,3,2,1,0:T(8,128)(2,1)S(1)}, u32[]{:S(2)}, u32[]{:S(2)}) collective-permute-start(bf16[2,2,6,64,1024]{4,3,2,1,0:T(8,128)(2,1)S(1)} %pad_maximum_fusion), channel_id=1, source_target_pairs={{0,1},{1,0},{2,3},{3,2},{4,5},{5,4},{6,7},{7,6},{8,9},{9,8},{10,11... | collective-permute-start | bytes 9437192 | tf_op jit(solution)/shard_map/ppermute | solution.py:364
  52.3 28.3 %collective-permute-start.15 = (bf16[4,256,512]{2,1,0:T(8,128)(2,1)S(1)}, bf16[4,256,512]{2,1,0:T(8,128)(2,1)S(1)}, u32[]{:S(2)}, u32[]{:S(2)}) collective-permute-start(bf16[4,256,512]{2,1,0:T(8,128)(2,1)S(1)} %pad_maximum_fusion.4.refs_8_), channel_id=1, source_target_pairs={{0,2},{1,3},{2,0},{3,1},{4,6},{5,7},{6,4},{7,5},{8,10},{9,11},{10,... | collective-permute-start | bytes 3145736 | tf_op jit(solution)/shard_map/ppermute | solution.py:367
  53.9 9.1 %collective-permute-start.12 = (bf16[256,512]{1,0:T(8,128)(2,1)S(1)}, bf16[256,512]{1,0:T(8,128)(2,1)S(1)}, u32[]{:S(2)}, u32[]{:S(2)}) collective-permute-start(bf16[256,512]{1,0:T(8,128)(2,1)S(1)} %get-tuple-element.41), channel_id=1, source_target_pairs={{0,4},{1,5},{2,6},{3,7},{4,8},{5,9},{6,10},{7,11},{8,12},{9,13},{1... | collective-permute-start | bytes 786440 | tf_op jit(solution)/shard_map/ppermute | solution.py:373
  54.1 22.9 %collective-permute-start.13 = (bf16[256,512]{1,0:T(8,128)(2,1)S(1)}, bf16[256,512]{1,0:T(8,128)(2,1)S(1)}, u32[]{:S(2)}, u32[]{:S(2)}) collective-permute-start(bf16[256,512]{1,0:T(8,128)(2,1)S(1)} %get-tuple-element.41), channel_id=1, source_target_pairs={{0,8},{1,9},{2,10},{3,11},{4,12},{5,13},{6,14},{7,15},{8,0},{9,1},... | collective-permute-start | bytes 786440 | tf_op jit(solution)/shard_map/ppermute | solution.py:373
  57.6 22.8 %collective-permute-start.14 = (bf16[256,512]{1,0:T(8,128)(2,1)S(1)}, bf16[256,512]{1,0:T(8,128)(2,1)S(1)}, u32[]{:S(2)}, u32[]{:S(2)}) collective-permute-start(bf16[256,512]{1,0:T(8,128)(2,1)S(1)} %get-tuple-element.41), channel_id=1, source_target_pairs={{0,12},{1,13},{2,14},{3,15},{4,0},{5,1},{6,2},{7,3},{8,4},{9,5},{1... | collective-permute-start | bytes 786440 | tf_op jit(solution)/shard_map/ppermute | solution.py:373
  81.6 25.3 %collective-permute-start.19 = (bf16[4,256,512]{2,1,0:T(8,128)(2,1)S(1)}, bf16[4,256,512]{2,1,0:T(8,128)(2,1)S(1)}, u32[]{:S(2)}, u32[]{:S(2)}) collective-permute-start(bf16[4,256,512]{2,1,0:T(8,128)(2,1)S(1)} %pad_maximum_fusion.5.refs_6_.refs_8_), channel_id=1, source_target_pairs={{0,2},{1,3},{2,0},{3,1},{4,6},{5,7},{6,4},{7,5},{8,10},{9,11},{10,... | collective-permute-start | bytes 3145736 | tf_op jit(solution)/shard_map/ppermute | solution.py:367
  82.1 19.0 %collective-permute-start.16 = (bf16[256,512]{1,0:T(8,128)(2,1)S(1)}, bf16[256,512]{1,0:T(8,128)(2,1)S(1)}, u32[]{:S(2)}, u32[]{:S(2)}) collective-permute-start(bf16[256,512]{1,0:T(8,128)(2,1)S(1)} %get-tuple-element.43), channel_id=1, source_target_pairs={{0,4},{1,5},{2,6},{3,7},{4,8},{5,9},{6,10},{7,11},{8,12},{9,13},{1... | collective-permute-start | bytes 786440 | tf_op jit(solution)/shard_map/ppermute | solution.py:373
  82.1 22.1 %collective-permute-start.17 = (bf16[256,512]{1,0:T(8,128)(2,1)S(1)}, bf16[256,512]{1,0:T(8,128)(2,1)S(1)}, u32[]{:S(2)}, u32[]{:S(2)}) collective-permute-start(bf16[256,512]{1,0:T(8,128)(2,1)S(1)} %get-tuple-element.43), channel_id=1, source_target_pairs={{0,8},{1,9},{2,10},{3,11},{4,12},{5,13},{6,14},{7,15},{8,0},{9,1},... | collective-permute-start | bytes 786440 | tf_op jit(solution)/shard_map/ppermute | solution.py:373
  84.2 22.5 %collective-permute-start.18 = (bf16[256,512]{1,0:T(8,128)(2,1)S(1)}, bf16[256,512]{1,0:T(8,128)(2,1)S(1)}, u32[]{:S(2)}, u32[]{:S(2)}) collective-permute-start(bf16[256,512]{1,0:T(8,128)(2,1)S(1)} %get-tuple-element.43), channel_id=1, source_target_pairs={{0,12},{1,13},{2,14},{3,15},{4,0},{5,1},{6,2},{7,3},{8,4},{9,5},{1... | collective-permute-start | bytes 786440 | tf_op jit(solution)/shard_map/ppermute | solution.py:373
  106.9 25.1 %collective-permute-start.23 = (bf16[4,256,512]{2,1,0:T(8,128)(2,1)S(1)}, bf16[4,256,512]{2,1,0:T(8,128)(2,1)S(1)}, u32[]{:S(2)}, u32[]{:S(2)}) collective-permute-start(bf16[4,256,512]{2,1,0:T(8,128)(2,1)S(1)} %pad_maximum_fusion.7.refs_6_), channel_id=1, source_target_pairs={{0,2},{1,3},{2,0},{3,1},{4,6},{5,7},{6,4},{7,5},{8,10},{9,11},{10,... | collective-permute-start | bytes 3145736 | tf_op jit(solution)/shard_map/ppermute | solution.py:367
  107.5 22.6 %collective-permute-start.20 = (bf16[256,512]{1,0:T(8,128)(2,1)S(1)}, bf16[256,512]{1,0:T(8,128)(2,1)S(1)}, u32[]{:S(2)}, u32[]{:S(2)}) collective-permute-start(bf16[256,512]{1,0:T(8,128)(2,1)S(1)} %copy-done.20), channel_id=1, source_target_pairs={{0,4},{1,5},{2,6},{3,7},{4,8},{5,9},{6,10},{7,11},{8,12},{9,13},{1... | collective-permute-start | bytes 786440 | tf_op jit(solution)/shard_map/ppermute | solution.py:373
  107.5 22.6 %collective-permute-start.21 = (bf16[256,512]{1,0:T(8,128)(2,1)S(1)}, bf16[256,512]{1,0:T(8,128)(2,1)S(1)}, u32[]{:S(2)}, u32[]{:S(2)}) collective-permute-start(bf16[256,512]{1,0:T(8,128)(2,1)S(1)} %copy-done.20), channel_id=1, source_target_pairs={{0,8},{1,9},{2,10},{3,11},{4,12},{5,13},{6,14},{7,15},{8,0},{9,1},... | collective-permute-start | bytes 786440 | tf_op jit(solution)/shard_map/ppermute | solution.py:373
  109.4 21.6 %collective-permute-start.22 = (bf16[256,512]{1,0:T(8,128)(2,1)S(1)}, bf16[256,512]{1,0:T(8,128)(2,1)S(1)}, u32[]{:S(2)}, u32[]{:S(2)}) collective-permute-start(bf16[256,512]{1,0:T(8,128)(2,1)S(1)} %copy-done.20), channel_id=1, source_target_pairs={{0,12},{1,13},{2,14},{3,15},{4,0},{5,1},{6,2},{7,3},{8,4},{9,5},{1... | collective-permute-start | bytes 786440 | tf_op jit(solution)/shard_map/ppermute | solution.py:373
  146.6 25.6 %collective-permute-start.24 = (bf16[4,256,512]{2,1,0:T(8,128)(2,1)S(1)}, bf16[4,256,512]{2,1,0:T(8,128)(2,1)S(1)}, u32[]{:S(2)}, u32[]{:S(2)}) collective-permute-start(bf16[4,256,512]{2,1,0:T(8,128)(2,1)S(1)} %pad_maximum_fusion.6.refs_6_.refs_8_), channel_id=1, source_target_pairs={{0,2},{1,3},{2,0},{3,1},{4,6},{5,7},{6,4},{7,5},{8,10},{9,11},{10,... | collective-permute-start | bytes 3145736 | tf_op jit(solution)/shard_map/ppermute | solution.py:367
  150.5 38.9 %collective-permute-start.28 = (bf16[2,6,64,1024]{3,2,1,0:T(8,128)(2,1)S(1)}, bf16[2,6,64,1024]{3,2,1,0:T(8,128)(2,1)S(1)}, u32[]{:S(2)}, u32[]{:S(2)}) collective-permute-start(bf16[2,6,64,1024]{3,2,1,0:T(8,128)(2,1)S(1)} %add_convert_fusion), channel_id=1, source_target_pairs={{0,16},{16,0},{1,17},{17,1},{2,18},{18,2},{3,19},{19,3},{4,20},{20... | collective-permute-start | bytes 4718600 | tf_op jit(solution)/shard_map/ppermute | solution.py:370
  (30 other events, 215.4 us)

commit v11 on v10

--- a/solution.py
+++ b/solution.py
@@ -85,28 +85,31 @@
     )
 
 
-VMEM_LIMIT = 56 * 1024 * 1024
+VMEM_LIMIT = 40 * 1024 * 1024
 BF16 = jnp.bfloat16
 F32 = jnp.float32
 
 
 def chunk_kernel(
-    offset, kind, units, sorted_ref, place_ref, perm_ref, near_ref, over_ref, far_ref, *refs
+    offset, kind, units, chips, sorted_ref, place_ref, perm_ref, *refs
 ):
     first, last = kind
     parts = len(units)
+    tokens_of, refs = refs[: len(chips) + 1], refs[len(chips) + 1 :]
     pieces, refs = refs[: 2 * parts], refs[2 * parts :]
     if first:
-        *outs, weights_ref, sems, lifted_ref, g_ref, act_ref, pre_ref = refs
+        *outs, tokens_ref, weights_ref, sems, lifted_ref, g_ref, act_ref, pre_ref = refs
     elif last:
-        out_in, back_in, *outs, weights_ref, sems, lifted_ref, g_ref, act_ref, pre_ref = refs[:-2]
+        out_in, back_in, *outs, tokens_ref, weights_ref, sems = refs[:-6]
+        lifted_ref, g_ref, act_ref, pre_ref = refs[-6:-2]
         out_acc, back_acc = refs[-2:]
     else:
-        out_in, back_in, *outs, weights_ref, sems, lifted_ref, g_ref, act_ref, pre_ref = refs
+        out_in, back_in, *outs, tokens_ref, weights_ref, sems = refs[:-4]
+        lifted_ref, g_ref, act_ref, pre_ref = refs[-4:]
     if not last:
         out_acc, back_acc = outs
     j = pl.program_id(0)
-    rows, seq = near_ref.shape[1:3]
+    rows, seq = tokens_ref.shape[2:4]
     per_block = lifted_ref.shape[0] // seq
     places = [(j + offset) * per_block + i for i in range(per_block)]
     lines, _, depth2, _ = weights_ref.shape
@@ -117,6 +120,11 @@
     def _():
         y, z = place_ref[0], place_ref[1]
         copies = []
+        for i, chip in enumerate(chips):
+            for k, ref in enumerate((tokens_of[i], tokens_of[-1].at[chip])):
+                copies.append(
+                    pltpu.make_async_copy(ref, tokens_ref.at[2 * i + k], sems.at[len(copies)])
+                )
         for part in range(parts):
             n = units[part][1]
             for to_y, (ref, start) in zip((y, 1 - y), pieces[2 * part : 2 * part + 2]):
@@ -140,16 +148,15 @@
     def pick_up(member):
         for i, at in enumerate(places):
             row = perm_ref[at]
-            source = jnp.where(here[i] == member, row // rows, 4)
+            source = row // rows - 2 * chips[0]
             tokens = pl.ds(i * seq, seq)
-            for k, ref in enumerate((near_ref, far_ref.at[0], over_ref, far_ref.at[1])):
-
-                @pl.when(source == k)
-                def _():
-                    lifted_ref[tokens, :] = ref[0, row - k * rows]
-                    g_ref[tokens, :] = ref[1, row - k * rows]
-
-            @pl.when(source == 4)
+
+            @pl.when(here[i] == member)
+            def _():
+                lifted_ref[tokens, :] = tokens_ref[source, 0, lax.rem(row, rows)]
+                g_ref[tokens, :] = tokens_ref[source, 1, lax.rem(row, rows)]
+
+            @pl.when(here[i] != member)
             def _():
                 lifted_ref[tokens, :] = jnp.zeros((seq, width), BF16)
                 g_ref[tokens, :] = jnp.zeros((seq, width), BF16)
@@ -220,7 +227,7 @@
                 low += n
 
 
-def chunk(kind, blocks, scalars, tokens_of, pieces, sums, outs=None, weight=1):
+def chunk(kind, blocks, chips, scalars, tokens_of, pieces, sums, outs=None, weight=1):
     first, last = kind
     offset, number, per_block = blocks
     _, rows, seq, width = tokens_of[0].shape
@@ -231,11 +238,8 @@
 
     tok = pl.BlockSpec((size, width), lambda j, *_: (j + offset, 0))
     hbm = pl.BlockSpec(memory_space=pl.ANY)
-    args = [*scalars, *tokens_of]
-    specs = [
-        pl.BlockSpec(a.shape, lambda *_, n=a.ndim: (0,) * n, pipeline_mode=pl.Buffered(1))
-        for a in tokens_of
-    ]
+    args = [*scalars, *(tokens_of[chip] for chip in chips), tokens_of[-1]]
+    specs = [hbm] * (len(chips) + 1)
     starts = []
     for _, _, *both in pieces:
         args += [array for array, _ in both]
@@ -245,8 +249,9 @@
     out_specs = [tok, tok]
     out_shape = [jax.ShapeDtypeStruct((4 * rows * seq, width), F32)] * 2
     scratch = [
+        pltpu.VMEM((2 * len(chips), 2, rows, seq, width), BF16),
         pltpu.VMEM((lines, 2, depth2, hidden), BF16),
-        pltpu.SemaphoreType.DMA((len(pieces) * 2 * lines,)),
+        pltpu.SemaphoreType.DMA((len(pieces) * 2 * lines + 2 * len(chips),)),
         pltpu.VMEM((size, width), BF16),
         pltpu.VMEM((size, width), BF16),
         pltpu.VMEM((size, hidden), BF16),
@@ -265,10 +270,10 @@
 
     def kernel(*refs):
         refs = list(refs)
-        base = len(scalars) + len(tokens_of)
+        base = len(scalars) + len(chips) + 1
         for i, start in enumerate(starts):
             refs[base + i] = (refs[base + i], start)
-        chunk_kernel(offset, kind, units, *refs)
+        chunk_kernel(offset, kind, units, chips, *refs)
 
     return pl.pallas_call(
         kernel,
@@ -390,12 +395,19 @@
 
     pick_own = member_pick[:, 0]
     pick_near = jnp.concatenate([pick_own, over_x(pick_own)])
-    mine = units_of(core)
-    theirs = after(partner(units_of(1 - core)), pick_near)
-    even = core == 0
-    shard = jnp.concatenate(
-        [jnp.where(even, mine, theirs), jnp.where(even, theirs, mine)], axis=2
-    ).reshape(members, 4 * depth, quarter + half)
+    def both_cores(mine, theirs):
+        even = core == 0
+        whole = jnp.concatenate(
+            [jnp.where(even, mine, theirs), jnp.where(even, theirs, mine)], axis=2
+        )
+        return whole.reshape(mine.shape[0], 4 * depth, mine.shape[3])
+
+    mine, given = units_of(core), units_of(1 - core)
+    head = 2 * unit
+    head_theirs = after(partner(given[:1, :, :, :head]), pick_near)
+    shard_head = both_cores(mine[:1, :, :, :head], head_theirs)
+    theirs = partner(after(given, head_theirs))
+    shard = both_cores(mine, theirs)
 
     groups = [
         [(0, 0, 2 * unit)],
@@ -404,9 +416,9 @@
         [(1, 3 * unit, 4 * unit)],
         [(0, quarter, half), (1, quarter, half)],
     ]
-    send = [
+    send = [shard_head[0]] + [
         jnp.concatenate([shard[m, :, at : at + n] for m, at, n in group], axis=1)
-        for group in groups
+        for group in groups[1:]
     ]
     here, there = [], []
 
@@ -433,7 +445,7 @@
 
     per_block = math.gcd(2 * rows, 4)
     per_chip = 2 * rows // per_block
-    pick_far = partner(after(pick_near, theirs))
+    pick_far = partner(after(pick_near, head_theirs))
 
     arrived = exchange(0, [])
     x = after(tokens_in, arrived[0]).astype(F32)
@@ -456,22 +468,18 @@
     arrived = exchange(1, arrived)
     arrived += [*scalars]
 
-    set_1, arrived = arrived, exchange(2, arrived)
-    far = partner(jnp.stack([near, after(over, *set_1)]))
+    arrived = exchange(2, arrived)
+    arrived += [over]
+
+    set_2, arrived = arrived, exchange(3, arrived)
+    far = partner(after(jnp.stack([near, over]), *set_2))
     arrived += [far]
     tokens_of = (near, over, far)
 
-    set_2, arrived = arrived, exchange(3, arrived)
-    whole = (0, 2 * per_chip, per_block)
-    sums = chunk(
-        (True, False), whole, scalars, (after(near, *set_2), over, far), chunk_pieces(0, 1), None
-    )
-    arrived += [sums[0]]
-
     set_3, arrived = arrived, exchange(4, arrived)
     sums = chunk(
-        (False, False), whole, scalars, tokens_of, chunk_pieces(2),
-        (after(sums[0], *set_3), sums[1]),
+        (True, False), (0, 2 * per_chip, per_block), (0, 1), scalars,
+        (after(near, *set_3), over, far), chunk_pieces(0, 1, 2), None,
     )
     arrived += [sums[0]]
 
@@ -479,17 +487,21 @@
     exchange(5, arrived)
     sums = (after(sums[0], *set_4), sums[1])
     *same, other_out, other_back = chunk(
-        (False, True), (0, per_chip, per_block), scalars, tokens_of, chunk_pieces(3), sums,
+        (False, True), (0, per_chip, per_block), (1,), scalars, tokens_of, chunk_pieces(3), sums,
         (BF16, BF16), 0,
     )
-    others = partner(jnp.stack([other_out, other_back]))
-    across = (jnp.stack(same).astype(F32) + others.astype(F32)).astype(BF16)
+    across = jnp.stack(
+        [
+            (a.astype(F32) + partner(b).astype(F32)).astype(BF16)
+            for a, b in zip(same, (other_out, other_back))
+        ]
+    )
     sums = tuple(after(a, across) for a in sums)
     across = over_x(across)
     own = (per_chip, per_chip, per_block)
-    sums = chunk((False, False), own, scalars, tokens_of, chunk_pieces(3), sums, None, 0)
+    sums = chunk((False, False), own, (0,), scalars, tokens_of, chunk_pieces(3), sums, None, 0)
     out, back, packed_out, packed_back = chunk(
-        (False, True), own, scalars, tokens_of, chunk_pieces(4), sums, (F32, BF16), 0
+        (False, True), own, (0,), scalars, tokens_of, chunk_pieces(4), sums, (F32, BF16), 0
     )
     return tuple(
         finish(

time: 200 us -> 183 us (0.915)
  Pallas kernels: 77.1 us -> 42.2 us
  waiting for transfers between devices: 75.1 us -> 86.4 us
  starting transfers between devices: 27.8 us -> 34.3 us
    pallas_call x5 -> x4, Pallas kernels: 71.2 us -> 39.3 us  [chunk(): pl.pallas_call(kernel, grid_spec=pltpu.PrefetchScalarGridSpec(num_scalar_...]
    ppermute x15, waiting for transfers between devices: 53.3 us -> 68 us  [shift_z(): lax.ppermute(a, 'row', [(i, (i + 4 * d) % ranks) for i in range(ranks)])]
    ppermute x5, starting transfers between devices: 4.38 us -> 8.38 us  [over_y(): return lax.ppermute(a, 'row', [(i, i ^ 2) for i in range(ranks)])]
    ppermute x15, starting transfers between devices: 18.1 us -> 21.5 us  [shift_z(): lax.ppermute(a, 'row', [(i, (i + 4 * d) % ranks) for i in range(ranks)])]
    pallas_call x1, Pallas kernels: 5.92 us -> 2.91 us  [finish(): pl.pallas_call(finish_kernel, grid_spec=pltpu.PrefetchScalarGridSpec(num_...]
    ppermute x3, waiting for transfers between devices: 5.78 us -> 2.94 us  [over_x(): return lax.ppermute(a, 'grp', [(0, 1), (1, 0)])]
    unnamed x50 -> x26, local copies, waits for them, and re-layouts: 6.12 us -> 8.11 us
    ppermute x6 -> x8, waiting for transfers between devices: 6.28 us -> 4.41 us  [partner(): return lax.ppermute(a, 'row', [(i, i ^ 1) for i in range(ranks)])]
  transfers between devices with their start and end apart: 29 -> 31, of which waited for: 18 -> 18; matrix products, arithmetic and copies ran while one was open for 3% -> 4% of each run, Pallas kernels for 30% -> 18%
where the time goes in v11:
time: 183 us; the launch traced here: 181 us
  waiting for transfers between devices  86.4 us (47%)
  Pallas kernels  42.2 us (23%)
  starting transfers between devices  34.3 us (19%)
  other arithmetic  8.87 us (5%)
  local copies, waits for them, and re-layouts  8.42 us (5%)
    ppermute x15, waiting for transfers between devices, shift_z(): lax.ppermute(a, 'row', [(i, (i + 4 * d) % ranks) for i in range(ranks)])  68 us
    pallas_call x4, Pallas kernels, chunk(): pl.pallas_call(kernel, grid_spec=pltpu.PrefetchScalarGridSpec(num_scalar_...  39.3 us
    ppermute x15, starting transfers between devices, shift_z(): lax.ppermute(a, 'row', [(i, (i + 4 * d) % ranks) for i in range(ranks)])  21.5 us
    ppermute x5, waiting for transfers between devices, over_y(): return lax.ppermute(a, 'row', [(i, i ^ 2) for i in range(ranks)])  11 us
    ppermute x5, starting transfers between devices, over_y(): return lax.ppermute(a, 'row', [(i, i ^ 2) for i in range(ranks)])  8.38 us
    unnamed x26, local copies, waits for them, and re-layouts  8.11 us
    ppermute x8, waiting for transfers between devices, partner(): return lax.ppermute(a, 'row', [(i, i ^ 1) for i in range(ranks)])  4.41 us
  transfers between devices with their start and end apart: 31, of which 18 were waited for; matrix products, arithmetic and copies ran while one was open for 4% of the time, Pallas kernels for 18%

profile of v11, /device:TPU:8, one launch (start us, length us, event | category | flops | bytes accessed | tf_op | source)
XLA Modules:
  0.0 181.2 jit_solution(3594507247746466505)
XLA Ops:
  10.9 1.8 collective-permute-start.7
  15.8 3.3 %collective-permute-done.3 = bf16[256,256]{1,0:T(8,128)(2,1)S(1)} collective-permute-done((bf16[256,256]{1,0:T(8,128)(2,1)S(1)}, bf16[256,256]{1,0:T(8,128)(2,1)S(1)}, u32[]{:S(2)}, u32[]{:S(2)}) %collective-permute-start.3) | collective-permute-done | bytes 131104 | tf_op jit(solution)/shard_map/ppermute | solution.py:378
  25.5 2.0 %collective-permute-start.8 = (bf16[256,512]{1,0:T(8,128)(2,1)S(1)}, bf16[256,512]{1,0:T(8,128)(2,1)S(1)}, u32[]{:S(2)}, u32[]{:S(2)}) collective-permute-start(bf16[256,512]{1,0:T(8,128)(2,1)S(1)} %get-tuple-element.37), channel_id=1, source_target_pairs={{0,4},{1,5},{2,6},{3,7},{4,8},{5,9},{6,10},{7,11},{8,12},{9,13},{1... | collective-permute-start | bytes 786440 | tf_op jit(solution)/shard_map/ppermute | solution.py:378
  27.5 3.4 %collective-permute-start.9 = (bf16[256,512]{1,0:T(8,128)(2,1)S(1)}, bf16[256,512]{1,0:T(8,128)(2,1)S(1)}, u32[]{:S(2)}, u32[]{:S(2)}) collective-permute-start(bf16[256,512]{1,0:T(8,128)(2,1)S(1)} %get-tuple-element.37), channel_id=1, source_target_pairs={{0,8},{1,9},{2,10},{3,11},{4,12},{5,13},{6,14},{7,15},{8,0},{9,1},... | collective-permute-start | bytes 786440 | tf_op jit(solution)/shard_map/ppermute | solution.py:378
  31.2 14.7 %collective-permute-done.10 = bf16[256,512]{1,0:T(8,128)(2,1)S(1)} collective-permute-done((bf16[256,512]{1,0:T(8,128)(2,1)S(1)}, bf16[256,512]{1,0:T(8,128)(2,1)S(1)}, u32[]{:S(2)}, u32[]{:S(2)}) %collective-permute-start.10) | collective-permute-done | bytes 262176 | tf_op jit(solution)/shard_map/ppermute | solution.py:378
  46.0 3.6 %collective-permute-done.9 = bf16[256,512]{1,0:T(8,128)(2,1)S(1)} collective-permute-done((bf16[256,512]{1,0:T(8,128)(2,1)S(1)}, bf16[256,512]{1,0:T(8,128)(2,1)S(1)}, u32[]{:S(2)}, u32[]{:S(2)}) %collective-permute-start.9) | collective-permute-done | bytes 262176 | tf_op jit(solution)/shard_map/ppermute | solution.py:378
  50.6 4.3 %collective-permute-start.13 = (bf16[256,512]{1,0:T(8,128)(2,1)S(1)}, bf16[256,512]{1,0:T(8,128)(2,1)S(1)}, u32[]{:S(2)}, u32[]{:S(2)}) collective-permute-start(bf16[256,512]{1,0:T(8,128)(2,1)S(1)} %get-tuple-element.39), channel_id=1, source_target_pairs={{0,8},{1,9},{2,10},{3,11},{4,12},{5,13},{6,14},{7,15},{8,0},{9,1},... | collective-permute-start | bytes 786440 | tf_op jit(solution)/shard_map/ppermute | solution.py:378
  56.0 3.7 %collective-permute-done.12 = bf16[256,512]{1,0:T(8,128)(2,1)S(1)} collective-permute-done((bf16[256,512]{1,0:T(8,128)(2,1)S(1)}, bf16[256,512]{1,0:T(8,128)(2,1)S(1)}, u32[]{:S(2)}, u32[]{:S(2)}) %collective-permute-start.12) | collective-permute-done | bytes 262176 | tf_op jit(solution)/shard_map/ppermute | solution.py:378
  59.7 13.1 %collective-permute-done.13 = bf16[256,512]{1,0:T(8,128)(2,1)S(1)} collective-permute-done((bf16[256,512]{1,0:T(8,128)(2,1)S(1)}, bf16[256,512]{1,0:T(8,128)(2,1)S(1)}, u32[]{:S(2)}, u32[]{:S(2)}) %collective-permute-start.13) | collective-permute-done | bytes 262176 | tf_op jit(solution)/shard_map/ppermute | solution.py:378
  72.8 3.9 %collective-permute-done.14 = bf16[256,512]{1,0:T(8,128)(2,1)S(1)} collective-permute-done((bf16[256,512]{1,0:T(8,128)(2,1)S(1)}, bf16[256,512]{1,0:T(8,128)(2,1)S(1)}, u32[]{:S(2)}, u32[]{:S(2)}) %collective-permute-start.14) | collective-permute-done | bytes 262176 | tf_op jit(solution)/shard_map/ppermute | solution.py:378
  79.0 1.9 %collective-permute-start.19 = (bf16[256,512]{1,0:T(8,128)(2,1)S(1)}, bf16[256,512]{1,0:T(8,128)(2,1)S(1)}, u32[]{:S(2)}, u32[]{:S(2)}) collective-permute-start(bf16[256,512]{1,0:T(8,128)(2,1)S(1)} %get-tuple-element.42), channel_id=1, source_target_pairs={{0,12},{1,13},{2,14},{3,15},{4,0},{5,1},{6,2},{7,3},{8,4},{9,5},{1... | collective-permute-start | bytes 786440 | tf_op jit(solution)/shard_map/ppermute | solution.py:378
  80.9 6.7 %collective-permute-done.17 = bf16[256,512]{1,0:T(8,128)(2,1)S(1)} collective-permute-done((bf16[256,512]{1,0:T(8,128)(2,1)S(1)}, bf16[256,512]{1,0:T(8,128)(2,1)S(1)}, u32[]{:S(2)}, u32[]{:S(2)}) %collective-permute-start.17) | collective-permute-done | bytes 262176 | tf_op jit(solution)/shard_map/ppermute | solution.py:378
  87.6 13.9 %collective-permute-done.18 = bf16[256,512]{1,0:T(8,128)(2,1)S(1)} collective-permute-done((bf16[256,512]{1,0:T(8,128)(2,1)S(1)}, bf16[256,512]{1,0:T(8,128)(2,1)S(1)}, u32[]{:S(2)}, u32[]{:S(2)}) %collective-permute-start.18) | collective-permute-done | bytes 262176 | tf_op jit(solution)/shard_map/ppermute | solution.py:378
  105.6 2.0 %collective-permute-start.23 = (bf16[256,512]{1,0:T(8,128)(2,1)S(1)}, bf16[256,512]{1,0:T(8,128)(2,1)S(1)}, u32[]{:S(2)}, u32[]{:S(2)}) collective-permute-start(bf16[256,512]{1,0:T(8,128)(2,1)S(1)} %get-tuple-element.44), channel_id=1, source_target_pairs={{0,12},{1,13},{2,14},{3,15},{4,0},{5,1},{6,2},{7,3},{8,4},{9,5},{1... | collective-permute-start | bytes 786440 | tf_op jit(solution)/shard_map/ppermute | solution.py:378
  107.6 18.6 %chunk.4 = (f32[1536,1024]{1,0:T(8,128)}, f32[1536,1024]{1,0:T(8,128)}) custom-call(s32[24]{0:T(128)S(1)} %pad_add_fusion.3.refs_0_, s32[2]{0:T(128)S(1)} %pad_add_fusion.4.refs_1_, s32[24]{0:T(128)S(1)} %pad_add_fusion.5.refs_2_, bf16[2,6,64,1024]{3,2,1,0:T(8,128)(2,1)S(1)} %get-tuple-element.46.refs_3_, ...), custom_call_target="tpu_custom_call" | custom-call | flops 10737418240 | bytes 36700160 | tf_op jit(solution)/shard_map/chunk/pallas_call | solution.py:278
  128.4 6.6 %chunk.5 = (bf16[6,64,1024]{2,1,0:T(8,128)(2,1)S(1)}, bf16[6,64,1024]{2,1,0:T(8,128)(2,1)S(1)}, bf16[6,64,1024]{2,1,0:T(8,128)(2,1)S(1)}, bf16[6,64,1024]{2,1,0:T(8,128)(2,1)S(1)}) custom-call(s32[24]{0:T(128)S(1)} %pad_add_fusion.3.refs_0_, s32[2]{0:T(128)S(1)} %pad_add_fusion.4.refs_1_, s32[24]{0:T(128)S(1)} %pad_add_fusion.5.refs_2_, ...), custom_call_target="tpu_custom_call" | custom-call | tf_op jit(solution)/shard_map/chunk/pallas_call | solution.py:278
  135.7 3.0 %collective-permute-start.25 = (bf16[4,256,512]{2,1,0:T(8,128)(2,1)S(1)}, bf16[4,256,512]{2,1,0:T(8,128)(2,1)S(1)}, u32[]{:S(2)}, u32[]{:S(2)}) collective-permute-start(bf16[4,256,512]{2,1,0:T(8,128)(2,1)S(1)} %pad_maximum_fusion.6.refs_5_.refs_7_), channel_id=1, source_target_pairs={{0,2},{1,3},{2,0},{3,1},{4,6},{5,7},{6,4},{7,5},{8,10},{9,11},{10,... | collective-permute-start | bytes 3145736 | tf_op jit(solution)/shard_map/ppermute | solution.py:372
  139.7 1.9 %copy-done = f32[1536,1024]{1,0:T(8,128)S(1)} copy-done((f32[1536,1024]{1,0:T(8,128)S(1)}, f32[1536,1024]{1,0:T(8,128)}, u32[]{:S(2)}) %copy-start) | copy-done | bytes 6291480
  141.6 6.9 %chunk.6 = (f32[1536,1024]{1,0:T(8,128)S(1)}, f32[1536,1024]{1,0:T(8,128)}) custom-call(s32[24]{0:T(128)S(1)} %pad_add_fusion.3.refs_0_, s32[2]{0:T(128)S(1)} %pad_add_fusion.4.refs_1_, s32[24]{0:T(128)S(1)} %pad_add_fusion.5.refs_2_, bf16[2,6,64,1024]{3,2,1,0:T(8,128)(2,1)S(1)} %get-tuple-element.46.refs_3_, ...), custom_call_target="tpu_custom_call", output_to_operand_aliasing={{0}: (7, {}), {1}: (8, {})} | custom-call | tf_op jit(solution)/shard_map/chunk/pallas_call | solution.py:278
  148.5 2.6 %copy-done.1 = f32[1536,1024]{1,0:T(8,128)} copy-done((f32[1536,1024]{1,0:T(8,128)}, f32[1536,1024]{1,0:T(8,128)S(1)}, u32[]{:S(2)}) %copy-start.1) | copy-done | bytes 6291480
  151.2 11.0 %collective-permute-done.25.refs_6_.refs_8_ = bf16[4,256,512]{2,1,0:T(8,128)(2,1)S(1)} collective-permute-done((bf16[4,256,512]{2,1,0:T(8,128)(2,1)S(1)}, bf16[4,256,512]{2,1,0:T(8,128)(2,1)S(1)}, u32[]{:S(2)}, u32[]{:S(2)}) %collective-permute-start.25) | collective-permute-done | bytes 1048608 | tf_op jit(solution)/shard_map/ppermute | solution.py:372
  162.2 7.1 %chunk.7 = (f32[6,64,1024]{2,1,0:T(8,128)S(1)}, f32[6,64,1024]{2,1,0:T(8,128)S(1)}, bf16[6,64,1024]{2,1,0:T(8,128)(2,1)S(1)}, bf16[6,64,1024]{2,1,0:T(8,128)(2,1)S(1)}) custom-call(s32[24]{0:T(128)S(1)} %pad_add_fusion.3.refs_0_, s32[2]{0:T(128)S(1)} %pad_add_fusion.4.refs_1_, s32[24]{0:T(128)S(1)} %pad_add_fusion.5.refs_2_, ...), custom_call_target="tpu_custom_call" | custom-call | tf_op jit(solution)/shard_map/chunk/pallas_call | solution.py:278
  172.8 2.9 %collective-permute-done.30.across_ref = bf16[2,6,64,1024]{3,2,1,0:T(8,128)(2,1)S(1)} collective-permute-done((bf16[2,6,64,1024]{3,2,1,0:T(8,128)(2,1)S(1)}, bf16[2,6,64,1024]{3,2,1,0:T(8,128)(2,1)S(1)}, u32[]{:S(2)}, u32[]{:S(2)}) %collective-permute-start.30) | collective-permute-done | bytes 1572896 | tf_op jit(solution)/shard_map/ppermute | solution.py:375
  178.3 2.9 %finish.1 = (bf16[6,64,1024]{2,1,0:T(8,128)(2,1)}, bf16[6,64,1024]{2,1,0:T(8,128)(2,1)}, f32[6,64]{1,0:T(8,128)}) custom-call(s32[6]{0:T(128)S(1)} %bitcast.60, bf16[6,64,1024]{2,1,0:T(8,128)(2,1)S(1)} %copy-done.2, bf16[6,64,1024]{2,1,0:T(8,128)(2,1)S(1)} %copy-done.4, f32[2,1024]{1,0:T(2,128)S(1)} %copy-done.7, ...), custom_call_target="tpu_custom_call" | custom-call | tf_op jit(solution)/shard_map/finish/pallas_call | solution.py:328
  (110 shorter events, 38.0 us)
Async XLA Ops:
  8.0 11.1 %collective-permute-start.3 = (bf16[256,256]{1,0:T(8,128)(2,1)S(1)}, bf16[256,256]{1,0:T(8,128)(2,1)S(1)}, u32[]{:S(2)}, u32[]{:S(2)}) collective-permute-start(bf16[256,256]{1,0:T(8,128)(2,1)S(1)} %bitcast.69), channel_id=1, source_target_pairs={{0,4},{1,5},{2,6},{3,7},{4,8},{5,9},{6,10},{7,11},{8,12},{9,13},{1... | collective-permute-start | bytes 393224 | tf_op jit(solution)/shard_map/ppermute | solution.py:378
  9.7 11.5 %collective-permute-start.6 = (bf16[256,256]{1,0:T(8,128)(2,1)S(1)}, bf16[256,256]{1,0:T(8,128)(2,1)S(1)}, u32[]{:S(2)}, u32[]{:S(2)}) collective-permute-start(bf16[256,256]{1,0:T(8,128)(2,1)S(1)} %bitcast.70), channel_id=1, source_target_pairs={{0,8},{1,9},{2,10},{3,11},{4,12},{5,13},{6,14},{7,15},{8,0},{9,1},... | collective-permute-start | bytes 393224 | tf_op jit(solution)/shard_map/ppermute | solution.py:378
  10.9 12.0 %collective-permute-start.7 = (bf16[256,256]{1,0:T(8,128)(2,1)S(1)}, bf16[256,256]{1,0:T(8,128)(2,1)S(1)}, u32[]{:S(2)}, u32[]{:S(2)}) collective-permute-start(bf16[256,256]{1,0:T(8,128)(2,1)S(1)} %bitcast.71), channel_id=1, source_target_pairs={{0,12},{1,13},{2,14},{3,15},{4,0},{5,1},{6,2},{7,3},{8,4},{9,5},{1... | collective-permute-start | bytes 393224 | tf_op jit(solution)/shard_map/ppermute | solution.py:378
  12.7 10.3 %collective-permute-start.5 = (bf16[2,2,64,1152]{3,2,0,1:T(8,128)(2,1)S(1)}, bf16[2,2,64,1152]{3,2,0,1:T(8,128)(2,1)S(1)}, u32[]{:S(2)}, u32[]{:S(2)}) collective-permute-start(bf16[2,2,64,1152]{3,2,0,1:T(8,128)(2,1)S(1)} %pad_maximum_fusion.9), channel_id=1, source_target_pairs={{0,1},{1,0},{2,3},{3,2},{4,5},{5,4},{6,7},{7,6},{8,9},{9,8},{10,11... | collective-permute-start | bytes 1769480 | tf_op jit(solution)/shard_map/ppermute | solution.py:369
  19.9 35.8 %collective-permute-start.4 = (bf16[2,6,64,1024]{3,2,1,0:T(8,128)(2,1)S(1)}, bf16[2,6,64,1024]{3,2,1,0:T(8,128)(2,1)S(1)}, u32[]{:S(2)}, u32[]{:S(2)}) collective-permute-start(bf16[2,6,64,1024]{3,2,1,0:T(8,128)(2,1)S(1)} %get-tuple-element.46.refs_3_), channel_id=1, source_target_pairs={{0,16},{16,0},{1,17},{17,1},{2,18},{18,2},{3,19},{19,3},{4,20},{20... | collective-permute-start | bytes 4718600 | tf_op jit(solution)/shard_map/ppermute | solution.py:375
  23.7 26.0 %collective-permute-start.11 = (bf16[4,256,256]{2,1,0:T(8,128)(2,1)S(1)}, bf16[4,256,256]{2,1,0:T(8,128)(2,1)S(1)}, u32[]{:S(2)}, u32[]{:S(2)}) collective-permute-start(bf16[4,256,256]{2,1,0:T(8,128)(2,1)S(1)} %pad_maximum_fusion.10.refs_6_), channel_id=1, source_target_pairs={{0,2},{1,3},{2,0},{3,1},{4,6},{5,7},{6,4},{7,5},{8,10},{9,11},{10,... | collective-permute-start | bytes 1572872 | tf_op jit(solution)/shard_map/ppermute | solution.py:372
  25.5 20.5 %collective-permute-start.10 = (bf16[256,512]{1,0:T(8,128)(2,1)S(1)}, bf16[256,512]{1,0:T(8,128)(2,1)S(1)}, u32[]{:S(2)}, u32[]{:S(2)}) collective-permute-start(bf16[256,512]{1,0:T(8,128)(2,1)S(1)} %get-tuple-element.37), channel_id=1, source_target_pairs={{0,12},{1,13},{2,14},{3,15},{4,0},{5,1},{6,2},{7,3},{8,4},{9,5},{1... | collective-permute-start | bytes 786440 | tf_op jit(solution)/shard_map/ppermute | solution.py:378
  25.5 20.4 %collective-permute-start.8 = (bf16[256,512]{1,0:T(8,128)(2,1)S(1)}, bf16[256,512]{1,0:T(8,128)(2,1)S(1)}, u32[]{:S(2)}, u32[]{:S(2)}) collective-permute-start(bf16[256,512]{1,0:T(8,128)(2,1)S(1)} %get-tuple-element.37), channel_id=1, source_target_pairs={{0,4},{1,5},{2,6},{3,7},{4,8},{5,9},{6,10},{7,11},{8,12},{9,13},{1... | collective-permute-start | bytes 786440 | tf_op jit(solution)/shard_map/ppermute | solution.py:378
  27.5 22.0 %collective-permute-start.9 = (bf16[256,512]{1,0:T(8,128)(2,1)S(1)}, bf16[256,512]{1,0:T(8,128)(2,1)S(1)}, u32[]{:S(2)}, u32[]{:S(2)}) collective-permute-start(bf16[256,512]{1,0:T(8,128)(2,1)S(1)} %get-tuple-element.37), channel_id=1, source_target_pairs={{0,8},{1,9},{2,10},{3,11},{4,12},{5,13},{6,14},{7,15},{8,0},{9,1},... | collective-permute-start | bytes 786440 | tf_op jit(solution)/shard_map/ppermute | solution.py:378
  49.7 26.9 %collective-permute-start.15 = (bf16[4,256,512]{2,1,0:T(8,128)(2,1)S(1)}, bf16[4,256,512]{2,1,0:T(8,128)(2,1)S(1)}, u32[]{:S(2)}, u32[]{:S(2)}) collective-permute-start(bf16[4,256,512]{2,1,0:T(8,128)(2,1)S(1)} %pad_maximum_fusion.4.refs_8_), channel_id=1, source_target_pairs={{0,2},{1,3},{2,0},{3,1},{4,6},{5,7},{6,4},{7,5},{8,10},{9,11},{10,... | collective-permute-start | bytes 3145736 | tf_op jit(solution)/shard_map/ppermute | solution.py:372
  50.3 9.4 %collective-permute-start.12 = (bf16[256,512]{1,0:T(8,128)(2,1)S(1)}, bf16[256,512]{1,0:T(8,128)(2,1)S(1)}, u32[]{:S(2)}, u32[]{:S(2)}) collective-permute-start(bf16[256,512]{1,0:T(8,128)(2,1)S(1)} %get-tuple-element.39), channel_id=1, source_target_pairs={{0,4},{1,5},{2,6},{3,7},{4,8},{5,9},{6,10},{7,11},{8,12},{9,13},{1... | collective-permute-start | bytes 786440 | tf_op jit(solution)/shard_map/ppermute | solution.py:378
  50.6 22.2 %collective-permute-start.13 = (bf16[256,512]{1,0:T(8,128)(2,1)S(1)}, bf16[256,512]{1,0:T(8,128)(2,1)S(1)}, u32[]{:S(2)}, u32[]{:S(2)}) collective-permute-start(bf16[256,512]{1,0:T(8,128)(2,1)S(1)} %get-tuple-element.39), channel_id=1, source_target_pairs={{0,8},{1,9},{2,10},{3,11},{4,12},{5,13},{6,14},{7,15},{8,0},{9,1},... | collective-permute-start | bytes 786440 | tf_op jit(solution)/shard_map/ppermute | solution.py:378
  54.9 21.8 %collective-permute-start.14 = (bf16[256,512]{1,0:T(8,128)(2,1)S(1)}, bf16[256,512]{1,0:T(8,128)(2,1)S(1)}, u32[]{:S(2)}, u32[]{:S(2)}) collective-permute-start(bf16[256,512]{1,0:T(8,128)(2,1)S(1)} %get-tuple-element.39), channel_id=1, source_target_pairs={{0,12},{1,13},{2,14},{3,15},{4,0},{5,1},{6,2},{7,3},{8,4},{9,5},{1... | collective-permute-start | bytes 786440 | tf_op jit(solution)/shard_map/ppermute | solution.py:378
  76.7 25.9 %collective-permute-start.16 = (bf16[2,2,6,64,1024]{4,3,2,1,0:T(8,128)(2,1)S(1)}, bf16[2,2,6,64,1024]{4,3,2,1,0:T(8,128)(2,1)S(1)}, u32[]{:S(2)}, u32[]{:S(2)}) collective-permute-start(bf16[2,2,6,64,1024]{4,3,2,1,0:T(8,128)(2,1)S(1)} %pad_maximum_fusion), channel_id=1, source_target_pairs={{0,1},{1,0},{2,3},{3,2},{4,5},{5,4},{6,7},{7,6},{8,9},{9,8},{10,11... | collective-permute-start | bytes 9437192 | tf_op jit(solution)/shard_map/ppermute | solution.py:369
  76.8 25.8 %collective-permute-start.20 = (bf16[4,256,512]{2,1,0:T(8,128)(2,1)S(1)}, bf16[4,256,512]{2,1,0:T(8,128)(2,1)S(1)}, u32[]{:S(2)}, u32[]{:S(2)}) collective-permute-start(bf16[4,256,512]{2,1,0:T(8,128)(2,1)S(1)} %pad_maximum_fusion.5.refs_10_.refs_12_), channel_id=1, source_target_pairs={{0,2},{1,3},{2,0},{3,1},{4,6},{5,7},{6,4},{7,5},{8,10},{9,11},{10,... | collective-permute-start | bytes 3145736 | tf_op jit(solution)/shard_map/ppermute | solution.py:372
  78.4 9.1 %collective-permute-start.17 = (bf16[256,512]{1,0:T(8,128)(2,1)S(1)}, bf16[256,512]{1,0:T(8,128)(2,1)S(1)}, u32[]{:S(2)}, u32[]{:S(2)}) collective-permute-start(bf16[256,512]{1,0:T(8,128)(2,1)S(1)} %get-tuple-element.42), channel_id=1, source_target_pairs={{0,4},{1,5},{2,6},{3,7},{4,8},{5,9},{6,10},{7,11},{8,12},{9,13},{1... | collective-permute-start | bytes 786440 | tf_op jit(solution)/shard_map/ppermute | solution.py:378
  78.4 23.1 %collective-permute-start.18 = (bf16[256,512]{1,0:T(8,128)(2,1)S(1)}, bf16[256,512]{1,0:T(8,128)(2,1)S(1)}, u32[]{:S(2)}, u32[]{:S(2)}) collective-permute-start(bf16[256,512]{1,0:T(8,128)(2,1)S(1)} %get-tuple-element.42), channel_id=1, source_target_pairs={{0,8},{1,9},{2,10},{3,11},{4,12},{5,13},{6,14},{7,15},{8,0},{9,1},... | collective-permute-start | bytes 786440 | tf_op jit(solution)/shard_map/ppermute | solution.py:378
  79.0 23.5 %collective-permute-start.19 = (bf16[256,512]{1,0:T(8,128)(2,1)S(1)}, bf16[256,512]{1,0:T(8,128)(2,1)S(1)}, u32[]{:S(2)}, u32[]{:S(2)}) collective-permute-start(bf16[256,512]{1,0:T(8,128)(2,1)S(1)} %get-tuple-element.42), channel_id=1, source_target_pairs={{0,12},{1,13},{2,14},{3,15},{4,0},{5,1},{6,2},{7,3},{8,4},{9,5},{1... | collective-permute-start | bytes 786440 | tf_op jit(solution)/shard_map/ppermute | solution.py:378
  102.6 25.8 %collective-permute-start.24 = (bf16[4,256,512]{2,1,0:T(8,128)(2,1)S(1)}, bf16[4,256,512]{2,1,0:T(8,128)(2,1)S(1)}, u32[]{:S(2)}, u32[]{:S(2)}) collective-permute-start(bf16[4,256,512]{2,1,0:T(8,128)(2,1)S(1)} %pad_maximum_fusion.7.refs_5_), channel_id=1, source_target_pairs={{0,2},{1,3},{2,0},{3,1},{4,6},{5,7},{6,4},{7,5},{8,10},{9,11},{10,... | collective-permute-start | bytes 3145736 | tf_op jit(solution)/shard_map/ppermute | solution.py:372
  104.2 22.1 %collective-permute-start.21 = (bf16[256,512]{1,0:T(8,128)(2,1)S(1)}, bf16[256,512]{1,0:T(8,128)(2,1)S(1)}, u32[]{:S(2)}, u32[]{:S(2)}) collective-permute-start(bf16[256,512]{1,0:T(8,128)(2,1)S(1)} %get-tuple-element.44), channel_id=1, source_target_pairs={{0,4},{1,5},{2,6},{3,7},{4,8},{5,9},{6,10},{7,11},{8,12},{9,13},{1... | collective-permute-start | bytes 786440 | tf_op jit(solution)/shard_map/ppermute | solution.py:378
  104.2 22.6 %collective-permute-start.22 = (bf16[256,512]{1,0:T(8,128)(2,1)S(1)}, bf16[256,512]{1,0:T(8,128)(2,1)S(1)}, u32[]{:S(2)}, u32[]{:S(2)}) collective-permute-start(bf16[256,512]{1,0:T(8,128)(2,1)S(1)} %get-tuple-element.44), channel_id=1, source_target_pairs={{0,8},{1,9},{2,10},{3,11},{4,12},{5,13},{6,14},{7,15},{8,0},{9,1},... | collective-permute-start | bytes 786440 | tf_op jit(solution)/shard_map/ppermute | solution.py:378
  105.6 22.8 %collective-permute-start.23 = (bf16[256,512]{1,0:T(8,128)(2,1)S(1)}, bf16[256,512]{1,0:T(8,128)(2,1)S(1)}, u32[]{:S(2)}, u32[]{:S(2)}) collective-permute-start(bf16[256,512]{1,0:T(8,128)(2,1)S(1)} %get-tuple-element.44), channel_id=1, source_target_pairs={{0,12},{1,13},{2,14},{3,15},{4,0},{5,1},{6,2},{7,3},{8,4},{9,5},{1... | collective-permute-start | bytes 786440 | tf_op jit(solution)/shard_map/ppermute | solution.py:378
  135.7 26.5 %collective-permute-start.25 = (bf16[4,256,512]{2,1,0:T(8,128)(2,1)S(1)}, bf16[4,256,512]{2,1,0:T(8,128)(2,1)S(1)}, u32[]{:S(2)}, u32[]{:S(2)}) collective-permute-start(bf16[4,256,512]{2,1,0:T(8,128)(2,1)S(1)} %pad_maximum_fusion.6.refs_5_.refs_7_), channel_id=1, source_target_pairs={{0,2},{1,3},{2,0},{3,1},{4,6},{5,7},{6,4},{7,5},{8,10},{9,11},{10,... | collective-permute-start | bytes 3145736 | tf_op jit(solution)/shard_map/ppermute | solution.py:372
  139.6 36.2 %collective-permute-start.30 = (bf16[2,6,64,1024]{3,2,1,0:T(8,128)(2,1)S(1)}, bf16[2,6,64,1024]{3,2,1,0:T(8,128)(2,1)S(1)}, u32[]{:S(2)}, u32[]{:S(2)}) collective-permute-start(bf16[2,6,64,1024]{3,2,1,0:T(8,128)(2,1)S(1)} %pad_maximum_fusion.2), channel_id=1, source_target_pairs={{0,16},{16,0},{1,17},{17,1},{2,18},{18,2},{3,19},{19,3},{4,20},{20... | collective-permute-start | bytes 4718600 | tf_op jit(solution)/shard_map/ppermute | solution.py:375
  (20 other events, 89.7 us)

commit v12 on v11

--- a/solution.py
+++ b/solution.py
@@ -296,19 +296,31 @@
     )(*args)
 
 
-def finish_kernel(
-    member_ref, x_ref, g_ref, gain_ref, out_ref, back_ref, other_out_ref, other_back_ref,
-    across_ref, value_ref, grad_ref, coupling_ref,
-):
-    rows, seq, width = x_ref.shape
+def finish_kernel(member_ref, gain_ref, *refs):
+    sources, (value_ref, grad_ref, coupling_ref), buffers, sems = (
+        refs[:7], refs[7:10], refs[10:17], refs[17]
+    )
+    rows, seq, width = value_ref.shape
+    copies = []
+    for r in range(rows):
+        for i, (source, buffer) in enumerate(zip(sources, buffers)):
+            at = (slice(None), r) if len(source.shape) == 4 else (r,)
+            copies.append(
+                pltpu.make_async_copy(source.at[at], buffer.at[at], sems.at[i, r])
+            )
+    for copy in copies:
+        copy.start()
+    x_ref, g_ref, out_ref, back_ref, other_out_ref, other_back_ref, across_ref = buffers
     diagonal = lax.broadcasted_iota(jnp.int32, (seq, seq), 0) == lax.broadcasted_iota(
         jnp.int32, (seq, seq), 1
     )
     for r in range(rows):
+        for copy in copies[7 * r : 7 * r + 7]:
+            copy.wait()
         x = x_ref[r].astype(F32)
         inv = 1.0 / jnp.sqrt(jnp.mean(x * x, axis=1, keepdims=True) + 1e-06)
         normed = x * inv
-        gain = gain_ref[pl.ds(member_ref[pl.program_id(0) * rows + r], 1), :]
+        gain = gain_ref[pl.ds(member_ref[r], 1), :]
         back = gain * (
             back_ref[r] + other_back_ref[r].astype(F32) + across_ref[1, r].astype(F32)
         )
@@ -317,32 +329,27 @@
         value_ref[r] = (x + out).astype(BF16)
         grad_ref[r] = (g_ref[r].astype(F32) + (back - normed * stat) * inv).astype(BF16)
         line = jnp.sum(jnp.where(diagonal, stat, 0.0), axis=0, keepdims=True)
-        coupling_ref[pl.ds(pl.program_id(0) * rows + r, 1), :] = line * math.sqrt(width)
-
-
-def finish(member_own, x, g, gain, *sums):
-    rows, seq, width = x.shape
-    step = math.gcd(rows, 2)
-    row = pl.BlockSpec((step, seq, width), lambda r, mem: (r, 0, 0))
-    two = pl.BlockSpec((2, step, seq, width), lambda r, mem: (0, r, 0, 0))
+        coupling_ref[pl.ds(r, 1), :] = line * math.sqrt(width)
+
+
+def finish(member_own, gain, *sources):
+    rows, seq, width = sources[0].shape
+    vmem = pl.BlockSpec(memory_space=pltpu.VMEM)
     return pl.pallas_call(
         finish_kernel,
-        grid_spec=pltpu.PrefetchScalarGridSpec(
-            num_scalar_prefetch=1,
-            grid=(rows // step,),
-            in_specs=[
-                row, row, pl.BlockSpec(gain.shape, lambda r, mem: (0, 0)), row, row, row, row, two
-            ],
-            out_specs=[row, row, pl.BlockSpec((rows, seq), lambda r, mem: (0, 0))],
-        ),
+        in_specs=[pl.BlockSpec(memory_space=pltpu.SMEM), vmem]
+        + [pl.BlockSpec(memory_space=pl.ANY)] * 7,
+        out_specs=[vmem] * 3,
         out_shape=[
             jax.ShapeDtypeStruct((rows, seq, width), BF16),
             jax.ShapeDtypeStruct((rows, seq, width), BF16),
             jax.ShapeDtypeStruct((rows, seq), F32),
         ],
-        compiler_params=pltpu.CompilerParams(vmem_limit_bytes=VMEM_LIMIT),
+        scratch_shapes=[pltpu.VMEM(a.shape, a.dtype) for a in sources]
+        + [pltpu.SemaphoreType.DMA((7, rows))],
+        compiler_params=pltpu.CompilerParams(vmem_limit_bytes=VMEM_LIMIT // 2),
         name="finish",
-    )(member_own, x, g, gain, *sums)
+    )(member_own, gain, *sources)
 
 
 def sort_rows(picks):
@@ -393,8 +400,6 @@
             axis=3,
         )
 
-    pick_own = member_pick[:, 0]
-    pick_near = jnp.concatenate([pick_own, over_x(pick_own)])
     def both_cores(mine, theirs):
         even = core == 0
         whole = jnp.concatenate(
@@ -402,12 +407,17 @@
         )
         return whole.reshape(mine.shape[0], 4 * depth, mine.shape[3])
 
-    mine, given = units_of(core), units_of(1 - core)
-    head = 2 * unit
-    head_theirs = after(partner(given[:1, :, :, :head]), pick_near)
-    shard_head = both_cores(mine[:1, :, :, :head], head_theirs)
-    theirs = partner(after(given, head_theirs))
-    shard = both_cores(mine, theirs)
+    def head_of(c):
+        at = (2 * x_at + c) * quarter
+        return jnp.stack(
+            [lax.dynamic_slice(a, (0, 0, at), (1, depth, 2 * unit)) for a in (up_proj, down_proj)],
+            axis=1,
+        )
+
+    head_theirs = partner(head_of(1 - core))
+    shard_head = both_cores(head_of(core), head_theirs)
+    theirs = partner(after(units_of(1 - core), head_theirs))
+    shard = both_cores(units_of(core), theirs)
 
     groups = [
         [(0, 0, 2 * unit)],
@@ -420,19 +430,20 @@
         jnp.concatenate([shard[m, :, at : at + n] for m, at, n in group], axis=1)
         for group in groups[1:]
     ]
-    here, there = [], []
-
-    def exchange(step, arrived):
+    here, there, shifted = [], [], []
+
+    def along_z(step, *waits):
         results = []
-        if step < len(groups):
-            mine = after(send[step], *arrived)
-            results += [shift_z(mine, d) for d in range(1, lines)]
-        if step > 0:
-            there.append(over_y(after(here[step - 1], *arrived)))
-            results.append(there[-1])
-        if step < len(groups):
-            here.append(jnp.stack([send[step], *results[: lines - 1]]))
-        return results
+        for d in range(1, lines):
+            mine = send[step]
+            if step:
+                mine = after(mine, *shifted[-1], *waits)
+            results.append(shift_z(mine, d))
+        shifted.append(results)
+        here.append(jnp.stack([send[step], *results]))
+
+    def across_y(step, *waits):
+        there.append(over_y(after(here[step], *there[-1:], *waits)))
 
     def chunk_pieces(*at):
         pieces = []
@@ -445,17 +456,19 @@
 
     per_block = math.gcd(2 * rows, 4)
     per_chip = 2 * rows // per_block
-    pick_far = partner(after(pick_near, head_theirs))
-
-    arrived = exchange(0, [])
-    x = after(tokens_in, arrived[0]).astype(F32)
+    along_z(0)
+    pick_own = member_pick[:, 0]
+    pick_near = jnp.concatenate([pick_own, over_x(after(pick_own, send[0]))])
+    x = after(tokens_in, shifted[0][0]).astype(F32)
     gain = jnp.zeros((rows, width), F32)
     for member in range(members):
         gain = jnp.where(pick_own[:, None] == member, norm_gain[member][None, :], gain)
     normed = x * (1.0 / jnp.sqrt(jnp.mean(x * x, axis=2, keepdims=True) + 1e-06))
     near = jnp.stack([(normed * gain[:, None, :]).astype(BF16), upstream])
     over = over_x(near)
-    arrived += [pick_far, *send[1:]]
+    along_z(1, pick_near, *send[2:])
+    across_y(0)
+    pick_far = partner(after(pick_near, shifted[0][-1]))
 
     perm, member_sorted = sort_rows(jnp.concatenate([pick_near[rows:], pick_far[rows:]]))
     perm_own, member_sorted_own = sort_rows(jnp.concatenate([pick_own, pick_far[:rows]]))
@@ -465,27 +478,20 @@
         jnp.concatenate([perm + 2 * rows, perm_own]),
     )
 
-    arrived = exchange(1, arrived)
-    arrived += [*scalars]
-
-    arrived = exchange(2, arrived)
-    arrived += [over]
-
-    set_2, arrived = arrived, exchange(3, arrived)
-    far = partner(after(jnp.stack([near, over]), *set_2))
-    arrived += [far]
+    along_z(2, there[0], *scalars)
+    across_y(1)
+    along_z(3, there[1], over)
+    across_y(2)
+    far = partner(after(jnp.stack([near, over]), *shifted[2], there[1]))
+    along_z(4, there[2], far)
+    across_y(3)
     tokens_of = (near, over, far)
-
-    set_3, arrived = arrived, exchange(4, arrived)
     sums = chunk(
         (True, False), (0, 2 * per_chip, per_block), (0, 1), scalars,
-        (after(near, *set_3), over, far), chunk_pieces(0, 1, 2), None,
-    )
-    arrived += [sums[0]]
-
-    set_4 = arrived
-    exchange(5, arrived)
-    sums = (after(sums[0], *set_4), sums[1])
+        (after(near, *shifted[3]), over, far), chunk_pieces(0, 1, 2), None,
+    )
+    across_y(4)
+    sums = (after(sums[0], *shifted[4]), sums[1])
     *same, other_out, other_back = chunk(
         (False, True), (0, per_chip, per_block), (1,), scalars, tokens_of, chunk_pieces(3), sums,
         (BF16, BF16), 0,
@@ -505,7 +511,7 @@
     )
     return tuple(
         finish(
-            pick_own, tokens_in, upstream, norm_gain, out, back,
+            pick_own, norm_gain, tokens_in, upstream, out, back,
             partner(packed_out), partner(packed_back), across,
         )
     )

time: 183 us -> 189 us (1.033)
  Pallas kernels: 42.2 us -> 48.8 us
  waiting for transfers between devices: 86.4 us -> 89.7 us
  starting transfers between devices: 34.3 us -> 32 us
  local copies, waits for them, and re-layouts: 8.42 us -> 6.5 us
    ppermute x3, waiting for transfers between devices: 2.94 us -> 8.67 us  [over_x(): return lax.ppermute(a, 'grp', [(0, 1), (1, 0)])]
    pallas_call x1, Pallas kernels: 2.91 us -> 7.79 us  [finish(): pl.pallas_call(finish_kernel, in_specs=[pl.BlockSpec(memory_space=pltpu.S...]
    unnamed x26 -> x18, local copies, waits for them, and re-layouts: 8.11 us -> 3.87 us
    ppermute x5, starting transfers between devices: 8.38 us -> 4.63 us  [over_y(): return lax.ppermute(a, 'row', [(i, i ^ 2) for i in range(ranks)])]
    ppermute x15, waiting for transfers between devices: 68 us -> 64.3 us  [shift_z(): lax.ppermute(a, 'row', [(i, (i + 4 * d) % ranks) for i in range(ranks)])]
  transfers between devices with their start and end apart: 31 -> 31, of which waited for: 18 -> 22; matrix products, arithmetic and copies ran while one was open for 4% -> 4% of each run, Pallas kernels for 18% -> 19%
where the time goes in v12:
time: 189 us; the launch traced here: 186 us
  waiting for transfers between devices  89.7 us (47%)
  Pallas kernels  48.8 us (26%)
  starting transfers between devices  32 us (17%)
  other arithmetic  8.28 us (4%)
  local copies, waits for them, and re-layouts  6.5 us (3%)
    ppermute x15, waiting for transfers between devices, shift_z(): lax.ppermute(a, 'row', [(i, (i + 4 * d) % ranks) for i in range(ranks)])  64.3 us
    pallas_call x4, Pallas kernels, chunk(): pl.pallas_call(kernel, grid_spec=pltpu.PrefetchScalarGridSpec(num_scalar_...  41 us
    ppermute x15, starting transfers between devices, shift_z(): lax.ppermute(a, 'row', [(i, (i + 4 * d) % ranks) for i in range(ranks)])  22.1 us
    ppermute x5, waiting for transfers between devices, over_y(): return lax.ppermute(a, 'row', [(i, i ^ 2) for i in range(ranks)])  12.3 us
    ppermute x3, waiting for transfers between devices, over_x(): return lax.ppermute(a, 'grp', [(0, 1), (1, 0)])  8.67 us
    pallas_call x1, Pallas kernels, finish(): pl.pallas_call(finish_kernel, in_specs=[pl.BlockSpec(memory_space=pltpu.S...  7.79 us
    ppermute x5, starting transfers between devices, over_y(): return lax.ppermute(a, 'row', [(i, i ^ 2) for i in range(ranks)])  4.63 us
    ppermute x8, waiting for transfers between devices, partner(): return lax.ppermute(a, 'row', [(i, i ^ 1) for i in range(ranks)])  4.45 us
  transfers between devices with their start and end apart: 31, of which 22 were waited for; matrix products, arithmetic and copies ran while one was open for 4% of the time, Pallas kernels for 19%

profile of v12, /device:TPU:8, one launch (start us, length us, event | category | flops | bytes accessed | tf_op | source)
XLA Modules:
  0.0 186.4 jit_solution(3054345235146869233)
XLA Ops:
  4.3 2.1 %fusion.6 = (bf16[2,2,64,896]{3,2,0,1:T(8,128)(2,1)S(1)}, bf16[2,2,64,896]{3,2,0,1:T(8,128)(2,1)}) fusion(s32[]{:T(128)S(6)} %select_n.77, bf16[2,1,64,4096]{3,2,0,1:T(8,128)(2,1)} %bitcast.69, bf16[2,1,64,4096]{3,2,0,1:T(8,128)(2,1)} %bitcast.71, s32[]{:T(128)S(6)} %select_n.78), kind=kLoop, calls=%fused_computation.31 | loop fusion | flops 1835008 | bytes 3014664 | tf_op jit(solution)/shard_map/stack | solution.py:392
  10.6 4.4 %collective-permute-start.7 = (bf16[256,256]{1,0:T(8,128)(2,1)S(1)}, bf16[256,256]{1,0:T(8,128)(2,1)S(1)}, u32[]{:S(2)}, u32[]{:S(2)}) collective-permute-start(bf16[256,256]{1,0:T(8,128)(2,1)S(1)} %bitcast.79), channel_id=1, source_target_pairs={{0,8},{1,9},{2,10},{3,11},{4,12},{5,13},{6,14},{7,15},{8,0},{9,1},... | collective-permute-start | bytes 393224 | tf_op jit(solution)/shard_map/ppermute | solution.py:385
  16.6 2.0 %collective-permute-done.1 = s32[6]{0:T(128)S(1)} collective-permute-done((s32[6]{0:T(128)S(1)}, s32[6]{0:T(128)S(1)}, u32[]{:S(2)}, u32[]{:S(2)}) %collective-permute-start.1) | collective-permute-done | bytes 56 | tf_op jit(solution)/shard_map/ppermute | solution.py:382
  19.7 2.4 %collective-permute-done.7 = bf16[256,256]{1,0:T(8,128)(2,1)S(1)} collective-permute-done((bf16[256,256]{1,0:T(8,128)(2,1)S(1)}, bf16[256,256]{1,0:T(8,128)(2,1)S(1)}, u32[]{:S(2)}, u32[]{:S(2)}) %collective-permute-start.7) | collective-permute-done | bytes 131104 | tf_op jit(solution)/shard_map/ppermute | solution.py:385
  28.4 3.4 %collective-permute-start.9 = (bf16[256,512]{1,0:T(8,128)(2,1)S(1)}, bf16[256,512]{1,0:T(8,128)(2,1)S(1)}, u32[]{:S(2)}, u32[]{:S(2)}) collective-permute-start(bf16[256,512]{1,0:T(8,128)(2,1)S(1)} %get-tuple-element.36), channel_id=1, source_target_pairs={{0,8},{1,9},{2,10},{3,11},{4,12},{5,13},{6,14},{7,15},{8,0},{9,1},... | collective-permute-start | bytes 786440 | tf_op jit(solution)/shard_map/ppermute | solution.py:385
  32.6 3.9 %collective-permute-done.8 = bf16[256,512]{1,0:T(8,128)(2,1)S(1)} collective-permute-done((bf16[256,512]{1,0:T(8,128)(2,1)S(1)}, bf16[256,512]{1,0:T(8,128)(2,1)S(1)}, u32[]{:S(2)}, u32[]{:S(2)}) %collective-permute-start.8) | collective-permute-done | bytes 262176 | tf_op jit(solution)/shard_map/ppermute | solution.py:385
  36.6 14.7 %collective-permute-done.9 = bf16[256,512]{1,0:T(8,128)(2,1)S(1)} collective-permute-done((bf16[256,512]{1,0:T(8,128)(2,1)S(1)}, bf16[256,512]{1,0:T(8,128)(2,1)S(1)}, u32[]{:S(2)}, u32[]{:S(2)}) %collective-permute-start.9) | collective-permute-done | bytes 262176 | tf_op jit(solution)/shard_map/ppermute | solution.py:385
  51.2 3.1 %collective-permute-done.10 = bf16[256,512]{1,0:T(8,128)(2,1)S(1)} collective-permute-done((bf16[256,512]{1,0:T(8,128)(2,1)S(1)}, bf16[256,512]{1,0:T(8,128)(2,1)S(1)}, u32[]{:S(2)}, u32[]{:S(2)}) %collective-permute-start.10) | collective-permute-done | bytes 262176 | tf_op jit(solution)/shard_map/ppermute | solution.py:385
  58.0 3.5 %collective-permute-done.5.refs_4_.refs_3_ = bf16[2,6,64,1024]{3,2,1,0:T(8,128)(2,1)S(1)} collective-permute-done((bf16[2,6,64,1024]{3,2,1,0:T(8,128)(2,1)S(1)}, bf16[2,6,64,1024]{3,2,1,0:T(8,128)(2,1)S(1)}, u32[]{:S(2)}, u32[]{:S(2)}) %collective-permute-start.5) | collective-permute-done | bytes 1572896 | tf_op jit(solution)/shard_map/ppermute | solution.py:382
  61.7 3.2 %collective-permute-done.12 = bf16[256,512]{1,0:T(8,128)(2,1)S(1)} collective-permute-done((bf16[256,512]{1,0:T(8,128)(2,1)S(1)}, bf16[256,512]{1,0:T(8,128)(2,1)S(1)}, u32[]{:S(2)}, u32[]{:S(2)}) %collective-permute-start.12) | collective-permute-done | bytes 262176 | tf_op jit(solution)/shard_map/ppermute | solution.py:385
  64.9 12.8 %collective-permute-done.13 = bf16[256,512]{1,0:T(8,128)(2,1)S(1)} collective-permute-done((bf16[256,512]{1,0:T(8,128)(2,1)S(1)}, bf16[256,512]{1,0:T(8,128)(2,1)S(1)}, u32[]{:S(2)}, u32[]{:S(2)}) %collective-permute-start.13) | collective-permute-done | bytes 262176 | tf_op jit(solution)/shard_map/ppermute | solution.py:385
  80.2 2.6 %collective-permute-start.18 = (bf16[256,512]{1,0:T(8,128)(2,1)S(1)}, bf16[256,512]{1,0:T(8,128)(2,1)S(1)}, u32[]{:S(2)}, u32[]{:S(2)}) collective-permute-start(bf16[256,512]{1,0:T(8,128)(2,1)S(1)} %get-tuple-element.40), channel_id=1, source_target_pairs={{0,8},{1,9},{2,10},{3,11},{4,12},{5,13},{6,14},{7,15},{8,0},{9,1},... | collective-permute-start | bytes 786440 | tf_op jit(solution)/shard_map/ppermute | solution.py:385
  82.7 2.0 %collective-permute-start.19 = (bf16[256,512]{1,0:T(8,128)(2,1)S(1)}, bf16[256,512]{1,0:T(8,128)(2,1)S(1)}, u32[]{:S(2)}, u32[]{:S(2)}) collective-permute-start(bf16[256,512]{1,0:T(8,128)(2,1)S(1)} %get-tuple-element.40), channel_id=1, source_target_pairs={{0,12},{1,13},{2,14},{3,15},{4,0},{5,1},{6,2},{7,3},{8,4},{9,5},{1... | collective-permute-start | bytes 786440 | tf_op jit(solution)/shard_map/ppermute | solution.py:385
  84.8 4.5 %collective-permute-done.17 = bf16[256,512]{1,0:T(8,128)(2,1)S(1)} collective-permute-done((bf16[256,512]{1,0:T(8,128)(2,1)S(1)}, bf16[256,512]{1,0:T(8,128)(2,1)S(1)}, u32[]{:S(2)}, u32[]{:S(2)}) %collective-permute-start.17) | collective-permute-done | bytes 262176 | tf_op jit(solution)/shard_map/ppermute | solution.py:385
  89.3 13.9 %collective-permute-done.18 = bf16[256,512]{1,0:T(8,128)(2,1)S(1)} collective-permute-done((bf16[256,512]{1,0:T(8,128)(2,1)S(1)}, bf16[256,512]{1,0:T(8,128)(2,1)S(1)}, u32[]{:S(2)}, u32[]{:S(2)}) %collective-permute-start.18) | collective-permute-done | bytes 262176 | tf_op jit(solution)/shard_map/ppermute | solution.py:385
  103.2 3.1 %collective-permute-done.19 = bf16[256,512]{1,0:T(8,128)(2,1)S(1)} collective-permute-done((bf16[256,512]{1,0:T(8,128)(2,1)S(1)}, bf16[256,512]{1,0:T(8,128)(2,1)S(1)}, u32[]{:S(2)}, u32[]{:S(2)}) %collective-permute-start.19) | collective-permute-done | bytes 262176 | tf_op jit(solution)/shard_map/ppermute | solution.py:385
  110.3 19.8 %chunk.4 = (f32[1536,1024]{1,0:T(8,128)}, f32[1536,1024]{1,0:T(8,128)}) custom-call(s32[24]{0:T(128)S(1)} %pad_add_fusion.3.refs_0_, s32[2]{0:T(128)S(1)} %pad_add_fusion.4.refs_1_, s32[24]{0:T(128)S(1)} %pad_add_fusion.5.refs_2_, bf16[2,6,64,1024]{3,2,1,0:T(8,128)(2,1)S(1)} %get-tuple-element.45.refs_3_, ...), custom_call_target="tpu_custom_call" | custom-call | flops 10737418240 | bytes 36700160 | tf_op jit(solution)/shard_map/chunk/pallas_call | solution.py:278
  131.6 6.3 %chunk.5 = (bf16[6,64,1024]{2,1,0:T(8,128)(2,1)S(1)}, bf16[6,64,1024]{2,1,0:T(8,128)(2,1)S(1)}, bf16[6,64,1024]{2,1,0:T(8,128)(2,1)S(1)}, bf16[6,64,1024]{2,1,0:T(8,128)(2,1)S(1)}) custom-call(s32[24]{0:T(128)S(1)} %pad_add_fusion.3.refs_0_, s32[2]{0:T(128)S(1)} %pad_add_fusion.4.refs_1_, s32[24]{0:T(128)S(1)} %pad_add_fusion.5.refs_2_, ...), custom_call_target="tpu_custom_call" | custom-call | tf_op jit(solution)/shard_map/chunk/pallas_call | solution.py:278
  143.0 6.9 %chunk.6 = (f32[1536,1024]{1,0:T(8,128)S(1)}, f32[1536,1024]{1,0:T(8,128)}) custom-call(s32[24]{0:T(128)S(1)} %pad_add_fusion.3.refs_0_, s32[2]{0:T(128)S(1)} %pad_add_fusion.4.refs_1_, s32[24]{0:T(128)S(1)} %pad_add_fusion.5.refs_2_, bf16[2,6,64,1024]{3,2,1,0:T(8,128)(2,1)S(1)} %get-tuple-element.45.refs_3_, ...), custom_call_target="tpu_custom_call", output_to_operand_aliasing={{0}: (7, {}), {1}: (8, {})} | custom-call | tf_op jit(solution)/shard_map/chunk/pallas_call | solution.py:278
  150.0 2.6 %copy-done.1 = f32[1536,1024]{1,0:T(8,128)} copy-done((f32[1536,1024]{1,0:T(8,128)}, f32[1536,1024]{1,0:T(8,128)S(1)}, u32[]{:S(2)}) %copy-start.1) | copy-done | bytes 6291480
  152.6 11.2 %collective-permute-done.25.refs_6_.refs_8_ = bf16[4,256,512]{2,1,0:T(8,128)(2,1)S(1)} collective-permute-done((bf16[4,256,512]{2,1,0:T(8,128)(2,1)S(1)}, bf16[4,256,512]{2,1,0:T(8,128)(2,1)S(1)}, u32[]{:S(2)}, u32[]{:S(2)}) %collective-permute-start.25) | collective-permute-done | bytes 1048608 | tf_op jit(solution)/shard_map/ppermute | solution.py:379
  163.8 8.0 %chunk.7 = (f32[6,64,1024]{2,1,0:T(8,128)S(1)}, f32[6,64,1024]{2,1,0:T(8,128)S(1)}, bf16[6,64,1024]{2,1,0:T(8,128)(2,1)S(1)}, bf16[6,64,1024]{2,1,0:T(8,128)(2,1)S(1)}) custom-call(s32[24]{0:T(128)S(1)} %pad_add_fusion.3.refs_0_, s32[2]{0:T(128)S(1)} %pad_add_fusion.4.refs_1_, s32[24]{0:T(128)S(1)} %pad_add_fusion.5.refs_2_, ...), custom_call_target="tpu_custom_call" | custom-call | tf_op jit(solution)/shard_map/chunk/pallas_call | solution.py:278
  175.3 3.2 %collective-permute-done.30.refs_6_ = bf16[2,6,64,1024]{3,2,1,0:T(8,128)(2,1)} collective-permute-done((bf16[2,6,64,1024]{3,2,1,0:T(8,128)(2,1)S(1)}, bf16[2,6,64,1024]{3,2,1,0:T(8,128)(2,1)}, u32[]{:S(2)}, u32[]{:S(2)}) %collective-permute-start.30) | collective-permute-done | bytes 1572896 | tf_op jit(solution)/shard_map/ppermute | solution.py:382
  178.5 7.8 %finish.1 = (bf16[6,64,1024]{2,1,0:T(8,128)(2,1)}, bf16[6,64,1024]{2,1,0:T(8,128)(2,1)}, f32[6,64]{1,0:T(8,128)}) custom-call(s32[6]{0:T(128)S(1)} %bitcast.68, f32[2,1024]{1,0:T(2,128)S(1)} %copy-done.4, bf16[6,64,1024]{2,1,0:T(8,128)(2,1)S(1)} %copy-done.2, bf16[6,64,1024]{2,1,0:T(8,128)(2,1)S(1)} %copy-done.3, ...), custom_call_target="tpu_custom_call" | custom-call | tf_op jit(solution)/shard_map/finish/pallas_call | solution.py:338
  (105 shorter events, 37.8 us)
Async XLA Ops:
  8.5 10.2 %collective-permute-start.2 = (bf16[256,256]{1,0:T(8,128)(2,1)S(1)}, bf16[256,256]{1,0:T(8,128)(2,1)S(1)}, u32[]{:S(2)}, u32[]{:S(2)}) collective-permute-start(bf16[256,256]{1,0:T(8,128)(2,1)S(1)} %bitcast.77), channel_id=1, source_target_pairs={{0,12},{1,13},{2,14},{3,15},{4,0},{5,1},{6,2},{7,3},{8,4},{9,5},{1... | collective-permute-start | bytes 393224 | tf_op jit(solution)/shard_map/ppermute | solution.py:385
  8.6 11.2 %collective-permute-start.4 = (bf16[256,256]{1,0:T(8,128)(2,1)S(1)}, bf16[256,256]{1,0:T(8,128)(2,1)S(1)}, u32[]{:S(2)}, u32[]{:S(2)}) collective-permute-start(bf16[256,256]{1,0:T(8,128)(2,1)S(1)} %bitcast.78), channel_id=1, source_target_pairs={{0,4},{1,5},{2,6},{3,7},{4,8},{5,9},{6,10},{7,11},{8,12},{9,13},{1... | collective-permute-start | bytes 393224 | tf_op jit(solution)/shard_map/ppermute | solution.py:385
  10.6 11.6 %collective-permute-start.7 = (bf16[256,256]{1,0:T(8,128)(2,1)S(1)}, bf16[256,256]{1,0:T(8,128)(2,1)S(1)}, u32[]{:S(2)}, u32[]{:S(2)}) collective-permute-start(bf16[256,256]{1,0:T(8,128)(2,1)S(1)} %bitcast.79), channel_id=1, source_target_pairs={{0,8},{1,9},{2,10},{3,11},{4,12},{5,13},{6,14},{7,15},{8,0},{9,1},... | collective-permute-start | bytes 393224 | tf_op jit(solution)/shard_map/ppermute | solution.py:385
  15.0 11.1 %collective-permute-start.6 = (bf16[2,2,64,1152]{3,2,0,1:T(8,128)(2,1)S(1)}, bf16[2,2,64,1152]{3,2,0,1:T(8,128)(2,1)S(1)}, u32[]{:S(2)}, u32[]{:S(2)}) collective-permute-start(bf16[2,2,64,1152]{3,2,0,1:T(8,128)(2,1)S(1)} %pad_maximum_fusion.9), channel_id=1, source_target_pairs={{0,1},{1,0},{2,3},{3,2},{4,5},{5,4},{6,7},{7,6},{8,9},{9,8},{10,11... | collective-permute-start | bytes 1769480 | tf_op jit(solution)/shard_map/ppermute | solution.py:376
  22.2 32.3 %collective-permute-start.11 = (bf16[4,256,256]{2,1,0:T(8,128)(2,1)S(1)}, bf16[4,256,256]{2,1,0:T(8,128)(2,1)S(1)}, u32[]{:S(2)}, u32[]{:S(2)}) collective-permute-start(bf16[4,256,256]{2,1,0:T(8,128)(2,1)S(1)} %pad_maximum_fusion.10.refs_6_), channel_id=1, source_target_pairs={{0,2},{1,3},{2,0},{3,1},{4,6},{5,7},{6,4},{7,5},{8,10},{9,11},{10,... | collective-permute-start | bytes 1572872 | tf_op jit(solution)/shard_map/ppermute | solution.py:379
  24.5 36.9 %collective-permute-start.5 = (bf16[2,6,64,1024]{3,2,1,0:T(8,128)(2,1)S(1)}, bf16[2,6,64,1024]{3,2,1,0:T(8,128)(2,1)S(1)}, u32[]{:S(2)}, u32[]{:S(2)}) collective-permute-start(bf16[2,6,64,1024]{3,2,1,0:T(8,128)(2,1)S(1)} %get-tuple-element.45.refs_3_), channel_id=1, source_target_pairs={{0,16},{16,0},{1,17},{17,1},{2,18},{18,2},{3,19},{19,3},{4,20},{20... | collective-permute-start | bytes 4718600 | tf_op jit(solution)/shard_map/ppermute | solution.py:382
  26.8 9.7 %collective-permute-start.8 = (bf16[256,512]{1,0:T(8,128)(2,1)S(1)}, bf16[256,512]{1,0:T(8,128)(2,1)S(1)}, u32[]{:S(2)}, u32[]{:S(2)}) collective-permute-start(bf16[256,512]{1,0:T(8,128)(2,1)S(1)} %get-tuple-element.36), channel_id=1, source_target_pairs={{0,4},{1,5},{2,6},{3,7},{4,8},{5,9},{6,10},{7,11},{8,12},{9,13},{1... | collective-permute-start | bytes 786440 | tf_op jit(solution)/shard_map/ppermute | solution.py:385
  28.4 22.8 %collective-permute-start.9 = (bf16[256,512]{1,0:T(8,128)(2,1)S(1)}, bf16[256,512]{1,0:T(8,128)(2,1)S(1)}, u32[]{:S(2)}, u32[]{:S(2)}) collective-permute-start(bf16[256,512]{1,0:T(8,128)(2,1)S(1)} %get-tuple-element.36), channel_id=1, source_target_pairs={{0,8},{1,9},{2,10},{3,11},{4,12},{5,13},{6,14},{7,15},{8,0},{9,1},... | collective-permute-start | bytes 786440 | tf_op jit(solution)/shard_map/ppermute | solution.py:385
  31.8 22.5 %collective-permute-start.10 = (bf16[256,512]{1,0:T(8,128)(2,1)S(1)}, bf16[256,512]{1,0:T(8,128)(2,1)S(1)}, u32[]{:S(2)}, u32[]{:S(2)}) collective-permute-start(bf16[256,512]{1,0:T(8,128)(2,1)S(1)} %get-tuple-element.36), channel_id=1, source_target_pairs={{0,12},{1,13},{2,14},{3,15},{4,0},{5,1},{6,2},{7,3},{8,4},{9,5},{1... | collective-permute-start | bytes 786440 | tf_op jit(solution)/shard_map/ppermute | solution.py:385
  54.5 24.5 %collective-permute-start.15 = (bf16[4,256,512]{2,1,0:T(8,128)(2,1)S(1)}, bf16[4,256,512]{2,1,0:T(8,128)(2,1)S(1)}, u32[]{:S(2)}, u32[]{:S(2)}) collective-permute-start(bf16[4,256,512]{2,1,0:T(8,128)(2,1)S(1)} %pad_maximum_fusion.4.refs_8_), channel_id=1, source_target_pairs={{0,2},{1,3},{2,0},{3,1},{4,6},{5,7},{6,4},{7,5},{8,10},{9,11},{10,... | collective-permute-start | bytes 3145736 | tf_op jit(solution)/shard_map/ppermute | solution.py:379
  55.6 9.2 %collective-permute-start.12 = (bf16[256,512]{1,0:T(8,128)(2,1)S(1)}, bf16[256,512]{1,0:T(8,128)(2,1)S(1)}, u32[]{:S(2)}, u32[]{:S(2)}) collective-permute-start(bf16[256,512]{1,0:T(8,128)(2,1)S(1)} %get-tuple-element.37), channel_id=1, source_target_pairs={{0,4},{1,5},{2,6},{3,7},{4,8},{5,9},{6,10},{7,11},{8,12},{9,13},{1... | collective-permute-start | bytes 786440 | tf_op jit(solution)/shard_map/ppermute | solution.py:385
  55.6 22.0 %collective-permute-start.13 = (bf16[256,512]{1,0:T(8,128)(2,1)S(1)}, bf16[256,512]{1,0:T(8,128)(2,1)S(1)}, u32[]{:S(2)}, u32[]{:S(2)}) collective-permute-start(bf16[256,512]{1,0:T(8,128)(2,1)S(1)} %get-tuple-element.37), channel_id=1, source_target_pairs={{0,8},{1,9},{2,10},{3,11},{4,12},{5,13},{6,14},{7,15},{8,0},{9,1},... | collective-permute-start | bytes 786440 | tf_op jit(solution)/shard_map/ppermute | solution.py:385
  56.0 22.4 %collective-permute-start.14 = (bf16[256,512]{1,0:T(8,128)(2,1)S(1)}, bf16[256,512]{1,0:T(8,128)(2,1)S(1)}, u32[]{:S(2)}, u32[]{:S(2)}) collective-permute-start(bf16[256,512]{1,0:T(8,128)(2,1)S(1)} %get-tuple-element.37), channel_id=1, source_target_pairs={{0,12},{1,13},{2,14},{3,15},{4,0},{5,1},{6,2},{7,3},{8,4},{9,5},{1... | collective-permute-start | bytes 786440 | tf_op jit(solution)/shard_map/ppermute | solution.py:385
  79.0 28.0 %collective-permute-start.16 = (bf16[2,2,6,64,1024]{4,3,2,1,0:T(8,128)(2,1)S(1)}, bf16[2,2,6,64,1024]{4,3,2,1,0:T(8,128)(2,1)S(1)}, u32[]{:S(2)}, u32[]{:S(2)}) collective-permute-start(bf16[2,2,6,64,1024]{4,3,2,1,0:T(8,128)(2,1)S(1)} %pad_maximum_fusion), channel_id=1, source_target_pairs={{0,1},{1,0},{2,3},{3,2},{4,5},{5,4},{6,7},{7,6},{8,9},{9,8},{10,11... | collective-permute-start | bytes 9437192 | tf_op jit(solution)/shard_map/ppermute | solution.py:376
  79.2 27.3 %collective-permute-start.20 = (bf16[4,256,512]{2,1,0:T(8,128)(2,1)S(1)}, bf16[4,256,512]{2,1,0:T(8,128)(2,1)S(1)}, u32[]{:S(2)}, u32[]{:S(2)}) collective-permute-start(bf16[4,256,512]{2,1,0:T(8,128)(2,1)S(1)} %pad_maximum_fusion.5.refs_10_.refs_12_), channel_id=1, source_target_pairs={{0,2},{1,3},{2,0},{3,1},{4,6},{5,7},{6,4},{7,5},{8,10},{9,11},{10,... | collective-permute-start | bytes 3145736 | tf_op jit(solution)/shard_map/ppermute | solution.py:379
  80.2 9.1 %collective-permute-start.17 = (bf16[256,512]{1,0:T(8,128)(2,1)S(1)}, bf16[256,512]{1,0:T(8,128)(2,1)S(1)}, u32[]{:S(2)}, u32[]{:S(2)}) collective-permute-start(bf16[256,512]{1,0:T(8,128)(2,1)S(1)} %get-tuple-element.40), channel_id=1, source_target_pairs={{0,4},{1,5},{2,6},{3,7},{4,8},{5,9},{6,10},{7,11},{8,12},{9,13},{1... | collective-permute-start | bytes 786440 | tf_op jit(solution)/shard_map/ppermute | solution.py:385
  80.2 23.1 %collective-permute-start.18 = (bf16[256,512]{1,0:T(8,128)(2,1)S(1)}, bf16[256,512]{1,0:T(8,128)(2,1)S(1)}, u32[]{:S(2)}, u32[]{:S(2)}) collective-permute-start(bf16[256,512]{1,0:T(8,128)(2,1)S(1)} %get-tuple-element.40), channel_id=1, source_target_pairs={{0,8},{1,9},{2,10},{3,11},{4,12},{5,13},{6,14},{7,15},{8,0},{9,1},... | collective-permute-start | bytes 786440 | tf_op jit(solution)/shard_map/ppermute | solution.py:385
  82.7 23.6 %collective-permute-start.19 = (bf16[256,512]{1,0:T(8,128)(2,1)S(1)}, bf16[256,512]{1,0:T(8,128)(2,1)S(1)}, u32[]{:S(2)}, u32[]{:S(2)}) collective-permute-start(bf16[256,512]{1,0:T(8,128)(2,1)S(1)} %get-tuple-element.40), channel_id=1, source_target_pairs={{0,12},{1,13},{2,14},{3,15},{4,0},{5,1},{6,2},{7,3},{8,4},{9,5},{1... | collective-permute-start | bytes 786440 | tf_op jit(solution)/shard_map/ppermute | solution.py:385
  106.5 25.1 %collective-permute-start.24 = (bf16[4,256,512]{2,1,0:T(8,128)(2,1)S(1)}, bf16[4,256,512]{2,1,0:T(8,128)(2,1)S(1)}, u32[]{:S(2)}, u32[]{:S(2)}) collective-permute-start(bf16[4,256,512]{2,1,0:T(8,128)(2,1)S(1)} %pad_maximum_fusion.7.refs_5_), channel_id=1, source_target_pairs={{0,2},{1,3},{2,0},{3,1},{4,6},{5,7},{6,4},{7,5},{8,10},{9,11},{10,... | collective-permute-start | bytes 3145736 | tf_op jit(solution)/shard_map/ppermute | solution.py:379
  107.0 23.1 %collective-permute-start.21 = (bf16[256,512]{1,0:T(8,128)(2,1)S(1)}, bf16[256,512]{1,0:T(8,128)(2,1)S(1)}, u32[]{:S(2)}, u32[]{:S(2)}) collective-permute-start(bf16[256,512]{1,0:T(8,128)(2,1)S(1)} %get-tuple-element.42), channel_id=1, source_target_pairs={{0,4},{1,5},{2,6},{3,7},{4,8},{5,9},{6,10},{7,11},{8,12},{9,13},{1... | collective-permute-start | bytes 786440 | tf_op jit(solution)/shard_map/ppermute | solution.py:385
  107.0 23.2 %collective-permute-start.22 = (bf16[256,512]{1,0:T(8,128)(2,1)S(1)}, bf16[256,512]{1,0:T(8,128)(2,1)S(1)}, u32[]{:S(2)}, u32[]{:S(2)}) collective-permute-start(bf16[256,512]{1,0:T(8,128)(2,1)S(1)} %get-tuple-element.42), channel_id=1, source_target_pairs={{0,8},{1,9},{2,10},{3,11},{4,12},{5,13},{6,14},{7,15},{8,0},{9,1},... | collective-permute-start | bytes 786440 | tf_op jit(solution)/shard_map/ppermute | solution.py:385
  108.3 22.8 %collective-permute-start.23 = (bf16[256,512]{1,0:T(8,128)(2,1)S(1)}, bf16[256,512]{1,0:T(8,128)(2,1)S(1)}, u32[]{:S(2)}, u32[]{:S(2)}) collective-permute-start(bf16[256,512]{1,0:T(8,128)(2,1)S(1)} %get-tuple-element.42), channel_id=1, source_target_pairs={{0,12},{1,13},{2,14},{3,15},{4,0},{5,1},{6,2},{7,3},{8,4},{9,5},{1... | collective-permute-start | bytes 786440 | tf_op jit(solution)/shard_map/ppermute | solution.py:385
  138.6 25.2 %collective-permute-start.25 = (bf16[4,256,512]{2,1,0:T(8,128)(2,1)S(1)}, bf16[4,256,512]{2,1,0:T(8,128)(2,1)S(1)}, u32[]{:S(2)}, u32[]{:S(2)}) collective-permute-start(bf16[4,256,512]{2,1,0:T(8,128)(2,1)S(1)} %pad_maximum_fusion.6.refs_5_.refs_7_), channel_id=1, source_target_pairs={{0,2},{1,3},{2,0},{3,1},{4,6},{5,7},{6,4},{7,5},{8,10},{9,11},{10,... | collective-permute-start | bytes 3145736 | tf_op jit(solution)/shard_map/ppermute | solution.py:379
  141.9 36.6 %collective-permute-start.30 = (bf16[2,6,64,1024]{3,2,1,0:T(8,128)(2,1)S(1)}, bf16[2,6,64,1024]{3,2,1,0:T(8,128)(2,1)}, u32[]{:S(2)}, u32[]{:S(2)}) collective-permute-start(bf16[2,6,64,1024]{3,2,1,0:T(8,128)(2,1)S(1)} %pad_maximum_fusion.2), channel_id=1, source_target_pairs={{0,16},{16,0},{1,17},{17,1},{2,18},{18,2},{3,19},{19,3},{4,20},{20... | collective-permute-start | bytes 4718600 | tf_op jit(solution)/shard_map/ppermute | solution.py:382
  (16 other events, 85.5 us)

commit v13 on v12

--- a/solution.py
+++ b/solution.py
@@ -236,7 +236,7 @@
     hidden = sum(n for _, n in units)
     size = per_block * seq
 
-    tok = pl.BlockSpec((size, width), lambda j, *_: (j + offset, 0))
+    tok = pl.BlockSpec((size, width), lambda j, *_: (j, 0))
     hbm = pl.BlockSpec(memory_space=pl.ANY)
     args = [*scalars, *(tokens_of[chip] for chip in chips), tokens_of[-1]]
     specs = [hbm] * (len(chips) + 1)
@@ -247,7 +247,7 @@
     specs += [hbm] * len(starts)
     alias = {}
     out_specs = [tok, tok]
-    out_shape = [jax.ShapeDtypeStruct((4 * rows * seq, width), F32)] * 2
+    out_shape = [jax.ShapeDtypeStruct((number * size, width), F32)] * 2
     scratch = [
         pltpu.VMEM((2 * len(chips), 2, rows, seq, width), BF16),
         pltpu.VMEM((lines, 2, depth2, hidden), BF16),
@@ -296,31 +296,19 @@
     )(*args)
 
 
-def finish_kernel(member_ref, gain_ref, *refs):
-    sources, (value_ref, grad_ref, coupling_ref), buffers, sems = (
-        refs[:7], refs[7:10], refs[10:17], refs[17]
-    )
-    rows, seq, width = value_ref.shape
-    copies = []
-    for r in range(rows):
-        for i, (source, buffer) in enumerate(zip(sources, buffers)):
-            at = (slice(None), r) if len(source.shape) == 4 else (r,)
-            copies.append(
-                pltpu.make_async_copy(source.at[at], buffer.at[at], sems.at[i, r])
-            )
-    for copy in copies:
-        copy.start()
-    x_ref, g_ref, out_ref, back_ref, other_out_ref, other_back_ref, across_ref = buffers
+def finish_kernel(
+    member_ref, x_ref, g_ref, gain_ref, out_ref, back_ref, other_out_ref, other_back_ref,
+    across_ref, value_ref, grad_ref, coupling_ref,
+):
+    rows, seq, width = x_ref.shape
     diagonal = lax.broadcasted_iota(jnp.int32, (seq, seq), 0) == lax.broadcasted_iota(
         jnp.int32, (seq, seq), 1
     )
     for r in range(rows):
-        for copy in copies[7 * r : 7 * r + 7]:
-            copy.wait()
         x = x_ref[r].astype(F32)
         inv = 1.0 / jnp.sqrt(jnp.mean(x * x, axis=1, keepdims=True) + 1e-06)
         normed = x * inv
-        gain = gain_ref[pl.ds(member_ref[r], 1), :]
+        gain = gain_ref[pl.ds(member_ref[pl.program_id(0) * rows + r], 1), :]
         back = gain * (
             back_ref[r] + other_back_ref[r].astype(F32) + across_ref[1, r].astype(F32)
         )
@@ -329,27 +317,32 @@
         value_ref[r] = (x + out).astype(BF16)
         grad_ref[r] = (g_ref[r].astype(F32) + (back - normed * stat) * inv).astype(BF16)
         line = jnp.sum(jnp.where(diagonal, stat, 0.0), axis=0, keepdims=True)
-        coupling_ref[pl.ds(r, 1), :] = line * math.sqrt(width)
-
-
-def finish(member_own, gain, *sources):
-    rows, seq, width = sources[0].shape
-    vmem = pl.BlockSpec(memory_space=pltpu.VMEM)
+        coupling_ref[pl.ds(pl.program_id(0) * rows + r, 1), :] = line * math.sqrt(width)
+
+
+def finish(member_own, x, g, gain, *sums):
+    rows, seq, width = x.shape
+    step = math.gcd(rows, 2)
+    row = pl.BlockSpec((step, seq, width), lambda r, mem: (r, 0, 0))
+    two = pl.BlockSpec((2, step, seq, width), lambda r, mem: (0, r, 0, 0))
     return pl.pallas_call(
         finish_kernel,
-        in_specs=[pl.BlockSpec(memory_space=pltpu.SMEM), vmem]
-        + [pl.BlockSpec(memory_space=pl.ANY)] * 7,
-        out_specs=[vmem] * 3,
+        grid_spec=pltpu.PrefetchScalarGridSpec(
+            num_scalar_prefetch=1,
+            grid=(rows // step,),
+            in_specs=[
+                row, row, pl.BlockSpec(gain.shape, lambda r, mem: (0, 0)), row, row, row, row, two
+            ],
+            out_specs=[row, row, pl.BlockSpec((rows, seq), lambda r, mem: (0, 0))],
+        ),
         out_shape=[
             jax.ShapeDtypeStruct((rows, seq, width), BF16),
             jax.ShapeDtypeStruct((rows, seq, width), BF16),
             jax.ShapeDtypeStruct((rows, seq), F32),
         ],
-        scratch_shapes=[pltpu.VMEM(a.shape, a.dtype) for a in sources]
-        + [pltpu.SemaphoreType.DMA((7, rows))],
         compiler_params=pltpu.CompilerParams(vmem_limit_bytes=VMEM_LIMIT // 2),
         name="finish",
-    )(member_own, gain, *sources)
+    )(member_own, x, g, gain, *sums)
 
 
 def sort_rows(picks):
@@ -389,9 +382,8 @@
 
     unit = hidden // 32
     quarter, half = 7 * unit, 2 * unit
-    both = jnp.stack([up_proj, down_proj], axis=1)
-
-    def units_of(c):
+
+    def units_of(c, both):
         return jnp.concatenate(
             [
                 lax.dynamic_slice_in_dim(both, (2 * x_at + c) * quarter, quarter, 3),
@@ -416,8 +408,9 @@
 
     head_theirs = partner(head_of(1 - core))
     shard_head = both_cores(head_of(core), head_theirs)
-    theirs = partner(after(units_of(1 - core), head_theirs))
-    shard = both_cores(units_of(core), theirs)
+    both = jnp.stack([after(up_proj, shard_head), down_proj], axis=1)
+    theirs = partner(units_of(1 - core, both))
+    shard = both_cores(units_of(core, both), theirs)
 
     groups = [
         [(0, 0, 2 * unit)],
@@ -486,14 +479,15 @@
     along_z(4, there[2], far)
     across_y(3)
     tokens_of = (near, over, far)
+    other_rows, own_rows = (0, per_chip, per_block), (per_chip, per_chip, per_block)
     sums = chunk(
-        (True, False), (0, 2 * per_chip, per_block), (0, 1), scalars,
-        (after(near, *shifted[3]), over, far), chunk_pieces(0, 1, 2), None,
+        (True, False), other_rows, (1,), scalars,
+        (near, after(over, *shifted[3]), far), chunk_pieces(0, 1, 2), None,
     )
     across_y(4)
     sums = (after(sums[0], *shifted[4]), sums[1])
     *same, other_out, other_back = chunk(
-        (False, True), (0, per_chip, per_block), (1,), scalars, tokens_of, chunk_pieces(3), sums,
+        (False, True), other_rows, (1,), scalars, tokens_of, chunk_pieces(3), sums,
         (BF16, BF16), 0,
     )
     across = jnp.stack(
@@ -502,16 +496,17 @@
             for a, b in zip(same, (other_out, other_back))
         ]
     )
-    sums = tuple(after(a, across) for a in sums)
+    tokens_of = (after(near, across), over, far)
     across = over_x(across)
-    own = (per_chip, per_chip, per_block)
-    sums = chunk((False, False), own, (0,), scalars, tokens_of, chunk_pieces(3), sums, None, 0)
+    sums = chunk(
+        (True, False), own_rows, (0,), scalars, tokens_of, chunk_pieces(0, 1, 2, 3), None, None, 0
+    )
     out, back, packed_out, packed_back = chunk(
-        (False, True), own, (0,), scalars, tokens_of, chunk_pieces(4), sums, (F32, BF16), 0
+        (False, True), own_rows, (0,), scalars, tokens_of, chunk_pieces(4), sums, (F32, BF16), 0
     )
     return tuple(
         finish(
-            pick_own, norm_gain, tokens_in, upstream, out, back,
+            pick_own, tokens_in, upstream, norm_gain, out, back,
             partner(packed_out), partner(packed_back), across,
         )
     )

time: 189 us -> 180 us (0.952); the launches traced: 186 us -> 180 us
  waiting for transfers between devices: 89.7 us -> 84.9 us
  Pallas kernels: 48.8 us -> 44.2 us
  local copies, waits for them, and re-layouts: 6.5 us -> 9.45 us
  starting transfers between devices: 32 us -> 34.5 us
  other arithmetic: 8.28 us -> 5.81 us
    ppermute x5, waiting for transfers between devices: 12.3 us -> 4.35 us  [over_y(): return lax.ppermute(a, 'row', [(i, i ^ 2) for i in range(ranks)])]
    pallas_call x1, Pallas kernels: 7.79 us -> 2.91 us  [finish(): pl.pallas_call(finish_kernel, grid_spec=pltpu.PrefetchScalarGridSpec(num_...]
    ppermute x15, waiting for transfers between devices: 64.3 us -> 67.6 us  [shift_z(): lax.ppermute(a, 'row', [(i, (i + 4 * d) % ranks) for i in range(ranks)])]
    unnamed x18 -> x28, local copies, waits for them, and re-layouts: 3.87 us -> 6.73 us
    ppermute x15, starting transfers between devices: 22.1 us -> 24.8 us  [shift_z(): lax.ppermute(a, 'row', [(i, (i + 4 * d) % ranks) for i in range(ranks)])]
  transfers between devices with their start and end apart: 31 -> 31, of which waited for: 22 -> 21; matrix products, arithmetic and copies ran while one was open for 4% -> 4% of each run, Pallas kernels for 19% -> 19%
where the time goes in v13:
time: 180 us
  waiting for transfers between devices  84.9 us (47%)
  Pallas kernels  44.2 us (25%)
  starting transfers between devices  34.5 us (19%)
  local copies, waits for them, and re-layouts  9.45 us (5%)
  other arithmetic  5.81 us (3%)
    ppermute x15, waiting for transfers between devices, shift_z(): lax.ppermute(a, 'row', [(i, (i + 4 * d) % ranks) for i in range(ranks)])  67.6 us
    pallas_call x4, Pallas kernels, chunk(): pl.pallas_call(kernel, grid_spec=pltpu.PrefetchScalarGridSpec(num_scalar_...  41.3 us
    ppermute x15, starting transfers between devices, shift_z(): lax.ppermute(a, 'row', [(i, (i + 4 * d) % ranks) for i in range(ranks)])  24.8 us
    ppermute x3, waiting for transfers between devices, over_x(): return lax.ppermute(a, 'grp', [(0, 1), (1, 0)])  7.71 us
    unnamed x28, local copies, waits for them, and re-layouts  6.73 us
    ppermute x5, starting transfers between devices, over_y(): return lax.ppermute(a, 'row', [(i, i ^ 2) for i in range(ranks)])  5.33 us
    ppermute x8, waiting for transfers between devices, partner(): return lax.ppermute(a, 'row', [(i, i ^ 1) for i in range(ranks)])  5.26 us
    ppermute x5, waiting for transfers between devices, over_y(): return lax.ppermute(a, 'row', [(i, i ^ 2) for i in range(ranks)])  4.35 us
  transfers between devices with their start and end apart: 31, of which 21 were waited for; matrix products, arithmetic and copies ran while one was open for 4% of the time, Pallas kernels for 19%

profile of v13, /device:TPU:8, one launch (start us, length us, event | category | flops | bytes accessed | tf_op | source)
XLA Modules:
  0.0 180.0 jit_solution(5878558297788799005)
XLA Ops:
  4.2 2.0 %collective-permute-start.4 = (bf16[256,256]{1,0:T(8,128)(2,1)S(1)}, bf16[256,256]{1,0:T(8,128)(2,1)S(1)}, u32[]{:S(2)}, u32[]{:S(2)}) collective-permute-start(bf16[256,256]{1,0:T(8,128)(2,1)S(1)} %bitcast.78), channel_id=1, source_target_pairs={{0,4},{1,5},{2,6},{3,7},{4,8},{5,9},{6,10},{7,11},{8,12},{9,13},{1... | collective-permute-start | bytes 393224 | tf_op jit(solution)/shard_map/ppermute | solution.py:378
  6.2 4.4 %collective-permute-start.7 = (bf16[256,256]{1,0:T(8,128)(2,1)S(1)}, bf16[256,256]{1,0:T(8,128)(2,1)S(1)}, u32[]{:S(2)}, u32[]{:S(2)}) collective-permute-start(bf16[256,256]{1,0:T(8,128)(2,1)S(1)} %bitcast.79), channel_id=1, source_target_pairs={{0,8},{1,9},{2,10},{3,11},{4,12},{5,13},{6,14},{7,15},{8,0},{9,1},... | collective-permute-start | bytes 393224 | tf_op jit(solution)/shard_map/ppermute | solution.py:378
  13.9 2.1 %collective-permute-done.1 = s32[6]{0:T(128)S(1)} collective-permute-done((s32[6]{0:T(128)S(1)}, s32[6]{0:T(128)S(1)}, u32[]{:S(2)}, u32[]{:S(2)}) %collective-permute-start.1) | collective-permute-done | bytes 56 | tf_op jit(solution)/shard_map/ppermute | solution.py:375
  22.4 2.7 %collective-permute-start.10 = (bf16[256,512]{1,0:T(8,128)(2,1)S(1)}, bf16[256,512]{1,0:T(8,128)(2,1)S(1)}, u32[]{:S(2)}, u32[]{:S(2)}) collective-permute-start(bf16[256,512]{1,0:T(8,128)(2,1)S(1)} %get-tuple-element.35), channel_id=1, source_target_pairs={{0,12},{1,13},{2,14},{3,15},{4,0},{5,1},{6,2},{7,3},{8,4},{9,5},{1... | collective-permute-start | bytes 786440 | tf_op jit(solution)/shard_map/ppermute | solution.py:378
  25.0 4.6 %collective-permute-start.9 = (bf16[256,512]{1,0:T(8,128)(2,1)S(1)}, bf16[256,512]{1,0:T(8,128)(2,1)S(1)}, u32[]{:S(2)}, u32[]{:S(2)}) collective-permute-start(bf16[256,512]{1,0:T(8,128)(2,1)S(1)} %get-tuple-element.35), channel_id=1, source_target_pairs={{0,8},{1,9},{2,10},{3,11},{4,12},{5,13},{6,14},{7,15},{8,0},{9,1},... | collective-permute-start | bytes 786440 | tf_op jit(solution)/shard_map/ppermute | solution.py:378
  30.0 8.2 %collective-permute-done.10 = bf16[256,512]{1,0:T(8,128)(2,1)S(1)} collective-permute-done((bf16[256,512]{1,0:T(8,128)(2,1)S(1)}, bf16[256,512]{1,0:T(8,128)(2,1)S(1)}, u32[]{:S(2)}, u32[]{:S(2)}) %collective-permute-start.10) | collective-permute-done | bytes 262176 | tf_op jit(solution)/shard_map/ppermute | solution.py:378
  40.1 7.8 %collective-permute-done.9 = bf16[256,512]{1,0:T(8,128)(2,1)S(1)} collective-permute-done((bf16[256,512]{1,0:T(8,128)(2,1)S(1)}, bf16[256,512]{1,0:T(8,128)(2,1)S(1)}, u32[]{:S(2)}, u32[]{:S(2)}) %collective-permute-start.9) | collective-permute-done | bytes 262176 | tf_op jit(solution)/shard_map/ppermute | solution.py:378
  49.1 3.7 %collective-permute-start.13 = (bf16[256,512]{1,0:T(8,128)(2,1)S(1)}, bf16[256,512]{1,0:T(8,128)(2,1)S(1)}, u32[]{:S(2)}, u32[]{:S(2)}) collective-permute-start(bf16[256,512]{1,0:T(8,128)(2,1)S(1)} %get-tuple-element.36), channel_id=1, source_target_pairs={{0,8},{1,9},{2,10},{3,11},{4,12},{5,13},{6,14},{7,15},{8,0},{9,1},... | collective-permute-start | bytes 786440 | tf_op jit(solution)/shard_map/ppermute | solution.py:378
  54.6 2.4 %collective-permute-done.5.refs_3_ = bf16[2,6,64,1024]{3,2,1,0:T(8,128)(2,1)S(1)} collective-permute-done((bf16[2,6,64,1024]{3,2,1,0:T(8,128)(2,1)S(1)}, bf16[2,6,64,1024]{3,2,1,0:T(8,128)(2,1)S(1)}, u32[]{:S(2)}, u32[]{:S(2)}) %collective-permute-start.5) | collective-permute-done | bytes 1572896 | tf_op jit(solution)/shard_map/ppermute | solution.py:375
  58.4 12.8 %collective-permute-done.13 = bf16[256,512]{1,0:T(8,128)(2,1)S(1)} collective-permute-done((bf16[256,512]{1,0:T(8,128)(2,1)S(1)}, bf16[256,512]{1,0:T(8,128)(2,1)S(1)}, u32[]{:S(2)}, u32[]{:S(2)}) %collective-permute-start.13) | collective-permute-done | bytes 262176 | tf_op jit(solution)/shard_map/ppermute | solution.py:378
  71.1 4.0 %collective-permute-done.14 = bf16[256,512]{1,0:T(8,128)(2,1)S(1)} collective-permute-done((bf16[256,512]{1,0:T(8,128)(2,1)S(1)}, bf16[256,512]{1,0:T(8,128)(2,1)S(1)}, u32[]{:S(2)}, u32[]{:S(2)}) %collective-permute-start.14) | collective-permute-done | bytes 262176 | tf_op jit(solution)/shard_map/ppermute | solution.py:378
  78.9 7.1 %collective-permute-done.17 = bf16[256,512]{1,0:T(8,128)(2,1)S(1)} collective-permute-done((bf16[256,512]{1,0:T(8,128)(2,1)S(1)}, bf16[256,512]{1,0:T(8,128)(2,1)S(1)}, u32[]{:S(2)}, u32[]{:S(2)}) %collective-permute-start.17) | collective-permute-done | bytes 262176 | tf_op jit(solution)/shard_map/ppermute | solution.py:378
  86.0 13.9 %collective-permute-done.18 = bf16[256,512]{1,0:T(8,128)(2,1)S(1)} collective-permute-done((bf16[256,512]{1,0:T(8,128)(2,1)S(1)}, bf16[256,512]{1,0:T(8,128)(2,1)S(1)}, u32[]{:S(2)}, u32[]{:S(2)}) %collective-permute-start.18) | collective-permute-done | bytes 262176 | tf_op jit(solution)/shard_map/ppermute | solution.py:378
  104.1 2.0 %collective-permute-start.24 = (bf16[256,512]{1,0:T(8,128)(2,1)S(1)}, bf16[256,512]{1,0:T(8,128)(2,1)S(1)}, u32[]{:S(2)}, u32[]{:S(2)}) collective-permute-start(bf16[256,512]{1,0:T(8,128)(2,1)S(1)} %get-tuple-element.44), channel_id=1, source_target_pairs={{0,12},{1,13},{2,14},{3,15},{4,0},{5,1},{6,2},{7,3},{8,4},{9,5},{1... | collective-permute-start | bytes 786440 | tf_op jit(solution)/shard_map/ppermute | solution.py:378
  106.1 10.3 %chunk.4 = (f32[768,1024]{1,0:T(8,128)S(1)}, f32[768,1024]{1,0:T(8,128)S(1)}) custom-call(s32[24]{0:T(128)S(1)} %pad_add_fusion.3.refs_0_, s32[2]{0:T(128)S(1)} %pad_add_fusion.4.refs_1_, s32[24]{0:T(128)S(1)} %pad_add_fusion.5.refs_2_, bf16[2,6,64,1024]{3,2,1,0:T(8,128)(2,1)S(1)} %collective-permute-done.5.refs_3_, bf16[2,2,6,64,1024]{4,3,2,1,0:T(8,128)(2,1)} %copy-done, ...), custom_call_target="tpu_custom_call" | custom-call | flops 5368709120 | bytes 20971520 | tf_op jit(solution)/shard_map/chunk/pallas_call | solution.py:278
  118.1 6.7 %collective-permute-done.23 = bf16[256,512]{1,0:T(8,128)(2,1)S(1)} collective-permute-done((bf16[256,512]{1,0:T(8,128)(2,1)S(1)}, bf16[256,512]{1,0:T(8,128)(2,1)S(1)}, u32[]{:S(2)}, u32[]{:S(2)}) %collective-permute-start.23) | collective-permute-done | bytes 262176 | tf_op jit(solution)/shard_map/ppermute | solution.py:378
  124.7 2.1 %collective-permute-done.24 = bf16[256,512]{1,0:T(8,128)(2,1)S(1)} collective-permute-done((bf16[256,512]{1,0:T(8,128)(2,1)S(1)}, bf16[256,512]{1,0:T(8,128)(2,1)S(1)}, u32[]{:S(2)}, u32[]{:S(2)}) %collective-permute-start.24) | collective-permute-done | bytes 262176 | tf_op jit(solution)/shard_map/ppermute | solution.py:378
  126.8 1.9 %copy-done.1 = bf16[2,2,6,64,1024]{4,3,2,1,0:T(8,128)(2,1)S(1)} copy-done((bf16[2,2,6,64,1024]{4,3,2,1,0:T(8,128)(2,1)S(1)}, bf16[2,2,6,64,1024]{4,3,2,1,0:T(8,128)(2,1)}, u32[]{:S(2)}) %copy-start.1) | copy-done | bytes 3145752
  128.7 7.9 %chunk.5 = (bf16[6,64,1024]{2,1,0:T(8,128)(2,1)S(1)}, bf16[6,64,1024]{2,1,0:T(8,128)(2,1)S(1)}, bf16[6,64,1024]{2,1,0:T(8,128)(2,1)S(1)}, bf16[6,64,1024]{2,1,0:T(8,128)(2,1)S(1)}) custom-call(s32[24]{0:T(128)S(1)} %pad_add_fusion.3.refs_0_, s32[2]{0:T(128)S(1)} %pad_add_fusion.4.refs_1_, s32[24]{0:T(128)S(1)} %pad_add_fusion.5.refs_2_, ...), custom_call_target="tpu_custom_call" | custom-call | tf_op jit(solution)/shard_map/chunk/pallas_call | solution.py:278
  141.6 15.3 %chunk.6 = (f32[768,1024]{1,0:T(8,128)S(1)}, f32[768,1024]{1,0:T(8,128)}) custom-call(s32[24]{0:T(128)S(1)} %pad_add_fusion.3.refs_0_, s32[2]{0:T(128)S(1)} %pad_add_fusion.4.refs_1_, s32[24]{0:T(128)S(1)} %pad_add_fusion.5.refs_2_, bf16[2,6,64,1024]{3,2,1,0:T(8,128)(2,1)S(1)} %get-tuple-element.51.refs_3_, bf16[2,2,6,64,1024]{4,3,2,1,0:T(8,128)(2,1)} %copy-done, ...), custom_call_target="tpu_custom_call" | custom-call | tf_op jit(solution)/shard_map/chunk/pallas_call | solution.py:278
  158.6 3.9 %collective-permute-done.27.refs_6_.refs_8_ = bf16[4,256,512]{2,1,0:T(8,128)(2,1)S(1)} collective-permute-done((bf16[4,256,512]{2,1,0:T(8,128)(2,1)S(1)}, bf16[4,256,512]{2,1,0:T(8,128)(2,1)S(1)}, u32[]{:S(2)}, u32[]{:S(2)}) %collective-permute-start.27) | collective-permute-done | bytes 1048608 | tf_op jit(solution)/shard_map/ppermute | solution.py:372
  162.5 7.8 %chunk.7 = (f32[6,64,1024]{2,1,0:T(8,128)S(1)}, f32[6,64,1024]{2,1,0:T(8,128)S(1)}, bf16[6,64,1024]{2,1,0:T(8,128)(2,1)S(1)}, bf16[6,64,1024]{2,1,0:T(8,128)(2,1)S(1)}) custom-call(s32[24]{0:T(128)S(1)} %pad_add_fusion.3.refs_0_, s32[2]{0:T(128)S(1)} %pad_add_fusion.4.refs_1_, s32[24]{0:T(128)S(1)} %pad_add_fusion.5.refs_2_, ...), custom_call_target="tpu_custom_call" | custom-call | tf_op jit(solution)/shard_map/chunk/pallas_call | solution.py:278
  173.8 3.2 %collective-permute-done.30.across_ref = bf16[2,6,64,1024]{3,2,1,0:T(8,128)(2,1)S(1)} collective-permute-done((bf16[2,6,64,1024]{3,2,1,0:T(8,128)(2,1)S(1)}, bf16[2,6,64,1024]{3,2,1,0:T(8,128)(2,1)S(1)}, u32[]{:S(2)}, u32[]{:S(2)}) %collective-permute-start.30) | collective-permute-done | bytes 1572896 | tf_op jit(solution)/shard_map/ppermute | solution.py:375
  177.1 2.9 %finish.1 = (bf16[6,64,1024]{2,1,0:T(8,128)(2,1)}, bf16[6,64,1024]{2,1,0:T(8,128)(2,1)}, f32[6,64]{1,0:T(8,128)}) custom-call(s32[6]{0:T(128)S(1)} %bitcast.68, bf16[6,64,1024]{2,1,0:T(8,128)(2,1)S(1)} %copy-done.3, bf16[6,64,1024]{2,1,0:T(8,128)(2,1)S(1)} %copy-done.5, f32[2,1024]{1,0:T(2,128)S(1)} %copy-done.10, ...), custom_call_target="tpu_custom_call" | custom-call | tf_op jit(solution)/shard_map/finish/pallas_call | solution.py:328
  (115 shorter events, 39.3 us)
Async XLA Ops:
  4.1 11.9 %collective-permute-start.2 = (bf16[256,256]{1,0:T(8,128)(2,1)S(1)}, bf16[256,256]{1,0:T(8,128)(2,1)S(1)}, u32[]{:S(2)}, u32[]{:S(2)}) collective-permute-start(bf16[256,256]{1,0:T(8,128)(2,1)S(1)} %bitcast.77), channel_id=1, source_target_pairs={{0,12},{1,13},{2,14},{3,15},{4,0},{5,1},{6,2},{7,3},{8,4},{9,5},{1... | collective-permute-start | bytes 393224 | tf_op jit(solution)/shard_map/ppermute | solution.py:378
  4.2 11.8 %collective-permute-start.4 = (bf16[256,256]{1,0:T(8,128)(2,1)S(1)}, bf16[256,256]{1,0:T(8,128)(2,1)S(1)}, u32[]{:S(2)}, u32[]{:S(2)}) collective-permute-start(bf16[256,256]{1,0:T(8,128)(2,1)S(1)} %bitcast.78), channel_id=1, source_target_pairs={{0,4},{1,5},{2,6},{3,7},{4,8},{5,9},{6,10},{7,11},{8,12},{9,13},{1... | collective-permute-start | bytes 393224 | tf_op jit(solution)/shard_map/ppermute | solution.py:378
  6.2 11.5 %collective-permute-start.7 = (bf16[256,256]{1,0:T(8,128)(2,1)S(1)}, bf16[256,256]{1,0:T(8,128)(2,1)S(1)}, u32[]{:S(2)}, u32[]{:S(2)}) collective-permute-start(bf16[256,256]{1,0:T(8,128)(2,1)S(1)} %bitcast.79), channel_id=1, source_target_pairs={{0,8},{1,9},{2,10},{3,11},{4,12},{5,13},{6,14},{7,15},{8,0},{9,1},... | collective-permute-start | bytes 393224 | tf_op jit(solution)/shard_map/ppermute | solution.py:378
  11.8 9.8 %collective-permute-start.6 = (bf16[2,2,64,1152]{3,2,0,1:T(8,128)(2,1)S(1)}, bf16[2,2,64,1152]{3,2,0,1:T(8,128)(2,1)S(1)}, u32[]{:S(2)}, u32[]{:S(2)}) collective-permute-start(bf16[2,2,64,1152]{3,2,0,1:T(8,128)(2,1)S(1)} %pad_maximum_fusion.9), channel_id=1, source_target_pairs={{0,1},{1,0},{2,3},{3,2},{4,5},{5,4},{6,7},{7,6},{8,9},{9,8},{10,11... | collective-permute-start | bytes 1769480 | tf_op jit(solution)/shard_map/ppermute | solution.py:369
  17.8 30.2 %collective-permute-start.11 = (bf16[4,256,256]{2,1,0:T(8,128)(2,1)S(1)}, bf16[4,256,256]{2,1,0:T(8,128)(2,1)S(1)}, u32[]{:S(2)}, u32[]{:S(2)}) collective-permute-start(bf16[4,256,256]{2,1,0:T(8,128)(2,1)S(1)} %pad_maximum_fusion.10.refs_5_), channel_id=1, source_target_pairs={{0,2},{1,3},{2,0},{3,1},{4,6},{5,7},{6,4},{7,5},{8,10},{9,11},{10,... | collective-permute-start | bytes 1572872 | tf_op jit(solution)/shard_map/ppermute | solution.py:372
  20.1 36.9 %collective-permute-start.5 = (bf16[2,6,64,1024]{3,2,1,0:T(8,128)(2,1)S(1)}, bf16[2,6,64,1024]{3,2,1,0:T(8,128)(2,1)S(1)}, u32[]{:S(2)}, u32[]{:S(2)}) collective-permute-start(bf16[2,6,64,1024]{3,2,1,0:T(8,128)(2,1)S(1)} %get-tuple-element.51.refs_3_), channel_id=1, source_target_pairs={{0,16},{16,0},{1,17},{17,1},{2,18},{18,2},{3,19},{19,3},{4,20},{20... | collective-permute-start | bytes 4718600 | tf_op jit(solution)/shard_map/ppermute | solution.py:375
  22.4 15.8 %collective-permute-start.10 = (bf16[256,512]{1,0:T(8,128)(2,1)S(1)}, bf16[256,512]{1,0:T(8,128)(2,1)S(1)}, u32[]{:S(2)}, u32[]{:S(2)}) collective-permute-start(bf16[256,512]{1,0:T(8,128)(2,1)S(1)} %get-tuple-element.35), channel_id=1, source_target_pairs={{0,12},{1,13},{2,14},{3,15},{4,0},{5,1},{6,2},{7,3},{8,4},{9,5},{1... | collective-permute-start | bytes 786440 | tf_op jit(solution)/shard_map/ppermute | solution.py:378
  25.0 15.0 %collective-permute-start.8 = (bf16[256,512]{1,0:T(8,128)(2,1)S(1)}, bf16[256,512]{1,0:T(8,128)(2,1)S(1)}, u32[]{:S(2)}, u32[]{:S(2)}) collective-permute-start(bf16[256,512]{1,0:T(8,128)(2,1)S(1)} %get-tuple-element.35), channel_id=1, source_target_pairs={{0,4},{1,5},{2,6},{3,7},{4,8},{5,9},{6,10},{7,11},{8,12},{9,13},{1... | collective-permute-start | bytes 786440 | tf_op jit(solution)/shard_map/ppermute | solution.py:378
  25.0 22.8 %collective-permute-start.9 = (bf16[256,512]{1,0:T(8,128)(2,1)S(1)}, bf16[256,512]{1,0:T(8,128)(2,1)S(1)}, u32[]{:S(2)}, u32[]{:S(2)}) collective-permute-start(bf16[256,512]{1,0:T(8,128)(2,1)S(1)} %get-tuple-element.35), channel_id=1, source_target_pairs={{0,8},{1,9},{2,10},{3,11},{4,12},{5,13},{6,14},{7,15},{8,0},{9,1},... | collective-permute-start | bytes 786440 | tf_op jit(solution)/shard_map/ppermute | solution.py:378
  48.0 27.1 %collective-permute-start.15 = (bf16[4,256,512]{2,1,0:T(8,128)(2,1)S(1)}, bf16[4,256,512]{2,1,0:T(8,128)(2,1)S(1)}, u32[]{:S(2)}, u32[]{:S(2)}) collective-permute-start(bf16[4,256,512]{2,1,0:T(8,128)(2,1)S(1)} %pad_maximum_fusion.4.refs_7_), channel_id=1, source_target_pairs={{0,2},{1,3},{2,0},{3,1},{4,6},{5,7},{6,4},{7,5},{8,10},{9,11},{10,... | collective-permute-start | bytes 3145736 | tf_op jit(solution)/shard_map/ppermute | solution.py:372
  49.1 9.2 %collective-permute-start.12 = (bf16[256,512]{1,0:T(8,128)(2,1)S(1)}, bf16[256,512]{1,0:T(8,128)(2,1)S(1)}, u32[]{:S(2)}, u32[]{:S(2)}) collective-permute-start(bf16[256,512]{1,0:T(8,128)(2,1)S(1)} %get-tuple-element.36), channel_id=1, source_target_pairs={{0,4},{1,5},{2,6},{3,7},{4,8},{5,9},{6,10},{7,11},{8,12},{9,13},{1... | collective-permute-start | bytes 786440 | tf_op jit(solution)/shard_map/ppermute | solution.py:378
  49.1 22.0 %collective-permute-start.13 = (bf16[256,512]{1,0:T(8,128)(2,1)S(1)}, bf16[256,512]{1,0:T(8,128)(2,1)S(1)}, u32[]{:S(2)}, u32[]{:S(2)}) collective-permute-start(bf16[256,512]{1,0:T(8,128)(2,1)S(1)} %get-tuple-element.36), channel_id=1, source_target_pairs={{0,8},{1,9},{2,10},{3,11},{4,12},{5,13},{6,14},{7,15},{8,0},{9,1},... | collective-permute-start | bytes 786440 | tf_op jit(solution)/shard_map/ppermute | solution.py:378
  52.9 22.2 %collective-permute-start.14 = (bf16[256,512]{1,0:T(8,128)(2,1)S(1)}, bf16[256,512]{1,0:T(8,128)(2,1)S(1)}, u32[]{:S(2)}, u32[]{:S(2)}) collective-permute-start(bf16[256,512]{1,0:T(8,128)(2,1)S(1)} %get-tuple-element.36), channel_id=1, source_target_pairs={{0,12},{1,13},{2,14},{3,15},{4,0},{5,1},{6,2},{7,3},{8,4},{9,5},{1... | collective-permute-start | bytes 786440 | tf_op jit(solution)/shard_map/ppermute | solution.py:378
  75.1 27.3 %collective-permute-start.16 = (bf16[2,2,6,64,1024]{4,3,2,1,0:T(8,128)(2,1)S(1)}, bf16[2,2,6,64,1024]{4,3,2,1,0:T(8,128)(2,1)S(1)}, u32[]{:S(2)}, u32[]{:S(2)}) collective-permute-start(bf16[2,2,6,64,1024]{4,3,2,1,0:T(8,128)(2,1)S(1)} %pad_maximum_fusion), channel_id=1, source_target_pairs={{0,1},{1,0},{2,3},{3,2},{4,5},{5,4},{6,7},{7,6},{8,9},{9,8},{10,11... | collective-permute-start | bytes 9437192 | tf_op jit(solution)/shard_map/ppermute | solution.py:369
  75.3 25.6 %collective-permute-start.20 = (bf16[4,256,512]{2,1,0:T(8,128)(2,1)S(1)}, bf16[4,256,512]{2,1,0:T(8,128)(2,1)S(1)}, u32[]{:S(2)}, u32[]{:S(2)}) collective-permute-start(bf16[4,256,512]{2,1,0:T(8,128)(2,1)S(1)} %pad_maximum_fusion.6.refs_9_.refs_11_), channel_id=1, source_target_pairs={{0,2},{1,3},{2,0},{3,1},{4,6},{5,7},{6,4},{7,5},{8,10},{9,11},{10,... | collective-permute-start | bytes 3145736 | tf_op jit(solution)/shard_map/ppermute | solution.py:372
  76.8 9.1 %collective-permute-start.17 = (bf16[256,512]{1,0:T(8,128)(2,1)S(1)}, bf16[256,512]{1,0:T(8,128)(2,1)S(1)}, u32[]{:S(2)}, u32[]{:S(2)}) collective-permute-start(bf16[256,512]{1,0:T(8,128)(2,1)S(1)} %get-tuple-element.39), channel_id=1, source_target_pairs={{0,4},{1,5},{2,6},{3,7},{4,8},{5,9},{6,10},{7,11},{8,12},{9,13},{1... | collective-permute-start | bytes 786440 | tf_op jit(solution)/shard_map/ppermute | solution.py:378
  76.8 23.1 %collective-permute-start.18 = (bf16[256,512]{1,0:T(8,128)(2,1)S(1)}, bf16[256,512]{1,0:T(8,128)(2,1)S(1)}, u32[]{:S(2)}, u32[]{:S(2)}) collective-permute-start(bf16[256,512]{1,0:T(8,128)(2,1)S(1)} %get-tuple-element.39), channel_id=1, source_target_pairs={{0,8},{1,9},{2,10},{3,11},{4,12},{5,13},{6,14},{7,15},{8,0},{9,1},... | collective-permute-start | bytes 786440 | tf_op jit(solution)/shard_map/ppermute | solution.py:378
  77.0 23.3 %collective-permute-start.19 = (bf16[256,512]{1,0:T(8,128)(2,1)S(1)}, bf16[256,512]{1,0:T(8,128)(2,1)S(1)}, u32[]{:S(2)}, u32[]{:S(2)}) collective-permute-start(bf16[256,512]{1,0:T(8,128)(2,1)S(1)} %get-tuple-element.39), channel_id=1, source_target_pairs={{0,12},{1,13},{2,14},{3,15},{4,0},{5,1},{6,2},{7,3},{8,4},{9,5},{1... | collective-permute-start | bytes 786440 | tf_op jit(solution)/shard_map/ppermute | solution.py:378
  100.9 26.0 %collective-permute-start.21 = (bf16[4,256,512]{2,1,0:T(8,128)(2,1)S(1)}, bf16[4,256,512]{2,1,0:T(8,128)(2,1)S(1)}, u32[]{:S(2)}, u32[]{:S(2)}) collective-permute-start(bf16[4,256,512]{2,1,0:T(8,128)(2,1)S(1)} %pad_maximum_fusion.5.refs_5_.refs_13_), channel_id=1, source_target_pairs={{0,2},{1,3},{2,0},{3,1},{4,6},{5,7},{6,4},{7,5},{8,10},{9,11},{10,... | collective-permute-start | bytes 3145736 | tf_op jit(solution)/shard_map/ppermute | solution.py:372
  102.4 15.6 %collective-permute-start.22 = (bf16[256,512]{1,0:T(8,128)(2,1)S(1)}, bf16[256,512]{1,0:T(8,128)(2,1)S(1)}, u32[]{:S(2)}, u32[]{:S(2)}) collective-permute-start(bf16[256,512]{1,0:T(8,128)(2,1)S(1)} %get-tuple-element.44), channel_id=1, source_target_pairs={{0,4},{1,5},{2,6},{3,7},{4,8},{5,9},{6,10},{7,11},{8,12},{9,13},{1... | collective-permute-start | bytes 786440 | tf_op jit(solution)/shard_map/ppermute | solution.py:378
  102.4 22.3 %collective-permute-start.23 = (bf16[256,512]{1,0:T(8,128)(2,1)S(1)}, bf16[256,512]{1,0:T(8,128)(2,1)S(1)}, u32[]{:S(2)}, u32[]{:S(2)}) collective-permute-start(bf16[256,512]{1,0:T(8,128)(2,1)S(1)} %get-tuple-element.44), channel_id=1, source_target_pairs={{0,8},{1,9},{2,10},{3,11},{4,12},{5,13},{6,14},{7,15},{8,0},{9,1},... | collective-permute-start | bytes 786440 | tf_op jit(solution)/shard_map/ppermute | solution.py:378
  104.1 22.7 %collective-permute-start.24 = (bf16[256,512]{1,0:T(8,128)(2,1)S(1)}, bf16[256,512]{1,0:T(8,128)(2,1)S(1)}, u32[]{:S(2)}, u32[]{:S(2)}) collective-permute-start(bf16[256,512]{1,0:T(8,128)(2,1)S(1)} %get-tuple-element.44), channel_id=1, source_target_pairs={{0,12},{1,13},{2,14},{3,15},{4,0},{5,1},{6,2},{7,3},{8,4},{9,5},{1... | collective-permute-start | bytes 786440 | tf_op jit(solution)/shard_map/ppermute | solution.py:378
  137.3 25.2 %collective-permute-start.27 = (bf16[4,256,512]{2,1,0:T(8,128)(2,1)S(1)}, bf16[4,256,512]{2,1,0:T(8,128)(2,1)S(1)}, u32[]{:S(2)}, u32[]{:S(2)}) collective-permute-start(bf16[4,256,512]{2,1,0:T(8,128)(2,1)S(1)} %pad_maximum_fusion.7.refs_5_.refs_7_), channel_id=1, source_target_pairs={{0,2},{1,3},{2,0},{3,1},{4,6},{5,7},{6,4},{7,5},{8,10},{9,11},{10,... | collective-permute-start | bytes 3145736 | tf_op jit(solution)/shard_map/ppermute | solution.py:372
  140.6 36.5 %collective-permute-start.30 = (bf16[2,6,64,1024]{3,2,1,0:T(8,128)(2,1)S(1)}, bf16[2,6,64,1024]{3,2,1,0:T(8,128)(2,1)S(1)}, u32[]{:S(2)}, u32[]{:S(2)}) collective-permute-start(bf16[2,6,64,1024]{3,2,1,0:T(8,128)(2,1)S(1)} %pad_maximum_fusion.2), channel_id=1, source_target_pairs={{0,16},{16,0},{1,17},{17,1},{2,18},{18,2},{3,19},{19,3},{4,20},{20... | collective-permute-start | bytes 4718600 | tf_op jit(solution)/shard_map/ppermute | solution.py:375
  (21 other events, 141.5 us)

commit v14 on v13

--- a/solution.py
+++ b/solution.py
@@ -91,12 +91,13 @@
 
 
 def chunk_kernel(
-    offset, kind, units, chips, sorted_ref, place_ref, perm_ref, *refs
+    offset, kind, units, chips, sources, sorted_ref, place_ref, perm_ref, *refs
 ):
     first, last = kind
     parts = len(units)
+    arrays = 1 + max(i for block in sources for i, _ in block)
     tokens_of, refs = refs[: len(chips) + 1], refs[len(chips) + 1 :]
-    pieces, refs = refs[: 2 * parts], refs[2 * parts :]
+    here_refs, there_refs, refs = refs[:arrays], refs[arrays : 2 * arrays], refs[2 * arrays :]
     if first:
         *outs, tokens_ref, weights_ref, sems, lifted_ref, g_ref, act_ref, pre_ref = refs
     elif last:
@@ -125,15 +126,15 @@
                 copies.append(
                     pltpu.make_async_copy(ref, tokens_ref.at[2 * i + k], sems.at[len(copies)])
                 )
-        for part in range(parts):
-            n = units[part][1]
-            for to_y, (ref, start) in zip((y, 1 - y), pieces[2 * part : 2 * part + 2]):
-                for d in range(lines):
-                    from_z = lax.rem(z + lines - d, lines)
+        for at, block in enumerate(sources):
+            for d, (i, place) in enumerate(block):
+                from_z = lax.rem(z + lines - d, lines)
+                for to_y, ref in ((y, here_refs[i]), (1 - y, there_refs[i])):
+                    n = ref.shape[2]
                     copies.append(
                         pltpu.make_async_copy(
-                            ref.at[d, :, pl.ds(start, n)],
-                            weights_ref.at[from_z, to_y, :, pl.ds(starts[part], n)],
+                            ref.at[place],
+                            weights_ref.at[from_z, to_y, :, pl.ds(at * n, n)],
                             sems.at[len(copies)],
                         )
                     )
@@ -227,31 +228,27 @@
                 low += n
 
 
-def chunk(kind, blocks, chips, scalars, tokens_of, pieces, sums, outs=None, weight=1):
+def chunk(kind, blocks, chips, scalars, tokens_of, weights, sums, outs=None, weight=1):
     first, last = kind
     offset, number, per_block = blocks
+    units, here, there, sources = weights
     _, rows, seq, width = tokens_of[0].shape
-    units = [(member, n) for member, n, *_ in pieces]
-    lines, depth2, _ = pieces[0][2][0].shape
+    lines = len(sources[0])
+    depth2 = here[0].shape[1]
     hidden = sum(n for _, n in units)
     size = per_block * seq
 
     tok = pl.BlockSpec((size, width), lambda j, *_: (j, 0))
     hbm = pl.BlockSpec(memory_space=pl.ANY)
-    args = [*scalars, *(tokens_of[chip] for chip in chips), tokens_of[-1]]
-    specs = [hbm] * (len(chips) + 1)
-    starts = []
-    for _, _, *both in pieces:
-        args += [array for array, _ in both]
-        starts += [start for _, start in both]
-    specs += [hbm] * len(starts)
+    args = [*scalars, *(tokens_of[chip] for chip in chips), tokens_of[-1], *here, *there]
+    specs = [pl.BlockSpec(memory_space=pltpu.HBM)] * (len(chips) + 1) + [hbm] * (2 * len(here))
     alias = {}
     out_specs = [tok, tok]
     out_shape = [jax.ShapeDtypeStruct((number * size, width), F32)] * 2
     scratch = [
         pltpu.VMEM((2 * len(chips), 2, rows, seq, width), BF16),
         pltpu.VMEM((lines, 2, depth2, hidden), BF16),
-        pltpu.SemaphoreType.DMA((len(pieces) * 2 * lines + 2 * len(chips),)),
+        pltpu.SemaphoreType.DMA((len(sources) * 2 * lines + 2 * len(chips),)),
         pltpu.VMEM((size, width), BF16),
         pltpu.VMEM((size, width), BF16),
         pltpu.VMEM((size, hidden), BF16),
@@ -268,15 +265,8 @@
         out_specs = [pl.BlockSpec(shape, lambda *_: (0, 0, 0))] * len(out_shape)
         scratch += [pltpu.VMEM((size, width), F32)] * 2
 
-    def kernel(*refs):
-        refs = list(refs)
-        base = len(scalars) + len(chips) + 1
-        for i, start in enumerate(starts):
-            refs[base + i] = (refs[base + i], start)
-        chunk_kernel(offset, kind, units, chips, *refs)
-
     return pl.pallas_call(
-        kernel,
+        functools.partial(chunk_kernel, offset, kind, units, chips, sources),
         grid_spec=pltpu.PrefetchScalarGridSpec(
             num_scalar_prefetch=len(scalars),
             grid=(number,),
@@ -412,6 +402,7 @@
     theirs = partner(units_of(1 - core, both))
     shard = both_cores(units_of(core, both), theirs)
 
+    block = 2 * unit
     groups = [
         [(0, 0, 2 * unit)],
         [(0, 2 * unit, 4 * unit)],
@@ -419,33 +410,43 @@
         [(1, 3 * unit, 4 * unit)],
         [(0, quarter, half), (1, quarter, half)],
     ]
+    own_with = [[(0, 0), (1, 0), (1, 1), (2, 0)], [(2, 1)], [(3, 0)], [(3, 1)], [(4, 0), (4, 1)]]
     send = [shard_head[0]] + [
         jnp.concatenate([shard[m, :, at : at + n] for m, at, n in group], axis=1)
         for group in groups[1:]
     ]
-    here, there, shifted = [], [], []
+    here, there, shifted, held = [], [], [], {}
 
     def along_z(step, *waits):
-        results = []
-        for d in range(1, lines):
-            mine = send[step]
-            if step:
-                mine = after(mine, *shifted[-1], *waits)
-            results.append(shift_z(mine, d))
-        shifted.append(results)
-        here.append(jnp.stack([send[step], *results]))
+        mine = after(send[step], *shifted[-1], *waits) if step else send[0]
+        shifted.append([shift_z(mine, d) for d in range(1, lines)])
 
     def across_y(step, *waits):
+        blocks = []
+        for group, i in own_with[step]:
+            held[group, i, 0] = (step, len(blocks))
+            blocks.append(send[group][:, i * block : (i + 1) * block])
+        for d, rows_from in enumerate(shifted[step]):
+            for i in range(rows_from.shape[1] // block):
+                held[step, i, d + 1] = (step, len(blocks))
+                blocks.append(rows_from[:, i * block : (i + 1) * block])
+        here.append(jnp.stack(blocks))
         there.append(over_y(after(here[step], *there[-1:], *waits)))
 
-    def chunk_pieces(*at):
-        pieces = []
-        for group in at:
-            start = 0
-            for member, _, n in groups[group]:
-                pieces.append((member, n, (here[group], start), (there[group], start)))
-                start += n
-        return pieces
+    def weights_of(*which):
+        units = [(member, n) for group in which for member, _, n in groups[group]]
+        sources = [
+            [held[group, i, d] for d in range(lines)]
+            for group in which
+            for i in range(send[group].shape[1] // block)
+        ]
+        used = sorted(set(array for block in sources for array, _ in block))
+        return (
+            units,
+            [here[i] for i in used],
+            [there[i] for i in used],
+            [[(used.index(i), at) for i, at in block] for block in sources],
+        )
 
     per_block = math.gcd(2 * rows, 4)
     per_chip = 2 * rows // per_block
@@ -457,10 +458,11 @@
     for member in range(members):
         gain = jnp.where(pick_own[:, None] == member, norm_gain[member][None, :], gain)
     normed = x * (1.0 / jnp.sqrt(jnp.mean(x * x, axis=2, keepdims=True) + 1e-06))
-    near = jnp.stack([(normed * gain[:, None, :]).astype(BF16), upstream])
-    over = over_x(near)
-    along_z(1, pick_near, *send[2:])
+    lifted = (normed * gain[:, None, :]).astype(BF16)
+    near = jnp.stack([lifted, upstream])
+    lifted_over = over_x(lifted)
     across_y(0)
+    along_z(1)
     pick_far = partner(after(pick_near, shifted[0][-1]))
 
     perm, member_sorted = sort_rows(jnp.concatenate([pick_near[rows:], pick_far[rows:]]))
@@ -471,8 +473,9 @@
         jnp.concatenate([perm + 2 * rows, perm_own]),
     )
 
-    along_z(2, there[0], *scalars)
+    along_z(2, there[0], lifted_over, *scalars)
     across_y(1)
+    over = jnp.stack([lifted_over, over_x(after(upstream, there[0], *shifted[1]))])
     along_z(3, there[1], over)
     across_y(2)
     far = partner(after(jnp.stack([near, over]), *shifted[2], there[1]))
@@ -482,12 +485,12 @@
     other_rows, own_rows = (0, per_chip, per_block), (per_chip, per_chip, per_block)
     sums = chunk(
         (True, False), other_rows, (1,), scalars,
-        (near, after(over, *shifted[3]), far), chunk_pieces(0, 1, 2), None,
+        (near, after(over, *shifted[3]), far), weights_of(0, 1, 2), None,
     )
     across_y(4)
     sums = (after(sums[0], *shifted[4]), sums[1])
     *same, other_out, other_back = chunk(
-        (False, True), other_rows, (1,), scalars, tokens_of, chunk_pieces(3), sums,
+        (False, True), other_rows, (1,), scalars, tokens_of, weights_of(3), sums,
         (BF16, BF16), 0,
     )
     across = jnp.stack(
@@ -499,10 +502,10 @@
     tokens_of = (after(near, across), over, far)
     across = over_x(across)
     sums = chunk(
-        (True, False), own_rows, (0,), scalars, tokens_of, chunk_pieces(0, 1, 2, 3), None, None, 0
+        (True, False), own_rows, (0,), scalars, tokens_of, weights_of(0, 1, 2, 3), None, None, 0
     )
     out, back, packed_out, packed_back = chunk(
-        (False, True), own_rows, (0,), scalars, tokens_of, chunk_pieces(4), sums, (F32, BF16), 0
+        (False, True), own_rows, (0,), scalars, tokens_of, weights_of(4), sums, (F32, BF16), 0
     )
     return tuple(
         finish(

time: 180 us -> 181 us (level)
  waiting for transfers between devices: 84.9 us -> 79.4 us
  local copies, waits for them, and re-layouts: 9.45 us -> 14.7 us
    ppermute x15, waiting for transfers between devices: 67.6 us -> 56.5 us  [shift_z(): lax.ppermute(a, 'row', [(i, (i + 4 * d) % ranks) for i in range(ranks)])]
    ppermute x3 -> x4, waiting for transfers between devices: 7.71 us -> 16.6 us  [over_x(): return lax.ppermute(a, 'grp', [(0, 1), (1, 0)])]
    unnamed x28 -> x67, local copies, waits for them, and re-layouts: 6.73 us -> 11.3 us
    ppermute x15, starting transfers between devices: 24.8 us -> 20.3 us  [shift_z(): lax.ppermute(a, 'row', [(i, (i + 4 * d) % ranks) for i in range(ranks)])]
    ppermute x8, waiting for transfers between devices: 5.26 us -> 2.91 us  [partner(): return lax.ppermute(a, 'row', [(i, i ^ 1) for i in range(ranks)])]
    ppermute x3 -> x4, starting transfers between devices: 3.11 us -> 5.31 us  [over_x(): return lax.ppermute(a, 'grp', [(0, 1), (1, 0)])]
  transfers between devices with their start and end apart: 31 -> 32, of which waited for: 21 -> 19; matrix products, arithmetic and copies ran while one was open for 4% -> 7% of each run, Pallas kernels for 19% -> 20%
where the time goes in v14:
time: 181 us; the launch traced here: 180 us
  waiting for transfers between devices  79.4 us (44%)
  Pallas kernels  45.5 us (25%)
  starting transfers between devices  32.7 us (18%)
  local copies, waits for them, and re-layouts  14.7 us (8%)
  other arithmetic  6.81 us (4%)
    ppermute x15, waiting for transfers between devices, shift_z(): lax.ppermute(a, 'row', [(i, (i + 4 * d) % ranks) for i in range(ranks)])  56.5 us
    pallas_call x4, Pallas kernels, chunk(): pl.pallas_call(functools.partial(chunk_kernel, offset, kind, units, chips...  42.6 us
    ppermute x15, starting transfers between devices, shift_z(): lax.ppermute(a, 'row', [(i, (i + 4 * d) % ranks) for i in range(ranks)])  20.3 us
    ppermute x4, waiting for transfers between devices, over_x(): return lax.ppermute(a, 'grp', [(0, 1), (1, 0)])  16.6 us
    unnamed x67, local copies, waits for them, and re-layouts  11.3 us
    ppermute x5, starting transfers between devices, over_y(): return lax.ppermute(a, 'row', [(i, i ^ 2) for i in range(ranks)])  5.71 us
    ppermute x4, starting transfers between devices, over_x(): return lax.ppermute(a, 'grp', [(0, 1), (1, 0)])  5.31 us
  transfers between devices with their start and end apart: 32, of which 19 were waited for; matrix products, arithmetic and copies ran while one was open for 7% of the time, Pallas kernels for 20%

profile of v14, /device:TPU:8, one launch (start us, length us, event | category | flops | bytes accessed | tf_op | source)
XLA Modules:
  0.0 180.4 jit_solution(12321970648734118389)
XLA Ops:
  4.1 2.0 %collective-permute-start.4 = (bf16[256,256]{1,0:T(8,128)(2,1)S(1)}, bf16[256,256]{1,0:T(8,128)(2,1)S(1)}, u32[]{:S(2)}, u32[]{:S(2)}) collective-permute-start(bf16[256,256]{1,0:T(8,128)(2,1)S(1)} %bitcast.190), channel_id=1, source_target_pairs={{0,4},{1,5},{2,6},{3,7},{4,8},{5,9},{6,10},{7,11},{8,12},{9,13},{1... | collective-permute-start | bytes 393224 | tf_op jit(solution)/shard_map/ppermute | solution.py:368
  6.2 4.5 %collective-permute-start.7 = (bf16[256,256]{1,0:T(8,128)(2,1)S(1)}, bf16[256,256]{1,0:T(8,128)(2,1)S(1)}, u32[]{:S(2)}, u32[]{:S(2)}) collective-permute-start(bf16[256,256]{1,0:T(8,128)(2,1)S(1)} %bitcast.192), channel_id=1, source_target_pairs={{0,8},{1,9},{2,10},{3,11},{4,12},{5,13},{6,14},{7,15},{8,0},{9,1},... | collective-permute-start | bytes 393224 | tf_op jit(solution)/shard_map/ppermute | solution.py:368
  19.4 3.5 %collective-permute-start.10 = (bf16[256,512]{1,0:T(8,128)(2,1)S(1)}, bf16[256,512]{1,0:T(8,128)(2,1)S(1)}, u32[]{:S(2)}, u32[]{:S(2)}) collective-permute-start(bf16[256,512]{1,0:T(8,128)(2,1)S(1)} %get-tuple-element.36), channel_id=1, source_target_pairs={{0,8},{1,9},{2,10},{3,11},{4,12},{5,13},{6,14},{7,15},{8,0},{9,1},... | collective-permute-start | bytes 786440 | tf_op jit(solution)/shard_map/ppermute | solution.py:368
  24.8 3.7 %collective-permute-done.9 = bf16[256,512]{1,0:T(8,128)(2,1)S(1)} collective-permute-done((bf16[256,512]{1,0:T(8,128)(2,1)S(1)}, bf16[256,512]{1,0:T(8,128)(2,1)S(1)}, u32[]{:S(2)}, u32[]{:S(2)}) %collective-permute-start.9) | collective-permute-done | bytes 262176 | tf_op jit(solution)/shard_map/ppermute | solution.py:368
  28.6 13.9 %collective-permute-done.10 = bf16[256,512]{1,0:T(8,128)(2,1)S(1)} collective-permute-done((bf16[256,512]{1,0:T(8,128)(2,1)S(1)}, bf16[256,512]{1,0:T(8,128)(2,1)S(1)}, u32[]{:S(2)}, u32[]{:S(2)}) %collective-permute-start.10) | collective-permute-done | bytes 262176 | tf_op jit(solution)/shard_map/ppermute | solution.py:368
  42.4 3.4 %collective-permute-done.11 = bf16[256,512]{1,0:T(8,128)(2,1)S(1)} collective-permute-done((bf16[256,512]{1,0:T(8,128)(2,1)S(1)}, bf16[256,512]{1,0:T(8,128)(2,1)S(1)}, u32[]{:S(2)}, u32[]{:S(2)}) %collective-permute-start.11) | collective-permute-done | bytes 262176 | tf_op jit(solution)/shard_map/ppermute | solution.py:368
  49.4 2.1 %collective-permute-start.14 = (bf16[256,512]{1,0:T(8,128)(2,1)S(1)}, bf16[256,512]{1,0:T(8,128)(2,1)S(1)}, u32[]{:S(2)}, u32[]{:S(2)}) collective-permute-start(bf16[256,512]{1,0:T(8,128)(2,1)S(1)} %pad_maximum_fusion.7), channel_id=1, source_target_pairs={{0,8},{1,9},{2,10},{3,11},{4,12},{5,13},{6,14},{7,15},{8,0},{9,1},... | collective-permute-start | bytes 786440 | tf_op jit(solution)/shard_map/ppermute | solution.py:368
  51.5 13.6 %collective-permute-done.12 = bf16[6,64,1024]{2,1,0:T(8,128)(2,1)S(1)} collective-permute-done((bf16[6,64,1024]{2,1,0:T(8,128)(2,1)S(1)}, bf16[6,64,1024]{2,1,0:T(8,128)(2,1)S(1)}, u32[]{:S(2)}, u32[]{:S(2)}) %collective-permute-start.12) | collective-permute-done | bytes 786464 | tf_op jit(solution)/shard_map/ppermute | solution.py:365
  67.4 3.3 %collective-permute-done.14 = bf16[256,512]{1,0:T(8,128)(2,1)S(1)} collective-permute-done((bf16[256,512]{1,0:T(8,128)(2,1)S(1)}, bf16[256,512]{1,0:T(8,128)(2,1)S(1)}, u32[]{:S(2)}, u32[]{:S(2)}) %collective-permute-start.14) | collective-permute-done | bytes 262176 | tf_op jit(solution)/shard_map/ppermute | solution.py:368
  72.4 2.1 %collective-permute-start.19 = (bf16[256,512]{1,0:T(8,128)(2,1)S(1)}, bf16[256,512]{1,0:T(8,128)(2,1)S(1)}, u32[]{:S(2)}, u32[]{:S(2)}) collective-permute-start(bf16[256,512]{1,0:T(8,128)(2,1)S(1)} %get-tuple-element.41), channel_id=1, source_target_pairs={{0,8},{1,9},{2,10},{3,11},{4,12},{5,13},{6,14},{7,15},{8,0},{9,1},... | collective-permute-start | bytes 786440 | tf_op jit(solution)/shard_map/ppermute | solution.py:368
  74.4 2.0 %collective-permute-start.20 = (bf16[256,512]{1,0:T(8,128)(2,1)S(1)}, bf16[256,512]{1,0:T(8,128)(2,1)S(1)}, u32[]{:S(2)}, u32[]{:S(2)}) collective-permute-start(bf16[256,512]{1,0:T(8,128)(2,1)S(1)} %get-tuple-element.41), channel_id=1, source_target_pairs={{0,12},{1,13},{2,14},{3,15},{4,0},{5,1},{6,2},{7,3},{8,4},{9,5},{1... | collective-permute-start | bytes 786440 | tf_op jit(solution)/shard_map/ppermute | solution.py:368
  77.0 4.5 %collective-permute-done.18 = bf16[256,512]{1,0:T(8,128)(2,1)S(1)} collective-permute-done((bf16[256,512]{1,0:T(8,128)(2,1)S(1)}, bf16[256,512]{1,0:T(8,128)(2,1)S(1)}, u32[]{:S(2)}, u32[]{:S(2)}) %collective-permute-start.18) | collective-permute-done | bytes 262176 | tf_op jit(solution)/shard_map/ppermute | solution.py:368
  81.5 14.2 %collective-permute-done.19 = bf16[256,512]{1,0:T(8,128)(2,1)S(1)} collective-permute-done((bf16[256,512]{1,0:T(8,128)(2,1)S(1)}, bf16[256,512]{1,0:T(8,128)(2,1)S(1)}, u32[]{:S(2)}, u32[]{:S(2)}) %collective-permute-start.19) | collective-permute-done | bytes 262176 | tf_op jit(solution)/shard_map/ppermute | solution.py:368
  95.7 2.5 %collective-permute-done.20 = bf16[256,512]{1,0:T(8,128)(2,1)S(1)} collective-permute-done((bf16[256,512]{1,0:T(8,128)(2,1)S(1)}, bf16[256,512]{1,0:T(8,128)(2,1)S(1)}, u32[]{:S(2)}, u32[]{:S(2)}) %collective-permute-start.20) | collective-permute-done | bytes 262176 | tf_op jit(solution)/shard_map/ppermute | solution.py:368
  99.9 2.7 %collective-permute-start.24 = (bf16[256,512]{1,0:T(8,128)(2,1)S(1)}, bf16[256,512]{1,0:T(8,128)(2,1)S(1)}, u32[]{:S(2)}, u32[]{:S(2)}) collective-permute-start(bf16[256,512]{1,0:T(8,128)(2,1)S(1)} %pad_maximum_fusion.8), channel_id=1, source_target_pairs={{0,8},{1,9},{2,10},{3,11},{4,12},{5,13},{6,14},{7,15},{8,0},{9,1},... | collective-permute-start | bytes 786440 | tf_op jit(solution)/shard_map/ppermute | solution.py:368
  102.7 11.5 %chunk.4 = (f32[768,1024]{1,0:T(8,128)S(1)}, f32[768,1024]{1,0:T(8,128)S(1)}) custom-call(s32[24]{0:T(128)S(1)} %pad_add_fusion.3.sorted_ref, s32[2]{0:T(128)S(1)} %pad_add_fusion.4.place_ref, s32[24]{0:T(128)S(1)} %pad_add_fusion.5.perm_ref, bf16[2,6,64,1024]{3,2,1,0:T(8,128)(2,1)S(1)} %get-tuple-element.44.refs_0_, bf16[2,2,6,64,1024]{4,3,2,1,0:T(8,128)(2,1)} %copy-done, ...), custom_call_target="tpu_custom_call" | custom-call | flops 5368709120 | bytes 20971520 | tf_op jit(solution)/shard_map/chunk/pallas_call | solution.py:268
  117.6 4.6 %collective-permute-done.24 = bf16[256,512]{1,0:T(8,128)(2,1)S(1)} collective-permute-done((bf16[256,512]{1,0:T(8,128)(2,1)S(1)}, bf16[256,512]{1,0:T(8,128)(2,1)S(1)}, u32[]{:S(2)}, u32[]{:S(2)}) %collective-permute-start.24) | collective-permute-done | bytes 262176 | tf_op jit(solution)/shard_map/ppermute | solution.py:368
  122.2 2.3 %collective-permute-done.25 = bf16[256,512]{1,0:T(8,128)(2,1)S(1)} collective-permute-done((bf16[256,512]{1,0:T(8,128)(2,1)S(1)}, bf16[256,512]{1,0:T(8,128)(2,1)S(1)}, u32[]{:S(2)}, u32[]{:S(2)}) %collective-permute-start.25) | collective-permute-done | bytes 262176 | tf_op jit(solution)/shard_map/ppermute | solution.py:368
  126.4 6.7 %chunk.5 = (bf16[6,64,1024]{2,1,0:T(8,128)(2,1)S(1)}, bf16[6,64,1024]{2,1,0:T(8,128)(2,1)S(1)}, bf16[6,64,1024]{2,1,0:T(8,128)(2,1)S(1)}, bf16[6,64,1024]{2,1,0:T(8,128)(2,1)S(1)}) custom-call(s32[24]{0:T(128)S(1)} %pad_add_fusion.3.sorted_ref, s32[2]{0:T(128)S(1)} %pad_add_fusion.4.place_ref, s32[24]{0:T(128)S(1)} %pad_add_fusion.5.perm_ref, ...), custom_call_target="tpu_custom_call" | custom-call | tf_op jit(solution)/shard_map/chunk/pallas_call | solution.py:268
  142.6 15.6 %chunk.6 = (f32[768,1024]{1,0:T(8,128)S(1)}, f32[768,1024]{1,0:T(8,128)}) custom-call(s32[24]{0:T(128)S(1)} %pad_add_fusion.3.sorted_ref, s32[2]{0:T(128)S(1)} %pad_add_fusion.4.place_ref, s32[24]{0:T(128)S(1)} %pad_add_fusion.5.perm_ref, bf16[2,6,64,1024]{3,2,1,0:T(8,128)(2,1)S(1)} %get-tuple-element.53.refs_0_, bf16[2,2,6,64,1024]{4,3,2,1,0:T(8,128)(2,1)} %copy-done, ...), custom_call_target="tpu_custom_call" | custom-call | tf_op jit(solution)/shard_map/chunk/pallas_call | solution.py:268
  159.9 3.1 %collective-permute-done.28.refs_3_ = bf16[8,256,256]{2,1,0:T(8,128)(2,1)S(1)} collective-permute-done((bf16[8,256,256]{2,1,0:T(8,128)(2,1)}, bf16[8,256,256]{2,1,0:T(8,128)(2,1)S(1)}, u32[]{:S(2)}, u32[]{:S(2)}) %collective-permute-start.28) | collective-permute-done | bytes 1048608 | tf_op jit(solution)/shard_map/ppermute | solution.py:362
  163.0 8.8 %chunk.7 = (f32[6,64,1024]{2,1,0:T(8,128)S(1)}, f32[6,64,1024]{2,1,0:T(8,128)S(1)}, bf16[6,64,1024]{2,1,0:T(8,128)(2,1)S(1)}, bf16[6,64,1024]{2,1,0:T(8,128)(2,1)S(1)}) custom-call(s32[24]{0:T(128)S(1)} %pad_add_fusion.3.sorted_ref, s32[2]{0:T(128)S(1)} %pad_add_fusion.4.place_ref, s32[24]{0:T(128)S(1)} %pad_add_fusion.5.perm_ref, ...), custom_call_target="tpu_custom_call" | custom-call | tf_op jit(solution)/shard_map/chunk/pallas_call | solution.py:268
  175.3 2.2 %collective-permute-done.31.across_ref = bf16[2,6,64,1024]{3,2,1,0:T(8,128)(2,1)S(1)} collective-permute-done((bf16[2,6,64,1024]{3,2,1,0:T(8,128)(2,1)}, bf16[2,6,64,1024]{3,2,1,0:T(8,128)(2,1)S(1)}, u32[]{:S(2)}, u32[]{:S(2)}) %collective-permute-start.31) | collective-permute-done | bytes 1572896 | tf_op jit(solution)/shard_map/ppermute | solution.py:365
  177.5 2.9 %finish.1 = (bf16[6,64,1024]{2,1,0:T(8,128)(2,1)}, bf16[6,64,1024]{2,1,0:T(8,128)(2,1)}, f32[6,64]{1,0:T(8,128)}) custom-call(s32[6]{0:T(128)S(1)} %bitcast.177, bf16[6,64,1024]{2,1,0:T(8,128)(2,1)S(1)} %copy-done.3, bf16[6,64,1024]{2,1,0:T(8,128)(2,1)S(1)} %copy-done.4, f32[2,1024]{1,0:T(2,128)S(1)} %copy-done.16, ...), custom_call_target="tpu_custom_call" | custom-call | tf_op jit(solution)/shard_map/finish/pallas_call | solution.py:318
  (159 shorter events, 43.4 us)
Async XLA Ops:
  4.1 12.0 %collective-permute-start.2 = (bf16[256,256]{1,0:T(8,128)(2,1)S(1)}, bf16[256,256]{1,0:T(8,128)(2,1)S(1)}, u32[]{:S(2)}, u32[]{:S(2)}) collective-permute-start(bf16[256,256]{1,0:T(8,128)(2,1)S(1)} %bitcast.189), channel_id=1, source_target_pairs={{0,12},{1,13},{2,14},{3,15},{4,0},{5,1},{6,2},{7,3},{8,4},{9,5},{1... | collective-permute-start | bytes 393224 | tf_op jit(solution)/shard_map/ppermute | solution.py:368
  4.1 11.2 %collective-permute-start.4 = (bf16[256,256]{1,0:T(8,128)(2,1)S(1)}, bf16[256,256]{1,0:T(8,128)(2,1)S(1)}, u32[]{:S(2)}, u32[]{:S(2)}) collective-permute-start(bf16[256,256]{1,0:T(8,128)(2,1)S(1)} %bitcast.190), channel_id=1, source_target_pairs={{0,4},{1,5},{2,6},{3,7},{4,8},{5,9},{6,10},{7,11},{8,12},{9,13},{1... | collective-permute-start | bytes 393224 | tf_op jit(solution)/shard_map/ppermute | solution.py:368
  6.2 13.1 %collective-permute-start.7 = (bf16[256,256]{1,0:T(8,128)(2,1)S(1)}, bf16[256,256]{1,0:T(8,128)(2,1)S(1)}, u32[]{:S(2)}, u32[]{:S(2)}) collective-permute-start(bf16[256,256]{1,0:T(8,128)(2,1)S(1)} %bitcast.192), channel_id=1, source_target_pairs={{0,8},{1,9},{2,10},{3,11},{4,12},{5,13},{6,14},{7,15},{8,0},{9,1},... | collective-permute-start | bytes 393224 | tf_op jit(solution)/shard_map/ppermute | solution.py:368
  16.2 32.4 %collective-permute-start.5 = (bf16[6,64,1024]{2,1,0:T(8,128)(2,1)S(1)}, bf16[6,64,1024]{2,1,0:T(8,128)(2,1)S(1)}, u32[]{:S(2)}, u32[]{:S(2)}) collective-permute-start(bf16[6,64,1024]{2,1,0:T(8,128)(2,1)S(1)} %fusion.2), channel_id=1, source_target_pairs={{0,16},{16,0},{1,17},{17,1},{2,18},{18,2},{3,19},{19,3},{4,20},{20... | collective-permute-start | bytes 2359304 | tf_op jit(solution)/shard_map/ppermute | solution.py:365
  19.3 9.2 %collective-permute-start.9 = (bf16[256,512]{1,0:T(8,128)(2,1)S(1)}, bf16[256,512]{1,0:T(8,128)(2,1)S(1)}, u32[]{:S(2)}, u32[]{:S(2)}) collective-permute-start(bf16[256,512]{1,0:T(8,128)(2,1)S(1)} %get-tuple-element.36), channel_id=1, source_target_pairs={{0,4},{1,5},{2,6},{3,7},{4,8},{5,9},{6,10},{7,11},{8,12},{9,13},{1... | collective-permute-start | bytes 786440 | tf_op jit(solution)/shard_map/ppermute | solution.py:368
  19.4 23.0 %collective-permute-start.10 = (bf16[256,512]{1,0:T(8,128)(2,1)S(1)}, bf16[256,512]{1,0:T(8,128)(2,1)S(1)}, u32[]{:S(2)}, u32[]{:S(2)}) collective-permute-start(bf16[256,512]{1,0:T(8,128)(2,1)S(1)} %get-tuple-element.36), channel_id=1, source_target_pairs={{0,8},{1,9},{2,10},{3,11},{4,12},{5,13},{6,14},{7,15},{8,0},{9,1},... | collective-permute-start | bytes 786440 | tf_op jit(solution)/shard_map/ppermute | solution.py:368
  22.8 23.0 %collective-permute-start.11 = (bf16[256,512]{1,0:T(8,128)(2,1)S(1)}, bf16[256,512]{1,0:T(8,128)(2,1)S(1)}, u32[]{:S(2)}, u32[]{:S(2)}) collective-permute-start(bf16[256,512]{1,0:T(8,128)(2,1)S(1)} %get-tuple-element.36), channel_id=1, source_target_pairs={{0,12},{1,13},{2,14},{3,15},{4,0},{5,1},{6,2},{7,3},{8,4},{9,5},{1... | collective-permute-start | bytes 786440 | tf_op jit(solution)/shard_map/ppermute | solution.py:368
  23.2 22.6 %collective-permute-start.8 = (bf16[7,256,256]{2,1,0:T(8,128)(2,1)S(1)}, bf16[7,256,256]{2,1,0:T(8,128)(2,1)S(1)}, u32[]{:S(2)}, u32[]{:S(2)}) collective-permute-start(bf16[7,256,256]{2,1,0:T(8,128)(2,1)S(1)} %bitcast_dynamic-update-slice_fusion.refs_2_), channel_id=1, source_target_pairs={{0,2},{1,3},{2,0},{3,1},{4,6},{5,7},{6,4},{7,5},{8,10},{9,11},{10,... | collective-permute-start | bytes 2752520 | tf_op jit(solution)/shard_map/ppermute | solution.py:362
  45.9 19.3 %collective-permute-start.12 = (bf16[6,64,1024]{2,1,0:T(8,128)(2,1)S(1)}, bf16[6,64,1024]{2,1,0:T(8,128)(2,1)S(1)}, u32[]{:S(2)}, u32[]{:S(2)}) collective-permute-start(bf16[6,64,1024]{2,1,0:T(8,128)(2,1)S(1)} %copy-done.4), channel_id=1, source_target_pairs={{0,16},{16,0},{1,17},{17,1},{2,18},{18,2},{3,19},{19,3},{4,20},{20... | collective-permute-start | bytes 2359304 | tf_op jit(solution)/shard_map/ppermute | solution.py:365
  46.8 25.4 %collective-permute-start.16 = (bf16[7,256,256]{2,1,0:T(8,128)(2,1)S(1)}, bf16[7,256,256]{2,1,0:T(8,128)(2,1)S(1)}, u32[]{:S(2)}, u32[]{:S(2)}) collective-permute-start(bf16[7,256,256]{2,1,0:T(8,128)(2,1)S(1)} %fusion.32.refs_3_), channel_id=1, source_target_pairs={{0,2},{1,3},{2,0},{3,1},{4,6},{5,7},{6,4},{7,5},{8,10},{9,11},{10,... | collective-permute-start | bytes 2752520 | tf_op jit(solution)/shard_map/ppermute | solution.py:362
  48.6 18.8 %collective-permute-start.13 = (bf16[256,512]{1,0:T(8,128)(2,1)S(1)}, bf16[256,512]{1,0:T(8,128)(2,1)S(1)}, u32[]{:S(2)}, u32[]{:S(2)}) collective-permute-start(bf16[256,512]{1,0:T(8,128)(2,1)S(1)} %pad_maximum_fusion.7), channel_id=1, source_target_pairs={{0,4},{1,5},{2,6},{3,7},{4,8},{5,9},{6,10},{7,11},{8,12},{9,13},{1... | collective-permute-start | bytes 786440 | tf_op jit(solution)/shard_map/ppermute | solution.py:368
  49.4 21.3 %collective-permute-start.14 = (bf16[256,512]{1,0:T(8,128)(2,1)S(1)}, bf16[256,512]{1,0:T(8,128)(2,1)S(1)}, u32[]{:S(2)}, u32[]{:S(2)}) collective-permute-start(bf16[256,512]{1,0:T(8,128)(2,1)S(1)} %pad_maximum_fusion.7), channel_id=1, source_target_pairs={{0,8},{1,9},{2,10},{3,11},{4,12},{5,13},{6,14},{7,15},{8,0},{9,1},... | collective-permute-start | bytes 786440 | tf_op jit(solution)/shard_map/ppermute | solution.py:368
  51.5 20.7 %collective-permute-start.15 = (bf16[256,512]{1,0:T(8,128)(2,1)S(1)}, bf16[256,512]{1,0:T(8,128)(2,1)S(1)}, u32[]{:S(2)}, u32[]{:S(2)}) collective-permute-start(bf16[256,512]{1,0:T(8,128)(2,1)S(1)} %pad_maximum_fusion.7), channel_id=1, source_target_pairs={{0,12},{1,13},{2,14},{3,15},{4,0},{5,1},{6,2},{7,3},{8,4},{9,5},{1... | collective-permute-start | bytes 786440 | tf_op jit(solution)/shard_map/ppermute | solution.py:368
  72.2 27.4 %collective-permute-start.17 = (bf16[2,2,6,64,1024]{4,3,2,1,0:T(8,128)(2,1)S(1)}, bf16[2,2,6,64,1024]{4,3,2,1,0:T(8,128)(2,1)S(1)}, u32[]{:S(2)}, u32[]{:S(2)}) collective-permute-start(bf16[2,2,6,64,1024]{4,3,2,1,0:T(8,128)(2,1)S(1)} %pad_maximum_fusion), channel_id=1, source_target_pairs={{0,1},{1,0},{2,3},{3,2},{4,5},{5,4},{6,7},{7,6},{8,9},{9,8},{10,11... | collective-permute-start | bytes 9437192 | tf_op jit(solution)/shard_map/ppermute | solution.py:359
  72.3 9.2 %collective-permute-start.18 = (bf16[256,512]{1,0:T(8,128)(2,1)S(1)}, bf16[256,512]{1,0:T(8,128)(2,1)S(1)}, u32[]{:S(2)}, u32[]{:S(2)}) collective-permute-start(bf16[256,512]{1,0:T(8,128)(2,1)S(1)} %get-tuple-element.41), channel_id=1, source_target_pairs={{0,4},{1,5},{2,6},{3,7},{4,8},{5,9},{6,10},{7,11},{8,12},{9,13},{1... | collective-permute-start | bytes 786440 | tf_op jit(solution)/shard_map/ppermute | solution.py:368
  72.4 23.3 %collective-permute-start.19 = (bf16[256,512]{1,0:T(8,128)(2,1)S(1)}, bf16[256,512]{1,0:T(8,128)(2,1)S(1)}, u32[]{:S(2)}, u32[]{:S(2)}) collective-permute-start(bf16[256,512]{1,0:T(8,128)(2,1)S(1)} %get-tuple-element.41), channel_id=1, source_target_pairs={{0,8},{1,9},{2,10},{3,11},{4,12},{5,13},{6,14},{7,15},{8,0},{9,1},... | collective-permute-start | bytes 786440 | tf_op jit(solution)/shard_map/ppermute | solution.py:368
  74.4 23.7 %collective-permute-start.20 = (bf16[256,512]{1,0:T(8,128)(2,1)S(1)}, bf16[256,512]{1,0:T(8,128)(2,1)S(1)}, u32[]{:S(2)}, u32[]{:S(2)}) collective-permute-start(bf16[256,512]{1,0:T(8,128)(2,1)S(1)} %get-tuple-element.41), channel_id=1, source_target_pairs={{0,12},{1,13},{2,14},{3,15},{4,0},{5,1},{6,2},{7,3},{8,4},{9,5},{1... | collective-permute-start | bytes 786440 | tf_op jit(solution)/shard_map/ppermute | solution.py:368
  76.5 21.9 %collective-permute-start.21 = (bf16[7,256,256]{2,1,0:T(8,128)(2,1)S(1)}, bf16[7,256,256]{2,1,0:T(8,128)(2,1)S(1)}, u32[]{:S(2)}, u32[]{:S(2)}) collective-permute-start(bf16[7,256,256]{2,1,0:T(8,128)(2,1)S(1)} %fusion.25.refs_4_.refs_2_), channel_id=1, source_target_pairs={{0,2},{1,3},{2,0},{3,1},{4,6},{5,7},{6,4},{7,5},{8,10},{9,11},{10,... | collective-permute-start | bytes 2752520 | tf_op jit(solution)/shard_map/ppermute | solution.py:362
  98.4 26.2 %collective-permute-start.22 = (bf16[7,256,256]{2,1,0:T(8,128)(2,1)S(1)}, bf16[7,256,256]{2,1,0:T(8,128)(2,1)S(1)}, u32[]{:S(2)}, u32[]{:S(2)}) collective-permute-start(bf16[7,256,256]{2,1,0:T(8,128)(2,1)S(1)} %fusion.18.refs_3_.refs_5_), channel_id=1, source_target_pairs={{0,2},{1,3},{2,0},{3,1},{4,6},{5,7},{6,4},{7,5},{8,10},{9,11},{10,... | collective-permute-start | bytes 2752520 | tf_op jit(solution)/shard_map/ppermute | solution.py:362
  99.6 18.0 %collective-permute-start.23 = (bf16[256,512]{1,0:T(8,128)(2,1)S(1)}, bf16[256,512]{1,0:T(8,128)(2,1)S(1)}, u32[]{:S(2)}, u32[]{:S(2)}) collective-permute-start(bf16[256,512]{1,0:T(8,128)(2,1)S(1)} %pad_maximum_fusion.8), channel_id=1, source_target_pairs={{0,4},{1,5},{2,6},{3,7},{4,8},{5,9},{6,10},{7,11},{8,12},{9,13},{1... | collective-permute-start | bytes 786440 | tf_op jit(solution)/shard_map/ppermute | solution.py:368
  99.9 22.3 %collective-permute-start.24 = (bf16[256,512]{1,0:T(8,128)(2,1)S(1)}, bf16[256,512]{1,0:T(8,128)(2,1)S(1)}, u32[]{:S(2)}, u32[]{:S(2)}) collective-permute-start(bf16[256,512]{1,0:T(8,128)(2,1)S(1)} %pad_maximum_fusion.8), channel_id=1, source_target_pairs={{0,8},{1,9},{2,10},{3,11},{4,12},{5,13},{6,14},{7,15},{8,0},{9,1},... | collective-permute-start | bytes 786440 | tf_op jit(solution)/shard_map/ppermute | solution.py:368
  102.7 21.9 %collective-permute-start.25 = (bf16[256,512]{1,0:T(8,128)(2,1)S(1)}, bf16[256,512]{1,0:T(8,128)(2,1)S(1)}, u32[]{:S(2)}, u32[]{:S(2)}) collective-permute-start(bf16[256,512]{1,0:T(8,128)(2,1)S(1)} %pad_maximum_fusion.8), channel_id=1, source_target_pairs={{0,12},{1,13},{2,14},{3,15},{4,0},{5,1},{6,2},{7,3},{8,4},{9,5},{1... | collective-permute-start | bytes 786440 | tf_op jit(solution)/shard_map/ppermute | solution.py:368
  137.7 25.4 %collective-permute-start.28 = (bf16[8,256,256]{2,1,0:T(8,128)(2,1)}, bf16[8,256,256]{2,1,0:T(8,128)(2,1)S(1)}, u32[]{:S(2)}, u32[]{:S(2)}) collective-permute-start(bf16[8,256,256]{2,1,0:T(8,128)(2,1)} %fusion.12.refs_2_), channel_id=1, source_target_pairs={{0,2},{1,3},{2,0},{3,1},{4,6},{5,7},{6,4},{7,5},{8,10},{9,11},{10,... | collective-permute-start | bytes 3145736 | tf_op jit(solution)/shard_map/ppermute | solution.py:362
  141.2 36.3 %collective-permute-start.31 = (bf16[2,6,64,1024]{3,2,1,0:T(8,128)(2,1)}, bf16[2,6,64,1024]{3,2,1,0:T(8,128)(2,1)S(1)}, u32[]{:S(2)}, u32[]{:S(2)}) collective-permute-start(bf16[2,6,64,1024]{3,2,1,0:T(8,128)(2,1)} %pad_maximum_fusion.3), channel_id=1, source_target_pairs={{0,16},{16,0},{1,17},{17,1},{2,18},{18,2},{3,19},{19,3},{4,20},{20... | collective-permute-start | bytes 4718600 | tf_op jit(solution)/shard_map/ppermute | solution.py:365
  (28 other events, 333.2 us)

commit v15 on v14

--- a/solution.py
+++ b/solution.py
@@ -85,7 +85,7 @@
     )
 
 
-VMEM_LIMIT = 40 * 1024 * 1024
+VMEM_LIMIT = 20 * 1024 * 1024
 BF16 = jnp.bfloat16
 F32 = jnp.float32
 
@@ -95,7 +95,7 @@
 ):
     first, last = kind
     parts = len(units)
-    arrays = 1 + max(i for block in sources for i, _ in block)
+    arrays = 1 + max(source[0] for source in sources)
     tokens_of, refs = refs[: len(chips) + 1], refs[len(chips) + 1 :]
     here_refs, there_refs, refs = refs[:arrays], refs[arrays : 2 * arrays], refs[2 * arrays :]
     if first:
@@ -126,18 +126,13 @@
                 copies.append(
                     pltpu.make_async_copy(ref, tokens_ref.at[2 * i + k], sems.at[len(copies)])
                 )
-        for at, block in enumerate(sources):
-            for d, (i, place) in enumerate(block):
-                from_z = lax.rem(z + lines - d, lines)
-                for to_y, ref in ((y, here_refs[i]), (1 - y, there_refs[i])):
-                    n = ref.shape[2]
-                    copies.append(
-                        pltpu.make_async_copy(
-                            ref.at[place],
-                            weights_ref.at[from_z, to_y, :, pl.ds(at * n, n)],
-                            sems.at[len(copies)],
-                        )
-                    )
+        for i, start, d, to_row, to_unit, n, wide in sources:
+            from_z = lax.rem(z + lines - d, lines)
+            for to_y, ref in ((y, here_refs[i]), (1 - y, there_refs[i])):
+                to = weights_ref.at[from_z, to_y, pl.ds(to_row, n), pl.ds(to_unit, wide)]
+                copies.append(
+                    pltpu.make_async_copy(ref.at[pl.ds(start, n)], to, sems.at[len(copies)])
+                )
         for copy in copies:
             copy.start()
         for copy in copies:
@@ -231,10 +226,8 @@
 def chunk(kind, blocks, chips, scalars, tokens_of, weights, sums, outs=None, weight=1):
     first, last = kind
     offset, number, per_block = blocks
-    units, here, there, sources = weights
+    units, lines, depth2, here, there, sources = weights
     _, rows, seq, width = tokens_of[0].shape
-    lines = len(sources[0])
-    depth2 = here[0].shape[1]
     hidden = sum(n for _, n in units)
     size = per_block * seq
 
@@ -248,7 +241,7 @@
     scratch = [
         pltpu.VMEM((2 * len(chips), 2, rows, seq, width), BF16),
         pltpu.VMEM((lines, 2, depth2, hidden), BF16),
-        pltpu.SemaphoreType.DMA((len(sources) * 2 * lines + 2 * len(chips),)),
+        pltpu.SemaphoreType.DMA((2 * len(sources) + 2 * len(chips),)),
         pltpu.VMEM((size, width), BF16),
         pltpu.VMEM((size, width), BF16),
         pltpu.VMEM((size, hidden), BF16),
@@ -398,11 +391,10 @@
 
     head_theirs = partner(head_of(1 - core))
     shard_head = both_cores(head_of(core), head_theirs)
-    both = jnp.stack([after(up_proj, shard_head), down_proj], axis=1)
-    theirs = partner(units_of(1 - core, both))
+    both = jnp.stack([after(up_proj, shard_head), after(down_proj, shard_head)], axis=1)
+    theirs = partner(after(units_of(1 - core, both), shard_head))
     shard = both_cores(units_of(core, both), theirs)
 
-    block = 2 * unit
     groups = [
         [(0, 0, 2 * unit)],
         [(0, 2 * unit, 4 * unit)],
@@ -410,43 +402,62 @@
         [(1, 3 * unit, 4 * unit)],
         [(0, quarter, half), (1, quarter, half)],
     ]
-    own_with = [[(0, 0), (1, 0), (1, 1), (2, 0)], [(2, 1)], [(3, 0)], [(3, 1)], [(4, 0), (4, 1)]]
-    send = [shard_head[0]] + [
-        jnp.concatenate([shard[m, :, at : at + n] for m, at, n in group], axis=1)
-        for group in groups[1:]
+    own_rows = 4 * depth
+    own_with = [
+        [(0, 0, own_rows), (1, 0, own_rows), (2, 0, own_rows // 2)],
+        [(2, own_rows // 2, own_rows // 2)],
+        [(3, 0, own_rows // 2)],
+        [(3, own_rows // 2, own_rows // 2)],
+        [(4, 0, own_rows)],
     ]
-    here, there, shifted, held = [], [], [], {}
+
+    def own(group, row, n, first=0, wide=None):
+        parts = []
+        last = first + (wide or sum(k for _, _, k in groups[group]))
+        at = 0
+        for member, start, k in groups[group]:
+            low, high = max(first, at), min(last, at + k)
+            if low < high:
+                parts.append(shard[member, row : row + n, start + low - at : start + high - at])
+            at += k
+        return jnp.concatenate(parts, axis=1)
+
+    send = [shard_head[0]] + [own(group, 0, own_rows) for group in range(1, len(groups))]
+    here, there, shifted, held = [], [], [], [[] for _ in groups]
 
     def along_z(step, *waits):
         mine = after(send[step], *shifted[-1], *waits) if step else send[0]
         shifted.append([shift_z(mine, d) for d in range(1, lines)])
 
     def across_y(step, *waits):
-        blocks = []
-        for group, i in own_with[step]:
-            held[group, i, 0] = (step, len(blocks))
-            blocks.append(send[group][:, i * block : (i + 1) * block])
+        wide = send[step].shape[1]
+        parts = []
+
+        def add(array, group, d, row, first):
+            start = sum(a.shape[0] for a in parts)
+            held[group].append((step, start, d, row, first, array.shape[0], wide))
+            parts.append(array)
+
+        for group, row, n in own_with[step]:
+            for first in range(0, send[group].shape[1], wide):
+                mine = send[0] if group == 0 else own(group, row, n, first, wide)
+                add(mine, group, 0, row, first)
         for d, rows_from in enumerate(shifted[step]):
-            for i in range(rows_from.shape[1] // block):
-                held[step, i, d + 1] = (step, len(blocks))
-                blocks.append(rows_from[:, i * block : (i + 1) * block])
-        here.append(jnp.stack(blocks))
+            add(rows_from, step, d + 1, 0, 0)
+        here.append(jnp.concatenate(parts))
         there.append(over_y(after(here[step], *there[-1:], *waits)))
 
     def weights_of(*which):
         units = [(member, n) for group in which for member, _, n in groups[group]]
-        sources = [
-            [held[group, i, d] for d in range(lines)]
-            for group in which
-            for i in range(send[group].shape[1] // block)
-        ]
-        used = sorted(set(array for block in sources for array, _ in block))
-        return (
-            units,
-            [here[i] for i in used],
-            [there[i] for i in used],
-            [[(used.index(i), at) for i, at in block] for block in sources],
-        )
+        used = sorted(set(source[0] for group in which for source in held[group]))
+        sources = []
+        at = 0
+        for group in which:
+            for i, start, d, row, first, n, wide in held[group]:
+                sources.append((used.index(i), start, d, row, at + first, n, wide))
+            at += send[group].shape[1]
+        arrays = [here[i] for i in used], [there[i] for i in used]
+        return units, lines, own_rows, *arrays, sources
 
     per_block = math.gcd(2 * rows, 4)
     per_chip = 2 * rows // per_block
@@ -482,15 +493,15 @@
     along_z(4, there[2], far)
     across_y(3)
     tokens_of = (near, over, far)
-    other_rows, own_rows = (0, per_chip, per_block), (per_chip, per_chip, per_block)
+    over_blocks, own_blocks = (0, per_chip, per_block), (per_chip, per_chip, per_block)
     sums = chunk(
-        (True, False), other_rows, (1,), scalars,
+        (True, False), over_blocks, (1,), scalars,
         (near, after(over, *shifted[3]), far), weights_of(0, 1, 2), None,
     )
     across_y(4)
     sums = (after(sums[0], *shifted[4]), sums[1])
     *same, other_out, other_back = chunk(
-        (False, True), other_rows, (1,), scalars, tokens_of, weights_of(3), sums,
+        (False, True), over_blocks, (1,), scalars, tokens_of, weights_of(3), sums,
         (BF16, BF16), 0,
     )
     across = jnp.stack(
@@ -502,10 +513,10 @@
     tokens_of = (after(near, across), over, far)
     across = over_x(across)
     sums = chunk(
-        (True, False), own_rows, (0,), scalars, tokens_of, weights_of(0, 1, 2, 3), None, None, 0
+        (True, False), own_blocks, (0,), scalars, tokens_of, weights_of(0, 1, 2, 3), None, None, 0
     )
     out, back, packed_out, packed_back = chunk(
-        (False, True), own_rows, (0,), scalars, tokens_of, weights_of(4), sums, (F32, BF16), 0
+        (False, True), own_blocks, (0,), scalars, tokens_of, weights_of(4), sums, (F32, BF16), 0
     )
     return tuple(
         finish(

time: 181 us -> 175 us (0.967)
  local copies, waits for them, and re-layouts: 14.7 us -> 2.83 us
  waiting for transfers between devices: 79.4 us -> 86.7 us
  Pallas kernels: 45.5 us -> 38.8 us
  starting transfers between devices: 32.7 us -> 37.8 us
    unnamed x67 -> x18, local copies, waits for them, and re-layouts: 11.3 us -> 0.1 us
    pallas_call x4, Pallas kernels: 42.6 us -> 35.9 us  [chunk(): pl.pallas_call(functools.partial(chunk_kernel, offset, kind, units, chips...]
    ppermute x4, waiting for transfers between devices: 16.6 us -> 20.9 us  [over_x(): return lax.ppermute(a, 'grp', [(0, 1), (1, 0)])]
    ppermute x5, waiting for transfers between devices: 3.29 us -> 6.77 us  [over_y(): return lax.ppermute(a, 'row', [(i, i ^ 2) for i in range(ranks)])]
    ppermute x15, starting transfers between devices: 20.3 us -> 23 us  [shift_z(): lax.ppermute(a, 'row', [(i, (i + 4 * d) % ranks) for i in range(ranks)])]
  transfers between devices with their start and end apart: 32 -> 32, of which waited for: 19 -> 17; matrix products, arithmetic and copies ran while one was open for 7% -> 4% of each run, Pallas kernels for 20% -> 18%
where the time goes in v15:
time: 175 us; the launch traced here: 173 us
  waiting for transfers between devices  86.7 us (50%)
  Pallas kernels  38.8 us (22%)
  starting transfers between devices  37.8 us (22%)
  other arithmetic  5.91 us (3%)
  local copies, waits for them, and re-layouts  2.83 us (2%)
    ppermute x15, waiting for transfers between devices, shift_z(): lax.ppermute(a, 'row', [(i, (i + 4 * d) % ranks) for i in range(ranks)])  56.2 us
    pallas_call x4, Pallas kernels, chunk(): pl.pallas_call(functools.partial(chunk_kernel, offset, kind, units, chips...  35.9 us
    ppermute x15, starting transfers between devices, shift_z(): lax.ppermute(a, 'row', [(i, (i + 4 * d) % ranks) for i in range(ranks)])  23 us
    ppermute x4, waiting for transfers between devices, over_x(): return lax.ppermute(a, 'grp', [(0, 1), (1, 0)])  20.9 us
    ppermute x5, starting transfers between devices, over_y(): return lax.ppermute(a, 'row', [(i, i ^ 2) for i in range(ranks)])  7.4 us
    ppermute x5, waiting for transfers between devices, over_y(): return lax.ppermute(a, 'row', [(i, i ^ 2) for i in range(ranks)])  6.77 us
    ppermute x4, starting transfers between devices, over_x(): return lax.ppermute(a, 'grp', [(0, 1), (1, 0)])  6.03 us
  transfers between devices with their start and end apart: 32, of which 17 were waited for; matrix products, arithmetic and copies ran while one was open for 4% of the time, Pallas kernels for 18%

profile of v15, /device:TPU:8, one launch (start us, length us, event | category | flops | bytes accessed | tf_op | source)
XLA Modules:
  0.0 173.2 jit_solution(8777204143715321495)
XLA Ops:
  6.2 4.5 %collective-permute-start.7 = (bf16[256,256]{1,0:T(8,128)(2,1)S(1)}, bf16[256,256]{1,0:T(8,128)(2,1)S(1)}, u32[]{:S(2)}, u32[]{:S(2)}) collective-permute-start(bf16[256,256]{1,0:T(8,128)(2,1)S(1)} %bitcast.95), channel_id=1, source_target_pairs={{0,8},{1,9},{2,10},{3,11},{4,12},{5,13},{6,14},{7,15},{8,0},{9,1},... | collective-permute-start | bytes 393224 | tf_op jit(solution)/shard_map/ppermute | solution.py:361
  21.1 3.5 %collective-permute-start.10 = (bf16[256,512]{1,0:T(8,128)(2,1)S(1)}, bf16[256,512]{1,0:T(8,128)(2,1)S(1)}, u32[]{:S(2)}, u32[]{:S(2)}) collective-permute-start(bf16[256,512]{1,0:T(8,128)(2,1)S(1)} %get-tuple-element.40), channel_id=1, source_target_pairs={{0,8},{1,9},{2,10},{3,11},{4,12},{5,13},{6,14},{7,15},{8,0},{9,1},... | collective-permute-start | bytes 786440 | tf_op jit(solution)/shard_map/ppermute | solution.py:361
  25.2 4.9 %collective-permute-done.9 = bf16[256,512]{1,0:T(8,128)(2,1)S(1)} collective-permute-done((bf16[256,512]{1,0:T(8,128)(2,1)S(1)}, bf16[256,512]{1,0:T(8,128)(2,1)S(1)}, u32[]{:S(2)}, u32[]{:S(2)}) %collective-permute-start.9) | collective-permute-done | bytes 262176 | tf_op jit(solution)/shard_map/ppermute | solution.py:361
  30.1 13.6 %collective-permute-done.10 = bf16[256,512]{1,0:T(8,128)(2,1)S(1)} collective-permute-done((bf16[256,512]{1,0:T(8,128)(2,1)S(1)}, bf16[256,512]{1,0:T(8,128)(2,1)S(1)}, u32[]{:S(2)}, u32[]{:S(2)}) %collective-permute-start.10) | collective-permute-done | bytes 262176 | tf_op jit(solution)/shard_map/ppermute | solution.py:361
  43.7 3.4 %collective-permute-done.11 = bf16[256,512]{1,0:T(8,128)(2,1)S(1)} collective-permute-done((bf16[256,512]{1,0:T(8,128)(2,1)S(1)}, bf16[256,512]{1,0:T(8,128)(2,1)S(1)}, u32[]{:S(2)}, u32[]{:S(2)}) %collective-permute-start.11) | collective-permute-done | bytes 262176 | tf_op jit(solution)/shard_map/ppermute | solution.py:361
  50.8 15.5 %collective-permute-done.12 = bf16[6,64,1024]{2,1,0:T(8,128)(2,1)S(1)} collective-permute-done((bf16[6,64,1024]{2,1,0:T(8,128)(2,1)S(1)}, bf16[6,64,1024]{2,1,0:T(8,128)(2,1)S(1)}, u32[]{:S(2)}, u32[]{:S(2)}) %collective-permute-start.12) | collective-permute-done | bytes 786464 | tf_op jit(solution)/shard_map/ppermute | solution.py:358
  66.8 4.0 %collective-permute-done.14 = bf16[256,512]{1,0:T(8,128)(2,1)S(1)} collective-permute-done((bf16[256,512]{1,0:T(8,128)(2,1)S(1)}, bf16[256,512]{1,0:T(8,128)(2,1)S(1)}, u32[]{:S(2)}, u32[]{:S(2)}) %collective-permute-start.14) | collective-permute-done | bytes 262176 | tf_op jit(solution)/shard_map/ppermute | solution.py:361
  72.5 3.4 %collective-permute-start.19 = (bf16[256,512]{1,0:T(8,128)(2,1)S(1)}, bf16[256,512]{1,0:T(8,128)(2,1)S(1)}, u32[]{:S(2)}, u32[]{:S(2)}) collective-permute-start(bf16[256,512]{1,0:T(8,128)(2,1)S(1)} %get-tuple-element.45), channel_id=1, source_target_pairs={{0,8},{1,9},{2,10},{3,11},{4,12},{5,13},{6,14},{7,15},{8,0},{9,1},... | collective-permute-start | bytes 786440 | tf_op jit(solution)/shard_map/ppermute | solution.py:361
  75.9 2.9 %collective-permute-start.18 = (bf16[256,512]{1,0:T(8,128)(2,1)S(1)}, bf16[256,512]{1,0:T(8,128)(2,1)S(1)}, u32[]{:S(2)}, u32[]{:S(2)}) collective-permute-start(bf16[256,512]{1,0:T(8,128)(2,1)S(1)} %get-tuple-element.45), channel_id=1, source_target_pairs={{0,4},{1,5},{2,6},{3,7},{4,8},{5,9},{6,10},{7,11},{8,12},{9,13},{1... | collective-permute-start | bytes 786440 | tf_op jit(solution)/shard_map/ppermute | solution.py:361
  78.8 2.8 %collective-permute-done.20 = bf16[256,512]{1,0:T(8,128)(2,1)S(1)} collective-permute-done((bf16[256,512]{1,0:T(8,128)(2,1)S(1)}, bf16[256,512]{1,0:T(8,128)(2,1)S(1)}, u32[]{:S(2)}, u32[]{:S(2)}) %collective-permute-start.20) | collective-permute-done | bytes 262176 | tf_op jit(solution)/shard_map/ppermute | solution.py:361
  81.6 12.2 %collective-permute-done.19 = bf16[256,512]{1,0:T(8,128)(2,1)S(1)} collective-permute-done((bf16[256,512]{1,0:T(8,128)(2,1)S(1)}, bf16[256,512]{1,0:T(8,128)(2,1)S(1)}, u32[]{:S(2)}, u32[]{:S(2)}) %collective-permute-start.19) | collective-permute-done | bytes 262176 | tf_op jit(solution)/shard_map/ppermute | solution.py:361
  93.8 4.9 %collective-permute-done.18 = bf16[256,512]{1,0:T(8,128)(2,1)S(1)} collective-permute-done((bf16[256,512]{1,0:T(8,128)(2,1)S(1)}, bf16[256,512]{1,0:T(8,128)(2,1)S(1)}, u32[]{:S(2)}, u32[]{:S(2)}) %collective-permute-start.18) | collective-permute-done | bytes 262176 | tf_op jit(solution)/shard_map/ppermute | solution.py:361
  99.4 2.5 %collective-permute-start.23 = (bf16[256,512]{1,0:T(8,128)(2,1)S(1)}, bf16[256,512]{1,0:T(8,128)(2,1)S(1)}, u32[]{:S(2)}, u32[]{:S(2)}) collective-permute-start(bf16[256,512]{1,0:T(8,128)(2,1)S(1)} %pad_maximum_fusion.12), channel_id=1, source_target_pairs={{0,4},{1,5},{2,6},{3,7},{4,8},{5,9},{6,10},{7,11},{8,12},{9,13},{1... | collective-permute-start | bytes 786440 | tf_op jit(solution)/shard_map/ppermute | solution.py:361
  103.5 11.7 %chunk.4 = (f32[768,1024]{1,0:T(8,128)S(1)}, f32[768,1024]{1,0:T(8,128)S(1)}) custom-call(s32[24]{0:T(128)S(1)} %pad_add_fusion.3.sorted_ref, s32[2]{0:T(128)S(1)} %pad_add_fusion.4.place_ref, s32[24]{0:T(128)S(1)} %pad_add_fusion.5.perm_ref, bf16[2,6,64,1024]{3,2,1,0:T(8,128)(2,1)S(1)} %get-tuple-element.48.refs_0_, ...), custom_call_target="tpu_custom_call" | custom-call | flops 5368709120 | bytes 20971520 | tf_op jit(solution)/shard_map/chunk/pallas_call | solution.py:261
  115.2 4.8 %collective-permute-done.23 = bf16[256,512]{1,0:T(8,128)(2,1)S(1)} collective-permute-done((bf16[256,512]{1,0:T(8,128)(2,1)S(1)}, bf16[256,512]{1,0:T(8,128)(2,1)S(1)}, u32[]{:S(2)}, u32[]{:S(2)}) %collective-permute-start.23) | collective-permute-done | bytes 262176 | tf_op jit(solution)/shard_map/ppermute | solution.py:361
  119.9 3.7 %collective-permute-done.24 = bf16[256,512]{1,0:T(8,128)(2,1)S(1)} collective-permute-done((bf16[256,512]{1,0:T(8,128)(2,1)S(1)}, bf16[256,512]{1,0:T(8,128)(2,1)S(1)}, u32[]{:S(2)}, u32[]{:S(2)}) %collective-permute-start.24) | collective-permute-done | bytes 262176 | tf_op jit(solution)/shard_map/ppermute | solution.py:361
  124.6 4.3 %chunk.5 = (bf16[6,64,1024]{2,1,0:T(8,128)(2,1)S(1)}, bf16[6,64,1024]{2,1,0:T(8,128)(2,1)S(1)}, bf16[6,64,1024]{2,1,0:T(8,128)(2,1)S(1)}, bf16[6,64,1024]{2,1,0:T(8,128)(2,1)S(1)}) custom-call(s32[24]{0:T(128)S(1)} %pad_add_fusion.3.sorted_ref, s32[2]{0:T(128)S(1)} %pad_add_fusion.4.place_ref, s32[24]{0:T(128)S(1)} %pad_add_fusion.5.perm_ref, ...), custom_call_target="tpu_custom_call" | custom-call | tf_op jit(solution)/shard_map/chunk/pallas_call | solution.py:261
  129.5 3.1 %collective-permute-start.28 = (bf16[1024,512]{1,0:T(8,128)(2,1)S(1)}, bf16[1024,512]{1,0:T(8,128)(2,1)S(1)}, u32[]{:S(2)}, u32[]{:S(2)}) collective-permute-start(bf16[1024,512]{1,0:T(8,128)(2,1)S(1)} %pad_maximum_fusion.5.refs_2_), channel_id=1, source_target_pairs={{0,2},{1,3},{2,0},{3,1},{4,6},{5,7},{6,4},{7,5},{8,10},{9,11},{10,... | collective-permute-start | bytes 3145736 | tf_op jit(solution)/shard_map/ppermute | solution.py:355
  133.4 2.1 %collective-permute-start.31 = (bf16[2,6,64,1024]{3,2,1,0:T(8,128)(2,1)S(1)}, bf16[2,6,64,1024]{3,2,1,0:T(8,128)(2,1)S(1)}, u32[]{:S(2)}, u32[]{:S(2)}) collective-permute-start(bf16[2,6,64,1024]{3,2,1,0:T(8,128)(2,1)S(1)} %pad_maximum_fusion.3), channel_id=1, source_target_pairs={{0,16},{16,0},{1,17},{17,1},{2,18},{18,2},{3,19},{19,3},{4,20},{20... | collective-permute-start | bytes 4718600 | tf_op jit(solution)/shard_map/ppermute | solution.py:358
  135.6 13.7 %chunk.6 = (f32[768,1024]{1,0:T(8,128)S(1)}, f32[768,1024]{1,0:T(8,128)S(1)}) custom-call(s32[24]{0:T(128)S(1)} %pad_add_fusion.3.sorted_ref, s32[2]{0:T(128)S(1)} %pad_add_fusion.4.place_ref, s32[24]{0:T(128)S(1)} %pad_add_fusion.5.perm_ref, bf16[2,6,64,1024]{3,2,1,0:T(8,128)(2,1)S(1)} %get-tuple-element.57.refs_0_, ...), custom_call_target="tpu_custom_call" | custom-call | tf_op jit(solution)/shard_map/chunk/pallas_call | solution.py:261
  149.3 6.8 %collective-permute-done.28.refs_3_ = bf16[1024,512]{1,0:T(8,128)(2,1)S(1)} collective-permute-done((bf16[1024,512]{1,0:T(8,128)(2,1)S(1)}, bf16[1024,512]{1,0:T(8,128)(2,1)S(1)}, u32[]{:S(2)}, u32[]{:S(2)}) %collective-permute-start.28) | collective-permute-done | bytes 1048608 | tf_op jit(solution)/shard_map/ppermute | solution.py:355
  156.0 6.2 %chunk.7 = (f32[6,64,1024]{2,1,0:T(8,128)S(1)}, f32[6,64,1024]{2,1,0:T(8,128)S(1)}, bf16[6,64,1024]{2,1,0:T(8,128)(2,1)S(1)}, bf16[6,64,1024]{2,1,0:T(8,128)(2,1)S(1)}) custom-call(s32[24]{0:T(128)S(1)} %pad_add_fusion.3.sorted_ref, s32[2]{0:T(128)S(1)} %pad_add_fusion.4.place_ref, s32[24]{0:T(128)S(1)} %pad_add_fusion.5.perm_ref, ...), custom_call_target="tpu_custom_call" | custom-call | tf_op jit(solution)/shard_map/chunk/pallas_call | solution.py:261
  165.7 4.6 %collective-permute-done.31.across_ref = bf16[2,6,64,1024]{3,2,1,0:T(8,128)(2,1)S(1)} collective-permute-done((bf16[2,6,64,1024]{3,2,1,0:T(8,128)(2,1)S(1)}, bf16[2,6,64,1024]{3,2,1,0:T(8,128)(2,1)S(1)}, u32[]{:S(2)}, u32[]{:S(2)}) %collective-permute-start.31) | collective-permute-done | bytes 1572896 | tf_op jit(solution)/shard_map/ppermute | solution.py:358
  170.3 2.9 %finish.1 = (bf16[6,64,1024]{2,1,0:T(8,128)(2,1)}, bf16[6,64,1024]{2,1,0:T(8,128)(2,1)}, f32[6,64]{1,0:T(8,128)}) custom-call(s32[6]{0:T(128)S(1)} %bitcast.75, bf16[6,64,1024]{2,1,0:T(8,128)(2,1)S(1)} %copy-done, bf16[6,64,1024]{2,1,0:T(8,128)(2,1)S(1)} %copy-done.1, f32[2,1024]{1,0:T(2,128)S(1)} %copy-done.2, ...), custom_call_target="tpu_custom_call" | custom-call | tf_op jit(solution)/shard_map/finish/pallas_call | solution.py:311
  (113 shorter events, 30.1 us)
Async XLA Ops:
  4.1 12.0 %collective-permute-start.2 = (bf16[256,256]{1,0:T(8,128)(2,1)S(1)}, bf16[256,256]{1,0:T(8,128)(2,1)S(1)}, u32[]{:S(2)}, u32[]{:S(2)}) collective-permute-start(bf16[256,256]{1,0:T(8,128)(2,1)S(1)} %bitcast.92), channel_id=1, source_target_pairs={{0,12},{1,13},{2,14},{3,15},{4,0},{5,1},{6,2},{7,3},{8,4},{9,5},{1... | collective-permute-start | bytes 393224 | tf_op jit(solution)/shard_map/ppermute | solution.py:361
  4.1 11.2 %collective-permute-start.4 = (bf16[256,256]{1,0:T(8,128)(2,1)S(1)}, bf16[256,256]{1,0:T(8,128)(2,1)S(1)}, u32[]{:S(2)}, u32[]{:S(2)}) collective-permute-start(bf16[256,256]{1,0:T(8,128)(2,1)S(1)} %bitcast.93), channel_id=1, source_target_pairs={{0,4},{1,5},{2,6},{3,7},{4,8},{5,9},{6,10},{7,11},{8,12},{9,13},{1... | collective-permute-start | bytes 393224 | tf_op jit(solution)/shard_map/ppermute | solution.py:361
  6.2 12.9 %collective-permute-start.7 = (bf16[256,256]{1,0:T(8,128)(2,1)S(1)}, bf16[256,256]{1,0:T(8,128)(2,1)S(1)}, u32[]{:S(2)}, u32[]{:S(2)}) collective-permute-start(bf16[256,256]{1,0:T(8,128)(2,1)S(1)} %bitcast.95), channel_id=1, source_target_pairs={{0,8},{1,9},{2,10},{3,11},{4,12},{5,13},{6,14},{7,15},{8,0},{9,1},... | collective-permute-start | bytes 393224 | tf_op jit(solution)/shard_map/ppermute | solution.py:361
  16.2 32.5 %collective-permute-start.5 = (bf16[6,64,1024]{2,1,0:T(8,128)(2,1)S(1)}, bf16[6,64,1024]{2,1,0:T(8,128)(2,1)S(1)}, u32[]{:S(2)}, u32[]{:S(2)}) collective-permute-start(bf16[6,64,1024]{2,1,0:T(8,128)(2,1)S(1)} %fusion.2), channel_id=1, source_target_pairs={{0,16},{16,0},{1,17},{17,1},{2,18},{18,2},{3,19},{19,3},{4,20},{20... | collective-permute-start | bytes 2359304 | tf_op jit(solution)/shard_map/ppermute | solution.py:358
  19.1 28.0 %collective-permute-start.8 = (bf16[1792,256]{1,0:T(8,128)(2,1)S(1)}, bf16[1792,256]{1,0:T(8,128)(2,1)S(1)}, u32[]{:S(2)}, u32[]{:S(2)}) collective-permute-start(bf16[1792,256]{1,0:T(8,128)(2,1)S(1)} %constant_dynamic-update-slice_fusion.refs_2_), channel_id=1, source_target_pairs={{0,2},{1,3},{2,0},{3,1},{4,6},{5,7},{6,4},{7,5},{8,10},{9,11},{10,... | collective-permute-start | bytes 2752520 | tf_op jit(solution)/shard_map/ppermute | solution.py:355
  20.9 9.2 %collective-permute-start.9 = (bf16[256,512]{1,0:T(8,128)(2,1)S(1)}, bf16[256,512]{1,0:T(8,128)(2,1)S(1)}, u32[]{:S(2)}, u32[]{:S(2)}) collective-permute-start(bf16[256,512]{1,0:T(8,128)(2,1)S(1)} %get-tuple-element.40), channel_id=1, source_target_pairs={{0,4},{1,5},{2,6},{3,7},{4,8},{5,9},{6,10},{7,11},{8,12},{9,13},{1... | collective-permute-start | bytes 786440 | tf_op jit(solution)/shard_map/ppermute | solution.py:361
  21.1 22.6 %collective-permute-start.10 = (bf16[256,512]{1,0:T(8,128)(2,1)S(1)}, bf16[256,512]{1,0:T(8,128)(2,1)S(1)}, u32[]{:S(2)}, u32[]{:S(2)}) collective-permute-start(bf16[256,512]{1,0:T(8,128)(2,1)S(1)} %get-tuple-element.40), channel_id=1, source_target_pairs={{0,8},{1,9},{2,10},{3,11},{4,12},{5,13},{6,14},{7,15},{8,0},{9,1},... | collective-permute-start | bytes 786440 | tf_op jit(solution)/shard_map/ppermute | solution.py:361
  24.6 22.5 %collective-permute-start.11 = (bf16[256,512]{1,0:T(8,128)(2,1)S(1)}, bf16[256,512]{1,0:T(8,128)(2,1)S(1)}, u32[]{:S(2)}, u32[]{:S(2)}) collective-permute-start(bf16[256,512]{1,0:T(8,128)(2,1)S(1)} %get-tuple-element.40), channel_id=1, source_target_pairs={{0,12},{1,13},{2,14},{3,15},{4,0},{5,1},{6,2},{7,3},{8,4},{9,5},{1... | collective-permute-start | bytes 786440 | tf_op jit(solution)/shard_map/ppermute | solution.py:361
  47.1 19.2 %collective-permute-start.12 = (bf16[6,64,1024]{2,1,0:T(8,128)(2,1)S(1)}, bf16[6,64,1024]{2,1,0:T(8,128)(2,1)S(1)}, u32[]{:S(2)}, u32[]{:S(2)}) collective-permute-start(bf16[6,64,1024]{2,1,0:T(8,128)(2,1)S(1)} %copy-done.1), channel_id=1, source_target_pairs={{0,16},{16,0},{1,17},{17,1},{2,18},{18,2},{3,19},{19,3},{4,20},{20... | collective-permute-start | bytes 2359304 | tf_op jit(solution)/shard_map/ppermute | solution.py:358
  48.1 22.7 %collective-permute-start.16 = (bf16[896,512]{1,0:T(8,128)(2,1)S(1)}, bf16[896,512]{1,0:T(8,128)(2,1)S(1)}, u32[]{:S(2)}, u32[]{:S(2)}) collective-permute-start(bf16[896,512]{1,0:T(8,128)(2,1)S(1)} %pad_maximum_fusion.6.refs_3_), channel_id=1, source_target_pairs={{0,2},{1,3},{2,0},{3,1},{4,6},{5,7},{6,4},{7,5},{8,10},{9,11},{10,... | collective-permute-start | bytes 2752520 | tf_op jit(solution)/shard_map/ppermute | solution.py:355
  48.7 18.1 %collective-permute-start.13 = (bf16[256,512]{1,0:T(8,128)(2,1)S(1)}, bf16[256,512]{1,0:T(8,128)(2,1)S(1)}, u32[]{:S(2)}, u32[]{:S(2)}) collective-permute-start(bf16[256,512]{1,0:T(8,128)(2,1)S(1)} %pad_maximum_fusion.11), channel_id=1, source_target_pairs={{0,4},{1,5},{2,6},{3,7},{4,8},{5,9},{6,10},{7,11},{8,12},{9,13},{1... | collective-permute-start | bytes 786440 | tf_op jit(solution)/shard_map/ppermute | solution.py:361
  48.8 22.0 %collective-permute-start.14 = (bf16[256,512]{1,0:T(8,128)(2,1)S(1)}, bf16[256,512]{1,0:T(8,128)(2,1)S(1)}, u32[]{:S(2)}, u32[]{:S(2)}) collective-permute-start(bf16[256,512]{1,0:T(8,128)(2,1)S(1)} %pad_maximum_fusion.11), channel_id=1, source_target_pairs={{0,8},{1,9},{2,10},{3,11},{4,12},{5,13},{6,14},{7,15},{8,0},{9,1},... | collective-permute-start | bytes 786440 | tf_op jit(solution)/shard_map/ppermute | solution.py:361
  48.9 21.9 %collective-permute-start.15 = (bf16[256,512]{1,0:T(8,128)(2,1)S(1)}, bf16[256,512]{1,0:T(8,128)(2,1)S(1)}, u32[]{:S(2)}, u32[]{:S(2)}) collective-permute-start(bf16[256,512]{1,0:T(8,128)(2,1)S(1)} %pad_maximum_fusion.11), channel_id=1, source_target_pairs={{0,12},{1,13},{2,14},{3,15},{4,0},{5,1},{6,2},{7,3},{8,4},{9,5},{1... | collective-permute-start | bytes 786440 | tf_op jit(solution)/shard_map/ppermute | solution.py:361
  70.8 28.6 %collective-permute-start.17 = (bf16[2,2,6,64,1024]{4,3,2,1,0:T(8,128)(2,1)S(1)}, bf16[2,2,6,64,1024]{4,3,2,1,0:T(8,128)(2,1)S(1)}, u32[]{:S(2)}, u32[]{:S(2)}) collective-permute-start(bf16[2,2,6,64,1024]{4,3,2,1,0:T(8,128)(2,1)S(1)} %pad_maximum_fusion), channel_id=1, source_target_pairs={{0,1},{1,0},{2,3},{3,2},{4,5},{5,4},{6,7},{7,6},{8,9},{9,8},{10,11... | collective-permute-start | bytes 9437192 | tf_op jit(solution)/shard_map/ppermute | solution.py:352
  70.9 27.9 %collective-permute-start.21 = (bf16[896,512]{1,0:T(8,128)(2,1)S(1)}, bf16[896,512]{1,0:T(8,128)(2,1)S(1)}, u32[]{:S(2)}, u32[]{:S(2)}) collective-permute-start(bf16[896,512]{1,0:T(8,128)(2,1)S(1)} %pad_maximum_fusion.7.refs_4_.refs_2_), channel_id=1, source_target_pairs={{0,2},{1,3},{2,0},{3,1},{4,6},{5,7},{6,4},{7,5},{8,10},{9,11},{10,... | collective-permute-start | bytes 2752520 | tf_op jit(solution)/shard_map/ppermute | solution.py:355
  72.5 9.1 %collective-permute-start.20 = (bf16[256,512]{1,0:T(8,128)(2,1)S(1)}, bf16[256,512]{1,0:T(8,128)(2,1)S(1)}, u32[]{:S(2)}, u32[]{:S(2)}) collective-permute-start(bf16[256,512]{1,0:T(8,128)(2,1)S(1)} %get-tuple-element.45), channel_id=1, source_target_pairs={{0,12},{1,13},{2,14},{3,15},{4,0},{5,1},{6,2},{7,3},{8,4},{9,5},{1... | collective-permute-start | bytes 786440 | tf_op jit(solution)/shard_map/ppermute | solution.py:361
  72.5 21.3 %collective-permute-start.19 = (bf16[256,512]{1,0:T(8,128)(2,1)S(1)}, bf16[256,512]{1,0:T(8,128)(2,1)S(1)}, u32[]{:S(2)}, u32[]{:S(2)}) collective-permute-start(bf16[256,512]{1,0:T(8,128)(2,1)S(1)} %get-tuple-element.45), channel_id=1, source_target_pairs={{0,8},{1,9},{2,10},{3,11},{4,12},{5,13},{6,14},{7,15},{8,0},{9,1},... | collective-permute-start | bytes 786440 | tf_op jit(solution)/shard_map/ppermute | solution.py:361
  75.9 22.8 %collective-permute-start.18 = (bf16[256,512]{1,0:T(8,128)(2,1)S(1)}, bf16[256,512]{1,0:T(8,128)(2,1)S(1)}, u32[]{:S(2)}, u32[]{:S(2)}) collective-permute-start(bf16[256,512]{1,0:T(8,128)(2,1)S(1)} %get-tuple-element.45), channel_id=1, source_target_pairs={{0,4},{1,5},{2,6},{3,7},{4,8},{5,9},{6,10},{7,11},{8,12},{9,13},{1... | collective-permute-start | bytes 786440 | tf_op jit(solution)/shard_map/ppermute | solution.py:361
  98.8 25.8 %collective-permute-start.22 = (bf16[896,512]{1,0:T(8,128)(2,1)S(1)}, bf16[896,512]{1,0:T(8,128)(2,1)S(1)}, u32[]{:S(2)}, u32[]{:S(2)}) collective-permute-start(bf16[896,512]{1,0:T(8,128)(2,1)S(1)} %pad_maximum_fusion.8.refs_3_.refs_5_), channel_id=1, source_target_pairs={{0,2},{1,3},{2,0},{3,1},{4,6},{5,7},{6,4},{7,5},{8,10},{9,11},{10,... | collective-permute-start | bytes 2752520 | tf_op jit(solution)/shard_map/ppermute | solution.py:355
  99.4 20.5 %collective-permute-start.23 = (bf16[256,512]{1,0:T(8,128)(2,1)S(1)}, bf16[256,512]{1,0:T(8,128)(2,1)S(1)}, u32[]{:S(2)}, u32[]{:S(2)}) collective-permute-start(bf16[256,512]{1,0:T(8,128)(2,1)S(1)} %pad_maximum_fusion.12), channel_id=1, source_target_pairs={{0,4},{1,5},{2,6},{3,7},{4,8},{5,9},{6,10},{7,11},{8,12},{9,13},{1... | collective-permute-start | bytes 786440 | tf_op jit(solution)/shard_map/ppermute | solution.py:361
  102.0 21.7 %collective-permute-start.24 = (bf16[256,512]{1,0:T(8,128)(2,1)S(1)}, bf16[256,512]{1,0:T(8,128)(2,1)S(1)}, u32[]{:S(2)}, u32[]{:S(2)}) collective-permute-start(bf16[256,512]{1,0:T(8,128)(2,1)S(1)} %pad_maximum_fusion.12), channel_id=1, source_target_pairs={{0,8},{1,9},{2,10},{3,11},{4,12},{5,13},{6,14},{7,15},{8,0},{9,1},... | collective-permute-start | bytes 786440 | tf_op jit(solution)/shard_map/ppermute | solution.py:361
  102.4 22.2 %collective-permute-start.25 = (bf16[256,512]{1,0:T(8,128)(2,1)S(1)}, bf16[256,512]{1,0:T(8,128)(2,1)S(1)}, u32[]{:S(2)}, u32[]{:S(2)}) collective-permute-start(bf16[256,512]{1,0:T(8,128)(2,1)S(1)} %pad_maximum_fusion.12), channel_id=1, source_target_pairs={{0,12},{1,13},{2,14},{3,15},{4,0},{5,1},{6,2},{7,3},{8,4},{9,5},{1... | collective-permute-start | bytes 786440 | tf_op jit(solution)/shard_map/ppermute | solution.py:361
  129.5 26.5 %collective-permute-start.28 = (bf16[1024,512]{1,0:T(8,128)(2,1)S(1)}, bf16[1024,512]{1,0:T(8,128)(2,1)S(1)}, u32[]{:S(2)}, u32[]{:S(2)}) collective-permute-start(bf16[1024,512]{1,0:T(8,128)(2,1)S(1)} %pad_maximum_fusion.5.refs_2_), channel_id=1, source_target_pairs={{0,2},{1,3},{2,0},{3,1},{4,6},{5,7},{6,4},{7,5},{8,10},{9,11},{10,... | collective-permute-start | bytes 3145736 | tf_op jit(solution)/shard_map/ppermute | solution.py:355
  133.4 36.8 %collective-permute-start.31 = (bf16[2,6,64,1024]{3,2,1,0:T(8,128)(2,1)S(1)}, bf16[2,6,64,1024]{3,2,1,0:T(8,128)(2,1)S(1)}, u32[]{:S(2)}, u32[]{:S(2)}) collective-permute-start(bf16[2,6,64,1024]{3,2,1,0:T(8,128)(2,1)S(1)} %pad_maximum_fusion.3), channel_id=1, source_target_pairs={{0,16},{16,0},{1,17},{17,1},{2,18},{18,2},{3,19},{19,3},{4,20},{20... | collective-permute-start | bytes 4718600 | tf_op jit(solution)/shard_map/ppermute | solution.py:358
  (14 other events, 63.9 us)

commit v16 on v15

--- a/solution.py
+++ b/solution.py
@@ -88,6 +88,10 @@
 VMEM_LIMIT = 20 * 1024 * 1024
 BF16 = jnp.bfloat16
 F32 = jnp.float32
+
+
+def along(z, d, lines):
+    return z ^ d if lines & (lines - 1) == 0 else (z + lines - d) % lines
 
 
 def chunk_kernel(
@@ -127,7 +131,7 @@
                     pltpu.make_async_copy(ref, tokens_ref.at[2 * i + k], sems.at[len(copies)])
                 )
         for i, start, d, to_row, to_unit, n, wide in sources:
-            from_z = lax.rem(z + lines - d, lines)
+            from_z = along(z, d, lines)
             for to_y, ref in ((y, here_refs[i]), (1 - y, there_refs[i])):
                 to = weights_ref.at[from_z, to_y, pl.ds(to_row, n), pl.ds(to_unit, wide)]
                 copies.append(
@@ -358,7 +362,8 @@
         return lax.ppermute(a, "grp", [(0, 1), (1, 0)])
 
     def shift_z(a, d):
-        return lax.ppermute(a, "row", [(i, (i + 4 * d) % ranks) for i in range(ranks)])
+        pairs = [(4 * along(i // 4, d, lines) + i % 4, i) for i in range(ranks)]
+        return lax.ppermute(a, "row", pairs)
 
     def after(a, *others):
         return lax.optimization_barrier((a, *others))[0]

time: 175 us -> 176 us (level); the launches traced: 173 us -> 176 us
  waiting for transfers between devices: 86.7 us -> 92.9 us
  starting transfers between devices: 37.8 us -> 33.7 us
    ppermute x15, waiting for transfers between devices: 56.2 us -> 64.1 us  [shift_z(): return lax.ppermute(a, 'row', pairs)]
    ppermute x15, starting transfers between devices: 23 us -> 19.2 us  [shift_z(): return lax.ppermute(a, 'row', pairs)]
    ppermute x5, waiting for transfers between devices: 6.77 us -> 4.81 us  [over_y(): return lax.ppermute(a, 'row', [(i, i ^ 2) for i in range(ranks)])]
  transfers between devices with their start and end apart: 32 -> 32, of which waited for: 17 -> 18; matrix products, arithmetic and copies ran while one was open for 4% -> 4% of each run, Pallas kernels for 18% -> 18%
where the time goes in v16:
time: 176 us
  waiting for transfers between devices  92.9 us (53%)
  Pallas kernels  39.5 us (22%)
  starting transfers between devices  33.7 us (19%)
  other arithmetic  5.91 us (3%)
  local copies, waits for them, and re-layouts  2.83 us (2%)
    ppermute x15, waiting for transfers between devices, shift_z(): return lax.ppermute(a, 'row', pairs)  64.1 us
    pallas_call x4, Pallas kernels, chunk(): pl.pallas_call(functools.partial(chunk_kernel, offset, kind, units, chips...  36.6 us
    ppermute x4, waiting for transfers between devices, over_x(): return lax.ppermute(a, 'grp', [(0, 1), (1, 0)])  20.1 us
    ppermute x15, starting transfers between devices, shift_z(): return lax.ppermute(a, 'row', pairs)  19.2 us
    ppermute x4, starting transfers between devices, over_x(): return lax.ppermute(a, 'grp', [(0, 1), (1, 0)])  7.23 us
    ppermute x5, starting transfers between devices, over_y(): return lax.ppermute(a, 'row', [(i, i ^ 2) for i in range(ranks)])  5.91 us
    ppermute x5, waiting for transfers between devices, over_y(): return lax.ppermute(a, 'row', [(i, i ^ 2) for i in range(ranks)])  4.81 us
    ppermute x8, waiting for transfers between devices, partner(): return lax.ppermute(a, 'row', [(i, i ^ 1) for i in range(ranks)])  3.81 us
  transfers between devices with their start and end apart: 32, of which 18 were waited for; matrix products, arithmetic and copies ran while one was open for 4% of the time, Pallas kernels for 18%

profile of v16, /device:TPU:8, one launch (start us, length us, event | category | flops | bytes accessed | tf_op | source)
XLA Modules:
  0.0 176.0 jit_solution(2807582246451286730)
XLA Ops:
  5.7 2.5 %collective-permute-start.4 = (bf16[256,256]{1,0:T(8,128)(2,1)S(1)}, bf16[256,256]{1,0:T(8,128)(2,1)S(1)}, u32[]{:S(2)}, u32[]{:S(2)}) collective-permute-start(bf16[256,256]{1,0:T(8,128)(2,1)S(1)} %bitcast.93), channel_id=1, source_target_pairs={{4,0},{5,1},{6,2},{7,3},{0,4},{1,5},{2,6},{3,7},{12,8},{13,9},{14,... | collective-permute-start | bytes 393224 | tf_op jit(solution)/shard_map/ppermute | solution.py:366
  12.1 3.2 %collective-permute-done.4 = bf16[256,256]{1,0:T(8,128)(2,1)S(1)} collective-permute-done((bf16[256,256]{1,0:T(8,128)(2,1)S(1)}, bf16[256,256]{1,0:T(8,128)(2,1)S(1)}, u32[]{:S(2)}, u32[]{:S(2)}) %collective-permute-start.4) | collective-permute-done | bytes 131104 | tf_op jit(solution)/shard_map/ppermute | solution.py:366
  24.7 7.2 %collective-permute-done.9 = bf16[256,512]{1,0:T(8,128)(2,1)S(1)} collective-permute-done((bf16[256,512]{1,0:T(8,128)(2,1)S(1)}, bf16[256,512]{1,0:T(8,128)(2,1)S(1)}, u32[]{:S(2)}, u32[]{:S(2)}) %collective-permute-start.9) | collective-permute-done | bytes 262176 | tf_op jit(solution)/shard_map/ppermute | solution.py:366
  31.9 8.9 %collective-permute-done.10 = bf16[256,512]{1,0:T(8,128)(2,1)S(1)} collective-permute-done((bf16[256,512]{1,0:T(8,128)(2,1)S(1)}, bf16[256,512]{1,0:T(8,128)(2,1)S(1)}, u32[]{:S(2)}, u32[]{:S(2)}) %collective-permute-start.10) | collective-permute-done | bytes 262176 | tf_op jit(solution)/shard_map/ppermute | solution.py:366
  40.9 6.3 %collective-permute-done.11 = bf16[256,512]{1,0:T(8,128)(2,1)S(1)} collective-permute-done((bf16[256,512]{1,0:T(8,128)(2,1)S(1)}, bf16[256,512]{1,0:T(8,128)(2,1)S(1)}, u32[]{:S(2)}, u32[]{:S(2)}) %collective-permute-start.11) | collective-permute-done | bytes 262176 | tf_op jit(solution)/shard_map/ppermute | solution.py:366
  48.8 2.3 %collective-permute-start.14 = (bf16[256,512]{1,0:T(8,128)(2,1)S(1)}, bf16[256,512]{1,0:T(8,128)(2,1)S(1)}, u32[]{:S(2)}, u32[]{:S(2)}) collective-permute-start(bf16[256,512]{1,0:T(8,128)(2,1)S(1)} %pad_maximum_fusion.11), channel_id=1, source_target_pairs={{8,0},{9,1},{10,2},{11,3},{12,4},{13,5},{14,6},{15,7},{0,8},{1,9},... | collective-permute-start | bytes 786440 | tf_op jit(solution)/shard_map/ppermute | solution.py:366
  52.3 13.0 %collective-permute-done.12 = bf16[6,64,1024]{2,1,0:T(8,128)(2,1)S(1)} collective-permute-done((bf16[6,64,1024]{2,1,0:T(8,128)(2,1)S(1)}, bf16[6,64,1024]{2,1,0:T(8,128)(2,1)S(1)}, u32[]{:S(2)}, u32[]{:S(2)}) %collective-permute-start.12) | collective-permute-done | bytes 786464 | tf_op jit(solution)/shard_map/ppermute | solution.py:362
  65.9 2.7 %collective-permute-done.14 = bf16[256,512]{1,0:T(8,128)(2,1)S(1)} collective-permute-done((bf16[256,512]{1,0:T(8,128)(2,1)S(1)}, bf16[256,512]{1,0:T(8,128)(2,1)S(1)}, u32[]{:S(2)}, u32[]{:S(2)}) %collective-permute-start.14) | collective-permute-done | bytes 262176 | tf_op jit(solution)/shard_map/ppermute | solution.py:366
  68.6 4.8 %collective-permute-done.15 = bf16[256,512]{1,0:T(8,128)(2,1)S(1)} collective-permute-done((bf16[256,512]{1,0:T(8,128)(2,1)S(1)}, bf16[256,512]{1,0:T(8,128)(2,1)S(1)}, u32[]{:S(2)}, u32[]{:S(2)}) %collective-permute-start.15) | collective-permute-done | bytes 262176 | tf_op jit(solution)/shard_map/ppermute | solution.py:366
  75.6 2.9 %collective-permute-start.18 = (bf16[256,512]{1,0:T(8,128)(2,1)S(1)}, bf16[256,512]{1,0:T(8,128)(2,1)S(1)}, u32[]{:S(2)}, u32[]{:S(2)}) collective-permute-start(bf16[256,512]{1,0:T(8,128)(2,1)S(1)} %get-tuple-element.45), channel_id=1, source_target_pairs={{4,0},{5,1},{6,2},{7,3},{0,4},{1,5},{2,6},{3,7},{12,8},{13,9},{14,... | collective-permute-start | bytes 786440 | tf_op jit(solution)/shard_map/ppermute | solution.py:366
  78.5 14.6 %collective-permute-done.20 = bf16[256,512]{1,0:T(8,128)(2,1)S(1)} collective-permute-done((bf16[256,512]{1,0:T(8,128)(2,1)S(1)}, bf16[256,512]{1,0:T(8,128)(2,1)S(1)}, u32[]{:S(2)}, u32[]{:S(2)}) %collective-permute-start.20) | collective-permute-done | bytes 262176 | tf_op jit(solution)/shard_map/ppermute | solution.py:366
  93.1 4.2 %collective-permute-done.19 = bf16[256,512]{1,0:T(8,128)(2,1)S(1)} collective-permute-done((bf16[256,512]{1,0:T(8,128)(2,1)S(1)}, bf16[256,512]{1,0:T(8,128)(2,1)S(1)}, u32[]{:S(2)}, u32[]{:S(2)}) %collective-permute-start.19) | collective-permute-done | bytes 262176 | tf_op jit(solution)/shard_map/ppermute | solution.py:366
  98.1 2.9 %collective-permute-start.23 = (bf16[256,512]{1,0:T(8,128)(2,1)S(1)}, bf16[256,512]{1,0:T(8,128)(2,1)S(1)}, u32[]{:S(2)}, u32[]{:S(2)}) collective-permute-start(bf16[256,512]{1,0:T(8,128)(2,1)S(1)} %pad_maximum_fusion.12), channel_id=1, source_target_pairs={{4,0},{5,1},{6,2},{7,3},{0,4},{1,5},{2,6},{3,7},{12,8},{13,9},{14,... | collective-permute-start | bytes 786440 | tf_op jit(solution)/shard_map/ppermute | solution.py:366
  102.5 10.7 %chunk.4 = (f32[768,1024]{1,0:T(8,128)S(1)}, f32[768,1024]{1,0:T(8,128)S(1)}) custom-call(s32[24]{0:T(128)S(1)} %pad_add_fusion.3.sorted_ref, s32[2]{0:T(128)S(1)} %pad_add_fusion.4.place_ref, s32[24]{0:T(128)S(1)} %pad_add_fusion.5.perm_ref, bf16[2,6,64,1024]{3,2,1,0:T(8,128)(2,1)S(1)} %get-tuple-element.48.refs_0_, ...), custom_call_target="tpu_custom_call" | custom-call | flops 5368709120 | bytes 20971520 | tf_op jit(solution)/shard_map/chunk/pallas_call | solution.py:265
  113.2 6.4 %collective-permute-done.24 = bf16[256,512]{1,0:T(8,128)(2,1)S(1)} collective-permute-done((bf16[256,512]{1,0:T(8,128)(2,1)S(1)}, bf16[256,512]{1,0:T(8,128)(2,1)S(1)}, u32[]{:S(2)}, u32[]{:S(2)}) %collective-permute-start.24) | collective-permute-done | bytes 262176 | tf_op jit(solution)/shard_map/ppermute | solution.py:366
  119.6 5.8 %collective-permute-done.25 = bf16[256,512]{1,0:T(8,128)(2,1)S(1)} collective-permute-done((bf16[256,512]{1,0:T(8,128)(2,1)S(1)}, bf16[256,512]{1,0:T(8,128)(2,1)S(1)}, u32[]{:S(2)}, u32[]{:S(2)}) %collective-permute-start.25) | collective-permute-done | bytes 262176 | tf_op jit(solution)/shard_map/ppermute | solution.py:366
  125.3 5.8 %chunk.5 = (bf16[6,64,1024]{2,1,0:T(8,128)(2,1)S(1)}, bf16[6,64,1024]{2,1,0:T(8,128)(2,1)S(1)}, bf16[6,64,1024]{2,1,0:T(8,128)(2,1)S(1)}, bf16[6,64,1024]{2,1,0:T(8,128)(2,1)S(1)}) custom-call(s32[24]{0:T(128)S(1)} %pad_add_fusion.3.sorted_ref, s32[2]{0:T(128)S(1)} %pad_add_fusion.4.place_ref, s32[24]{0:T(128)S(1)} %pad_add_fusion.5.perm_ref, ...), custom_call_target="tpu_custom_call" | custom-call | tf_op jit(solution)/shard_map/chunk/pallas_call | solution.py:265
  135.1 3.3 %collective-permute-start.31 = (bf16[2,6,64,1024]{3,2,1,0:T(8,128)(2,1)S(1)}, bf16[2,6,64,1024]{3,2,1,0:T(8,128)(2,1)S(1)}, u32[]{:S(2)}, u32[]{:S(2)}) collective-permute-start(bf16[2,6,64,1024]{3,2,1,0:T(8,128)(2,1)S(1)} %pad_maximum_fusion.3), channel_id=1, source_target_pairs={{0,16},{16,0},{1,17},{17,1},{2,18},{18,2},{3,19},{19,3},{4,20},{20... | collective-permute-start | bytes 4718600 | tf_op jit(solution)/shard_map/ppermute | solution.py:362
  138.4 13.8 %chunk.6 = (f32[768,1024]{1,0:T(8,128)S(1)}, f32[768,1024]{1,0:T(8,128)S(1)}) custom-call(s32[24]{0:T(128)S(1)} %pad_add_fusion.3.sorted_ref, s32[2]{0:T(128)S(1)} %pad_add_fusion.4.place_ref, s32[24]{0:T(128)S(1)} %pad_add_fusion.5.perm_ref, bf16[2,6,64,1024]{3,2,1,0:T(8,128)(2,1)S(1)} %get-tuple-element.57.refs_0_, ...), custom_call_target="tpu_custom_call" | custom-call | tf_op jit(solution)/shard_map/chunk/pallas_call | solution.py:265
  152.2 4.8 %collective-permute-done.28.refs_3_ = bf16[1024,512]{1,0:T(8,128)(2,1)S(1)} collective-permute-done((bf16[1024,512]{1,0:T(8,128)(2,1)S(1)}, bf16[1024,512]{1,0:T(8,128)(2,1)S(1)}, u32[]{:S(2)}, u32[]{:S(2)}) %collective-permute-start.28) | collective-permute-done | bytes 1048608 | tf_op jit(solution)/shard_map/ppermute | solution.py:359
  157.0 6.3 %chunk.7 = (f32[6,64,1024]{2,1,0:T(8,128)S(1)}, f32[6,64,1024]{2,1,0:T(8,128)S(1)}, bf16[6,64,1024]{2,1,0:T(8,128)(2,1)S(1)}, bf16[6,64,1024]{2,1,0:T(8,128)(2,1)S(1)}) custom-call(s32[24]{0:T(128)S(1)} %pad_add_fusion.3.sorted_ref, s32[2]{0:T(128)S(1)} %pad_add_fusion.4.place_ref, s32[24]{0:T(128)S(1)} %pad_add_fusion.5.perm_ref, ...), custom_call_target="tpu_custom_call" | custom-call | tf_op jit(solution)/shard_map/chunk/pallas_call | solution.py:265
  163.9 1.8 %collective-permute-done.29.other_out_ref = bf16[6,64,1024]{2,1,0:T(8,128)(2,1)S(1)} collective-permute-done((bf16[6,64,1024]{2,1,0:T(8,128)(2,1)S(1)}, bf16[6,64,1024]{2,1,0:T(8,128)(2,1)S(1)}, u32[]{:S(2)}, u32[]{:S(2)}) %collective-permute-start.29) | collective-permute-done | bytes 786464 | tf_op jit(solution)/shard_map/ppermute | solution.py:356
  166.8 6.3 %collective-permute-done.31.across_ref = bf16[2,6,64,1024]{3,2,1,0:T(8,128)(2,1)S(1)} collective-permute-done((bf16[2,6,64,1024]{3,2,1,0:T(8,128)(2,1)S(1)}, bf16[2,6,64,1024]{3,2,1,0:T(8,128)(2,1)S(1)}, u32[]{:S(2)}, u32[]{:S(2)}) %collective-permute-start.31) | collective-permute-done | bytes 1572896 | tf_op jit(solution)/shard_map/ppermute | solution.py:362
  173.1 2.9 %finish.1 = (bf16[6,64,1024]{2,1,0:T(8,128)(2,1)}, bf16[6,64,1024]{2,1,0:T(8,128)(2,1)}, f32[6,64]{1,0:T(8,128)}) custom-call(s32[6]{0:T(128)S(1)} %bitcast.75, bf16[6,64,1024]{2,1,0:T(8,128)(2,1)S(1)} %copy-done, bf16[6,64,1024]{2,1,0:T(8,128)(2,1)S(1)} %copy-done.1, f32[2,1024]{1,0:T(2,128)S(1)} %copy-done.2, ...), custom_call_target="tpu_custom_call" | custom-call | tf_op jit(solution)/shard_map/finish/pallas_call | solution.py:315
  (113 shorter events, 31.5 us)
Async XLA Ops:
  4.1 12.1 %collective-permute-start.2 = (bf16[256,256]{1,0:T(8,128)(2,1)S(1)}, bf16[256,256]{1,0:T(8,128)(2,1)S(1)}, u32[]{:S(2)}, u32[]{:S(2)}) collective-permute-start(bf16[256,256]{1,0:T(8,128)(2,1)S(1)} %bitcast.92), channel_id=1, source_target_pairs={{12,0},{13,1},{14,2},{15,3},{8,4},{9,5},{10,6},{11,7},{4,8},{5,9},... | collective-permute-start | bytes 393224 | tf_op jit(solution)/shard_map/ppermute | solution.py:366
  5.7 9.6 %collective-permute-start.4 = (bf16[256,256]{1,0:T(8,128)(2,1)S(1)}, bf16[256,256]{1,0:T(8,128)(2,1)S(1)}, u32[]{:S(2)}, u32[]{:S(2)}) collective-permute-start(bf16[256,256]{1,0:T(8,128)(2,1)S(1)} %bitcast.93), channel_id=1, source_target_pairs={{4,0},{5,1},{6,2},{7,3},{0,4},{1,5},{2,6},{3,7},{12,8},{13,9},{14,... | collective-permute-start | bytes 393224 | tf_op jit(solution)/shard_map/ppermute | solution.py:366
  8.2 10.9 %collective-permute-start.7 = (bf16[256,256]{1,0:T(8,128)(2,1)S(1)}, bf16[256,256]{1,0:T(8,128)(2,1)S(1)}, u32[]{:S(2)}, u32[]{:S(2)}) collective-permute-start(bf16[256,256]{1,0:T(8,128)(2,1)S(1)} %bitcast.95), channel_id=1, source_target_pairs={{8,0},{9,1},{10,2},{11,3},{12,4},{13,5},{14,6},{15,7},{0,8},{1,9},... | collective-permute-start | bytes 393224 | tf_op jit(solution)/shard_map/ppermute | solution.py:366
  16.2 32.5 %collective-permute-start.5 = (bf16[6,64,1024]{2,1,0:T(8,128)(2,1)S(1)}, bf16[6,64,1024]{2,1,0:T(8,128)(2,1)S(1)}, u32[]{:S(2)}, u32[]{:S(2)}) collective-permute-start(bf16[6,64,1024]{2,1,0:T(8,128)(2,1)S(1)} %fusion.2), channel_id=1, source_target_pairs={{0,16},{16,0},{1,17},{17,1},{2,18},{18,2},{3,19},{19,3},{4,20},{20... | collective-permute-start | bytes 2359304 | tf_op jit(solution)/shard_map/ppermute | solution.py:362
  19.1 28.0 %collective-permute-start.8 = (bf16[1792,256]{1,0:T(8,128)(2,1)S(1)}, bf16[1792,256]{1,0:T(8,128)(2,1)S(1)}, u32[]{:S(2)}, u32[]{:S(2)}) collective-permute-start(bf16[1792,256]{1,0:T(8,128)(2,1)S(1)} %constant_dynamic-update-slice_fusion.refs_2_), channel_id=1, source_target_pairs={{0,2},{1,3},{2,0},{3,1},{4,6},{5,7},{6,4},{7,5},{8,10},{9,11},{10,... | collective-permute-start | bytes 2752520 | tf_op jit(solution)/shard_map/ppermute | solution.py:359
  20.9 11.0 %collective-permute-start.9 = (bf16[256,512]{1,0:T(8,128)(2,1)S(1)}, bf16[256,512]{1,0:T(8,128)(2,1)S(1)}, u32[]{:S(2)}, u32[]{:S(2)}) collective-permute-start(bf16[256,512]{1,0:T(8,128)(2,1)S(1)} %get-tuple-element.40), channel_id=1, source_target_pairs={{4,0},{5,1},{6,2},{7,3},{0,4},{1,5},{2,6},{3,7},{12,8},{13,9},{14,... | collective-permute-start | bytes 786440 | tf_op jit(solution)/shard_map/ppermute | solution.py:366
  21.9 19.0 %collective-permute-start.10 = (bf16[256,512]{1,0:T(8,128)(2,1)S(1)}, bf16[256,512]{1,0:T(8,128)(2,1)S(1)}, u32[]{:S(2)}, u32[]{:S(2)}) collective-permute-start(bf16[256,512]{1,0:T(8,128)(2,1)S(1)} %get-tuple-element.40), channel_id=1, source_target_pairs={{8,0},{9,1},{10,2},{11,3},{12,4},{13,5},{14,6},{15,7},{0,8},{1,9},... | collective-permute-start | bytes 786440 | tf_op jit(solution)/shard_map/ppermute | solution.py:366
  22.9 24.2 %collective-permute-start.11 = (bf16[256,512]{1,0:T(8,128)(2,1)S(1)}, bf16[256,512]{1,0:T(8,128)(2,1)S(1)}, u32[]{:S(2)}, u32[]{:S(2)}) collective-permute-start(bf16[256,512]{1,0:T(8,128)(2,1)S(1)} %get-tuple-element.40), channel_id=1, source_target_pairs={{12,0},{13,1},{14,2},{15,3},{8,4},{9,5},{10,6},{11,7},{4,8},{5,9},... | collective-permute-start | bytes 786440 | tf_op jit(solution)/shard_map/ppermute | solution.py:366
  47.1 18.2 %collective-permute-start.12 = (bf16[6,64,1024]{2,1,0:T(8,128)(2,1)S(1)}, bf16[6,64,1024]{2,1,0:T(8,128)(2,1)S(1)}, u32[]{:S(2)}, u32[]{:S(2)}) collective-permute-start(bf16[6,64,1024]{2,1,0:T(8,128)(2,1)S(1)} %copy-done.1), channel_id=1, source_target_pairs={{0,16},{16,0},{1,17},{17,1},{2,18},{18,2},{3,19},{19,3},{4,20},{20... | collective-permute-start | bytes 2359304 | tf_op jit(solution)/shard_map/ppermute | solution.py:362
  48.1 25.2 %collective-permute-start.16 = (bf16[896,512]{1,0:T(8,128)(2,1)S(1)}, bf16[896,512]{1,0:T(8,128)(2,1)S(1)}, u32[]{:S(2)}, u32[]{:S(2)}) collective-permute-start(bf16[896,512]{1,0:T(8,128)(2,1)S(1)} %pad_maximum_fusion.6.refs_3_), channel_id=1, source_target_pairs={{0,2},{1,3},{2,0},{3,1},{4,6},{5,7},{6,4},{7,5},{8,10},{9,11},{10,... | collective-permute-start | bytes 2752520 | tf_op jit(solution)/shard_map/ppermute | solution.py:359
  48.7 17.1 %collective-permute-start.13 = (bf16[256,512]{1,0:T(8,128)(2,1)S(1)}, bf16[256,512]{1,0:T(8,128)(2,1)S(1)}, u32[]{:S(2)}, u32[]{:S(2)}) collective-permute-start(bf16[256,512]{1,0:T(8,128)(2,1)S(1)} %pad_maximum_fusion.11), channel_id=1, source_target_pairs={{4,0},{5,1},{6,2},{7,3},{0,4},{1,5},{2,6},{3,7},{12,8},{13,9},{14,... | collective-permute-start | bytes 786440 | tf_op jit(solution)/shard_map/ppermute | solution.py:366
  48.8 19.8 %collective-permute-start.14 = (bf16[256,512]{1,0:T(8,128)(2,1)S(1)}, bf16[256,512]{1,0:T(8,128)(2,1)S(1)}, u32[]{:S(2)}, u32[]{:S(2)}) collective-permute-start(bf16[256,512]{1,0:T(8,128)(2,1)S(1)} %pad_maximum_fusion.11), channel_id=1, source_target_pairs={{8,0},{9,1},{10,2},{11,3},{12,4},{13,5},{14,6},{15,7},{0,8},{1,9},... | collective-permute-start | bytes 786440 | tf_op jit(solution)/shard_map/ppermute | solution.py:366
  51.1 22.2 %collective-permute-start.15 = (bf16[256,512]{1,0:T(8,128)(2,1)S(1)}, bf16[256,512]{1,0:T(8,128)(2,1)S(1)}, u32[]{:S(2)}, u32[]{:S(2)}) collective-permute-start(bf16[256,512]{1,0:T(8,128)(2,1)S(1)} %pad_maximum_fusion.11), channel_id=1, source_target_pairs={{12,0},{13,1},{14,2},{15,3},{8,4},{9,5},{10,6},{11,7},{4,8},{5,9},... | collective-permute-start | bytes 786440 | tf_op jit(solution)/shard_map/ppermute | solution.py:366
  73.3 24.7 %collective-permute-start.17 = (bf16[2,2,6,64,1024]{4,3,2,1,0:T(8,128)(2,1)S(1)}, bf16[2,2,6,64,1024]{4,3,2,1,0:T(8,128)(2,1)S(1)}, u32[]{:S(2)}, u32[]{:S(2)}) collective-permute-start(bf16[2,2,6,64,1024]{4,3,2,1,0:T(8,128)(2,1)S(1)} %pad_maximum_fusion), channel_id=1, source_target_pairs={{0,1},{1,0},{2,3},{3,2},{4,5},{5,4},{6,7},{7,6},{8,9},{9,8},{10,11... | collective-permute-start | bytes 9437192 | tf_op jit(solution)/shard_map/ppermute | solution.py:356
  73.4 24.0 %collective-permute-start.21 = (bf16[896,512]{1,0:T(8,128)(2,1)S(1)}, bf16[896,512]{1,0:T(8,128)(2,1)S(1)}, u32[]{:S(2)}, u32[]{:S(2)}) collective-permute-start(bf16[896,512]{1,0:T(8,128)(2,1)S(1)} %pad_maximum_fusion.7.refs_4_.refs_2_), channel_id=1, source_target_pairs={{0,2},{1,3},{2,0},{3,1},{4,6},{5,7},{6,4},{7,5},{8,10},{9,11},{10,... | collective-permute-start | bytes 2752520 | tf_op jit(solution)/shard_map/ppermute | solution.py:359
  75.0 18.1 %collective-permute-start.20 = (bf16[256,512]{1,0:T(8,128)(2,1)S(1)}, bf16[256,512]{1,0:T(8,128)(2,1)S(1)}, u32[]{:S(2)}, u32[]{:S(2)}) collective-permute-start(bf16[256,512]{1,0:T(8,128)(2,1)S(1)} %get-tuple-element.45), channel_id=1, source_target_pairs={{12,0},{13,1},{14,2},{15,3},{8,4},{9,5},{10,6},{11,7},{4,8},{5,9},... | collective-permute-start | bytes 786440 | tf_op jit(solution)/shard_map/ppermute | solution.py:366
  75.6 21.8 %collective-permute-start.19 = (bf16[256,512]{1,0:T(8,128)(2,1)S(1)}, bf16[256,512]{1,0:T(8,128)(2,1)S(1)}, u32[]{:S(2)}, u32[]{:S(2)}) collective-permute-start(bf16[256,512]{1,0:T(8,128)(2,1)S(1)} %get-tuple-element.45), channel_id=1, source_target_pairs={{8,0},{9,1},{10,2},{11,3},{12,4},{13,5},{14,6},{15,7},{0,8},{1,9},... | collective-permute-start | bytes 786440 | tf_op jit(solution)/shard_map/ppermute | solution.py:366
  75.6 21.8 %collective-permute-start.18 = (bf16[256,512]{1,0:T(8,128)(2,1)S(1)}, bf16[256,512]{1,0:T(8,128)(2,1)S(1)}, u32[]{:S(2)}, u32[]{:S(2)}) collective-permute-start(bf16[256,512]{1,0:T(8,128)(2,1)S(1)} %get-tuple-element.45), channel_id=1, source_target_pairs={{4,0},{5,1},{6,2},{7,3},{0,4},{1,5},{2,6},{3,7},{12,8},{13,9},{14,... | collective-permute-start | bytes 786440 | tf_op jit(solution)/shard_map/ppermute | solution.py:366
  97.4 27.9 %collective-permute-start.22 = (bf16[896,512]{1,0:T(8,128)(2,1)S(1)}, bf16[896,512]{1,0:T(8,128)(2,1)S(1)}, u32[]{:S(2)}, u32[]{:S(2)}) collective-permute-start(bf16[896,512]{1,0:T(8,128)(2,1)S(1)} %pad_maximum_fusion.8.refs_3_.refs_5_), channel_id=1, source_target_pairs={{0,2},{1,3},{2,0},{3,1},{4,6},{5,7},{6,4},{7,5},{8,10},{9,11},{10,... | collective-permute-start | bytes 2752520 | tf_op jit(solution)/shard_map/ppermute | solution.py:359
  98.1 15.1 %collective-permute-start.23 = (bf16[256,512]{1,0:T(8,128)(2,1)S(1)}, bf16[256,512]{1,0:T(8,128)(2,1)S(1)}, u32[]{:S(2)}, u32[]{:S(2)}) collective-permute-start(bf16[256,512]{1,0:T(8,128)(2,1)S(1)} %pad_maximum_fusion.12), channel_id=1, source_target_pairs={{4,0},{5,1},{6,2},{7,3},{0,4},{1,5},{2,6},{3,7},{12,8},{13,9},{14,... | collective-permute-start | bytes 786440 | tf_op jit(solution)/shard_map/ppermute | solution.py:366
  100.9 18.6 %collective-permute-start.24 = (bf16[256,512]{1,0:T(8,128)(2,1)S(1)}, bf16[256,512]{1,0:T(8,128)(2,1)S(1)}, u32[]{:S(2)}, u32[]{:S(2)}) collective-permute-start(bf16[256,512]{1,0:T(8,128)(2,1)S(1)} %pad_maximum_fusion.12), channel_id=1, source_target_pairs={{8,0},{9,1},{10,2},{11,3},{12,4},{13,5},{14,6},{15,7},{0,8},{1,9},... | collective-permute-start | bytes 786440 | tf_op jit(solution)/shard_map/ppermute | solution.py:366
  101.6 23.7 %collective-permute-start.25 = (bf16[256,512]{1,0:T(8,128)(2,1)S(1)}, bf16[256,512]{1,0:T(8,128)(2,1)S(1)}, u32[]{:S(2)}, u32[]{:S(2)}) collective-permute-start(bf16[256,512]{1,0:T(8,128)(2,1)S(1)} %pad_maximum_fusion.12), channel_id=1, source_target_pairs={{12,0},{13,1},{14,2},{15,3},{8,4},{9,5},{10,6},{11,7},{4,8},{5,9},... | collective-permute-start | bytes 786440 | tf_op jit(solution)/shard_map/ppermute | solution.py:366
  131.8 25.2 %collective-permute-start.28 = (bf16[1024,512]{1,0:T(8,128)(2,1)S(1)}, bf16[1024,512]{1,0:T(8,128)(2,1)S(1)}, u32[]{:S(2)}, u32[]{:S(2)}) collective-permute-start(bf16[1024,512]{1,0:T(8,128)(2,1)S(1)} %pad_maximum_fusion.5.refs_2_), channel_id=1, source_target_pairs={{0,2},{1,3},{2,0},{3,1},{4,6},{5,7},{6,4},{7,5},{8,10},{9,11},{10,... | collective-permute-start | bytes 3145736 | tf_op jit(solution)/shard_map/ppermute | solution.py:359
  135.1 38.0 %collective-permute-start.31 = (bf16[2,6,64,1024]{3,2,1,0:T(8,128)(2,1)S(1)}, bf16[2,6,64,1024]{3,2,1,0:T(8,128)(2,1)S(1)}, u32[]{:S(2)}, u32[]{:S(2)}) collective-permute-start(bf16[2,6,64,1024]{3,2,1,0:T(8,128)(2,1)S(1)} %pad_maximum_fusion.3), channel_id=1, source_target_pairs={{0,16},{16,0},{1,17},{17,1},{2,18},{18,2},{3,19},{19,3},{4,20},{20... | collective-permute-start | bytes 4718600 | tf_op jit(solution)/shard_map/ppermute | solution.py:362
  (14 other events, 61.8 us)

commit v17 on v16

--- a/solution.py
+++ b/solution.py
@@ -503,7 +503,6 @@
         (True, False), over_blocks, (1,), scalars,
         (near, after(over, *shifted[3]), far), weights_of(0, 1, 2), None,
     )
-    across_y(4)
     sums = (after(sums[0], *shifted[4]), sums[1])
     *same, other_out, other_back = chunk(
         (False, True), over_blocks, (1,), scalars, tokens_of, weights_of(3), sums,
@@ -515,6 +514,7 @@
             for a, b in zip(same, (other_out, other_back))
         ]
     )
+    across_y(4, across)
     tokens_of = (after(near, across), over, far)
     across = over_x(across)
     sums = chunk(

time: 176 us -> 175 us (level); the launches traced: 176 us -> 172 us
  waiting for transfers between devices: 92.9 us -> 87.3 us
  starting transfers between devices: 33.7 us -> 36 us
    ppermute x15, waiting for transfers between devices: 64.1 us -> 55.4 us  [shift_z(): return lax.ppermute(a, 'row', pairs)]
    ppermute x5, waiting for transfers between devices: 4.81 us -> 9.78 us  [over_y(): return lax.ppermute(a, 'row', [(i, i ^ 2) for i in range(ranks)])]
    ppermute x15, starting transfers between devices: 19.2 us -> 23.3 us  [shift_z(): return lax.ppermute(a, 'row', pairs)]
    ppermute x4, starting transfers between devices: 7.23 us -> 3.94 us  [over_x(): return lax.ppermute(a, 'grp', [(0, 1), (1, 0)])]
  transfers between devices with their start and end apart: 32 -> 32, of which waited for: 18 -> 16; matrix products, arithmetic and copies ran while one was open for 4% -> 4% of each run, Pallas kernels for 18% -> 18%
where the time goes in v17:
time: 175 us; the launch traced here: 172 us
  waiting for transfers between devices  87.3 us (50%)
  Pallas kernels  39.3 us (22%)
  starting transfers between devices  36 us (21%)
  other arithmetic  5.9 us (3%)
  local copies, waits for them, and re-layouts  2.82 us (2%)
    ppermute x15, waiting for transfers between devices, shift_z(): return lax.ppermute(a, 'row', pairs)  55.4 us
    pallas_call x4, Pallas kernels, chunk(): pl.pallas_call(functools.partial(chunk_kernel, offset, kind, units, chips...  36.4 us
    ppermute x15, starting transfers between devices, shift_z(): return lax.ppermute(a, 'row', pairs)  23.3 us
    ppermute x4, waiting for transfers between devices, over_x(): return lax.ppermute(a, 'grp', [(0, 1), (1, 0)])  19.7 us
    ppermute x5, waiting for transfers between devices, over_y(): return lax.ppermute(a, 'row', [(i, i ^ 2) for i in range(ranks)])  9.78 us
    ppermute x5, starting transfers between devices, over_y(): return lax.ppermute(a, 'row', [(i, i ^ 2) for i in range(ranks)])  7.41 us
    ppermute x4, starting transfers between devices, over_x(): return lax.ppermute(a, 'grp', [(0, 1), (1, 0)])  3.94 us
  transfers between devices with their start and end apart: 32, of which 16 were waited for; matrix products, arithmetic and copies ran while one was open for 4% of the time, Pallas kernels for 18%

profile of v17, /device:TPU:8, one launch (start us, length us, event | category | flops | bytes accessed | tf_op | source)
XLA Modules:
  0.0 172.5 jit_solution(12496367000188015070)
XLA Ops:
  4.1 2.7 %collective-permute-start.7 = (bf16[256,256]{1,0:T(8,128)(2,1)S(1)}, bf16[256,256]{1,0:T(8,128)(2,1)S(1)}, u32[]{:S(2)}, u32[]{:S(2)}) collective-permute-start(bf16[256,256]{1,0:T(8,128)(2,1)S(1)} %bitcast.92), channel_id=1, source_target_pairs={{8,0},{9,1},{10,2},{11,3},{12,4},{13,5},{14,6},{15,7},{0,8},{1,9},... | collective-permute-start | bytes 393224 | tf_op jit(solution)/shard_map/ppermute | solution.py:366
  11.5 2.8 %collective-permute-done.4 = bf16[256,256]{1,0:T(8,128)(2,1)S(1)} collective-permute-done((bf16[256,256]{1,0:T(8,128)(2,1)S(1)}, bf16[256,256]{1,0:T(8,128)(2,1)S(1)}, u32[]{:S(2)}, u32[]{:S(2)}) %collective-permute-start.4) | collective-permute-done | bytes 131104 | tf_op jit(solution)/shard_map/ppermute | solution.py:366
  15.1 3.3 %collective-permute-done.2 = bf16[256,256]{1,0:T(8,128)(2,1)S(1)} collective-permute-done((bf16[256,256]{1,0:T(8,128)(2,1)S(1)}, bf16[256,256]{1,0:T(8,128)(2,1)S(1)}, u32[]{:S(2)}, u32[]{:S(2)}) %collective-permute-start.2) | collective-permute-done | bytes 131104 | tf_op jit(solution)/shard_map/ppermute | solution.py:366
  23.1 2.5 %collective-permute-start.11 = (bf16[256,512]{1,0:T(8,128)(2,1)S(1)}, bf16[256,512]{1,0:T(8,128)(2,1)S(1)}, u32[]{:S(2)}, u32[]{:S(2)}) collective-permute-start(bf16[256,512]{1,0:T(8,128)(2,1)S(1)} %get-tuple-element.40), channel_id=1, source_target_pairs={{12,0},{13,1},{14,2},{15,3},{8,4},{9,5},{10,6},{11,7},{4,8},{5,9},... | collective-permute-start | bytes 786440 | tf_op jit(solution)/shard_map/ppermute | solution.py:366
  27.5 15.2 %collective-permute-done.11 = bf16[256,512]{1,0:T(8,128)(2,1)S(1)} collective-permute-done((bf16[256,512]{1,0:T(8,128)(2,1)S(1)}, bf16[256,512]{1,0:T(8,128)(2,1)S(1)}, u32[]{:S(2)}, u32[]{:S(2)}) %collective-permute-start.11) | collective-permute-done | bytes 262176 | tf_op jit(solution)/shard_map/ppermute | solution.py:366
  42.6 4.6 %collective-permute-done.10 = bf16[256,512]{1,0:T(8,128)(2,1)S(1)} collective-permute-done((bf16[256,512]{1,0:T(8,128)(2,1)S(1)}, bf16[256,512]{1,0:T(8,128)(2,1)S(1)}, u32[]{:S(2)}, u32[]{:S(2)}) %collective-permute-start.10) | collective-permute-done | bytes 262176 | tf_op jit(solution)/shard_map/ppermute | solution.py:366
  49.4 4.3 %collective-permute-start.14 = (bf16[256,512]{1,0:T(8,128)(2,1)S(1)}, bf16[256,512]{1,0:T(8,128)(2,1)S(1)}, u32[]{:S(2)}, u32[]{:S(2)}) collective-permute-start(bf16[256,512]{1,0:T(8,128)(2,1)S(1)} %pad_maximum_fusion.11), channel_id=1, source_target_pairs={{8,0},{9,1},{10,2},{11,3},{12,4},{13,5},{14,6},{15,7},{0,8},{1,9},... | collective-permute-start | bytes 786440 | tf_op jit(solution)/shard_map/ppermute | solution.py:366
  53.8 12.9 %collective-permute-done.12 = bf16[6,64,1024]{2,1,0:T(8,128)(2,1)S(1)} collective-permute-done((bf16[6,64,1024]{2,1,0:T(8,128)(2,1)S(1)}, bf16[6,64,1024]{2,1,0:T(8,128)(2,1)S(1)}, u32[]{:S(2)}, u32[]{:S(2)}) %collective-permute-start.12) | collective-permute-done | bytes 786464 | tf_op jit(solution)/shard_map/ppermute | solution.py:362
  67.2 2.2 %collective-permute-done.15 = bf16[256,512]{1,0:T(8,128)(2,1)S(1)} collective-permute-done((bf16[256,512]{1,0:T(8,128)(2,1)S(1)}, bf16[256,512]{1,0:T(8,128)(2,1)S(1)}, u32[]{:S(2)}, u32[]{:S(2)}) %collective-permute-start.15) | collective-permute-done | bytes 262176 | tf_op jit(solution)/shard_map/ppermute | solution.py:366
  69.4 2.0 %collective-permute-done.14 = bf16[256,512]{1,0:T(8,128)(2,1)S(1)} collective-permute-done((bf16[256,512]{1,0:T(8,128)(2,1)S(1)}, bf16[256,512]{1,0:T(8,128)(2,1)S(1)}, u32[]{:S(2)}, u32[]{:S(2)}) %collective-permute-start.14) | collective-permute-done | bytes 262176 | tf_op jit(solution)/shard_map/ppermute | solution.py:366
  74.7 4.3 %collective-permute-start.19 = (bf16[256,512]{1,0:T(8,128)(2,1)S(1)}, bf16[256,512]{1,0:T(8,128)(2,1)S(1)}, u32[]{:S(2)}, u32[]{:S(2)}) collective-permute-start(bf16[256,512]{1,0:T(8,128)(2,1)S(1)} %get-tuple-element.45), channel_id=1, source_target_pairs={{8,0},{9,1},{10,2},{11,3},{12,4},{13,5},{14,6},{15,7},{0,8},{1,9},... | collective-permute-start | bytes 786440 | tf_op jit(solution)/shard_map/ppermute | solution.py:366
  79.0 14.5 %collective-permute-done.20 = bf16[256,512]{1,0:T(8,128)(2,1)S(1)} collective-permute-done((bf16[256,512]{1,0:T(8,128)(2,1)S(1)}, bf16[256,512]{1,0:T(8,128)(2,1)S(1)}, u32[]{:S(2)}, u32[]{:S(2)}) %collective-permute-start.20) | collective-permute-done | bytes 262176 | tf_op jit(solution)/shard_map/ppermute | solution.py:366
  93.5 4.0 %collective-permute-done.19 = bf16[256,512]{1,0:T(8,128)(2,1)S(1)} collective-permute-done((bf16[256,512]{1,0:T(8,128)(2,1)S(1)}, bf16[256,512]{1,0:T(8,128)(2,1)S(1)}, u32[]{:S(2)}, u32[]{:S(2)}) %collective-permute-start.19) | collective-permute-done | bytes 262176 | tf_op jit(solution)/shard_map/ppermute | solution.py:366
  98.8 4.3 %collective-permute-start.24 = (bf16[256,512]{1,0:T(8,128)(2,1)S(1)}, bf16[256,512]{1,0:T(8,128)(2,1)S(1)}, u32[]{:S(2)}, u32[]{:S(2)}) collective-permute-start(bf16[256,512]{1,0:T(8,128)(2,1)S(1)} %pad_maximum_fusion.12), channel_id=1, source_target_pairs={{8,0},{9,1},{10,2},{11,3},{12,4},{13,5},{14,6},{15,7},{0,8},{1,9},... | collective-permute-start | bytes 786440 | tf_op jit(solution)/shard_map/ppermute | solution.py:366
  103.1 10.7 %chunk.4 = (f32[768,1024]{1,0:T(8,128)S(1)}, f32[768,1024]{1,0:T(8,128)S(1)}) custom-call(s32[24]{0:T(128)S(1)} %pad_add_fusion.3.sorted_ref, s32[2]{0:T(128)S(1)} %pad_add_fusion.4.place_ref, s32[24]{0:T(128)S(1)} %pad_add_fusion.5.perm_ref, bf16[2,6,64,1024]{3,2,1,0:T(8,128)(2,1)S(1)} %get-tuple-element.48.refs_0_, ...), custom_call_target="tpu_custom_call" | custom-call | flops 5368709120 | bytes 20971520 | tf_op jit(solution)/shard_map/chunk/pallas_call | solution.py:265
  113.8 4.9 %collective-permute-done.25 = bf16[256,512]{1,0:T(8,128)(2,1)S(1)} collective-permute-done((bf16[256,512]{1,0:T(8,128)(2,1)S(1)}, bf16[256,512]{1,0:T(8,128)(2,1)S(1)}, u32[]{:S(2)}, u32[]{:S(2)}) %collective-permute-start.25) | collective-permute-done | bytes 262176 | tf_op jit(solution)/shard_map/ppermute | solution.py:366
  118.8 1.7 collective-permute-done.24
  120.5 5.8 %chunk.5 = (bf16[6,64,1024]{2,1,0:T(8,128)(2,1)S(1)}, bf16[6,64,1024]{2,1,0:T(8,128)(2,1)S(1)}, bf16[6,64,1024]{2,1,0:T(8,128)(2,1)S(1)}, bf16[6,64,1024]{2,1,0:T(8,128)(2,1)S(1)}) custom-call(s32[24]{0:T(128)S(1)} %pad_add_fusion.3.sorted_ref, s32[2]{0:T(128)S(1)} %pad_add_fusion.4.place_ref, s32[24]{0:T(128)S(1)} %pad_add_fusion.5.perm_ref, ...), custom_call_target="tpu_custom_call" | custom-call | tf_op jit(solution)/shard_map/chunk/pallas_call | solution.py:265
  130.3 3.1 %collective-permute-start.28 = (bf16[1024,512]{1,0:T(8,128)(2,1)S(1)}, bf16[1024,512]{1,0:T(8,128)(2,1)S(1)}, u32[]{:S(2)}, u32[]{:S(2)}) collective-permute-start(bf16[1024,512]{1,0:T(8,128)(2,1)S(1)} %pad_maximum_fusion.5.refs_2_), channel_id=1, source_target_pairs={{0,2},{1,3},{2,0},{3,1},{4,6},{5,7},{6,4},{7,5},{8,10},{9,11},{10,... | collective-permute-start | bytes 3145736 | tf_op jit(solution)/shard_map/ppermute | solution.py:359
  133.4 13.7 %chunk.6 = (f32[768,1024]{1,0:T(8,128)S(1)}, f32[768,1024]{1,0:T(8,128)S(1)}) custom-call(s32[24]{0:T(128)S(1)} %pad_add_fusion.3.sorted_ref, s32[2]{0:T(128)S(1)} %pad_add_fusion.4.place_ref, s32[24]{0:T(128)S(1)} %pad_add_fusion.5.perm_ref, bf16[2,6,64,1024]{3,2,1,0:T(8,128)(2,1)S(1)} %get-tuple-element.57.refs_0_, ...), custom_call_target="tpu_custom_call" | custom-call | tf_op jit(solution)/shard_map/chunk/pallas_call | solution.py:265
  147.1 9.8 %collective-permute-done.28.refs_3_ = bf16[1024,512]{1,0:T(8,128)(2,1)S(1)} collective-permute-done((bf16[1024,512]{1,0:T(8,128)(2,1)S(1)}, bf16[1024,512]{1,0:T(8,128)(2,1)S(1)}, u32[]{:S(2)}, u32[]{:S(2)}) %collective-permute-start.28) | collective-permute-done | bytes 1048608 | tf_op jit(solution)/shard_map/ppermute | solution.py:359
  156.8 6.2 %chunk.7 = (f32[6,64,1024]{2,1,0:T(8,128)S(1)}, f32[6,64,1024]{2,1,0:T(8,128)S(1)}, bf16[6,64,1024]{2,1,0:T(8,128)(2,1)S(1)}, bf16[6,64,1024]{2,1,0:T(8,128)(2,1)S(1)}) custom-call(s32[24]{0:T(128)S(1)} %pad_add_fusion.3.sorted_ref, s32[2]{0:T(128)S(1)} %pad_add_fusion.4.place_ref, s32[24]{0:T(128)S(1)} %pad_add_fusion.5.perm_ref, ...), custom_call_target="tpu_custom_call" | custom-call | tf_op jit(solution)/shard_map/chunk/pallas_call | solution.py:265
  163.6 5.9 %collective-permute-done.31.across_ref = bf16[2,6,64,1024]{3,2,1,0:T(8,128)(2,1)S(1)} collective-permute-done((bf16[2,6,64,1024]{3,2,1,0:T(8,128)(2,1)S(1)}, bf16[2,6,64,1024]{3,2,1,0:T(8,128)(2,1)S(1)}, u32[]{:S(2)}, u32[]{:S(2)}) %collective-permute-start.31) | collective-permute-done | bytes 1572896 | tf_op jit(solution)/shard_map/ppermute | solution.py:362
  169.5 2.9 %finish.1 = (bf16[6,64,1024]{2,1,0:T(8,128)(2,1)}, bf16[6,64,1024]{2,1,0:T(8,128)(2,1)}, f32[6,64]{1,0:T(8,128)}) custom-call(s32[6]{0:T(128)S(1)} %bitcast.75, bf16[6,64,1024]{2,1,0:T(8,128)(2,1)S(1)} %copy-done, bf16[6,64,1024]{2,1,0:T(8,128)(2,1)S(1)} %copy-done.1, f32[2,1024]{1,0:T(2,128)S(1)} %copy-done.2, ...), custom_call_target="tpu_custom_call" | custom-call | tf_op jit(solution)/shard_map/finish/pallas_call | solution.py:315
  (113 shorter events, 26.9 us)
Async XLA Ops:
  4.1 17.2 %collective-permute-start.7 = (bf16[256,256]{1,0:T(8,128)(2,1)S(1)}, bf16[256,256]{1,0:T(8,128)(2,1)S(1)}, u32[]{:S(2)}, u32[]{:S(2)}) collective-permute-start(bf16[256,256]{1,0:T(8,128)(2,1)S(1)} %bitcast.92), channel_id=1, source_target_pairs={{8,0},{9,1},{10,2},{11,3},{12,4},{13,5},{14,6},{15,7},{0,8},{1,9},... | collective-permute-start | bytes 393224 | tf_op jit(solution)/shard_map/ppermute | solution.py:366
  7.2 11.3 %collective-permute-start.2 = (bf16[256,256]{1,0:T(8,128)(2,1)S(1)}, bf16[256,256]{1,0:T(8,128)(2,1)S(1)}, u32[]{:S(2)}, u32[]{:S(2)}) collective-permute-start(bf16[256,256]{1,0:T(8,128)(2,1)S(1)} %bitcast.94), channel_id=1, source_target_pairs={{12,0},{13,1},{14,2},{15,3},{8,4},{9,5},{10,6},{11,7},{4,8},{5,9},... | collective-permute-start | bytes 393224 | tf_op jit(solution)/shard_map/ppermute | solution.py:366
  10.5 10.2 %collective-permute-start.6 = (bf16[2,2,64,1152]{3,2,0,1:T(8,128)(2,1)S(1)}, bf16[2,2,64,1152]{3,2,0,1:T(8,128)(2,1)S(1)}, u32[]{:S(2)}, u32[]{:S(2)}) collective-permute-start(bf16[2,2,64,1152]{3,2,0,1:T(8,128)(2,1)S(1)} %pad_maximum_fusion.10), channel_id=1, source_target_pairs={{0,1},{1,0},{2,3},{3,2},{4,5},{5,4},{6,7},{7,6},{8,9},{9,8},{10,11... | collective-permute-start | bytes 1769480 | tf_op jit(solution)/shard_map/ppermute | solution.py:356
  18.5 30.4 %collective-permute-start.5 = (bf16[6,64,1024]{2,1,0:T(8,128)(2,1)S(1)}, bf16[6,64,1024]{2,1,0:T(8,128)(2,1)S(1)}, u32[]{:S(2)}, u32[]{:S(2)}) collective-permute-start(bf16[6,64,1024]{2,1,0:T(8,128)(2,1)S(1)} %fusion.2), channel_id=1, source_target_pairs={{0,16},{16,0},{1,17},{17,1},{2,18},{18,2},{3,19},{19,3},{4,20},{20... | collective-permute-start | bytes 2359304 | tf_op jit(solution)/shard_map/ppermute | solution.py:362
  21.4 25.9 %collective-permute-start.8 = (bf16[1792,256]{1,0:T(8,128)(2,1)S(1)}, bf16[1792,256]{1,0:T(8,128)(2,1)S(1)}, u32[]{:S(2)}, u32[]{:S(2)}) collective-permute-start(bf16[1792,256]{1,0:T(8,128)(2,1)S(1)} %constant_dynamic-update-slice_fusion.refs_2_), channel_id=1, source_target_pairs={{0,2},{1,3},{2,0},{3,1},{4,6},{5,7},{6,4},{7,5},{8,10},{9,11},{10,... | collective-permute-start | bytes 2752520 | tf_op jit(solution)/shard_map/ppermute | solution.py:359
  23.1 19.5 %collective-permute-start.11 = (bf16[256,512]{1,0:T(8,128)(2,1)S(1)}, bf16[256,512]{1,0:T(8,128)(2,1)S(1)}, u32[]{:S(2)}, u32[]{:S(2)}) collective-permute-start(bf16[256,512]{1,0:T(8,128)(2,1)S(1)} %get-tuple-element.40), channel_id=1, source_target_pairs={{12,0},{13,1},{14,2},{15,3},{8,4},{9,5},{10,6},{11,7},{4,8},{5,9},... | collective-permute-start | bytes 786440 | tf_op jit(solution)/shard_map/ppermute | solution.py:366
  25.7 21.6 %collective-permute-start.10 = (bf16[256,512]{1,0:T(8,128)(2,1)S(1)}, bf16[256,512]{1,0:T(8,128)(2,1)S(1)}, u32[]{:S(2)}, u32[]{:S(2)}) collective-permute-start(bf16[256,512]{1,0:T(8,128)(2,1)S(1)} %get-tuple-element.40), channel_id=1, source_target_pairs={{8,0},{9,1},{10,2},{11,3},{12,4},{13,5},{14,6},{15,7},{0,8},{1,9},... | collective-permute-start | bytes 786440 | tf_op jit(solution)/shard_map/ppermute | solution.py:366
  25.7 21.6 %collective-permute-start.9 = (bf16[256,512]{1,0:T(8,128)(2,1)S(1)}, bf16[256,512]{1,0:T(8,128)(2,1)S(1)}, u32[]{:S(2)}, u32[]{:S(2)}) collective-permute-start(bf16[256,512]{1,0:T(8,128)(2,1)S(1)} %get-tuple-element.40), channel_id=1, source_target_pairs={{4,0},{5,1},{6,2},{7,3},{0,4},{1,5},{2,6},{3,7},{12,8},{13,9},{14,... | collective-permute-start | bytes 786440 | tf_op jit(solution)/shard_map/ppermute | solution.py:366
  47.3 19.5 %collective-permute-start.12 = (bf16[6,64,1024]{2,1,0:T(8,128)(2,1)S(1)}, bf16[6,64,1024]{2,1,0:T(8,128)(2,1)S(1)}, u32[]{:S(2)}, u32[]{:S(2)}) collective-permute-start(bf16[6,64,1024]{2,1,0:T(8,128)(2,1)S(1)} %copy-done.1), channel_id=1, source_target_pairs={{0,16},{16,0},{1,17},{17,1},{2,18},{18,2},{3,19},{19,3},{4,20},{20... | collective-permute-start | bytes 2359304 | tf_op jit(solution)/shard_map/ppermute | solution.py:362
  48.2 23.2 %collective-permute-start.16 = (bf16[896,512]{1,0:T(8,128)(2,1)S(1)}, bf16[896,512]{1,0:T(8,128)(2,1)S(1)}, u32[]{:S(2)}, u32[]{:S(2)}) collective-permute-start(bf16[896,512]{1,0:T(8,128)(2,1)S(1)} %pad_maximum_fusion.6.refs_3_), channel_id=1, source_target_pairs={{0,2},{1,3},{2,0},{3,1},{4,6},{5,7},{6,4},{7,5},{8,10},{9,11},{10,... | collective-permute-start | bytes 2752520 | tf_op jit(solution)/shard_map/ppermute | solution.py:359
  48.9 20.5 %collective-permute-start.15 = (bf16[256,512]{1,0:T(8,128)(2,1)S(1)}, bf16[256,512]{1,0:T(8,128)(2,1)S(1)}, u32[]{:S(2)}, u32[]{:S(2)}) collective-permute-start(bf16[256,512]{1,0:T(8,128)(2,1)S(1)} %pad_maximum_fusion.11), channel_id=1, source_target_pairs={{12,0},{13,1},{14,2},{15,3},{8,4},{9,5},{10,6},{11,7},{4,8},{5,9},... | collective-permute-start | bytes 786440 | tf_op jit(solution)/shard_map/ppermute | solution.py:366
  49.4 22.1 %collective-permute-start.14 = (bf16[256,512]{1,0:T(8,128)(2,1)S(1)}, bf16[256,512]{1,0:T(8,128)(2,1)S(1)}, u32[]{:S(2)}, u32[]{:S(2)}) collective-permute-start(bf16[256,512]{1,0:T(8,128)(2,1)S(1)} %pad_maximum_fusion.11), channel_id=1, source_target_pairs={{8,0},{9,1},{10,2},{11,3},{12,4},{13,5},{14,6},{15,7},{0,8},{1,9},... | collective-permute-start | bytes 786440 | tf_op jit(solution)/shard_map/ppermute | solution.py:366
  53.7 17.8 %collective-permute-start.13 = (bf16[256,512]{1,0:T(8,128)(2,1)S(1)}, bf16[256,512]{1,0:T(8,128)(2,1)S(1)}, u32[]{:S(2)}, u32[]{:S(2)}) collective-permute-start(bf16[256,512]{1,0:T(8,128)(2,1)S(1)} %pad_maximum_fusion.11), channel_id=1, source_target_pairs={{4,0},{5,1},{6,2},{7,3},{0,4},{1,5},{2,6},{3,7},{12,8},{13,9},{14,... | collective-permute-start | bytes 786440 | tf_op jit(solution)/shard_map/ppermute | solution.py:366
  71.5 26.7 %collective-permute-start.17 = (bf16[2,2,6,64,1024]{4,3,2,1,0:T(8,128)(2,1)S(1)}, bf16[2,2,6,64,1024]{4,3,2,1,0:T(8,128)(2,1)S(1)}, u32[]{:S(2)}, u32[]{:S(2)}) collective-permute-start(bf16[2,2,6,64,1024]{4,3,2,1,0:T(8,128)(2,1)S(1)} %pad_maximum_fusion), channel_id=1, source_target_pairs={{0,1},{1,0},{2,3},{3,2},{4,5},{5,4},{6,7},{7,6},{8,9},{9,8},{10,11... | collective-permute-start | bytes 9437192 | tf_op jit(solution)/shard_map/ppermute | solution.py:356
  71.6 26.0 %collective-permute-start.21 = (bf16[896,512]{1,0:T(8,128)(2,1)S(1)}, bf16[896,512]{1,0:T(8,128)(2,1)S(1)}, u32[]{:S(2)}, u32[]{:S(2)}) collective-permute-start(bf16[896,512]{1,0:T(8,128)(2,1)S(1)} %pad_maximum_fusion.7.refs_4_.refs_2_), channel_id=1, source_target_pairs={{0,2},{1,3},{2,0},{3,1},{4,6},{5,7},{6,4},{7,5},{8,10},{9,11},{10,... | collective-permute-start | bytes 2752520 | tf_op jit(solution)/shard_map/ppermute | solution.py:359
  73.2 20.4 %collective-permute-start.20 = (bf16[256,512]{1,0:T(8,128)(2,1)S(1)}, bf16[256,512]{1,0:T(8,128)(2,1)S(1)}, u32[]{:S(2)}, u32[]{:S(2)}) collective-permute-start(bf16[256,512]{1,0:T(8,128)(2,1)S(1)} %get-tuple-element.45), channel_id=1, source_target_pairs={{12,0},{13,1},{14,2},{15,3},{8,4},{9,5},{10,6},{11,7},{4,8},{5,9},... | collective-permute-start | bytes 786440 | tf_op jit(solution)/shard_map/ppermute | solution.py:366
  74.7 22.8 %collective-permute-start.19 = (bf16[256,512]{1,0:T(8,128)(2,1)S(1)}, bf16[256,512]{1,0:T(8,128)(2,1)S(1)}, u32[]{:S(2)}, u32[]{:S(2)}) collective-permute-start(bf16[256,512]{1,0:T(8,128)(2,1)S(1)} %get-tuple-element.45), channel_id=1, source_target_pairs={{8,0},{9,1},{10,2},{11,3},{12,4},{13,5},{14,6},{15,7},{0,8},{1,9},... | collective-permute-start | bytes 786440 | tf_op jit(solution)/shard_map/ppermute | solution.py:366
  79.0 18.5 %collective-permute-start.18 = (bf16[256,512]{1,0:T(8,128)(2,1)S(1)}, bf16[256,512]{1,0:T(8,128)(2,1)S(1)}, u32[]{:S(2)}, u32[]{:S(2)}) collective-permute-start(bf16[256,512]{1,0:T(8,128)(2,1)S(1)} %get-tuple-element.45), channel_id=1, source_target_pairs={{4,0},{5,1},{6,2},{7,3},{0,4},{1,5},{2,6},{3,7},{12,8},{13,9},{14,... | collective-permute-start | bytes 786440 | tf_op jit(solution)/shard_map/ppermute | solution.py:366
  97.6 22.9 %collective-permute-start.22 = (bf16[896,512]{1,0:T(8,128)(2,1)S(1)}, bf16[896,512]{1,0:T(8,128)(2,1)S(1)}, u32[]{:S(2)}, u32[]{:S(2)}) collective-permute-start(bf16[896,512]{1,0:T(8,128)(2,1)S(1)} %pad_maximum_fusion.8.refs_3_.refs_5_), channel_id=1, source_target_pairs={{0,2},{1,3},{2,0},{3,1},{4,6},{5,7},{6,4},{7,5},{8,10},{9,11},{10,... | collective-permute-start | bytes 2752520 | tf_op jit(solution)/shard_map/ppermute | solution.py:359
  98.2 20.5 %collective-permute-start.25 = (bf16[256,512]{1,0:T(8,128)(2,1)S(1)}, bf16[256,512]{1,0:T(8,128)(2,1)S(1)}, u32[]{:S(2)}, u32[]{:S(2)}) collective-permute-start(bf16[256,512]{1,0:T(8,128)(2,1)S(1)} %pad_maximum_fusion.12), channel_id=1, source_target_pairs={{12,0},{13,1},{14,2},{15,3},{8,4},{9,5},{10,6},{11,7},{4,8},{5,9},... | collective-permute-start | bytes 786440 | tf_op jit(solution)/shard_map/ppermute | solution.py:366
  98.8 21.7 %collective-permute-start.24 = (bf16[256,512]{1,0:T(8,128)(2,1)S(1)}, bf16[256,512]{1,0:T(8,128)(2,1)S(1)}, u32[]{:S(2)}, u32[]{:S(2)}) collective-permute-start(bf16[256,512]{1,0:T(8,128)(2,1)S(1)} %pad_maximum_fusion.12), channel_id=1, source_target_pairs={{8,0},{9,1},{10,2},{11,3},{12,4},{13,5},{14,6},{15,7},{0,8},{1,9},... | collective-permute-start | bytes 786440 | tf_op jit(solution)/shard_map/ppermute | solution.py:366
  103.0 17.4 %collective-permute-start.23 = (bf16[256,512]{1,0:T(8,128)(2,1)S(1)}, bf16[256,512]{1,0:T(8,128)(2,1)S(1)}, u32[]{:S(2)}, u32[]{:S(2)}) collective-permute-start(bf16[256,512]{1,0:T(8,128)(2,1)S(1)} %pad_maximum_fusion.12), channel_id=1, source_target_pairs={{4,0},{5,1},{6,2},{7,3},{0,4},{1,5},{2,6},{3,7},{12,8},{13,9},{14,... | collective-permute-start | bytes 786440 | tf_op jit(solution)/shard_map/ppermute | solution.py:366
  130.3 26.6 %collective-permute-start.28 = (bf16[1024,512]{1,0:T(8,128)(2,1)S(1)}, bf16[1024,512]{1,0:T(8,128)(2,1)S(1)}, u32[]{:S(2)}, u32[]{:S(2)}) collective-permute-start(bf16[1024,512]{1,0:T(8,128)(2,1)S(1)} %pad_maximum_fusion.5.refs_2_), channel_id=1, source_target_pairs={{0,2},{1,3},{2,0},{3,1},{4,6},{5,7},{6,4},{7,5},{8,10},{9,11},{10,... | collective-permute-start | bytes 3145736 | tf_op jit(solution)/shard_map/ppermute | solution.py:359
  133.4 36.2 %collective-permute-start.31 = (bf16[2,6,64,1024]{3,2,1,0:T(8,128)(2,1)S(1)}, bf16[2,6,64,1024]{3,2,1,0:T(8,128)(2,1)S(1)}, u32[]{:S(2)}, u32[]{:S(2)}) collective-permute-start(bf16[2,6,64,1024]{3,2,1,0:T(8,128)(2,1)S(1)} %pad_maximum_fusion.3), channel_id=1, source_target_pairs={{0,16},{16,0},{1,17},{17,1},{2,18},{18,2},{3,19},{19,3},{4,20},{20... | collective-permute-start | bytes 4718600 | tf_op jit(solution)/shard_map/ppermute | solution.py:362
  (14 other events, 67.9 us)

commit v18 on v15

--- a/solution.py
+++ b/solution.py
@@ -281,7 +281,7 @@
 
 def finish_kernel(
     member_ref, x_ref, g_ref, gain_ref, out_ref, back_ref, other_out_ref, other_back_ref,
-    across_ref, value_ref, grad_ref, coupling_ref,
+    across_out_ref, across_back_ref, value_ref, grad_ref, coupling_ref,
 ):
     rows, seq, width = x_ref.shape
     diagonal = lax.broadcasted_iota(jnp.int32, (seq, seq), 0) == lax.broadcasted_iota(
@@ -293,10 +293,10 @@
         normed = x * inv
         gain = gain_ref[pl.ds(member_ref[pl.program_id(0) * rows + r], 1), :]
         back = gain * (
-            back_ref[r] + other_back_ref[r].astype(F32) + across_ref[1, r].astype(F32)
+            back_ref[r] + other_back_ref[r].astype(F32) + across_back_ref[r].astype(F32)
         )
         stat = jnp.sum(normed * back, axis=1, keepdims=True) / width
-        out = out_ref[r] + other_out_ref[r].astype(F32) + across_ref[0, r].astype(F32)
+        out = out_ref[r] + other_out_ref[r].astype(F32) + across_out_ref[r].astype(F32)
         value_ref[r] = (x + out).astype(BF16)
         grad_ref[r] = (g_ref[r].astype(F32) + (back - normed * stat) * inv).astype(BF16)
         line = jnp.sum(jnp.where(diagonal, stat, 0.0), axis=0, keepdims=True)
@@ -307,14 +307,13 @@
     rows, seq, width = x.shape
     step = math.gcd(rows, 2)
     row = pl.BlockSpec((step, seq, width), lambda r, mem: (r, 0, 0))
-    two = pl.BlockSpec((2, step, seq, width), lambda r, mem: (0, r, 0, 0))
     return pl.pallas_call(
         finish_kernel,
         grid_spec=pltpu.PrefetchScalarGridSpec(
             num_scalar_prefetch=1,
             grid=(rows // step,),
             in_specs=[
-                row, row, pl.BlockSpec(gain.shape, lambda r, mem: (0, 0)), row, row, row, row, two
+                row, row, pl.BlockSpec(gain.shape, lambda r, mem: (0, 0)), row, row, row, row, row, row
             ],
             out_specs=[row, row, pl.BlockSpec((rows, seq), lambda r, mem: (0, 0))],
         ),
@@ -504,14 +503,12 @@
         (False, True), over_blocks, (1,), scalars, tokens_of, weights_of(3), sums,
         (BF16, BF16), 0,
     )
-    across = jnp.stack(
-        [
-            (a.astype(F32) + partner(b).astype(F32)).astype(BF16)
-            for a, b in zip(same, (other_out, other_back))
-        ]
-    )
-    tokens_of = (after(near, across), over, far)
-    across = over_x(across)
+    summed = [
+        (a.astype(F32) + partner(b).astype(F32)).astype(BF16)
+        for a, b in zip(same, (other_out, other_back))
+    ]
+    tokens_of = (after(near, *summed), over, far)
+    across = [over_x(a) for a in summed]
     sums = chunk(
         (True, False), own_blocks, (0,), scalars, tokens_of, weights_of(0, 1, 2, 3), None, None, 0
     )
@@ -521,7 +518,7 @@
     return tuple(
         finish(
             pick_own, tokens_in, upstream, norm_gain, out, back,
-            partner(packed_out), partner(packed_back), across,
+            partner(packed_out), partner(packed_back), *across,
         )
     )
 

time: 175 us -> 174 us (level)
    ppermute x4 -> x5, waiting for transfers between devices: 20.9 us -> 23.7 us  [over_x(): return lax.ppermute(a, 'grp', [(0, 1), (1, 0)])]
    ppermute x8, waiting for transfers between devices: 2.91 us -> 0.14 us  [partner(): return lax.ppermute(a, 'row', [(i, i ^ 1) for i in range(ranks)])]
    ppermute x4 -> x5, starting transfers between devices: 6.03 us -> 7.44 us  [over_x(): return lax.ppermute(a, 'grp', [(0, 1), (1, 0)])]
  transfers between devices with their start and end apart: 32 -> 33, of which waited for: 17 -> 16; matrix products, arithmetic and copies ran while one was open for 4% -> 4% of each run, Pallas kernels for 18% -> 18%
where the time goes in v18:
time: 174 us; the launch traced here: 173 us
  waiting for transfers between devices  86.6 us (50%)
  Pallas kernels  39.3 us (23%)
  starting transfers between devices  37.7 us (22%)
  other arithmetic  5.76 us (3%)
  local copies, waits for them, and re-layouts  2.83 us (2%)
    ppermute x15, waiting for transfers between devices, shift_z(): lax.ppermute(a, 'row', [(i, (i + 4 * d) % ranks) for i in range(ranks)])  57.3 us
    pallas_call x4, Pallas kernels, chunk(): pl.pallas_call(functools.partial(chunk_kernel, offset, kind, units, chips...  36.5 us
    ppermute x5, waiting for transfers between devices, over_x(): return lax.ppermute(a, 'grp', [(0, 1), (1, 0)])  23.7 us
    ppermute x15, starting transfers between devices, shift_z(): lax.ppermute(a, 'row', [(i, (i + 4 * d) % ranks) for i in range(ranks)])  23 us
    ppermute x5, starting transfers between devices, over_x(): return lax.ppermute(a, 'grp', [(0, 1), (1, 0)])  7.44 us
    ppermute x5, starting transfers between devices, over_y(): return lax.ppermute(a, 'row', [(i, i ^ 2) for i in range(ranks)])  5.9 us
    ppermute x5, waiting for transfers between devices, over_y(): return lax.ppermute(a, 'row', [(i, i ^ 2) for i in range(ranks)])  5.48 us
  transfers between devices with their start and end apart: 33, of which 16 were waited for; matrix products, arithmetic and copies ran while one was open for 4% of the time, Pallas kernels for 18%

profile of v18, /device:TPU:8, one launch (start us, length us, event | category | flops | bytes accessed | tf_op | source)
XLA Modules:
  0.0 173.4 jit_solution(13483849558683191984)
XLA Ops:
  4.1 2.0 %collective-permute-start.4 = (bf16[256,256]{1,0:T(8,128)(2,1)S(1)}, bf16[256,256]{1,0:T(8,128)(2,1)S(1)}, u32[]{:S(2)}, u32[]{:S(2)}) collective-permute-start(bf16[256,256]{1,0:T(8,128)(2,1)S(1)} %bitcast.89), channel_id=1, source_target_pairs={{0,4},{1,5},{2,6},{3,7},{4,8},{5,9},{6,10},{7,11},{8,12},{9,13},{1... | collective-permute-start | bytes 393224 | tf_op jit(solution)/shard_map/ppermute | solution.py:360
  6.2 4.5 %collective-permute-start.7 = (bf16[256,256]{1,0:T(8,128)(2,1)S(1)}, bf16[256,256]{1,0:T(8,128)(2,1)S(1)}, u32[]{:S(2)}, u32[]{:S(2)}) collective-permute-start(bf16[256,256]{1,0:T(8,128)(2,1)S(1)} %bitcast.91), channel_id=1, source_target_pairs={{0,8},{1,9},{2,10},{3,11},{4,12},{5,13},{6,14},{7,15},{8,0},{9,1},... | collective-permute-start | bytes 393224 | tf_op jit(solution)/shard_map/ppermute | solution.py:360
  21.1 3.5 %collective-permute-start.10 = (bf16[256,512]{1,0:T(8,128)(2,1)S(1)}, bf16[256,512]{1,0:T(8,128)(2,1)S(1)}, u32[]{:S(2)}, u32[]{:S(2)}) collective-permute-start(bf16[256,512]{1,0:T(8,128)(2,1)S(1)} %get-tuple-element.40), channel_id=1, source_target_pairs={{0,8},{1,9},{2,10},{3,11},{4,12},{5,13},{6,14},{7,15},{8,0},{9,1},... | collective-permute-start | bytes 786440 | tf_op jit(solution)/shard_map/ppermute | solution.py:360
  25.2 4.9 %collective-permute-done.9 = bf16[256,512]{1,0:T(8,128)(2,1)S(1)} collective-permute-done((bf16[256,512]{1,0:T(8,128)(2,1)S(1)}, bf16[256,512]{1,0:T(8,128)(2,1)S(1)}, u32[]{:S(2)}, u32[]{:S(2)}) %collective-permute-start.9) | collective-permute-done | bytes 262176 | tf_op jit(solution)/shard_map/ppermute | solution.py:360
  30.1 13.6 %collective-permute-done.10 = bf16[256,512]{1,0:T(8,128)(2,1)S(1)} collective-permute-done((bf16[256,512]{1,0:T(8,128)(2,1)S(1)}, bf16[256,512]{1,0:T(8,128)(2,1)S(1)}, u32[]{:S(2)}, u32[]{:S(2)}) %collective-permute-start.10) | collective-permute-done | bytes 262176 | tf_op jit(solution)/shard_map/ppermute | solution.py:360
  43.7 3.4 %collective-permute-done.11 = bf16[256,512]{1,0:T(8,128)(2,1)S(1)} collective-permute-done((bf16[256,512]{1,0:T(8,128)(2,1)S(1)}, bf16[256,512]{1,0:T(8,128)(2,1)S(1)}, u32[]{:S(2)}, u32[]{:S(2)}) %collective-permute-start.11) | collective-permute-done | bytes 262176 | tf_op jit(solution)/shard_map/ppermute | solution.py:360
  50.8 15.5 %collective-permute-done.12 = bf16[6,64,1024]{2,1,0:T(8,128)(2,1)S(1)} collective-permute-done((bf16[6,64,1024]{2,1,0:T(8,128)(2,1)S(1)}, bf16[6,64,1024]{2,1,0:T(8,128)(2,1)S(1)}, u32[]{:S(2)}, u32[]{:S(2)}) %collective-permute-start.12) | collective-permute-done | bytes 786464 | tf_op jit(solution)/shard_map/ppermute | solution.py:357
  66.8 4.0 %collective-permute-done.14 = bf16[256,512]{1,0:T(8,128)(2,1)S(1)} collective-permute-done((bf16[256,512]{1,0:T(8,128)(2,1)S(1)}, bf16[256,512]{1,0:T(8,128)(2,1)S(1)}, u32[]{:S(2)}, u32[]{:S(2)}) %collective-permute-start.14) | collective-permute-done | bytes 262176 | tf_op jit(solution)/shard_map/ppermute | solution.py:360
  72.5 3.4 %collective-permute-start.19 = (bf16[256,512]{1,0:T(8,128)(2,1)S(1)}, bf16[256,512]{1,0:T(8,128)(2,1)S(1)}, u32[]{:S(2)}, u32[]{:S(2)}) collective-permute-start(bf16[256,512]{1,0:T(8,128)(2,1)S(1)} %get-tuple-element.45), channel_id=1, source_target_pairs={{0,8},{1,9},{2,10},{3,11},{4,12},{5,13},{6,14},{7,15},{8,0},{9,1},... | collective-permute-start | bytes 786440 | tf_op jit(solution)/shard_map/ppermute | solution.py:360
  75.9 2.9 %collective-permute-start.18 = (bf16[256,512]{1,0:T(8,128)(2,1)S(1)}, bf16[256,512]{1,0:T(8,128)(2,1)S(1)}, u32[]{:S(2)}, u32[]{:S(2)}) collective-permute-start(bf16[256,512]{1,0:T(8,128)(2,1)S(1)} %get-tuple-element.45), channel_id=1, source_target_pairs={{0,4},{1,5},{2,6},{3,7},{4,8},{5,9},{6,10},{7,11},{8,12},{9,13},{1... | collective-permute-start | bytes 786440 | tf_op jit(solution)/shard_map/ppermute | solution.py:360
  78.8 2.8 %collective-permute-done.20 = bf16[256,512]{1,0:T(8,128)(2,1)S(1)} collective-permute-done((bf16[256,512]{1,0:T(8,128)(2,1)S(1)}, bf16[256,512]{1,0:T(8,128)(2,1)S(1)}, u32[]{:S(2)}, u32[]{:S(2)}) %collective-permute-start.20) | collective-permute-done | bytes 262176 | tf_op jit(solution)/shard_map/ppermute | solution.py:360
  81.6 12.2 %collective-permute-done.19 = bf16[256,512]{1,0:T(8,128)(2,1)S(1)} collective-permute-done((bf16[256,512]{1,0:T(8,128)(2,1)S(1)}, bf16[256,512]{1,0:T(8,128)(2,1)S(1)}, u32[]{:S(2)}, u32[]{:S(2)}) %collective-permute-start.19) | collective-permute-done | bytes 262176 | tf_op jit(solution)/shard_map/ppermute | solution.py:360
  93.8 4.9 %collective-permute-done.18 = bf16[256,512]{1,0:T(8,128)(2,1)S(1)} collective-permute-done((bf16[256,512]{1,0:T(8,128)(2,1)S(1)}, bf16[256,512]{1,0:T(8,128)(2,1)S(1)}, u32[]{:S(2)}, u32[]{:S(2)}) %collective-permute-start.18) | collective-permute-done | bytes 262176 | tf_op jit(solution)/shard_map/ppermute | solution.py:360
  99.4 2.5 %collective-permute-start.23 = (bf16[256,512]{1,0:T(8,128)(2,1)S(1)}, bf16[256,512]{1,0:T(8,128)(2,1)S(1)}, u32[]{:S(2)}, u32[]{:S(2)}) collective-permute-start(bf16[256,512]{1,0:T(8,128)(2,1)S(1)} %pad_maximum_fusion.11), channel_id=1, source_target_pairs={{0,4},{1,5},{2,6},{3,7},{4,8},{5,9},{6,10},{7,11},{8,12},{9,13},{1... | collective-permute-start | bytes 786440 | tf_op jit(solution)/shard_map/ppermute | solution.py:360
  103.5 10.5 %chunk.4 = (f32[768,1024]{1,0:T(8,128)S(1)}, f32[768,1024]{1,0:T(8,128)S(1)}) custom-call(s32[24]{0:T(128)S(1)} %pad_add_fusion.3.sorted_ref, s32[2]{0:T(128)S(1)} %pad_add_fusion.4.place_ref, s32[24]{0:T(128)S(1)} %pad_add_fusion.5.perm_ref, bf16[2,6,64,1024]{3,2,1,0:T(8,128)(2,1)S(1)} %get-tuple-element.48.refs_0_, ...), custom_call_target="tpu_custom_call" | custom-call | flops 5368709120 | bytes 20971520 | tf_op jit(solution)/shard_map/chunk/pallas_call | solution.py:261
  114.0 5.9 %collective-permute-done.23 = bf16[256,512]{1,0:T(8,128)(2,1)S(1)} collective-permute-done((bf16[256,512]{1,0:T(8,128)(2,1)S(1)}, bf16[256,512]{1,0:T(8,128)(2,1)S(1)}, u32[]{:S(2)}, u32[]{:S(2)}) %collective-permute-start.23) | collective-permute-done | bytes 262176 | tf_op jit(solution)/shard_map/ppermute | solution.py:360
  119.9 3.7 %collective-permute-done.24 = bf16[256,512]{1,0:T(8,128)(2,1)S(1)} collective-permute-done((bf16[256,512]{1,0:T(8,128)(2,1)S(1)}, bf16[256,512]{1,0:T(8,128)(2,1)S(1)}, u32[]{:S(2)}, u32[]{:S(2)}) %collective-permute-start.24) | collective-permute-done | bytes 262176 | tf_op jit(solution)/shard_map/ppermute | solution.py:360
  124.6 5.8 %chunk.5 = (bf16[6,64,1024]{2,1,0:T(8,128)(2,1)S(1)}, bf16[6,64,1024]{2,1,0:T(8,128)(2,1)S(1)}, bf16[6,64,1024]{2,1,0:T(8,128)(2,1)S(1)}, bf16[6,64,1024]{2,1,0:T(8,128)(2,1)S(1)}) custom-call(s32[24]{0:T(128)S(1)} %pad_add_fusion.3.sorted_ref, s32[2]{0:T(128)S(1)} %pad_add_fusion.4.place_ref, s32[24]{0:T(128)S(1)} %pad_add_fusion.5.perm_ref, ...), custom_call_target="tpu_custom_call" | custom-call | tf_op jit(solution)/shard_map/chunk/pallas_call | solution.py:261
  133.1 2.7 %collective-permute-start.31 = (bf16[6,64,1024]{2,1,0:T(8,128)(2,1)S(1)}, bf16[6,64,1024]{2,1,0:T(8,128)(2,1)S(1)}, u32[]{:S(2)}, u32[]{:S(2)}) collective-permute-start(bf16[6,64,1024]{2,1,0:T(8,128)(2,1)S(1)} %add_convert_fusion.1), channel_id=1, source_target_pairs={{0,16},{16,0},{1,17},{17,1},{2,18},{18,2},{3,19},{19,3},{4,20},{20... | collective-permute-start | bytes 2359304 | tf_op jit(solution)/shard_map/ppermute | solution.py:357
  136.9 13.8 %chunk.6 = (f32[768,1024]{1,0:T(8,128)S(1)}, f32[768,1024]{1,0:T(8,128)S(1)}) custom-call(s32[24]{0:T(128)S(1)} %pad_add_fusion.3.sorted_ref, s32[2]{0:T(128)S(1)} %pad_add_fusion.4.place_ref, s32[24]{0:T(128)S(1)} %pad_add_fusion.5.perm_ref, bf16[2,6,64,1024]{3,2,1,0:T(8,128)(2,1)S(1)} %get-tuple-element.57.refs_0_, ...), custom_call_target="tpu_custom_call" | custom-call | tf_op jit(solution)/shard_map/chunk/pallas_call | solution.py:261
  150.8 5.5 %collective-permute-done.28.refs_3_ = bf16[1024,512]{1,0:T(8,128)(2,1)S(1)} collective-permute-done((bf16[1024,512]{1,0:T(8,128)(2,1)S(1)}, bf16[1024,512]{1,0:T(8,128)(2,1)S(1)}, u32[]{:S(2)}, u32[]{:S(2)}) %collective-permute-start.28) | collective-permute-done | bytes 1048608 | tf_op jit(solution)/shard_map/ppermute | solution.py:354
  156.3 6.3 %chunk.7 = (f32[6,64,1024]{2,1,0:T(8,128)S(1)}, f32[6,64,1024]{2,1,0:T(8,128)S(1)}, bf16[6,64,1024]{2,1,0:T(8,128)(2,1)S(1)}, bf16[6,64,1024]{2,1,0:T(8,128)(2,1)S(1)}) custom-call(s32[24]{0:T(128)S(1)} %pad_add_fusion.3.sorted_ref, s32[2]{0:T(128)S(1)} %pad_add_fusion.4.place_ref, s32[24]{0:T(128)S(1)} %pad_add_fusion.5.perm_ref, ...), custom_call_target="tpu_custom_call" | custom-call | tf_op jit(solution)/shard_map/chunk/pallas_call | solution.py:261
  163.1 7.4 %collective-permute-done.32.across_back_ref = bf16[6,64,1024]{2,1,0:T(8,128)(2,1)S(1)} collective-permute-done((bf16[6,64,1024]{2,1,0:T(8,128)(2,1)S(1)}, bf16[6,64,1024]{2,1,0:T(8,128)(2,1)S(1)}, u32[]{:S(2)}, u32[]{:S(2)}) %collective-permute-start.32) | collective-permute-done | bytes 786464 | tf_op jit(solution)/shard_map/ppermute | solution.py:357
  170.5 2.8 %finish.1 = (bf16[6,64,1024]{2,1,0:T(8,128)(2,1)}, bf16[6,64,1024]{2,1,0:T(8,128)(2,1)}, f32[6,64]{1,0:T(8,128)}) custom-call(s32[6]{0:T(128)S(1)} %bitcast.71, bf16[6,64,1024]{2,1,0:T(8,128)(2,1)S(1)} %copy-done, bf16[6,64,1024]{2,1,0:T(8,128)(2,1)S(1)} %copy-done.1, f32[2,1024]{1,0:T(2,128)S(1)} %copy-done.2, ...), custom_call_target="tpu_custom_call" | custom-call | tf_op jit(solution)/shard_map/finish/pallas_call | solution.py:310
  (114 shorter events, 27.6 us)
Async XLA Ops:
  4.1 12.0 %collective-permute-start.2 = (bf16[256,256]{1,0:T(8,128)(2,1)S(1)}, bf16[256,256]{1,0:T(8,128)(2,1)S(1)}, u32[]{:S(2)}, u32[]{:S(2)}) collective-permute-start(bf16[256,256]{1,0:T(8,128)(2,1)S(1)} %bitcast.88), channel_id=1, source_target_pairs={{0,12},{1,13},{2,14},{3,15},{4,0},{5,1},{6,2},{7,3},{8,4},{9,5},{1... | collective-permute-start | bytes 393224 | tf_op jit(solution)/shard_map/ppermute | solution.py:360
  4.1 11.2 %collective-permute-start.4 = (bf16[256,256]{1,0:T(8,128)(2,1)S(1)}, bf16[256,256]{1,0:T(8,128)(2,1)S(1)}, u32[]{:S(2)}, u32[]{:S(2)}) collective-permute-start(bf16[256,256]{1,0:T(8,128)(2,1)S(1)} %bitcast.89), channel_id=1, source_target_pairs={{0,4},{1,5},{2,6},{3,7},{4,8},{5,9},{6,10},{7,11},{8,12},{9,13},{1... | collective-permute-start | bytes 393224 | tf_op jit(solution)/shard_map/ppermute | solution.py:360
  6.2 12.9 %collective-permute-start.7 = (bf16[256,256]{1,0:T(8,128)(2,1)S(1)}, bf16[256,256]{1,0:T(8,128)(2,1)S(1)}, u32[]{:S(2)}, u32[]{:S(2)}) collective-permute-start(bf16[256,256]{1,0:T(8,128)(2,1)S(1)} %bitcast.91), channel_id=1, source_target_pairs={{0,8},{1,9},{2,10},{3,11},{4,12},{5,13},{6,14},{7,15},{8,0},{9,1},... | collective-permute-start | bytes 393224 | tf_op jit(solution)/shard_map/ppermute | solution.py:360
  16.2 32.5 %collective-permute-start.5 = (bf16[6,64,1024]{2,1,0:T(8,128)(2,1)S(1)}, bf16[6,64,1024]{2,1,0:T(8,128)(2,1)S(1)}, u32[]{:S(2)}, u32[]{:S(2)}) collective-permute-start(bf16[6,64,1024]{2,1,0:T(8,128)(2,1)S(1)} %fusion.2), channel_id=1, source_target_pairs={{0,16},{16,0},{1,17},{17,1},{2,18},{18,2},{3,19},{19,3},{4,20},{20... | collective-permute-start | bytes 2359304 | tf_op jit(solution)/shard_map/ppermute | solution.py:357
  19.1 28.0 %collective-permute-start.8 = (bf16[1792,256]{1,0:T(8,128)(2,1)S(1)}, bf16[1792,256]{1,0:T(8,128)(2,1)S(1)}, u32[]{:S(2)}, u32[]{:S(2)}) collective-permute-start(bf16[1792,256]{1,0:T(8,128)(2,1)S(1)} %constant_dynamic-update-slice_fusion.refs_2_), channel_id=1, source_target_pairs={{0,2},{1,3},{2,0},{3,1},{4,6},{5,7},{6,4},{7,5},{8,10},{9,11},{10,... | collective-permute-start | bytes 2752520 | tf_op jit(solution)/shard_map/ppermute | solution.py:354
  20.9 9.2 %collective-permute-start.9 = (bf16[256,512]{1,0:T(8,128)(2,1)S(1)}, bf16[256,512]{1,0:T(8,128)(2,1)S(1)}, u32[]{:S(2)}, u32[]{:S(2)}) collective-permute-start(bf16[256,512]{1,0:T(8,128)(2,1)S(1)} %get-tuple-element.40), channel_id=1, source_target_pairs={{0,4},{1,5},{2,6},{3,7},{4,8},{5,9},{6,10},{7,11},{8,12},{9,13},{1... | collective-permute-start | bytes 786440 | tf_op jit(solution)/shard_map/ppermute | solution.py:360
  21.1 22.6 %collective-permute-start.10 = (bf16[256,512]{1,0:T(8,128)(2,1)S(1)}, bf16[256,512]{1,0:T(8,128)(2,1)S(1)}, u32[]{:S(2)}, u32[]{:S(2)}) collective-permute-start(bf16[256,512]{1,0:T(8,128)(2,1)S(1)} %get-tuple-element.40), channel_id=1, source_target_pairs={{0,8},{1,9},{2,10},{3,11},{4,12},{5,13},{6,14},{7,15},{8,0},{9,1},... | collective-permute-start | bytes 786440 | tf_op jit(solution)/shard_map/ppermute | solution.py:360
  24.6 22.5 %collective-permute-start.11 = (bf16[256,512]{1,0:T(8,128)(2,1)S(1)}, bf16[256,512]{1,0:T(8,128)(2,1)S(1)}, u32[]{:S(2)}, u32[]{:S(2)}) collective-permute-start(bf16[256,512]{1,0:T(8,128)(2,1)S(1)} %get-tuple-element.40), channel_id=1, source_target_pairs={{0,12},{1,13},{2,14},{3,15},{4,0},{5,1},{6,2},{7,3},{8,4},{9,5},{1... | collective-permute-start | bytes 786440 | tf_op jit(solution)/shard_map/ppermute | solution.py:360
  47.1 19.2 %collective-permute-start.12 = (bf16[6,64,1024]{2,1,0:T(8,128)(2,1)S(1)}, bf16[6,64,1024]{2,1,0:T(8,128)(2,1)S(1)}, u32[]{:S(2)}, u32[]{:S(2)}) collective-permute-start(bf16[6,64,1024]{2,1,0:T(8,128)(2,1)S(1)} %copy-done.1), channel_id=1, source_target_pairs={{0,16},{16,0},{1,17},{17,1},{2,18},{18,2},{3,19},{19,3},{4,20},{20... | collective-permute-start | bytes 2359304 | tf_op jit(solution)/shard_map/ppermute | solution.py:357
  48.1 22.7 %collective-permute-start.16 = (bf16[896,512]{1,0:T(8,128)(2,1)S(1)}, bf16[896,512]{1,0:T(8,128)(2,1)S(1)}, u32[]{:S(2)}, u32[]{:S(2)}) collective-permute-start(bf16[896,512]{1,0:T(8,128)(2,1)S(1)} %pad_maximum_fusion.5.refs_3_), channel_id=1, source_target_pairs={{0,2},{1,3},{2,0},{3,1},{4,6},{5,7},{6,4},{7,5},{8,10},{9,11},{10,... | collective-permute-start | bytes 2752520 | tf_op jit(solution)/shard_map/ppermute | solution.py:354
  48.7 18.1 %collective-permute-start.13 = (bf16[256,512]{1,0:T(8,128)(2,1)S(1)}, bf16[256,512]{1,0:T(8,128)(2,1)S(1)}, u32[]{:S(2)}, u32[]{:S(2)}) collective-permute-start(bf16[256,512]{1,0:T(8,128)(2,1)S(1)} %pad_maximum_fusion.10), channel_id=1, source_target_pairs={{0,4},{1,5},{2,6},{3,7},{4,8},{5,9},{6,10},{7,11},{8,12},{9,13},{1... | collective-permute-start | bytes 786440 | tf_op jit(solution)/shard_map/ppermute | solution.py:360
  48.8 22.0 %collective-permute-start.14 = (bf16[256,512]{1,0:T(8,128)(2,1)S(1)}, bf16[256,512]{1,0:T(8,128)(2,1)S(1)}, u32[]{:S(2)}, u32[]{:S(2)}) collective-permute-start(bf16[256,512]{1,0:T(8,128)(2,1)S(1)} %pad_maximum_fusion.10), channel_id=1, source_target_pairs={{0,8},{1,9},{2,10},{3,11},{4,12},{5,13},{6,14},{7,15},{8,0},{9,1},... | collective-permute-start | bytes 786440 | tf_op jit(solution)/shard_map/ppermute | solution.py:360
  48.9 21.9 %collective-permute-start.15 = (bf16[256,512]{1,0:T(8,128)(2,1)S(1)}, bf16[256,512]{1,0:T(8,128)(2,1)S(1)}, u32[]{:S(2)}, u32[]{:S(2)}) collective-permute-start(bf16[256,512]{1,0:T(8,128)(2,1)S(1)} %pad_maximum_fusion.10), channel_id=1, source_target_pairs={{0,12},{1,13},{2,14},{3,15},{4,0},{5,1},{6,2},{7,3},{8,4},{9,5},{1... | collective-permute-start | bytes 786440 | tf_op jit(solution)/shard_map/ppermute | solution.py:360
  70.8 28.6 %collective-permute-start.17 = (bf16[2,2,6,64,1024]{4,3,2,1,0:T(8,128)(2,1)S(1)}, bf16[2,2,6,64,1024]{4,3,2,1,0:T(8,128)(2,1)S(1)}, u32[]{:S(2)}, u32[]{:S(2)}) collective-permute-start(bf16[2,2,6,64,1024]{4,3,2,1,0:T(8,128)(2,1)S(1)} %pad_maximum_fusion), channel_id=1, source_target_pairs={{0,1},{1,0},{2,3},{3,2},{4,5},{5,4},{6,7},{7,6},{8,9},{9,8},{10,11... | collective-permute-start | bytes 9437192 | tf_op jit(solution)/shard_map/ppermute | solution.py:351
  70.9 27.9 %collective-permute-start.21 = (bf16[896,512]{1,0:T(8,128)(2,1)S(1)}, bf16[896,512]{1,0:T(8,128)(2,1)S(1)}, u32[]{:S(2)}, u32[]{:S(2)}) collective-permute-start(bf16[896,512]{1,0:T(8,128)(2,1)S(1)} %pad_maximum_fusion.6.refs_4_.refs_2_), channel_id=1, source_target_pairs={{0,2},{1,3},{2,0},{3,1},{4,6},{5,7},{6,4},{7,5},{8,10},{9,11},{10,... | collective-permute-start | bytes 2752520 | tf_op jit(solution)/shard_map/ppermute | solution.py:354
  72.5 21.3 %collective-permute-start.19 = (bf16[256,512]{1,0:T(8,128)(2,1)S(1)}, bf16[256,512]{1,0:T(8,128)(2,1)S(1)}, u32[]{:S(2)}, u32[]{:S(2)}) collective-permute-start(bf16[256,512]{1,0:T(8,128)(2,1)S(1)} %get-tuple-element.45), channel_id=1, source_target_pairs={{0,8},{1,9},{2,10},{3,11},{4,12},{5,13},{6,14},{7,15},{8,0},{9,1},... | collective-permute-start | bytes 786440 | tf_op jit(solution)/shard_map/ppermute | solution.py:360
  75.9 22.8 %collective-permute-start.18 = (bf16[256,512]{1,0:T(8,128)(2,1)S(1)}, bf16[256,512]{1,0:T(8,128)(2,1)S(1)}, u32[]{:S(2)}, u32[]{:S(2)}) collective-permute-start(bf16[256,512]{1,0:T(8,128)(2,1)S(1)} %get-tuple-element.45), channel_id=1, source_target_pairs={{0,4},{1,5},{2,6},{3,7},{4,8},{5,9},{6,10},{7,11},{8,12},{9,13},{1... | collective-permute-start | bytes 786440 | tf_op jit(solution)/shard_map/ppermute | solution.py:360
  98.8 25.8 %collective-permute-start.22 = (bf16[896,512]{1,0:T(8,128)(2,1)S(1)}, bf16[896,512]{1,0:T(8,128)(2,1)S(1)}, u32[]{:S(2)}, u32[]{:S(2)}) collective-permute-start(bf16[896,512]{1,0:T(8,128)(2,1)S(1)} %pad_maximum_fusion.7.refs_3_.refs_5_), channel_id=1, source_target_pairs={{0,2},{1,3},{2,0},{3,1},{4,6},{5,7},{6,4},{7,5},{8,10},{9,11},{10,... | collective-permute-start | bytes 2752520 | tf_op jit(solution)/shard_map/ppermute | solution.py:354
  99.4 20.5 %collective-permute-start.23 = (bf16[256,512]{1,0:T(8,128)(2,1)S(1)}, bf16[256,512]{1,0:T(8,128)(2,1)S(1)}, u32[]{:S(2)}, u32[]{:S(2)}) collective-permute-start(bf16[256,512]{1,0:T(8,128)(2,1)S(1)} %pad_maximum_fusion.11), channel_id=1, source_target_pairs={{0,4},{1,5},{2,6},{3,7},{4,8},{5,9},{6,10},{7,11},{8,12},{9,13},{1... | collective-permute-start | bytes 786440 | tf_op jit(solution)/shard_map/ppermute | solution.py:360
  102.0 21.7 %collective-permute-start.24 = (bf16[256,512]{1,0:T(8,128)(2,1)S(1)}, bf16[256,512]{1,0:T(8,128)(2,1)S(1)}, u32[]{:S(2)}, u32[]{:S(2)}) collective-permute-start(bf16[256,512]{1,0:T(8,128)(2,1)S(1)} %pad_maximum_fusion.11), channel_id=1, source_target_pairs={{0,8},{1,9},{2,10},{3,11},{4,12},{5,13},{6,14},{7,15},{8,0},{9,1},... | collective-permute-start | bytes 786440 | tf_op jit(solution)/shard_map/ppermute | solution.py:360
  102.4 22.2 %collective-permute-start.25 = (bf16[256,512]{1,0:T(8,128)(2,1)S(1)}, bf16[256,512]{1,0:T(8,128)(2,1)S(1)}, u32[]{:S(2)}, u32[]{:S(2)}) collective-permute-start(bf16[256,512]{1,0:T(8,128)(2,1)S(1)} %pad_maximum_fusion.11), channel_id=1, source_target_pairs={{0,12},{1,13},{2,14},{3,15},{4,0},{5,1},{6,2},{7,3},{8,4},{9,5},{1... | collective-permute-start | bytes 786440 | tf_op jit(solution)/shard_map/ppermute | solution.py:360
  131.0 25.2 %collective-permute-start.28 = (bf16[1024,512]{1,0:T(8,128)(2,1)S(1)}, bf16[1024,512]{1,0:T(8,128)(2,1)S(1)}, u32[]{:S(2)}, u32[]{:S(2)}) collective-permute-start(bf16[1024,512]{1,0:T(8,128)(2,1)S(1)} %pad_maximum_fusion.4.refs_2_), channel_id=1, source_target_pairs={{0,2},{1,3},{2,0},{3,1},{4,6},{5,7},{6,4},{7,5},{8,10},{9,11},{10,... | collective-permute-start | bytes 3145736 | tf_op jit(solution)/shard_map/ppermute | solution.py:354
  133.1 30.0 %collective-permute-start.31 = (bf16[6,64,1024]{2,1,0:T(8,128)(2,1)S(1)}, bf16[6,64,1024]{2,1,0:T(8,128)(2,1)S(1)}, u32[]{:S(2)}, u32[]{:S(2)}) collective-permute-start(bf16[6,64,1024]{2,1,0:T(8,128)(2,1)S(1)} %add_convert_fusion.1), channel_id=1, source_target_pairs={{0,16},{16,0},{1,17},{17,1},{2,18},{18,2},{3,19},{19,3},{4,20},{20... | collective-permute-start | bytes 2359304 | tf_op jit(solution)/shard_map/ppermute | solution.py:357
  136.1 34.4 %collective-permute-start.32 = (bf16[6,64,1024]{2,1,0:T(8,128)(2,1)S(1)}, bf16[6,64,1024]{2,1,0:T(8,128)(2,1)S(1)}, u32[]{:S(2)}, u32[]{:S(2)}) collective-permute-start(bf16[6,64,1024]{2,1,0:T(8,128)(2,1)S(1)} %add_convert_fusion), channel_id=1, source_target_pairs={{0,16},{16,0},{1,17},{17,1},{2,18},{18,2},{3,19},{19,3},{4,20},{20... | collective-permute-start | bytes 2359304 | tf_op jit(solution)/shard_map/ppermute | solution.py:357
  (15 other events, 83.1 us)

commit v19 on v18

--- a/solution.py
+++ b/solution.py
@@ -460,6 +460,7 @@
 
     per_block = math.gcd(2 * rows, 4)
     per_chip = 2 * rows // per_block
+    g_over = over_x(upstream)
     along_z(0)
     pick_own = member_pick[:, 0]
     pick_near = jnp.concatenate([pick_own, over_x(after(pick_own, send[0]))])
@@ -485,7 +486,7 @@
 
     along_z(2, there[0], lifted_over, *scalars)
     across_y(1)
-    over = jnp.stack([lifted_over, over_x(after(upstream, there[0], *shifted[1]))])
+    over = jnp.stack([lifted_over, g_over])
     along_z(3, there[1], over)
     across_y(2)
     far = partner(after(jnp.stack([near, over]), *shifted[2], there[1]))
@@ -498,7 +499,7 @@
         (near, after(over, *shifted[3]), far), weights_of(0, 1, 2), None,
     )
     across_y(4)
-    sums = (after(sums[0], *shifted[4]), sums[1])
+    sums = (after(sums[0], shifted[4][0]), sums[1])
     *same, other_out, other_back = chunk(
         (False, True), over_blocks, (1,), scalars, tokens_of, weights_of(3), sums,
         (BF16, BF16), 0,

time: 174 us -> 179 us (1.029)
  the two profiles are of different devices: /device:TPU:8 before, /device:TPU:0 now
where the time goes in v19:
time: 179 us
  waiting for transfers between devices  84.7 us (47%)
  starting transfers between devices  45.5 us (25%)
  Pallas kernels  39 us (22%)
  other arithmetic  5.75 us (3%)
  local copies, waits for them, and re-layouts  2.83 us (2%)
    ppermute x15, waiting for transfers between devices, shift_z(): lax.ppermute(a, 'row', [(i, (i + 4 * d) % ranks) for i in range(ranks)])  46.7 us
    pallas_call x4, Pallas kernels, chunk(): pl.pallas_call(functools.partial(chunk_kernel, offset, kind, units, chips...  36.2 us
    ppermute x15, starting transfers between devices, shift_z(): lax.ppermute(a, 'row', [(i, (i + 4 * d) % ranks) for i in range(ranks)])  30.7 us
    ppermute x5, waiting for transfers between devices, over_x(): return lax.ppermute(a, 'grp', [(0, 1), (1, 0)])  23.1 us
    ppermute x5, waiting for transfers between devices, over_y(): return lax.ppermute(a, 'row', [(i, i ^ 2) for i in range(ranks)])  13.4 us
    ppermute x5, starting transfers between devices, over_x(): return lax.ppermute(a, 'grp', [(0, 1), (1, 0)])  6.79 us
    ppermute x5, starting transfers between devices, over_y(): return lax.ppermute(a, 'row', [(i, i ^ 2) for i in range(ranks)])  5.75 us
  transfers between devices with their start and end apart: 33, of which 13 were waited for; matrix products, arithmetic and copies ran while one was open for 4% of the time, Pallas kernels for 20%

profile of v19, /device:TPU:0, one launch (start us, length us, event | category | flops | bytes accessed | tf_op | source)
XLA Modules:
  0.0 178.9 jit_solution(6400759846172865742)
XLA Ops:
  2.8 2.6 %collective-permute-start.6 = (bf16[6,64,1024]{2,1,0:T(8,128)(2,1)}, bf16[6,64,1024]{2,1,0:T(8,128)(2,1)S(1)}, u32[]{:S(2)}, u32[]{:S(2)}) collective-permute-start(bf16[6,64,1024]{2,1,0:T(8,128)(2,1)} %g_ref.1), channel_id=1, source_target_pairs={{0,16},{16,0},{1,17},{17,1},{2,18},{18,2},{3,19},{19,3},{4,20},{20... | collective-permute-start | bytes 2359304 | tf_op jit(solution)/shard_map/ppermute | solution.py:357
  7.0 3.7 %collective-permute-start.2 = (bf16[256,256]{1,0:T(8,128)(2,1)S(1)}, bf16[256,256]{1,0:T(8,128)(2,1)S(1)}, u32[]{:S(2)}, u32[]{:S(2)}) collective-permute-start(bf16[256,256]{1,0:T(8,128)(2,1)S(1)} %bitcast.88), channel_id=1, source_target_pairs={{0,12},{1,13},{2,14},{3,15},{4,0},{5,1},{6,2},{7,3},{8,4},{9,5},{1... | collective-permute-start | bytes 393224 | tf_op jit(solution)/shard_map/ppermute | solution.py:360
  13.6 10.2 %collective-permute-done.1 = s32[6]{0:T(128)S(1)} collective-permute-done((s32[6]{0:T(128)}, s32[6]{0:T(128)S(1)}, u32[]{:S(2)}, u32[]{:S(2)}) %collective-permute-start.1) | collective-permute-done | bytes 56 | tf_op jit(solution)/shard_map/ppermute | solution.py:357
  27.4 1.9 %collective-permute-start.12 = (bf16[1792,256]{1,0:T(8,128)(2,1)S(1)}, bf16[1792,256]{1,0:T(8,128)(2,1)S(1)}, u32[]{:S(2)}, u32[]{:S(2)}) collective-permute-start(bf16[1792,256]{1,0:T(8,128)(2,1)S(1)} %constant_dynamic-update-slice_fusion.refs_2_), channel_id=1, source_target_pairs={{0,2},{1,3},{2,0},{3,1},{4,6},{5,7},{6,4},{7,5},{8,10},{9,11},{10,... | collective-permute-start | bytes 2752520 | tf_op jit(solution)/shard_map/ppermute | solution.py:354
  31.1 2.6 %collective-permute-start.10 = (bf16[256,512]{1,0:T(8,128)(2,1)S(1)}, bf16[256,512]{1,0:T(8,128)(2,1)S(1)}, u32[]{:S(2)}, u32[]{:S(2)}) collective-permute-start(bf16[256,512]{1,0:T(8,128)(2,1)S(1)} %get-tuple-element.39), channel_id=1, source_target_pairs={{0,8},{1,9},{2,10},{3,11},{4,12},{5,13},{6,14},{7,15},{8,0},{9,1},... | collective-permute-start | bytes 786440 | tf_op jit(solution)/shard_map/ppermute | solution.py:360
  35.1 5.3 %collective-permute-done.9 = bf16[256,512]{1,0:T(8,128)(2,1)S(1)} collective-permute-done((bf16[256,512]{1,0:T(8,128)(2,1)S(1)}, bf16[256,512]{1,0:T(8,128)(2,1)S(1)}, u32[]{:S(2)}, u32[]{:S(2)}) %collective-permute-start.9) | collective-permute-done | bytes 262176 | tf_op jit(solution)/shard_map/ppermute | solution.py:360
  41.9 8.9 %collective-permute-done.10 = bf16[256,512]{1,0:T(8,128)(2,1)S(1)} collective-permute-done((bf16[256,512]{1,0:T(8,128)(2,1)S(1)}, bf16[256,512]{1,0:T(8,128)(2,1)S(1)}, u32[]{:S(2)}, u32[]{:S(2)}) %collective-permute-start.10) | collective-permute-done | bytes 262176 | tf_op jit(solution)/shard_map/ppermute | solution.py:360
  51.9 6.3 %collective-permute-done.5 = bf16[6,64,1024]{2,1,0:T(8,128)(2,1)S(1)} collective-permute-done((bf16[6,64,1024]{2,1,0:T(8,128)(2,1)S(1)}, bf16[6,64,1024]{2,1,0:T(8,128)(2,1)S(1)}, u32[]{:S(2)}, u32[]{:S(2)}) %collective-permute-start.5) | collective-permute-done | bytes 786464 | tf_op jit(solution)/shard_map/ppermute | solution.py:357
  58.2 4.2 %collective-permute-start.13 = (bf16[256,512]{1,0:T(8,128)(2,1)S(1)}, bf16[256,512]{1,0:T(8,128)(2,1)S(1)}, u32[]{:S(2)}, u32[]{:S(2)}) collective-permute-start(bf16[256,512]{1,0:T(8,128)(2,1)S(1)} %pad_maximum_fusion.10), channel_id=1, source_target_pairs={{0,4},{1,5},{2,6},{3,7},{4,8},{5,9},{6,10},{7,11},{8,12},{9,13},{1... | collective-permute-start | bytes 786440 | tf_op jit(solution)/shard_map/ppermute | solution.py:360
  62.4 1.9 %collective-permute-start.14 = (bf16[256,512]{1,0:T(8,128)(2,1)S(1)}, bf16[256,512]{1,0:T(8,128)(2,1)S(1)}, u32[]{:S(2)}, u32[]{:S(2)}) collective-permute-start(bf16[256,512]{1,0:T(8,128)(2,1)S(1)} %pad_maximum_fusion.10), channel_id=1, source_target_pairs={{0,8},{1,9},{2,10},{3,11},{4,12},{5,13},{6,14},{7,15},{8,0},{9,1},... | collective-permute-start | bytes 786440 | tf_op jit(solution)/shard_map/ppermute | solution.py:360
  64.3 2.9 %collective-permute-start.15 = (bf16[256,512]{1,0:T(8,128)(2,1)S(1)}, bf16[256,512]{1,0:T(8,128)(2,1)S(1)}, u32[]{:S(2)}, u32[]{:S(2)}) collective-permute-start(bf16[256,512]{1,0:T(8,128)(2,1)S(1)} %pad_maximum_fusion.10), channel_id=1, source_target_pairs={{0,12},{1,13},{2,14},{3,15},{4,0},{5,1},{6,2},{7,3},{8,4},{9,5},{1... | collective-permute-start | bytes 786440 | tf_op jit(solution)/shard_map/ppermute | solution.py:360
  69.3 7.6 %collective-permute-done.14 = bf16[256,512]{1,0:T(8,128)(2,1)S(1)} collective-permute-done((bf16[256,512]{1,0:T(8,128)(2,1)S(1)}, bf16[256,512]{1,0:T(8,128)(2,1)S(1)}, u32[]{:S(2)}, u32[]{:S(2)}) %collective-permute-start.14) | collective-permute-done | bytes 262176 | tf_op jit(solution)/shard_map/ppermute | solution.py:360
  78.4 6.4 %collective-permute-start.20 = (bf16[256,512]{1,0:T(8,128)(2,1)S(1)}, bf16[256,512]{1,0:T(8,128)(2,1)S(1)}, u32[]{:S(2)}, u32[]{:S(2)}) collective-permute-start(bf16[256,512]{1,0:T(8,128)(2,1)S(1)} %get-tuple-element.43), channel_id=1, source_target_pairs={{0,12},{1,13},{2,14},{3,15},{4,0},{5,1},{6,2},{7,3},{8,4},{9,5},{1... | collective-permute-start | bytes 786440 | tf_op jit(solution)/shard_map/ppermute | solution.py:360
  86.0 5.6 %collective-permute-done.20 = bf16[256,512]{1,0:T(8,128)(2,1)S(1)} collective-permute-done((bf16[256,512]{1,0:T(8,128)(2,1)S(1)}, bf16[256,512]{1,0:T(8,128)(2,1)S(1)}, u32[]{:S(2)}, u32[]{:S(2)}) %collective-permute-start.20) | collective-permute-done | bytes 262176 | tf_op jit(solution)/shard_map/ppermute | solution.py:360
  91.5 17.7 %collective-permute-done.19 = bf16[256,512]{1,0:T(8,128)(2,1)S(1)} collective-permute-done((bf16[256,512]{1,0:T(8,128)(2,1)S(1)}, bf16[256,512]{1,0:T(8,128)(2,1)S(1)}, u32[]{:S(2)}, u32[]{:S(2)}) %collective-permute-start.19) | collective-permute-done | bytes 262176 | tf_op jit(solution)/shard_map/ppermute | solution.py:360
  110.3 3.8 %collective-permute-start.27 = (bf16[256,512]{1,0:T(8,128)(2,1)S(1)}, bf16[256,512]{1,0:T(8,128)(2,1)S(1)}, u32[]{:S(2)}, u32[]{:S(2)}) collective-permute-start(bf16[256,512]{1,0:T(8,128)(2,1)S(1)} %pad_maximum_fusion.11), channel_id=1, source_target_pairs={{0,12},{1,13},{2,14},{3,15},{4,0},{5,1},{6,2},{7,3},{8,4},{9,5},{1... | collective-permute-start | bytes 786440 | tf_op jit(solution)/shard_map/ppermute | solution.py:360
  114.1 10.5 %chunk.4 = (f32[768,1024]{1,0:T(8,128)S(1)}, f32[768,1024]{1,0:T(8,128)S(1)}) custom-call(s32[24]{0:T(128)S(1)} %pad_add_fusion.3.sorted_ref, s32[2]{0:T(128)S(1)} %pad_add_fusion.4.place_ref, s32[24]{0:T(128)S(1)} %pad_add_fusion.5.perm_ref, bf16[2,6,64,1024]{3,2,1,0:T(8,128)(2,1)S(1)} %get-tuple-element.46.refs_0_, ...), custom_call_target="tpu_custom_call" | custom-call | flops 5368709120 | bytes 20971520 | tf_op jit(solution)/shard_map/chunk/pallas_call | solution.py:261
  124.6 6.4 %collective-permute-done.22.refs_5_.refs_9_ = bf16[896,512]{1,0:T(8,128)(2,1)S(1)} collective-permute-done((bf16[896,512]{1,0:T(8,128)(2,1)S(1)}, bf16[896,512]{1,0:T(8,128)(2,1)S(1)}, u32[]{:S(2)}, u32[]{:S(2)}) %collective-permute-start.22) | collective-permute-done | bytes 917536 | tf_op jit(solution)/shard_map/ppermute | solution.py:354
  131.0 5.8 %chunk.5 = (bf16[6,64,1024]{2,1,0:T(8,128)(2,1)S(1)}, bf16[6,64,1024]{2,1,0:T(8,128)(2,1)S(1)}, bf16[6,64,1024]{2,1,0:T(8,128)(2,1)S(1)}, bf16[6,64,1024]{2,1,0:T(8,128)(2,1)S(1)}) custom-call(s32[24]{0:T(128)S(1)} %pad_add_fusion.3.sorted_ref, s32[2]{0:T(128)S(1)} %pad_add_fusion.4.place_ref, s32[24]{0:T(128)S(1)} %pad_add_fusion.5.perm_ref, ...), custom_call_target="tpu_custom_call" | custom-call | tf_op jit(solution)/shard_map/chunk/pallas_call | solution.py:261
  142.0 13.7 %chunk.6 = (f32[768,1024]{1,0:T(8,128)S(1)}, f32[768,1024]{1,0:T(8,128)S(1)}) custom-call(s32[24]{0:T(128)S(1)} %pad_add_fusion.3.sorted_ref, s32[2]{0:T(128)S(1)} %pad_add_fusion.4.place_ref, s32[24]{0:T(128)S(1)} %pad_add_fusion.5.perm_ref, bf16[2,6,64,1024]{3,2,1,0:T(8,128)(2,1)S(1)} %get-tuple-element.55.refs_0_, ...), custom_call_target="tpu_custom_call" | custom-call | tf_op jit(solution)/shard_map/chunk/pallas_call | solution.py:261
  155.7 7.0 %collective-permute-done.28.refs_3_ = bf16[1024,512]{1,0:T(8,128)(2,1)S(1)} collective-permute-done((bf16[1024,512]{1,0:T(8,128)(2,1)S(1)}, bf16[1024,512]{1,0:T(8,128)(2,1)S(1)}, u32[]{:S(2)}, u32[]{:S(2)}) %collective-permute-start.28) | collective-permute-done | bytes 1048608 | tf_op jit(solution)/shard_map/ppermute | solution.py:354
  162.7 6.2 %chunk.7 = (f32[6,64,1024]{2,1,0:T(8,128)S(1)}, f32[6,64,1024]{2,1,0:T(8,128)S(1)}, bf16[6,64,1024]{2,1,0:T(8,128)(2,1)S(1)}, bf16[6,64,1024]{2,1,0:T(8,128)(2,1)S(1)}) custom-call(s32[24]{0:T(128)S(1)} %pad_add_fusion.3.sorted_ref, s32[2]{0:T(128)S(1)} %pad_add_fusion.4.place_ref, s32[24]{0:T(128)S(1)} %pad_add_fusion.5.perm_ref, ...), custom_call_target="tpu_custom_call" | custom-call | tf_op jit(solution)/shard_map/chunk/pallas_call | solution.py:261
  169.5 6.5 %collective-permute-done.32.across_back_ref = bf16[6,64,1024]{2,1,0:T(8,128)(2,1)S(1)} collective-permute-done((bf16[6,64,1024]{2,1,0:T(8,128)(2,1)S(1)}, bf16[6,64,1024]{2,1,0:T(8,128)(2,1)S(1)}, u32[]{:S(2)}, u32[]{:S(2)}) %collective-permute-start.32) | collective-permute-done | bytes 786464 | tf_op jit(solution)/shard_map/ppermute | solution.py:357
  176.0 2.8 %finish.1 = (bf16[6,64,1024]{2,1,0:T(8,128)(2,1)}, bf16[6,64,1024]{2,1,0:T(8,128)(2,1)}, f32[6,64]{1,0:T(8,128)}) custom-call(s32[6]{0:T(128)S(1)} %bitcast.71, bf16[6,64,1024]{2,1,0:T(8,128)(2,1)S(1)} %copy-done, bf16[6,64,1024]{2,1,0:T(8,128)(2,1)S(1)} %copy-done.1, f32[2,1024]{1,0:T(2,128)S(1)} %copy-done.2, ...), custom_call_target="tpu_custom_call" | custom-call | tf_op jit(solution)/shard_map/finish/pallas_call | solution.py:310
  (114 shorter events, 27.3 us)
Async XLA Ops:
  2.8 64.4 %collective-permute-start.6 = (bf16[6,64,1024]{2,1,0:T(8,128)(2,1)}, bf16[6,64,1024]{2,1,0:T(8,128)(2,1)S(1)}, u32[]{:S(2)}, u32[]{:S(2)}) collective-permute-start(bf16[6,64,1024]{2,1,0:T(8,128)(2,1)} %g_ref.1), channel_id=1, source_target_pairs={{0,16},{16,0},{1,17},{17,1},{2,18},{18,2},{3,19},{19,3},{4,20},{20... | collective-permute-start | bytes 2359304 | tf_op jit(solution)/shard_map/ppermute | solution.py:357
  7.0 17.7 %collective-permute-start.2 = (bf16[256,256]{1,0:T(8,128)(2,1)S(1)}, bf16[256,256]{1,0:T(8,128)(2,1)S(1)}, u32[]{:S(2)}, u32[]{:S(2)}) collective-permute-start(bf16[256,256]{1,0:T(8,128)(2,1)S(1)} %bitcast.88), channel_id=1, source_target_pairs={{0,12},{1,13},{2,14},{3,15},{4,0},{5,1},{6,2},{7,3},{8,4},{9,5},{1... | collective-permute-start | bytes 393224 | tf_op jit(solution)/shard_map/ppermute | solution.py:360
  10.7 13.2 %collective-permute-start.4 = (bf16[256,256]{1,0:T(8,128)(2,1)S(1)}, bf16[256,256]{1,0:T(8,128)(2,1)S(1)}, u32[]{:S(2)}, u32[]{:S(2)}) collective-permute-start(bf16[256,256]{1,0:T(8,128)(2,1)S(1)} %bitcast.89), channel_id=1, source_target_pairs={{0,4},{1,5},{2,6},{3,7},{4,8},{5,9},{6,10},{7,11},{8,12},{9,13},{1... | collective-permute-start | bytes 393224 | tf_op jit(solution)/shard_map/ppermute | solution.py:360
  10.7 16.6 %collective-permute-start.8 = (bf16[256,256]{1,0:T(8,128)(2,1)S(1)}, bf16[256,256]{1,0:T(8,128)(2,1)S(1)}, u32[]{:S(2)}, u32[]{:S(2)}) collective-permute-start(bf16[256,256]{1,0:T(8,128)(2,1)S(1)} %bitcast.90), channel_id=1, source_target_pairs={{0,8},{1,9},{2,10},{3,11},{4,12},{5,13},{6,14},{7,15},{8,0},{9,1},... | collective-permute-start | bytes 393224 | tf_op jit(solution)/shard_map/ppermute | solution.py:360
  11.7 12.1 %collective-permute-start.1 = (s32[6]{0:T(128)}, s32[6]{0:T(128)S(1)}, u32[]{:S(2)}, u32[]{:S(2)}) collective-permute-start(s32[6]{0:T(128)} %bitcast.68), channel_id=1, source_target_pairs={{0,16},{16,0},{1,17},{17,1},{2,18},{18,2},{3,19},{19,3},{4,20},{20... | collective-permute-start | bytes 80 | tf_op jit(solution)/shard_map/ppermute | solution.py:357
  27.4 23.5 %collective-permute-start.12 = (bf16[1792,256]{1,0:T(8,128)(2,1)S(1)}, bf16[1792,256]{1,0:T(8,128)(2,1)S(1)}, u32[]{:S(2)}, u32[]{:S(2)}) collective-permute-start(bf16[1792,256]{1,0:T(8,128)(2,1)S(1)} %constant_dynamic-update-slice_fusion.refs_2_), channel_id=1, source_target_pairs={{0,2},{1,3},{2,0},{3,1},{4,6},{5,7},{6,4},{7,5},{8,10},{9,11},{10,... | collective-permute-start | bytes 2752520 | tf_op jit(solution)/shard_map/ppermute | solution.py:354
  31.1 19.7 %collective-permute-start.10 = (bf16[256,512]{1,0:T(8,128)(2,1)S(1)}, bf16[256,512]{1,0:T(8,128)(2,1)S(1)}, u32[]{:S(2)}, u32[]{:S(2)}) collective-permute-start(bf16[256,512]{1,0:T(8,128)(2,1)S(1)} %get-tuple-element.39), channel_id=1, source_target_pairs={{0,8},{1,9},{2,10},{3,11},{4,12},{5,13},{6,14},{7,15},{8,0},{9,1},... | collective-permute-start | bytes 786440 | tf_op jit(solution)/shard_map/ppermute | solution.py:360
  33.7 17.1 %collective-permute-start.11 = (bf16[256,512]{1,0:T(8,128)(2,1)S(1)}, bf16[256,512]{1,0:T(8,128)(2,1)S(1)}, u32[]{:S(2)}, u32[]{:S(2)}) collective-permute-start(bf16[256,512]{1,0:T(8,128)(2,1)S(1)} %get-tuple-element.39), channel_id=1, source_target_pairs={{0,12},{1,13},{2,14},{3,15},{4,0},{5,1},{6,2},{7,3},{8,4},{9,5},{1... | collective-permute-start | bytes 786440 | tf_op jit(solution)/shard_map/ppermute | solution.py:360
  40.4 17.8 %collective-permute-start.5 = (bf16[6,64,1024]{2,1,0:T(8,128)(2,1)S(1)}, bf16[6,64,1024]{2,1,0:T(8,128)(2,1)S(1)}, u32[]{:S(2)}, u32[]{:S(2)}) collective-permute-start(bf16[6,64,1024]{2,1,0:T(8,128)(2,1)S(1)} %fusion.2), channel_id=1, source_target_pairs={{0,16},{16,0},{1,17},{17,1},{2,18},{18,2},{3,19},{19,3},{4,20},{20... | collective-permute-start | bytes 2359304 | tf_op jit(solution)/shard_map/ppermute | solution.py:357
  50.9 26.1 %collective-permute-start.16 = (bf16[896,512]{1,0:T(8,128)(2,1)S(1)}, bf16[896,512]{1,0:T(8,128)(2,1)S(1)}, u32[]{:S(2)}, u32[]{:S(2)}) collective-permute-start(bf16[896,512]{1,0:T(8,128)(2,1)S(1)} %pad_maximum_fusion.5.refs_3_), channel_id=1, source_target_pairs={{0,2},{1,3},{2,0},{3,1},{4,6},{5,7},{6,4},{7,5},{8,10},{9,11},{10,... | collective-permute-start | bytes 2752520 | tf_op jit(solution)/shard_map/ppermute | solution.py:354
  62.4 14.6 %collective-permute-start.14 = (bf16[256,512]{1,0:T(8,128)(2,1)S(1)}, bf16[256,512]{1,0:T(8,128)(2,1)S(1)}, u32[]{:S(2)}, u32[]{:S(2)}) collective-permute-start(bf16[256,512]{1,0:T(8,128)(2,1)S(1)} %pad_maximum_fusion.10), channel_id=1, source_target_pairs={{0,8},{1,9},{2,10},{3,11},{4,12},{5,13},{6,14},{7,15},{8,0},{9,1},... | collective-permute-start | bytes 786440 | tf_op jit(solution)/shard_map/ppermute | solution.py:360
  64.3 12.7 %collective-permute-start.15 = (bf16[256,512]{1,0:T(8,128)(2,1)S(1)}, bf16[256,512]{1,0:T(8,128)(2,1)S(1)}, u32[]{:S(2)}, u32[]{:S(2)}) collective-permute-start(bf16[256,512]{1,0:T(8,128)(2,1)S(1)} %pad_maximum_fusion.10), channel_id=1, source_target_pairs={{0,12},{1,13},{2,14},{3,15},{4,0},{5,1},{6,2},{7,3},{8,4},{9,5},{1... | collective-permute-start | bytes 786440 | tf_op jit(solution)/shard_map/ppermute | solution.py:360
  77.0 33.2 %collective-permute-start.17 = (bf16[2,2,6,64,1024]{4,3,2,1,0:T(8,128)(2,1)S(1)}, bf16[2,2,6,64,1024]{4,3,2,1,0:T(8,128)(2,1)S(1)}, u32[]{:S(2)}, u32[]{:S(2)}) collective-permute-start(bf16[2,2,6,64,1024]{4,3,2,1,0:T(8,128)(2,1)S(1)} %pad_maximum_fusion), channel_id=1, source_target_pairs={{0,1},{1,0},{2,3},{3,2},{4,5},{5,4},{6,7},{7,6},{8,9},{9,8},{10,11... | collective-permute-start | bytes 9437192 | tf_op jit(solution)/shard_map/ppermute | solution.py:351
  77.1 32.2 %collective-permute-start.21 = (bf16[896,512]{1,0:T(8,128)(2,1)S(1)}, bf16[896,512]{1,0:T(8,128)(2,1)S(1)}, u32[]{:S(2)}, u32[]{:S(2)}) collective-permute-start(bf16[896,512]{1,0:T(8,128)(2,1)S(1)} %pad_maximum_fusion.6.refs_4_.refs_2_), channel_id=1, source_target_pairs={{0,2},{1,3},{2,0},{3,1},{4,6},{5,7},{6,4},{7,5},{8,10},{9,11},{10,... | collective-permute-start | bytes 2752520 | tf_op jit(solution)/shard_map/ppermute | solution.py:354
  78.4 13.1 %collective-permute-start.20 = (bf16[256,512]{1,0:T(8,128)(2,1)S(1)}, bf16[256,512]{1,0:T(8,128)(2,1)S(1)}, u32[]{:S(2)}, u32[]{:S(2)}) collective-permute-start(bf16[256,512]{1,0:T(8,128)(2,1)S(1)} %get-tuple-element.43), channel_id=1, source_target_pairs={{0,12},{1,13},{2,14},{3,15},{4,0},{5,1},{6,2},{7,3},{8,4},{9,5},{1... | collective-permute-start | bytes 786440 | tf_op jit(solution)/shard_map/ppermute | solution.py:360
  84.8 24.4 %collective-permute-start.19 = (bf16[256,512]{1,0:T(8,128)(2,1)S(1)}, bf16[256,512]{1,0:T(8,128)(2,1)S(1)}, u32[]{:S(2)}, u32[]{:S(2)}) collective-permute-start(bf16[256,512]{1,0:T(8,128)(2,1)S(1)} %get-tuple-element.43), channel_id=1, source_target_pairs={{0,8},{1,9},{2,10},{3,11},{4,12},{5,13},{6,14},{7,15},{8,0},{9,1},... | collective-permute-start | bytes 786440 | tf_op jit(solution)/shard_map/ppermute | solution.py:360
  86.0 23.3 %collective-permute-start.18 = (bf16[256,512]{1,0:T(8,128)(2,1)S(1)}, bf16[256,512]{1,0:T(8,128)(2,1)S(1)}, u32[]{:S(2)}, u32[]{:S(2)}) collective-permute-start(bf16[256,512]{1,0:T(8,128)(2,1)S(1)} %get-tuple-element.43), channel_id=1, source_target_pairs={{0,4},{1,5},{2,6},{3,7},{4,8},{5,9},{6,10},{7,11},{8,12},{9,13},{1... | collective-permute-start | bytes 786440 | tf_op jit(solution)/shard_map/ppermute | solution.py:360
  109.3 21.7 %collective-permute-start.22 = (bf16[896,512]{1,0:T(8,128)(2,1)S(1)}, bf16[896,512]{1,0:T(8,128)(2,1)S(1)}, u32[]{:S(2)}, u32[]{:S(2)}) collective-permute-start(bf16[896,512]{1,0:T(8,128)(2,1)S(1)} %pad_maximum_fusion.7.refs_3_.refs_5_), channel_id=1, source_target_pairs={{0,2},{1,3},{2,0},{3,1},{4,6},{5,7},{6,4},{7,5},{8,10},{9,11},{10,... | collective-permute-start | bytes 2752520 | tf_op jit(solution)/shard_map/ppermute | solution.py:354
  110.2 14.4 %collective-permute-start.23 = (bf16[256,512]{1,0:T(8,128)(2,1)S(1)}, bf16[256,512]{1,0:T(8,128)(2,1)S(1)}, u32[]{:S(2)}, u32[]{:S(2)}) collective-permute-start(bf16[256,512]{1,0:T(8,128)(2,1)S(1)} %pad_maximum_fusion.11), channel_id=1, source_target_pairs={{0,4},{1,5},{2,6},{3,7},{4,8},{5,9},{6,10},{7,11},{8,12},{9,13},{1... | collective-permute-start | bytes 786440 | tf_op jit(solution)/shard_map/ppermute | solution.py:360
  110.3 27.2 %collective-permute-start.27 = (bf16[256,512]{1,0:T(8,128)(2,1)S(1)}, bf16[256,512]{1,0:T(8,128)(2,1)S(1)}, u32[]{:S(2)}, u32[]{:S(2)}) collective-permute-start(bf16[256,512]{1,0:T(8,128)(2,1)S(1)} %pad_maximum_fusion.11), channel_id=1, source_target_pairs={{0,12},{1,13},{2,14},{3,15},{4,0},{5,1},{6,2},{7,3},{8,4},{9,5},{1... | collective-permute-start | bytes 786440 | tf_op jit(solution)/shard_map/ppermute | solution.py:360
  114.1 23.4 %collective-permute-start.26 = (bf16[256,512]{1,0:T(8,128)(2,1)S(1)}, bf16[256,512]{1,0:T(8,128)(2,1)S(1)}, u32[]{:S(2)}, u32[]{:S(2)}) collective-permute-start(bf16[256,512]{1,0:T(8,128)(2,1)S(1)} %pad_maximum_fusion.11), channel_id=1, source_target_pairs={{0,8},{1,9},{2,10},{3,11},{4,12},{5,13},{6,14},{7,15},{8,0},{9,1},... | collective-permute-start | bytes 786440 | tf_op jit(solution)/shard_map/ppermute | solution.py:360
  137.5 25.2 %collective-permute-start.28 = (bf16[1024,512]{1,0:T(8,128)(2,1)S(1)}, bf16[1024,512]{1,0:T(8,128)(2,1)S(1)}, u32[]{:S(2)}, u32[]{:S(2)}) collective-permute-start(bf16[1024,512]{1,0:T(8,128)(2,1)S(1)} %pad_maximum_fusion.4.refs_2_), channel_id=1, source_target_pairs={{0,2},{1,3},{2,0},{3,1},{4,6},{5,7},{6,4},{7,5},{8,10},{9,11},{10,... | collective-permute-start | bytes 3145736 | tf_op jit(solution)/shard_map/ppermute | solution.py:354
  139.5 30.0 %collective-permute-start.31 = (bf16[6,64,1024]{2,1,0:T(8,128)(2,1)S(1)}, bf16[6,64,1024]{2,1,0:T(8,128)(2,1)S(1)}, u32[]{:S(2)}, u32[]{:S(2)}) collective-permute-start(bf16[6,64,1024]{2,1,0:T(8,128)(2,1)S(1)} %add_convert_fusion.1), channel_id=1, source_target_pairs={{0,16},{16,0},{1,17},{17,1},{2,18},{18,2},{3,19},{19,3},{4,20},{20... | collective-permute-start | bytes 2359304 | tf_op jit(solution)/shard_map/ppermute | solution.py:357
  140.7 35.4 %collective-permute-start.32 = (bf16[6,64,1024]{2,1,0:T(8,128)(2,1)S(1)}, bf16[6,64,1024]{2,1,0:T(8,128)(2,1)S(1)}, u32[]{:S(2)}, u32[]{:S(2)}) collective-permute-start(bf16[6,64,1024]{2,1,0:T(8,128)(2,1)S(1)} %add_convert_fusion), channel_id=1, source_target_pairs={{0,16},{16,0},{1,17},{17,1},{2,18},{18,2},{3,19},{19,3},{4,20},{20... | collective-permute-start | bytes 2359304 | tf_op jit(solution)/shard_map/ppermute | solution.py:357
  (15 other events, 99.9 us)

commit v20 on v18

--- a/solution.py
+++ b/solution.py
@@ -498,7 +498,7 @@
         (near, after(over, *shifted[3]), far), weights_of(0, 1, 2), None,
     )
     across_y(4)
-    sums = (after(sums[0], *shifted[4]), sums[1])
+    sums = (after(sums[0], shifted[4][0]), sums[1])
     *same, other_out, other_back = chunk(
         (False, True), over_blocks, (1,), scalars, tokens_of, weights_of(3), sums,
         (BF16, BF16), 0,

time: 174 us -> 171 us (0.983); the launches traced: 173 us -> 168 us
  waiting for transfers between devices: 86.6 us -> 83.6 us
  starting transfers between devices: 37.7 us -> 35.9 us
    ppermute x15, waiting for transfers between devices: 57.3 us -> 52.6 us  [shift_z(): lax.ppermute(a, 'row', [(i, (i + 4 * d) % ranks) for i in range(ranks)])]
    ppermute x5, waiting for transfers between devices: 5.48 us -> 7.57 us  [over_y(): return lax.ppermute(a, 'row', [(i, i ^ 2) for i in range(ranks)])]
  transfers between devices with their start and end apart: 33 -> 33, of which waited for: 16 -> 15; matrix products, arithmetic and copies ran while one was open for 4% -> 4% of each run, Pallas kernels for 18% -> 21%
where the time goes in v20:
time: 171 us; the launch traced here: 168 us
  waiting for transfers between devices  83.6 us (49%)
  Pallas kernels  39 us (23%)
  starting transfers between devices  35.9 us (21%)
  other arithmetic  5.76 us (3%)
  local copies, waits for them, and re-layouts  2.83 us (2%)
    ppermute x15, waiting for transfers between devices, shift_z(): lax.ppermute(a, 'row', [(i, (i + 4 * d) % ranks) for i in range(ranks)])  52.6 us
    pallas_call x4, Pallas kernels, chunk(): pl.pallas_call(functools.partial(chunk_kernel, offset, kind, units, chips...  36.2 us
    ppermute x15, starting transfers between devices, shift_z(): lax.ppermute(a, 'row', [(i, (i + 4 * d) % ranks) for i in range(ranks)])  23.2 us
    ppermute x5, waiting for transfers between devices, over_x(): return lax.ppermute(a, 'grp', [(0, 1), (1, 0)])  22.8 us
    ppermute x5, waiting for transfers between devices, over_y(): return lax.ppermute(a, 'row', [(i, i ^ 2) for i in range(ranks)])  7.57 us
    ppermute x5, starting transfers between devices, over_x(): return lax.ppermute(a, 'grp', [(0, 1), (1, 0)])  6.07 us
    ppermute x5, starting transfers between devices, over_y(): return lax.ppermute(a, 'row', [(i, i ^ 2) for i in range(ranks)])  5.35 us
  transfers between devices with their start and end apart: 33, of which 15 were waited for; matrix products, arithmetic and copies ran while one was open for 4% of the time, Pallas kernels for 21%

profile of v20, /device:TPU:8, one launch (start us, length us, event | category | flops | bytes accessed | tf_op | source)
XLA Modules:
  0.0 168.4 jit_solution(14768035707503460969)
XLA Ops:
  4.1 2.0 %collective-permute-start.4 = (bf16[256,256]{1,0:T(8,128)(2,1)S(1)}, bf16[256,256]{1,0:T(8,128)(2,1)S(1)}, u32[]{:S(2)}, u32[]{:S(2)}) collective-permute-start(bf16[256,256]{1,0:T(8,128)(2,1)S(1)} %bitcast.89), channel_id=1, source_target_pairs={{0,4},{1,5},{2,6},{3,7},{4,8},{5,9},{6,10},{7,11},{8,12},{9,13},{1... | collective-permute-start | bytes 393224 | tf_op jit(solution)/shard_map/ppermute | solution.py:360
  6.2 4.5 %collective-permute-start.7 = (bf16[256,256]{1,0:T(8,128)(2,1)S(1)}, bf16[256,256]{1,0:T(8,128)(2,1)S(1)}, u32[]{:S(2)}, u32[]{:S(2)}) collective-permute-start(bf16[256,256]{1,0:T(8,128)(2,1)S(1)} %bitcast.91), channel_id=1, source_target_pairs={{0,8},{1,9},{2,10},{3,11},{4,12},{5,13},{6,14},{7,15},{8,0},{9,1},... | collective-permute-start | bytes 393224 | tf_op jit(solution)/shard_map/ppermute | solution.py:360
  21.1 3.5 %collective-permute-start.10 = (bf16[256,512]{1,0:T(8,128)(2,1)S(1)}, bf16[256,512]{1,0:T(8,128)(2,1)S(1)}, u32[]{:S(2)}, u32[]{:S(2)}) collective-permute-start(bf16[256,512]{1,0:T(8,128)(2,1)S(1)} %get-tuple-element.40), channel_id=1, source_target_pairs={{0,8},{1,9},{2,10},{3,11},{4,12},{5,13},{6,14},{7,15},{8,0},{9,1},... | collective-permute-start | bytes 786440 | tf_op jit(solution)/shard_map/ppermute | solution.py:360
  25.2 4.9 %collective-permute-done.9 = bf16[256,512]{1,0:T(8,128)(2,1)S(1)} collective-permute-done((bf16[256,512]{1,0:T(8,128)(2,1)S(1)}, bf16[256,512]{1,0:T(8,128)(2,1)S(1)}, u32[]{:S(2)}, u32[]{:S(2)}) %collective-permute-start.9) | collective-permute-done | bytes 262176 | tf_op jit(solution)/shard_map/ppermute | solution.py:360
  30.1 13.6 %collective-permute-done.10 = bf16[256,512]{1,0:T(8,128)(2,1)S(1)} collective-permute-done((bf16[256,512]{1,0:T(8,128)(2,1)S(1)}, bf16[256,512]{1,0:T(8,128)(2,1)S(1)}, u32[]{:S(2)}, u32[]{:S(2)}) %collective-permute-start.10) | collective-permute-done | bytes 262176 | tf_op jit(solution)/shard_map/ppermute | solution.py:360
  43.7 3.4 %collective-permute-done.11 = bf16[256,512]{1,0:T(8,128)(2,1)S(1)} collective-permute-done((bf16[256,512]{1,0:T(8,128)(2,1)S(1)}, bf16[256,512]{1,0:T(8,128)(2,1)S(1)}, u32[]{:S(2)}, u32[]{:S(2)}) %collective-permute-start.11) | collective-permute-done | bytes 262176 | tf_op jit(solution)/shard_map/ppermute | solution.py:360
  48.9 1.9 %collective-permute-start.15 = (bf16[256,512]{1,0:T(8,128)(2,1)S(1)}, bf16[256,512]{1,0:T(8,128)(2,1)S(1)}, u32[]{:S(2)}, u32[]{:S(2)}) collective-permute-start(bf16[256,512]{1,0:T(8,128)(2,1)S(1)} %pad_maximum_fusion.10), channel_id=1, source_target_pairs={{0,12},{1,13},{2,14},{3,15},{4,0},{5,1},{6,2},{7,3},{8,4},{9,5},{1... | collective-permute-start | bytes 786440 | tf_op jit(solution)/shard_map/ppermute | solution.py:360
  50.8 15.5 %collective-permute-done.12 = bf16[6,64,1024]{2,1,0:T(8,128)(2,1)S(1)} collective-permute-done((bf16[6,64,1024]{2,1,0:T(8,128)(2,1)S(1)}, bf16[6,64,1024]{2,1,0:T(8,128)(2,1)S(1)}, u32[]{:S(2)}, u32[]{:S(2)}) %collective-permute-start.12) | collective-permute-done | bytes 786464 | tf_op jit(solution)/shard_map/ppermute | solution.py:357
  66.8 4.0 %collective-permute-done.14 = bf16[256,512]{1,0:T(8,128)(2,1)S(1)} collective-permute-done((bf16[256,512]{1,0:T(8,128)(2,1)S(1)}, bf16[256,512]{1,0:T(8,128)(2,1)S(1)}, u32[]{:S(2)}, u32[]{:S(2)}) %collective-permute-start.14) | collective-permute-done | bytes 262176 | tf_op jit(solution)/shard_map/ppermute | solution.py:360
  72.5 3.4 %collective-permute-start.19 = (bf16[256,512]{1,0:T(8,128)(2,1)S(1)}, bf16[256,512]{1,0:T(8,128)(2,1)S(1)}, u32[]{:S(2)}, u32[]{:S(2)}) collective-permute-start(bf16[256,512]{1,0:T(8,128)(2,1)S(1)} %get-tuple-element.45), channel_id=1, source_target_pairs={{0,8},{1,9},{2,10},{3,11},{4,12},{5,13},{6,14},{7,15},{8,0},{9,1},... | collective-permute-start | bytes 786440 | tf_op jit(solution)/shard_map/ppermute | solution.py:360
  75.9 2.9 %collective-permute-start.18 = (bf16[256,512]{1,0:T(8,128)(2,1)S(1)}, bf16[256,512]{1,0:T(8,128)(2,1)S(1)}, u32[]{:S(2)}, u32[]{:S(2)}) collective-permute-start(bf16[256,512]{1,0:T(8,128)(2,1)S(1)} %get-tuple-element.45), channel_id=1, source_target_pairs={{0,4},{1,5},{2,6},{3,7},{4,8},{5,9},{6,10},{7,11},{8,12},{9,13},{1... | collective-permute-start | bytes 786440 | tf_op jit(solution)/shard_map/ppermute | solution.py:360
  78.8 2.8 %collective-permute-done.20 = bf16[256,512]{1,0:T(8,128)(2,1)S(1)} collective-permute-done((bf16[256,512]{1,0:T(8,128)(2,1)S(1)}, bf16[256,512]{1,0:T(8,128)(2,1)S(1)}, u32[]{:S(2)}, u32[]{:S(2)}) %collective-permute-start.20) | collective-permute-done | bytes 262176 | tf_op jit(solution)/shard_map/ppermute | solution.py:360
  81.6 12.2 %collective-permute-done.19 = bf16[256,512]{1,0:T(8,128)(2,1)S(1)} collective-permute-done((bf16[256,512]{1,0:T(8,128)(2,1)S(1)}, bf16[256,512]{1,0:T(8,128)(2,1)S(1)}, u32[]{:S(2)}, u32[]{:S(2)}) %collective-permute-start.19) | collective-permute-done | bytes 262176 | tf_op jit(solution)/shard_map/ppermute | solution.py:360
  93.8 4.9 %collective-permute-done.18 = bf16[256,512]{1,0:T(8,128)(2,1)S(1)} collective-permute-done((bf16[256,512]{1,0:T(8,128)(2,1)S(1)}, bf16[256,512]{1,0:T(8,128)(2,1)S(1)}, u32[]{:S(2)}, u32[]{:S(2)}) %collective-permute-start.18) | collective-permute-done | bytes 262176 | tf_op jit(solution)/shard_map/ppermute | solution.py:360
  99.4 2.5 %collective-permute-start.23 = (bf16[256,512]{1,0:T(8,128)(2,1)S(1)}, bf16[256,512]{1,0:T(8,128)(2,1)S(1)}, u32[]{:S(2)}, u32[]{:S(2)}) collective-permute-start(bf16[256,512]{1,0:T(8,128)(2,1)S(1)} %pad_maximum_fusion.11), channel_id=1, source_target_pairs={{0,4},{1,5},{2,6},{3,7},{4,8},{5,9},{6,10},{7,11},{8,12},{9,13},{1... | collective-permute-start | bytes 786440 | tf_op jit(solution)/shard_map/ppermute | solution.py:360
  102.0 1.7 %collective-permute-start.26 = (bf16[256,512]{1,0:T(8,128)(2,1)S(1)}, bf16[256,512]{1,0:T(8,128)(2,1)S(1)}, u32[]{:S(2)}, u32[]{:S(2)}) collective-permute-start(bf16[256,512]{1,0:T(8,128)(2,1)S(1)} %pad_maximum_fusion.11), channel_id=1, source_target_pairs={{0,8},{1,9},{2,10},{3,11},{4,12},{5,13},{6,14},{7,15},{8,0},{9,1},... | collective-permute-start | bytes 786440 | tf_op jit(solution)/shard_map/ppermute | solution.py:360
  103.7 10.5 %chunk.4 = (f32[768,1024]{1,0:T(8,128)S(1)}, f32[768,1024]{1,0:T(8,128)S(1)}) custom-call(s32[24]{0:T(128)S(1)} %pad_add_fusion.3.sorted_ref, s32[2]{0:T(128)S(1)} %pad_add_fusion.4.place_ref, s32[24]{0:T(128)S(1)} %pad_add_fusion.5.perm_ref, bf16[2,6,64,1024]{3,2,1,0:T(8,128)(2,1)S(1)} %get-tuple-element.48.refs_0_, ...), custom_call_target="tpu_custom_call" | custom-call | flops 5368709120 | bytes 20971520 | tf_op jit(solution)/shard_map/chunk/pallas_call | solution.py:261
  114.2 5.8 %collective-permute-done.23 = bf16[256,512]{1,0:T(8,128)(2,1)S(1)} collective-permute-done((bf16[256,512]{1,0:T(8,128)(2,1)S(1)}, bf16[256,512]{1,0:T(8,128)(2,1)S(1)}, u32[]{:S(2)}, u32[]{:S(2)}) %collective-permute-start.23) | collective-permute-done | bytes 262176 | tf_op jit(solution)/shard_map/ppermute | solution.py:360
  120.5 5.8 %chunk.5 = (bf16[6,64,1024]{2,1,0:T(8,128)(2,1)S(1)}, bf16[6,64,1024]{2,1,0:T(8,128)(2,1)S(1)}, bf16[6,64,1024]{2,1,0:T(8,128)(2,1)S(1)}, bf16[6,64,1024]{2,1,0:T(8,128)(2,1)S(1)}) custom-call(s32[24]{0:T(128)S(1)} %pad_add_fusion.3.sorted_ref, s32[2]{0:T(128)S(1)} %pad_add_fusion.4.place_ref, s32[24]{0:T(128)S(1)} %pad_add_fusion.5.perm_ref, ...), custom_call_target="tpu_custom_call" | custom-call | tf_op jit(solution)/shard_map/chunk/pallas_call | solution.py:261
  131.5 13.7 %chunk.6 = (f32[768,1024]{1,0:T(8,128)S(1)}, f32[768,1024]{1,0:T(8,128)S(1)}) custom-call(s32[24]{0:T(128)S(1)} %pad_add_fusion.3.sorted_ref, s32[2]{0:T(128)S(1)} %pad_add_fusion.4.place_ref, s32[24]{0:T(128)S(1)} %pad_add_fusion.5.perm_ref, bf16[2,6,64,1024]{3,2,1,0:T(8,128)(2,1)S(1)} %get-tuple-element.57.refs_0_, ...), custom_call_target="tpu_custom_call" | custom-call | tf_op jit(solution)/shard_map/chunk/pallas_call | solution.py:261
  145.2 7.0 %collective-permute-done.28.refs_3_ = bf16[1024,512]{1,0:T(8,128)(2,1)S(1)} collective-permute-done((bf16[1024,512]{1,0:T(8,128)(2,1)S(1)}, bf16[1024,512]{1,0:T(8,128)(2,1)S(1)}, u32[]{:S(2)}, u32[]{:S(2)}) %collective-permute-start.28) | collective-permute-done | bytes 1048608 | tf_op jit(solution)/shard_map/ppermute | solution.py:354
  152.2 6.2 %chunk.7 = (f32[6,64,1024]{2,1,0:T(8,128)S(1)}, f32[6,64,1024]{2,1,0:T(8,128)S(1)}, bf16[6,64,1024]{2,1,0:T(8,128)(2,1)S(1)}, bf16[6,64,1024]{2,1,0:T(8,128)(2,1)S(1)}) custom-call(s32[24]{0:T(128)S(1)} %pad_add_fusion.3.sorted_ref, s32[2]{0:T(128)S(1)} %pad_add_fusion.4.place_ref, s32[24]{0:T(128)S(1)} %pad_add_fusion.5.perm_ref, ...), custom_call_target="tpu_custom_call" | custom-call | tf_op jit(solution)/shard_map/chunk/pallas_call | solution.py:261
  159.0 6.5 %collective-permute-done.32.across_back_ref = bf16[6,64,1024]{2,1,0:T(8,128)(2,1)S(1)} collective-permute-done((bf16[6,64,1024]{2,1,0:T(8,128)(2,1)S(1)}, bf16[6,64,1024]{2,1,0:T(8,128)(2,1)S(1)}, u32[]{:S(2)}, u32[]{:S(2)}) %collective-permute-start.32) | collective-permute-done | bytes 786464 | tf_op jit(solution)/shard_map/ppermute | solution.py:357
  165.5 2.8 %finish.1 = (bf16[6,64,1024]{2,1,0:T(8,128)(2,1)}, bf16[6,64,1024]{2,1,0:T(8,128)(2,1)}, f32[6,64]{1,0:T(8,128)}) custom-call(s32[6]{0:T(128)S(1)} %bitcast.71, bf16[6,64,1024]{2,1,0:T(8,128)(2,1)S(1)} %copy-done, bf16[6,64,1024]{2,1,0:T(8,128)(2,1)S(1)} %copy-done.1, f32[2,1024]{1,0:T(2,128)S(1)} %copy-done.2, ...), custom_call_target="tpu_custom_call" | custom-call | tf_op jit(solution)/shard_map/finish/pallas_call | solution.py:310
  (114 shorter events, 25.1 us)
Async XLA Ops:
  4.1 12.0 %collective-permute-start.2 = (bf16[256,256]{1,0:T(8,128)(2,1)S(1)}, bf16[256,256]{1,0:T(8,128)(2,1)S(1)}, u32[]{:S(2)}, u32[]{:S(2)}) collective-permute-start(bf16[256,256]{1,0:T(8,128)(2,1)S(1)} %bitcast.88), channel_id=1, source_target_pairs={{0,12},{1,13},{2,14},{3,15},{4,0},{5,1},{6,2},{7,3},{8,4},{9,5},{1... | collective-permute-start | bytes 393224 | tf_op jit(solution)/shard_map/ppermute | solution.py:360
  4.1 11.2 %collective-permute-start.4 = (bf16[256,256]{1,0:T(8,128)(2,1)S(1)}, bf16[256,256]{1,0:T(8,128)(2,1)S(1)}, u32[]{:S(2)}, u32[]{:S(2)}) collective-permute-start(bf16[256,256]{1,0:T(8,128)(2,1)S(1)} %bitcast.89), channel_id=1, source_target_pairs={{0,4},{1,5},{2,6},{3,7},{4,8},{5,9},{6,10},{7,11},{8,12},{9,13},{1... | collective-permute-start | bytes 393224 | tf_op jit(solution)/shard_map/ppermute | solution.py:360
  6.2 12.9 %collective-permute-start.7 = (bf16[256,256]{1,0:T(8,128)(2,1)S(1)}, bf16[256,256]{1,0:T(8,128)(2,1)S(1)}, u32[]{:S(2)}, u32[]{:S(2)}) collective-permute-start(bf16[256,256]{1,0:T(8,128)(2,1)S(1)} %bitcast.91), channel_id=1, source_target_pairs={{0,8},{1,9},{2,10},{3,11},{4,12},{5,13},{6,14},{7,15},{8,0},{9,1},... | collective-permute-start | bytes 393224 | tf_op jit(solution)/shard_map/ppermute | solution.py:360
  16.2 32.5 %collective-permute-start.5 = (bf16[6,64,1024]{2,1,0:T(8,128)(2,1)S(1)}, bf16[6,64,1024]{2,1,0:T(8,128)(2,1)S(1)}, u32[]{:S(2)}, u32[]{:S(2)}) collective-permute-start(bf16[6,64,1024]{2,1,0:T(8,128)(2,1)S(1)} %fusion.2), channel_id=1, source_target_pairs={{0,16},{16,0},{1,17},{17,1},{2,18},{18,2},{3,19},{19,3},{4,20},{20... | collective-permute-start | bytes 2359304 | tf_op jit(solution)/shard_map/ppermute | solution.py:357
  19.1 28.0 %collective-permute-start.8 = (bf16[1792,256]{1,0:T(8,128)(2,1)S(1)}, bf16[1792,256]{1,0:T(8,128)(2,1)S(1)}, u32[]{:S(2)}, u32[]{:S(2)}) collective-permute-start(bf16[1792,256]{1,0:T(8,128)(2,1)S(1)} %constant_dynamic-update-slice_fusion.refs_2_), channel_id=1, source_target_pairs={{0,2},{1,3},{2,0},{3,1},{4,6},{5,7},{6,4},{7,5},{8,10},{9,11},{10,... | collective-permute-start | bytes 2752520 | tf_op jit(solution)/shard_map/ppermute | solution.py:354
  20.9 9.2 %collective-permute-start.9 = (bf16[256,512]{1,0:T(8,128)(2,1)S(1)}, bf16[256,512]{1,0:T(8,128)(2,1)S(1)}, u32[]{:S(2)}, u32[]{:S(2)}) collective-permute-start(bf16[256,512]{1,0:T(8,128)(2,1)S(1)} %get-tuple-element.40), channel_id=1, source_target_pairs={{0,4},{1,5},{2,6},{3,7},{4,8},{5,9},{6,10},{7,11},{8,12},{9,13},{1... | collective-permute-start | bytes 786440 | tf_op jit(solution)/shard_map/ppermute | solution.py:360
  21.1 22.6 %collective-permute-start.10 = (bf16[256,512]{1,0:T(8,128)(2,1)S(1)}, bf16[256,512]{1,0:T(8,128)(2,1)S(1)}, u32[]{:S(2)}, u32[]{:S(2)}) collective-permute-start(bf16[256,512]{1,0:T(8,128)(2,1)S(1)} %get-tuple-element.40), channel_id=1, source_target_pairs={{0,8},{1,9},{2,10},{3,11},{4,12},{5,13},{6,14},{7,15},{8,0},{9,1},... | collective-permute-start | bytes 786440 | tf_op jit(solution)/shard_map/ppermute | solution.py:360
  24.6 22.5 %collective-permute-start.11 = (bf16[256,512]{1,0:T(8,128)(2,1)S(1)}, bf16[256,512]{1,0:T(8,128)(2,1)S(1)}, u32[]{:S(2)}, u32[]{:S(2)}) collective-permute-start(bf16[256,512]{1,0:T(8,128)(2,1)S(1)} %get-tuple-element.40), channel_id=1, source_target_pairs={{0,12},{1,13},{2,14},{3,15},{4,0},{5,1},{6,2},{7,3},{8,4},{9,5},{1... | collective-permute-start | bytes 786440 | tf_op jit(solution)/shard_map/ppermute | solution.py:360
  47.1 19.2 %collective-permute-start.12 = (bf16[6,64,1024]{2,1,0:T(8,128)(2,1)S(1)}, bf16[6,64,1024]{2,1,0:T(8,128)(2,1)S(1)}, u32[]{:S(2)}, u32[]{:S(2)}) collective-permute-start(bf16[6,64,1024]{2,1,0:T(8,128)(2,1)S(1)} %copy-done.1), channel_id=1, source_target_pairs={{0,16},{16,0},{1,17},{17,1},{2,18},{18,2},{3,19},{19,3},{4,20},{20... | collective-permute-start | bytes 2359304 | tf_op jit(solution)/shard_map/ppermute | solution.py:357
  48.1 22.7 %collective-permute-start.16 = (bf16[896,512]{1,0:T(8,128)(2,1)S(1)}, bf16[896,512]{1,0:T(8,128)(2,1)S(1)}, u32[]{:S(2)}, u32[]{:S(2)}) collective-permute-start(bf16[896,512]{1,0:T(8,128)(2,1)S(1)} %pad_maximum_fusion.5.refs_3_), channel_id=1, source_target_pairs={{0,2},{1,3},{2,0},{3,1},{4,6},{5,7},{6,4},{7,5},{8,10},{9,11},{10,... | collective-permute-start | bytes 2752520 | tf_op jit(solution)/shard_map/ppermute | solution.py:354
  48.7 18.1 %collective-permute-start.13 = (bf16[256,512]{1,0:T(8,128)(2,1)S(1)}, bf16[256,512]{1,0:T(8,128)(2,1)S(1)}, u32[]{:S(2)}, u32[]{:S(2)}) collective-permute-start(bf16[256,512]{1,0:T(8,128)(2,1)S(1)} %pad_maximum_fusion.10), channel_id=1, source_target_pairs={{0,4},{1,5},{2,6},{3,7},{4,8},{5,9},{6,10},{7,11},{8,12},{9,13},{1... | collective-permute-start | bytes 786440 | tf_op jit(solution)/shard_map/ppermute | solution.py:360
  48.8 22.0 %collective-permute-start.14 = (bf16[256,512]{1,0:T(8,128)(2,1)S(1)}, bf16[256,512]{1,0:T(8,128)(2,1)S(1)}, u32[]{:S(2)}, u32[]{:S(2)}) collective-permute-start(bf16[256,512]{1,0:T(8,128)(2,1)S(1)} %pad_maximum_fusion.10), channel_id=1, source_target_pairs={{0,8},{1,9},{2,10},{3,11},{4,12},{5,13},{6,14},{7,15},{8,0},{9,1},... | collective-permute-start | bytes 786440 | tf_op jit(solution)/shard_map/ppermute | solution.py:360
  48.9 21.9 %collective-permute-start.15 = (bf16[256,512]{1,0:T(8,128)(2,1)S(1)}, bf16[256,512]{1,0:T(8,128)(2,1)S(1)}, u32[]{:S(2)}, u32[]{:S(2)}) collective-permute-start(bf16[256,512]{1,0:T(8,128)(2,1)S(1)} %pad_maximum_fusion.10), channel_id=1, source_target_pairs={{0,12},{1,13},{2,14},{3,15},{4,0},{5,1},{6,2},{7,3},{8,4},{9,5},{1... | collective-permute-start | bytes 786440 | tf_op jit(solution)/shard_map/ppermute | solution.py:360
  70.8 28.6 %collective-permute-start.17 = (bf16[2,2,6,64,1024]{4,3,2,1,0:T(8,128)(2,1)S(1)}, bf16[2,2,6,64,1024]{4,3,2,1,0:T(8,128)(2,1)S(1)}, u32[]{:S(2)}, u32[]{:S(2)}) collective-permute-start(bf16[2,2,6,64,1024]{4,3,2,1,0:T(8,128)(2,1)S(1)} %pad_maximum_fusion), channel_id=1, source_target_pairs={{0,1},{1,0},{2,3},{3,2},{4,5},{5,4},{6,7},{7,6},{8,9},{9,8},{10,11... | collective-permute-start | bytes 9437192 | tf_op jit(solution)/shard_map/ppermute | solution.py:351
  70.9 27.9 %collective-permute-start.21 = (bf16[896,512]{1,0:T(8,128)(2,1)S(1)}, bf16[896,512]{1,0:T(8,128)(2,1)S(1)}, u32[]{:S(2)}, u32[]{:S(2)}) collective-permute-start(bf16[896,512]{1,0:T(8,128)(2,1)S(1)} %pad_maximum_fusion.6.refs_4_.refs_2_), channel_id=1, source_target_pairs={{0,2},{1,3},{2,0},{3,1},{4,6},{5,7},{6,4},{7,5},{8,10},{9,11},{10,... | collective-permute-start | bytes 2752520 | tf_op jit(solution)/shard_map/ppermute | solution.py:354
  72.5 21.3 %collective-permute-start.19 = (bf16[256,512]{1,0:T(8,128)(2,1)S(1)}, bf16[256,512]{1,0:T(8,128)(2,1)S(1)}, u32[]{:S(2)}, u32[]{:S(2)}) collective-permute-start(bf16[256,512]{1,0:T(8,128)(2,1)S(1)} %get-tuple-element.45), channel_id=1, source_target_pairs={{0,8},{1,9},{2,10},{3,11},{4,12},{5,13},{6,14},{7,15},{8,0},{9,1},... | collective-permute-start | bytes 786440 | tf_op jit(solution)/shard_map/ppermute | solution.py:360
  75.9 22.8 %collective-permute-start.18 = (bf16[256,512]{1,0:T(8,128)(2,1)S(1)}, bf16[256,512]{1,0:T(8,128)(2,1)S(1)}, u32[]{:S(2)}, u32[]{:S(2)}) collective-permute-start(bf16[256,512]{1,0:T(8,128)(2,1)S(1)} %get-tuple-element.45), channel_id=1, source_target_pairs={{0,4},{1,5},{2,6},{3,7},{4,8},{5,9},{6,10},{7,11},{8,12},{9,13},{1... | collective-permute-start | bytes 786440 | tf_op jit(solution)/shard_map/ppermute | solution.py:360
  98.8 21.7 %collective-permute-start.22 = (bf16[896,512]{1,0:T(8,128)(2,1)S(1)}, bf16[896,512]{1,0:T(8,128)(2,1)S(1)}, u32[]{:S(2)}, u32[]{:S(2)}) collective-permute-start(bf16[896,512]{1,0:T(8,128)(2,1)S(1)} %pad_maximum_fusion.7.refs_3_.refs_5_), channel_id=1, source_target_pairs={{0,2},{1,3},{2,0},{3,1},{4,6},{5,7},{6,4},{7,5},{8,10},{9,11},{10,... | collective-permute-start | bytes 2752520 | tf_op jit(solution)/shard_map/ppermute | solution.py:354
  99.4 20.5 %collective-permute-start.23 = (bf16[256,512]{1,0:T(8,128)(2,1)S(1)}, bf16[256,512]{1,0:T(8,128)(2,1)S(1)}, u32[]{:S(2)}, u32[]{:S(2)}) collective-permute-start(bf16[256,512]{1,0:T(8,128)(2,1)S(1)} %pad_maximum_fusion.11), channel_id=1, source_target_pairs={{0,4},{1,5},{2,6},{3,7},{4,8},{5,9},{6,10},{7,11},{8,12},{9,13},{1... | collective-permute-start | bytes 786440 | tf_op jit(solution)/shard_map/ppermute | solution.py:360
  102.0 25.0 %collective-permute-start.27 = (bf16[256,512]{1,0:T(8,128)(2,1)S(1)}, bf16[256,512]{1,0:T(8,128)(2,1)S(1)}, u32[]{:S(2)}, u32[]{:S(2)}) collective-permute-start(bf16[256,512]{1,0:T(8,128)(2,1)S(1)} %pad_maximum_fusion.11), channel_id=1, source_target_pairs={{0,12},{1,13},{2,14},{3,15},{4,0},{5,1},{6,2},{7,3},{8,4},{9,5},{1... | collective-permute-start | bytes 786440 | tf_op jit(solution)/shard_map/ppermute | solution.py:360
  102.0 25.0 %collective-permute-start.26 = (bf16[256,512]{1,0:T(8,128)(2,1)S(1)}, bf16[256,512]{1,0:T(8,128)(2,1)S(1)}, u32[]{:S(2)}, u32[]{:S(2)}) collective-permute-start(bf16[256,512]{1,0:T(8,128)(2,1)S(1)} %pad_maximum_fusion.11), channel_id=1, source_target_pairs={{0,8},{1,9},{2,10},{3,11},{4,12},{5,13},{6,14},{7,15},{8,0},{9,1},... | collective-permute-start | bytes 786440 | tf_op jit(solution)/shard_map/ppermute | solution.py:360
  127.0 25.2 %collective-permute-start.28 = (bf16[1024,512]{1,0:T(8,128)(2,1)S(1)}, bf16[1024,512]{1,0:T(8,128)(2,1)S(1)}, u32[]{:S(2)}, u32[]{:S(2)}) collective-permute-start(bf16[1024,512]{1,0:T(8,128)(2,1)S(1)} %pad_maximum_fusion.4.refs_2_), channel_id=1, source_target_pairs={{0,2},{1,3},{2,0},{3,1},{4,6},{5,7},{6,4},{7,5},{8,10},{9,11},{10,... | collective-permute-start | bytes 3145736 | tf_op jit(solution)/shard_map/ppermute | solution.py:354
  129.0 30.0 %collective-permute-start.31 = (bf16[6,64,1024]{2,1,0:T(8,128)(2,1)S(1)}, bf16[6,64,1024]{2,1,0:T(8,128)(2,1)S(1)}, u32[]{:S(2)}, u32[]{:S(2)}) collective-permute-start(bf16[6,64,1024]{2,1,0:T(8,128)(2,1)S(1)} %add_convert_fusion.1), channel_id=1, source_target_pairs={{0,16},{16,0},{1,17},{17,1},{2,18},{18,2},{3,19},{19,3},{4,20},{20... | collective-permute-start | bytes 2359304 | tf_op jit(solution)/shard_map/ppermute | solution.py:357
  130.6 34.9 %collective-permute-start.32 = (bf16[6,64,1024]{2,1,0:T(8,128)(2,1)S(1)}, bf16[6,64,1024]{2,1,0:T(8,128)(2,1)S(1)}, u32[]{:S(2)}, u32[]{:S(2)}) collective-permute-start(bf16[6,64,1024]{2,1,0:T(8,128)(2,1)S(1)} %add_convert_fusion), channel_id=1, source_target_pairs={{0,16},{16,0},{1,17},{17,1},{2,18},{18,2},{3,19},{19,3},{4,20},{20... | collective-permute-start | bytes 2359304 | tf_op jit(solution)/shard_map/ppermute | solution.py:357
  (15 other events, 79.0 us)

commit v21 on v20

--- a/solution.py
+++ b/solution.py
@@ -88,6 +88,10 @@
 VMEM_LIMIT = 20 * 1024 * 1024
 BF16 = jnp.bfloat16
 F32 = jnp.float32
+
+
+def along(z, d, lines):
+    return z ^ d if lines & (lines - 1) == 0 else (z + lines - d) % lines
 
 
 def chunk_kernel(
@@ -127,7 +131,7 @@
                     pltpu.make_async_copy(ref, tokens_ref.at[2 * i + k], sems.at[len(copies)])
                 )
         for i, start, d, to_row, to_unit, n, wide in sources:
-            from_z = lax.rem(z + lines - d, lines)
+            from_z = along(z, d, lines)
             for to_y, ref in ((y, here_refs[i]), (1 - y, there_refs[i])):
                 to = weights_ref.at[from_z, to_y, pl.ds(to_row, n), pl.ds(to_unit, wide)]
                 copies.append(
@@ -357,7 +361,8 @@
         return lax.ppermute(a, "grp", [(0, 1), (1, 0)])
 
     def shift_z(a, d):
-        return lax.ppermute(a, "row", [(i, (i + 4 * d) % ranks) for i in range(ranks)])
+        pairs = [(4 * along(i // 4, d, lines) + i % 4, i) for i in range(ranks)]
+        return lax.ppermute(a, "row", pairs)
 
     def after(a, *others):
         return lax.optimization_barrier((a, *others))[0]
@@ -404,9 +409,9 @@
     own_rows = 4 * depth
     own_with = [
         [(0, 0, own_rows), (1, 0, own_rows), (2, 0, own_rows // 2)],
-        [(2, own_rows // 2, own_rows // 2)],
-        [(3, 0, own_rows // 2)],
-        [(3, own_rows // 2, own_rows // 2)],
+        [(2, own_rows // 2, own_rows // 2), (3, own_rows // 2, own_rows // 4)],
+        [(3, 0, own_rows // 2), (3, 3 * own_rows // 4, own_rows // 4)],
+        [],
         [(4, 0, own_rows)],
     ]
 

time: 171 us -> 168 us (0.982); the launches traced: 168 us -> 167 us
  starting transfers between devices: 35.9 us -> 33.6 us
    ppermute x15, starting transfers between devices: 23.2 us -> 19.2 us  [shift_z(): return lax.ppermute(a, 'row', pairs)]
    ppermute x15, waiting for transfers between devices: 52.6 us -> 55.9 us  [shift_z(): return lax.ppermute(a, 'row', pairs)]
    ppermute x5, waiting for transfers between devices: 22.8 us -> 19.7 us  [over_x(): return lax.ppermute(a, 'grp', [(0, 1), (1, 0)])]
  transfers between devices with their start and end apart: 33 -> 33, of which waited for: 15 -> 15; matrix products, arithmetic and copies ran while one was open for 4% -> 4% of each run, Pallas kernels for 21% -> 22%
where the time goes in v21:
time: 168 us; the launch traced here: 167 us
  waiting for transfers between devices  84.5 us (50%)
  Pallas kernels  39.3 us (23%)
  starting transfers between devices  33.6 us (20%)
  other arithmetic  5.61 us (3%)
  local copies, waits for them, and re-layouts  2.99 us (2%)
    ppermute x15, waiting for transfers between devices, shift_z(): return lax.ppermute(a, 'row', pairs)  55.9 us
    pallas_call x4, Pallas kernels, chunk(): pl.pallas_call(functools.partial(chunk_kernel, offset, kind, units, chips...  36.5 us
    ppermute x5, waiting for transfers between devices, over_x(): return lax.ppermute(a, 'grp', [(0, 1), (1, 0)])  19.7 us
    ppermute x15, starting transfers between devices, shift_z(): return lax.ppermute(a, 'row', pairs)  19.2 us
    ppermute x5, waiting for transfers between devices, over_y(): return lax.ppermute(a, 'row', [(i, i ^ 2) for i in range(ranks)])  8.82 us
    ppermute x5, starting transfers between devices, over_y(): return lax.ppermute(a, 'row', [(i, i ^ 2) for i in range(ranks)])  6.92 us
    ppermute x5, starting transfers between devices, over_x(): return lax.ppermute(a, 'grp', [(0, 1), (1, 0)])  6.13 us
  transfers between devices with their start and end apart: 33, of which 15 were waited for; matrix products, arithmetic and copies ran while one was open for 4% of the time, Pallas kernels for 22%

profile of v21, /device:TPU:8, one launch (start us, length us, event | category | flops | bytes accessed | tf_op | source)
XLA Modules:
  0.0 167.2 jit_solution(2308002292115687763)
XLA Ops:
  4.1 1.6 collective-permute-start.2
  5.7 2.5 %collective-permute-start.4 = (bf16[256,256]{1,0:T(8,128)(2,1)S(1)}, bf16[256,256]{1,0:T(8,128)(2,1)S(1)}, u32[]{:S(2)}, u32[]{:S(2)}) collective-permute-start(bf16[256,256]{1,0:T(8,128)(2,1)S(1)} %bitcast.98), channel_id=1, source_target_pairs={{4,0},{5,1},{6,2},{7,3},{0,4},{1,5},{2,6},{3,7},{12,8},{13,9},{14,... | collective-permute-start | bytes 393224 | tf_op jit(solution)/shard_map/ppermute | solution.py:365
  12.1 3.2 %collective-permute-done.4 = bf16[256,256]{1,0:T(8,128)(2,1)S(1)} collective-permute-done((bf16[256,256]{1,0:T(8,128)(2,1)S(1)}, bf16[256,256]{1,0:T(8,128)(2,1)S(1)}, u32[]{:S(2)}, u32[]{:S(2)}) %collective-permute-start.4) | collective-permute-done | bytes 131104 | tf_op jit(solution)/shard_map/ppermute | solution.py:365
  24.7 6.1 %collective-permute-done.9 = bf16[256,512]{1,0:T(8,128)(2,1)S(1)} collective-permute-done((bf16[256,512]{1,0:T(8,128)(2,1)S(1)}, bf16[256,512]{1,0:T(8,128)(2,1)S(1)}, u32[]{:S(2)}, u32[]{:S(2)}) %collective-permute-start.9) | collective-permute-done | bytes 262176 | tf_op jit(solution)/shard_map/ppermute | solution.py:365
  30.9 8.5 %collective-permute-done.10 = bf16[256,512]{1,0:T(8,128)(2,1)S(1)} collective-permute-done((bf16[256,512]{1,0:T(8,128)(2,1)S(1)}, bf16[256,512]{1,0:T(8,128)(2,1)S(1)}, u32[]{:S(2)}, u32[]{:S(2)}) %collective-permute-start.10) | collective-permute-done | bytes 262176 | tf_op jit(solution)/shard_map/ppermute | solution.py:365
  39.4 6.5 %collective-permute-done.11 = bf16[256,512]{1,0:T(8,128)(2,1)S(1)} collective-permute-done((bf16[256,512]{1,0:T(8,128)(2,1)S(1)}, bf16[256,512]{1,0:T(8,128)(2,1)S(1)}, u32[]{:S(2)}, u32[]{:S(2)}) %collective-permute-start.11) | collective-permute-done | bytes 262176 | tf_op jit(solution)/shard_map/ppermute | solution.py:365
  49.2 1.6 collective-permute-start.14
  52.1 12.3 %collective-permute-done.12 = bf16[6,64,1024]{2,1,0:T(8,128)(2,1)S(1)} collective-permute-done((bf16[6,64,1024]{2,1,0:T(8,128)(2,1)S(1)}, bf16[6,64,1024]{2,1,0:T(8,128)(2,1)S(1)}, u32[]{:S(2)}, u32[]{:S(2)}) %collective-permute-start.12) | collective-permute-done | bytes 786464 | tf_op jit(solution)/shard_map/ppermute | solution.py:361
  64.9 3.9 %collective-permute-done.14 = bf16[256,512]{1,0:T(8,128)(2,1)S(1)} collective-permute-done((bf16[256,512]{1,0:T(8,128)(2,1)S(1)}, bf16[256,512]{1,0:T(8,128)(2,1)S(1)}, u32[]{:S(2)}, u32[]{:S(2)}) %collective-permute-start.14) | collective-permute-done | bytes 262176 | tf_op jit(solution)/shard_map/ppermute | solution.py:365
  68.8 4.6 %collective-permute-done.15 = bf16[256,512]{1,0:T(8,128)(2,1)S(1)} collective-permute-done((bf16[256,512]{1,0:T(8,128)(2,1)S(1)}, bf16[256,512]{1,0:T(8,128)(2,1)S(1)}, u32[]{:S(2)}, u32[]{:S(2)}) %collective-permute-start.15) | collective-permute-done | bytes 262176 | tf_op jit(solution)/shard_map/ppermute | solution.py:365
  74.1 2.3 %collective-permute-start.19 = (bf16[256,512]{1,0:T(8,128)(2,1)S(1)}, bf16[256,512]{1,0:T(8,128)(2,1)S(1)}, u32[]{:S(2)}, u32[]{:S(2)}) collective-permute-start(bf16[256,512]{1,0:T(8,128)(2,1)S(1)} %get-tuple-element.45), channel_id=1, source_target_pairs={{8,0},{9,1},{10,2},{11,3},{12,4},{13,5},{14,6},{15,7},{0,8},{1,9},... | collective-permute-start | bytes 786440 | tf_op jit(solution)/shard_map/ppermute | solution.py:365
  77.6 7.4 %collective-permute-done.18 = bf16[256,512]{1,0:T(8,128)(2,1)S(1)} collective-permute-done((bf16[256,512]{1,0:T(8,128)(2,1)S(1)}, bf16[256,512]{1,0:T(8,128)(2,1)S(1)}, u32[]{:S(2)}, u32[]{:S(2)}) %collective-permute-start.18) | collective-permute-done | bytes 262176 | tf_op jit(solution)/shard_map/ppermute | solution.py:365
  85.1 9.3 %collective-permute-done.19 = bf16[256,512]{1,0:T(8,128)(2,1)S(1)} collective-permute-done((bf16[256,512]{1,0:T(8,128)(2,1)S(1)}, bf16[256,512]{1,0:T(8,128)(2,1)S(1)}, u32[]{:S(2)}, u32[]{:S(2)}) %collective-permute-start.19) | collective-permute-done | bytes 262176 | tf_op jit(solution)/shard_map/ppermute | solution.py:365
  94.3 6.3 %collective-permute-done.20 = bf16[256,512]{1,0:T(8,128)(2,1)S(1)} collective-permute-done((bf16[256,512]{1,0:T(8,128)(2,1)S(1)}, bf16[256,512]{1,0:T(8,128)(2,1)S(1)}, u32[]{:S(2)}, u32[]{:S(2)}) %collective-permute-start.20) | collective-permute-done | bytes 262176 | tf_op jit(solution)/shard_map/ppermute | solution.py:365
  103.3 3.5 %collective-permute-start.26 = (bf16[256,512]{1,0:T(8,128)(2,1)S(1)}, bf16[256,512]{1,0:T(8,128)(2,1)S(1)}, u32[]{:S(2)}, u32[]{:S(2)}) collective-permute-start(bf16[256,512]{1,0:T(8,128)(2,1)S(1)} %pad_maximum_fusion.8), channel_id=1, source_target_pairs={{8,0},{9,1},{10,2},{11,3},{12,4},{13,5},{14,6},{15,7},{0,8},{1,9},... | collective-permute-start | bytes 786440 | tf_op jit(solution)/shard_map/ppermute | solution.py:365
  106.8 10.7 %chunk.4 = (f32[768,1024]{1,0:T(8,128)S(1)}, f32[768,1024]{1,0:T(8,128)S(1)}) custom-call(s32[24]{0:T(128)S(1)} %pad_add_fusion.3.sorted_ref, s32[2]{0:T(128)S(1)} %pad_add_fusion.4.place_ref, s32[24]{0:T(128)S(1)} %pad_add_fusion.5.perm_ref, bf16[2,6,64,1024]{3,2,1,0:T(8,128)(2,1)S(1)} %get-tuple-element.48.refs_0_, ...), custom_call_target="tpu_custom_call" | custom-call | flops 5368709120 | bytes 20971520 | tf_op jit(solution)/shard_map/chunk/pallas_call | solution.py:265
  117.5 1.8 %collective-permute-done.22.refs_7_.refs_9_ = bf16[768,512]{1,0:T(8,128)(2,1)S(1)} collective-permute-done((bf16[768,512]{1,0:T(8,128)(2,1)S(1)}, bf16[768,512]{1,0:T(8,128)(2,1)S(1)}, u32[]{:S(2)}, u32[]{:S(2)}) %collective-permute-start.22) | collective-permute-done | bytes 786464 | tf_op jit(solution)/shard_map/ppermute | solution.py:358
  119.3 5.9 %chunk.5 = (bf16[6,64,1024]{2,1,0:T(8,128)(2,1)S(1)}, bf16[6,64,1024]{2,1,0:T(8,128)(2,1)S(1)}, bf16[6,64,1024]{2,1,0:T(8,128)(2,1)S(1)}, bf16[6,64,1024]{2,1,0:T(8,128)(2,1)S(1)}) custom-call(s32[24]{0:T(128)S(1)} %pad_add_fusion.3.sorted_ref, s32[2]{0:T(128)S(1)} %pad_add_fusion.4.place_ref, s32[24]{0:T(128)S(1)} %pad_add_fusion.5.perm_ref, ...), custom_call_target="tpu_custom_call" | custom-call | tf_op jit(solution)/shard_map/chunk/pallas_call | solution.py:265
  125.8 1.6 collective-permute-start.28
  130.4 13.7 %chunk.6 = (f32[768,1024]{1,0:T(8,128)S(1)}, f32[768,1024]{1,0:T(8,128)S(1)}) custom-call(s32[24]{0:T(128)S(1)} %pad_add_fusion.3.sorted_ref, s32[2]{0:T(128)S(1)} %pad_add_fusion.4.place_ref, s32[24]{0:T(128)S(1)} %pad_add_fusion.5.perm_ref, bf16[2,6,64,1024]{3,2,1,0:T(8,128)(2,1)S(1)} %get-tuple-element.57.refs_0_, ...), custom_call_target="tpu_custom_call" | custom-call | tf_op jit(solution)/shard_map/chunk/pallas_call | solution.py:265
  144.1 7.0 %collective-permute-done.28.refs_3_ = bf16[1024,512]{1,0:T(8,128)(2,1)S(1)} collective-permute-done((bf16[1024,512]{1,0:T(8,128)(2,1)S(1)}, bf16[1024,512]{1,0:T(8,128)(2,1)S(1)}, u32[]{:S(2)}, u32[]{:S(2)}) %collective-permute-start.28) | collective-permute-done | bytes 1048608 | tf_op jit(solution)/shard_map/ppermute | solution.py:358
  151.1 6.2 %chunk.7 = (f32[6,64,1024]{2,1,0:T(8,128)S(1)}, f32[6,64,1024]{2,1,0:T(8,128)S(1)}, bf16[6,64,1024]{2,1,0:T(8,128)(2,1)S(1)}, bf16[6,64,1024]{2,1,0:T(8,128)(2,1)S(1)}) custom-call(s32[24]{0:T(128)S(1)} %pad_add_fusion.3.sorted_ref, s32[2]{0:T(128)S(1)} %pad_add_fusion.4.place_ref, s32[24]{0:T(128)S(1)} %pad_add_fusion.5.perm_ref, ...), custom_call_target="tpu_custom_call" | custom-call | tf_op jit(solution)/shard_map/chunk/pallas_call | solution.py:265
  157.8 6.5 %collective-permute-done.32.across_back_ref = bf16[6,64,1024]{2,1,0:T(8,128)(2,1)S(1)} collective-permute-done((bf16[6,64,1024]{2,1,0:T(8,128)(2,1)S(1)}, bf16[6,64,1024]{2,1,0:T(8,128)(2,1)S(1)}, u32[]{:S(2)}, u32[]{:S(2)}) %collective-permute-start.32) | collective-permute-done | bytes 786464 | tf_op jit(solution)/shard_map/ppermute | solution.py:361
  164.4 2.8 %finish.1 = (bf16[6,64,1024]{2,1,0:T(8,128)(2,1)}, bf16[6,64,1024]{2,1,0:T(8,128)(2,1)}, f32[6,64]{1,0:T(8,128)}) custom-call(s32[6]{0:T(128)S(1)} %bitcast.79, bf16[6,64,1024]{2,1,0:T(8,128)(2,1)S(1)} %copy-done, bf16[6,64,1024]{2,1,0:T(8,128)(2,1)S(1)} %copy-done.1, f32[2,1024]{1,0:T(2,128)S(1)} %copy-done.2, ...), custom_call_target="tpu_custom_call" | custom-call | tf_op jit(solution)/shard_map/finish/pallas_call | solution.py:314
  (121 shorter events, 30.1 us)
Async XLA Ops:
  4.1 12.1 %collective-permute-start.2 = (bf16[256,256]{1,0:T(8,128)(2,1)S(1)}, bf16[256,256]{1,0:T(8,128)(2,1)S(1)}, u32[]{:S(2)}, u32[]{:S(2)}) collective-permute-start(bf16[256,256]{1,0:T(8,128)(2,1)S(1)} %bitcast.97), channel_id=1, source_target_pairs={{12,0},{13,1},{14,2},{15,3},{8,4},{9,5},{10,6},{11,7},{4,8},{5,9},... | collective-permute-start | bytes 393224 | tf_op jit(solution)/shard_map/ppermute | solution.py:365
  8.2 11.2 %collective-permute-start.7 = (bf16[256,256]{1,0:T(8,128)(2,1)S(1)}, bf16[256,256]{1,0:T(8,128)(2,1)S(1)}, u32[]{:S(2)}, u32[]{:S(2)}) collective-permute-start(bf16[256,256]{1,0:T(8,128)(2,1)S(1)} %bitcast.100), channel_id=1, source_target_pairs={{8,0},{9,1},{10,2},{11,3},{12,4},{13,5},{14,6},{15,7},{0,8},{1,9},... | collective-permute-start | bytes 393224 | tf_op jit(solution)/shard_map/ppermute | solution.py:365
  16.2 32.3 %collective-permute-start.5 = (bf16[6,64,1024]{2,1,0:T(8,128)(2,1)S(1)}, bf16[6,64,1024]{2,1,0:T(8,128)(2,1)S(1)}, u32[]{:S(2)}, u32[]{:S(2)}) collective-permute-start(bf16[6,64,1024]{2,1,0:T(8,128)(2,1)S(1)} %fusion.2), channel_id=1, source_target_pairs={{0,16},{16,0},{1,17},{17,1},{2,18},{18,2},{3,19},{19,3},{4,20},{20... | collective-permute-start | bytes 2359304 | tf_op jit(solution)/shard_map/ppermute | solution.py:361
  19.4 11.4 %collective-permute-start.9 = (bf16[256,512]{1,0:T(8,128)(2,1)S(1)}, bf16[256,512]{1,0:T(8,128)(2,1)S(1)}, u32[]{:S(2)}, u32[]{:S(2)}) collective-permute-start(bf16[256,512]{1,0:T(8,128)(2,1)S(1)} %get-tuple-element.40), channel_id=1, source_target_pairs={{4,0},{5,1},{6,2},{7,3},{0,4},{1,5},{2,6},{3,7},{12,8},{13,9},{14,... | collective-permute-start | bytes 786440 | tf_op jit(solution)/shard_map/ppermute | solution.py:365
  20.3 19.0 %collective-permute-start.10 = (bf16[256,512]{1,0:T(8,128)(2,1)S(1)}, bf16[256,512]{1,0:T(8,128)(2,1)S(1)}, u32[]{:S(2)}, u32[]{:S(2)}) collective-permute-start(bf16[256,512]{1,0:T(8,128)(2,1)S(1)} %get-tuple-element.40), channel_id=1, source_target_pairs={{8,0},{9,1},{10,2},{11,3},{12,4},{13,5},{14,6},{15,7},{0,8},{1,9},... | collective-permute-start | bytes 786440 | tf_op jit(solution)/shard_map/ppermute | solution.py:365
  21.4 24.5 %collective-permute-start.11 = (bf16[256,512]{1,0:T(8,128)(2,1)S(1)}, bf16[256,512]{1,0:T(8,128)(2,1)S(1)}, u32[]{:S(2)}, u32[]{:S(2)}) collective-permute-start(bf16[256,512]{1,0:T(8,128)(2,1)S(1)} %get-tuple-element.40), channel_id=1, source_target_pairs={{12,0},{13,1},{14,2},{15,3},{8,4},{9,5},{10,6},{11,7},{4,8},{5,9},... | collective-permute-start | bytes 786440 | tf_op jit(solution)/shard_map/ppermute | solution.py:365
  23.1 22.9 %collective-permute-start.8 = (bf16[1792,256]{1,0:T(8,128)(2,1)S(1)}, bf16[1792,256]{1,0:T(8,128)(2,1)S(1)}, u32[]{:S(2)}, u32[]{:S(2)}) collective-permute-start(bf16[1792,256]{1,0:T(8,128)(2,1)S(1)} %constant_dynamic-update-slice_fusion.refs_2_), channel_id=1, source_target_pairs={{0,2},{1,3},{2,0},{3,1},{4,6},{5,7},{6,4},{7,5},{8,10},{9,11},{10,... | collective-permute-start | bytes 2752520 | tf_op jit(solution)/shard_map/ppermute | solution.py:358
  45.9 18.5 %collective-permute-start.12 = (bf16[6,64,1024]{2,1,0:T(8,128)(2,1)S(1)}, bf16[6,64,1024]{2,1,0:T(8,128)(2,1)S(1)}, u32[]{:S(2)}, u32[]{:S(2)}) collective-permute-start(bf16[6,64,1024]{2,1,0:T(8,128)(2,1)S(1)} %copy-done.1), channel_id=1, source_target_pairs={{0,16},{16,0},{1,17},{17,1},{2,18},{18,2},{3,19},{19,3},{4,20},{20... | collective-permute-start | bytes 2359304 | tf_op jit(solution)/shard_map/ppermute | solution.py:361
  46.8 26.6 %collective-permute-start.16 = (bf16[960,512]{1,0:T(8,128)(2,1)S(1)}, bf16[960,512]{1,0:T(8,128)(2,1)S(1)}, u32[]{:S(2)}, u32[]{:S(2)}) collective-permute-start(bf16[960,512]{1,0:T(8,128)(2,1)S(1)} %constant_dynamic-update-slice_fusion.4.refs_3_.refs_2_), channel_id=1, source_target_pairs={{0,2},{1,3},{2,0},{3,1},{4,6},{5,7},{6,4},{7,5},{8,10},{9,11},{10,... | collective-permute-start | bytes 2949128 | tf_op jit(solution)/shard_map/ppermute | solution.py:358
  48.5 16.4 %collective-permute-start.13 = (bf16[256,512]{1,0:T(8,128)(2,1)S(1)}, bf16[256,512]{1,0:T(8,128)(2,1)S(1)}, u32[]{:S(2)}, u32[]{:S(2)}) collective-permute-start(bf16[256,512]{1,0:T(8,128)(2,1)S(1)} %pad_maximum_fusion.7), channel_id=1, source_target_pairs={{4,0},{5,1},{6,2},{7,3},{0,4},{1,5},{2,6},{3,7},{12,8},{13,9},{14,... | collective-permute-start | bytes 786440 | tf_op jit(solution)/shard_map/ppermute | solution.py:365
  49.2 19.6 %collective-permute-start.14 = (bf16[256,512]{1,0:T(8,128)(2,1)S(1)}, bf16[256,512]{1,0:T(8,128)(2,1)S(1)}, u32[]{:S(2)}, u32[]{:S(2)}) collective-permute-start(bf16[256,512]{1,0:T(8,128)(2,1)S(1)} %pad_maximum_fusion.7), channel_id=1, source_target_pairs={{8,0},{9,1},{10,2},{11,3},{12,4},{13,5},{14,6},{15,7},{0,8},{1,9},... | collective-permute-start | bytes 786440 | tf_op jit(solution)/shard_map/ppermute | solution.py:365
  50.8 22.6 %collective-permute-start.15 = (bf16[256,512]{1,0:T(8,128)(2,1)S(1)}, bf16[256,512]{1,0:T(8,128)(2,1)S(1)}, u32[]{:S(2)}, u32[]{:S(2)}) collective-permute-start(bf16[256,512]{1,0:T(8,128)(2,1)S(1)} %pad_maximum_fusion.7), channel_id=1, source_target_pairs={{12,0},{13,1},{14,2},{15,3},{8,4},{9,5},{10,6},{11,7},{4,8},{5,9},... | collective-permute-start | bytes 786440 | tf_op jit(solution)/shard_map/ppermute | solution.py:365
  73.5 28.8 %collective-permute-start.17 = (bf16[2,2,6,64,1024]{4,3,2,1,0:T(8,128)(2,1)S(1)}, bf16[2,2,6,64,1024]{4,3,2,1,0:T(8,128)(2,1)S(1)}, u32[]{:S(2)}, u32[]{:S(2)}) collective-permute-start(bf16[2,2,6,64,1024]{4,3,2,1,0:T(8,128)(2,1)S(1)} %pad_maximum_fusion), channel_id=1, source_target_pairs={{0,1},{1,0},{2,3},{3,2},{4,5},{5,4},{6,7},{7,6},{8,9},{9,8},{10,11... | collective-permute-start | bytes 9437192 | tf_op jit(solution)/shard_map/ppermute | solution.py:355
  73.5 27.1 %collective-permute-start.21 = (bf16[960,512]{1,0:T(8,128)(2,1)S(1)}, bf16[960,512]{1,0:T(8,128)(2,1)S(1)}, u32[]{:S(2)}, u32[]{:S(2)}) collective-permute-start(bf16[960,512]{1,0:T(8,128)(2,1)S(1)} %constant_dynamic-update-slice_fusion.7.refs_4_.refs_3_), channel_id=1, source_target_pairs={{0,2},{1,3},{2,0},{3,1},{4,6},{5,7},{6,4},{7,5},{8,10},{9,11},{10,... | collective-permute-start | bytes 2949128 | tf_op jit(solution)/shard_map/ppermute | solution.py:358
  74.1 10.9 %collective-permute-start.18 = (bf16[256,512]{1,0:T(8,128)(2,1)S(1)}, bf16[256,512]{1,0:T(8,128)(2,1)S(1)}, u32[]{:S(2)}, u32[]{:S(2)}) collective-permute-start(bf16[256,512]{1,0:T(8,128)(2,1)S(1)} %get-tuple-element.45), channel_id=1, source_target_pairs={{4,0},{5,1},{6,2},{7,3},{0,4},{1,5},{2,6},{3,7},{12,8},{13,9},{14,... | collective-permute-start | bytes 786440 | tf_op jit(solution)/shard_map/ppermute | solution.py:365
  74.1 20.2 %collective-permute-start.19 = (bf16[256,512]{1,0:T(8,128)(2,1)S(1)}, bf16[256,512]{1,0:T(8,128)(2,1)S(1)}, u32[]{:S(2)}, u32[]{:S(2)}) collective-permute-start(bf16[256,512]{1,0:T(8,128)(2,1)S(1)} %get-tuple-element.45), channel_id=1, source_target_pairs={{8,0},{9,1},{10,2},{11,3},{12,4},{13,5},{14,6},{15,7},{0,8},{1,9},... | collective-permute-start | bytes 786440 | tf_op jit(solution)/shard_map/ppermute | solution.py:365
  76.4 24.2 %collective-permute-start.20 = (bf16[256,512]{1,0:T(8,128)(2,1)S(1)}, bf16[256,512]{1,0:T(8,128)(2,1)S(1)}, u32[]{:S(2)}, u32[]{:S(2)}) collective-permute-start(bf16[256,512]{1,0:T(8,128)(2,1)S(1)} %get-tuple-element.45), channel_id=1, source_target_pairs={{12,0},{13,1},{14,2},{15,3},{8,4},{9,5},{10,6},{11,7},{4,8},{5,9},... | collective-permute-start | bytes 786440 | tf_op jit(solution)/shard_map/ppermute | solution.py:365
  100.7 18.6 %collective-permute-start.22 = (bf16[768,512]{1,0:T(8,128)(2,1)S(1)}, bf16[768,512]{1,0:T(8,128)(2,1)S(1)}, u32[]{:S(2)}, u32[]{:S(2)}) collective-permute-start(bf16[768,512]{1,0:T(8,128)(2,1)S(1)} %constant_dynamic-update-slice_fusion.10.refs_4_.refs_5_), channel_id=1, source_target_pairs={{0,2},{1,3},{2,0},{3,1},{4,6},{5,7},{6,4},{7,5},{8,10},{9,11},{10,... | collective-permute-start | bytes 2359304 | tf_op jit(solution)/shard_map/ppermute | solution.py:358
  102.3 15.1 %collective-permute-start.23 = (bf16[256,512]{1,0:T(8,128)(2,1)S(1)}, bf16[256,512]{1,0:T(8,128)(2,1)S(1)}, u32[]{:S(2)}, u32[]{:S(2)}) collective-permute-start(bf16[256,512]{1,0:T(8,128)(2,1)S(1)} %pad_maximum_fusion.8), channel_id=1, source_target_pairs={{4,0},{5,1},{6,2},{7,3},{0,4},{1,5},{2,6},{3,7},{12,8},{13,9},{14,... | collective-permute-start | bytes 786440 | tf_op jit(solution)/shard_map/ppermute | solution.py:365
  102.4 23.4 %collective-permute-start.27 = (bf16[256,512]{1,0:T(8,128)(2,1)S(1)}, bf16[256,512]{1,0:T(8,128)(2,1)S(1)}, u32[]{:S(2)}, u32[]{:S(2)}) collective-permute-start(bf16[256,512]{1,0:T(8,128)(2,1)S(1)} %pad_maximum_fusion.8), channel_id=1, source_target_pairs={{12,0},{13,1},{14,2},{15,3},{8,4},{9,5},{10,6},{11,7},{4,8},{5,9},... | collective-permute-start | bytes 786440 | tf_op jit(solution)/shard_map/ppermute | solution.py:365
  103.3 22.5 %collective-permute-start.26 = (bf16[256,512]{1,0:T(8,128)(2,1)S(1)}, bf16[256,512]{1,0:T(8,128)(2,1)S(1)}, u32[]{:S(2)}, u32[]{:S(2)}) collective-permute-start(bf16[256,512]{1,0:T(8,128)(2,1)S(1)} %pad_maximum_fusion.8), channel_id=1, source_target_pairs={{8,0},{9,1},{10,2},{11,3},{12,4},{13,5},{14,6},{15,7},{0,8},{1,9},... | collective-permute-start | bytes 786440 | tf_op jit(solution)/shard_map/ppermute | solution.py:365
  125.8 25.2 %collective-permute-start.28 = (bf16[1024,512]{1,0:T(8,128)(2,1)S(1)}, bf16[1024,512]{1,0:T(8,128)(2,1)S(1)}, u32[]{:S(2)}, u32[]{:S(2)}) collective-permute-start(bf16[1024,512]{1,0:T(8,128)(2,1)S(1)} %pad_maximum_fusion.4.refs_2_), channel_id=1, source_target_pairs={{0,2},{1,3},{2,0},{3,1},{4,6},{5,7},{6,4},{7,5},{8,10},{9,11},{10,... | collective-permute-start | bytes 3145736 | tf_op jit(solution)/shard_map/ppermute | solution.py:358
  127.9 30.0 %collective-permute-start.31 = (bf16[6,64,1024]{2,1,0:T(8,128)(2,1)S(1)}, bf16[6,64,1024]{2,1,0:T(8,128)(2,1)S(1)}, u32[]{:S(2)}, u32[]{:S(2)}) collective-permute-start(bf16[6,64,1024]{2,1,0:T(8,128)(2,1)S(1)} %add_convert_fusion.1), channel_id=1, source_target_pairs={{0,16},{16,0},{1,17},{17,1},{2,18},{18,2},{3,19},{19,3},{4,20},{20... | collective-permute-start | bytes 2359304 | tf_op jit(solution)/shard_map/ppermute | solution.py:361
  129.4 35.0 %collective-permute-start.32 = (bf16[6,64,1024]{2,1,0:T(8,128)(2,1)S(1)}, bf16[6,64,1024]{2,1,0:T(8,128)(2,1)S(1)}, u32[]{:S(2)}, u32[]{:S(2)}) collective-permute-start(bf16[6,64,1024]{2,1,0:T(8,128)(2,1)S(1)} %add_convert_fusion), channel_id=1, source_target_pairs={{0,16},{16,0},{1,17},{17,1},{2,18},{18,2},{3,19},{19,3},{4,20},{20... | collective-permute-start | bytes 2359304 | tf_op jit(solution)/shard_map/ppermute | solution.py:361
  (15 other events, 77.8 us)

commit v22 on v21

--- a/solution.py
+++ b/solution.py
@@ -401,16 +401,16 @@
 
     groups = [
         [(0, 0, 2 * unit)],
-        [(0, 2 * unit, 4 * unit)],
-        [(0, 6 * unit, unit), (1, 0, 3 * unit)],
-        [(1, 3 * unit, 4 * unit)],
+        [(0, 2 * unit, 5 * unit)],
+        [(1, 0, 4 * unit)],
+        [(1, 4 * unit, 3 * unit)],
         [(0, quarter, half), (1, quarter, half)],
     ]
     own_rows = 4 * depth
     own_with = [
-        [(0, 0, own_rows), (1, 0, own_rows), (2, 0, own_rows // 2)],
-        [(2, own_rows // 2, own_rows // 2), (3, own_rows // 2, own_rows // 4)],
-        [(3, 0, own_rows // 2), (3, 3 * own_rows // 4, own_rows // 4)],
+        [(0, 0, own_rows), (1, 0, own_rows), (2, 0, own_rows), (3, 0, own_rows)],
+        [],
+        [],
         [],
         [(4, 0, own_rows)],
     ]
@@ -434,7 +434,7 @@
         shifted.append([shift_z(mine, d) for d in range(1, lines)])
 
     def across_y(step, *waits):
-        wide = send[step].shape[1]
+        wide = send[step].shape[1] if step else unit
         parts = []
 
         def add(array, group, d, row, first):
@@ -444,10 +444,15 @@
 
         for group, row, n in own_with[step]:
             for first in range(0, send[group].shape[1], wide):
-                mine = send[0] if group == 0 else own(group, row, n, first, wide)
+                mine = (
+                    own(group, row, n, first, wide)
+                    if group
+                    else send[0][:, first : first + wide]
+                )
                 add(mine, group, 0, row, first)
         for d, rows_from in enumerate(shifted[step]):
-            add(rows_from, step, d + 1, 0, 0)
+            for first in range(0, rows_from.shape[1], wide):
+                add(rows_from[:, first : first + wide], step, d + 1, 0, first)
         here.append(jnp.concatenate(parts))
         there.append(over_y(after(here[step], *there[-1:], *waits)))
 

time: 168 us -> 168 us (level); the launches traced: 167 us -> 165 us
  Pallas kernels: 39.3 us -> 37.6 us
    ppermute x5, waiting for transfers between devices: 8.82 us -> 4.68 us  [over_y(): return lax.ppermute(a, 'row', [(i, i ^ 2) for i in range(ranks)])]
    ppermute x15, waiting for transfers between devices: 55.9 us -> 59.5 us  [shift_z(): return lax.ppermute(a, 'row', pairs)]
  transfers between devices with their start and end apart: 33 -> 33, of which waited for: 15 -> 16; matrix products, arithmetic and copies ran while one was open for 4% -> 4% of each run, Pallas kernels for 22% -> 21%
where the time goes in v22:
time: 168 us; the launch traced here: 165 us
  waiting for transfers between devices  83.3 us (50%)
  Pallas kernels  37.6 us (22%)
  starting transfers between devices  33.3 us (20%)
  other arithmetic  5.61 us (3%)
  local copies, waits for them, and re-layouts  3.45 us (2%)
    ppermute x15, waiting for transfers between devices, shift_z(): return lax.ppermute(a, 'row', pairs)  59.5 us
    pallas_call x4, Pallas kernels, chunk(): pl.pallas_call(functools.partial(chunk_kernel, offset, kind, units, chips...  34.8 us
    ppermute x15, starting transfers between devices, shift_z(): return lax.ppermute(a, 'row', pairs)  19.4 us
    ppermute x5, waiting for transfers between devices, over_x(): return lax.ppermute(a, 'grp', [(0, 1), (1, 0)])  19.1 us
    ppermute x5, starting transfers between devices, over_x(): return lax.ppermute(a, 'grp', [(0, 1), (1, 0)])  6.76 us
    ppermute x5, starting transfers between devices, over_y(): return lax.ppermute(a, 'row', [(i, i ^ 2) for i in range(ranks)])  5.9 us
    ppermute x5, waiting for transfers between devices, over_y(): return lax.ppermute(a, 'row', [(i, i ^ 2) for i in range(ranks)])  4.68 us
  transfers between devices with their start and end apart: 33, of which 16 were waited for; matrix products, arithmetic and copies ran while one was open for 4% of the time, Pallas kernels for 21%

profile of v22, /device:TPU:8, one launch (start us, length us, event | category | flops | bytes accessed | tf_op | source)
XLA Modules:
  0.0 164.5 jit_solution(2543178287235536567)
XLA Ops:
  4.1 1.6 collective-permute-start.2
  5.7 2.5 %collective-permute-start.4 = (bf16[256,256]{1,0:T(8,128)(2,1)S(1)}, bf16[256,256]{1,0:T(8,128)(2,1)S(1)}, u32[]{:S(2)}, u32[]{:S(2)}) collective-permute-start(bf16[256,256]{1,0:T(8,128)(2,1)S(1)} %bitcast.117), channel_id=1, source_target_pairs={{4,0},{5,1},{6,2},{7,3},{0,4},{1,5},{2,6},{3,7},{12,8},{13,9},{14,... | collective-permute-start | bytes 393224 | tf_op jit(solution)/shard_map/ppermute | solution.py:365
  13.3 2.1 %collective-permute-done.4 = bf16[256,256]{1,0:T(8,128)(2,1)S(1)} collective-permute-done((bf16[256,256]{1,0:T(8,128)(2,1)S(1)}, bf16[256,256]{1,0:T(8,128)(2,1)S(1)}, u32[]{:S(2)}, u32[]{:S(2)}) %collective-permute-start.4) | collective-permute-done | bytes 131104 | tf_op jit(solution)/shard_map/ppermute | solution.py:365
  18.5 1.6 collective-permute-start.8
  24.8 9.7 %collective-permute-done.9 = bf16[256,640]{1,0:T(8,128)(2,1)S(1)} collective-permute-done((bf16[256,640]{1,0:T(8,128)(2,1)S(1)}, bf16[256,640]{1,0:T(8,128)(2,1)S(1)}, u32[]{:S(2)}, u32[]{:S(2)}) %collective-permute-start.9) | collective-permute-done | bytes 327712 | tf_op jit(solution)/shard_map/ppermute | solution.py:365
  34.5 11.2 %collective-permute-done.10 = bf16[256,640]{1,0:T(8,128)(2,1)S(1)} collective-permute-done((bf16[256,640]{1,0:T(8,128)(2,1)S(1)}, bf16[256,640]{1,0:T(8,128)(2,1)S(1)}, u32[]{:S(2)}, u32[]{:S(2)}) %collective-permute-start.10) | collective-permute-done | bytes 327712 | tf_op jit(solution)/shard_map/ppermute | solution.py:365
  45.7 6.4 %collective-permute-done.11 = bf16[256,640]{1,0:T(8,128)(2,1)S(1)} collective-permute-done((bf16[256,640]{1,0:T(8,128)(2,1)S(1)}, bf16[256,640]{1,0:T(8,128)(2,1)S(1)}, u32[]{:S(2)}, u32[]{:S(2)}) %collective-permute-start.11) | collective-permute-done | bytes 327712 | tf_op jit(solution)/shard_map/ppermute | solution.py:365
  54.5 2.9 %collective-permute-start.14 = (bf16[256,512]{1,0:T(8,128)(2,1)S(1)}, bf16[256,512]{1,0:T(8,128)(2,1)S(1)}, u32[]{:S(2)}, u32[]{:S(2)}) collective-permute-start(bf16[256,512]{1,0:T(8,128)(2,1)S(1)} %slice_bitcast_fusion.1), channel_id=1, source_target_pairs={{8,0},{9,1},{10,2},{11,3},{12,4},{13,5},{14,6},{15,7},{0,8},{1,9},... | collective-permute-start | bytes 786440 | tf_op jit(solution)/shard_map/ppermute | solution.py:365
  58.0 11.9 %collective-permute-done.12 = bf16[6,64,1024]{2,1,0:T(8,128)(2,1)S(1)} collective-permute-done((bf16[6,64,1024]{2,1,0:T(8,128)(2,1)S(1)}, bf16[6,64,1024]{2,1,0:T(8,128)(2,1)S(1)}, u32[]{:S(2)}, u32[]{:S(2)}) %collective-permute-start.12) | collective-permute-done | bytes 786464 | tf_op jit(solution)/shard_map/ppermute | solution.py:361
  70.4 4.1 %collective-permute-done.14 = bf16[256,512]{1,0:T(8,128)(2,1)S(1)} collective-permute-done((bf16[256,512]{1,0:T(8,128)(2,1)S(1)}, bf16[256,512]{1,0:T(8,128)(2,1)S(1)}, u32[]{:S(2)}, u32[]{:S(2)}) %collective-permute-start.14) | collective-permute-done | bytes 262176 | tf_op jit(solution)/shard_map/ppermute | solution.py:365
  74.4 4.3 %collective-permute-done.15 = bf16[256,512]{1,0:T(8,128)(2,1)S(1)} collective-permute-done((bf16[256,512]{1,0:T(8,128)(2,1)S(1)}, bf16[256,512]{1,0:T(8,128)(2,1)S(1)}, u32[]{:S(2)}, u32[]{:S(2)}) %collective-permute-start.15) | collective-permute-done | bytes 262176 | tf_op jit(solution)/shard_map/ppermute | solution.py:365
  80.5 2.9 %collective-permute-start.19 = (bf16[256,384]{1,0:T(8,128)(2,1)S(1)}, bf16[256,384]{1,0:T(8,128)(2,1)S(1)}, u32[]{:S(2)}, u32[]{:S(2)}) collective-permute-start(bf16[256,384]{1,0:T(8,128)(2,1)S(1)} %slice_bitcast_fusion.2), channel_id=1, source_target_pairs={{8,0},{9,1},{10,2},{11,3},{12,4},{13,5},{14,6},{15,7},{0,8},{1,9},... | collective-permute-start | bytes 589832 | tf_op jit(solution)/shard_map/ppermute | solution.py:365
  84.1 4.9 %collective-permute-done.18 = bf16[256,384]{1,0:T(8,128)(2,1)S(1)} collective-permute-done((bf16[256,384]{1,0:T(8,128)(2,1)S(1)}, bf16[256,384]{1,0:T(8,128)(2,1)S(1)}, u32[]{:S(2)}, u32[]{:S(2)}) %collective-permute-start.18) | collective-permute-done | bytes 196640 | tf_op jit(solution)/shard_map/ppermute | solution.py:365
  89.0 8.2 %collective-permute-done.19 = bf16[256,384]{1,0:T(8,128)(2,1)S(1)} collective-permute-done((bf16[256,384]{1,0:T(8,128)(2,1)S(1)}, bf16[256,384]{1,0:T(8,128)(2,1)S(1)}, u32[]{:S(2)}, u32[]{:S(2)}) %collective-permute-start.19) | collective-permute-done | bytes 196640 | tf_op jit(solution)/shard_map/ppermute | solution.py:365
  97.2 4.2 %collective-permute-done.20 = bf16[256,384]{1,0:T(8,128)(2,1)S(1)} collective-permute-done((bf16[256,384]{1,0:T(8,128)(2,1)S(1)}, bf16[256,384]{1,0:T(8,128)(2,1)S(1)}, u32[]{:S(2)}, u32[]{:S(2)}) %collective-permute-start.20) | collective-permute-done | bytes 196640 | tf_op jit(solution)/shard_map/ppermute | solution.py:365
  103.7 2.8 %collective-permute-start.26 = (bf16[256,512]{1,0:T(8,128)(2,1)S(1)}, bf16[256,512]{1,0:T(8,128)(2,1)S(1)}, u32[]{:S(2)}, u32[]{:S(2)}) collective-permute-start(bf16[256,512]{1,0:T(8,128)(2,1)S(1)} %pad_maximum_fusion.7), channel_id=1, source_target_pairs={{8,0},{9,1},{10,2},{11,3},{12,4},{13,5},{14,6},{15,7},{0,8},{1,9},... | collective-permute-start | bytes 786440 | tf_op jit(solution)/shard_map/ppermute | solution.py:365
  106.5 9.7 %chunk.4 = (f32[768,1024]{1,0:T(8,128)S(1)}, f32[768,1024]{1,0:T(8,128)S(1)}) custom-call(s32[24]{0:T(128)S(1)} %pad_add_fusion.3.sorted_ref, s32[2]{0:T(128)S(1)} %pad_add_fusion.4.place_ref, s32[24]{0:T(128)S(1)} %pad_add_fusion.5.perm_ref, bf16[2,6,64,1024]{3,2,1,0:T(8,128)(2,1)S(1)} %get-tuple-element.48.refs_0_, ...), custom_call_target="tpu_custom_call" | custom-call | flops 5905580032 | bytes 21495808 | tf_op jit(solution)/shard_map/chunk/pallas_call | solution.py:265
  116.3 5.0 %chunk.5 = (bf16[6,64,1024]{2,1,0:T(8,128)(2,1)S(1)}, bf16[6,64,1024]{2,1,0:T(8,128)(2,1)S(1)}, bf16[6,64,1024]{2,1,0:T(8,128)(2,1)S(1)}, bf16[6,64,1024]{2,1,0:T(8,128)(2,1)S(1)}) custom-call(s32[24]{0:T(128)S(1)} %pad_add_fusion.3.sorted_ref, s32[2]{0:T(128)S(1)} %pad_add_fusion.4.place_ref, s32[24]{0:T(128)S(1)} %pad_add_fusion.5.perm_ref, ...), custom_call_target="tpu_custom_call" | custom-call | tf_op jit(solution)/shard_map/chunk/pallas_call | solution.py:265
  122.7 2.4 %collective-permute-done.26 = bf16[256,512]{1,0:T(8,128)(2,1)S(1)} collective-permute-done((bf16[256,512]{1,0:T(8,128)(2,1)S(1)}, bf16[256,512]{1,0:T(8,128)(2,1)S(1)}, u32[]{:S(2)}, u32[]{:S(2)}) %collective-permute-start.26) | collective-permute-done | bytes 262176 | tf_op jit(solution)/shard_map/ppermute | solution.py:365
  129.6 14.0 %chunk.6 = (f32[768,1024]{1,0:T(8,128)S(1)}, f32[768,1024]{1,0:T(8,128)S(1)}) custom-call(s32[24]{0:T(128)S(1)} %pad_add_fusion.3.sorted_ref, s32[2]{0:T(128)S(1)} %pad_add_fusion.4.place_ref, s32[24]{0:T(128)S(1)} %pad_add_fusion.5.perm_ref, bf16[2,6,64,1024]{3,2,1,0:T(8,128)(2,1)S(1)} %get-tuple-element.57.refs_0_, ...), custom_call_target="tpu_custom_call" | custom-call | tf_op jit(solution)/shard_map/chunk/pallas_call | solution.py:265
  143.6 4.7 %collective-permute-done.28.refs_3_ = bf16[1024,512]{1,0:T(8,128)(2,1)S(1)} collective-permute-done((bf16[1024,512]{1,0:T(8,128)(2,1)S(1)}, bf16[1024,512]{1,0:T(8,128)(2,1)S(1)}, u32[]{:S(2)}, u32[]{:S(2)}) %collective-permute-start.28) | collective-permute-done | bytes 1048608 | tf_op jit(solution)/shard_map/ppermute | solution.py:358
  148.3 6.1 %chunk.7 = (f32[6,64,1024]{2,1,0:T(8,128)S(1)}, f32[6,64,1024]{2,1,0:T(8,128)S(1)}, bf16[6,64,1024]{2,1,0:T(8,128)(2,1)S(1)}, bf16[6,64,1024]{2,1,0:T(8,128)(2,1)S(1)}) custom-call(s32[24]{0:T(128)S(1)} %pad_add_fusion.3.sorted_ref, s32[2]{0:T(128)S(1)} %pad_add_fusion.4.place_ref, s32[24]{0:T(128)S(1)} %pad_add_fusion.5.perm_ref, ...), custom_call_target="tpu_custom_call" | custom-call | tf_op jit(solution)/shard_map/chunk/pallas_call | solution.py:265
  154.9 6.7 %collective-permute-done.32.across_back_ref = bf16[6,64,1024]{2,1,0:T(8,128)(2,1)S(1)} collective-permute-done((bf16[6,64,1024]{2,1,0:T(8,128)(2,1)S(1)}, bf16[6,64,1024]{2,1,0:T(8,128)(2,1)S(1)}, u32[]{:S(2)}, u32[]{:S(2)}) %collective-permute-start.32) | collective-permute-done | bytes 786464 | tf_op jit(solution)/shard_map/ppermute | solution.py:361
  161.7 2.8 %finish.1 = (bf16[6,64,1024]{2,1,0:T(8,128)(2,1)}, bf16[6,64,1024]{2,1,0:T(8,128)(2,1)}, f32[6,64]{1,0:T(8,128)}) custom-call(s32[6]{0:T(128)S(1)} %bitcast.93, bf16[6,64,1024]{2,1,0:T(8,128)(2,1)S(1)} %copy-done, bf16[6,64,1024]{2,1,0:T(8,128)(2,1)S(1)} %copy-done.1, f32[2,1024]{1,0:T(2,128)S(1)} %copy-done.2, ...), custom_call_target="tpu_custom_call" | custom-call | tf_op jit(solution)/shard_map/finish/pallas_call | solution.py:314
  (128 shorter events, 30.6 us)
Async XLA Ops:
  4.1 9.2 %collective-permute-start.2 = (bf16[256,256]{1,0:T(8,128)(2,1)S(1)}, bf16[256,256]{1,0:T(8,128)(2,1)S(1)}, u32[]{:S(2)}, u32[]{:S(2)}) collective-permute-start(bf16[256,256]{1,0:T(8,128)(2,1)S(1)} %bitcast.116), channel_id=1, source_target_pairs={{12,0},{13,1},{14,2},{15,3},{8,4},{9,5},{10,6},{11,7},{4,8},{5,9},... | collective-permute-start | bytes 393224 | tf_op jit(solution)/shard_map/ppermute | solution.py:365
  5.7 9.6 %collective-permute-start.4 = (bf16[256,256]{1,0:T(8,128)(2,1)S(1)}, bf16[256,256]{1,0:T(8,128)(2,1)S(1)}, u32[]{:S(2)}, u32[]{:S(2)}) collective-permute-start(bf16[256,256]{1,0:T(8,128)(2,1)S(1)} %bitcast.117), channel_id=1, source_target_pairs={{4,0},{5,1},{6,2},{7,3},{0,4},{1,5},{2,6},{3,7},{12,8},{13,9},{14,... | collective-permute-start | bytes 393224 | tf_op jit(solution)/shard_map/ppermute | solution.py:365
  8.2 10.2 %collective-permute-start.7 = (bf16[256,256]{1,0:T(8,128)(2,1)S(1)}, bf16[256,256]{1,0:T(8,128)(2,1)S(1)}, u32[]{:S(2)}, u32[]{:S(2)}) collective-permute-start(bf16[256,256]{1,0:T(8,128)(2,1)S(1)} %bitcast.119), channel_id=1, source_target_pairs={{8,0},{9,1},{10,2},{11,3},{12,4},{13,5},{14,6},{15,7},{0,8},{1,9},... | collective-permute-start | bytes 393224 | tf_op jit(solution)/shard_map/ppermute | solution.py:365
  15.8 38.6 %collective-permute-start.5 = (bf16[6,64,1024]{2,1,0:T(8,128)(2,1)S(1)}, bf16[6,64,1024]{2,1,0:T(8,128)(2,1)S(1)}, u32[]{:S(2)}, u32[]{:S(2)}) collective-permute-start(bf16[6,64,1024]{2,1,0:T(8,128)(2,1)S(1)} %fusion.2), channel_id=1, source_target_pairs={{0,16},{16,0},{1,17},{17,1},{2,18},{18,2},{3,19},{19,3},{4,20},{20... | collective-permute-start | bytes 2359304 | tf_op jit(solution)/shard_map/ppermute | solution.py:361
  18.5 33.6 %collective-permute-start.8 = (bf16[5120,128]{1,0:T(8,128)(2,1)S(1)}, bf16[5120,128]{1,0:T(8,128)(2,1)S(1)}, u32[]{:S(2)}, u32[]{:S(2)}) collective-permute-start(bf16[5120,128]{1,0:T(8,128)(2,1)S(1)} %slice_dynamic-update-slice_fusion.refs_2_), channel_id=1, source_target_pairs={{0,2},{1,3},{2,0},{3,1},{4,6},{5,7},{6,4},{7,5},{8,10},{9,11},{10,... | collective-permute-start | bytes 3932168 | tf_op jit(solution)/shard_map/ppermute | solution.py:358
  20.7 13.8 %collective-permute-start.9 = (bf16[256,640]{1,0:T(8,128)(2,1)S(1)}, bf16[256,640]{1,0:T(8,128)(2,1)S(1)}, u32[]{:S(2)}, u32[]{:S(2)}) collective-permute-start(bf16[256,640]{1,0:T(8,128)(2,1)S(1)} %slice_bitcast_fusion), channel_id=1, source_target_pairs={{4,0},{5,1},{6,2},{7,3},{0,4},{1,5},{2,6},{3,7},{12,8},{13,9},{14,... | collective-permute-start | bytes 983048 | tf_op jit(solution)/shard_map/ppermute | solution.py:365
  22.4 23.3 %collective-permute-start.10 = (bf16[256,640]{1,0:T(8,128)(2,1)S(1)}, bf16[256,640]{1,0:T(8,128)(2,1)S(1)}, u32[]{:S(2)}, u32[]{:S(2)}) collective-permute-start(bf16[256,640]{1,0:T(8,128)(2,1)S(1)} %slice_bitcast_fusion), channel_id=1, source_target_pairs={{8,0},{9,1},{10,2},{11,3},{12,4},{13,5},{14,6},{15,7},{0,8},{1,9},... | collective-permute-start | bytes 983048 | tf_op jit(solution)/shard_map/ppermute | solution.py:365
  23.6 28.5 %collective-permute-start.11 = (bf16[256,640]{1,0:T(8,128)(2,1)S(1)}, bf16[256,640]{1,0:T(8,128)(2,1)S(1)}, u32[]{:S(2)}, u32[]{:S(2)}) collective-permute-start(bf16[256,640]{1,0:T(8,128)(2,1)S(1)} %slice_bitcast_fusion), channel_id=1, source_target_pairs={{12,0},{13,1},{14,2},{15,3},{8,4},{9,5},{10,6},{11,7},{4,8},{5,9},... | collective-permute-start | bytes 983048 | tf_op jit(solution)/shard_map/ppermute | solution.py:365
  52.1 17.7 %collective-permute-start.12 = (bf16[6,64,1024]{2,1,0:T(8,128)(2,1)S(1)}, bf16[6,64,1024]{2,1,0:T(8,128)(2,1)S(1)}, u32[]{:S(2)}, u32[]{:S(2)}) collective-permute-start(bf16[6,64,1024]{2,1,0:T(8,128)(2,1)S(1)} %copy-done.1), channel_id=1, source_target_pairs={{0,16},{16,0},{1,17},{17,1},{2,18},{18,2},{3,19},{19,3},{4,20},{20... | collective-permute-start | bytes 2359304 | tf_op jit(solution)/shard_map/ppermute | solution.py:361
  53.7 25.1 %collective-permute-start.16 = (bf16[768,640]{1,0:T(8,128)(2,1)S(1)}, bf16[768,640]{1,0:T(8,128)(2,1)S(1)}, u32[]{:S(2)}, u32[]{:S(2)}) collective-permute-start(bf16[768,640]{1,0:T(8,128)(2,1)S(1)} %constant_dynamic-update-slice_fusion.refs_3_), channel_id=1, source_target_pairs={{0,2},{1,3},{2,0},{3,1},{4,6},{5,7},{6,4},{7,5},{8,10},{9,11},{10,... | collective-permute-start | bytes 2949128 | tf_op jit(solution)/shard_map/ppermute | solution.py:358
  54.4 15.9 %collective-permute-start.13 = (bf16[256,512]{1,0:T(8,128)(2,1)S(1)}, bf16[256,512]{1,0:T(8,128)(2,1)S(1)}, u32[]{:S(2)}, u32[]{:S(2)}) collective-permute-start(bf16[256,512]{1,0:T(8,128)(2,1)S(1)} %slice_bitcast_fusion.1), channel_id=1, source_target_pairs={{4,0},{5,1},{6,2},{7,3},{0,4},{1,5},{2,6},{3,7},{12,8},{13,9},{14,... | collective-permute-start | bytes 786440 | tf_op jit(solution)/shard_map/ppermute | solution.py:365
  54.5 19.9 %collective-permute-start.14 = (bf16[256,512]{1,0:T(8,128)(2,1)S(1)}, bf16[256,512]{1,0:T(8,128)(2,1)S(1)}, u32[]{:S(2)}, u32[]{:S(2)}) collective-permute-start(bf16[256,512]{1,0:T(8,128)(2,1)S(1)} %slice_bitcast_fusion.1), channel_id=1, source_target_pairs={{8,0},{9,1},{10,2},{11,3},{12,4},{13,5},{14,6},{15,7},{0,8},{1,9},... | collective-permute-start | bytes 786440 | tf_op jit(solution)/shard_map/ppermute | solution.py:365
  57.4 21.3 %collective-permute-start.15 = (bf16[256,512]{1,0:T(8,128)(2,1)S(1)}, bf16[256,512]{1,0:T(8,128)(2,1)S(1)}, u32[]{:S(2)}, u32[]{:S(2)}) collective-permute-start(bf16[256,512]{1,0:T(8,128)(2,1)S(1)} %slice_bitcast_fusion.1), channel_id=1, source_target_pairs={{12,0},{13,1},{14,2},{15,3},{8,4},{9,5},{10,6},{11,7},{4,8},{5,9},... | collective-permute-start | bytes 786440 | tf_op jit(solution)/shard_map/ppermute | solution.py:365
  78.7 23.3 %collective-permute-start.17 = (bf16[2,2,6,64,1024]{4,3,2,1,0:T(8,128)(2,1)S(1)}, bf16[2,2,6,64,1024]{4,3,2,1,0:T(8,128)(2,1)S(1)}, u32[]{:S(2)}, u32[]{:S(2)}) collective-permute-start(bf16[2,2,6,64,1024]{4,3,2,1,0:T(8,128)(2,1)S(1)} %pad_maximum_fusion), channel_id=1, source_target_pairs={{0,1},{1,0},{2,3},{3,2},{4,5},{5,4},{6,7},{7,6},{8,9},{9,8},{10,11... | collective-permute-start | bytes 9437192 | tf_op jit(solution)/shard_map/ppermute | solution.py:355
  78.8 22.6 %collective-permute-start.21 = (bf16[768,512]{1,0:T(8,128)(2,1)S(1)}, bf16[768,512]{1,0:T(8,128)(2,1)S(1)}, u32[]{:S(2)}, u32[]{:S(2)}) collective-permute-start(bf16[768,512]{1,0:T(8,128)(2,1)S(1)} %constant_dynamic-update-slice_fusion.6.refs_4_), channel_id=1, source_target_pairs={{0,2},{1,3},{2,0},{3,1},{4,6},{5,7},{6,4},{7,5},{8,10},{9,11},{10,... | collective-permute-start | bytes 2359304 | tf_op jit(solution)/shard_map/ppermute | solution.py:358
  80.5 16.6 %collective-permute-start.19 = (bf16[256,384]{1,0:T(8,128)(2,1)S(1)}, bf16[256,384]{1,0:T(8,128)(2,1)S(1)}, u32[]{:S(2)}, u32[]{:S(2)}) collective-permute-start(bf16[256,384]{1,0:T(8,128)(2,1)S(1)} %slice_bitcast_fusion.2), channel_id=1, source_target_pairs={{8,0},{9,1},{10,2},{11,3},{12,4},{13,5},{14,6},{15,7},{0,8},{1,9},... | collective-permute-start | bytes 589832 | tf_op jit(solution)/shard_map/ppermute | solution.py:365
  83.5 17.9 %collective-permute-start.20 = (bf16[256,384]{1,0:T(8,128)(2,1)S(1)}, bf16[256,384]{1,0:T(8,128)(2,1)S(1)}, u32[]{:S(2)}, u32[]{:S(2)}) collective-permute-start(bf16[256,384]{1,0:T(8,128)(2,1)S(1)} %slice_bitcast_fusion.2), channel_id=1, source_target_pairs={{12,0},{13,1},{14,2},{15,3},{8,4},{9,5},{10,6},{11,7},{4,8},{5,9},... | collective-permute-start | bytes 589832 | tf_op jit(solution)/shard_map/ppermute | solution.py:365
  101.4 14.8 %collective-permute-start.22 = (bf16[768,384]{1,0:T(8,128)(2,1)S(1)}, bf16[768,384]{1,0:T(8,128)(2,1)S(1)}, u32[]{:S(2)}, u32[]{:S(2)}) collective-permute-start(bf16[768,384]{1,0:T(8,128)(2,1)S(1)} %constant_dynamic-update-slice_fusion.3.refs_3_.refs_5_), channel_id=1, source_target_pairs={{0,2},{1,3},{2,0},{3,1},{4,6},{5,7},{6,4},{7,5},{8,10},{9,11},{10,... | collective-permute-start | bytes 1769480 | tf_op jit(solution)/shard_map/ppermute | solution.py:358
  102.0 14.2 %collective-permute-start.23 = (bf16[256,512]{1,0:T(8,128)(2,1)S(1)}, bf16[256,512]{1,0:T(8,128)(2,1)S(1)}, u32[]{:S(2)}, u32[]{:S(2)}) collective-permute-start(bf16[256,512]{1,0:T(8,128)(2,1)S(1)} %pad_maximum_fusion.7), channel_id=1, source_target_pairs={{4,0},{5,1},{6,2},{7,3},{0,4},{1,5},{2,6},{3,7},{12,8},{13,9},{14,... | collective-permute-start | bytes 786440 | tf_op jit(solution)/shard_map/ppermute | solution.py:365
  102.1 20.5 %collective-permute-start.27 = (bf16[256,512]{1,0:T(8,128)(2,1)S(1)}, bf16[256,512]{1,0:T(8,128)(2,1)S(1)}, u32[]{:S(2)}, u32[]{:S(2)}) collective-permute-start(bf16[256,512]{1,0:T(8,128)(2,1)S(1)} %pad_maximum_fusion.7), channel_id=1, source_target_pairs={{12,0},{13,1},{14,2},{15,3},{8,4},{9,5},{10,6},{11,7},{4,8},{5,9},... | collective-permute-start | bytes 786440 | tf_op jit(solution)/shard_map/ppermute | solution.py:365
  103.7 21.4 %collective-permute-start.26 = (bf16[256,512]{1,0:T(8,128)(2,1)S(1)}, bf16[256,512]{1,0:T(8,128)(2,1)S(1)}, u32[]{:S(2)}, u32[]{:S(2)}) collective-permute-start(bf16[256,512]{1,0:T(8,128)(2,1)S(1)} %pad_maximum_fusion.7), channel_id=1, source_target_pairs={{8,0},{9,1},{10,2},{11,3},{12,4},{13,5},{14,6},{15,7},{0,8},{1,9},... | collective-permute-start | bytes 786440 | tf_op jit(solution)/shard_map/ppermute | solution.py:365
  125.2 23.1 %collective-permute-start.28 = (bf16[1024,512]{1,0:T(8,128)(2,1)S(1)}, bf16[1024,512]{1,0:T(8,128)(2,1)S(1)}, u32[]{:S(2)}, u32[]{:S(2)}) collective-permute-start(bf16[1024,512]{1,0:T(8,128)(2,1)S(1)} %pad_maximum_fusion.4.refs_2_), channel_id=1, source_target_pairs={{0,2},{1,3},{2,0},{3,1},{4,6},{5,7},{6,4},{7,5},{8,10},{9,11},{10,... | collective-permute-start | bytes 3145736 | tf_op jit(solution)/shard_map/ppermute | solution.py:358
  127.1 27.8 %collective-permute-start.31 = (bf16[6,64,1024]{2,1,0:T(8,128)(2,1)S(1)}, bf16[6,64,1024]{2,1,0:T(8,128)(2,1)S(1)}, u32[]{:S(2)}, u32[]{:S(2)}) collective-permute-start(bf16[6,64,1024]{2,1,0:T(8,128)(2,1)S(1)} %add_convert_fusion.1), channel_id=1, source_target_pairs={{0,16},{16,0},{1,17},{17,1},{2,18},{18,2},{3,19},{19,3},{4,20},{20... | collective-permute-start | bytes 2359304 | tf_op jit(solution)/shard_map/ppermute | solution.py:361
  128.0 33.6 %collective-permute-start.32 = (bf16[6,64,1024]{2,1,0:T(8,128)(2,1)S(1)}, bf16[6,64,1024]{2,1,0:T(8,128)(2,1)S(1)}, u32[]{:S(2)}, u32[]{:S(2)}) collective-permute-start(bf16[6,64,1024]{2,1,0:T(8,128)(2,1)S(1)} %add_convert_fusion), channel_id=1, source_target_pairs={{0,16},{16,0},{1,17},{17,1},{2,18},{18,2},{3,19},{19,3},{4,20},{20... | collective-permute-start | bytes 2359304 | tf_op jit(solution)/shard_map/ppermute | solution.py:361
  (15 other events, 84.6 us)
